TPU v7x, 32 devices: a whole 2x2x4 slice. The times are simulated.
32 devices in a mesh: head: 4 (over y, x), ctx: 8 (over z, core).
Axes of the slice: x: 2, y: 2, z: 4, core: 2. Of those that a mesh axis runs over, the one named last changes fastest.
Arguments:
- queries: bfloat16 [16, 128, 2048], P('ctx', 'head'), may hold values from -8 to 8
- key_vectors: bfloat16 [16, 128, 256], P('ctx', 'head'), may hold values from -8 to 8
- value_vectors: bfloat16 [16, 128, 256], P('ctx', 'head'), may hold values from -4 to 4
- out_grad: bfloat16 [16, 128, 2048], P('ctx', 'head'), may hold values from -4 to 4
- block_order: int32 [16], replicated, may hold values from 0 to 15, each once
Outputs:
- attended: bfloat16 [16, 128, 2048], P('ctx', 'head')
- query_grad: bfloat16 [16, 128, 2048], P('ctx', 'head')
- key_grad: bfloat16 [16, 128, 256], P('ctx', 'head')
- value_grad: bfloat16 [16, 128, 256], P('ctx', 'head')
All inputs are finite; a program needn't handle non-finite values.
Results may differ from a plain program's by a relative error of at most 0.025.
Values may be sent and summed in bfloat16 or wider, within the bound.
No kernel may reach another device: no remote copies, remote signals or barrier semaphores. Data moves between devices by JAX's collectives and lax.ppermute only.
A program may use at most 64 MiB of HBM per device.

v0:
```python
import math

import jax
import jax.numpy as jnp
from jax import lax
from jax.sharding import PartitionSpec as P

HD = 128


LOWEST = -1e30


def from_behind(block, axis, distance):
    devices = range(lax.axis_size(axis))
    route = [((i - distance) % len(devices), i) for i in devices]
    return lax.ppermute(block, axis, route)


def row_positions(block_order, first_row, row_count, block_len):
    row_index = first_row + jnp.arange(row_count, dtype=jnp.int32)
    block_id = row_index // block_len
    matches = block_id[:, None] == jnp.arange(block_order.shape[0], dtype=jnp.int32)[None, :]
    picked = jnp.sum(jnp.where(matches, block_order[None, :], 0), axis=1)
    return picked * block_len + row_index % block_len


def contract_rows(left_side, right_side):
    return lax.dot_general(
        left_side, right_side, (((1,), (1,)), ((), ())), preferred_element_type=jnp.float32
    )


def contract_cols(left_side, right_side):
    return lax.dot_general(
        left_side, right_side, (((0,), (0,)), ((), ())), preferred_element_type=jnp.float32
    )


def forward_tile(running, key_part, value_part, part_pos, query_rows, query_pos, scaling):
    row_max, row_sum, weighted = running
    scores = contract_rows(query_rows, key_part) * scaling
    allowed = part_pos[None, :] <= query_pos[:, None]
    new_max = jnp.maximum(row_max, jnp.max(jnp.where(allowed, scores, LOWEST), axis=1))
    weights = jnp.where(allowed, jnp.exp(scores - new_max[:, None]), 0.0)
    factor = jnp.exp(row_max - new_max)
    weighted = weighted * factor[:, None] + jnp.dot(
        weights.astype(jnp.bfloat16), value_part, preferred_element_type=jnp.float32
    )
    return (new_max, row_sum * factor + jnp.sum(weights, axis=1), weighted)


def cycle_tile(
    state,
    key_part,
    value_part,
    part_pos,
    query_rows,
    grad_rows,
    query_pos,
    log_total,
    row_delta,
    scaling,
):
    query_total, key_acc, value_acc = state
    scores = contract_rows(query_rows, key_part) * scaling
    allowed = part_pos[None, :] <= query_pos[:, None]
    probs = jnp.where(allowed, jnp.exp(scores - log_total[:, None]), 0.0)
    grad_weights = contract_rows(grad_rows, value_part)
    grad_scores = (probs * (grad_weights - row_delta[:, None])).astype(jnp.bfloat16)
    query_total = query_total + jnp.dot(grad_scores, key_part, preferred_element_type=jnp.float32)
    key_acc = key_acc + contract_cols(grad_scores, query_rows)
    value_acc = value_acc + contract_cols(probs.astype(jnp.bfloat16), grad_rows)
    return (query_total, key_acc, value_acc)


def shards(queries, key_vectors, value_vectors, out_grad, block_order):
    head_devices = lax.axis_size("head")
    halves, token_rows, query_width = queries.shape
    kv_heads = key_vectors.shape[2] // HD
    repeat_count = head_devices // kv_heads
    scaling = 1.0 / math.sqrt(HD)

    def widen(source):
        grouped = source.reshape(halves, token_rows, kv_heads, 1, HD)
        return jnp.broadcast_to(grouped, (halves, token_rows, kv_heads, repeat_count, HD)).reshape(
            halves, token_rows, head_devices * HD
        )

    query_local, grad_local, key_local, value_local = (
        lax.all_to_all(queries, "head", split_axis=2, concat_axis=1, tiled=True),
        lax.all_to_all(out_grad, "head", split_axis=2, concat_axis=1, tiled=True),
        lax.all_to_all(widen(key_vectors), "head", split_axis=2, concat_axis=1, tiled=True),
        lax.all_to_all(widen(value_vectors), "head", split_axis=2, concat_axis=1, tiled=True),
    )
    block_len = query_local.shape[1]
    rows_here = halves * block_len
    per_row = query_local.shape[2] // HD
    total_rows = rows_here * per_row
    query_rows = query_local.reshape(total_rows, HD)
    grad_rows = grad_local.reshape(total_rows, HD)
    key_rows = key_local.reshape(rows_here, HD)
    value_rows = value_local.reshape(rows_here, HD)
    key_pos = row_positions(block_order, lax.axis_index("ctx") * rows_here, rows_here, block_len)
    query_pos = jnp.repeat(key_pos, per_row)
    start_state = (
        jnp.full((total_rows,), LOWEST, jnp.float32),
        jnp.zeros((total_rows,), jnp.float32),
        jnp.zeros((total_rows, HD), jnp.float32),
    )

    def forward_piece(running, pieces, first_row):
        key_part, value_part = pieces
        part_pos = row_positions(block_order, first_row, key_part.shape[0], block_len)
        return forward_tile(running, key_part, value_part, part_pos, query_rows, query_pos, scaling)

    whole_keys, whole_values = (
        lax.all_gather(key_rows, "ctx", axis=0, tiled=True),
        lax.all_gather(value_rows, "ctx", axis=0, tiled=True),
    )
    piece_rows = whole_keys.shape[0] // 4

    def forward_step(block_step, running):
        first_row = block_step * piece_rows
        key_part = lax.dynamic_slice_in_dim(whole_keys, first_row, piece_rows, 0)
        value_part = lax.dynamic_slice_in_dim(whole_values, first_row, piece_rows, 0)
        return forward_piece(running, (key_part, value_part), first_row)

    row_max, row_sum, weighted = lax.fori_loop(0, 4, forward_step, start_state)
    log_total = row_max + jnp.log(row_sum)
    attended = (weighted / row_sum[:, None]).astype(jnp.bfloat16)
    attended_wide = lax.optimization_barrier(attended).astype(jnp.float32)
    row_delta = jnp.sum(grad_rows.astype(jnp.float32) * attended_wide, axis=1)
    empty_keys = jnp.zeros((rows_here, HD), jnp.float32)
    grad_state = (jnp.zeros((total_rows, HD), jnp.float32), empty_keys, empty_keys)
    ctx_devices = lax.axis_size("ctx")
    own_index = lax.axis_index("ctx")

    def owner_tile(step, state):
        owner = (own_index - step) % ctx_devices
        first_row = owner * rows_here
        key_part = lax.dynamic_slice_in_dim(whole_keys, first_row, rows_here, 0)
        value_part = lax.dynamic_slice_in_dim(whole_values, first_row, rows_here, 0)
        part_pos = row_positions(block_order, first_row, rows_here, block_len)
        return cycle_tile(
            state,
            key_part,
            value_part,
            part_pos,
            query_rows,
            grad_rows,
            query_pos,
            log_total,
            row_delta,
            scaling,
        )

    first_state = owner_tile(0, grad_state)

    def cycle_step(step, state):
        query_total, key_acc, value_acc = state
        key_acc, value_acc = (
            from_behind(key_acc.astype(jnp.bfloat16), "ctx", 1).astype(key_acc.dtype),
            from_behind(value_acc.astype(jnp.bfloat16), "ctx", 1).astype(value_acc.dtype),
        )
        return owner_tile(step, (query_total, key_acc, value_acc))

    query_total, key_acc, value_acc = lax.fori_loop(1, ctx_devices, cycle_step, first_state)
    key_total, value_total = (
        from_behind(key_acc.astype(jnp.bfloat16), "ctx", 1).astype(key_acc.dtype),
        from_behind(value_acc.astype(jnp.bfloat16), "ctx", 1).astype(value_acc.dtype),
    )
    query_heads = (query_total * scaling).reshape(halves, block_len, per_row * HD)
    key_heads = (key_total * scaling).reshape(halves, block_len, HD)
    value_heads = value_total.reshape(halves, block_len, HD)
    attended_back, query_back, key_back, value_back = (
        lax.all_to_all(
            attended_wide.reshape(halves, block_len, per_row * HD).astype(jnp.bfloat16),
            "head",
            split_axis=1,
            concat_axis=2,
            tiled=True,
        ).astype(jnp.float32),
        lax.all_to_all(
            query_heads.astype(jnp.bfloat16), "head", split_axis=1, concat_axis=2, tiled=True
        ).astype(query_heads.dtype),
        lax.all_to_all(
            key_heads.astype(jnp.bfloat16), "head", split_axis=1, concat_axis=2, tiled=True
        ).astype(key_heads.dtype),
        lax.all_to_all(
            value_heads.astype(jnp.bfloat16), "head", split_axis=1, concat_axis=2, tiled=True
        ).astype(value_heads.dtype),
    )
    key_sum = jnp.sum(
        key_back.reshape(halves, token_rows, kv_heads, repeat_count, HD), axis=3
    ).reshape(halves, token_rows, kv_heads * HD)
    value_sum = jnp.sum(
        value_back.reshape(halves, token_rows, kv_heads, repeat_count, HD), axis=3
    ).reshape(halves, token_rows, kv_heads * HD)
    return (
        attended_back.astype(jnp.bfloat16),
        query_back.astype(jnp.bfloat16),
        key_sum.astype(jnp.bfloat16),
        value_sum.astype(jnp.bfloat16),
    )


def solution(mesh):
    placed = (
        P("ctx", "head", None),
        P("ctx", "head", None),
        P("ctx", "head", None),
        P("ctx", "head", None),
        P(),
    )
    return jax.shard_map(
        shards,
        mesh=mesh,
        in_specs=placed,
        out_specs=(
            P("ctx", "head", None),
            P("ctx", "head", None),
            P("ctx", "head", None),
            P("ctx", "head", None),
        ),
        check_vma=False,
    )
```

profile of v0, /device:TPU:0, one launch (start us, length us, event | category | flops | bytes accessed | tf_op | source)
XLA Modules:
  0.0 165.8 jit_solution(10646157961130624552)
XLA Ops:
  0.6 0.9 copy.81
  1.7 0.9 reshape.210
  2.6 5.3 %all-to-all-start.2 = ((bf16[4,2,4096]{2,1,0:T(2,128)(2,1)}), bf16[4,2,4096]{2,1,0:T(2,128)(2,1)S(1)}, u32[]{:S(2)}, u32[]{:S(2)}) async-start(bf16[4,2,4096]{2,1,0:T(2,128)(2,1)} %reshape.210), calls=%async_computation.2 | async-start | bytes 131072 | tf_op jit(solution)/shard_map/all_to_all | solution.py:94
  8.0 0.7 select_reduce_fusion.2
  8.7 0.9 copy.79
  9.7 0.9 reshape.206
  10.6 2.1 %all-to-all-done.2 = bf16[4,2,4096]{2,1,0:T(2,128)(2,1)S(1)} async-done(((bf16[4,2,4096]{2,1,0:T(2,128)(2,1)}), bf16[4,2,4096]{2,1,0:T(2,128)(2,1)S(1)}, u32[]{:S(2)}, u32[]{:S(2)}) %all-to-all-start.2) | async-done | bytes 65568 | tf_op jit(solution)/shard_map/all_to_all | solution.py:94
  12.8 3.3 %all-to-all-start = ((bf16[4,2,4096]{2,1,0:T(2,128)(2,1)}), bf16[4,2,4096]{2,1,0:T(2,128)(2,1)S(1)}, u32[]{:S(2)}, u32[]{:S(2)}) async-start(bf16[4,2,4096]{2,1,0:T(2,128)(2,1)} %reshape.206), calls=%async_computation | async-start | bytes 131072 | tf_op jit(solution)/shard_map/all_to_all | solution.py:93
  16.9 0.7 copy.60
  17.6 1.7 %reshape.208 = bf16[4,2,16384]{2,1,0:T(2,128)(2,1)} reshape(bf16[2048,2,32]{2,1,0:T(2,128)(2,1)S(1)} %bitcast.125) | data formatting | bytes 524288
  19.3 0.7 copy.68
  20.0 1.7 %reshape.212 = bf16[4,2,16384]{2,1,0:T(2,128)(2,1)} reshape(bf16[2048,2,32]{2,1,0:T(2,128)(2,1)S(1)} %bitcast.126) | data formatting | bytes 524288
  22.1 4.2 %all-to-all-start.1 = ((bf16[4,2,16384]{2,1,0:T(2,128)(2,1)}), bf16[4,2,16384]{2,1,0:T(2,128)(2,1)S(1)}, u32[]{:S(2)}, u32[]{:S(2)}) async-start(bf16[4,2,16384]{2,1,0:T(2,128)(2,1)} %reshape.208), calls=%async_computation.1 | async-start | bytes 524288 | tf_op jit(solution)/shard_map/all_to_all | solution.py:91
  26.6 15.4 %all_gather.6 = bf16[2048,128]{1,0:T(8,128)(2,1)S(1)} all-gather(bf16[256,128]{1,0:T(8,128)(2,1)S(1)} %bitcast.138), channel_id=1, replica_groups=mesh['head'=4,'ctx'=8] {'ctx'}, dimensions={0}, use_global_device_ids=true | all-gather | bytes 589824 | tf_op jit(solution)/shard_map/all_gather | solution.py:118
  42.0 14.8 %all_gather.7 = bf16[2048,128]{1,0:T(8,128)(2,1)S(1)} all-gather(bf16[256,128]{1,0:T(8,128)(2,1)S(1)} %bitcast.135), channel_id=1, replica_groups=mesh['head'=4,'ctx'=8] {'ctx'}, dimensions={0}, use_global_device_ids=true | all-gather | bytes 589824 | tf_op jit(solution)/shard_map/all_gather | solution.py:119
  56.9 4.2 %all-to-all-start.4 = ((bf16[4,2,16384]{2,1,0:T(2,128)(2,1)}), bf16[4,2,16384]{2,1,0:T(2,128)(2,1)}, u32[]{:S(2)}, u32[]{:S(2)}) async-start(bf16[4,2,16384]{2,1,0:T(2,128)(2,1)} %reshape.212), calls=%async_computation.4 | async-start | bytes 524288 | tf_op jit(solution)/shard_map/all_to_all | solution.py:92
  61.6 0.7 copy.61
  62.5 8.8 %while.42 = (s32[]{:T(128)}, f32[1024]{0:T(1024)S(1)}, f32[1024]{0:T(1024)S(1)}, f32[1024,128]{1,0:T(8,128)S(1)}, s32[16]{0:T(128)S(1)}, /*index=5*/bf16[2048,12...) while((s32[]{:T(128)}, f32[1024]{0:T(1024)S(1)}, ...), condition=%wide.region_5.6_spmd.clone, body=%wide.region_1.5_spmd.clone.sunk | while | flops 276213248 | bytes 7972111 | solution.py:129
  63.8 0.8 convolution_add_fusion.5
  66.0 0.8 convolution_add_fusion.5
  68.2 0.8 convolution_add_fusion.5
  70.4 0.8 convolution_add_fusion.5
  71.5 3.0 %reshape.213 = bf16[2048,2,32]{2,1,0:T(2,128)(2,1)S(1)} reshape(bf16[4,2,16384]{2,1,0:T(2,128)(2,1)} %all-to-all-done.4) | data formatting | bytes 524288
  74.6 0.7 copy.69
  77.3 45.8 %while.41 = (s32[]{:T(128)}, f32[1024,128]{1,0:T(8,128)S(1)}, bf16[256,128]{1,0:T(8,128)(2,1)S(1)}, bf16[256,128]{1,0:T(8,128)(2,1)S(1)}, s32[]{:T(128)}, /*inde...) while((s32[]{:T(128)}, f32[1024,128]{1,0:T(8,128)S(1)}, ...), condition=%wide.region_10.11_spmd.clone, body=%wide.region_8.10_spmd.clone.sunk | while | flops 337988864 | bytes 7831032 | solution.py:168
  77.7 1.2 collective-permute-start
  80.3 2.5 %collective-permute-done.1 = bf16[256,128]{1,0:T(8,128)(2,1)S(1)} collective-permute-done((bf16[256,128]{1,0:T(8,128)(2,1)S(1)}, bf16[256,128]{1,0:T(8,128)(2,1)S(1)}, u32[]{:S(2)}, u32[]{:S(2)}) %collective-permute-start.1) | collective-permute-done | bytes 65568 | tf_op jit(solution)/shard_map/while/body/eval_jaxpr/ppermute | solution.py:17
  85.4 4.0 %collective-permute-done.1 = bf16[256,128]{1,0:T(8,128)(2,1)S(1)} collective-permute-done((bf16[256,128]{1,0:T(8,128)(2,1)S(1)}, bf16[256,128]{1,0:T(8,128)(2,1)S(1)}, u32[]{:S(2)}, u32[]{:S(2)}) %collective-permute-start.1) | collective-permute-done | bytes 65568 | tf_op jit(solution)/shard_map/while/body/eval_jaxpr/ppermute | solution.py:17
  92.0 4.0 %collective-permute-done.1 = bf16[256,128]{1,0:T(8,128)(2,1)S(1)} collective-permute-done((bf16[256,128]{1,0:T(8,128)(2,1)S(1)}, bf16[256,128]{1,0:T(8,128)(2,1)S(1)}, u32[]{:S(2)}, u32[]{:S(2)}) %collective-permute-start.1) | collective-permute-done | bytes 65568 | tf_op jit(solution)/shard_map/while/body/eval_jaxpr/ppermute | solution.py:17
  98.5 4.0 %collective-permute-done.1 = bf16[256,128]{1,0:T(8,128)(2,1)S(1)} collective-permute-done((bf16[256,128]{1,0:T(8,128)(2,1)S(1)}, bf16[256,128]{1,0:T(8,128)(2,1)S(1)}, u32[]{:S(2)}, u32[]{:S(2)}) %collective-permute-start.1) | collective-permute-done | bytes 65568 | tf_op jit(solution)/shard_map/while/body/eval_jaxpr/ppermute | solution.py:17
  105.0 4.0 %collective-permute-done.1 = bf16[256,128]{1,0:T(8,128)(2,1)S(1)} collective-permute-done((bf16[256,128]{1,0:T(8,128)(2,1)S(1)}, bf16[256,128]{1,0:T(8,128)(2,1)S(1)}, u32[]{:S(2)}, u32[]{:S(2)}) %collective-permute-start.1) | collective-permute-done | bytes 65568 | tf_op jit(solution)/shard_map/while/body/eval_jaxpr/ppermute | solution.py:17
  111.6 4.0 %collective-permute-done.1 = bf16[256,128]{1,0:T(8,128)(2,1)S(1)} collective-permute-done((bf16[256,128]{1,0:T(8,128)(2,1)S(1)}, bf16[256,128]{1,0:T(8,128)(2,1)S(1)}, u32[]{:S(2)}, u32[]{:S(2)}) %collective-permute-start.1) | collective-permute-done | bytes 65568 | tf_op jit(solution)/shard_map/while/body/eval_jaxpr/ppermute | solution.py:17
  118.1 4.0 %collective-permute-done.1 = bf16[256,128]{1,0:T(8,128)(2,1)S(1)} collective-permute-done((bf16[256,128]{1,0:T(8,128)(2,1)S(1)}, bf16[256,128]{1,0:T(8,128)(2,1)S(1)}, u32[]{:S(2)}, u32[]{:S(2)}) %collective-permute-start.1) | collective-permute-done | bytes 65568 | tf_op jit(solution)/shard_map/while/body/eval_jaxpr/ppermute | solution.py:17
  123.2 5.4 %collective-permute-done.3 = bf16[256,128]{1,0:T(8,128)(2,1)S(1)} collective-permute-done((bf16[256,128]{1,0:T(8,128)(2,1)S(1)}, bf16[256,128]{1,0:T(8,128)(2,1)S(1)}, u32[]{:S(2)}, u32[]{:S(2)}) %collective-permute-start.3) | collective-permute-done | bytes 65568 | tf_op jit(solution)/shard_map/ppermute | solution.py:17
  128.7 0.7 copy.76
  129.3 4.2 %all-to-all-start.7 = ((bf16[2,128,128]{2,0,1:T(2,128)(2,1)}), bf16[2,128,128]{2,0,1:T(2,128)(2,1)S(1)}, u32[]{:S(2)}, u32[]{:S(2)}) async-start(bf16[2,128,128]{2,0,1:T(2,128)(2,1)} %copy.76), calls=%async_computation.7 | async-start | bytes 131072 | tf_op jit(solution)/shard_map/all_to_all | solution.py:190
  133.6 0.7 copy.73
  134.3 4.1 %all-to-all-done.7 = bf16[2,128,128]{2,0,1:T(2,128)(2,1)S(1)} async-done(((bf16[2,128,128]{2,0,1:T(2,128)(2,1)}), bf16[2,128,128]{2,0,1:T(2,128)(2,1)S(1)}, u32[]{:S(2)}, u32[]{:S(2)}) %all-to-all-start.7) | async-done | bytes 65568 | tf_op jit(solution)/shard_map/all_to_all | solution.py:190
  138.4 3.3 %all-to-all-start.6 = ((bf16[2,128,128]{2,0,1:T(2,128)(2,1)}), bf16[2,128,128]{2,0,1:T(2,128)(2,1)S(1)}, u32[]{:S(2)}, u32[]{:S(2)}) async-start(bf16[2,128,128]{2,0,1:T(2,128)(2,1)} %copy.73), calls=%async_computation.6 | async-start | bytes 131072 | tf_op jit(solution)/shard_map/all_to_all | solution.py:187
  141.9 1.0 copy.65
  142.8 3.8 %all-to-all-done.6 = bf16[2,128,128]{2,0,1:T(2,128)(2,1)S(1)} async-done(((bf16[2,128,128]{2,0,1:T(2,128)(2,1)}), bf16[2,128,128]{2,0,1:T(2,128)(2,1)S(1)}, u32[]{:S(2)}, u32[]{:S(2)}) %all-to-all-start.6) | async-done | bytes 65568 | tf_op jit(solution)/shard_map/all_to_all | solution.py:187
  146.6 3.4 %all-to-all-start.3 = ((bf16[2,128,512]{2,0,1:T(2,128)(2,1)}), bf16[2,128,512]{2,0,1:T(2,128)(2,1)S(1)}, u32[]{:S(2)}, u32[]{:S(2)}) async-start(bf16[2,128,512]{2,0,1:T(2,128)(2,1)} %copy.65), calls=%async_computation.3 | async-start | bytes 524288 | tf_op jit(solution)/shard_map/all_to_all | solution.py:177
  150.2 1.0 copy.70
  151.2 5.1 %all-to-all-done.3 = bf16[2,128,512]{2,0,1:T(2,128)(2,1)S(1)} async-done(((bf16[2,128,512]{2,0,1:T(2,128)(2,1)}), bf16[2,128,512]{2,0,1:T(2,128)(2,1)S(1)}, u32[]{:S(2)}, u32[]{:S(2)}) %all-to-all-start.3) | async-done | bytes 262176 | tf_op jit(solution)/shard_map/all_to_all | solution.py:177
  156.3 3.4 %all-to-all-start.5 = ((bf16[2,128,512]{2,0,1:T(2,128)(2,1)}), bf16[2,128,512]{2,0,1:T(2,128)(2,1)S(1)}, u32[]{:S(2)}, u32[]{:S(2)}) async-start(bf16[2,128,512]{2,0,1:T(2,128)(2,1)} %copy.70), calls=%async_computation.5 | async-start | bytes 524288 | tf_op jit(solution)/shard_map/all_to_all | solution.py:184
  161.3 0.7 copy.87
  162.0 3.0 %all-to-all-done.5 = bf16[2,128,512]{2,0,1:T(2,128)(2,1)S(1)} async-done(((bf16[2,128,512]{2,0,1:T(2,128)(2,1)}), bf16[2,128,512]{2,0,1:T(2,128)(2,1)S(1)}, u32[]{:S(2)}, u32[]{:S(2)}) %all-to-all-start.5) | async-done | bytes 262176 | tf_op jit(solution)/shard_map/all_to_all | solution.py:184
  165.1 0.7 copy.88
  (187 shorter events, 29.4 us)
Async XLA Ops:
  0.6 16.2 %copy-start = (bf16[2,32,2048]{2,1,0:T(8,128)(2,1)S(1)}, bf16[2,32,2048]{2,1,0:T(8,128)(2,1)}, u32[]{:S(2)}) copy-start(bf16[2,32,2048]{2,1,0:T(8,128)(2,1)} %param.9) | copy-start | bytes 786436
  2.6 16.7 %copy-start.1 = (bf16[2,32,2048]{2,1,0:T(8,128)(2,1)S(1)}, bf16[2,32,2048]{2,1,0:T(8,128)(2,1)}, u32[]{:S(2)}) copy-start(bf16[2,32,2048]{2,1,0:T(8,128)(2,1)} %param.12) | copy-start | bytes 786436
  2.6 10.1 %all-to-all-start.2 = ((bf16[4,2,4096]{2,1,0:T(2,128)(2,1)}), bf16[4,2,4096]{2,1,0:T(2,128)(2,1)S(1)}, u32[]{:S(2)}, u32[]{:S(2)}) async-start(bf16[4,2,4096]{2,1,0:T(2,128)(2,1)} %reshape.210), calls=%async_computation.2 | async-start | bytes 131072 | tf_op jit(solution)/shard_map/all_to_all | solution.py:94
  12.8 9.3 %all-to-all-start = ((bf16[4,2,4096]{2,1,0:T(2,128)(2,1)}), bf16[4,2,4096]{2,1,0:T(2,128)(2,1)S(1)}, u32[]{:S(2)}, u32[]{:S(2)}) async-start(bf16[4,2,4096]{2,1,0:T(2,128)(2,1)} %reshape.206), calls=%async_computation | async-start | bytes 131072 | tf_op jit(solution)/shard_map/all_to_all | solution.py:93
  22.1 34.8 %all-to-all-start.1 = ((bf16[4,2,16384]{2,1,0:T(2,128)(2,1)}), bf16[4,2,16384]{2,1,0:T(2,128)(2,1)S(1)}, u32[]{:S(2)}, u32[]{:S(2)}) async-start(bf16[4,2,16384]{2,1,0:T(2,128)(2,1)} %reshape.208), calls=%async_computation.1 | async-start | bytes 524288 | tf_op jit(solution)/shard_map/all_to_all | solution.py:91
  42.0 20.4 %copy-start.2 = (s32[16]{0:T(128)S(1)}, s32[16]{0:T(128)}, u32[]{:S(2)}) copy-start(s32[16]{0:T(128)} %param.13) | copy-start | bytes 196
  56.9 14.6 %all-to-all-start.4 = ((bf16[4,2,16384]{2,1,0:T(2,128)(2,1)}), bf16[4,2,16384]{2,1,0:T(2,128)(2,1)}, u32[]{:S(2)}, u32[]{:S(2)}) async-start(bf16[4,2,16384]{2,1,0:T(2,128)(2,1)} %reshape.212), calls=%async_computation.4 | async-start | bytes 524288 | tf_op jit(solution)/shard_map/all_to_all | solution.py:92
  71.2 4.4 %copy-start.5 = (s32[256]{0:T(256)S(1)}, s32[256]{0:T(256)}, u32[]{:S(2)}) copy-start(s32[256]{0:T(256)} %get-tuple-element.702) | copy-start | bytes 3076
  71.5 4.5 %copy-start.3 = (f32[1024]{0:T(1024)}, f32[1024]{0:T(1024)S(1)}, u32[]{:S(2)}) copy-start(f32[1024]{0:T(1024)S(1)} %log_add_fusion) | copy-start | bytes 12292
  76.3 1.0 copy-start.4
  77.3 5.5 %collective-permute-start.1 = (bf16[256,128]{1,0:T(8,128)(2,1)S(1)}, bf16[256,128]{1,0:T(8,128)(2,1)S(1)}, u32[]{:S(2)}, u32[]{:S(2)}) collective-permute-start(bf16[256,128]{1,0:T(8,128)(2,1)S(1)} %get-tuple-element.906), channel_id=1, source_target_pairs={{7,0},{0,1},{1,2},{2,3},{3,4},{4,5},{5,6},{6,7},{15,8},{8,9},{9,10... | collective-permute-start | bytes 196616 | tf_op jit(solution)/shard_map/while/body/eval_jaxpr/ppermute | solution.py:17
  77.7 5.8 %collective-permute-start = (bf16[256,128]{1,0:T(8,128)(2,1)S(1)}, bf16[256,128]{1,0:T(8,128)(2,1)S(1)}, u32[]{:S(2)}, u32[]{:S(2)}) collective-permute-start(bf16[256,128]{1,0:T(8,128)(2,1)S(1)} %get-tuple-element.905), channel_id=1, source_target_pairs={{7,0},{0,1},{1,2},{2,3},{3,4},{4,5},{5,6},{6,7},{15,8},{8,9},{9,10... | collective-permute-start | bytes 196616 | tf_op jit(solution)/shard_map/while/body/eval_jaxpr/ppermute | solution.py:17
  83.9 5.5 %collective-permute-start.1 = (bf16[256,128]{1,0:T(8,128)(2,1)S(1)}, bf16[256,128]{1,0:T(8,128)(2,1)S(1)}, u32[]{:S(2)}, u32[]{:S(2)}) collective-permute-start(bf16[256,128]{1,0:T(8,128)(2,1)S(1)} %get-tuple-element.906), channel_id=1, source_target_pairs={{7,0},{0,1},{1,2},{2,3},{3,4},{4,5},{5,6},{6,7},{15,8},{8,9},{9,10... | collective-permute-start | bytes 196616 | tf_op jit(solution)/shard_map/while/body/eval_jaxpr/ppermute | solution.py:17
  83.9 6.2 %collective-permute-start = (bf16[256,128]{1,0:T(8,128)(2,1)S(1)}, bf16[256,128]{1,0:T(8,128)(2,1)S(1)}, u32[]{:S(2)}, u32[]{:S(2)}) collective-permute-start(bf16[256,128]{1,0:T(8,128)(2,1)S(1)} %get-tuple-element.905), channel_id=1, source_target_pairs={{7,0},{0,1},{1,2},{2,3},{3,4},{4,5},{5,6},{6,7},{15,8},{8,9},{9,10... | collective-permute-start | bytes 196616 | tf_op jit(solution)/shard_map/while/body/eval_jaxpr/ppermute | solution.py:17
  90.4 5.5 %collective-permute-start.1 = (bf16[256,128]{1,0:T(8,128)(2,1)S(1)}, bf16[256,128]{1,0:T(8,128)(2,1)S(1)}, u32[]{:S(2)}, u32[]{:S(2)}) collective-permute-start(bf16[256,128]{1,0:T(8,128)(2,1)S(1)} %get-tuple-element.906), channel_id=1, source_target_pairs={{7,0},{0,1},{1,2},{2,3},{3,4},{4,5},{5,6},{6,7},{15,8},{8,9},{9,10... | collective-permute-start | bytes 196616 | tf_op jit(solution)/shard_map/while/body/eval_jaxpr/ppermute | solution.py:17
  90.5 6.2 %collective-permute-start = (bf16[256,128]{1,0:T(8,128)(2,1)S(1)}, bf16[256,128]{1,0:T(8,128)(2,1)S(1)}, u32[]{:S(2)}, u32[]{:S(2)}) collective-permute-start(bf16[256,128]{1,0:T(8,128)(2,1)S(1)} %get-tuple-element.905), channel_id=1, source_target_pairs={{7,0},{0,1},{1,2},{2,3},{3,4},{4,5},{5,6},{6,7},{15,8},{8,9},{9,10... | collective-permute-start | bytes 196616 | tf_op jit(solution)/shard_map/while/body/eval_jaxpr/ppermute | solution.py:17
  96.9 5.5 %collective-permute-start.1 = (bf16[256,128]{1,0:T(8,128)(2,1)S(1)}, bf16[256,128]{1,0:T(8,128)(2,1)S(1)}, u32[]{:S(2)}, u32[]{:S(2)}) collective-permute-start(bf16[256,128]{1,0:T(8,128)(2,1)S(1)} %get-tuple-element.906), channel_id=1, source_target_pairs={{7,0},{0,1},{1,2},{2,3},{3,4},{4,5},{5,6},{6,7},{15,8},{8,9},{9,10... | collective-permute-start | bytes 196616 | tf_op jit(solution)/shard_map/while/body/eval_jaxpr/ppermute | solution.py:17
  97.0 6.2 %collective-permute-start = (bf16[256,128]{1,0:T(8,128)(2,1)S(1)}, bf16[256,128]{1,0:T(8,128)(2,1)S(1)}, u32[]{:S(2)}, u32[]{:S(2)}) collective-permute-start(bf16[256,128]{1,0:T(8,128)(2,1)S(1)} %get-tuple-element.905), channel_id=1, source_target_pairs={{7,0},{0,1},{1,2},{2,3},{3,4},{4,5},{5,6},{6,7},{15,8},{8,9},{9,10... | collective-permute-start | bytes 196616 | tf_op jit(solution)/shard_map/while/body/eval_jaxpr/ppermute | solution.py:17
  103.5 5.5 %collective-permute-start.1 = (bf16[256,128]{1,0:T(8,128)(2,1)S(1)}, bf16[256,128]{1,0:T(8,128)(2,1)S(1)}, u32[]{:S(2)}, u32[]{:S(2)}) collective-permute-start(bf16[256,128]{1,0:T(8,128)(2,1)S(1)} %get-tuple-element.906), channel_id=1, source_target_pairs={{7,0},{0,1},{1,2},{2,3},{3,4},{4,5},{5,6},{6,7},{15,8},{8,9},{9,10... | collective-permute-start | bytes 196616 | tf_op jit(solution)/shard_map/while/body/eval_jaxpr/ppermute | solution.py:17
  103.5 6.2 %collective-permute-start = (bf16[256,128]{1,0:T(8,128)(2,1)S(1)}, bf16[256,128]{1,0:T(8,128)(2,1)S(1)}, u32[]{:S(2)}, u32[]{:S(2)}) collective-permute-start(bf16[256,128]{1,0:T(8,128)(2,1)S(1)} %get-tuple-element.905), channel_id=1, source_target_pairs={{7,0},{0,1},{1,2},{2,3},{3,4},{4,5},{5,6},{6,7},{15,8},{8,9},{9,10... | collective-permute-start | bytes 196616 | tf_op jit(solution)/shard_map/while/body/eval_jaxpr/ppermute | solution.py:17
  110.0 5.5 %collective-permute-start.1 = (bf16[256,128]{1,0:T(8,128)(2,1)S(1)}, bf16[256,128]{1,0:T(8,128)(2,1)S(1)}, u32[]{:S(2)}, u32[]{:S(2)}) collective-permute-start(bf16[256,128]{1,0:T(8,128)(2,1)S(1)} %get-tuple-element.906), channel_id=1, source_target_pairs={{7,0},{0,1},{1,2},{2,3},{3,4},{4,5},{5,6},{6,7},{15,8},{8,9},{9,10... | collective-permute-start | bytes 196616 | tf_op jit(solution)/shard_map/while/body/eval_jaxpr/ppermute | solution.py:17
  110.1 6.2 %collective-permute-start = (bf16[256,128]{1,0:T(8,128)(2,1)S(1)}, bf16[256,128]{1,0:T(8,128)(2,1)S(1)}, u32[]{:S(2)}, u32[]{:S(2)}) collective-permute-start(bf16[256,128]{1,0:T(8,128)(2,1)S(1)} %get-tuple-element.905), channel_id=1, source_target_pairs={{7,0},{0,1},{1,2},{2,3},{3,4},{4,5},{5,6},{6,7},{15,8},{8,9},{9,10... | collective-permute-start | bytes 196616 | tf_op jit(solution)/shard_map/while/body/eval_jaxpr/ppermute | solution.py:17
  116.6 5.5 %collective-permute-start.1 = (bf16[256,128]{1,0:T(8,128)(2,1)S(1)}, bf16[256,128]{1,0:T(8,128)(2,1)S(1)}, u32[]{:S(2)}, u32[]{:S(2)}) collective-permute-start(bf16[256,128]{1,0:T(8,128)(2,1)S(1)} %get-tuple-element.906), channel_id=1, source_target_pairs={{7,0},{0,1},{1,2},{2,3},{3,4},{4,5},{5,6},{6,7},{15,8},{8,9},{9,10... | collective-permute-start | bytes 196616 | tf_op jit(solution)/shard_map/while/body/eval_jaxpr/ppermute | solution.py:17
  116.6 6.2 %collective-permute-start = (bf16[256,128]{1,0:T(8,128)(2,1)S(1)}, bf16[256,128]{1,0:T(8,128)(2,1)S(1)}, u32[]{:S(2)}, u32[]{:S(2)}) collective-permute-start(bf16[256,128]{1,0:T(8,128)(2,1)S(1)} %get-tuple-element.905), channel_id=1, source_target_pairs={{7,0},{0,1},{1,2},{2,3},{3,4},{4,5},{5,6},{6,7},{15,8},{8,9},{9,10... | collective-permute-start | bytes 196616 | tf_op jit(solution)/shard_map/while/body/eval_jaxpr/ppermute | solution.py:17
  123.1 5.5 %collective-permute-start.3 = (bf16[256,128]{1,0:T(8,128)(2,1)S(1)}, bf16[256,128]{1,0:T(8,128)(2,1)S(1)}, u32[]{:S(2)}, u32[]{:S(2)}) collective-permute-start(bf16[256,128]{1,0:T(8,128)(2,1)S(1)} %get-tuple-element.588), channel_id=1, source_target_pairs={{7,0},{0,1},{1,2},{2,3},{3,4},{4,5},{5,6},{6,7},{15,8},{8,9},{9,10... | collective-permute-start | bytes 196616 | tf_op jit(solution)/shard_map/ppermute | solution.py:17
  123.2 10.4 %collective-permute-start.2 = (bf16[256,128]{1,0:T(8,128)(2,1)S(1)}, bf16[256,128]{1,0:T(8,128)(2,1)S(1)}, u32[]{:S(2)}, u32[]{:S(2)}) collective-permute-start(bf16[256,128]{1,0:T(8,128)(2,1)S(1)} %get-tuple-element.587), channel_id=1, source_target_pairs={{7,0},{0,1},{1,2},{2,3},{3,4},{4,5},{5,6},{6,7},{15,8},{8,9},{9,10... | collective-permute-start | bytes 196616 | tf_op jit(solution)/shard_map/ppermute | solution.py:17
  129.3 9.0 %all-to-all-start.7 = ((bf16[2,128,128]{2,0,1:T(2,128)(2,1)}), bf16[2,128,128]{2,0,1:T(2,128)(2,1)S(1)}, u32[]{:S(2)}, u32[]{:S(2)}) async-start(bf16[2,128,128]{2,0,1:T(2,128)(2,1)} %copy.76), calls=%async_computation.7 | async-start | bytes 131072 | tf_op jit(solution)/shard_map/all_to_all | solution.py:190
  138.4 8.2 %all-to-all-start.6 = ((bf16[2,128,128]{2,0,1:T(2,128)(2,1)}), bf16[2,128,128]{2,0,1:T(2,128)(2,1)S(1)}, u32[]{:S(2)}, u32[]{:S(2)}) async-start(bf16[2,128,128]{2,0,1:T(2,128)(2,1)} %copy.73), calls=%async_computation.6 | async-start | bytes 131072 | tf_op jit(solution)/shard_map/all_to_all | solution.py:187
  146.6 9.7 %all-to-all-start.3 = ((bf16[2,128,512]{2,0,1:T(2,128)(2,1)}), bf16[2,128,512]{2,0,1:T(2,128)(2,1)S(1)}, u32[]{:S(2)}, u32[]{:S(2)}) async-start(bf16[2,128,512]{2,0,1:T(2,128)(2,1)} %copy.65), calls=%async_computation.3 | async-start | bytes 524288 | tf_op jit(solution)/shard_map/all_to_all | solution.py:177
  156.3 8.8 %all-to-all-start.5 = ((bf16[2,128,512]{2,0,1:T(2,128)(2,1)}), bf16[2,128,512]{2,0,1:T(2,128)(2,1)S(1)}, u32[]{:S(2)}, u32[]{:S(2)}) async-start(bf16[2,128,512]{2,0,1:T(2,128)(2,1)} %copy.70), calls=%async_computation.5 | async-start | bytes 524288 | tf_op jit(solution)/shard_map/all_to_all | solution.py:184
where the time goes:
time: 167 us; the launch traced here: 166 us
  waiting for transfers between devices  52.9 us (32%)
  starting transfers between devices  33.7 us (20%)
  blocking collectives  30.3 us (18%)
  local copies, waits for them, and re-layouts  23.7 us (14%)
  matrix products  17.9 us (11%)
  other arithmetic  5.33 us (3%)
    ppermute x16, waiting for transfers between devices, from_behind(): return lax.ppermute(block, axis, route)  34.7 us
    all_gather x1, blocking collectives, shards(): lax.all_gather(key_rows, 'ctx', axis=0, tiled=True)  15.4 us
    all_gather x1, blocking collectives, shards(): lax.all_gather(value_rows, 'ctx', axis=0, tiled=True)  14.8 us
    unnamed x22, local copies, waits for them, and re-layouts  10.6 us
    dot_general x20, matrix products, contract_rows(): lax.dot_general(left_side, right_side, (((1,), (1,)), ((), ())), preferre...  7.22 us
    all_to_all x1, starting transfers between devices, shards(): lax.all_to_all(widen(value_vectors), 'head', split_axis=2, concat_axis=1,...  5.29 us
    all_to_all x1, waiting for transfers between devices, shards(): lax.all_to_all(attended_wide.reshape(halves, block_len, per_row * HD).ast...  5.11 us
    dot_general x16, matrix products, contract_cols(): lax.dot_general(left_side, right_side, (((0,), (0,)), ((), ())), preferre...  4.56 us
  transfers between devices with their start and end apart: 24, of which 20 were waited for; matrix products, arithmetic and copies ran while one was open for 22% of the time, Pallas kernels for 0%

commit v1 on v0

v1 whole, which is shorter than its diff:
```python
import functools
import math

import jax
import jax.numpy as jnp
from jax import lax
from jax.experimental import pallas as pl
from jax.experimental.pallas import tpu as pltpu
from jax.sharding import PartitionSpec as P

HD = 128
BF = jnp.bfloat16
F32 = jnp.float32
LOWEST = -1e30
LANES = 256


def params(*arrays_bytes):
    limit = int(sum(arrays_bytes)) + (12 << 20)
    return pltpu.CompilerParams(vmem_limit_bytes=min(limit, 60 << 20))


def nbytes(*shapes):
    return sum(math.prod(s.shape) * s.dtype.itemsize for s in shapes)


VMEM = pl.BlockSpec(memory_space=pltpu.VMEM)
SMEM = pl.BlockSpec(memory_space=pltpu.SMEM)


def swap(block, axis, mask):
    size = lax.axis_size(axis)
    return lax.ppermute(block, axis, [(i, i ^ mask) for i in range(size)])


def pack_kv_kernel(kv, key_ref, value_ref, out_ref):
    for dest in range(out_ref.shape[0]):
        cols = pl.ds((dest % kv) * HD, HD)
        out_ref[dest, :, :HD] = key_ref[:, cols]
        out_ref[dest, :, HD:] = value_ref[:, cols]


def pack_q_kernel(kv, core_ref, query_ref, grad_ref, keep_ref, send_ref):
    width = keep_ref.shape[2]
    for core in range(kv):

        @pl.when(core_ref[0] == core)
        def _():
            mine = pl.ds(core * width, width)
            keep_ref[0] = query_ref[:, mine]
            keep_ref[1] = grad_ref[:, mine]
            for step in range(1, kv):
                theirs = pl.ds((core ^ step) * width, width)
                send_ref[step - 1, 0] = query_ref[:, theirs]
                send_ref[step - 1, 1] = grad_ref[:, theirs]


def attend_kernel(
    kv,
    block_len,
    block_rows,
    tile_rows,
    heads,
    chunks,
    order_ref,
    place_ref,
    *refs,
):
    keep_ref, recv_ref = refs[0], refs[1]
    kv_refs = refs[2 : 2 + chunks]
    out_keep, out_send = refs[2 + chunks], refs[3 + chunks]
    dkv_refs = refs[4 + chunks : 4 + 2 * chunks]
    q_all, do_all, e_ref, p_ref, ds_ref = refs[4 + 2 * chunks :]
    rows = keep_ref.shape[1]
    ctx_size = kv_refs[0].shape[0]
    chunk_keys = ctx_size * rows
    blocks_here = rows // block_rows
    lanes = heads * tile_rows
    scaling = 1.0 / math.sqrt(HD)
    expo = scaling * math.log2(math.e)
    head_place = place_ref[0]
    pair_start = place_ref[1]
    core = place_ref[2]

    def part_q(step):
        return keep_ref if step == 0 else recv_ref.at[step - 1]

    def part_out(step):
        return out_keep if step == 0 else out_send.at[step - 1]

    lane_row = lax.broadcasted_iota(jnp.int32, (1, lanes), 1) % tile_rows
    key_iota = lax.broadcasted_iota(jnp.int32, (block_rows, lanes), 0)
    tiles = [(step, start) for step in range(kv) for start in range(0, rows, tile_rows)]
    for tile, (step, start) in enumerate(tiles):
        source = part_q(step)
        span = pl.ds(start, tile_rows)
        out_span = pl.ds(tile * lanes, lanes)
        for n in range(heads):
            at = pl.ds(tile * lanes + n * tile_rows, tile_rows)
            q_all[at, :] = source[0, span, pl.ds(n * HD, HD)]
            do_all[at, :] = source[1, span, pl.ds(n * HD, HD)]
        q = q_all[out_span, :]
        do = do_all[out_span, :]
        source_ctx = pair_start + (core ^ step)
        query_pos = jnp.zeros((1, lanes), jnp.int32)
        for b in range(start // block_rows, -(-(start + tile_rows) // block_rows)):
            block_pos = order_ref[source_ctx * blocks_here + b] * block_len + head_place * block_rows
            here = (lane_row + start) // block_rows == b
            query_pos = jnp.where(here, block_pos + (lane_row + start) % block_rows, query_pos)
        gap = query_pos - key_iota
        row_max = jnp.full((8, lanes), LOWEST, F32)
        for m in range(chunks):
            keys = kv_refs[m][:, :, :HD].reshape(chunk_keys, HD)
            scores = lax.dot_general(keys, q, (((1,), (1,)), ((), ())), preferred_element_type=F32)
            chunk_head = head_place ^ m
            for j in range(chunk_keys // block_rows):
                key_pos = order_ref[j] * block_len + chunk_head * block_rows
                part = scores[j * block_rows : (j + 1) * block_rows]
                part = jnp.where(gap >= key_pos, part, LOWEST)
                e_ref[pl.ds(m * chunk_keys + j * block_rows, block_rows), :] = part
                row_max = jnp.maximum(row_max, jnp.max(part.reshape(block_rows // 8, 8, lanes), axis=0))
        top = jnp.max(row_max, axis=0, keepdims=True) * expo
        row_sum = jnp.zeros((8, lanes), F32)
        for m in range(chunks):
            span_keys = pl.ds(m * chunk_keys, chunk_keys)
            part = jnp.exp2(e_ref[span_keys, :] * expo - top)
            e_ref[span_keys, :] = part
            row_sum = row_sum + jnp.sum(part.reshape(chunk_keys // 8, 8, lanes), axis=0)
        inverse = 1.0 / jnp.sum(row_sum, axis=0, keepdims=True)
        mixed = jnp.zeros((HD, lanes), F32)
        for m in range(chunks):
            span_keys = pl.ds(m * chunk_keys, chunk_keys)
            probs = (e_ref[span_keys, :] * inverse).astype(BF)
            p_ref[span_keys, out_span] = probs
            values = kv_refs[m][:, :, HD:].reshape(chunk_keys, HD)
            mixed = mixed + lax.dot_general(
                values, probs, (((0,), (0,)), ((), ())), preferred_element_type=F32
            )
        attended = mixed.T.astype(BF)
        for n in range(heads):
            part_out(step)[0, span, pl.ds(n * HD, HD)] = attended[n * tile_rows : (n + 1) * tile_rows]
        delta = jnp.sum(
            do.astype(F32).T * mixed.astype(BF).astype(F32), axis=0, keepdims=True
        )
        q_grad = jnp.zeros((HD, lanes), F32)
        for m in range(chunks):
            span_keys = pl.ds(m * chunk_keys, chunk_keys)
            values = kv_refs[m][:, :, HD:].reshape(chunk_keys, HD)
            keys = kv_refs[m][:, :, :HD].reshape(chunk_keys, HD)
            grad_w = lax.dot_general(values, do, (((1,), (1,)), ((), ())), preferred_element_type=F32)
            grad_s = ((e_ref[span_keys, :] * inverse) * (grad_w - delta)).astype(BF)
            ds_ref[span_keys, out_span] = grad_s
            q_grad = q_grad + lax.dot_general(
                keys, grad_s, (((0,), (0,)), ((), ())), preferred_element_type=F32
            )
        q_grad = (q_grad.T * scaling).astype(BF)
        for n in range(heads):
            part_out(step)[1, span, pl.ds(n * HD, HD)] = q_grad[n * tile_rows : (n + 1) * tile_rows]
    for m in range(chunks):
        span_keys = pl.ds(m * chunk_keys, chunk_keys)
        k_grad = jnp.dot(ds_ref[span_keys, :], q_all[...], preferred_element_type=F32)
        v_grad = jnp.dot(p_ref[span_keys, :], do_all[...], preferred_element_type=F32)
        dkv_refs[m][:, :, :HD] = k_grad.astype(BF).reshape(ctx_size, rows, HD)
        dkv_refs[m][:, :, HD:] = v_grad.astype(BF).reshape(ctx_size, rows, HD)


def sum_kernel(*refs):
    total = refs[0][...].astype(F32)
    for ref in refs[1:-1]:
        total = total + ref[...].astype(F32)
    refs[-1][...] = total.astype(BF)


def finish_kv_kernel(kv, scaling, parts_ref, key_ref, value_ref):
    for g in range(kv):
        total = parts_ref[g].astype(F32)
        for source in range(g + kv, parts_ref.shape[0], kv):
            total = total + parts_ref[source].astype(F32)
        cols = pl.ds(g * HD, HD)
        key_ref[:, cols] = (total[:, :HD] * scaling).astype(BF)
        value_ref[:, cols] = total[:, HD:].astype(BF)


def finish_q_kernel(kv, core_ref, keep_ref, recv_ref, att_ref, grad_ref):
    width = keep_ref.shape[2]
    for core in range(kv):

        @pl.when(core_ref[0] == core)
        def _():
            mine = pl.ds(core * width, width)
            att_ref[:, mine] = keep_ref[0]
            grad_ref[:, mine] = keep_ref[1]
            for step in range(1, kv):
                theirs = pl.ds((core ^ step) * width, width)
                att_ref[:, theirs] = recv_ref[step - 1, 0]
                grad_ref[:, theirs] = recv_ref[step - 1, 1]


def call(kernel, ins, specs, outs, scratch=(), scratch_bytes=0, cost=None, name=None):
    out_specs = [VMEM] * len(outs)
    single = len(outs) == 1
    return pl.pallas_call(
        kernel,
        out_shape=outs[0] if single else tuple(outs),
        in_specs=specs,
        out_specs=out_specs[0] if single else tuple(out_specs),
        scratch_shapes=list(scratch),
        compiler_params=params(nbytes(*ins), nbytes(*outs), scratch_bytes),
        cost_estimate=cost,
        name=name,
    )(*ins)


def shards(queries, key_vectors, value_vectors, out_grad, block_order):
    heads_devices = lax.axis_size("head")
    ctx_devices = lax.axis_size("ctx")
    halves, block_rows, query_width = queries.shape
    kv = key_vectors.shape[2] // HD
    rows = halves * block_rows
    width = query_width // kv
    group = width // HD
    block_len = block_rows * heads_devices
    ctx = lax.axis_index("ctx").astype(jnp.int32)
    core = (ctx % kv).reshape(1)
    place = jnp.stack([lax.axis_index("head").astype(jnp.int32), ctx - ctx % kv, ctx % kv])
    queries = queries.reshape(rows, query_width)
    out_grad = out_grad.reshape(rows, query_width)
    key_vectors = key_vectors.reshape(rows, kv * HD)
    value_vectors = value_vectors.reshape(rows, kv * HD)

    def shape(*dims):
        return jax.ShapeDtypeStruct(dims, BF)

    kv_send = call(
        functools.partial(pack_kv_kernel, kv),
        (key_vectors, value_vectors),
        [VMEM] * 2,
        [shape(ctx_devices, rows, 2 * HD)],
        name="pack_kv",
    )
    kv_own = lax.all_to_all(kv_send, "ctx", split_axis=0, concat_axis=0, tiled=True)
    keep, send = call(
        functools.partial(pack_q_kernel, kv),
        (core, queries, out_grad),
        [SMEM, VMEM, VMEM],
        [shape(2, rows, width), shape(kv - 1, 2, rows, width)],
        name="pack_q",
    )
    recv = jnp.stack([swap(send[step - 1], "ctx", step) for step in range(1, kv)])
    kv_parts = [kv_own] + [swap(kv_own, "head", m) for m in range(1, heads_devices)]

    tile_rows = block_rows if block_rows % 16 == 0 else rows
    lanes = group * tile_rows
    keys = heads_devices * ctx_devices * rows
    query_rows = kv * group * rows
    scratch = [
        pltpu.VMEM((query_rows, HD), BF),
        pltpu.VMEM((query_rows, HD), BF),
        pltpu.VMEM((keys, lanes), F32),
        pltpu.VMEM((keys, query_rows), BF),
        pltpu.VMEM((keys, query_rows), BF),
    ]
    outs = call(
        functools.partial(
            attend_kernel, kv, block_len, block_rows, tile_rows, group, heads_devices
        ),
        (block_order, place, keep, recv, *kv_parts),
        [SMEM, SMEM] + [VMEM] * (2 + heads_devices),
        [shape(2, rows, width), shape(kv - 1, 2, rows, width)]
        + [shape(ctx_devices, rows, 2 * HD)] * heads_devices,
        scratch,
        4 * query_rows * HD + keys * (4 * lanes + 4 * query_rows),
        name="attend",
    )
    out_keep, out_send = outs[0], outs[1]
    dkv = outs[2:]
    dkv_parts = [dkv[0]] + [swap(dkv[m], "head", m) for m in range(1, heads_devices)]
    out_recv = jnp.stack([swap(out_send[step - 1], "ctx", step) for step in range(1, kv)])
    dkv_sum = call(
        sum_kernel,
        tuple(dkv_parts),
        [VMEM] * heads_devices,
        [shape(ctx_devices, rows, 2 * HD)],
        name="sum_heads",
    )
    dkv_back = lax.all_to_all(dkv_sum, "ctx", split_axis=0, concat_axis=0, tiled=True)
    attended, query_grad = call(
        functools.partial(finish_q_kernel, kv),
        (core, out_keep, out_recv),
        [SMEM, VMEM, VMEM],
        [shape(rows, query_width)] * 2,
        name="finish_q",
    )
    key_grad, value_grad = call(
        functools.partial(finish_kv_kernel, kv, 1.0 / math.sqrt(HD)),
        (dkv_back,),
        [VMEM],
        [shape(rows, kv * HD)] * 2,
        name="finish_kv",
    )
    return (
        attended.reshape(halves, block_rows, query_width),
        query_grad.reshape(halves, block_rows, query_width),
        key_grad.reshape(halves, block_rows, kv * HD),
        value_grad.reshape(halves, block_rows, kv * HD),
    )


def solution(mesh):
    split = P("ctx", "head", None)
    return jax.shard_map(
        shards,
        mesh=mesh,
        in_specs=(split, split, split, split, P()),
        out_specs=(split, split, split, split),
        check_vma=False,
    )
```

time: 167 us -> 74.4 us (0.45)
  blocking collectives: 30.3 us -> 0 us
  local copies, waits for them, and re-layouts: 23.7 us -> 2.17 us
  matrix products: 17.9 us -> 0 us
  starting transfers between devices: 33.7 us -> 17.9 us
  Pallas kernels: 0 us -> 13.4 us
  waiting for transfers between devices: 52.9 us -> 39.7 us
  other arithmetic: 5.33 us -> 0.08 us
    all_gather x2 -> x0, blocking collectives: 30.3 us -> none  [the longest x1 15.4 us: shards(): lax.all_gather(key_rows, 'ctx', axis=0, tiled=True)]
    all_to_all x8 -> x2, starting transfers between devices: 31.3 us -> 9.87 us  [the longest x1 6.46 us: shards(): lax.all_to_all(kv_send, 'ctx', split_axis=0, concat_axis=0, tiled=True)]
    dot_general x48 -> x0, matrix products: 17.9 us -> none  [the longest x20 7.22 us: contract_rows(): lax.dot_general(left_side, right_side, (((1,), (1,)), ((), ())), preferre...]
    pallas_call x0 -> x6, Pallas kernels: none -> 13.4 us  [call(): pl.pallas_call(kernel, out_shape=outs[0] if single else tuple(outs), in_s...]
    ppermute x16 -> x8, waiting for transfers between devices: 34.7 us -> 23.4 us  [swap(): return lax.ppermute(block, axis, [(i, i ^ mask) for i in range(size)])]
    unnamed x22 -> x10, local copies, waits for them, and re-layouts: 10.6 us -> 2.17 us
    ppermute x16 -> x8, starting transfers between devices: 2.43 us -> 8.01 us  [swap(): return lax.ppermute(block, axis, [(i, i ^ mask) for i in range(size)])]
    convert_element_type x8 -> x0, local copies, waits for them, and re-layouts: 4.95 us -> none  [the longest x2 1.14 us: shards(): attended_wide.reshape(halves, block_len, per_row * HD).astype(jnp.bfloat16)]
  transfers between devices with their start and end apart: 24 -> 10, of which waited for: 20 -> 8; matrix products, arithmetic and copies ran while one was open for 22% -> 0% of each run, Pallas kernels for 0% -> 1%
where the time goes in v1:
time: 74.4 us; the launch traced here: 74 us
  waiting for transfers between devices  39.7 us (53%)
  starting transfers between devices  17.9 us (24%)
  Pallas kernels  13.4 us (18%)
  local copies, waits for them, and re-layouts  2.17 us (3%)
    ppermute x8, waiting for transfers between devices, swap(): return lax.ppermute(block, axis, [(i, i ^ mask) for i in range(size)])  23.4 us
    pallas_call x6, Pallas kernels, call(): pl.pallas_call(kernel, out_shape=outs[0] if single else tuple(outs), in_s...  13.4 us
    all_to_all x1, waiting for transfers between devices, shards(): lax.all_to_all(kv_send, 'ctx', split_axis=0, concat_axis=0, tiled=True)  9.11 us
    ppermute x8, starting transfers between devices, swap(): return lax.ppermute(block, axis, [(i, i ^ mask) for i in range(size)])  8.01 us
    all_to_all x1, waiting for transfers between devices, shards(): lax.all_to_all(dkv_sum, 'ctx', split_axis=0, concat_axis=0, tiled=True)  7.23 us
    all_to_all x1, starting transfers between devices, shards(): lax.all_to_all(kv_send, 'ctx', split_axis=0, concat_axis=0, tiled=True)  6.46 us
    all_to_all x1, starting transfers between devices, shards(): lax.all_to_all(dkv_sum, 'ctx', split_axis=0, concat_axis=0, tiled=True)  3.41 us
    unnamed x10, local copies, waits for them, and re-layouts  2.17 us
  transfers between devices with their start and end apart: 10, of which 8 were waited for; matrix products, arithmetic and copies ran while one was open for 0% of the time, Pallas kernels for 1%

profile of v1, /device:TPU:0, one launch (start us, length us, event | category | flops | bytes accessed | tf_op | source)
XLA Modules:
  0.0 74.0 jit_solution(10534191040911603422)
XLA Ops:
  0.6 0.0 copy-start.2
  0.6 0.7 %copy-done.2 = bf16[2,32,256]{2,1,0:T(8,128)(2,1)S(1)} copy-done((bf16[2,32,256]{2,1,0:T(8,128)(2,1)S(1)}, bf16[2,32,256]{2,1,0:T(8,128)(2,1)}, u32[]{:S(2)}) %copy-start.2) | copy-done | bytes 32792
  1.4 0.0 copy-start.3
  1.4 0.8 %copy-done.3 = bf16[2,32,256]{2,1,0:T(8,128)(2,1)S(1)} copy-done((bf16[2,32,256]{2,1,0:T(8,128)(2,1)S(1)}, bf16[2,32,256]{2,1,0:T(8,128)(2,1)}, u32[]{:S(2)}) %copy-start.3) | copy-done | bytes 32792
  2.1 0.7 pack_kv.1
  2.9 0.0 copy-start
  2.9 0.0 copy-start.1
  2.9 6.5 %all-to-all-start = ((bf16[8,64,256]{2,1,0:T(8,128)(2,1)}), bf16[8,64,256]{2,1,0:T(8,128)(2,1)S(1)}, u32[]{:S(2)}, u32[]{:S(2)}) async-start(bf16[8,64,256]{2,1,0:T(8,128)(2,1)} %pack_kv.1), calls=%async_computation | async-start | bytes 524288 | tf_op jit(solution)/shard_map/all_to_all | solution.py:241
  9.3 0.0 copy-done
  9.4 0.0 copy-done.1
  9.4 0.6 collective-permute-start
  10.0 9.1 %all-to-all-done.refs_2_ = bf16[8,64,256]{2,1,0:T(8,128)(2,1)S(1)} async-done(((bf16[8,64,256]{2,1,0:T(8,128)(2,1)}), bf16[8,64,256]{2,1,0:T(8,128)(2,1)S(1)}, u32[]{:S(2)}, u32[]{:S(2)}) %all-to-all-start) | async-done | bytes 262176 | tf_op jit(solution)/shard_map/all_to_all | solution.py:241
  19.1 2.4 %collective-permute-start.3 = (bf16[8,64,256]{2,1,0:T(8,128)(2,1)S(1)}, bf16[8,64,256]{2,1,0:T(8,128)(2,1)S(1)}, u32[]{:S(2)}, u32[]{:S(2)}) collective-permute-start(bf16[8,64,256]{2,1,0:T(8,128)(2,1)S(1)} %all-to-all-done.refs_2_), channel_id=1, source_target_pairs={{0,24},{8,16},{16,8},{24,0},{1,25},{9,17},{17,9},{25,1},{2,26},{10... | collective-permute-start | bytes 786440 | tf_op jit(solution)/shard_map/ppermute | solution.py:33
  21.5 0.5 collective-permute-start.2
  22.0 0.5 collective-permute-start.1
  22.6 0.1 pad_add_fusion.place_ref
  22.7 0.0 collective-permute-done
  22.7 6.6 %collective-permute-done.3.refs_5_ = bf16[8,64,256]{2,1,0:T(8,128)(2,1)S(1)} collective-permute-done((bf16[8,64,256]{2,1,0:T(8,128)(2,1)S(1)}, bf16[8,64,256]{2,1,0:T(8,128)(2,1)S(1)}, u32[]{:S(2)}, u32[]{:S(2)}) %collective-permute-start.3) | collective-permute-done | bytes 262176 | tf_op jit(solution)/shard_map/ppermute | solution.py:33
  29.3 4.0 %collective-permute-done.2.refs_4_ = bf16[8,64,256]{2,1,0:T(8,128)(2,1)S(1)} collective-permute-done((bf16[8,64,256]{2,1,0:T(8,128)(2,1)S(1)}, bf16[8,64,256]{2,1,0:T(8,128)(2,1)S(1)}, u32[]{:S(2)}, u32[]{:S(2)}) %collective-permute-start.2) | collective-permute-done | bytes 262176 | tf_op jit(solution)/shard_map/ppermute | solution.py:33
  33.3 0.1 collective-permute-done.1.refs_3_
  33.4 0.0 copy-start.4
  33.4 0.7 copy-done.4
  34.0 10.3 %attend.1 = (bf16[2,64,1024]{2,1,0:T(8,128)(2,1)S(1)}, bf16[1,2,64,1024]{3,2,1,0:T(8,128)(2,1)S(1)}, bf16[8,64,256]{2,1,0:T(8,128)(2,1)S(1)}, bf16[8,64,256]{2,1...) custom-call(s32[16]{0:T(128)S(1)} %copy-done.4, s32[3]{0:T(128)S(1)} %pad_add_fusion.place_ref, ...), custom_call_target="tpu_custom_call" | custom-call | tf_op jit(solution)/shard_map/attend/pallas_call | solution.py:202
  44.4 1.6 %collective-permute-start.5 = (bf16[8,64,256]{2,1,0:T(8,128)(2,1)S(1)}, bf16[8,64,256]{2,1,0:T(8,128)(2,1)S(1)}, u32[]{:S(2)}, u32[]{:S(2)}) collective-permute-start(bf16[8,64,256]{2,1,0:T(8,128)(2,1)S(1)} %get-tuple-element.23), channel_id=1, source_target_pairs={{0,8},{8,0},{16,24},{24,16},{1,9},{9,1},{17,25},{25,17},{2,10},{10... | collective-permute-start | bytes 786440 | tf_op jit(solution)/shard_map/ppermute | solution.py:33
  45.9 0.7 collective-permute-start.6
  46.6 1.3 %collective-permute-start.7 = (bf16[8,64,256]{2,1,0:T(8,128)(2,1)S(1)}, bf16[8,64,256]{2,1,0:T(8,128)(2,1)S(1)}, u32[]{:S(2)}, u32[]{:S(2)}) collective-permute-start(bf16[8,64,256]{2,1,0:T(8,128)(2,1)S(1)} %get-tuple-element.25), channel_id=1, source_target_pairs={{0,24},{8,16},{16,8},{24,0},{1,25},{9,17},{17,9},{25,1},{2,26},{10... | collective-permute-start | bytes 786440 | tf_op jit(solution)/shard_map/ppermute | solution.py:33
  47.9 5.7 %collective-permute-done.5.refs_1_ = bf16[8,64,256]{2,1,0:T(8,128)(2,1)S(1)} collective-permute-done((bf16[8,64,256]{2,1,0:T(8,128)(2,1)S(1)}, bf16[8,64,256]{2,1,0:T(8,128)(2,1)S(1)}, u32[]{:S(2)}, u32[]{:S(2)}) %collective-permute-start.5) | collective-permute-done | bytes 262176 | tf_op jit(solution)/shard_map/ppermute | solution.py:33
  53.6 5.8 %collective-permute-done.6.refs_2_ = bf16[8,64,256]{2,1,0:T(8,128)(2,1)S(1)} collective-permute-done((bf16[8,64,256]{2,1,0:T(8,128)(2,1)S(1)}, bf16[8,64,256]{2,1,0:T(8,128)(2,1)S(1)}, u32[]{:S(2)}, u32[]{:S(2)}) %collective-permute-start.6) | collective-permute-done | bytes 262176 | tf_op jit(solution)/shard_map/ppermute | solution.py:33
  59.4 0.0 collective-permute-done.7.refs_3_
  59.4 0.8 %sum_heads.1 = bf16[8,64,256]{2,1,0:T(8,128)(2,1)} custom-call(bf16[8,64,256]{2,1,0:T(8,128)(2,1)S(1)} %get-tuple-element.22.refs_0_, bf16[8,64,256]{2,1,0:T(8,128)(2,1)S(1)} %collective-permute-done.5.refs_1_, bf16[8,64,256]{2,1,0:T(8,128)(2,1)S(1)} %collective-permute-done.6.refs_2_, bf16[8,64,256]{2,1,0:T(8,128)(2,1)S(1)} %collective-permute-done.7.refs_3_), custom_call_target="tpu_custom_call" | custom-call | tf_op jit(solution)/shard_map/sum_heads/pallas_call | solution.py:202
  60.2 3.4 %all-to-all-start.1 = ((bf16[8,64,256]{2,1,0:T(8,128)(2,1)}), bf16[8,64,256]{2,1,0:T(8,128)(2,1)S(1)}, u32[]{:S(2)}, u32[]{:S(2)}) async-start(bf16[8,64,256]{2,1,0:T(8,128)(2,1)} %sum_heads.1), calls=%async_computation.1 | async-start | bytes 524288 | tf_op jit(solution)/shard_map/all_to_all | solution.py:286
  63.6 0.4 collective-permute-start.4
  64.0 1.2 %collective-permute-done.4 = bf16[2,64,1024]{2,1,0:T(8,128)(2,1)S(1)} collective-permute-done((bf16[2,64,1024]{2,1,0:T(8,128)(2,1)S(1)}, bf16[2,64,1024]{2,1,0:T(8,128)(2,1)S(1)}, u32[]{:S(2)}, u32[]{:S(2)}) %collective-permute-start.4) | collective-permute-done | bytes 262176 | tf_op jit(solution)/shard_map/ppermute | solution.py:33
  65.2 0.8 %finish_q.1 = (bf16[64,2048]{1,0:T(8,128)(2,1)}, bf16[64,2048]{1,0:T(8,128)(2,1)}) custom-call(s32[1]{0:T(128)} %bitcast.core_ref, bf16[2,64,1024]{2,1,0:T(8,128)(2,1)S(1)} %get-tuple-element.18.keep_ref, bf16[1,2,64,1024]{3,2,1,0:T(8,128)(2,1)S(1)} %bitcast.17), custom_call_target="tpu_custom_call" | custom-call | tf_op jit(solution)/shard_map/finish_q/pallas_call | solution.py:202
  66.1 7.2 %all-to-all-done.1.parts_ref = bf16[8,64,256]{2,1,0:T(8,128)(2,1)S(1)} async-done(((bf16[8,64,256]{2,1,0:T(8,128)(2,1)}), bf16[8,64,256]{2,1,0:T(8,128)(2,1)S(1)}, u32[]{:S(2)}, u32[]{:S(2)}) %all-to-all-start.1) | async-done | bytes 262176 | tf_op jit(solution)/shard_map/all_to_all | solution.py:286
  73.3 0.7 finish_kv.1
  (1 shorter events, 0.0 us)
Async XLA Ops:
  0.6 0.8 %copy-start.2 = (bf16[2,32,256]{2,1,0:T(8,128)(2,1)S(1)}, bf16[2,32,256]{2,1,0:T(8,128)(2,1)}, u32[]{:S(2)}) copy-start(bf16[2,32,256]{2,1,0:T(8,128)(2,1)} %param.6) | copy-start | bytes 98308
  1.4 0.8 %copy-start.3 = (bf16[2,32,256]{2,1,0:T(8,128)(2,1)S(1)}, bf16[2,32,256]{2,1,0:T(8,128)(2,1)}, u32[]{:S(2)}) copy-start(bf16[2,32,256]{2,1,0:T(8,128)(2,1)} %param.7) | copy-start | bytes 98308
  2.9 6.5 %copy-start = (bf16[2,32,2048]{2,1,0:T(8,128)(2,1)S(1)}, bf16[2,32,2048]{2,1,0:T(8,128)(2,1)}, u32[]{:S(2)}) copy-start(bf16[2,32,2048]{2,1,0:T(8,128)(2,1)} %param.5) | copy-start | bytes 786436
  2.9 6.5 %copy-start.1 = (bf16[2,32,2048]{2,1,0:T(8,128)(2,1)S(1)}, bf16[2,32,2048]{2,1,0:T(8,128)(2,1)}, u32[]{:S(2)}) copy-start(bf16[2,32,2048]{2,1,0:T(8,128)(2,1)} %param.8) | copy-start | bytes 786436
  2.9 16.2 %all-to-all-start = ((bf16[8,64,256]{2,1,0:T(8,128)(2,1)}), bf16[8,64,256]{2,1,0:T(8,128)(2,1)S(1)}, u32[]{:S(2)}, u32[]{:S(2)}) async-start(bf16[8,64,256]{2,1,0:T(8,128)(2,1)} %pack_kv.1), calls=%async_computation | async-start | bytes 524288 | tf_op jit(solution)/shard_map/all_to_all | solution.py:241
  9.4 13.2 %collective-permute-start = (bf16[2,64,1024]{2,1,0:T(8,128)(2,1)S(1)}, bf16[2,64,1024]{2,1,0:T(8,128)(2,1)S(1)}, u32[]{:S(2)}, u32[]{:S(2)}) collective-permute-start(bf16[2,64,1024]{2,1,0:T(8,128)(2,1)S(1)} %bitcast.22), channel_id=1, source_target_pairs={{0,1},{1,0},{2,3},{3,2},{4,5},{5,4},{6,7},{7,6},{8,9},{9,8},{10,11... | collective-permute-start | bytes 786440 | tf_op jit(solution)/shard_map/ppermute | solution.py:33
  19.1 10.2 %collective-permute-start.3 = (bf16[8,64,256]{2,1,0:T(8,128)(2,1)S(1)}, bf16[8,64,256]{2,1,0:T(8,128)(2,1)S(1)}, u32[]{:S(2)}, u32[]{:S(2)}) collective-permute-start(bf16[8,64,256]{2,1,0:T(8,128)(2,1)S(1)} %all-to-all-done.refs_2_), channel_id=1, source_target_pairs={{0,24},{8,16},{16,8},{24,0},{1,25},{9,17},{17,9},{25,1},{2,26},{10... | collective-permute-start | bytes 786440 | tf_op jit(solution)/shard_map/ppermute | solution.py:33
  21.5 11.8 %collective-permute-start.2 = (bf16[8,64,256]{2,1,0:T(8,128)(2,1)S(1)}, bf16[8,64,256]{2,1,0:T(8,128)(2,1)S(1)}, u32[]{:S(2)}, u32[]{:S(2)}) collective-permute-start(bf16[8,64,256]{2,1,0:T(8,128)(2,1)S(1)} %all-to-all-done.refs_2_), channel_id=1, source_target_pairs={{0,16},{8,24},{16,0},{24,8},{1,17},{9,25},{17,1},{25,9},{2,18},{10... | collective-permute-start | bytes 786440 | tf_op jit(solution)/shard_map/ppermute | solution.py:33
  22.0 11.3 %collective-permute-start.1 = (bf16[8,64,256]{2,1,0:T(8,128)(2,1)S(1)}, bf16[8,64,256]{2,1,0:T(8,128)(2,1)S(1)}, u32[]{:S(2)}, u32[]{:S(2)}) collective-permute-start(bf16[8,64,256]{2,1,0:T(8,128)(2,1)S(1)} %all-to-all-done.refs_2_), channel_id=1, source_target_pairs={{0,8},{8,0},{16,24},{24,16},{1,9},{9,1},{17,25},{25,17},{2,10},{10... | collective-permute-start | bytes 786440 | tf_op jit(solution)/shard_map/ppermute | solution.py:33
  33.4 0.7 copy-start.4
  44.4 9.2 %collective-permute-start.5 = (bf16[8,64,256]{2,1,0:T(8,128)(2,1)S(1)}, bf16[8,64,256]{2,1,0:T(8,128)(2,1)S(1)}, u32[]{:S(2)}, u32[]{:S(2)}) collective-permute-start(bf16[8,64,256]{2,1,0:T(8,128)(2,1)S(1)} %get-tuple-element.23), channel_id=1, source_target_pairs={{0,8},{8,0},{16,24},{24,16},{1,9},{9,1},{17,25},{25,17},{2,10},{10... | collective-permute-start | bytes 786440 | tf_op jit(solution)/shard_map/ppermute | solution.py:33
  45.9 13.5 %collective-permute-start.6 = (bf16[8,64,256]{2,1,0:T(8,128)(2,1)S(1)}, bf16[8,64,256]{2,1,0:T(8,128)(2,1)S(1)}, u32[]{:S(2)}, u32[]{:S(2)}) collective-permute-start(bf16[8,64,256]{2,1,0:T(8,128)(2,1)S(1)} %get-tuple-element.24), channel_id=1, source_target_pairs={{0,16},{8,24},{16,0},{24,8},{1,17},{9,25},{17,1},{25,9},{2,18},{10... | collective-permute-start | bytes 786440 | tf_op jit(solution)/shard_map/ppermute | solution.py:33
  46.6 12.7 %collective-permute-start.7 = (bf16[8,64,256]{2,1,0:T(8,128)(2,1)S(1)}, bf16[8,64,256]{2,1,0:T(8,128)(2,1)S(1)}, u32[]{:S(2)}, u32[]{:S(2)}) collective-permute-start(bf16[8,64,256]{2,1,0:T(8,128)(2,1)S(1)} %get-tuple-element.25), channel_id=1, source_target_pairs={{0,24},{8,16},{16,8},{24,0},{1,25},{9,17},{17,9},{25,1},{2,26},{10... | collective-permute-start | bytes 786440 | tf_op jit(solution)/shard_map/ppermute | solution.py:33
  60.2 13.1 %all-to-all-start.1 = ((bf16[8,64,256]{2,1,0:T(8,128)(2,1)}), bf16[8,64,256]{2,1,0:T(8,128)(2,1)S(1)}, u32[]{:S(2)}, u32[]{:S(2)}) async-start(bf16[8,64,256]{2,1,0:T(8,128)(2,1)} %sum_heads.1), calls=%async_computation.1 | async-start | bytes 524288 | tf_op jit(solution)/shard_map/all_to_all | solution.py:286
  63.6 1.6 %collective-permute-start.4 = (bf16[2,64,1024]{2,1,0:T(8,128)(2,1)S(1)}, bf16[2,64,1024]{2,1,0:T(8,128)(2,1)S(1)}, u32[]{:S(2)}, u32[]{:S(2)}) collective-permute-start(bf16[2,64,1024]{2,1,0:T(8,128)(2,1)S(1)} %bitcast.21), channel_id=1, source_target_pairs={{0,1},{1,0},{2,3},{3,2},{4,5},{5,4},{6,7},{7,6},{8,9},{9,8},{10,11... | collective-permute-start | bytes 786440 | tf_op jit(solution)/shard_map/ppermute | solution.py:33

commit v2 on v1

v2 whole, which is shorter than its diff:
```python
import functools
import math

import jax
import jax.numpy as jnp
from jax import lax
from jax.experimental import pallas as pl
from jax.experimental.pallas import tpu as pltpu
from jax.sharding import PartitionSpec as P

HD = 128
BF = jnp.bfloat16
F32 = jnp.float32
LOWEST = -1e30
LANES = 256


def params(*arrays_bytes):
    limit = int(sum(arrays_bytes)) + (12 << 20)
    return pltpu.CompilerParams(vmem_limit_bytes=min(limit, 60 << 20))


def nbytes(*shapes):
    return sum(math.prod(s.shape) * s.dtype.itemsize for s in shapes)


VMEM = pl.BlockSpec(memory_space=pltpu.VMEM)
SMEM = pl.BlockSpec(memory_space=pltpu.SMEM)


def swap(block, axis, mask):
    size = lax.axis_size(axis)
    return lax.ppermute(block, axis, [(i, i ^ mask) for i in range(size)])


def pack_kv_kernel(kv, core_ref, *refs):
    out_ref = refs[-1]
    for core in range(kv):

        @pl.when(core_ref[0] == core)
        def _():
            cols = pl.ds(core * HD, HD)
            for step in range(kv):
                out_ref[step, :, :HD] = refs[2 * step][:, cols]
                out_ref[step, :, HD:] = refs[2 * step + 1][:, cols]


def attend_kernel(
    kv,
    block_len,
    block_rows,
    tile_rows,
    heads,
    chunks,
    order_ref,
    place_ref,
    *refs,
):
    q_refs, do_refs = refs[:kv], refs[kv : 2 * kv]
    refs = refs[2 * kv :]
    kv_refs, refs = refs[:chunks], refs[chunks:]
    out_refs, refs = refs[:kv], refs[kv:]
    dkv_refs, refs = refs[:chunks], refs[chunks:]
    q_all, do_all, e_ref, p_ref, ds_ref = refs
    rows = q_refs[0].shape[0]
    z_size = kv_refs[0].shape[0]
    chunk_keys = z_size * kv * rows
    blocks_here = rows // block_rows
    lanes = heads * tile_rows
    scaling = 1.0 / math.sqrt(HD)
    expo = scaling * math.log2(math.e)
    head_place = place_ref[0]
    z_place = place_ref[1]
    core = place_ref[2]
    first_col = core * (heads * HD)
    lane_row = lax.broadcasted_iota(jnp.int32, (1, lanes), 1) % tile_rows
    key_iota = lax.broadcasted_iota(jnp.int32, (block_rows, lanes), 0)
    tiles = [(step, start) for step in range(kv) for start in range(0, rows, tile_rows)]
    for tile, (step, start) in enumerate(tiles):
        span = pl.ds(start, tile_rows)
        out_span = pl.ds(tile * lanes, lanes)
        for n in range(heads):
            at = pl.ds(tile * lanes + n * tile_rows, tile_rows)
            cols = pl.ds(pl.multiple_of(first_col + n * HD, HD), HD)
            q_all[at, :] = q_refs[step][span, cols]
            do_all[at, :] = do_refs[step][span, cols]
        q = q_all[out_span, :]
        do = do_all[out_span, :]
        source_ctx = z_place * kv + (core ^ step)
        query_pos = jnp.zeros((1, lanes), jnp.int32)
        for b in range(start // block_rows, -(-(start + tile_rows) // block_rows)):
            block_pos = order_ref[source_ctx * blocks_here + b] * block_len + head_place * block_rows
            here = (lane_row + start) // block_rows == b
            query_pos = jnp.where(here, block_pos + (lane_row + start) % block_rows, query_pos)
        gap = query_pos - key_iota
        row_max = jnp.full((8, lanes), LOWEST, F32)
        for m in range(chunks):
            keys = kv_refs[m][:, :, :, :HD].reshape(chunk_keys, HD)
            scores = lax.dot_general(keys, q, (((1,), (1,)), ((), ())), preferred_element_type=F32)
            chunk_head = head_place ^ m
            for j in range(chunk_keys // block_rows):
                m_z, s_b = divmod(j, kv * blocks_here)
                s, b = divmod(s_b, blocks_here)
                stored = ((z_place ^ m_z) * kv + (core ^ s)) * blocks_here + b
                key_pos = order_ref[stored] * block_len + chunk_head * block_rows
                part = scores[j * block_rows : (j + 1) * block_rows]
                part = jnp.where(gap >= key_pos, part, LOWEST)
                e_ref[pl.ds(m * chunk_keys + j * block_rows, block_rows), :] = part
                row_max = jnp.maximum(row_max, jnp.max(part.reshape(block_rows // 8, 8, lanes), axis=0))
        top = jnp.max(row_max, axis=0, keepdims=True) * expo
        row_sum = jnp.zeros((8, lanes), F32)
        for m in range(chunks):
            span_keys = pl.ds(m * chunk_keys, chunk_keys)
            part = jnp.exp2(e_ref[span_keys, :] * expo - top)
            e_ref[span_keys, :] = part
            row_sum = row_sum + jnp.sum(part.reshape(chunk_keys // 8, 8, lanes), axis=0)
        inverse = 1.0 / jnp.sum(row_sum, axis=0, keepdims=True)
        mixed = jnp.zeros((HD, lanes), F32)
        for m in range(chunks):
            span_keys = pl.ds(m * chunk_keys, chunk_keys)
            probs = (e_ref[span_keys, :] * inverse).astype(BF)
            p_ref[span_keys, out_span] = probs
            values = kv_refs[m][:, :, :, HD:].reshape(chunk_keys, HD)
            mixed = mixed + lax.dot_general(
                values, probs, (((0,), (0,)), ((), ())), preferred_element_type=F32
            )
        attended = mixed.T.astype(BF)
        for n in range(heads):
            out_refs[step][0, span, pl.ds(n * HD, HD)] = attended[n * tile_rows : (n + 1) * tile_rows]
        delta = jnp.sum(
            do.astype(F32).T * mixed.astype(BF).astype(F32), axis=0, keepdims=True
        )
        q_grad = jnp.zeros((HD, lanes), F32)
        for m in range(chunks):
            span_keys = pl.ds(m * chunk_keys, chunk_keys)
            values = kv_refs[m][:, :, :, HD:].reshape(chunk_keys, HD)
            keys = kv_refs[m][:, :, :, :HD].reshape(chunk_keys, HD)
            grad_w = lax.dot_general(values, do, (((1,), (1,)), ((), ())), preferred_element_type=F32)
            grad_s = ((e_ref[span_keys, :] * inverse) * (grad_w - delta)).astype(BF)
            ds_ref[span_keys, out_span] = grad_s
            q_grad = q_grad + lax.dot_general(
                keys, grad_s, (((0,), (0,)), ((), ())), preferred_element_type=F32
            )
        q_grad = (q_grad.T * scaling).astype(BF)
        for n in range(heads):
            out_refs[step][1, span, pl.ds(n * HD, HD)] = q_grad[n * tile_rows : (n + 1) * tile_rows]
    for m in range(chunks):
        span_keys = pl.ds(m * chunk_keys, chunk_keys)
        k_grad = jnp.dot(ds_ref[span_keys, :], q_all[...], preferred_element_type=F32)
        v_grad = jnp.dot(p_ref[span_keys, :], do_all[...], preferred_element_type=F32)
        dkv_refs[m][:, :, :, :HD] = k_grad.astype(BF).reshape(z_size, kv, rows, HD)
        dkv_refs[m][:, :, :, HD:] = v_grad.astype(BF).reshape(z_size, kv, rows, HD)


def sum_heads_kernel(parts, *refs):
    for m_z, out_ref in enumerate(refs[parts:]):
        total = refs[0][m_z].astype(F32)
        for ref in refs[1:parts]:
            total = total + ref[m_z].astype(F32)
        out_ref[...] = total.astype(BF)


def sum_z_kernel(kv, *refs):
    ins, outs = refs[:-kv], refs[-kv:]
    for s, out_ref in enumerate(outs):
        total = ins[0][s].astype(F32)
        for ref in ins[1:]:
            total = total + ref[s].astype(F32)
        out_ref[...] = total.astype(BF)


def finish_kv_kernel(kv, scaling, core_ref, *refs):
    key_ref, value_ref = refs[kv:]
    for core in range(kv):

        @pl.when(core_ref[0] == core)
        def _():
            for s in range(kv):
                cols = pl.ds((core ^ s) * HD, HD)
                key_ref[:, cols] = (refs[s][:, :HD].astype(F32) * scaling).astype(BF)
                value_ref[:, cols] = refs[s][:, HD:]


def finish_q_kernel(kv, core_ref, *refs):
    att_ref, grad_ref = refs[kv:]
    width = refs[0].shape[2]
    for core in range(kv):

        @pl.when(core_ref[0] == core)
        def _():
            for s in range(kv):
                cols = pl.ds((core ^ s) * width, width)
                att_ref[:, cols] = refs[s][0]
                grad_ref[:, cols] = refs[s][1]


def call(kernel, ins, specs, outs, scratch=(), scratch_bytes=0, cost=None, name=None):
    out_specs = [VMEM] * len(outs)
    single = len(outs) == 1
    return pl.pallas_call(
        kernel,
        out_shape=outs[0] if single else tuple(outs),
        in_specs=specs,
        out_specs=out_specs[0] if single else tuple(out_specs),
        scratch_shapes=list(scratch),
        compiler_params=params(nbytes(*ins), nbytes(*outs), scratch_bytes),
        cost_estimate=cost,
        name=name,
    )(*ins)


def shards(queries, key_vectors, value_vectors, out_grad, block_order):
    heads_devices = lax.axis_size("head")
    ctx_devices = lax.axis_size("ctx")
    halves, block_rows, query_width = queries.shape
    kv = key_vectors.shape[2] // HD
    rows = halves * block_rows
    width = query_width // kv
    group = width // HD
    block_len = block_rows * heads_devices
    ctx = lax.axis_index("ctx").astype(jnp.int32)
    core = (ctx % kv).reshape(1)
    z_devices = ctx_devices // kv
    place = jnp.stack([lax.axis_index("head").astype(jnp.int32), ctx // kv, ctx % kv])
    queries = queries.reshape(rows, query_width)
    out_grad = out_grad.reshape(rows, query_width)
    key_vectors = key_vectors.reshape(rows, kv * HD)
    value_vectors = value_vectors.reshape(rows, kv * HD)

    def shape(*dims):
        return jax.ShapeDtypeStruct(dims, BF)

    def from_cores(block):
        return [block] + [swap(block, "ctx", step) for step in range(1, kv)]

    def from_z(block):
        return [block] + [swap(block, "ctx", m * kv) for m in range(1, z_devices)]

    def from_heads(block):
        return [block] + [swap(block, "head", m) for m in range(1, heads_devices)]

    key_parts, value_parts = from_cores(key_vectors), from_cores(value_vectors)
    piece = call(
        functools.partial(pack_kv_kernel, kv),
        (core, *[part for pair in zip(key_parts, value_parts) for part in pair]),
        [SMEM] + [VMEM] * (2 * kv),
        [shape(kv, rows, 2 * HD)],
        name="pack_kv",
    )
    column = jnp.stack(from_z(piece))
    kv_parts = from_heads(column)
    query_parts, grad_parts = from_cores(queries), from_cores(out_grad)

    tile_rows = block_rows if block_rows % 16 == 0 else rows
    lanes = group * tile_rows
    keys = heads_devices * ctx_devices * rows
    query_rows = kv * group * rows
    scratch = [
        pltpu.VMEM((query_rows, HD), BF),
        pltpu.VMEM((query_rows, HD), BF),
        pltpu.VMEM((keys, lanes), F32),
        pltpu.VMEM((keys, query_rows), BF),
        pltpu.VMEM((keys, query_rows), BF),
    ]
    outs = call(
        functools.partial(
            attend_kernel, kv, block_len, block_rows, tile_rows, group, heads_devices
        ),
        (block_order, place, *query_parts, *grad_parts, *kv_parts),
        [SMEM, SMEM] + [VMEM] * (2 * kv + heads_devices),
        [shape(2, rows, width)] * kv + [shape(z_devices, kv, rows, 2 * HD)] * heads_devices,
        scratch,
        4 * query_rows * HD + keys * (4 * lanes + 4 * query_rows),
        name="attend",
    )
    out_parts, dkv = outs[:kv], outs[kv:]
    dkv_parts = [dkv[0]] + [swap(dkv[m], "head", m) for m in range(1, heads_devices)]
    out_parts = [out_parts[0]] + [swap(out_parts[s], "ctx", s) for s in range(1, kv)]
    z_parts = call(
        functools.partial(sum_heads_kernel, heads_devices),
        tuple(dkv_parts),
        [VMEM] * heads_devices,
        [shape(kv, rows, 2 * HD)] * z_devices,
        name="sum_heads",
    )
    z_parts = [z_parts[0]] + [swap(z_parts[m], "ctx", m * kv) for m in range(1, z_devices)]
    core_parts = call(
        functools.partial(sum_z_kernel, kv),
        tuple(z_parts),
        [VMEM] * z_devices,
        [shape(rows, 2 * HD)] * kv,
        name="sum_z",
    )
    core_parts = [core_parts[0]] + [swap(core_parts[s], "ctx", s) for s in range(1, kv)]
    attended, query_grad = call(
        functools.partial(finish_q_kernel, kv),
        (core, *out_parts),
        [SMEM] + [VMEM] * kv,
        [shape(rows, query_width)] * 2,
        name="finish_q",
    )
    key_grad, value_grad = call(
        functools.partial(finish_kv_kernel, kv, 1.0 / math.sqrt(HD)),
        (core, *core_parts),
        [SMEM] + [VMEM] * kv,
        [shape(rows, kv * HD)] * 2,
        name="finish_kv",
    )
    return (
        attended.reshape(halves, block_rows, query_width),
        query_grad.reshape(halves, block_rows, query_width),
        key_grad.reshape(halves, block_rows, kv * HD),
        value_grad.reshape(halves, block_rows, kv * HD),
    )


def solution(mesh):
    split = P("ctx", "head", None)
    return jax.shard_map(
        shards,
        mesh=mesh,
        in_specs=(split, split, split, split, P()),
        out_specs=(split, split, split, split),
        check_vma=False,
    )
```

time: 74.4 us -> 65.5 us (0.88)
  waiting for transfers between devices: 39.7 us -> 33.6 us
  Pallas kernels: 13.4 us -> 12 us
  local copies, waits for them, and re-layouts: 2.17 us -> 0.77 us
    all_to_all x2 -> x0, waiting for transfers between devices: 16.3 us -> none  [the longest x1 9.11 us: shards(): lax.all_to_all(kv_send, 'ctx', split_axis=0, concat_axis=0, tiled=True)]
    ppermute x8 -> x18, starting transfers between devices: 8.01 us -> 18.2 us  [swap(): return lax.ppermute(block, axis, [(i, i ^ mask) for i in range(size)])]
    ppermute x8 -> x18, waiting for transfers between devices: 23.4 us -> 33.6 us  [swap(): return lax.ppermute(block, axis, [(i, i ^ mask) for i in range(size)])]
    all_to_all x2 -> x0, starting transfers between devices: 9.87 us -> none  [the longest x1 6.46 us: shards(): lax.all_to_all(kv_send, 'ctx', split_axis=0, concat_axis=0, tiled=True)]
    pallas_call x6, Pallas kernels: 13.4 us -> 12 us  [call(): pl.pallas_call(kernel, out_shape=outs[0] if single else tuple(outs), in_s...]
    unnamed x10, local copies, waits for them, and re-layouts: 2.17 us -> 0.77 us
  transfers between devices with their start and end apart: 10 -> 18, of which waited for: 8 -> 13; matrix products, arithmetic and copies ran while one was open for 0% -> 0% of each run, Pallas kernels for 1% -> 2%
where the time goes in v2:
time: 65.5 us; the launch traced here: 65.4 us
  waiting for transfers between devices  33.6 us (51%)
  starting transfers between devices  18.2 us (28%)
  Pallas kernels  12 us (18%)
  local copies, waits for them, and re-layouts  0.77 us (1%)
  between operations  0.71 us (1%)
    ppermute x18, waiting for transfers between devices, swap(): return lax.ppermute(block, axis, [(i, i ^ mask) for i in range(size)])  33.6 us
    ppermute x18, starting transfers between devices, swap(): return lax.ppermute(block, axis, [(i, i ^ mask) for i in range(size)])  18.2 us
    pallas_call x6, Pallas kernels, call(): pl.pallas_call(kernel, out_shape=outs[0] if single else tuple(outs), in_s...  12 us
  transfers between devices with their start and end apart: 18, of which 13 were waited for; matrix products, arithmetic and copies ran while one was open for 0% of the time, Pallas kernels for 2%

profile of v2, /device:TPU:0, one launch (start us, length us, event | category | flops | bytes accessed | tf_op | source)
XLA Modules:
  0.0 65.4 jit_solution(13457774761450099823)
XLA Ops:
  0.6 0.0 copy-start.2
  0.6 0.5 collective-permute-start.2
  1.2 0.1 collective-permute-start.3
  1.2 1.0 %collective-permute-done.2.refs_2_ = bf16[64,256]{1,0:T(8,128)(2,1)S(1)} collective-permute-done((bf16[64,256]{1,0:T(8,128)(2,1)}, bf16[64,256]{1,0:T(8,128)(2,1)S(1)}, u32[]{:S(2)}, u32[]{:S(2)}) %collective-permute-start.2) | collective-permute-done | bytes 32800 | tf_op jit(solution)/shard_map/ppermute | solution.py:33
  2.2 0.3 collective-permute-done.3.refs_3_
  2.6 0.0 copy-done.2
  2.6 0.0 copy-start.3
  2.6 0.8 %copy-done.3 = bf16[2,32,256]{2,1,0:T(8,128)(2,1)S(1)} copy-done((bf16[2,32,256]{2,1,0:T(8,128)(2,1)S(1)}, bf16[2,32,256]{2,1,0:T(8,128)(2,1)}, u32[]{:S(2)}) %copy-start.3) | copy-done | bytes 32792
  3.4 4.8 %collective-permute-start.6 = (bf16[2,64,256]{2,1,0:T(8,128)(2,1)S(1)}, bf16[2,64,256]{2,1,0:T(8,128)(2,1)S(1)}, u32[]{:S(2)}, u32[]{:S(2)}) collective-permute-start(bf16[2,64,256]{2,1,0:T(8,128)(2,1)S(1)} %pack_kv.1), channel_id=1, source_target_pairs={{0,6},{1,7},{2,4},{3,5},{4,2},{5,3},{6,0},{7,1},{8,14},{9,15},{10,... | collective-permute-start | bytes 196616 | tf_op jit(solution)/shard_map/ppermute | solution.py:33
  8.2 0.0 collective-permute-start.5
  8.2 0.6 collective-permute-start.4
  8.8 0.0 collective-permute-start
  8.8 0.5 collective-permute-start.1
  9.3 1.6 %collective-permute-done.6 = bf16[2,64,256]{2,1,0:T(8,128)(2,1)S(1)} collective-permute-done((bf16[2,64,256]{2,1,0:T(8,128)(2,1)S(1)}, bf16[2,64,256]{2,1,0:T(8,128)(2,1)S(1)}, u32[]{:S(2)}, u32[]{:S(2)}) %collective-permute-start.6) | collective-permute-done | bytes 65568 | tf_op jit(solution)/shard_map/ppermute | solution.py:33
  11.0 3.2 %collective-permute-done.5 = bf16[2,64,256]{2,1,0:T(8,128)(2,1)S(1)} collective-permute-done((bf16[2,64,256]{2,1,0:T(8,128)(2,1)S(1)}, bf16[2,64,256]{2,1,0:T(8,128)(2,1)S(1)}, u32[]{:S(2)}, u32[]{:S(2)}) %collective-permute-start.5) | collective-permute-done | bytes 65568 | tf_op jit(solution)/shard_map/ppermute | solution.py:33
  14.2 0.0 collective-permute-done.4
  14.2 2.5 %collective-permute-start.9 = (bf16[4,2,64,256]{3,2,1,0:T(8,128)(2,1)S(1)}, bf16[4,2,64,256]{3,2,1,0:T(8,128)(2,1)S(1)}, u32[]{:S(2)}, u32[]{:S(2)}) collective-permute-start(bf16[4,2,64,256]{3,2,1,0:T(8,128)(2,1)S(1)} %pad_maximum_fusion.refs_4_), channel_id=1, source_target_pairs={{0,24},{8,16},{16,8},{24,0},{1,25},{9,17},{17,9},{25,1},{2,26},{10... | collective-permute-start | bytes 786440 | tf_op jit(solution)/shard_map/ppermute | solution.py:33
  16.7 0.5 collective-permute-start.8
  17.2 0.5 collective-permute-start.7
  17.8 0.1 pad_add_fusion.place_ref
  17.8 0.0 collective-permute-done.refs_1_
  17.8 0.0 collective-permute-done.1.refs_3_
  17.8 6.6 %collective-permute-done.9.refs_7_ = bf16[4,2,64,256]{3,2,1,0:T(8,128)(2,1)S(1)} collective-permute-done((bf16[4,2,64,256]{3,2,1,0:T(8,128)(2,1)S(1)}, bf16[4,2,64,256]{3,2,1,0:T(8,128)(2,1)S(1)}, u32[]{:S(2)}, u32[]{:S(2)}) %collective-permute-start.9) | collective-permute-done | bytes 262176 | tf_op jit(solution)/shard_map/ppermute | solution.py:33
  24.4 4.3 %collective-permute-done.8.refs_6_ = bf16[4,2,64,256]{3,2,1,0:T(8,128)(2,1)S(1)} collective-permute-done((bf16[4,2,64,256]{3,2,1,0:T(8,128)(2,1)S(1)}, bf16[4,2,64,256]{3,2,1,0:T(8,128)(2,1)S(1)}, u32[]{:S(2)}, u32[]{:S(2)}) %collective-permute-start.8) | collective-permute-done | bytes 262176 | tf_op jit(solution)/shard_map/ppermute | solution.py:33
  28.7 0.1 collective-permute-done.7.refs_5_
  28.8 0.0 copy-done
  28.8 0.0 copy-done.1
  28.8 0.0 copy-done.4
  28.8 10.3 %attend.1 = (bf16[2,64,1024]{2,1,0:T(8,128)(2,1)S(1)}, bf16[2,64,1024]{2,1,0:T(8,128)(2,1)S(1)}, bf16[4,2,64,256]{3,2,1,0:T(8,128)(2,1)S(1)}, bf16[4,2,64,256]{3...) custom-call(s32[16]{0:T(128)S(1)} %copy-done.4, ...), custom_call_target="tpu_custom_call" | custom-call | tf_op jit(solution)/shard_map/attend/pallas_call | solution.py:200
  39.1 1.6 %collective-permute-start.11 = (bf16[4,2,64,256]{3,2,1,0:T(8,128)(2,1)S(1)}, bf16[4,2,64,256]{3,2,1,0:T(8,128)(2,1)S(1)}, u32[]{:S(2)}, u32[]{:S(2)}) collective-permute-start(bf16[4,2,64,256]{3,2,1,0:T(8,128)(2,1)S(1)} %get-tuple-element.25), channel_id=1, source_target_pairs={{0,8},{8,0},{16,24},{24,16},{1,9},{9,1},{17,25},{25,17},{2,10},{10... | collective-permute-start | bytes 786440 | tf_op jit(solution)/shard_map/ppermute | solution.py:33
  40.7 0.7 %collective-permute-start.12 = (bf16[4,2,64,256]{3,2,1,0:T(8,128)(2,1)S(1)}, bf16[4,2,64,256]{3,2,1,0:T(8,128)(2,1)S(1)}, u32[]{:S(2)}, u32[]{:S(2)}) collective-permute-start(bf16[4,2,64,256]{3,2,1,0:T(8,128)(2,1)S(1)} %get-tuple-element.26), channel_id=1, source_target_pairs={{0,16},{8,24},{16,0},{24,8},{1,17},{9,25},{17,1},{25,9},{2,18},{10... | collective-permute-start | bytes 786440 | tf_op jit(solution)/shard_map/ppermute | solution.py:33
  41.4 1.3 %collective-permute-start.13 = (bf16[4,2,64,256]{3,2,1,0:T(8,128)(2,1)S(1)}, bf16[4,2,64,256]{3,2,1,0:T(8,128)(2,1)S(1)}, u32[]{:S(2)}, u32[]{:S(2)}) collective-permute-start(bf16[4,2,64,256]{3,2,1,0:T(8,128)(2,1)S(1)} %get-tuple-element.27), channel_id=1, source_target_pairs={{0,24},{8,16},{16,8},{24,0},{1,25},{9,17},{17,9},{25,1},{2,26},{10... | collective-permute-start | bytes 786440 | tf_op jit(solution)/shard_map/ppermute | solution.py:33
  42.7 0.0 collective-permute-start.10
  42.7 5.7 %collective-permute-done.11.refs_1_ = bf16[4,2,64,256]{3,2,1,0:T(8,128)(2,1)S(1)} collective-permute-done((bf16[4,2,64,256]{3,2,1,0:T(8,128)(2,1)S(1)}, bf16[4,2,64,256]{3,2,1,0:T(8,128)(2,1)S(1)}, u32[]{:S(2)}, u32[]{:S(2)}) %collective-permute-start.11) | collective-permute-done | bytes 262176 | tf_op jit(solution)/shard_map/ppermute | solution.py:33
  48.4 5.8 %collective-permute-done.12.refs_2_ = bf16[4,2,64,256]{3,2,1,0:T(8,128)(2,1)S(1)} collective-permute-done((bf16[4,2,64,256]{3,2,1,0:T(8,128)(2,1)S(1)}, bf16[4,2,64,256]{3,2,1,0:T(8,128)(2,1)S(1)}, u32[]{:S(2)}, u32[]{:S(2)}) %collective-permute-start.12) | collective-permute-done | bytes 262176 | tf_op jit(solution)/shard_map/ppermute | solution.py:33
  54.2 0.0 collective-permute-done.13.refs_3_
  54.2 0.1 sum_heads.1
  54.3 1.1 %collective-permute-start.14 = (bf16[2,64,256]{2,1,0:T(8,128)(2,1)S(1)}, bf16[2,64,256]{2,1,0:T(8,128)(2,1)S(1)}, u32[]{:S(2)}, u32[]{:S(2)}) collective-permute-start(bf16[2,64,256]{2,1,0:T(8,128)(2,1)S(1)} %get-tuple-element.29), channel_id=1, source_target_pairs={{0,2},{1,3},{2,0},{3,1},{4,6},{5,7},{6,4},{7,5},{8,10},{9,11},{10,... | collective-permute-start | bytes 196616 | tf_op jit(solution)/shard_map/ppermute | solution.py:33
  55.4 1.8 %collective-permute-start.15 = (bf16[2,64,256]{2,1,0:T(8,128)(2,1)S(1)}, bf16[2,64,256]{2,1,0:T(8,128)(2,1)S(1)}, u32[]{:S(2)}, u32[]{:S(2)}) collective-permute-start(bf16[2,64,256]{2,1,0:T(8,128)(2,1)S(1)} %get-tuple-element.30), channel_id=1, source_target_pairs={{0,4},{1,5},{2,6},{3,7},{4,0},{5,1},{6,2},{7,3},{8,12},{9,13},{10,... | collective-permute-start | bytes 196616 | tf_op jit(solution)/shard_map/ppermute | solution.py:33
  57.3 1.5 %collective-permute-start.16 = (bf16[2,64,256]{2,1,0:T(8,128)(2,1)S(1)}, bf16[2,64,256]{2,1,0:T(8,128)(2,1)S(1)}, u32[]{:S(2)}, u32[]{:S(2)}) collective-permute-start(bf16[2,64,256]{2,1,0:T(8,128)(2,1)S(1)} %get-tuple-element.31), channel_id=1, source_target_pairs={{0,6},{1,7},{2,4},{3,5},{4,2},{5,3},{6,0},{7,1},{8,14},{9,15},{10,... | collective-permute-start | bytes 196616 | tf_op jit(solution)/shard_map/ppermute | solution.py:33
  58.8 0.2 collective-permute-done.14.refs_1_
  59.0 3.0 %collective-permute-done.15.refs_2_ = bf16[2,64,256]{2,1,0:T(8,128)(2,1)S(1)} collective-permute-done((bf16[2,64,256]{2,1,0:T(8,128)(2,1)S(1)}, bf16[2,64,256]{2,1,0:T(8,128)(2,1)S(1)}, u32[]{:S(2)}, u32[]{:S(2)}) %collective-permute-start.15) | collective-permute-done | bytes 65568 | tf_op jit(solution)/shard_map/ppermute | solution.py:33
  62.0 1.4 %collective-permute-done.16.refs_3_ = bf16[2,64,256]{2,1,0:T(8,128)(2,1)S(1)} collective-permute-done((bf16[2,64,256]{2,1,0:T(8,128)(2,1)S(1)}, bf16[2,64,256]{2,1,0:T(8,128)(2,1)S(1)}, u32[]{:S(2)}, u32[]{:S(2)}) %collective-permute-start.16) | collective-permute-done | bytes 65568 | tf_op jit(solution)/shard_map/ppermute | solution.py:33
  63.4 0.1 collective-permute-start.17
  63.5 0.0 collective-permute-done.10.refs_1_
  63.5 0.8 %finish_q.1 = (bf16[64,2048]{1,0:T(8,128)(2,1)}, bf16[64,2048]{1,0:T(8,128)(2,1)}) custom-call(s32[1]{0:T(128)} %bitcast.core_ref, bf16[2,64,1024]{2,1,0:T(8,128)(2,1)S(1)} %get-tuple-element.20.refs_0_, bf16[2,64,1024]{2,1,0:T(8,128)(2,1)S(1)} %collective-permute-done.10.refs_1_), custom_call_target="tpu_custom_call" | custom-call | tf_op jit(solution)/shard_map/finish_q/pallas_call | solution.py:200
  64.4 0.3 collective-permute-done.17.refs_1_
  64.7 0.6 finish_kv.1
  (6 shorter events, 0.1 us)
Async XLA Ops:
  0.6 1.9 %copy-start.2 = (bf16[2,32,256]{2,1,0:T(8,128)(2,1)S(1)}, bf16[2,32,256]{2,1,0:T(8,128)(2,1)}, u32[]{:S(2)}) copy-start(bf16[2,32,256]{2,1,0:T(8,128)(2,1)} %param.6) | copy-start | bytes 98308
  0.6 1.6 %collective-permute-start.2 = (bf16[64,256]{1,0:T(8,128)(2,1)}, bf16[64,256]{1,0:T(8,128)(2,1)S(1)}, u32[]{:S(2)}, u32[]{:S(2)}) collective-permute-start(bf16[64,256]{1,0:T(8,128)(2,1)} %bitcast.20), channel_id=1, source_target_pairs={{0,1},{1,0},{2,3},{3,2},{4,5},{5,4},{6,7},{7,6},{8,9},{9,8},{10,11... | collective-permute-start | bytes 98312 | tf_op jit(solution)/shard_map/ppermute | solution.py:33
  1.2 1.4 %collective-permute-start.3 = (bf16[64,256]{1,0:T(8,128)(2,1)}, bf16[64,256]{1,0:T(8,128)(2,1)S(1)}, u32[]{:S(2)}, u32[]{:S(2)}) collective-permute-start(bf16[64,256]{1,0:T(8,128)(2,1)} %bitcast.22), channel_id=1, source_target_pairs={{0,1},{1,0},{2,3},{3,2},{4,5},{5,4},{6,7},{7,6},{8,9},{9,8},{10,11... | collective-permute-start | bytes 98312 | tf_op jit(solution)/shard_map/ppermute | solution.py:33
  2.6 0.8 %copy-start.3 = (bf16[2,32,256]{2,1,0:T(8,128)(2,1)S(1)}, bf16[2,32,256]{2,1,0:T(8,128)(2,1)}, u32[]{:S(2)}) copy-start(bf16[2,32,256]{2,1,0:T(8,128)(2,1)} %param.7) | copy-start | bytes 98308
  3.4 7.6 %collective-permute-start.6 = (bf16[2,64,256]{2,1,0:T(8,128)(2,1)S(1)}, bf16[2,64,256]{2,1,0:T(8,128)(2,1)S(1)}, u32[]{:S(2)}, u32[]{:S(2)}) collective-permute-start(bf16[2,64,256]{2,1,0:T(8,128)(2,1)S(1)} %pack_kv.1), channel_id=1, source_target_pairs={{0,6},{1,7},{2,4},{3,5},{4,2},{5,3},{6,0},{7,1},{8,14},{9,15},{10,... | collective-permute-start | bytes 196616 | tf_op jit(solution)/shard_map/ppermute | solution.py:33
  8.2 6.0 %collective-permute-start.5 = (bf16[2,64,256]{2,1,0:T(8,128)(2,1)S(1)}, bf16[2,64,256]{2,1,0:T(8,128)(2,1)S(1)}, u32[]{:S(2)}, u32[]{:S(2)}) collective-permute-start(bf16[2,64,256]{2,1,0:T(8,128)(2,1)S(1)} %pack_kv.1), channel_id=1, source_target_pairs={{0,4},{1,5},{2,6},{3,7},{4,0},{5,1},{6,2},{7,3},{8,12},{9,13},{10,... | collective-permute-start | bytes 196616 | tf_op jit(solution)/shard_map/ppermute | solution.py:33
  8.2 6.0 %collective-permute-start.4 = (bf16[2,64,256]{2,1,0:T(8,128)(2,1)S(1)}, bf16[2,64,256]{2,1,0:T(8,128)(2,1)S(1)}, u32[]{:S(2)}, u32[]{:S(2)}) collective-permute-start(bf16[2,64,256]{2,1,0:T(8,128)(2,1)S(1)} %pack_kv.1), channel_id=1, source_target_pairs={{0,2},{1,3},{2,0},{3,1},{4,6},{5,7},{6,4},{7,5},{8,10},{9,11},{10,... | collective-permute-start | bytes 196616 | tf_op jit(solution)/shard_map/ppermute | solution.py:33
  8.8 9.0 %collective-permute-start = (bf16[64,2048]{1,0:T(8,128)(2,1)}, bf16[64,2048]{1,0:T(8,128)(2,1)S(1)}, u32[]{:S(2)}, u32[]{:S(2)}) collective-permute-start(bf16[64,2048]{1,0:T(8,128)(2,1)} %bitcast.16), channel_id=1, source_target_pairs={{0,1},{1,0},{2,3},{3,2},{4,5},{5,4},{6,7},{7,6},{8,9},{9,8},{10,11... | collective-permute-start | bytes 786440 | tf_op jit(solution)/shard_map/ppermute | solution.py:33
  8.8 9.0 %collective-permute-start.1 = (bf16[64,2048]{1,0:T(8,128)(2,1)}, bf16[64,2048]{1,0:T(8,128)(2,1)S(1)}, u32[]{:S(2)}, u32[]{:S(2)}) collective-permute-start(bf16[64,2048]{1,0:T(8,128)(2,1)} %bitcast.18), channel_id=1, source_target_pairs={{0,1},{1,0},{2,3},{3,2},{4,5},{5,4},{6,7},{7,6},{8,9},{9,8},{10,11... | collective-permute-start | bytes 786440 | tf_op jit(solution)/shard_map/ppermute | solution.py:33
  14.2 14.7 %copy-start = (bf16[2,32,2048]{2,1,0:T(8,128)(2,1)S(1)}, bf16[2,32,2048]{2,1,0:T(8,128)(2,1)}, u32[]{:S(2)}) copy-start(bf16[2,32,2048]{2,1,0:T(8,128)(2,1)} %param.5) | copy-start | bytes 786436
  14.2 14.7 %copy-start.1 = (bf16[2,32,2048]{2,1,0:T(8,128)(2,1)S(1)}, bf16[2,32,2048]{2,1,0:T(8,128)(2,1)}, u32[]{:S(2)}) copy-start(bf16[2,32,2048]{2,1,0:T(8,128)(2,1)} %param.8) | copy-start | bytes 786436
  14.2 10.2 %collective-permute-start.9 = (bf16[4,2,64,256]{3,2,1,0:T(8,128)(2,1)S(1)}, bf16[4,2,64,256]{3,2,1,0:T(8,128)(2,1)S(1)}, u32[]{:S(2)}, u32[]{:S(2)}) collective-permute-start(bf16[4,2,64,256]{3,2,1,0:T(8,128)(2,1)S(1)} %pad_maximum_fusion.refs_4_), channel_id=1, source_target_pairs={{0,24},{8,16},{16,8},{24,0},{1,25},{9,17},{17,9},{25,1},{2,26},{10... | collective-permute-start | bytes 786440 | tf_op jit(solution)/shard_map/ppermute | solution.py:33
  16.7 12.0 %collective-permute-start.8 = (bf16[4,2,64,256]{3,2,1,0:T(8,128)(2,1)S(1)}, bf16[4,2,64,256]{3,2,1,0:T(8,128)(2,1)S(1)}, u32[]{:S(2)}, u32[]{:S(2)}) collective-permute-start(bf16[4,2,64,256]{3,2,1,0:T(8,128)(2,1)S(1)} %pad_maximum_fusion.refs_4_), channel_id=1, source_target_pairs={{0,16},{8,24},{16,0},{24,8},{1,17},{9,25},{17,1},{25,9},{2,18},{10... | collective-permute-start | bytes 786440 | tf_op jit(solution)/shard_map/ppermute | solution.py:33
  17.2 11.6 %collective-permute-start.7 = (bf16[4,2,64,256]{3,2,1,0:T(8,128)(2,1)S(1)}, bf16[4,2,64,256]{3,2,1,0:T(8,128)(2,1)S(1)}, u32[]{:S(2)}, u32[]{:S(2)}) collective-permute-start(bf16[4,2,64,256]{3,2,1,0:T(8,128)(2,1)S(1)} %pad_maximum_fusion.refs_4_), channel_id=1, source_target_pairs={{0,8},{8,0},{16,24},{24,16},{1,9},{9,1},{17,25},{25,17},{2,10},{10... | collective-permute-start | bytes 786440 | tf_op jit(solution)/shard_map/ppermute | solution.py:33
  17.8 11.1 %copy-start.4 = (s32[16]{0:T(128)S(1)}, s32[16]{0:T(128)}, u32[]{:S(2)}) copy-start(s32[16]{0:T(128)} %order_ref.1) | copy-start | bytes 196
  39.1 9.3 %collective-permute-start.11 = (bf16[4,2,64,256]{3,2,1,0:T(8,128)(2,1)S(1)}, bf16[4,2,64,256]{3,2,1,0:T(8,128)(2,1)S(1)}, u32[]{:S(2)}, u32[]{:S(2)}) collective-permute-start(bf16[4,2,64,256]{3,2,1,0:T(8,128)(2,1)S(1)} %get-tuple-element.25), channel_id=1, source_target_pairs={{0,8},{8,0},{16,24},{24,16},{1,9},{9,1},{17,25},{25,17},{2,10},{10... | collective-permute-start | bytes 786440 | tf_op jit(solution)/shard_map/ppermute | solution.py:33
  40.7 13.5 %collective-permute-start.12 = (bf16[4,2,64,256]{3,2,1,0:T(8,128)(2,1)S(1)}, bf16[4,2,64,256]{3,2,1,0:T(8,128)(2,1)S(1)}, u32[]{:S(2)}, u32[]{:S(2)}) collective-permute-start(bf16[4,2,64,256]{3,2,1,0:T(8,128)(2,1)S(1)} %get-tuple-element.26), channel_id=1, source_target_pairs={{0,16},{8,24},{16,0},{24,8},{1,17},{9,25},{17,1},{25,9},{2,18},{10... | collective-permute-start | bytes 786440 | tf_op jit(solution)/shard_map/ppermute | solution.py:33
  41.4 12.7 %collective-permute-start.13 = (bf16[4,2,64,256]{3,2,1,0:T(8,128)(2,1)S(1)}, bf16[4,2,64,256]{3,2,1,0:T(8,128)(2,1)S(1)}, u32[]{:S(2)}, u32[]{:S(2)}) collective-permute-start(bf16[4,2,64,256]{3,2,1,0:T(8,128)(2,1)S(1)} %get-tuple-element.27), channel_id=1, source_target_pairs={{0,24},{8,16},{16,8},{24,0},{1,25},{9,17},{17,9},{25,1},{2,26},{10... | collective-permute-start | bytes 786440 | tf_op jit(solution)/shard_map/ppermute | solution.py:33
  42.7 20.8 %collective-permute-start.10 = (bf16[2,64,1024]{2,1,0:T(8,128)(2,1)S(1)}, bf16[2,64,1024]{2,1,0:T(8,128)(2,1)S(1)}, u32[]{:S(2)}, u32[]{:S(2)}) collective-permute-start(bf16[2,64,1024]{2,1,0:T(8,128)(2,1)S(1)} %get-tuple-element.21), channel_id=1, source_target_pairs={{0,1},{1,0},{2,3},{3,2},{4,5},{5,4},{6,7},{7,6},{8,9},{9,8},{10,11... | collective-permute-start | bytes 786440 | tf_op jit(solution)/shard_map/ppermute | solution.py:33
  54.3 4.7 %collective-permute-start.14 = (bf16[2,64,256]{2,1,0:T(8,128)(2,1)S(1)}, bf16[2,64,256]{2,1,0:T(8,128)(2,1)S(1)}, u32[]{:S(2)}, u32[]{:S(2)}) collective-permute-start(bf16[2,64,256]{2,1,0:T(8,128)(2,1)S(1)} %get-tuple-element.29), channel_id=1, source_target_pairs={{0,2},{1,3},{2,0},{3,1},{4,6},{5,7},{6,4},{7,5},{8,10},{9,11},{10,... | collective-permute-start | bytes 196616 | tf_op jit(solution)/shard_map/ppermute | solution.py:33
  55.4 6.6 %collective-permute-start.15 = (bf16[2,64,256]{2,1,0:T(8,128)(2,1)S(1)}, bf16[2,64,256]{2,1,0:T(8,128)(2,1)S(1)}, u32[]{:S(2)}, u32[]{:S(2)}) collective-permute-start(bf16[2,64,256]{2,1,0:T(8,128)(2,1)S(1)} %get-tuple-element.30), channel_id=1, source_target_pairs={{0,4},{1,5},{2,6},{3,7},{4,0},{5,1},{6,2},{7,3},{8,12},{9,13},{10,... | collective-permute-start | bytes 196616 | tf_op jit(solution)/shard_map/ppermute | solution.py:33
  57.3 6.1 %collective-permute-start.16 = (bf16[2,64,256]{2,1,0:T(8,128)(2,1)S(1)}, bf16[2,64,256]{2,1,0:T(8,128)(2,1)S(1)}, u32[]{:S(2)}, u32[]{:S(2)}) collective-permute-start(bf16[2,64,256]{2,1,0:T(8,128)(2,1)S(1)} %get-tuple-element.31), channel_id=1, source_target_pairs={{0,6},{1,7},{2,4},{3,5},{4,2},{5,3},{6,0},{7,1},{8,14},{9,15},{10,... | collective-permute-start | bytes 196616 | tf_op jit(solution)/shard_map/ppermute | solution.py:33
  63.4 1.3 %collective-permute-start.17 = (bf16[64,256]{1,0:T(8,128)(2,1)S(1)}, bf16[64,256]{1,0:T(8,128)(2,1)S(1)}, u32[]{:S(2)}, u32[]{:S(2)}) collective-permute-start(bf16[64,256]{1,0:T(8,128)(2,1)S(1)} %get-tuple-element.33), channel_id=1, source_target_pairs={{0,1},{1,0},{2,3},{3,2},{4,5},{5,4},{6,7},{7,6},{8,9},{9,8},{10,11... | collective-permute-start | bytes 98312 | tf_op jit(solution)/shard_map/ppermute | solution.py:33

commit v3 on v2

--- a/solution.py
+++ b/solution.py
@@ -12,7 +12,7 @@
 BF = jnp.bfloat16
 F32 = jnp.float32
 LOWEST = -1e30
-LANES = 256
+CORES = 2
 
 
 def params(*arrays_bytes):
@@ -33,16 +33,39 @@
     return lax.ppermute(block, axis, [(i, i ^ mask) for i in range(size)])
 
 
-def pack_kv_kernel(kv, core_ref, *refs):
+def pack_own_kernel(kv, group_ref, key_ref, value_ref, out_ref):
+    for g in range(kv):
+
+        @pl.when(group_ref[0] == g)
+        def _():
+            cols = pl.ds(g * HD, HD)
+            out_ref[:, :HD] = key_ref[:, cols]
+            out_ref[:, HD:] = value_ref[:, cols]
+
+
+def pack_kv_kernel(kv, group_ref, own_ref, *refs):
     out_ref = refs[-1]
-    for core in range(kv):
-
-        @pl.when(core_ref[0] == core)
-        def _():
-            cols = pl.ds(core * HD, HD)
-            for step in range(kv):
-                out_ref[step, :, :HD] = refs[2 * step][:, cols]
-                out_ref[step, :, HD:] = refs[2 * step + 1][:, cols]
+    out_ref[0] = own_ref[...]
+    for g in range(kv):
+
+        @pl.when(group_ref[0] == g)
+        def _():
+            cols = pl.ds(g * HD, HD)
+            for s in range(1, kv):
+                out_ref[s, :, :HD] = refs[2 * s - 2][:, cols]
+                out_ref[s, :, HD:] = refs[2 * s - 1][:, cols]
+
+
+def pack_q_kernel(kv, group_ref, query_ref, grad_ref, *out_refs):
+    width = out_refs[0].shape[2]
+    for g in range(kv):
+
+        @pl.when(group_ref[0] == g)
+        def _():
+            for s in range(1, kv):
+                cols = pl.ds((g ^ s) * width, width)
+                out_refs[s - 1][0] = query_ref[:, cols]
+                out_refs[s - 1][1] = grad_ref[:, cols]
 
 
 def attend_kernel(
@@ -51,18 +74,19 @@
     block_rows,
     tile_rows,
     heads,
+    cores,
     chunks,
     order_ref,
     place_ref,
     *refs,
 ):
-    q_refs, do_refs = refs[:kv], refs[kv : 2 * kv]
-    refs = refs[2 * kv :]
+    q_own, do_own, refs = refs[0], refs[1], refs[2:]
+    q_parts, refs = refs[: kv - 1], refs[kv - 1 :]
     kv_refs, refs = refs[:chunks], refs[chunks:]
     out_refs, refs = refs[:kv], refs[kv:]
     dkv_refs, refs = refs[:chunks], refs[chunks:]
     q_all, do_all, e_ref, p_ref, ds_ref = refs
-    rows = q_refs[0].shape[0]
+    rows = q_own.shape[0]
     z_size = kv_refs[0].shape[0]
     chunk_keys = z_size * kv * rows
     blocks_here = rows // block_rows
@@ -70,9 +94,8 @@
     scaling = 1.0 / math.sqrt(HD)
     expo = scaling * math.log2(math.e)
     head_place = place_ref[0]
-    z_place = place_ref[1]
-    core = place_ref[2]
-    first_col = core * (heads * HD)
+    ctx_place = place_ref[1]
+    first_col = (head_place % kv) * (heads * HD)
     lane_row = lax.broadcasted_iota(jnp.int32, (1, lanes), 1) % tile_rows
     key_iota = lax.broadcasted_iota(jnp.int32, (block_rows, lanes), 0)
     tiles = [(step, start) for step in range(kv) for start in range(0, rows, tile_rows)]
@@ -81,15 +104,19 @@
         out_span = pl.ds(tile * lanes, lanes)
         for n in range(heads):
             at = pl.ds(tile * lanes + n * tile_rows, tile_rows)
-            cols = pl.ds(pl.multiple_of(first_col + n * HD, HD), HD)
-            q_all[at, :] = q_refs[step][span, cols]
-            do_all[at, :] = do_refs[step][span, cols]
+            if step == 0:
+                cols = pl.ds(pl.multiple_of(first_col + n * HD, HD), HD)
+                q_all[at, :] = q_own[span, cols]
+                do_all[at, :] = do_own[span, cols]
+            else:
+                q_all[at, :] = q_parts[step - 1][0, span, pl.ds(n * HD, HD)]
+                do_all[at, :] = q_parts[step - 1][1, span, pl.ds(n * HD, HD)]
         q = q_all[out_span, :]
         do = do_all[out_span, :]
-        source_ctx = z_place * kv + (core ^ step)
+        part_row = (head_place ^ step) * block_rows
         query_pos = jnp.zeros((1, lanes), jnp.int32)
         for b in range(start // block_rows, -(-(start + tile_rows) // block_rows)):
-            block_pos = order_ref[source_ctx * blocks_here + b] * block_len + head_place * block_rows
+            block_pos = order_ref[ctx_place * blocks_here + b] * block_len + part_row
             here = (lane_row + start) // block_rows == b
             query_pos = jnp.where(here, block_pos + (lane_row + start) % block_rows, query_pos)
         gap = query_pos - key_iota
@@ -97,12 +124,12 @@
         for m in range(chunks):
             keys = kv_refs[m][:, :, :, :HD].reshape(chunk_keys, HD)
             scores = lax.dot_general(keys, q, (((1,), (1,)), ((), ())), preferred_element_type=F32)
-            chunk_head = head_place ^ m
+            a, core = divmod(m, cores)
             for j in range(chunk_keys // block_rows):
                 m_z, s_b = divmod(j, kv * blocks_here)
                 s, b = divmod(s_b, blocks_here)
-                stored = ((z_place ^ m_z) * kv + (core ^ s)) * blocks_here + b
-                key_pos = order_ref[stored] * block_len + chunk_head * block_rows
+                stored = (ctx_place ^ (m_z * cores + core)) * blocks_here + b
+                key_pos = order_ref[stored] * block_len + (head_place ^ (a * kv + s)) * block_rows
                 part = scores[j * block_rows : (j + 1) * block_rows]
                 part = jnp.where(gap >= key_pos, part, LOWEST)
                 e_ref[pl.ds(m * chunk_keys + j * block_rows, block_rows), :] = part
@@ -160,6 +187,12 @@
         out_ref[...] = total.astype(BF)
 
 
+def sum_cores_kernel(count, *refs):
+    for a in range(count):
+        total = refs[2 * a][...].astype(F32) + refs[2 * a + 1][...].astype(F32)
+        refs[2 * count + a][...] = total.astype(BF)
+
+
 def sum_z_kernel(kv, *refs):
     ins, outs = refs[:-kv], refs[-kv:]
     for s, out_ref in enumerate(outs):
@@ -169,27 +202,27 @@
         out_ref[...] = total.astype(BF)
 
 
-def finish_kv_kernel(kv, scaling, core_ref, *refs):
+def finish_kv_kernel(kv, scaling, group_ref, *refs):
     key_ref, value_ref = refs[kv:]
-    for core in range(kv):
-
-        @pl.when(core_ref[0] == core)
+    for g in range(kv):
+
+        @pl.when(group_ref[0] == g)
         def _():
             for s in range(kv):
-                cols = pl.ds((core ^ s) * HD, HD)
+                cols = pl.ds((g ^ s) * HD, HD)
                 key_ref[:, cols] = (refs[s][:, :HD].astype(F32) * scaling).astype(BF)
                 value_ref[:, cols] = refs[s][:, HD:]
 
 
-def finish_q_kernel(kv, core_ref, *refs):
+def finish_q_kernel(kv, group_ref, *refs):
     att_ref, grad_ref = refs[kv:]
     width = refs[0].shape[2]
-    for core in range(kv):
-
-        @pl.when(core_ref[0] == core)
+    for g in range(kv):
+
+        @pl.when(group_ref[0] == g)
         def _():
             for s in range(kv):
-                cols = pl.ds((core ^ s) * width, width)
+                cols = pl.ds((g ^ s) * width, width)
                 att_ref[:, cols] = refs[s][0]
                 grad_ref[:, cols] = refs[s][1]
 
@@ -218,10 +251,12 @@
     width = query_width // kv
     group = width // HD
     block_len = block_rows * heads_devices
-    ctx = lax.axis_index("ctx").astype(jnp.int32)
-    core = (ctx % kv).reshape(1)
-    z_devices = ctx_devices // kv
-    place = jnp.stack([lax.axis_index("head").astype(jnp.int32), ctx // kv, ctx % kv])
+    head = lax.axis_index("head").astype(jnp.int32)
+    place = jnp.stack([head, lax.axis_index("ctx").astype(jnp.int32)])
+    own_group = (head % kv).reshape(1)
+    cores = CORES if ctx_devices % CORES == 0 else 1
+    z_devices = ctx_devices // cores
+    spans = heads_devices // kv
     queries = queries.reshape(rows, query_width)
     out_grad = out_grad.reshape(rows, query_width)
     key_vectors = key_vectors.reshape(rows, kv * HD)
@@ -230,26 +265,36 @@
     def shape(*dims):
         return jax.ShapeDtypeStruct(dims, BF)
 
-    def from_cores(block):
-        return [block] + [swap(block, "ctx", step) for step in range(1, kv)]
-
-    def from_z(block):
-        return [block] + [swap(block, "ctx", m * kv) for m in range(1, z_devices)]
-
-    def from_heads(block):
-        return [block] + [swap(block, "head", m) for m in range(1, heads_devices)]
-
-    key_parts, value_parts = from_cores(key_vectors), from_cores(value_vectors)
+    key_parts = [swap(key_vectors, "head", s) for s in range(1, kv)]
+    value_parts = [swap(value_vectors, "head", s) for s in range(1, kv)]
+    own = call(
+        functools.partial(pack_own_kernel, kv),
+        (own_group, key_vectors, value_vectors),
+        [SMEM, VMEM, VMEM],
+        [shape(rows, 2 * HD)],
+        name="pack_own",
+    )
     piece = call(
         functools.partial(pack_kv_kernel, kv),
-        (core, *[part for pair in zip(key_parts, value_parts) for part in pair]),
-        [SMEM] + [VMEM] * (2 * kv),
+        (own_group, own, *[part for pair in zip(key_parts, value_parts) for part in pair]),
+        [SMEM] + [VMEM] * (2 * kv - 1),
         [shape(kv, rows, 2 * HD)],
         name="pack_kv",
     )
-    column = jnp.stack(from_z(piece))
-    kv_parts = from_heads(column)
-    query_parts, grad_parts = from_cores(queries), from_cores(out_grad)
+    column = jnp.stack([piece] + [swap(piece, "ctx", m * cores) for m in range(1, z_devices)])
+    q_sends = pl.pallas_call(
+        functools.partial(pack_q_kernel, kv),
+        out_shape=[shape(2, rows, width)] * (kv - 1),
+        in_specs=[SMEM, VMEM, VMEM],
+        out_specs=[VMEM] * (kv - 1),
+        name="pack_q",
+    )(own_group, queries, out_grad)
+    q_parts = [swap(q_sends[s - 1], "head", s) for s in range(1, kv)]
+    kv_parts = []
+    for a in range(spans):
+        part = column if a == 0 else swap(column, "head", a * kv)
+        kv_parts += [part] + [swap(part, "ctx", core) for core in range(1, cores)]
+    chunks = spans * cores
 
     tile_rows = block_rows if block_rows % 16 == 0 else rows
     lanes = group * tile_rows
@@ -264,44 +309,57 @@
     ]
     outs = call(
         functools.partial(
-            attend_kernel, kv, block_len, block_rows, tile_rows, group, heads_devices
+            attend_kernel, kv, block_len, block_rows, tile_rows, group, cores, chunks
         ),
-        (block_order, place, *query_parts, *grad_parts, *kv_parts),
-        [SMEM, SMEM] + [VMEM] * (2 * kv + heads_devices),
-        [shape(2, rows, width)] * kv + [shape(z_devices, kv, rows, 2 * HD)] * heads_devices,
+        (block_order, place, queries, out_grad, *q_parts, *kv_parts),
+        [SMEM, SMEM] + [VMEM] * (1 + kv + chunks),
+        [shape(2, rows, width)] * kv + [shape(z_devices, kv, rows, 2 * HD)] * chunks,
         scratch,
         4 * query_rows * HD + keys * (4 * lanes + 4 * query_rows),
         name="attend",
     )
     out_parts, dkv = outs[:kv], outs[kv:]
-    dkv_parts = [dkv[0]] + [swap(dkv[m], "head", m) for m in range(1, heads_devices)]
-    out_parts = [out_parts[0]] + [swap(out_parts[s], "ctx", s) for s in range(1, kv)]
+    if cores > 1:
+        both = [
+            part
+            for a in range(spans)
+            for part in (dkv[a * cores], swap(dkv[a * cores + 1], "ctx", 1))
+        ]
+        dkv = call(
+            functools.partial(sum_cores_kernel, spans),
+            tuple(both),
+            [VMEM] * (2 * spans),
+            [shape(z_devices, kv, rows, 2 * HD)] * spans,
+            name="sum_cores",
+        )
+    span_parts = [dkv[0]] + [swap(dkv[a], "head", a * kv) for a in range(1, spans)]
+    out_parts = [out_parts[0]] + [swap(out_parts[s], "head", s) for s in range(1, kv)]
     z_parts = call(
-        functools.partial(sum_heads_kernel, heads_devices),
-        tuple(dkv_parts),
-        [VMEM] * heads_devices,
+        functools.partial(sum_heads_kernel, spans),
+        tuple(span_parts),
+        [VMEM] * spans,
         [shape(kv, rows, 2 * HD)] * z_devices,
         name="sum_heads",
     )
-    z_parts = [z_parts[0]] + [swap(z_parts[m], "ctx", m * kv) for m in range(1, z_devices)]
-    core_parts = call(
+    z_parts = [z_parts[0]] + [swap(z_parts[m], "ctx", m * cores) for m in range(1, z_devices)]
+    pair_parts = call(
         functools.partial(sum_z_kernel, kv),
         tuple(z_parts),
         [VMEM] * z_devices,
         [shape(rows, 2 * HD)] * kv,
         name="sum_z",
     )
-    core_parts = [core_parts[0]] + [swap(core_parts[s], "ctx", s) for s in range(1, kv)]
+    pair_parts = [pair_parts[0]] + [swap(pair_parts[s], "head", s) for s in range(1, kv)]
     attended, query_grad = call(
         functools.partial(finish_q_kernel, kv),
-        (core, *out_parts),
+        (own_group, *out_parts),
         [SMEM] + [VMEM] * kv,
         [shape(rows, query_width)] * 2,
         name="finish_q",
     )
     key_grad, value_grad = call(
         functools.partial(finish_kv_kernel, kv, 1.0 / math.sqrt(HD)),
-        (core, *core_parts),
+        (own_group, *pair_parts),
         [SMEM] + [VMEM] * kv,
         [shape(rows, kv * HD)] * 2,
         name="finish_kv",

time: 65.5 us -> 61.6 us (0.940)
  waiting for transfers between devices: 33.6 us -> 30.4 us
  starting transfers between devices: 18.2 us -> 15.5 us
  Pallas kernels: 12 us -> 13.8 us
    ppermute x18 -> x17, waiting for transfers between devices: 33.6 us -> 30.4 us  [swap(): return lax.ppermute(block, axis, [(i, i ^ mask) for i in range(size)])]
    ppermute x18 -> x17, starting transfers between devices: 18.2 us -> 15.5 us  [swap(): return lax.ppermute(block, axis, [(i, i ^ mask) for i in range(size)])]
    pallas_call x0 -> x1, Pallas kernels: none -> 1.81 us  [shards(): pl.pallas_call(functools.partial(pack_q_kernel, kv), out_shape=[shape(2,...]
    pallas_call x6 -> x8, Pallas kernels: 12 us -> 12 us  [call(): pl.pallas_call(kernel, out_shape=outs[0] if single else tuple(outs), in_s...]
  transfers between devices with their start and end apart: 18 -> 17, of which waited for: 13 -> 12; matrix products, arithmetic and copies ran while one was open for 0% -> 0% of each run, Pallas kernels for 2% -> 4%
where the time goes in v3:
time: 61.6 us; the launch traced here: 61.4 us
  waiting for transfers between devices  30.4 us (49%)
  starting transfers between devices  15.5 us (25%)
  Pallas kernels  13.8 us (22%)
  local copies, waits for them, and re-layouts  0.8 us (1%)
  between operations  0.72 us (1%)
    ppermute x17, waiting for transfers between devices, swap(): return lax.ppermute(block, axis, [(i, i ^ mask) for i in range(size)])  30.4 us
    ppermute x17, starting transfers between devices, swap(): return lax.ppermute(block, axis, [(i, i ^ mask) for i in range(size)])  15.5 us
    pallas_call x8, Pallas kernels, call(): pl.pallas_call(kernel, out_shape=outs[0] if single else tuple(outs), in_s...  12 us
    pallas_call x1, Pallas kernels, shards(): pl.pallas_call(functools.partial(pack_q_kernel, kv), out_shape=[shape(2,...  1.81 us
  transfers between devices with their start and end apart: 17, of which 12 were waited for; matrix products, arithmetic and copies ran while one was open for 0% of the time, Pallas kernels for 4%

profile of v3, /device:TPU:0, one launch (start us, length us, event | category | flops | bytes accessed | tf_op | source)
XLA Modules:
  0.0 61.4 jit_solution(12249194034044228937)
XLA Ops:
  0.6 0.0 copy-start.2
  0.6 3.0 %collective-permute-start.1 = (bf16[64,256]{1,0:T(8,128)(2,1)}, bf16[64,256]{1,0:T(8,128)(2,1)S(1)}, u32[]{:S(2)}, u32[]{:S(2)}) collective-permute-start(bf16[64,256]{1,0:T(8,128)(2,1)} %bitcast.20), channel_id=1, source_target_pairs={{0,8},{8,0},{16,24},{24,16},{1,9},{9,1},{17,25},{25,17},{2,10},{10... | collective-permute-start | bytes 98312 | tf_op jit(solution)/shard_map/ppermute | solution.py:33
  3.6 0.1 collective-permute-start.2
  3.7 0.0 copy-done.2
  3.7 0.0 copy-start.3
  3.7 0.8 %copy-done.3 = bf16[2,32,256]{2,1,0:T(8,128)(2,1)S(1)} copy-done((bf16[2,32,256]{2,1,0:T(8,128)(2,1)S(1)}, bf16[2,32,256]{2,1,0:T(8,128)(2,1)}, u32[]{:S(2)}) %copy-start.3) | copy-done | bytes 32792
  4.5 1.2 %collective-permute-done.1.refs_0_ = bf16[64,256]{1,0:T(8,128)(2,1)S(1)} collective-permute-done((bf16[64,256]{1,0:T(8,128)(2,1)}, bf16[64,256]{1,0:T(8,128)(2,1)S(1)}, u32[]{:S(2)}, u32[]{:S(2)}) %collective-permute-start.1) | collective-permute-done | bytes 32800 | tf_op jit(solution)/shard_map/ppermute | solution.py:33
  5.7 2.0 %collective-permute-done.2.refs_1_ = bf16[64,256]{1,0:T(8,128)(2,1)S(1)} collective-permute-done((bf16[64,256]{1,0:T(8,128)(2,1)}, bf16[64,256]{1,0:T(8,128)(2,1)S(1)}, u32[]{:S(2)}, u32[]{:S(2)}) %collective-permute-start.2) | collective-permute-done | bytes 32800 | tf_op jit(solution)/shard_map/ppermute | solution.py:33
  7.8 3.7 %collective-permute-start.5 = (bf16[2,64,256]{2,1,0:T(8,128)(2,1)S(1)}, bf16[2,64,256]{2,1,0:T(8,128)(2,1)S(1)}, u32[]{:S(2)}, u32[]{:S(2)}) collective-permute-start(bf16[2,64,256]{2,1,0:T(8,128)(2,1)S(1)} %pack_kv.1), channel_id=1, source_target_pairs={{0,6},{1,7},{2,4},{3,5},{4,2},{5,3},{6,0},{7,1},{8,14},{9,15},{10,... | collective-permute-start | bytes 196616 | tf_op jit(solution)/shard_map/ppermute | solution.py:33
  11.5 0.0 collective-permute-start.4
  11.5 0.8 %collective-permute-start.3 = (bf16[2,64,256]{2,1,0:T(8,128)(2,1)S(1)}, bf16[2,64,256]{2,1,0:T(8,128)(2,1)S(1)}, u32[]{:S(2)}, u32[]{:S(2)}) collective-permute-start(bf16[2,64,256]{2,1,0:T(8,128)(2,1)S(1)} %pack_kv.1), channel_id=1, source_target_pairs={{0,2},{1,3},{2,0},{3,1},{4,6},{5,7},{6,4},{7,5},{8,10},{9,11},{10,... | collective-permute-start | bytes 196616 | tf_op jit(solution)/shard_map/ppermute | solution.py:33
  12.2 1.8 %collective-permute-done.5 = bf16[2,64,256]{2,1,0:T(8,128)(2,1)S(1)} collective-permute-done((bf16[2,64,256]{2,1,0:T(8,128)(2,1)S(1)}, bf16[2,64,256]{2,1,0:T(8,128)(2,1)S(1)}, u32[]{:S(2)}, u32[]{:S(2)}) %collective-permute-start.5) | collective-permute-done | bytes 65568 | tf_op jit(solution)/shard_map/ppermute | solution.py:33
  14.1 2.7 %collective-permute-done.4 = bf16[2,64,256]{2,1,0:T(8,128)(2,1)S(1)} collective-permute-done((bf16[2,64,256]{2,1,0:T(8,128)(2,1)S(1)}, bf16[2,64,256]{2,1,0:T(8,128)(2,1)S(1)}, u32[]{:S(2)}, u32[]{:S(2)}) %collective-permute-start.4) | collective-permute-done | bytes 65568 | tf_op jit(solution)/shard_map/ppermute | solution.py:33
  16.8 0.0 collective-permute-done.3
  16.9 1.6 %collective-permute-start.7 = (bf16[4,2,64,256]{3,2,1,0:T(8,128)(2,1)S(1)}, bf16[4,2,64,256]{3,2,1,0:T(8,128)(2,1)S(1)}, u32[]{:S(2)}, u32[]{:S(2)}) collective-permute-start(bf16[4,2,64,256]{3,2,1,0:T(8,128)(2,1)S(1)} %pad_maximum_fusion.refs_3_), channel_id=1, source_target_pairs={{0,16},{8,24},{16,0},{24,8},{1,17},{9,25},{17,1},{25,9},{2,18},{10... | collective-permute-start | bytes 786440 | tf_op jit(solution)/shard_map/ppermute | solution.py:33
  18.5 1.8 %pack_q.1 = bf16[2,64,1024]{2,1,0:T(8,128)(2,1)} custom-call(s32[1]{0:T(128)} %bitcast.group_ref, bf16[64,2048]{1,0:T(8,128)(2,1)} %bitcast.15, bf16[64,2048]{1,0:T(8,128)(2,1)} %bitcast.17), custom_call_target="tpu_custom_call" | custom-call | tf_op jit(solution)/shard_map/pack_q/pallas_call | solution.py:285
  20.3 0.3 collective-permute-start
  20.6 0.0 collective-permute-start.6
  20.6 3.1 %collective-permute-done.7.refs_5_ = bf16[4,2,64,256]{3,2,1,0:T(8,128)(2,1)S(1)} collective-permute-done((bf16[4,2,64,256]{3,2,1,0:T(8,128)(2,1)S(1)}, bf16[4,2,64,256]{3,2,1,0:T(8,128)(2,1)S(1)}, u32[]{:S(2)}, u32[]{:S(2)}) %collective-permute-start.7) | collective-permute-done | bytes 262176 | tf_op jit(solution)/shard_map/ppermute | solution.py:33
  23.7 0.0 collective-permute-start.8
  23.7 0.1 pad_add_fusion.place_ref
  23.8 3.2 %collective-permute-done.refs_2_ = bf16[2,64,1024]{2,1,0:T(8,128)(2,1)S(1)} collective-permute-done((bf16[2,64,1024]{2,1,0:T(8,128)(2,1)}, bf16[2,64,1024]{2,1,0:T(8,128)(2,1)S(1)}, u32[]{:S(2)}, u32[]{:S(2)}) %collective-permute-start) | collective-permute-done | bytes 262176 | tf_op jit(solution)/shard_map/ppermute | solution.py:33
  27.0 0.0 collective-permute-done.6.refs_4_
  27.0 0.0 collective-permute-done.8.refs_6_
  27.0 0.0 copy-done
  27.0 0.0 copy-done.1
  27.0 0.0 copy-done.4
  27.0 10.3 %attend.1 = (bf16[2,64,1024]{2,1,0:T(8,128)(2,1)S(1)}, bf16[2,64,1024]{2,1,0:T(8,128)(2,1)S(1)}, bf16[4,2,64,256]{3,2,1,0:T(8,128)(2,1)S(1)}, bf16[4,2,64,256]{3...) custom-call(s32[16]{0:T(128)S(1)} %copy-done.4, ...), custom_call_target="tpu_custom_call" | custom-call | tf_op jit(solution)/shard_map/attend/pallas_call | solution.py:233
  37.3 0.1 collective-permute-start.10
  37.4 0.5 collective-permute-start.11
  37.9 1.0 %collective-permute-done.10.refs_1_ = bf16[4,2,64,256]{3,2,1,0:T(8,128)(2,1)S(1)} collective-permute-done((bf16[4,2,64,256]{3,2,1,0:T(8,128)(2,1)S(1)}, bf16[4,2,64,256]{3,2,1,0:T(8,128)(2,1)S(1)}, u32[]{:S(2)}, u32[]{:S(2)}) %collective-permute-start.10) | collective-permute-done | bytes 262176 | tf_op jit(solution)/shard_map/ppermute | solution.py:33
  38.9 0.4 collective-permute-done.11.refs_3_
  39.3 0.1 sum_cores.1
  39.4 0.6 collective-permute-start.12
  40.0 0.3 collective-permute-start.9
  40.3 7.6 %collective-permute-done.12.refs_1_ = bf16[4,2,64,256]{3,2,1,0:T(8,128)(2,1)S(1)} collective-permute-done((bf16[4,2,64,256]{3,2,1,0:T(8,128)(2,1)S(1)}, bf16[4,2,64,256]{3,2,1,0:T(8,128)(2,1)S(1)}, u32[]{:S(2)}, u32[]{:S(2)}) %collective-permute-start.12) | collective-permute-done | bytes 262176 | tf_op jit(solution)/shard_map/ppermute | solution.py:33
  47.8 0.1 sum_heads.1
  47.9 0.3 collective-permute-start.13
  48.2 2.3 %collective-permute-start.14 = (bf16[2,64,256]{2,1,0:T(8,128)(2,1)S(1)}, bf16[2,64,256]{2,1,0:T(8,128)(2,1)S(1)}, u32[]{:S(2)}, u32[]{:S(2)}) collective-permute-start(bf16[2,64,256]{2,1,0:T(8,128)(2,1)S(1)} %get-tuple-element.34), channel_id=1, source_target_pairs={{0,4},{1,5},{2,6},{3,7},{4,0},{5,1},{6,2},{7,3},{8,12},{9,13},{10,... | collective-permute-start | bytes 196616 | tf_op jit(solution)/shard_map/ppermute | solution.py:33
  50.6 1.8 %collective-permute-start.15 = (bf16[2,64,256]{2,1,0:T(8,128)(2,1)S(1)}, bf16[2,64,256]{2,1,0:T(8,128)(2,1)S(1)}, u32[]{:S(2)}, u32[]{:S(2)}) collective-permute-start(bf16[2,64,256]{2,1,0:T(8,128)(2,1)S(1)} %get-tuple-element.35), channel_id=1, source_target_pairs={{0,6},{1,7},{2,4},{3,5},{4,2},{5,3},{6,0},{7,1},{8,14},{9,15},{10,... | collective-permute-start | bytes 196616 | tf_op jit(solution)/shard_map/ppermute | solution.py:33
  52.4 0.0 collective-permute-done.13.refs_1_
  52.4 3.1 %collective-permute-done.14.refs_2_ = bf16[2,64,256]{2,1,0:T(8,128)(2,1)S(1)} collective-permute-done((bf16[2,64,256]{2,1,0:T(8,128)(2,1)S(1)}, bf16[2,64,256]{2,1,0:T(8,128)(2,1)S(1)}, u32[]{:S(2)}, u32[]{:S(2)}) %collective-permute-start.14) | collective-permute-done | bytes 65568 | tf_op jit(solution)/shard_map/ppermute | solution.py:33
  55.5 1.2 %collective-permute-done.15.refs_3_ = bf16[2,64,256]{2,1,0:T(8,128)(2,1)S(1)} collective-permute-done((bf16[2,64,256]{2,1,0:T(8,128)(2,1)S(1)}, bf16[2,64,256]{2,1,0:T(8,128)(2,1)S(1)}, u32[]{:S(2)}, u32[]{:S(2)}) %collective-permute-start.15) | collective-permute-done | bytes 65568 | tf_op jit(solution)/shard_map/ppermute | solution.py:33
  56.8 0.2 collective-permute-start.16
  57.0 0.0 collective-permute-done.9.refs_1_
  57.0 0.8 %finish_q.1 = (bf16[64,2048]{1,0:T(8,128)(2,1)}, bf16[64,2048]{1,0:T(8,128)(2,1)}) custom-call(s32[1]{0:T(128)} %bitcast.group_ref, bf16[2,64,1024]{2,1,0:T(8,128)(2,1)S(1)} %get-tuple-element.22.refs_0_, bf16[2,64,1024]{2,1,0:T(8,128)(2,1)S(1)} %collective-permute-done.9.refs_1_), custom_call_target="tpu_custom_call" | custom-call | tf_op jit(solution)/shard_map/finish_q/pallas_call | solution.py:233
  57.8 3.0 %collective-permute-done.16.refs_1_ = bf16[64,256]{1,0:T(8,128)(2,1)S(1)} collective-permute-done((bf16[64,256]{1,0:T(8,128)(2,1)S(1)}, bf16[64,256]{1,0:T(8,128)(2,1)S(1)}, u32[]{:S(2)}, u32[]{:S(2)}) %collective-permute-start.16) | collective-permute-done | bytes 32800 | tf_op jit(solution)/shard_map/ppermute | solution.py:33
  60.7 0.6 %finish_kv.1 = (bf16[64,256]{1,0:T(8,128)(2,1)}, bf16[64,256]{1,0:T(8,128)(2,1)}) custom-call(s32[1]{0:T(128)} %bitcast.group_ref, bf16[64,256]{1,0:T(8,128)(2,1)S(1)} %get-tuple-element.36.refs_0_, bf16[64,256]{1,0:T(8,128)(2,1)S(1)} %collective-permute-done.16.refs_1_), custom_call_target="tpu_custom_call" | custom-call | tf_op jit(solution)/shard_map/finish_kv/pallas_call | solution.py:233
  (7 shorter events, 0.1 us)
Async XLA Ops:
  0.6 3.1 %copy-start.2 = (bf16[2,32,256]{2,1,0:T(8,128)(2,1)S(1)}, bf16[2,32,256]{2,1,0:T(8,128)(2,1)}, u32[]{:S(2)}) copy-start(bf16[2,32,256]{2,1,0:T(8,128)(2,1)} %param.6) | copy-start | bytes 98308
  0.6 5.1 %collective-permute-start.1 = (bf16[64,256]{1,0:T(8,128)(2,1)}, bf16[64,256]{1,0:T(8,128)(2,1)S(1)}, u32[]{:S(2)}, u32[]{:S(2)}) collective-permute-start(bf16[64,256]{1,0:T(8,128)(2,1)} %bitcast.20), channel_id=1, source_target_pairs={{0,8},{8,0},{16,24},{24,16},{1,9},{9,1},{17,25},{25,17},{2,10},{10... | collective-permute-start | bytes 98312 | tf_op jit(solution)/shard_map/ppermute | solution.py:33
  3.6 4.1 %collective-permute-start.2 = (bf16[64,256]{1,0:T(8,128)(2,1)}, bf16[64,256]{1,0:T(8,128)(2,1)S(1)}, u32[]{:S(2)}, u32[]{:S(2)}) collective-permute-start(bf16[64,256]{1,0:T(8,128)(2,1)} %bitcast.22), channel_id=1, source_target_pairs={{0,8},{8,0},{16,24},{24,16},{1,9},{9,1},{17,25},{25,17},{2,10},{10... | collective-permute-start | bytes 98312 | tf_op jit(solution)/shard_map/ppermute | solution.py:33
  3.7 0.8 %copy-start.3 = (bf16[2,32,256]{2,1,0:T(8,128)(2,1)S(1)}, bf16[2,32,256]{2,1,0:T(8,128)(2,1)}, u32[]{:S(2)}) copy-start(bf16[2,32,256]{2,1,0:T(8,128)(2,1)} %param.7) | copy-start | bytes 98308
  7.8 6.3 %collective-permute-start.5 = (bf16[2,64,256]{2,1,0:T(8,128)(2,1)S(1)}, bf16[2,64,256]{2,1,0:T(8,128)(2,1)S(1)}, u32[]{:S(2)}, u32[]{:S(2)}) collective-permute-start(bf16[2,64,256]{2,1,0:T(8,128)(2,1)S(1)} %pack_kv.1), channel_id=1, source_target_pairs={{0,6},{1,7},{2,4},{3,5},{4,2},{5,3},{6,0},{7,1},{8,14},{9,15},{10,... | collective-permute-start | bytes 196616 | tf_op jit(solution)/shard_map/ppermute | solution.py:33
  11.5 5.4 %collective-permute-start.4 = (bf16[2,64,256]{2,1,0:T(8,128)(2,1)S(1)}, bf16[2,64,256]{2,1,0:T(8,128)(2,1)S(1)}, u32[]{:S(2)}, u32[]{:S(2)}) collective-permute-start(bf16[2,64,256]{2,1,0:T(8,128)(2,1)S(1)} %pack_kv.1), channel_id=1, source_target_pairs={{0,4},{1,5},{2,6},{3,7},{4,0},{5,1},{6,2},{7,3},{8,12},{9,13},{10,... | collective-permute-start | bytes 196616 | tf_op jit(solution)/shard_map/ppermute | solution.py:33
  11.5 5.4 %collective-permute-start.3 = (bf16[2,64,256]{2,1,0:T(8,128)(2,1)S(1)}, bf16[2,64,256]{2,1,0:T(8,128)(2,1)S(1)}, u32[]{:S(2)}, u32[]{:S(2)}) collective-permute-start(bf16[2,64,256]{2,1,0:T(8,128)(2,1)S(1)} %pack_kv.1), channel_id=1, source_target_pairs={{0,2},{1,3},{2,0},{3,1},{4,6},{5,7},{6,4},{7,5},{8,10},{9,11},{10,... | collective-permute-start | bytes 196616 | tf_op jit(solution)/shard_map/ppermute | solution.py:33
  16.9 6.9 %collective-permute-start.7 = (bf16[4,2,64,256]{3,2,1,0:T(8,128)(2,1)S(1)}, bf16[4,2,64,256]{3,2,1,0:T(8,128)(2,1)S(1)}, u32[]{:S(2)}, u32[]{:S(2)}) collective-permute-start(bf16[4,2,64,256]{3,2,1,0:T(8,128)(2,1)S(1)} %pad_maximum_fusion.refs_3_), channel_id=1, source_target_pairs={{0,16},{8,24},{16,0},{24,8},{1,17},{9,25},{17,1},{25,9},{2,18},{10... | collective-permute-start | bytes 786440 | tf_op jit(solution)/shard_map/ppermute | solution.py:33
  18.4 8.5 %copy-start = (bf16[2,32,2048]{2,1,0:T(8,128)(2,1)S(1)}, bf16[2,32,2048]{2,1,0:T(8,128)(2,1)}, u32[]{:S(2)}) copy-start(bf16[2,32,2048]{2,1,0:T(8,128)(2,1)} %param.5) | copy-start | bytes 786436
  18.4 8.5 %copy-start.1 = (bf16[2,32,2048]{2,1,0:T(8,128)(2,1)S(1)}, bf16[2,32,2048]{2,1,0:T(8,128)(2,1)}, u32[]{:S(2)}) copy-start(bf16[2,32,2048]{2,1,0:T(8,128)(2,1)} %param.8) | copy-start | bytes 786436
  20.3 6.7 %collective-permute-start = (bf16[2,64,1024]{2,1,0:T(8,128)(2,1)}, bf16[2,64,1024]{2,1,0:T(8,128)(2,1)S(1)}, u32[]{:S(2)}, u32[]{:S(2)}) collective-permute-start(bf16[2,64,1024]{2,1,0:T(8,128)(2,1)} %pack_q.1), channel_id=1, source_target_pairs={{0,8},{8,0},{16,24},{24,16},{1,9},{9,1},{17,25},{25,17},{2,10},{10... | collective-permute-start | bytes 786440 | tf_op jit(solution)/shard_map/ppermute | solution.py:33
  20.6 6.4 %collective-permute-start.6 = (bf16[4,2,64,256]{3,2,1,0:T(8,128)(2,1)S(1)}, bf16[4,2,64,256]{3,2,1,0:T(8,128)(2,1)S(1)}, u32[]{:S(2)}, u32[]{:S(2)}) collective-permute-start(bf16[4,2,64,256]{3,2,1,0:T(8,128)(2,1)S(1)} %pad_maximum_fusion.refs_3_), channel_id=1, source_target_pairs={{0,1},{1,0},{2,3},{3,2},{4,5},{5,4},{6,7},{7,6},{8,9},{9,8},{10,11... | collective-permute-start | bytes 786440 | tf_op jit(solution)/shard_map/ppermute | solution.py:33
  23.7 3.3 %collective-permute-start.8 = (bf16[4,2,64,256]{3,2,1,0:T(8,128)(2,1)S(1)}, bf16[4,2,64,256]{3,2,1,0:T(8,128)(2,1)S(1)}, u32[]{:S(2)}, u32[]{:S(2)}) collective-permute-start(bf16[4,2,64,256]{3,2,1,0:T(8,128)(2,1)S(1)} %collective-permute-done.7.refs_5_), channel_id=1, source_target_pairs={{0,1},{1,0},{2,3},{3,2},{4,5},{5,4},{6,7},{7,6},{8,9},{9,8},{10,11... | collective-permute-start | bytes 786440 | tf_op jit(solution)/shard_map/ppermute | solution.py:33
  23.7 3.3 %copy-start.4 = (s32[16]{0:T(128)S(1)}, s32[16]{0:T(128)}, u32[]{:S(2)}) copy-start(s32[16]{0:T(128)} %order_ref.1) | copy-start | bytes 196
  37.3 1.6 %collective-permute-start.10 = (bf16[4,2,64,256]{3,2,1,0:T(8,128)(2,1)S(1)}, bf16[4,2,64,256]{3,2,1,0:T(8,128)(2,1)S(1)}, u32[]{:S(2)}, u32[]{:S(2)}) collective-permute-start(bf16[4,2,64,256]{3,2,1,0:T(8,128)(2,1)S(1)} %get-tuple-element.27), channel_id=1, source_target_pairs={{0,1},{1,0},{2,3},{3,2},{4,5},{5,4},{6,7},{7,6},{8,9},{9,8},{10,11... | collective-permute-start | bytes 786440 | tf_op jit(solution)/shard_map/ppermute | solution.py:33
  37.4 1.9 %collective-permute-start.11 = (bf16[4,2,64,256]{3,2,1,0:T(8,128)(2,1)S(1)}, bf16[4,2,64,256]{3,2,1,0:T(8,128)(2,1)S(1)}, u32[]{:S(2)}, u32[]{:S(2)}) collective-permute-start(bf16[4,2,64,256]{3,2,1,0:T(8,128)(2,1)S(1)} %get-tuple-element.29), channel_id=1, source_target_pairs={{0,1},{1,0},{2,3},{3,2},{4,5},{5,4},{6,7},{7,6},{8,9},{9,8},{10,11... | collective-permute-start | bytes 786440 | tf_op jit(solution)/shard_map/ppermute | solution.py:33
  39.4 8.4 %collective-permute-start.12 = (bf16[4,2,64,256]{3,2,1,0:T(8,128)(2,1)S(1)}, bf16[4,2,64,256]{3,2,1,0:T(8,128)(2,1)S(1)}, u32[]{:S(2)}, u32[]{:S(2)}) collective-permute-start(bf16[4,2,64,256]{3,2,1,0:T(8,128)(2,1)S(1)} %get-tuple-element.31), channel_id=1, source_target_pairs={{0,16},{8,24},{16,0},{24,8},{1,17},{9,25},{17,1},{25,9},{2,18},{10... | collective-permute-start | bytes 786440 | tf_op jit(solution)/shard_map/ppermute | solution.py:33
  40.0 17.0 %collective-permute-start.9 = (bf16[2,64,1024]{2,1,0:T(8,128)(2,1)S(1)}, bf16[2,64,1024]{2,1,0:T(8,128)(2,1)S(1)}, u32[]{:S(2)}, u32[]{:S(2)}) collective-permute-start(bf16[2,64,1024]{2,1,0:T(8,128)(2,1)S(1)} %get-tuple-element.23), channel_id=1, source_target_pairs={{0,8},{8,0},{16,24},{24,16},{1,9},{9,1},{17,25},{25,17},{2,10},{10... | collective-permute-start | bytes 786440 | tf_op jit(solution)/shard_map/ppermute | solution.py:33
  47.9 4.5 %collective-permute-start.13 = (bf16[2,64,256]{2,1,0:T(8,128)(2,1)S(1)}, bf16[2,64,256]{2,1,0:T(8,128)(2,1)S(1)}, u32[]{:S(2)}, u32[]{:S(2)}) collective-permute-start(bf16[2,64,256]{2,1,0:T(8,128)(2,1)S(1)} %get-tuple-element.33), channel_id=1, source_target_pairs={{0,2},{1,3},{2,0},{3,1},{4,6},{5,7},{6,4},{7,5},{8,10},{9,11},{10,... | collective-permute-start | bytes 196616 | tf_op jit(solution)/shard_map/ppermute | solution.py:33
  48.2 7.2 %collective-permute-start.14 = (bf16[2,64,256]{2,1,0:T(8,128)(2,1)S(1)}, bf16[2,64,256]{2,1,0:T(8,128)(2,1)S(1)}, u32[]{:S(2)}, u32[]{:S(2)}) collective-permute-start(bf16[2,64,256]{2,1,0:T(8,128)(2,1)S(1)} %get-tuple-element.34), channel_id=1, source_target_pairs={{0,4},{1,5},{2,6},{3,7},{4,0},{5,1},{6,2},{7,3},{8,12},{9,13},{10,... | collective-permute-start | bytes 196616 | tf_op jit(solution)/shard_map/ppermute | solution.py:33
  50.6 6.2 %collective-permute-start.15 = (bf16[2,64,256]{2,1,0:T(8,128)(2,1)S(1)}, bf16[2,64,256]{2,1,0:T(8,128)(2,1)S(1)}, u32[]{:S(2)}, u32[]{:S(2)}) collective-permute-start(bf16[2,64,256]{2,1,0:T(8,128)(2,1)S(1)} %get-tuple-element.35), channel_id=1, source_target_pairs={{0,6},{1,7},{2,4},{3,5},{4,2},{5,3},{6,0},{7,1},{8,14},{9,15},{10,... | collective-permute-start | bytes 196616 | tf_op jit(solution)/shard_map/ppermute | solution.py:33
  56.8 4.0 %collective-permute-start.16 = (bf16[64,256]{1,0:T(8,128)(2,1)S(1)}, bf16[64,256]{1,0:T(8,128)(2,1)S(1)}, u32[]{:S(2)}, u32[]{:S(2)}) collective-permute-start(bf16[64,256]{1,0:T(8,128)(2,1)S(1)} %get-tuple-element.37), channel_id=1, source_target_pairs={{0,8},{8,0},{16,24},{24,16},{1,9},{9,1},{17,25},{25,17},{2,10},{10... | collective-permute-start | bytes 98312 | tf_op jit(solution)/shard_map/ppermute | solution.py:33

commit v4 on v3

v4 whole, which is shorter than its diff:
```python
import functools
import math

import jax
import jax.numpy as jnp
from jax import lax
from jax.experimental import pallas as pl
from jax.experimental.pallas import tpu as pltpu
from jax.sharding import PartitionSpec as P

HD = 128
CORES = 2
BF = jnp.bfloat16
F32 = jnp.float32
LOWEST = -1e30
FLOOR = -1e29
SCALING = 1.0 / math.sqrt(HD)
EXPO = SCALING * math.log2(math.e)

VMEM = pl.BlockSpec(memory_space=pltpu.VMEM)
SMEM = pl.BlockSpec(memory_space=pltpu.SMEM)
HBM = pl.BlockSpec(memory_space=pltpu.HBM)


def swap(block, axis, mask):
    size = lax.axis_size(axis)
    return lax.ppermute(block, axis, [(i, i ^ mask) for i in range(size)])


def nbytes(arrays):
    return sum(math.prod(a.shape) * a.dtype.itemsize for a in arrays)


def after(blocks, earlier):
    return lax.optimization_barrier((tuple(blocks), tuple(earlier)))[0]


def call(kernel, name, ins, outs, specs=None, scratch=(), extra=0, flops=0):
    limit = nbytes(ins) + nbytes(outs) + extra + (12 << 20)
    return pl.pallas_call(
        kernel,
        out_shape=list(outs),
        in_specs=specs or [VMEM] * len(ins),
        out_specs=[VMEM] * len(outs),
        scratch_shapes=list(scratch),
        compiler_params=pltpu.CompilerParams(vmem_limit_bytes=min(limit, 60 << 20)),
        cost_estimate=pl.CostEstimate(
            flops=flops, bytes_accessed=nbytes(ins) + nbytes(outs), transcendentals=0
        ),
        name=name,
    )(*ins)


def dot(left, right):
    return jnp.dot(left, right, preferred_element_type=F32)


def dot_rows(left, right):
    return lax.dot_general(left, right, (((1,), (1,)), ((), ())), preferred_element_type=F32)


def pack_own_kernel(kv, group_ref, key_ref, value_ref, query_ref, grad_ref, *refs):
    out_ref, q_outs, refs = refs[0], refs[1 : kv + 1], refs[kv + 1 :]
    key_buf, value_buf, query_buf, grad_buf, sems = refs
    pairs = ((key_ref, key_buf), (value_ref, value_buf), (query_ref, query_buf), (grad_ref, grad_buf))
    copies = [pltpu.make_async_copy(src, dst, sems.at[i]) for i, (src, dst) in enumerate(pairs)]
    for copy in copies:
        copy.start()
    for copy in copies:
        copy.wait()
    width = q_outs[0].shape[2]
    for g in range(kv):

        @pl.when(group_ref[0] == g)
        def _():
            cols = pl.ds(g * HD, HD)
            out_ref[:, :HD] = key_buf[:, cols]
            out_ref[:, HD:] = value_buf[:, cols]
            for s in range(kv):
                theirs = pl.ds((g ^ s) * width, width)
                q_outs[s][0] = query_buf[:, theirs]
                q_outs[s][1] = grad_buf[:, theirs]


def pack_kv_kernel(kv, group_ref, own_ref, *refs):
    out_ref = refs[-1]
    out_ref[0] = own_ref[...]
    for g in range(kv):

        @pl.when(group_ref[0] == g)
        def _():
            cols = pl.ds(g * HD, HD)
            for s in range(1, kv):
                out_ref[s, :, :HD] = refs[2 * s - 2][:, cols]
                out_ref[s, :, HD:] = refs[2 * s - 1][:, cols]


class Plan:
    def __init__(self, kv, block_len, block_rows, rows, group, cores, z_devices):
        self.kv, self.block_len, self.block_rows, self.rows = kv, block_len, block_rows, rows
        self.group, self.cores, self.z_devices = group, cores, z_devices
        self.blocks = rows // block_rows
        self.tile_rows = block_rows if block_rows % 16 == 0 else rows
        self.lanes = group * self.tile_rows
        self.query_rows = kv * group * rows
        self.chunk_keys = z_devices * kv * rows
        self.tiles = [(s, start) for s in range(kv) for start in range(0, rows, self.tile_rows)]

    def at(self, tile):
        return pl.ds(tile * self.lanes, self.lanes)

    def keys_at(self, i):
        return pl.ds(i * self.chunk_keys, self.chunk_keys)

    def gap(self, tile, info_ref):
        s, start = self.tiles[tile]
        head, ctx = info_ref[0], info_ref[1]
        row = lax.broadcasted_iota(jnp.int32, (1, self.lanes), 1) % self.tile_rows + start
        pos = jnp.zeros((1, self.lanes), jnp.int32)
        for b in range(start // self.block_rows, -(-(start + self.tile_rows) // self.block_rows)):
            first = info_ref[2 + ctx * self.blocks + b] * self.block_len + (head ^ s) * self.block_rows
            pos = jnp.where(row // self.block_rows == b, first + row % self.block_rows, pos)
        return pos - lax.broadcasted_iota(jnp.int32, (self.block_rows, self.lanes), 0)

    def masked(self, scores, gap, chunk, info_ref):
        head, ctx = info_ref[0], info_ref[1]
        a, core = divmod(chunk, self.cores)
        for j in range(self.chunk_keys // self.block_rows):
            m, rest = divmod(j, self.kv * self.blocks)
            s, b = divmod(rest, self.blocks)
            stored = (ctx ^ (m * self.cores + core)) * self.blocks + b
            first = info_ref[2 + stored] * self.block_len + (head ^ (a * self.kv + s)) * self.block_rows
            part = scores[j * self.block_rows : (j + 1) * self.block_rows]
            yield j * self.block_rows, jnp.where(gap >= first, part, LOWEST)

    def turn(self, kv_refs, turned_ref):
        for i, ref in enumerate(kv_refs):
            turned_ref[:, self.keys_at(i)] = ref[...].reshape(self.chunk_keys, 2 * HD).T

    def keys(self, ref):
        return ref[:, :, :, :HD].reshape(self.chunk_keys, HD)

    def values(self, ref):
        return ref[:, :, :, HD:].reshape(self.chunk_keys, HD)

    def fold(self, block):
        return block.reshape(block.shape[0] // 8, 8, self.lanes)

    def scores(self, tile, first_chunk, kv_refs, q, e_ref, cols, info_ref):
        gap = self.gap(tile, info_ref)
        top = jnp.full((8, self.lanes), FLOOR, F32)
        for i, ref in enumerate(kv_refs):
            scores = dot_rows(self.keys(ref), q)
            for row, part in self.masked(scores, gap, first_chunk + i, info_ref):
                e_ref[pl.ds(i * self.chunk_keys + row, part.shape[0]), cols] = part
                top = jnp.maximum(top, jnp.max(self.fold(part), axis=0))
        return jnp.max(top, axis=0, keepdims=True)

    def exponents(self, count, e_ref, cols, top):
        total = jnp.zeros((8, self.lanes), F32)
        for i in range(count):
            part = jnp.exp2(e_ref[self.keys_at(i), cols] * EXPO - top * EXPO)
            e_ref[self.keys_at(i), cols] = part
            total = total + jnp.sum(self.fold(part), axis=0)
        return jnp.sum(total, axis=0, keepdims=True)

    def store_heads(self, out_ref, tile, turned):
        s, start = self.tiles[tile]
        block = turned.T.astype(BF)
        for n in range(self.group):
            piece = block[n * self.tile_rows : (n + 1) * self.tile_rows]
            out_ref[pl.ds(start, self.tile_rows), pl.ds(n * HD, HD)] = piece

    def back(self, kv_refs, dkv_refs, p_ref, ds_ref, q_ref, do_ref):
        shape = (self.z_devices, self.kv, self.rows, HD)
        for i, out_ref in enumerate(dkv_refs):
            k_grad = dot(ds_ref[self.keys_at(i), :], q_ref[...])
            v_grad = dot(p_ref[self.keys_at(i), :], do_ref[...])
            out_ref[:, :, :, :HD] = k_grad.astype(BF).reshape(shape)
            out_ref[:, :, :, HD:] = v_grad.astype(BF).reshape(shape)


def near_kernel(plan, info_ref, *refs):
    kv, chunks = plan.kv, plan.cores
    q_parts, refs = refs[:kv], refs[kv:]
    kv_refs, refs = refs[:chunks], refs[chunks:]
    q_all, do_all, e_ref, top_ref, sum_ref, mix_ref, turned_ref = refs
    plan.turn(kv_refs, turned_ref)
    for tile, (s, start) in enumerate(plan.tiles):
        span = pl.ds(start, plan.tile_rows)
        for n in range(plan.group):
            at = pl.ds(tile * plan.lanes + n * plan.tile_rows, plan.tile_rows)
            q_all[at, :] = q_parts[s][0, span, pl.ds(n * HD, HD)]
            do_all[at, :] = q_parts[s][1, span, pl.ds(n * HD, HD)]
    for tile in range(len(plan.tiles)):
        at = plan.at(tile)
        top = plan.scores(tile, 0, kv_refs, q_all[at, :], e_ref, at, info_ref)
        top_ref[:, at] = top
        sum_ref[:, at] = plan.exponents(chunks, e_ref, at, top)
        mixed = jnp.zeros((HD, plan.lanes), F32)
        for i in range(chunks):
            weights = e_ref[plan.keys_at(i), at].astype(BF)
            mixed = mixed + dot(turned_ref[pl.ds(HD, HD), plan.keys_at(i)], weights)
        mix_ref[:, at] = mixed


def far_kernel(plan, chunks, info_ref, q_all, do_all, near_top, near_sum, near_mix, *refs):
    kv = plan.kv
    kv_refs, refs = refs[:chunks], refs[chunks:]
    att_refs, refs = refs[:kv], refs[kv:]
    near_scale, delta_ref, q_grad_ref = refs[:3]
    dkv_refs, refs = refs[3 : 3 + chunks], refs[3 + chunks :]
    turned_ref, e_ref, p_ref, ds_ref = refs
    here = pl.ds(0, plan.lanes)
    plan.turn(kv_refs, turned_ref)
    for tile, (s, _) in enumerate(plan.tiles):
        at = plan.at(tile)
        top = plan.scores(tile, plan.cores, kv_refs, q_all[at, :], e_ref, here, info_ref)
        top = jnp.maximum(top, near_top[:, at])
        total = plan.exponents(chunks, e_ref, here, top)
        factor = jnp.exp2((near_top[:, at] - top) * EXPO)
        inverse = 1.0 / (total + factor * near_sum[:, at])
        near_scale[:, at] = factor * inverse
        mixed = near_mix[:, at] * (factor * inverse)
        for i in range(chunks):
            probs = (e_ref[plan.keys_at(i), here] * inverse).astype(BF)
            p_ref[plan.keys_at(i), at] = probs
            mixed = mixed + dot(turned_ref[pl.ds(HD, HD), plan.keys_at(i)], probs)
        plan.store_heads(att_refs[s], tile, mixed)
        do = do_all[at, :]
        delta = jnp.sum(do.astype(F32).T * mixed.astype(BF).astype(F32), axis=0, keepdims=True)
        delta_ref[:, at] = delta
        q_grad = jnp.zeros((HD, plan.lanes), F32)
        for i, ref in enumerate(kv_refs):
            probs = e_ref[plan.keys_at(i), here] * inverse
            grad_s = (probs * (dot_rows(plan.values(ref), do) - delta)).astype(BF)
            ds_ref[plan.keys_at(i), at] = grad_s
            q_grad = q_grad + dot(turned_ref[pl.ds(0, HD), plan.keys_at(i)], grad_s)
        q_grad_ref[:, at] = q_grad
    plan.back(kv_refs, dkv_refs, p_ref, ds_ref, q_all, do_all)


def near_back_kernel(plan, chunk, q_all, do_all, e_ref, near_scale, delta_ref, q_grad_in, kv_ref, *refs):
    outs, (dkv_ref, turned_ref, p_ref, ds_ref) = refs[:-4], refs[-4:]
    plan.turn([kv_ref], turned_ref)
    for tile, (s, _) in enumerate(plan.tiles):
        at = plan.at(tile)
        do = do_all[at, :]
        probs = e_ref[plan.keys_at(chunk), at] * near_scale[:, at]
        p_ref[:, at] = probs.astype(BF)
        grad_s = (probs * (dot_rows(plan.values(kv_ref), do) - delta_ref[:, at])).astype(BF)
        ds_ref[:, at] = grad_s
        q_grad = q_grad_in[:, at] + dot(turned_ref[pl.ds(0, HD), :], grad_s)
        if chunk == 0:
            plan.store_heads(outs[s], tile, q_grad * SCALING)
        else:
            outs[0][:, at] = q_grad
    plan.back([kv_ref], [dkv_ref], p_ref, ds_ref, q_all, do_all)


def add_kernel(*refs):
    total = refs[0][...].astype(F32)
    for ref in refs[1:-1]:
        total = total + ref[...].astype(F32)
    refs[-1][...] = total.astype(BF)


def sum_heads_kernel(parts, *refs):
    for m_z, out_ref in enumerate(refs[parts:]):
        total = refs[0][m_z].astype(F32)
        for ref in refs[1:parts]:
            total = total + ref[m_z].astype(F32)
        out_ref[...] = total.astype(BF)


def sum_z_kernel(kv, *refs):
    ins, outs = refs[:-kv], refs[-kv:]
    for s, out_ref in enumerate(outs):
        total = ins[0][s].astype(F32)
        for ref in ins[1:]:
            total = total + ref[s].astype(F32)
        out_ref[...] = total.astype(BF)


def finish_kv_kernel(kv, group_ref, *refs):
    key_ref, value_ref = refs[kv:]
    for g in range(kv):

        @pl.when(group_ref[0] == g)
        def _():
            for s in range(kv):
                cols = pl.ds((g ^ s) * HD, HD)
                key_ref[:, cols] = (refs[s][:, :HD].astype(F32) * SCALING).astype(BF)
                value_ref[:, cols] = refs[s][:, HD:]


def finish_q_kernel(kv, group_ref, *refs):
    att_ref, grad_ref = refs[2 * kv :]
    width = refs[0].shape[1]
    for g in range(kv):

        @pl.when(group_ref[0] == g)
        def _():
            for s in range(kv):
                cols = pl.ds((g ^ s) * width, width)
                att_ref[:, cols] = refs[s][...]
                grad_ref[:, cols] = refs[kv + s][...]


def shards(queries, key_vectors, value_vectors, out_grad, block_order):
    heads_devices = lax.axis_size("head")
    ctx_devices = lax.axis_size("ctx")
    halves, block_rows, query_width = queries.shape
    kv = key_vectors.shape[2] // HD
    rows = halves * block_rows
    width = query_width // kv
    cores = CORES if ctx_devices % CORES == 0 else 1
    z_devices = ctx_devices // cores
    spans = heads_devices // kv
    plan = Plan(kv, block_rows * heads_devices, block_rows, rows, width // HD, cores, z_devices)
    head = lax.axis_index("head").astype(jnp.int32)
    place = jnp.stack([head, lax.axis_index("ctx").astype(jnp.int32)])
    info = jnp.concatenate([place, block_order])
    own_group = (head % kv).reshape(1)
    queries = queries.reshape(rows, query_width)
    out_grad = out_grad.reshape(rows, query_width)
    key_vectors = key_vectors.reshape(rows, kv * HD)
    value_vectors = value_vectors.reshape(rows, kv * HD)

    def bf(*dims):
        return jax.ShapeDtypeStruct(dims, BF)

    def f32(*dims):
        return jax.ShapeDtypeStruct(dims, F32)

    def with_swaps(blocks):
        return [blocks[0]] + [swap(blocks[s], "head", s) for s in range(1, kv)]

    key_parts = [swap(key_vectors, "head", s) for s in range(1, kv)]
    value_parts = [swap(value_vectors, "head", s) for s in range(1, kv)]
    own, *q_parts = pl.pallas_call(
        functools.partial(pack_own_kernel, kv),
        out_shape=[bf(rows, 2 * HD)] + [bf(2, rows, width)] * kv,
        in_specs=[SMEM] + [HBM] * 4,
        out_specs=[VMEM] * (kv + 1),
        scratch_shapes=[pltpu.VMEM((rows, kv * HD), BF)] * 2
        + [pltpu.VMEM((rows, query_width), BF)] * 2
        + [pltpu.SemaphoreType.DMA((4,))],
        name="pack_own",
    )(own_group, key_vectors, value_vectors, queries, out_grad)
    q_parts = with_swaps(q_parts)
    piece = call(
        functools.partial(pack_kv_kernel, kv),
        "pack_kv",
        (own_group, own, *[part for pair in zip(key_parts, value_parts) for part in pair]),
        [bf(kv, rows, 2 * HD)],
        [SMEM] + [VMEM] * (2 * kv - 1),
    )[0]
    column = jnp.stack([piece] + [swap(piece, "ctx", m * cores) for m in range(1, z_devices)])
    columns = [swap(column, "head", a * kv) for a in range(1, spans)]
    near_kv = [column] + [swap(column, "ctx", core) for core in range(1, cores)]
    far_chunks = len(columns) * cores

    near_keys = len(near_kv) * plan.chunk_keys
    far_keys = far_chunks * plan.chunk_keys
    query_rows = plan.query_rows
    row = f32(1, query_rows)
    q_all, do_all, near_e, near_top, near_sum, near_mix = call(
        functools.partial(near_kernel, plan),
        "attend_near",
        (info, *q_parts, *near_kv),
        [bf(query_rows, HD)] * 2 + [f32(near_keys, query_rows), row, row, f32(HD, query_rows)],
        [SMEM] + [VMEM] * (kv + len(near_kv)),
        [pltpu.VMEM((2 * HD, near_keys), BF)],
        near_keys * 4 * HD,
        8 * near_keys * query_rows * HD,
    )
    columns = after(columns, [near_top])
    far_kv = []
    for part in columns:
        far_kv += [part] + [swap(part, "ctx", core) for core in range(1, cores)]
    outs = call(
        functools.partial(far_kernel, plan, len(far_kv)),
        "attend_far",
        (info, q_all, do_all, near_top, near_sum, near_mix, *far_kv),
        [bf(rows, width)] * kv
        + [row, row, f32(HD, query_rows)]
        + [bf(z_devices, kv, rows, 2 * HD)] * len(far_kv),
        [SMEM] + [VMEM] * (5 + len(far_kv)),
        [
            pltpu.VMEM((2 * HD, far_keys), BF),
            pltpu.VMEM((far_keys, plan.lanes), F32),
            pltpu.VMEM((far_keys, query_rows), BF),
            pltpu.VMEM((far_keys, query_rows), BF),
        ],
        far_keys * (4 * HD + 4 * plan.lanes + 4 * query_rows),
        16 * far_keys * query_rows * HD,
    )
    att_parts, outs = outs[:kv], outs[kv:]
    (near_scale, delta, far_q_grad), far_dkv = outs[:3], outs[3:]
    sums = []
    for a in range(spans - 1):
        parts = far_dkv[a * cores : (a + 1) * cores]
        swapped = [swap(parts[core], "ctx", core) for core in range(1, cores)]
        sums += call(add_kernel, "sum_cores", (parts[0], *swapped), [bf(*parts[0].shape)])
    near_dkv, q_grad = [], far_q_grad
    for chunk in reversed(range(cores)):
        q_outs = [f32(HD, query_rows)] if chunk else [bf(rows, width)] * kv
        outs = call(
            functools.partial(near_back_kernel, plan, chunk),
            "attend_near_back",
            (q_all, do_all, near_e, near_scale, delta, q_grad, near_kv[chunk]),
            q_outs + [bf(z_devices, kv, rows, 2 * HD)],
            None,
            [
                pltpu.VMEM((2 * HD, plan.chunk_keys), BF),
                pltpu.VMEM((plan.chunk_keys, query_rows), BF),
                pltpu.VMEM((plan.chunk_keys, query_rows), BF),
            ],
            plan.chunk_keys * (4 * HD + 4 * query_rows),
            12 * plan.chunk_keys * query_rows * HD,
        )
        q_grad = outs[0]
        near_dkv = [swap(outs[-1], "ctx", chunk) if chunk else outs[-1]] + near_dkv
    q_grad_parts = outs[:-1]
    sums = [swap(part, "head", (a + 1) * kv) for a, part in enumerate(sums)]
    sums = near_dkv + sums
    z_parts = call(
        functools.partial(sum_heads_kernel, len(sums)),
        "sum_heads",
        sums,
        [bf(kv, rows, 2 * HD)] * z_devices,
    )
    z_parts = [z_parts[0]] + [swap(z_parts[m], "ctx", m * cores) for m in range(1, z_devices)]
    pair_parts = call(
        functools.partial(sum_z_kernel, kv), "sum_z", z_parts, [bf(rows, 2 * HD)] * kv
    )
    pair_parts = with_swaps(pair_parts)
    attended, query_grad = call(
        functools.partial(finish_q_kernel, kv),
        "finish_q",
        (own_group, *with_swaps(att_parts), *with_swaps(q_grad_parts)),
        [bf(rows, query_width)] * 2,
        [SMEM] + [VMEM] * (2 * kv),
    )
    key_grad, value_grad = call(
        functools.partial(finish_kv_kernel, kv),
        "finish_kv",
        (own_group, *pair_parts),
        [bf(rows, kv * HD)] * 2,
        [SMEM] + [VMEM] * kv,
    )
    return (
        attended.reshape(halves, block_rows, query_width),
        query_grad.reshape(halves, block_rows, query_width),
        key_grad.reshape(halves, block_rows, kv * HD),
        value_grad.reshape(halves, block_rows, kv * HD),
    )


def solution(mesh):
    split = P("ctx", "head", None)
    return jax.shard_map(
        shards,
        mesh=mesh,
        in_specs=(split, split, split, split, P()),
        out_specs=(split, split, split, split),
        check_vma=False,
    )
```

time: 61.6 us -> 58.9 us (0.956)
  waiting for transfers between devices: 30.4 us -> 20.1 us
  starting transfers between devices: 15.5 us -> 18.7 us
  Pallas kernels: 13.8 us -> 16.6 us
  local copies, waits for them, and re-layouts: 0.8 us -> 1.71 us
  other arithmetic: 0.11 us -> 0.77 us
    ppermute x17 -> x18, waiting for transfers between devices: 30.4 us -> 20.1 us  [swap(): return lax.ppermute(block, axis, [(i, i ^ mask) for i in range(size)])]
    ppermute x17 -> x18, starting transfers between devices: 15.5 us -> 18.7 us  [swap(): return lax.ppermute(block, axis, [(i, i ^ mask) for i in range(size)])]
    pallas_call x9 -> x11, Pallas kernels: 13.8 us -> 16.6 us  [the longest x10 14.7 us: call(): pl.pallas_call(kernel, out_shape=list(outs), in_specs=specs or [VMEM] * l...]
    unnamed x10 -> x4, local copies, waits for them, and re-layouts: 0.8 us -> 1.71 us
    concatenate x0 -> x1, other arithmetic: none -> 0.73 us  [shards(): info = jnp.concatenate([place, block_order])]
  transfers between devices with their start and end apart: 17 -> 18, of which waited for: 12 -> 10; matrix products, arithmetic and copies ran while one was open for 0% -> 1% of each run, Pallas kernels for 4% -> 17%
where the time goes in v4:
time: 58.9 us; the launch traced here: 58.6 us
  waiting for transfers between devices  20.1 us (34%)
  starting transfers between devices  18.7 us (32%)
  Pallas kernels  16.6 us (28%)
  local copies, waits for them, and re-layouts  1.71 us (3%)
  other arithmetic  0.77 us (1%)
  between operations  0.72 us (1%)
    ppermute x18, waiting for transfers between devices, swap(): return lax.ppermute(block, axis, [(i, i ^ mask) for i in range(size)])  20.1 us
    ppermute x18, starting transfers between devices, swap(): return lax.ppermute(block, axis, [(i, i ^ mask) for i in range(size)])  18.7 us
    pallas_call x10, Pallas kernels, call(): pl.pallas_call(kernel, out_shape=list(outs), in_specs=specs or [VMEM] * l...  14.7 us
    pallas_call x1, Pallas kernels, shards(): pl.pallas_call(functools.partial(pack_own_kernel, kv), out_shape=[bf(rows...  1.94 us
    unnamed x4, local copies, waits for them, and re-layouts  1.71 us
  transfers between devices with their start and end apart: 18, of which 10 were waited for; matrix products, arithmetic and copies ran while one was open for 1% of the time, Pallas kernels for 17%

profile of v4, /device:TPU:0, one launch (start us, length us, event | category | flops | bytes accessed | tf_op | source)
XLA Modules:
  0.0 58.6 jit_solution(6675288445863154291)
XLA Ops:
  0.6 3.0 %collective-permute-start.1 = (bf16[64,256]{1,0:T(8,128)(2,1)}, bf16[64,256]{1,0:T(8,128)(2,1)S(1)}, u32[]{:S(2)}, u32[]{:S(2)}) collective-permute-start(bf16[64,256]{1,0:T(8,128)(2,1)} %bitcast.21), channel_id=1, source_target_pairs={{0,8},{8,0},{16,24},{24,16},{1,9},{9,1},{17,25},{25,17},{2,10},{10... | collective-permute-start | bytes 98312 | tf_op jit(solution)/shard_map/ppermute | solution.py:27
  3.6 0.1 collective-permute-start.2
  3.7 1.9 %pack_own.1 = (bf16[64,256]{1,0:T(8,128)(2,1)}, bf16[2,64,1024]{2,1,0:T(8,128)(2,1)}, bf16[2,64,1024]{2,1,0:T(8,128)(2,1)}) custom-call(s32[1]{0:T(128)} %bitcast.group_ref, bf16[64,256]{1,0:T(8,128)(2,1)} %bitcast.22, bf16[64,256]{1,0:T(8,128)(2,1)} %bitcast.24, bf16[64,2048]{1,0:T(8,128)(2,1)} %bitcast.16, bf16[64,2048]{1,0:T(8,128)(2,1)} %bitcast.17), custom_call_target="tpu_custom_call" | custom-call | tf_op jit(solution)/shard_map/pack_own/pallas_call | solution.py:341
  5.7 0.1 collective-permute-done.1.refs_0_
  5.7 2.0 %collective-permute-done.2.refs_1_ = bf16[64,256]{1,0:T(8,128)(2,1)S(1)} collective-permute-done((bf16[64,256]{1,0:T(8,128)(2,1)}, bf16[64,256]{1,0:T(8,128)(2,1)S(1)}, u32[]{:S(2)}, u32[]{:S(2)}) %collective-permute-start.2) | collective-permute-done | bytes 32800 | tf_op jit(solution)/shard_map/ppermute | solution.py:27
  7.8 0.8 %copy-done = bf16[64,256]{1,0:T(8,128)(2,1)S(1)} copy-done((bf16[64,256]{1,0:T(8,128)(2,1)S(1)}, bf16[64,256]{1,0:T(8,128)(2,1)}, u32[]{:S(2)}) %copy-start) | copy-done | bytes 32792
  8.5 3.7 %collective-permute-start.5 = (bf16[2,64,256]{2,1,0:T(8,128)(2,1)S(1)}, bf16[2,64,256]{2,1,0:T(8,128)(2,1)S(1)}, u32[]{:S(2)}, u32[]{:S(2)}) collective-permute-start(bf16[2,64,256]{2,1,0:T(8,128)(2,1)S(1)} %pack_kv.1), channel_id=1, source_target_pairs={{0,6},{1,7},{2,4},{3,5},{4,2},{5,3},{6,0},{7,1},{8,14},{9,15},{10,... | collective-permute-start | bytes 196616 | tf_op jit(solution)/shard_map/ppermute | solution.py:27
  12.2 0.0 collective-permute-start.4
  12.2 0.8 %collective-permute-start.3 = (bf16[2,64,256]{2,1,0:T(8,128)(2,1)S(1)}, bf16[2,64,256]{2,1,0:T(8,128)(2,1)S(1)}, u32[]{:S(2)}, u32[]{:S(2)}) collective-permute-start(bf16[2,64,256]{2,1,0:T(8,128)(2,1)S(1)} %pack_kv.1), channel_id=1, source_target_pairs={{0,2},{1,3},{2,0},{3,1},{4,6},{5,7},{6,4},{7,5},{8,10},{9,11},{10,... | collective-permute-start | bytes 196616 | tf_op jit(solution)/shard_map/ppermute | solution.py:27
  13.0 0.4 collective-permute-start
  13.4 1.4 %collective-permute-done.5 = bf16[2,64,256]{2,1,0:T(8,128)(2,1)S(1)} collective-permute-done((bf16[2,64,256]{2,1,0:T(8,128)(2,1)S(1)}, bf16[2,64,256]{2,1,0:T(8,128)(2,1)S(1)}, u32[]{:S(2)}, u32[]{:S(2)}) %collective-permute-start.5) | collective-permute-done | bytes 65568 | tf_op jit(solution)/shard_map/ppermute | solution.py:27
  14.8 2.7 %collective-permute-done.4 = bf16[2,64,256]{2,1,0:T(8,128)(2,1)S(1)} collective-permute-done((bf16[2,64,256]{2,1,0:T(8,128)(2,1)S(1)}, bf16[2,64,256]{2,1,0:T(8,128)(2,1)S(1)}, u32[]{:S(2)}, u32[]{:S(2)}) %collective-permute-start.4) | collective-permute-done | bytes 65568 | tf_op jit(solution)/shard_map/ppermute | solution.py:27
  17.6 0.0 collective-permute-done.3
  17.6 0.1 collective-permute-start.6
  17.7 1.6 %collective-permute-start.7 = (bf16[4,2,64,256]{3,2,1,0:T(8,128)(2,1)S(1)}, bf16[4,2,64,256]{3,2,1,0:T(8,128)(2,1)S(1)}, u32[]{:S(2)}, u32[]{:S(2)}) collective-permute-start(bf16[4,2,64,256]{3,2,1,0:T(8,128)(2,1)S(1)} %pad_maximum_fusion.refs_2_.kv_ref), channel_id=1, source_target_pairs={{0,16},{8,24},{16,0},{24,8},{1,17},{9,25},{17,1},{25,9},{2,18},{10... | collective-permute-start | bytes 786440 | tf_op jit(solution)/shard_map/ppermute | solution.py:27
  19.3 0.7 %pad_add_fusion.info_ref = s32[18]{0:T(128)S(1)} fusion(s32[16]{0:T(128)} %param.9, s32[1]{0:T(128)} %bitcast.2, s32[1]{0:T(128)} %bitcast.1), kind=kLoop, calls=%fused_computation.1 | loop fusion | flops 36 | bytes 144 | tf_op jit(solution)/shard_map/concatenate | solution.py:323
  20.0 0.0 collective-permute-done.refs_1_
  20.0 0.0 collective-permute-done.6.refs_3_.kv_ref
  20.0 0.9 %copy-done.1 = bf16[2,64,1024]{2,1,0:T(8,128)(2,1)S(1)} copy-done((bf16[2,64,1024]{2,1,0:T(8,128)(2,1)S(1)}, bf16[2,64,1024]{2,1,0:T(8,128)(2,1)}, u32[]{:S(2)}) %copy-start.1) | copy-done | bytes 262168
  21.0 3.3 %attend_near.1 = (bf16[1024,128]{1,0:T(8,128)(2,1)S(1)}, bf16[1024,128]{1,0:T(8,128)(2,1)S(1)}, f32[1024,1024]{1,0:T(8,128)S(1)}, f32[1,1024]{1,0:T(1,128)S(1)},...) custom-call(s32[18]{0:T(128)S(1)} %pad_add_fusion.info_ref, bf16[2,64,1024]{2,1,0:T(8,128)(2,1)S(1)} %copy-done.1, ...), custom_call_target="tpu_custom_call" | custom-call | flops 1073741824 | bytes 6299720 | tf_op jit(solution)/shard_map/attend_near/pallas_call | solution.py:40
  24.3 2.1 %collective-permute-done.7.refs_0_ = bf16[4,2,64,256]{3,2,1,0:T(8,128)(2,1)S(1)} collective-permute-done((bf16[4,2,64,256]{3,2,1,0:T(8,128)(2,1)S(1)}, bf16[4,2,64,256]{3,2,1,0:T(8,128)(2,1)S(1)}, u32[]{:S(2)}, u32[]{:S(2)}) %collective-permute-start.7) | collective-permute-done | bytes 262176 | tf_op jit(solution)/shard_map/ppermute | solution.py:27
  26.4 0.0 collective-permute-start.8
  26.4 1.5 %collective-permute-done.8.refs_1_ = bf16[4,2,64,256]{3,2,1,0:T(8,128)(2,1)S(1)} collective-permute-done((bf16[4,2,64,256]{3,2,1,0:T(8,128)(2,1)S(1)}, bf16[4,2,64,256]{3,2,1,0:T(8,128)(2,1)S(1)}, u32[]{:S(2)}, u32[]{:S(2)}) %collective-permute-start.8) | collective-permute-done | bytes 262176 | tf_op jit(solution)/shard_map/ppermute | solution.py:27
  28.0 6.0 %attend_far.1 = (bf16[64,1024]{1,0:T(8,128)(2,1)S(1)}, bf16[64,1024]{1,0:T(8,128)(2,1)S(1)}, f32[1,1024]{1,0:T(1,128)S(1)}, f32[1,1024]{1,0:T(1,128)S(1)}, f32[1...) custom-call(s32[18]{0:T(128)S(1)} %pad_add_fusion.info_ref, ...), custom_call_target="tpu_custom_call" | custom-call | flops 2147483648 | bytes 2900040 | tf_op jit(solution)/shard_map/attend_far/pallas_call | solution.py:40
  33.9 0.2 collective-permute-start.12
  34.1 1.9 %attend_near_back.2 = (f32[128,1024]{1,0:T(8,128)S(1)}, bf16[4,2,64,256]{3,2,1,0:T(8,128)(2,1)S(1)}) custom-call(bf16[1024,128]{1,0:T(8,128)(2,1)S(1)} %get-tuple-element.39.q_all, bf16[1024,128]{1,0:T(8,128)(2,1)S(1)} %get-tuple-element.40.do_all, f32[1024,1024]{1,0:T(8,128)S(1)} %get-tuple-element.47.e_ref, f32[1,1024]{1,0:T(1,128)S(1)} %get-tuple-element.48.near_scale, ...), custom_call_target="tpu_custom_call" | custom-call | flops 805306368 | bytes 6299648 | tf_op jit(solution)/shard_map/attend_near_back/pallas_call | solution.py:40
  36.0 0.4 collective-permute-start.11
  36.4 0.0 collective-permute-done.12.refs_1_
  36.4 0.1 sum_cores.1
  36.5 1.6 %collective-permute-start.13 = (bf16[4,2,64,256]{3,2,1,0:T(8,128)(2,1)S(1)}, bf16[4,2,64,256]{3,2,1,0:T(8,128)(2,1)S(1)}, u32[]{:S(2)}, u32[]{:S(2)}) collective-permute-start(bf16[4,2,64,256]{3,2,1,0:T(8,128)(2,1)S(1)} %sum_cores.1), channel_id=1, source_target_pairs={{0,16},{8,24},{16,0},{24,8},{1,17},{9,25},{17,1},{25,9},{2,18},{10... | collective-permute-start | bytes 786440 | tf_op jit(solution)/shard_map/ppermute | solution.py:27
  38.1 0.3 collective-permute-start.9
  38.4 1.9 %attend_near_back.3 = (bf16[64,1024]{1,0:T(8,128)(2,1)S(1)}, bf16[64,1024]{1,0:T(8,128)(2,1)S(1)}, bf16[4,2,64,256]{3,2,1,0:T(8,128)(2,1)S(1)}) custom-call(bf16[1024,128]{1,0:T(8,128)(2,1)S(1)} %get-tuple-element.39.q_all, bf16[1024,128]{1,0:T(8,128)(2,1)S(1)} %get-tuple-element.40.do_all, f32[1024,1024]{1,0:T(8,128)S(1)} %get-tuple-element.47.e_ref, ...), custom_call_target="tpu_custom_call" | custom-call | flops 805306368 | bytes 6037504 | tf_op jit(solution)/shard_map/attend_near_back/pallas_call | solution.py:40
  40.3 1.8 %collective-permute-start.10 = (bf16[64,1024]{1,0:T(8,128)(2,1)S(1)}, bf16[64,1024]{1,0:T(8,128)(2,1)S(1)}, u32[]{:S(2)}, u32[]{:S(2)}) collective-permute-start(bf16[64,1024]{1,0:T(8,128)(2,1)S(1)} %get-tuple-element.53), channel_id=1, source_target_pairs={{0,8},{8,0},{16,24},{24,16},{1,9},{9,1},{17,25},{25,17},{2,10},{10... | collective-permute-start | bytes 393224 | tf_op jit(solution)/shard_map/ppermute | solution.py:27
  42.1 0.0 collective-permute-done.11.refs_1_
  42.1 2.8 %collective-permute-done.13.refs_2_ = bf16[4,2,64,256]{3,2,1,0:T(8,128)(2,1)S(1)} collective-permute-done((bf16[4,2,64,256]{3,2,1,0:T(8,128)(2,1)S(1)}, bf16[4,2,64,256]{3,2,1,0:T(8,128)(2,1)S(1)}, u32[]{:S(2)}, u32[]{:S(2)}) %collective-permute-start.13) | collective-permute-done | bytes 262176 | tf_op jit(solution)/shard_map/ppermute | solution.py:27
  44.9 0.1 sum_heads.1
  45.0 0.4 collective-permute-start.14
  45.5 2.3 %collective-permute-start.15 = (bf16[2,64,256]{2,1,0:T(8,128)(2,1)S(1)}, bf16[2,64,256]{2,1,0:T(8,128)(2,1)S(1)}, u32[]{:S(2)}, u32[]{:S(2)}) collective-permute-start(bf16[2,64,256]{2,1,0:T(8,128)(2,1)S(1)} %get-tuple-element.62), channel_id=1, source_target_pairs={{0,4},{1,5},{2,6},{3,7},{4,0},{5,1},{6,2},{7,3},{8,12},{9,13},{10,... | collective-permute-start | bytes 196616 | tf_op jit(solution)/shard_map/ppermute | solution.py:27
  47.8 1.7 %collective-permute-start.16 = (bf16[2,64,256]{2,1,0:T(8,128)(2,1)S(1)}, bf16[2,64,256]{2,1,0:T(8,128)(2,1)S(1)}, u32[]{:S(2)}, u32[]{:S(2)}) collective-permute-start(bf16[2,64,256]{2,1,0:T(8,128)(2,1)S(1)} %get-tuple-element.63), channel_id=1, source_target_pairs={{0,6},{1,7},{2,4},{3,5},{4,2},{5,3},{6,0},{7,1},{8,14},{9,15},{10,... | collective-permute-start | bytes 196616 | tf_op jit(solution)/shard_map/ppermute | solution.py:27
  49.5 0.0 collective-permute-done.14.refs_1_
  49.5 3.1 %collective-permute-done.15.refs_2_ = bf16[2,64,256]{2,1,0:T(8,128)(2,1)S(1)} collective-permute-done((bf16[2,64,256]{2,1,0:T(8,128)(2,1)S(1)}, bf16[2,64,256]{2,1,0:T(8,128)(2,1)S(1)}, u32[]{:S(2)}, u32[]{:S(2)}) %collective-permute-start.15) | collective-permute-done | bytes 65568 | tf_op jit(solution)/shard_map/ppermute | solution.py:27
  52.6 1.4 %collective-permute-done.16.refs_3_ = bf16[2,64,256]{2,1,0:T(8,128)(2,1)S(1)} collective-permute-done((bf16[2,64,256]{2,1,0:T(8,128)(2,1)S(1)}, bf16[2,64,256]{2,1,0:T(8,128)(2,1)S(1)}, u32[]{:S(2)}, u32[]{:S(2)}) %collective-permute-start.16) | collective-permute-done | bytes 65568 | tf_op jit(solution)/shard_map/ppermute | solution.py:27
  54.0 0.3 collective-permute-start.17
  54.3 0.0 collective-permute-done.9.refs_1_
  54.3 0.0 collective-permute-done.10.refs_3_
  54.3 0.8 %finish_q.1 = (bf16[64,2048]{1,0:T(8,128)(2,1)}, bf16[64,2048]{1,0:T(8,128)(2,1)}) custom-call(s32[1]{0:T(128)} %bitcast.group_ref, bf16[64,1024]{1,0:T(8,128)(2,1)S(1)} %get-tuple-element.45.refs_0_, bf16[64,1024]{1,0:T(8,128)(2,1)S(1)} %collective-permute-done.9.refs_1_, bf16[64,1024]{1,0:T(8,128)(2,1)S(1)} %get-tuple-element.52.refs_2_, ...), custom_call_target="tpu_custom_call" | custom-call | bytes 1048580 | tf_op jit(solution)/shard_map/finish_q/pallas_call | solution.py:40
  55.1 2.8 %collective-permute-done.17.refs_1_ = bf16[64,256]{1,0:T(8,128)(2,1)S(1)} collective-permute-done((bf16[64,256]{1,0:T(8,128)(2,1)S(1)}, bf16[64,256]{1,0:T(8,128)(2,1)S(1)}, u32[]{:S(2)}, u32[]{:S(2)}) %collective-permute-start.17) | collective-permute-done | bytes 32800 | tf_op jit(solution)/shard_map/ppermute | solution.py:27
  58.0 0.6 %finish_kv.1 = (bf16[64,256]{1,0:T(8,128)(2,1)}, bf16[64,256]{1,0:T(8,128)(2,1)}) custom-call(s32[1]{0:T(128)} %bitcast.group_ref, bf16[64,256]{1,0:T(8,128)(2,1)S(1)} %get-tuple-element.64.refs_0_, bf16[64,256]{1,0:T(8,128)(2,1)S(1)} %collective-permute-done.17.refs_1_), custom_call_target="tpu_custom_call" | custom-call | bytes 131076 | tf_op jit(solution)/shard_map/finish_kv/pallas_call | solution.py:40
  (5 shorter events, 0.1 us)
Async XLA Ops:
  0.6 5.1 %collective-permute-start.1 = (bf16[64,256]{1,0:T(8,128)(2,1)}, bf16[64,256]{1,0:T(8,128)(2,1)S(1)}, u32[]{:S(2)}, u32[]{:S(2)}) collective-permute-start(bf16[64,256]{1,0:T(8,128)(2,1)} %bitcast.21), channel_id=1, source_target_pairs={{0,8},{8,0},{16,24},{24,16},{1,9},{9,1},{17,25},{25,17},{2,10},{10... | collective-permute-start | bytes 98312 | tf_op jit(solution)/shard_map/ppermute | solution.py:27
  3.6 4.1 %collective-permute-start.2 = (bf16[64,256]{1,0:T(8,128)(2,1)}, bf16[64,256]{1,0:T(8,128)(2,1)S(1)}, u32[]{:S(2)}, u32[]{:S(2)}) collective-permute-start(bf16[64,256]{1,0:T(8,128)(2,1)} %bitcast.23), channel_id=1, source_target_pairs={{0,8},{8,0},{16,24},{24,16},{1,9},{9,1},{17,25},{25,17},{2,10},{10... | collective-permute-start | bytes 98312 | tf_op jit(solution)/shard_map/ppermute | solution.py:27
  7.8 0.8 %copy-start = (bf16[64,256]{1,0:T(8,128)(2,1)S(1)}, bf16[64,256]{1,0:T(8,128)(2,1)}, u32[]{:S(2)}) copy-start(bf16[64,256]{1,0:T(8,128)(2,1)} %get-tuple-element.38.own_ref) | copy-start | bytes 98308
  8.5 6.3 %collective-permute-start.5 = (bf16[2,64,256]{2,1,0:T(8,128)(2,1)S(1)}, bf16[2,64,256]{2,1,0:T(8,128)(2,1)S(1)}, u32[]{:S(2)}, u32[]{:S(2)}) collective-permute-start(bf16[2,64,256]{2,1,0:T(8,128)(2,1)S(1)} %pack_kv.1), channel_id=1, source_target_pairs={{0,6},{1,7},{2,4},{3,5},{4,2},{5,3},{6,0},{7,1},{8,14},{9,15},{10,... | collective-permute-start | bytes 196616 | tf_op jit(solution)/shard_map/ppermute | solution.py:27
  12.2 5.4 %collective-permute-start.4 = (bf16[2,64,256]{2,1,0:T(8,128)(2,1)S(1)}, bf16[2,64,256]{2,1,0:T(8,128)(2,1)S(1)}, u32[]{:S(2)}, u32[]{:S(2)}) collective-permute-start(bf16[2,64,256]{2,1,0:T(8,128)(2,1)S(1)} %pack_kv.1), channel_id=1, source_target_pairs={{0,4},{1,5},{2,6},{3,7},{4,0},{5,1},{6,2},{7,3},{8,12},{9,13},{10,... | collective-permute-start | bytes 196616 | tf_op jit(solution)/shard_map/ppermute | solution.py:27
  12.2 5.4 %collective-permute-start.3 = (bf16[2,64,256]{2,1,0:T(8,128)(2,1)S(1)}, bf16[2,64,256]{2,1,0:T(8,128)(2,1)S(1)}, u32[]{:S(2)}, u32[]{:S(2)}) collective-permute-start(bf16[2,64,256]{2,1,0:T(8,128)(2,1)S(1)} %pack_kv.1), channel_id=1, source_target_pairs={{0,2},{1,3},{2,0},{3,1},{4,6},{5,7},{6,4},{7,5},{8,10},{9,11},{10,... | collective-permute-start | bytes 196616 | tf_op jit(solution)/shard_map/ppermute | solution.py:27
  13.0 7.0 %collective-permute-start = (bf16[2,64,1024]{2,1,0:T(8,128)(2,1)}, bf16[2,64,1024]{2,1,0:T(8,128)(2,1)S(1)}, u32[]{:S(2)}, u32[]{:S(2)}) collective-permute-start(bf16[2,64,1024]{2,1,0:T(8,128)(2,1)} %get-tuple-element.37), channel_id=1, source_target_pairs={{0,8},{8,0},{16,24},{24,16},{1,9},{9,1},{17,25},{25,17},{2,10},{10... | collective-permute-start | bytes 786440 | tf_op jit(solution)/shard_map/ppermute | solution.py:27
  17.6 2.4 %collective-permute-start.6 = (bf16[4,2,64,256]{3,2,1,0:T(8,128)(2,1)S(1)}, bf16[4,2,64,256]{3,2,1,0:T(8,128)(2,1)S(1)}, u32[]{:S(2)}, u32[]{:S(2)}) collective-permute-start(bf16[4,2,64,256]{3,2,1,0:T(8,128)(2,1)S(1)} %pad_maximum_fusion.refs_2_.kv_ref), channel_id=1, source_target_pairs={{0,1},{1,0},{2,3},{3,2},{4,5},{5,4},{6,7},{7,6},{8,9},{9,8},{10,11... | collective-permute-start | bytes 786440 | tf_op jit(solution)/shard_map/ppermute | solution.py:27
  17.7 8.7 %collective-permute-start.7 = (bf16[4,2,64,256]{3,2,1,0:T(8,128)(2,1)S(1)}, bf16[4,2,64,256]{3,2,1,0:T(8,128)(2,1)S(1)}, u32[]{:S(2)}, u32[]{:S(2)}) collective-permute-start(bf16[4,2,64,256]{3,2,1,0:T(8,128)(2,1)S(1)} %pad_maximum_fusion.refs_2_.kv_ref), channel_id=1, source_target_pairs={{0,16},{8,24},{16,0},{24,8},{1,17},{9,25},{17,1},{25,9},{2,18},{10... | collective-permute-start | bytes 786440 | tf_op jit(solution)/shard_map/ppermute | solution.py:27
  20.0 1.0 %copy-start.1 = (bf16[2,64,1024]{2,1,0:T(8,128)(2,1)S(1)}, bf16[2,64,1024]{2,1,0:T(8,128)(2,1)}, u32[]{:S(2)}) copy-start(bf16[2,64,1024]{2,1,0:T(8,128)(2,1)} %get-tuple-element.36.refs_0_) | copy-start | bytes 786436
  26.4 1.5 %collective-permute-start.8 = (bf16[4,2,64,256]{3,2,1,0:T(8,128)(2,1)S(1)}, bf16[4,2,64,256]{3,2,1,0:T(8,128)(2,1)S(1)}, u32[]{:S(2)}, u32[]{:S(2)}) collective-permute-start(bf16[4,2,64,256]{3,2,1,0:T(8,128)(2,1)S(1)} %collective-permute-done.7.refs_0_), channel_id=1, source_target_pairs={{0,1},{1,0},{2,3},{3,2},{4,5},{5,4},{6,7},{7,6},{8,9},{9,8},{10,11... | collective-permute-start | bytes 786440 | tf_op jit(solution)/shard_map/ppermute | solution.py:27
  33.9 2.5 %collective-permute-start.12 = (bf16[4,2,64,256]{3,2,1,0:T(8,128)(2,1)S(1)}, bf16[4,2,64,256]{3,2,1,0:T(8,128)(2,1)S(1)}, u32[]{:S(2)}, u32[]{:S(2)}) collective-permute-start(bf16[4,2,64,256]{3,2,1,0:T(8,128)(2,1)S(1)} %get-tuple-element.59), channel_id=1, source_target_pairs={{0,1},{1,0},{2,3},{3,2},{4,5},{5,4},{6,7},{7,6},{8,9},{9,8},{10,11... | collective-permute-start | bytes 786440 | tf_op jit(solution)/shard_map/ppermute | solution.py:27
  36.0 6.1 %collective-permute-start.11 = (bf16[4,2,64,256]{3,2,1,0:T(8,128)(2,1)S(1)}, bf16[4,2,64,256]{3,2,1,0:T(8,128)(2,1)S(1)}, u32[]{:S(2)}, u32[]{:S(2)}) collective-permute-start(bf16[4,2,64,256]{3,2,1,0:T(8,128)(2,1)S(1)} %get-tuple-element.57), channel_id=1, source_target_pairs={{0,1},{1,0},{2,3},{3,2},{4,5},{5,4},{6,7},{7,6},{8,9},{9,8},{10,11... | collective-permute-start | bytes 786440 | tf_op jit(solution)/shard_map/ppermute | solution.py:27
  36.5 8.4 %collective-permute-start.13 = (bf16[4,2,64,256]{3,2,1,0:T(8,128)(2,1)S(1)}, bf16[4,2,64,256]{3,2,1,0:T(8,128)(2,1)S(1)}, u32[]{:S(2)}, u32[]{:S(2)}) collective-permute-start(bf16[4,2,64,256]{3,2,1,0:T(8,128)(2,1)S(1)} %sum_cores.1), channel_id=1, source_target_pairs={{0,16},{8,24},{16,0},{24,8},{1,17},{9,25},{17,1},{25,9},{2,18},{10... | collective-permute-start | bytes 786440 | tf_op jit(solution)/shard_map/ppermute | solution.py:27
  38.1 16.2 %collective-permute-start.9 = (bf16[64,1024]{1,0:T(8,128)(2,1)S(1)}, bf16[64,1024]{1,0:T(8,128)(2,1)S(1)}, u32[]{:S(2)}, u32[]{:S(2)}) collective-permute-start(bf16[64,1024]{1,0:T(8,128)(2,1)S(1)} %get-tuple-element.46), channel_id=1, source_target_pairs={{0,8},{8,0},{16,24},{24,16},{1,9},{9,1},{17,25},{25,17},{2,10},{10... | collective-permute-start | bytes 393224 | tf_op jit(solution)/shard_map/ppermute | solution.py:27
  40.3 14.0 %collective-permute-start.10 = (bf16[64,1024]{1,0:T(8,128)(2,1)S(1)}, bf16[64,1024]{1,0:T(8,128)(2,1)S(1)}, u32[]{:S(2)}, u32[]{:S(2)}) collective-permute-start(bf16[64,1024]{1,0:T(8,128)(2,1)S(1)} %get-tuple-element.53), channel_id=1, source_target_pairs={{0,8},{8,0},{16,24},{24,16},{1,9},{9,1},{17,25},{25,17},{2,10},{10... | collective-permute-start | bytes 393224 | tf_op jit(solution)/shard_map/ppermute | solution.py:27
  45.0 4.5 %collective-permute-start.14 = (bf16[2,64,256]{2,1,0:T(8,128)(2,1)S(1)}, bf16[2,64,256]{2,1,0:T(8,128)(2,1)S(1)}, u32[]{:S(2)}, u32[]{:S(2)}) collective-permute-start(bf16[2,64,256]{2,1,0:T(8,128)(2,1)S(1)} %get-tuple-element.61), channel_id=1, source_target_pairs={{0,2},{1,3},{2,0},{3,1},{4,6},{5,7},{6,4},{7,5},{8,10},{9,11},{10,... | collective-permute-start | bytes 196616 | tf_op jit(solution)/shard_map/ppermute | solution.py:27
  45.5 7.1 %collective-permute-start.15 = (bf16[2,64,256]{2,1,0:T(8,128)(2,1)S(1)}, bf16[2,64,256]{2,1,0:T(8,128)(2,1)S(1)}, u32[]{:S(2)}, u32[]{:S(2)}) collective-permute-start(bf16[2,64,256]{2,1,0:T(8,128)(2,1)S(1)} %get-tuple-element.62), channel_id=1, source_target_pairs={{0,4},{1,5},{2,6},{3,7},{4,0},{5,1},{6,2},{7,3},{8,12},{9,13},{10,... | collective-permute-start | bytes 196616 | tf_op jit(solution)/shard_map/ppermute | solution.py:27
  47.8 6.2 %collective-permute-start.16 = (bf16[2,64,256]{2,1,0:T(8,128)(2,1)S(1)}, bf16[2,64,256]{2,1,0:T(8,128)(2,1)S(1)}, u32[]{:S(2)}, u32[]{:S(2)}) collective-permute-start(bf16[2,64,256]{2,1,0:T(8,128)(2,1)S(1)} %get-tuple-element.63), channel_id=1, source_target_pairs={{0,6},{1,7},{2,4},{3,5},{4,2},{5,3},{6,0},{7,1},{8,14},{9,15},{10,... | collective-permute-start | bytes 196616 | tf_op jit(solution)/shard_map/ppermute | solution.py:27
  54.0 4.0 %collective-permute-start.17 = (bf16[64,256]{1,0:T(8,128)(2,1)S(1)}, bf16[64,256]{1,0:T(8,128)(2,1)S(1)}, u32[]{:S(2)}, u32[]{:S(2)}) collective-permute-start(bf16[64,256]{1,0:T(8,128)(2,1)S(1)} %get-tuple-element.65), channel_id=1, source_target_pairs={{0,8},{8,0},{16,24},{24,16},{1,9},{9,1},{17,25},{25,17},{2,10},{10... | collective-permute-start | bytes 98312 | tf_op jit(solution)/shard_map/ppermute | solution.py:27

commit v5 on v4

--- a/solution.py
+++ b/solution.py
@@ -19,7 +19,6 @@
 
 VMEM = pl.BlockSpec(memory_space=pltpu.VMEM)
 SMEM = pl.BlockSpec(memory_space=pltpu.SMEM)
-HBM = pl.BlockSpec(memory_space=pltpu.HBM)
 
 
 def swap(block, axis, mask):
@@ -32,6 +31,8 @@
 
 
 def after(blocks, earlier):
+    if not earlier:
+        return tuple(blocks)
     return lax.optimization_barrier((tuple(blocks), tuple(earlier)))[0]
 
 
@@ -59,52 +60,46 @@
     return lax.dot_general(left, right, (((1,), (1,)), ((), ())), preferred_element_type=F32)
 
 
-def pack_own_kernel(kv, group_ref, key_ref, value_ref, query_ref, grad_ref, *refs):
-    out_ref, q_outs, refs = refs[0], refs[1 : kv + 1], refs[kv + 1 :]
-    key_buf, value_buf, query_buf, grad_buf, sems = refs
-    pairs = ((key_ref, key_buf), (value_ref, value_buf), (query_ref, query_buf), (grad_ref, grad_buf))
-    copies = [pltpu.make_async_copy(src, dst, sems.at[i]) for i, (src, dst) in enumerate(pairs)]
-    for copy in copies:
-        copy.start()
-    for copy in copies:
-        copy.wait()
-    width = q_outs[0].shape[2]
-    for g in range(kv):
-
-        @pl.when(group_ref[0] == g)
-        def _():
-            cols = pl.ds(g * HD, HD)
-            out_ref[:, :HD] = key_buf[:, cols]
-            out_ref[:, HD:] = value_buf[:, cols]
-            for s in range(kv):
-                theirs = pl.ds((g ^ s) * width, width)
-                q_outs[s][0] = query_buf[:, theirs]
-                q_outs[s][1] = grad_buf[:, theirs]
-
-
-def pack_kv_kernel(kv, group_ref, own_ref, *refs):
+def pack_kv_kernel(kv, group_ref, *refs):
     out_ref = refs[-1]
-    out_ref[0] = own_ref[...]
+    out_ref[0] = refs[0][...]
     for g in range(kv):
 
         @pl.when(group_ref[0] == g)
         def _():
             cols = pl.ds(g * HD, HD)
             for s in range(1, kv):
-                out_ref[s, :, :HD] = refs[2 * s - 2][:, cols]
-                out_ref[s, :, HD:] = refs[2 * s - 1][:, cols]
+                out_ref[s, :, :HD] = refs[2 * s - 1][:, cols]
+                out_ref[s, :, HD:] = refs[2 * s][:, cols]
+
+
+def pack_q_kernel(kv, group_ref, query_ref, grad_ref, *out_refs):
+    width = out_refs[0].shape[2]
+    for g in range(kv):
+
+        @pl.when(group_ref[0] == g)
+        def _():
+            for s in range(kv):
+                cols = pl.ds((g ^ s) * width, width)
+                out_refs[s][0] = query_ref[:, cols]
+                out_refs[s][1] = grad_ref[:, cols]
 
 
 class Plan:
-    def __init__(self, kv, block_len, block_rows, rows, group, cores, z_devices):
+    def __init__(self, kv, block_len, block_rows, rows, group, cores, z_devices, parts):
         self.kv, self.block_len, self.block_rows, self.rows = kv, block_len, block_rows, rows
-        self.group, self.cores, self.z_devices = group, cores, z_devices
+        self.group, self.cores, self.parts, self.z_part = group, cores, parts, z_devices // parts
         self.blocks = rows // block_rows
         self.tile_rows = block_rows if block_rows % 16 == 0 else rows
         self.lanes = group * self.tile_rows
         self.query_rows = kv * group * rows
-        self.chunk_keys = z_devices * kv * rows
+        self.part_keys = self.z_part * kv * rows
+        self.chunk_keys = parts * self.part_keys
         self.tiles = [(s, start) for s in range(kv) for start in range(0, rows, self.tile_rows)]
+
+    def zone(self, part):
+        first = (self.parts - 1 - part) * self.z_part
+        return range(first, first + self.z_part)
 
     def at(self, tile):
         return pl.ds(tile * self.lanes, self.lanes)
@@ -124,14 +119,14 @@
 
     def masked(self, scores, gap, chunk, info_ref):
         head, ctx = info_ref[0], info_ref[1]
-        a, core = divmod(chunk, self.cores)
+        a, core = chunk
         for j in range(self.chunk_keys // self.block_rows):
             m, rest = divmod(j, self.kv * self.blocks)
             s, b = divmod(rest, self.blocks)
             stored = (ctx ^ (m * self.cores + core)) * self.blocks + b
             first = info_ref[2 + stored] * self.block_len + (head ^ (a * self.kv + s)) * self.block_rows
-            part = scores[j * self.block_rows : (j + 1) * self.block_rows]
-            yield j * self.block_rows, jnp.where(gap >= first, part, LOWEST)
+            block = scores[j * self.block_rows : (j + 1) * self.block_rows]
+            yield j * self.block_rows, jnp.where(gap >= first, block, LOWEST)
 
     def turn(self, kv_refs, turned_ref):
         for i, ref in enumerate(kv_refs):
@@ -146,12 +141,12 @@
     def fold(self, block):
         return block.reshape(block.shape[0] // 8, 8, self.lanes)
 
-    def scores(self, tile, first_chunk, kv_refs, q, e_ref, cols, info_ref):
+    def scores(self, tile, chunks, kv_refs, q, e_ref, cols, info_ref):
         gap = self.gap(tile, info_ref)
         top = jnp.full((8, self.lanes), FLOOR, F32)
         for i, ref in enumerate(kv_refs):
             scores = dot_rows(self.keys(ref), q)
-            for row, part in self.masked(scores, gap, first_chunk + i, info_ref):
+            for row, part in self.masked(scores, gap, chunks[i], info_ref):
                 e_ref[pl.ds(i * self.chunk_keys + row, part.shape[0]), cols] = part
                 top = jnp.maximum(top, jnp.max(self.fold(part), axis=0))
         return jnp.max(top, axis=0, keepdims=True)
@@ -172,18 +167,19 @@
             out_ref[pl.ds(start, self.tile_rows), pl.ds(n * HD, HD)] = piece
 
     def back(self, kv_refs, dkv_refs, p_ref, ds_ref, q_ref, do_ref):
-        shape = (self.z_devices, self.kv, self.rows, HD)
-        for i, out_ref in enumerate(dkv_refs):
-            k_grad = dot(ds_ref[self.keys_at(i), :], q_ref[...])
-            v_grad = dot(p_ref[self.keys_at(i), :], do_ref[...])
-            out_ref[:, :, :, :HD] = k_grad.astype(BF).reshape(shape)
-            out_ref[:, :, :, HD:] = v_grad.astype(BF).reshape(shape)
-
-
-def near_kernel(plan, info_ref, *refs):
-    kv, chunks = plan.kv, plan.cores
+        shape = (self.z_part, self.kv, self.rows, HD)
+        for i in range(len(kv_refs)):
+            for part in range(self.parts):
+                at = pl.ds(i * self.chunk_keys + self.zone(part)[0] * self.kv * self.rows, self.part_keys)
+                out_ref = dkv_refs[i * self.parts + part]
+                out_ref[:, :, :, :HD] = dot(ds_ref[at, :], q_ref[...]).astype(BF).reshape(shape)
+                out_ref[:, :, :, HD:] = dot(p_ref[at, :], do_ref[...]).astype(BF).reshape(shape)
+
+
+def near_kernel(plan, chunks, info_ref, *refs):
+    kv, count = plan.kv, len(chunks)
     q_parts, refs = refs[:kv], refs[kv:]
-    kv_refs, refs = refs[:chunks], refs[chunks:]
+    kv_refs, refs = refs[:count], refs[count:]
     q_all, do_all, e_ref, top_ref, sum_ref, mix_ref, turned_ref = refs
     plan.turn(kv_refs, turned_ref)
     for tile, (s, start) in enumerate(plan.tiles):
@@ -194,35 +190,35 @@
             do_all[at, :] = q_parts[s][1, span, pl.ds(n * HD, HD)]
     for tile in range(len(plan.tiles)):
         at = plan.at(tile)
-        top = plan.scores(tile, 0, kv_refs, q_all[at, :], e_ref, at, info_ref)
+        top = plan.scores(tile, chunks, kv_refs, q_all[at, :], e_ref, at, info_ref)
         top_ref[:, at] = top
-        sum_ref[:, at] = plan.exponents(chunks, e_ref, at, top)
+        sum_ref[:, at] = plan.exponents(count, e_ref, at, top)
         mixed = jnp.zeros((HD, plan.lanes), F32)
-        for i in range(chunks):
+        for i in range(count):
             weights = e_ref[plan.keys_at(i), at].astype(BF)
             mixed = mixed + dot(turned_ref[pl.ds(HD, HD), plan.keys_at(i)], weights)
         mix_ref[:, at] = mixed
 
 
 def far_kernel(plan, chunks, info_ref, q_all, do_all, near_top, near_sum, near_mix, *refs):
-    kv = plan.kv
-    kv_refs, refs = refs[:chunks], refs[chunks:]
+    kv, count = plan.kv, len(chunks)
+    kv_refs, refs = refs[:count], refs[count:]
     att_refs, refs = refs[:kv], refs[kv:]
     near_scale, delta_ref, q_grad_ref = refs[:3]
-    dkv_refs, refs = refs[3 : 3 + chunks], refs[3 + chunks :]
+    dkv_refs, refs = refs[3 : 3 + count * plan.parts], refs[3 + count * plan.parts :]
     turned_ref, e_ref, p_ref, ds_ref = refs
     here = pl.ds(0, plan.lanes)
     plan.turn(kv_refs, turned_ref)
     for tile, (s, _) in enumerate(plan.tiles):
         at = plan.at(tile)
-        top = plan.scores(tile, plan.cores, kv_refs, q_all[at, :], e_ref, here, info_ref)
+        top = plan.scores(tile, chunks, kv_refs, q_all[at, :], e_ref, here, info_ref)
         top = jnp.maximum(top, near_top[:, at])
-        total = plan.exponents(chunks, e_ref, here, top)
+        total = plan.exponents(count, e_ref, here, top)
         factor = jnp.exp2((near_top[:, at] - top) * EXPO)
         inverse = 1.0 / (total + factor * near_sum[:, at])
         near_scale[:, at] = factor * inverse
         mixed = near_mix[:, at] * (factor * inverse)
-        for i in range(chunks):
+        for i in range(count):
             probs = (e_ref[plan.keys_at(i), here] * inverse).astype(BF)
             p_ref[plan.keys_at(i), at] = probs
             mixed = mixed + dot(turned_ref[pl.ds(HD, HD), plan.keys_at(i)], probs)
@@ -241,7 +237,8 @@
 
 
 def near_back_kernel(plan, chunk, q_all, do_all, e_ref, near_scale, delta_ref, q_grad_in, kv_ref, *refs):
-    outs, (dkv_ref, turned_ref, p_ref, ds_ref) = refs[:-4], refs[-4:]
+    refs, (turned_ref, p_ref, ds_ref) = refs[:-3], refs[-3:]
+    outs, dkv_refs = refs[: -plan.parts], refs[-plan.parts :]
     plan.turn([kv_ref], turned_ref)
     for tile, (s, _) in enumerate(plan.tiles):
         at = plan.at(tile)
@@ -255,7 +252,7 @@
             plan.store_heads(outs[s], tile, q_grad * SCALING)
         else:
             outs[0][:, at] = q_grad
-    plan.back([kv_ref], [dkv_ref], p_ref, ds_ref, q_all, do_all)
+    plan.back([kv_ref], dkv_refs, p_ref, ds_ref, q_all, do_all)
 
 
 def add_kernel(*refs):
@@ -317,7 +314,9 @@
     cores = CORES if ctx_devices % CORES == 0 else 1
     z_devices = ctx_devices // cores
     spans = heads_devices // kv
-    plan = Plan(kv, block_rows * heads_devices, block_rows, rows, width // HD, cores, z_devices)
+    parts = 2 if z_devices % 2 == 0 else 1
+    plan = Plan(kv, block_rows * heads_devices, block_rows, rows, width // HD, cores, z_devices, parts)
+    z_part = plan.z_part
     head = lax.axis_index("head").astype(jnp.int32)
     place = jnp.stack([head, lax.axis_index("ctx").astype(jnp.int32)])
     info = jnp.concatenate([place, block_order])
@@ -336,19 +335,20 @@
     def with_swaps(blocks):
         return [blocks[0]] + [swap(blocks[s], "head", s) for s in range(1, kv)]
 
-    key_parts = [swap(key_vectors, "head", s) for s in range(1, kv)]
-    value_parts = [swap(value_vectors, "head", s) for s in range(1, kv)]
-    own, *q_parts = pl.pallas_call(
-        functools.partial(pack_own_kernel, kv),
-        out_shape=[bf(rows, 2 * HD)] + [bf(2, rows, width)] * kv,
-        in_specs=[SMEM] + [HBM] * 4,
-        out_specs=[VMEM] * (kv + 1),
-        scratch_shapes=[pltpu.VMEM((rows, kv * HD), BF)] * 2
-        + [pltpu.VMEM((rows, query_width), BF)] * 2
-        + [pltpu.SemaphoreType.DMA((4,))],
-        name="pack_own",
-    )(own_group, key_vectors, value_vectors, queries, out_grad)
-    q_parts = with_swaps(q_parts)
+    key_parts = with_swaps([key_vectors] * kv)[1:]
+    value_parts = with_swaps([value_vectors] * kv)[1:]
+    mine = (head % kv) * HD
+    own = jnp.concatenate(
+        [lax.dynamic_slice_in_dim(block, mine, HD, 1) for block in (key_vectors, value_vectors)], axis=1
+    )
+    q_parts = call(
+        functools.partial(pack_q_kernel, kv),
+        "pack_q",
+        (own_group, queries, out_grad),
+        [bf(2, rows, width)] * kv,
+        [SMEM, VMEM, VMEM],
+    )
+    own = after([own], q_parts[1:])[0]
     piece = call(
         functools.partial(pack_kv_kernel, kv),
         "pack_kv",
@@ -356,17 +356,22 @@
         [bf(kv, rows, 2 * HD)],
         [SMEM] + [VMEM] * (2 * kv - 1),
     )[0]
-    column = jnp.stack([piece] + [swap(piece, "ctx", m * cores) for m in range(1, z_devices)])
+    pieces = [swap(piece, "ctx", m * cores) for m in reversed(range(1, z_devices))]
+    pieces = [piece] + pieces[::-1]
+    q_parts = with_swaps(q_parts)
+    column = jnp.stack(pieces)
     columns = [swap(column, "head", a * kv) for a in range(1, spans)]
     near_kv = [column] + [swap(column, "ctx", core) for core in range(1, cores)]
-    far_chunks = len(columns) * cores
-
-    near_keys = len(near_kv) * plan.chunk_keys
-    far_keys = far_chunks * plan.chunk_keys
+    near_chunks = [(0, core) for core in range(cores)]
+    far_chunks = [(a, core) for a in range(1, spans) for core in range(cores)]
+
+    keys = plan.chunk_keys
+    near_keys, far_keys = len(near_chunks) * keys, len(far_chunks) * keys
     query_rows = plan.query_rows
     row = f32(1, query_rows)
+    dkv = bf(z_part, kv, rows, 2 * HD)
     q_all, do_all, near_e, near_top, near_sum, near_mix = call(
-        functools.partial(near_kernel, plan),
+        functools.partial(near_kernel, plan, near_chunks),
         "attend_near",
         (info, *q_parts, *near_kv),
         [bf(query_rows, HD)] * 2 + [f32(near_keys, query_rows), row, row, f32(HD, query_rows)],
@@ -375,17 +380,14 @@
         near_keys * 4 * HD,
         8 * near_keys * query_rows * HD,
     )
-    columns = after(columns, [near_top])
     far_kv = []
-    for part in columns:
+    for part in after(columns, [near_top]):
         far_kv += [part] + [swap(part, "ctx", core) for core in range(1, cores)]
     outs = call(
-        functools.partial(far_kernel, plan, len(far_kv)),
+        functools.partial(far_kernel, plan, far_chunks),
         "attend_far",
         (info, q_all, do_all, near_top, near_sum, near_mix, *far_kv),
-        [bf(rows, width)] * kv
-        + [row, row, f32(HD, query_rows)]
-        + [bf(z_devices, kv, rows, 2 * HD)] * len(far_kv),
+        [bf(rows, width)] * kv + [row, row, f32(HD, query_rows)] + [dkv] * (parts * len(far_kv)),
         [SMEM] + [VMEM] * (5 + len(far_kv)),
         [
             pltpu.VMEM((2 * HD, far_keys), BF),
@@ -397,43 +399,52 @@
         16 * far_keys * query_rows * HD,
     )
     att_parts, outs = outs[:kv], outs[kv:]
-    (near_scale, delta, far_q_grad), far_dkv = outs[:3], outs[3:]
-    sums = []
+    (near_scale, delta, q_grad), far_dkv = outs[:3], outs[3:]
+
+    sums = [[] for _ in range(parts)]
     for a in range(spans - 1):
-        parts = far_dkv[a * cores : (a + 1) * cores]
-        swapped = [swap(parts[core], "ctx", core) for core in range(1, cores)]
-        sums += call(add_kernel, "sum_cores", (parts[0], *swapped), [bf(*parts[0].shape)])
-    near_dkv, q_grad = [], far_q_grad
-    for chunk in reversed(range(cores)):
-        q_outs = [f32(HD, query_rows)] if chunk else [bf(rows, width)] * kv
+        earlier = []
+        for p in range(parts):
+            ours = [far_dkv[(a * cores + core) * parts + p] for core in range(cores)]
+            both = [ours[0]] + [swap(ours[core], "ctx", core) for core in range(1, cores)]
+            total = call(add_kernel, "sum_cores", after(both, earlier), [dkv])[0]
+            earlier = [total]
+            sums[p].append(swap(total, "head", (a + 1) * kv))
+    for core in reversed(range(cores)):
+        q_outs = [f32(HD, query_rows)] if core else [bf(rows, width)] * kv
         outs = call(
-            functools.partial(near_back_kernel, plan, chunk),
+            functools.partial(near_back_kernel, plan, core),
             "attend_near_back",
-            (q_all, do_all, near_e, near_scale, delta, q_grad, near_kv[chunk]),
-            q_outs + [bf(z_devices, kv, rows, 2 * HD)],
+            (q_all, do_all, near_e, near_scale, delta, q_grad, near_kv[core]),
+            q_outs + [dkv] * parts,
             None,
             [
-                pltpu.VMEM((2 * HD, plan.chunk_keys), BF),
-                pltpu.VMEM((plan.chunk_keys, query_rows), BF),
-                pltpu.VMEM((plan.chunk_keys, query_rows), BF),
+                pltpu.VMEM((2 * HD, keys), BF),
+                pltpu.VMEM((keys, query_rows), BF),
+                pltpu.VMEM((keys, query_rows), BF),
             ],
-            plan.chunk_keys * (4 * HD + 4 * query_rows),
-            12 * plan.chunk_keys * query_rows * HD,
+            keys * (4 * HD + 4 * query_rows),
+            12 * keys * query_rows * HD,
         )
         q_grad = outs[0]
-        near_dkv = [swap(outs[-1], "ctx", chunk) if chunk else outs[-1]] + near_dkv
-    q_grad_parts = outs[:-1]
-    sums = [swap(part, "head", (a + 1) * kv) for a, part in enumerate(sums)]
-    sums = near_dkv + sums
-    z_parts = call(
-        functools.partial(sum_heads_kernel, len(sums)),
-        "sum_heads",
-        sums,
-        [bf(kv, rows, 2 * HD)] * z_devices,
-    )
-    z_parts = [z_parts[0]] + [swap(z_parts[m], "ctx", m * cores) for m in range(1, z_devices)]
+        for p in range(parts):
+            part = outs[len(q_outs) + p]
+            sums[p].append(swap(part, "ctx", core) if core else part)
+    q_grad_parts = outs[:kv]
+    z_parts = [None] * z_devices
+    for p in range(parts):
+        totals = call(
+            functools.partial(sum_heads_kernel, len(sums[p])),
+            "sum_heads",
+            sums[p],
+            [bf(kv, rows, 2 * HD)] * z_part,
+        )
+
+        for m, total in zip(plan.zone(p), totals):
+            z_parts[m] = swap(total, "ctx", m * cores) if m else total
+    ordered = [z_parts[m] for p in range(parts) for m in plan.zone(p)]
     pair_parts = call(
-        functools.partial(sum_z_kernel, kv), "sum_z", z_parts, [bf(rows, 2 * HD)] * kv
+        functools.partial(sum_z_kernel, kv), "sum_z", ordered, [bf(rows, 2 * HD)] * kv
     )
     pair_parts = with_swaps(pair_parts)
     attended, query_grad = call(

time: 58.9 us -> 55.9 us (0.949)
  waiting for transfers between devices: 20.1 us -> 14.8 us
  starting transfers between devices: 18.7 us -> 21.1 us
  Pallas kernels: 16.6 us -> 14.9 us
  local copies, waits for them, and re-layouts: 1.71 us -> 3.34 us
    ppermute x18 -> x21, waiting for transfers between devices: 20.1 us -> 14.8 us  [swap(): return lax.ppermute(block, axis, [(i, i ^ mask) for i in range(size)])]
    ppermute x18 -> x21, starting transfers between devices: 18.7 us -> 21.1 us  [swap(): return lax.ppermute(block, axis, [(i, i ^ mask) for i in range(size)])]
    pallas_call x1 -> x0, Pallas kernels: 1.94 us -> none  [shards(): pl.pallas_call(functools.partial(pack_own_kernel, kv), out_shape=[bf(rows...]
    dynamic_slice x0 -> x2, local copies, waits for them, and re-layouts: none -> 1.44 us  [shards(): lax.dynamic_slice_in_dim(block, mine, HD, 1)]
    pallas_call x10 -> x13, Pallas kernels: 14.7 us -> 14.9 us  [call(): pl.pallas_call(kernel, out_shape=list(outs), in_specs=specs or [VMEM] * l...]
  transfers between devices with their start and end apart: 18 -> 21, of which waited for: 10 -> 9; matrix products, arithmetic and copies ran while one was open for 1% -> 4% of each run, Pallas kernels for 17% -> 15%
where the time goes in v5:
time: 55.9 us; the launch traced here: 55.6 us
  starting transfers between devices  21.1 us (38%)
  Pallas kernels  14.9 us (27%)
  waiting for transfers between devices  14.8 us (26%)
  local copies, waits for them, and re-layouts  3.34 us (6%)
  other arithmetic  0.77 us (1%)
  between operations  0.73 us (1%)
    ppermute x21, starting transfers between devices, swap(): return lax.ppermute(block, axis, [(i, i ^ mask) for i in range(size)])  21.1 us
    pallas_call x13, Pallas kernels, call(): pl.pallas_call(kernel, out_shape=list(outs), in_specs=specs or [VMEM] * l...  14.9 us
    ppermute x21, waiting for transfers between devices, swap(): return lax.ppermute(block, axis, [(i, i ^ mask) for i in range(size)])  14.8 us
    unnamed x4, local copies, waits for them, and re-layouts  1.9 us
    dynamic_slice x2, local copies, waits for them, and re-layouts, shards(): lax.dynamic_slice_in_dim(block, mine, HD, 1)  1.44 us
  transfers between devices with their start and end apart: 21, of which 9 were waited for; matrix products, arithmetic and copies ran while one was open for 4% of the time, Pallas kernels for 15%

profile of v5, /device:TPU:0, one launch (start us, length us, event | category | flops | bytes accessed | tf_op | source)
XLA Modules:
  0.0 55.6 jit_solution(10742662476221707050)
XLA Ops:
  0.6 3.0 %collective-permute-start.1 = (bf16[64,256]{1,0:T(8,128)(2,1)}, bf16[64,256]{1,0:T(8,128)(2,1)S(1)}, u32[]{:S(2)}, u32[]{:S(2)}) collective-permute-start(bf16[64,256]{1,0:T(8,128)(2,1)} %bitcast.21), channel_id=1, source_target_pairs={{0,8},{8,0},{16,24},{24,16},{1,9},{9,1},{17,25},{25,17},{2,10},{10... | collective-permute-start | bytes 98312 | tf_op jit(solution)/shard_map/ppermute | solution.py:26
  3.6 0.1 collective-permute-start.2
  3.7 0.7 %constant_dynamic-slice_fusion.1 = bf16[64,128]{1,0:T(8,128)(2,1)S(1)} fusion(bf16[64,256]{1,0:T(8,128)(2,1)} %bitcast.22, s32[]{:T(128)S(6)} %select_n.14), kind=kLoop, calls=%fused_computation.4 | loop fusion | bytes 32772 | tf_op jit(solution)/shard_map/dynamic_slice | solution.py:342
  4.4 0.7 %constant_dynamic-slice_fusion = bf16[64,128]{1,0:T(8,128)(2,1)S(1)} fusion(bf16[64,256]{1,0:T(8,128)(2,1)} %bitcast.24, s32[]{:T(128)S(6)} %select_n.14), kind=kLoop, calls=%fused_computation.3 | loop fusion | bytes 32772 | tf_op jit(solution)/shard_map/dynamic_slice | solution.py:342
  5.2 0.9 %copy-done = bf16[2,32,2048]{2,1,0:T(8,128)(2,1)S(1)} copy-done((bf16[2,32,2048]{2,1,0:T(8,128)(2,1)S(1)}, bf16[2,32,2048]{2,1,0:T(8,128)(2,1)}, u32[]{:S(2)}) %copy-start) | copy-done | bytes 262168
  6.1 0.9 %copy-done.1 = bf16[2,32,2048]{2,1,0:T(8,128)(2,1)S(1)} copy-done((bf16[2,32,2048]{2,1,0:T(8,128)(2,1)S(1)}, bf16[2,32,2048]{2,1,0:T(8,128)(2,1)}, u32[]{:S(2)}) %copy-start.1) | copy-done | bytes 262168
  7.1 0.0 collective-permute-done.1.refs_1_
  7.1 0.6 %collective-permute-done.2.refs_2_ = bf16[64,256]{1,0:T(8,128)(2,1)S(1)} collective-permute-done((bf16[64,256]{1,0:T(8,128)(2,1)}, bf16[64,256]{1,0:T(8,128)(2,1)S(1)}, u32[]{:S(2)}, u32[]{:S(2)}) %collective-permute-start.2) | collective-permute-done | bytes 32800 | tf_op jit(solution)/shard_map/ppermute | solution.py:26
  7.8 3.7 %collective-permute-start.5 = (bf16[2,64,256]{2,1,0:T(8,128)(2,1)S(1)}, bf16[2,64,256]{2,1,0:T(8,128)(2,1)S(1)}, u32[]{:S(2)}, u32[]{:S(2)}) collective-permute-start(bf16[2,64,256]{2,1,0:T(8,128)(2,1)S(1)} %pack_kv.1), channel_id=1, source_target_pairs={{0,6},{1,7},{2,4},{3,5},{4,2},{5,3},{6,0},{7,1},{8,14},{9,15},{10,... | collective-permute-start | bytes 196616 | tf_op jit(solution)/shard_map/ppermute | solution.py:26
  11.4 0.0 collective-permute-start.4
  11.5 0.8 %collective-permute-start.3 = (bf16[2,64,256]{2,1,0:T(8,128)(2,1)S(1)}, bf16[2,64,256]{2,1,0:T(8,128)(2,1)S(1)}, u32[]{:S(2)}, u32[]{:S(2)}) collective-permute-start(bf16[2,64,256]{2,1,0:T(8,128)(2,1)S(1)} %pack_kv.1), channel_id=1, source_target_pairs={{0,2},{1,3},{2,0},{3,1},{4,6},{5,7},{6,4},{7,5},{8,10},{9,11},{10,... | collective-permute-start | bytes 196616 | tf_op jit(solution)/shard_map/ppermute | solution.py:26
  12.2 1.3 %collective-permute-start = (bf16[2,64,1024]{2,1,0:T(8,128)(2,1)S(1)}, bf16[2,64,1024]{2,1,0:T(8,128)(2,1)S(1)}, u32[]{:S(2)}, u32[]{:S(2)}) collective-permute-start(bf16[2,64,1024]{2,1,0:T(8,128)(2,1)S(1)} %get-tuple-element.43), channel_id=1, source_target_pairs={{0,8},{8,0},{16,24},{24,16},{1,9},{9,1},{17,25},{25,17},{2,10},{10... | collective-permute-start | bytes 786440 | tf_op jit(solution)/shard_map/ppermute | solution.py:26
  13.5 0.7 %collective-permute-done.5 = bf16[2,64,256]{2,1,0:T(8,128)(2,1)S(1)} collective-permute-done((bf16[2,64,256]{2,1,0:T(8,128)(2,1)S(1)}, bf16[2,64,256]{2,1,0:T(8,128)(2,1)S(1)}, u32[]{:S(2)}, u32[]{:S(2)}) %collective-permute-start.5) | collective-permute-done | bytes 65568 | tf_op jit(solution)/shard_map/ppermute | solution.py:26
  14.3 2.5 %collective-permute-done.4 = bf16[2,64,256]{2,1,0:T(8,128)(2,1)S(1)} collective-permute-done((bf16[2,64,256]{2,1,0:T(8,128)(2,1)S(1)}, bf16[2,64,256]{2,1,0:T(8,128)(2,1)S(1)}, u32[]{:S(2)}, u32[]{:S(2)}) %collective-permute-start.4) | collective-permute-done | bytes 65568 | tf_op jit(solution)/shard_map/ppermute | solution.py:26
  16.8 0.1 collective-permute-start.6
  16.9 1.6 %collective-permute-start.7 = (bf16[4,2,64,256]{3,2,1,0:T(8,128)(2,1)S(1)}, bf16[4,2,64,256]{3,2,1,0:T(8,128)(2,1)S(1)}, u32[]{:S(2)}, u32[]{:S(2)}) collective-permute-start(bf16[4,2,64,256]{3,2,1,0:T(8,128)(2,1)S(1)} %pad_maximum_fusion.refs_2_.kv_ref), channel_id=1, source_target_pairs={{0,16},{8,24},{16,0},{24,8},{1,17},{9,25},{17,1},{25,9},{2,18},{10... | collective-permute-start | bytes 786440 | tf_op jit(solution)/shard_map/ppermute | solution.py:26
  18.5 0.7 %pad_add_fusion.info_ref = s32[18]{0:T(128)S(1)} fusion(s32[16]{0:T(128)} %param.9, s32[1]{0:T(128)} %bitcast.2, s32[1]{0:T(128)} %bitcast.1), kind=kLoop, calls=%fused_computation.2 | loop fusion | flops 36 | bytes 144 | tf_op jit(solution)/shard_map/concatenate | solution.py:322
  19.2 0.0 collective-permute-done.refs_1_
  19.2 0.0 collective-permute-done.6.refs_3_.kv_ref
  19.2 3.3 %attend_near.1 = (bf16[1024,128]{1,0:T(8,128)(2,1)S(1)}, bf16[1024,128]{1,0:T(8,128)(2,1)S(1)}, f32[1024,1024]{1,0:T(8,128)S(1)}, f32[1,1024]{1,0:T(1,128)S(1)},...) custom-call(s32[18]{0:T(128)S(1)} %pad_add_fusion.info_ref, bf16[2,64,1024]{2,1,0:T(8,128)(2,1)S(1)} %get-tuple-element.42.refs_0_, ...), custom_call_target="tpu_custom_call" | custom-call | flops 1073741824 | bytes 6299720 | tf_op jit(solution)/shard_map/attend_near/pallas_call | solution.py:41
  22.5 3.1 %collective-permute-done.7.refs_0_ = bf16[4,2,64,256]{3,2,1,0:T(8,128)(2,1)S(1)} collective-permute-done((bf16[4,2,64,256]{3,2,1,0:T(8,128)(2,1)S(1)}, bf16[4,2,64,256]{3,2,1,0:T(8,128)(2,1)S(1)}, u32[]{:S(2)}, u32[]{:S(2)}) %collective-permute-start.7) | collective-permute-done | bytes 262176 | tf_op jit(solution)/shard_map/ppermute | solution.py:26
  25.6 0.0 collective-permute-start.8
  25.6 1.5 %collective-permute-done.8.refs_1_ = bf16[4,2,64,256]{3,2,1,0:T(8,128)(2,1)S(1)} collective-permute-done((bf16[4,2,64,256]{3,2,1,0:T(8,128)(2,1)S(1)}, bf16[4,2,64,256]{3,2,1,0:T(8,128)(2,1)S(1)}, u32[]{:S(2)}, u32[]{:S(2)}) %collective-permute-start.8) | collective-permute-done | bytes 262176 | tf_op jit(solution)/shard_map/ppermute | solution.py:26
  27.2 6.0 %attend_far.1 = (bf16[64,1024]{1,0:T(8,128)(2,1)S(1)}, bf16[64,1024]{1,0:T(8,128)(2,1)S(1)}, f32[1,1024]{1,0:T(1,128)S(1)}, f32[1,1024]{1,0:T(1,128)S(1)}, f32[1...) custom-call(s32[18]{0:T(128)S(1)} %pad_add_fusion.info_ref, ...), custom_call_target="tpu_custom_call" | custom-call | flops 2147483648 | bytes 2900040 | tf_op jit(solution)/shard_map/attend_far/pallas_call | solution.py:41
  33.2 0.2 collective-permute-start.11
  33.4 0.4 collective-permute-start.16
  33.8 1.9 %attend_near_back.2 = (f32[128,1024]{1,0:T(8,128)S(1)}, bf16[2,2,64,256]{3,2,1,0:T(8,128)(2,1)S(1)}, bf16[2,2,64,256]{3,2,1,0:T(8,128)(2,1)S(1)}) custom-call(bf16[1024,128]{1,0:T(8,128)(2,1)S(1)} %get-tuple-element.45.q_all, bf16[1024,128]{1,0:T(8,128)(2,1)S(1)} %get-tuple-element.46.do_all, f32[1024,1024]{1,0:T(8,128)S(1)} %get-tuple-element.53.e_ref, ...), custom_call_target="tpu_custom_call" | custom-call | flops 805306368 | bytes 6299648 | tf_op jit(solution)/shard_map/attend_near_back/pallas_call | solution.py:41
  35.7 0.2 collective-permute-start.13
  35.9 0.4 collective-permute-start.18
  36.3 1.6 %collective-permute-start.12 = (bf16[2,2,64,256]{3,2,1,0:T(8,128)(2,1)S(1)}, bf16[2,2,64,256]{3,2,1,0:T(8,128)(2,1)S(1)}, u32[]{:S(2)}, u32[]{:S(2)}) collective-permute-start(bf16[2,2,64,256]{3,2,1,0:T(8,128)(2,1)S(1)} %sum_cores.2), channel_id=1, source_target_pairs={{0,16},{8,24},{16,0},{24,8},{1,17},{9,25},{17,1},{25,9},{2,18},{10... | collective-permute-start | bytes 393224 | tf_op jit(solution)/shard_map/ppermute | solution.py:26
  37.9 0.0 collective-permute-done.16.refs_1_
  37.9 0.6 %collective-permute-start.17 = (bf16[2,2,64,256]{3,2,1,0:T(8,128)(2,1)S(1)}, bf16[2,2,64,256]{3,2,1,0:T(8,128)(2,1)S(1)}, u32[]{:S(2)}, u32[]{:S(2)}) collective-permute-start(bf16[2,2,64,256]{3,2,1,0:T(8,128)(2,1)S(1)} %sum_cores.3), channel_id=1, source_target_pairs={{0,16},{8,24},{16,0},{24,8},{1,17},{9,25},{17,1},{25,9},{2,18},{10... | collective-permute-start | bytes 393224 | tf_op jit(solution)/shard_map/ppermute | solution.py:26
  38.5 1.2 %collective-permute-start.9 = (bf16[64,1024]{1,0:T(8,128)(2,1)S(1)}, bf16[64,1024]{1,0:T(8,128)(2,1)S(1)}, u32[]{:S(2)}, u32[]{:S(2)}) collective-permute-start(bf16[64,1024]{1,0:T(8,128)(2,1)S(1)} %get-tuple-element.52), channel_id=1, source_target_pairs={{0,8},{8,0},{16,24},{24,16},{1,9},{9,1},{17,25},{25,17},{2,10},{10... | collective-permute-start | bytes 393224 | tf_op jit(solution)/shard_map/ppermute | solution.py:26
  39.7 1.9 %attend_near_back.3 = (bf16[64,1024]{1,0:T(8,128)(2,1)S(1)}, bf16[64,1024]{1,0:T(8,128)(2,1)S(1)}, bf16[2,2,64,256]{3,2,1,0:T(8,128)(2,1)S(1)}, bf16[2,2,64,256]{3,2,1,0:T(8,128)(2,1)S(1)}) custom-call(bf16[1024,128]{1,0:T(8,128)(2,1)S(1)} %get-tuple-element.45.q_all, bf16[1024,128]{1,0:T(8,128)(2,1)S(1)} %get-tuple-element.46.do_all, ...), custom_call_target="tpu_custom_call" | custom-call | flops 805306368 | bytes 6037504 | tf_op jit(solution)/shard_map/attend_near_back/pallas_call | solution.py:41
  41.6 0.9 %collective-permute-start.10 = (bf16[64,1024]{1,0:T(8,128)(2,1)S(1)}, bf16[64,1024]{1,0:T(8,128)(2,1)S(1)}, u32[]{:S(2)}, u32[]{:S(2)}) collective-permute-start(bf16[64,1024]{1,0:T(8,128)(2,1)S(1)} %get-tuple-element.59), channel_id=1, source_target_pairs={{0,8},{8,0},{16,24},{24,16},{1,9},{9,1},{17,25},{25,17},{2,10},{10... | collective-permute-start | bytes 393224 | tf_op jit(solution)/shard_map/ppermute | solution.py:26
  42.5 0.2 collective-permute-done.12.refs_0_
  42.7 0.1 sum_heads.2
  42.8 1.9 %collective-permute-start.14 = (bf16[2,64,256]{2,1,0:T(8,128)(2,1)S(1)}, bf16[2,64,256]{2,1,0:T(8,128)(2,1)S(1)}, u32[]{:S(2)}, u32[]{:S(2)}) collective-permute-start(bf16[2,64,256]{2,1,0:T(8,128)(2,1)S(1)} %get-tuple-element.66), channel_id=1, source_target_pairs={{0,4},{1,5},{2,6},{3,7},{4,0},{5,1},{6,2},{7,3},{8,12},{9,13},{10,... | collective-permute-start | bytes 196616 | tf_op jit(solution)/shard_map/ppermute | solution.py:26
  44.7 1.1 %collective-permute-start.15 = (bf16[2,64,256]{2,1,0:T(8,128)(2,1)S(1)}, bf16[2,64,256]{2,1,0:T(8,128)(2,1)S(1)}, u32[]{:S(2)}, u32[]{:S(2)}) collective-permute-start(bf16[2,64,256]{2,1,0:T(8,128)(2,1)S(1)} %get-tuple-element.67), channel_id=1, source_target_pairs={{0,6},{1,7},{2,4},{3,5},{4,2},{5,3},{6,0},{7,1},{8,14},{9,15},{10,... | collective-permute-start | bytes 196616 | tf_op jit(solution)/shard_map/ppermute | solution.py:26
  45.8 0.1 sum_heads.3
  45.9 0.6 %collective-permute-start.19 = (bf16[2,64,256]{2,1,0:T(8,128)(2,1)S(1)}, bf16[2,64,256]{2,1,0:T(8,128)(2,1)S(1)}, u32[]{:S(2)}, u32[]{:S(2)}) collective-permute-start(bf16[2,64,256]{2,1,0:T(8,128)(2,1)S(1)} %get-tuple-element.75), channel_id=1, source_target_pairs={{0,2},{1,3},{2,0},{3,1},{4,6},{5,7},{6,4},{7,5},{8,10},{9,11},{10,... | collective-permute-start | bytes 196616 | tf_op jit(solution)/shard_map/ppermute | solution.py:26
  46.4 3.0 %collective-permute-done.14.refs_0_ = bf16[2,64,256]{2,1,0:T(8,128)(2,1)S(1)} collective-permute-done((bf16[2,64,256]{2,1,0:T(8,128)(2,1)S(1)}, bf16[2,64,256]{2,1,0:T(8,128)(2,1)S(1)}, u32[]{:S(2)}, u32[]{:S(2)}) %collective-permute-start.14) | collective-permute-done | bytes 65568 | tf_op jit(solution)/shard_map/ppermute | solution.py:26
  49.4 1.5 %collective-permute-done.15.refs_1_ = bf16[2,64,256]{2,1,0:T(8,128)(2,1)S(1)} collective-permute-done((bf16[2,64,256]{2,1,0:T(8,128)(2,1)S(1)}, bf16[2,64,256]{2,1,0:T(8,128)(2,1)S(1)}, u32[]{:S(2)}, u32[]{:S(2)}) %collective-permute-start.15) | collective-permute-done | bytes 65568 | tf_op jit(solution)/shard_map/ppermute | solution.py:26
  50.9 0.0 collective-permute-done.19.refs_3_
  50.9 1.6 %collective-permute-start.20 = (bf16[64,256]{1,0:T(8,128)(2,1)S(1)}, bf16[64,256]{1,0:T(8,128)(2,1)S(1)}, u32[]{:S(2)}, u32[]{:S(2)}) collective-permute-start(bf16[64,256]{1,0:T(8,128)(2,1)S(1)} %get-tuple-element.77), channel_id=1, source_target_pairs={{0,8},{8,0},{16,24},{24,16},{1,9},{9,1},{17,25},{25,17},{2,10},{10... | collective-permute-start | bytes 98312 | tf_op jit(solution)/shard_map/ppermute | solution.py:26
  52.5 0.8 %finish_q.1 = (bf16[64,2048]{1,0:T(8,128)(2,1)}, bf16[64,2048]{1,0:T(8,128)(2,1)}) custom-call(s32[1]{0:T(128)} %bitcast.group_ref, bf16[64,1024]{1,0:T(8,128)(2,1)S(1)} %get-tuple-element.51.refs_0_, bf16[64,1024]{1,0:T(8,128)(2,1)S(1)} %collective-permute-done.9.refs_1_, bf16[64,1024]{1,0:T(8,128)(2,1)S(1)} %get-tuple-element.58.refs_2_, ...), custom_call_target="tpu_custom_call" | custom-call | bytes 1048580 | tf_op jit(solution)/shard_map/finish_q/pallas_call | solution.py:41
  53.3 1.6 %collective-permute-done.20.refs_1_ = bf16[64,256]{1,0:T(8,128)(2,1)S(1)} collective-permute-done((bf16[64,256]{1,0:T(8,128)(2,1)S(1)}, bf16[64,256]{1,0:T(8,128)(2,1)S(1)}, u32[]{:S(2)}, u32[]{:S(2)}) %collective-permute-start.20) | collective-permute-done | bytes 32800 | tf_op jit(solution)/shard_map/ppermute | solution.py:26
  54.9 0.6 %finish_kv.1 = (bf16[64,256]{1,0:T(8,128)(2,1)}, bf16[64,256]{1,0:T(8,128)(2,1)}) custom-call(s32[1]{0:T(128)} %bitcast.group_ref, bf16[64,256]{1,0:T(8,128)(2,1)S(1)} %get-tuple-element.76.refs_0_, bf16[64,256]{1,0:T(8,128)(2,1)S(1)} %collective-permute-done.20.refs_1_), custom_call_target="tpu_custom_call" | custom-call | bytes 131076 | tf_op jit(solution)/shard_map/finish_kv/pallas_call | solution.py:41
  (16 shorter events, 0.2 us)
Async XLA Ops:
  0.6 6.5 %collective-permute-start.1 = (bf16[64,256]{1,0:T(8,128)(2,1)}, bf16[64,256]{1,0:T(8,128)(2,1)S(1)}, u32[]{:S(2)}, u32[]{:S(2)}) collective-permute-start(bf16[64,256]{1,0:T(8,128)(2,1)} %bitcast.21), channel_id=1, source_target_pairs={{0,8},{8,0},{16,24},{24,16},{1,9},{9,1},{17,25},{25,17},{2,10},{10... | collective-permute-start | bytes 98312 | tf_op jit(solution)/shard_map/ppermute | solution.py:26
  3.6 4.1 %collective-permute-start.2 = (bf16[64,256]{1,0:T(8,128)(2,1)}, bf16[64,256]{1,0:T(8,128)(2,1)S(1)}, u32[]{:S(2)}, u32[]{:S(2)}) collective-permute-start(bf16[64,256]{1,0:T(8,128)(2,1)} %bitcast.23), channel_id=1, source_target_pairs={{0,8},{8,0},{16,24},{24,16},{1,9},{9,1},{17,25},{25,17},{2,10},{10... | collective-permute-start | bytes 98312 | tf_op jit(solution)/shard_map/ppermute | solution.py:26
  5.2 0.9 %copy-start = (bf16[2,32,2048]{2,1,0:T(8,128)(2,1)S(1)}, bf16[2,32,2048]{2,1,0:T(8,128)(2,1)}, u32[]{:S(2)}) copy-start(bf16[2,32,2048]{2,1,0:T(8,128)(2,1)} %param.5) | copy-start | bytes 786436
  6.1 0.9 %copy-start.1 = (bf16[2,32,2048]{2,1,0:T(8,128)(2,1)S(1)}, bf16[2,32,2048]{2,1,0:T(8,128)(2,1)}, u32[]{:S(2)}) copy-start(bf16[2,32,2048]{2,1,0:T(8,128)(2,1)} %param.8) | copy-start | bytes 786436
  7.8 6.5 %collective-permute-start.5 = (bf16[2,64,256]{2,1,0:T(8,128)(2,1)S(1)}, bf16[2,64,256]{2,1,0:T(8,128)(2,1)S(1)}, u32[]{:S(2)}, u32[]{:S(2)}) collective-permute-start(bf16[2,64,256]{2,1,0:T(8,128)(2,1)S(1)} %pack_kv.1), channel_id=1, source_target_pairs={{0,6},{1,7},{2,4},{3,5},{4,2},{5,3},{6,0},{7,1},{8,14},{9,15},{10,... | collective-permute-start | bytes 196616 | tf_op jit(solution)/shard_map/ppermute | solution.py:26
  11.4 5.3 %collective-permute-start.4 = (bf16[2,64,256]{2,1,0:T(8,128)(2,1)S(1)}, bf16[2,64,256]{2,1,0:T(8,128)(2,1)S(1)}, u32[]{:S(2)}, u32[]{:S(2)}) collective-permute-start(bf16[2,64,256]{2,1,0:T(8,128)(2,1)S(1)} %pack_kv.1), channel_id=1, source_target_pairs={{0,4},{1,5},{2,6},{3,7},{4,0},{5,1},{6,2},{7,3},{8,12},{9,13},{10,... | collective-permute-start | bytes 196616 | tf_op jit(solution)/shard_map/ppermute | solution.py:26
  11.5 5.3 %collective-permute-start.3 = (bf16[2,64,256]{2,1,0:T(8,128)(2,1)S(1)}, bf16[2,64,256]{2,1,0:T(8,128)(2,1)S(1)}, u32[]{:S(2)}, u32[]{:S(2)}) collective-permute-start(bf16[2,64,256]{2,1,0:T(8,128)(2,1)S(1)} %pack_kv.1), channel_id=1, source_target_pairs={{0,2},{1,3},{2,0},{3,1},{4,6},{5,7},{6,4},{7,5},{8,10},{9,11},{10,... | collective-permute-start | bytes 196616 | tf_op jit(solution)/shard_map/ppermute | solution.py:26
  12.2 7.0 %collective-permute-start = (bf16[2,64,1024]{2,1,0:T(8,128)(2,1)S(1)}, bf16[2,64,1024]{2,1,0:T(8,128)(2,1)S(1)}, u32[]{:S(2)}, u32[]{:S(2)}) collective-permute-start(bf16[2,64,1024]{2,1,0:T(8,128)(2,1)S(1)} %get-tuple-element.43), channel_id=1, source_target_pairs={{0,8},{8,0},{16,24},{24,16},{1,9},{9,1},{17,25},{25,17},{2,10},{10... | collective-permute-start | bytes 786440 | tf_op jit(solution)/shard_map/ppermute | solution.py:26
  16.8 2.4 %collective-permute-start.6 = (bf16[4,2,64,256]{3,2,1,0:T(8,128)(2,1)S(1)}, bf16[4,2,64,256]{3,2,1,0:T(8,128)(2,1)S(1)}, u32[]{:S(2)}, u32[]{:S(2)}) collective-permute-start(bf16[4,2,64,256]{3,2,1,0:T(8,128)(2,1)S(1)} %pad_maximum_fusion.refs_2_.kv_ref), channel_id=1, source_target_pairs={{0,1},{1,0},{2,3},{3,2},{4,5},{5,4},{6,7},{7,6},{8,9},{9,8},{10,11... | collective-permute-start | bytes 786440 | tf_op jit(solution)/shard_map/ppermute | solution.py:26
  16.9 8.7 %collective-permute-start.7 = (bf16[4,2,64,256]{3,2,1,0:T(8,128)(2,1)S(1)}, bf16[4,2,64,256]{3,2,1,0:T(8,128)(2,1)S(1)}, u32[]{:S(2)}, u32[]{:S(2)}) collective-permute-start(bf16[4,2,64,256]{3,2,1,0:T(8,128)(2,1)S(1)} %pad_maximum_fusion.refs_2_.kv_ref), channel_id=1, source_target_pairs={{0,16},{8,24},{16,0},{24,8},{1,17},{9,25},{17,1},{25,9},{2,18},{10... | collective-permute-start | bytes 786440 | tf_op jit(solution)/shard_map/ppermute | solution.py:26
  25.6 1.5 %collective-permute-start.8 = (bf16[4,2,64,256]{3,2,1,0:T(8,128)(2,1)S(1)}, bf16[4,2,64,256]{3,2,1,0:T(8,128)(2,1)S(1)}, u32[]{:S(2)}, u32[]{:S(2)}) collective-permute-start(bf16[4,2,64,256]{3,2,1,0:T(8,128)(2,1)S(1)} %collective-permute-done.7.refs_0_), channel_id=1, source_target_pairs={{0,1},{1,0},{2,3},{3,2},{4,5},{5,4},{6,7},{7,6},{8,9},{9,8},{10,11... | collective-permute-start | bytes 786440 | tf_op jit(solution)/shard_map/ppermute | solution.py:26
  33.2 3.1 %collective-permute-start.11 = (bf16[2,2,64,256]{3,2,1,0:T(8,128)(2,1)S(1)}, bf16[2,2,64,256]{3,2,1,0:T(8,128)(2,1)S(1)}, u32[]{:S(2)}, u32[]{:S(2)}) collective-permute-start(bf16[2,2,64,256]{3,2,1,0:T(8,128)(2,1)S(1)} %get-tuple-element.63), channel_id=1, source_target_pairs={{0,1},{1,0},{2,3},{3,2},{4,5},{5,4},{6,7},{7,6},{8,9},{9,8},{10,11... | collective-permute-start | bytes 393224 | tf_op jit(solution)/shard_map/ppermute | solution.py:26
  33.4 4.5 %collective-permute-start.16 = (bf16[2,2,64,256]{3,2,1,0:T(8,128)(2,1)S(1)}, bf16[2,2,64,256]{3,2,1,0:T(8,128)(2,1)S(1)}, u32[]{:S(2)}, u32[]{:S(2)}) collective-permute-start(bf16[2,2,64,256]{3,2,1,0:T(8,128)(2,1)S(1)} %get-tuple-element.69), channel_id=1, source_target_pairs={{0,1},{1,0},{2,3},{3,2},{4,5},{5,4},{6,7},{7,6},{8,9},{9,8},{10,11... | collective-permute-start | bytes 393224 | tf_op jit(solution)/shard_map/ppermute | solution.py:26
  35.7 5.9 %collective-permute-start.13 = (bf16[2,2,64,256]{3,2,1,0:T(8,128)(2,1)S(1)}, bf16[2,2,64,256]{3,2,1,0:T(8,128)(2,1)S(1)}, u32[]{:S(2)}, u32[]{:S(2)}) collective-permute-start(bf16[2,2,64,256]{3,2,1,0:T(8,128)(2,1)S(1)} %get-tuple-element.64), channel_id=1, source_target_pairs={{0,1},{1,0},{2,3},{3,2},{4,5},{5,4},{6,7},{7,6},{8,9},{9,8},{10,11... | collective-permute-start | bytes 393224 | tf_op jit(solution)/shard_map/ppermute | solution.py:26
  35.9 8.8 %collective-permute-start.18 = (bf16[2,2,64,256]{3,2,1,0:T(8,128)(2,1)S(1)}, bf16[2,2,64,256]{3,2,1,0:T(8,128)(2,1)S(1)}, u32[]{:S(2)}, u32[]{:S(2)}) collective-permute-start(bf16[2,2,64,256]{3,2,1,0:T(8,128)(2,1)S(1)} %get-tuple-element.72), channel_id=1, source_target_pairs={{0,1},{1,0},{2,3},{3,2},{4,5},{5,4},{6,7},{7,6},{8,9},{9,8},{10,11... | collective-permute-start | bytes 393224 | tf_op jit(solution)/shard_map/ppermute | solution.py:26
  36.3 6.4 %collective-permute-start.12 = (bf16[2,2,64,256]{3,2,1,0:T(8,128)(2,1)S(1)}, bf16[2,2,64,256]{3,2,1,0:T(8,128)(2,1)S(1)}, u32[]{:S(2)}, u32[]{:S(2)}) collective-permute-start(bf16[2,2,64,256]{3,2,1,0:T(8,128)(2,1)S(1)} %sum_cores.2), channel_id=1, source_target_pairs={{0,16},{8,24},{16,0},{24,8},{1,17},{9,25},{17,1},{25,9},{2,18},{10... | collective-permute-start | bytes 393224 | tf_op jit(solution)/shard_map/ppermute | solution.py:26
  37.9 7.9 %collective-permute-start.17 = (bf16[2,2,64,256]{3,2,1,0:T(8,128)(2,1)S(1)}, bf16[2,2,64,256]{3,2,1,0:T(8,128)(2,1)S(1)}, u32[]{:S(2)}, u32[]{:S(2)}) collective-permute-start(bf16[2,2,64,256]{3,2,1,0:T(8,128)(2,1)S(1)} %sum_cores.3), channel_id=1, source_target_pairs={{0,16},{8,24},{16,0},{24,8},{1,17},{9,25},{17,1},{25,9},{2,18},{10... | collective-permute-start | bytes 393224 | tf_op jit(solution)/shard_map/ppermute | solution.py:26
  38.5 14.0 %collective-permute-start.9 = (bf16[64,1024]{1,0:T(8,128)(2,1)S(1)}, bf16[64,1024]{1,0:T(8,128)(2,1)S(1)}, u32[]{:S(2)}, u32[]{:S(2)}) collective-permute-start(bf16[64,1024]{1,0:T(8,128)(2,1)S(1)} %get-tuple-element.52), channel_id=1, source_target_pairs={{0,8},{8,0},{16,24},{24,16},{1,9},{9,1},{17,25},{25,17},{2,10},{10... | collective-permute-start | bytes 393224 | tf_op jit(solution)/shard_map/ppermute | solution.py:26
  41.6 10.9 %collective-permute-start.10 = (bf16[64,1024]{1,0:T(8,128)(2,1)S(1)}, bf16[64,1024]{1,0:T(8,128)(2,1)S(1)}, u32[]{:S(2)}, u32[]{:S(2)}) collective-permute-start(bf16[64,1024]{1,0:T(8,128)(2,1)S(1)} %get-tuple-element.59), channel_id=1, source_target_pairs={{0,8},{8,0},{16,24},{24,16},{1,9},{9,1},{17,25},{25,17},{2,10},{10... | collective-permute-start | bytes 393224 | tf_op jit(solution)/shard_map/ppermute | solution.py:26
  42.8 6.6 %collective-permute-start.14 = (bf16[2,64,256]{2,1,0:T(8,128)(2,1)S(1)}, bf16[2,64,256]{2,1,0:T(8,128)(2,1)S(1)}, u32[]{:S(2)}, u32[]{:S(2)}) collective-permute-start(bf16[2,64,256]{2,1,0:T(8,128)(2,1)S(1)} %get-tuple-element.66), channel_id=1, source_target_pairs={{0,4},{1,5},{2,6},{3,7},{4,0},{5,1},{6,2},{7,3},{8,12},{9,13},{10,... | collective-permute-start | bytes 196616 | tf_op jit(solution)/shard_map/ppermute | solution.py:26
  44.7 6.2 %collective-permute-start.15 = (bf16[2,64,256]{2,1,0:T(8,128)(2,1)S(1)}, bf16[2,64,256]{2,1,0:T(8,128)(2,1)S(1)}, u32[]{:S(2)}, u32[]{:S(2)}) collective-permute-start(bf16[2,64,256]{2,1,0:T(8,128)(2,1)S(1)} %get-tuple-element.67), channel_id=1, source_target_pairs={{0,6},{1,7},{2,4},{3,5},{4,2},{5,3},{6,0},{7,1},{8,14},{9,15},{10,... | collective-permute-start | bytes 196616 | tf_op jit(solution)/shard_map/ppermute | solution.py:26
  45.9 5.0 %collective-permute-start.19 = (bf16[2,64,256]{2,1,0:T(8,128)(2,1)S(1)}, bf16[2,64,256]{2,1,0:T(8,128)(2,1)S(1)}, u32[]{:S(2)}, u32[]{:S(2)}) collective-permute-start(bf16[2,64,256]{2,1,0:T(8,128)(2,1)S(1)} %get-tuple-element.75), channel_id=1, source_target_pairs={{0,2},{1,3},{2,0},{3,1},{4,6},{5,7},{6,4},{7,5},{8,10},{9,11},{10,... | collective-permute-start | bytes 196616 | tf_op jit(solution)/shard_map/ppermute | solution.py:26
  50.9 4.0 %collective-permute-start.20 = (bf16[64,256]{1,0:T(8,128)(2,1)S(1)}, bf16[64,256]{1,0:T(8,128)(2,1)S(1)}, u32[]{:S(2)}, u32[]{:S(2)}) collective-permute-start(bf16[64,256]{1,0:T(8,128)(2,1)S(1)} %get-tuple-element.77), channel_id=1, source_target_pairs={{0,8},{8,0},{16,24},{24,16},{1,9},{9,1},{17,25},{25,17},{2,10},{10... | collective-permute-start | bytes 98312 | tf_op jit(solution)/shard_map/ppermute | solution.py:26

commit v6 on v5

--- a/solution.py
+++ b/solution.py
@@ -141,11 +141,11 @@
     def fold(self, block):
         return block.reshape(block.shape[0] // 8, 8, self.lanes)
 
-    def scores(self, tile, chunks, kv_refs, q, e_ref, cols, info_ref):
+    def scores(self, tile, chunks, kv_refs, q_t, e_ref, cols, info_ref):
         gap = self.gap(tile, info_ref)
         top = jnp.full((8, self.lanes), FLOOR, F32)
         for i, ref in enumerate(kv_refs):
-            scores = dot_rows(self.keys(ref), q)
+            scores = dot(self.keys(ref), q_t)
             for row, part in self.masked(scores, gap, chunks[i], info_ref):
                 e_ref[pl.ds(i * self.chunk_keys + row, part.shape[0]), cols] = part
                 top = jnp.maximum(top, jnp.max(self.fold(part), axis=0))
@@ -176,83 +176,103 @@
                 out_ref[:, :, :, HD:] = dot(p_ref[at, :], do_ref[...]).astype(BF).reshape(shape)
 
 
+def forward_part(plan, chunks, info_ref, q_t, kv_refs, e_ref, top_ref, sum_ref, mix_ref, turned_ref):
+    plan.turn(kv_refs, turned_ref)
+    for tile in range(len(plan.tiles)):
+        at = plan.at(tile)
+        top = plan.scores(tile, chunks, kv_refs, q_t[:, at], e_ref, at, info_ref)
+        top_ref[:, at] = top
+        sum_ref[:, at] = plan.exponents(len(chunks), e_ref, at, top)
+        mixed = jnp.zeros((HD, plan.lanes), F32)
+        for i in range(len(chunks)):
+            weights = e_ref[plan.keys_at(i), at].astype(BF)
+            mixed = mixed + dot(turned_ref[pl.ds(HD, HD), plan.keys_at(i)], weights)
+        mix_ref[:, at] = mixed
+
+
 def near_kernel(plan, chunks, info_ref, *refs):
     kv, count = plan.kv, len(chunks)
     q_parts, refs = refs[:kv], refs[kv:]
     kv_refs, refs = refs[:count], refs[count:]
-    q_all, do_all, e_ref, top_ref, sum_ref, mix_ref, turned_ref = refs
-    plan.turn(kv_refs, turned_ref)
+    (q_all, do_all, q_t, do_t), refs = refs[:4], refs[4:]
     for tile, (s, start) in enumerate(plan.tiles):
         span = pl.ds(start, plan.tile_rows)
         for n in range(plan.group):
             at = pl.ds(tile * plan.lanes + n * plan.tile_rows, plan.tile_rows)
             q_all[at, :] = q_parts[s][0, span, pl.ds(n * HD, HD)]
             do_all[at, :] = q_parts[s][1, span, pl.ds(n * HD, HD)]
-    for tile in range(len(plan.tiles)):
         at = plan.at(tile)
-        top = plan.scores(tile, chunks, kv_refs, q_all[at, :], e_ref, at, info_ref)
-        top_ref[:, at] = top
-        sum_ref[:, at] = plan.exponents(count, e_ref, at, top)
-        mixed = jnp.zeros((HD, plan.lanes), F32)
-        for i in range(count):
-            weights = e_ref[plan.keys_at(i), at].astype(BF)
-            mixed = mixed + dot(turned_ref[pl.ds(HD, HD), plan.keys_at(i)], weights)
-        mix_ref[:, at] = mixed
-
-
-def far_kernel(plan, chunks, info_ref, q_all, do_all, near_top, near_sum, near_mix, *refs):
+        q_t[:, at] = q_all[at, :].T
+        do_t[:, at] = do_all[at, :].T
+    forward_part(plan, chunks, info_ref, q_t, kv_refs, *refs)
+
+
+def mid_kernel(plan, chunks, info_ref, q_t, *refs):
+    forward_part(plan, chunks, info_ref, q_t, refs[: len(chunks)], *refs[len(chunks) :])
+
+
+def far_kernel(plan, chunks, others, info_ref, q_all, do_all, q_t, do_t, *refs):
     kv, count = plan.kv, len(chunks)
+    partial, refs = [refs[3 * i : 3 * i + 3] for i in range(others)], refs[3 * others :]
     kv_refs, refs = refs[:count], refs[count:]
     att_refs, refs = refs[:kv], refs[kv:]
-    near_scale, delta_ref, q_grad_ref = refs[:3]
-    dkv_refs, refs = refs[3 : 3 + count * plan.parts], refs[3 + count * plan.parts :]
-    turned_ref, e_ref, p_ref, ds_ref = refs
+    scale_refs, (delta_ref, q_grad_ref), refs = refs[:others], refs[others : others + 2], refs[others + 2 :]
+    dkv_refs, (turned_ref, e_ref, p_ref, ds_ref) = refs[:-4], refs[-4:]
     here = pl.ds(0, plan.lanes)
     plan.turn(kv_refs, turned_ref)
     for tile, (s, _) in enumerate(plan.tiles):
         at = plan.at(tile)
-        top = plan.scores(tile, chunks, kv_refs, q_all[at, :], e_ref, here, info_ref)
-        top = jnp.maximum(top, near_top[:, at])
+        top = plan.scores(tile, chunks, kv_refs, q_t[:, at], e_ref, here, info_ref)
+        for top_ref, _, _ in partial:
+            top = jnp.maximum(top, top_ref[:, at])
         total = plan.exponents(count, e_ref, here, top)
-        factor = jnp.exp2((near_top[:, at] - top) * EXPO)
-        inverse = 1.0 / (total + factor * near_sum[:, at])
-        near_scale[:, at] = factor * inverse
-        mixed = near_mix[:, at] * (factor * inverse)
+        factors = [jnp.exp2((top_ref[:, at] - top) * EXPO) for top_ref, _, _ in partial]
+        for factor, (_, sum_ref, _) in zip(factors, partial):
+            total = total + factor * sum_ref[:, at]
+        inverse = 1.0 / total
+        mixed = jnp.zeros((HD, plan.lanes), F32)
+        for factor, scale_ref, (_, _, mix_ref) in zip(factors, scale_refs, partial):
+            scale_ref[:, at] = factor * inverse
+            mixed = mixed + mix_ref[:, at] * (factor * inverse)
         for i in range(count):
             probs = (e_ref[plan.keys_at(i), here] * inverse).astype(BF)
             p_ref[plan.keys_at(i), at] = probs
             mixed = mixed + dot(turned_ref[pl.ds(HD, HD), plan.keys_at(i)], probs)
+        mixed = mixed.astype(BF).astype(F32)
         plan.store_heads(att_refs[s], tile, mixed)
-        do = do_all[at, :]
-        delta = jnp.sum(do.astype(F32).T * mixed.astype(BF).astype(F32), axis=0, keepdims=True)
+        do = do_t[:, at]
+        delta = jnp.sum(do.astype(F32) * mixed, axis=0, keepdims=True)
         delta_ref[:, at] = delta
         q_grad = jnp.zeros((HD, plan.lanes), F32)
         for i, ref in enumerate(kv_refs):
             probs = e_ref[plan.keys_at(i), here] * inverse
-            grad_s = (probs * (dot_rows(plan.values(ref), do) - delta)).astype(BF)
+            grad_s = (probs * (dot(plan.values(ref), do) - delta)).astype(BF)
             ds_ref[plan.keys_at(i), at] = grad_s
             q_grad = q_grad + dot(turned_ref[pl.ds(0, HD), plan.keys_at(i)], grad_s)
         q_grad_ref[:, at] = q_grad
     plan.back(kv_refs, dkv_refs, p_ref, ds_ref, q_all, do_all)
 
 
-def near_back_kernel(plan, chunk, q_all, do_all, e_ref, near_scale, delta_ref, q_grad_in, kv_ref, *refs):
+def back_kernel(plan, rows_at, last, order, q_all, do_all, do_t, e_ref, scale_ref, delta_ref, q_grad_in, *refs):
+    count = len(rows_at)
+    kv_refs, refs = refs[:count], refs[count + order :]
     refs, (turned_ref, p_ref, ds_ref) = refs[:-3], refs[-3:]
-    outs, dkv_refs = refs[: -plan.parts], refs[-plan.parts :]
-    plan.turn([kv_ref], turned_ref)
+    outs, dkv_refs = refs[: -plan.parts * count], refs[-plan.parts * count :]
+    plan.turn(kv_refs, turned_ref)
     for tile, (s, _) in enumerate(plan.tiles):
         at = plan.at(tile)
-        do = do_all[at, :]
-        probs = e_ref[plan.keys_at(chunk), at] * near_scale[:, at]
-        p_ref[:, at] = probs.astype(BF)
-        grad_s = (probs * (dot_rows(plan.values(kv_ref), do) - delta_ref[:, at])).astype(BF)
-        ds_ref[:, at] = grad_s
-        q_grad = q_grad_in[:, at] + dot(turned_ref[pl.ds(0, HD), :], grad_s)
-        if chunk == 0:
+        q_grad = q_grad_in[:, at]
+        for i, ref in enumerate(kv_refs):
+            probs = e_ref[plan.keys_at(rows_at[i]), at] * scale_ref[:, at]
+            p_ref[plan.keys_at(i), at] = probs.astype(BF)
+            grad_s = (probs * (dot(plan.values(ref), do_t[:, at]) - delta_ref[:, at])).astype(BF)
+            ds_ref[plan.keys_at(i), at] = grad_s
+            q_grad = q_grad + dot(turned_ref[pl.ds(0, HD), plan.keys_at(i)], grad_s)
+        if last:
             plan.store_heads(outs[s], tile, q_grad * SCALING)
         else:
             outs[0][:, at] = q_grad
-    plan.back([kv_ref], dkv_refs, p_ref, ds_ref, q_all, do_all)
+    plan.back(kv_refs, dkv_refs, p_ref, ds_ref, q_all, do_all)
 
 
 def add_kernel(*refs):
@@ -363,32 +383,46 @@
     columns = [swap(column, "head", a * kv) for a in range(1, spans)]
     near_kv = [column] + [swap(column, "ctx", core) for core in range(1, cores)]
     near_chunks = [(0, core) for core in range(cores)]
-    far_chunks = [(a, core) for a in range(1, spans) for core in range(cores)]
+    mid_chunks = [(a, 0) for a in range(1, spans)]
+    far_chunks = [(a, core) for a in range(1, spans) for core in range(1, cores)]
 
     keys = plan.chunk_keys
-    near_keys, far_keys = len(near_chunks) * keys, len(far_chunks) * keys
     query_rows = plan.query_rows
-    row = f32(1, query_rows)
+    row, column_out = f32(1, query_rows), f32(HD, query_rows)
     dkv = bf(z_part, kv, rows, 2 * HD)
-    q_all, do_all, near_e, near_top, near_sum, near_mix = call(
+
+    def part_outs(chunks):
+        return [f32(len(chunks) * keys, query_rows), row, row, column_out]
+
+    q_all, do_all, q_t, do_t, near_e, *near = call(
         functools.partial(near_kernel, plan, near_chunks),
         "attend_near",
         (info, *q_parts, *near_kv),
-        [bf(query_rows, HD)] * 2 + [f32(near_keys, query_rows), row, row, f32(HD, query_rows)],
+        [bf(query_rows, HD)] * 2 + [bf(HD, query_rows)] * 2 + part_outs(near_chunks),
         [SMEM] + [VMEM] * (kv + len(near_kv)),
-        [pltpu.VMEM((2 * HD, near_keys), BF)],
-        near_keys * 4 * HD,
-        8 * near_keys * query_rows * HD,
-    )
-    far_kv = []
-    for part in after(columns, [near_top]):
-        far_kv += [part] + [swap(part, "ctx", core) for core in range(1, cores)]
+        [pltpu.VMEM((2 * HD, cores * keys), BF)],
+        cores * keys * 4 * HD,
+        8 * cores * keys * query_rows * HD,
+    )
+    mid_kv = after(columns, [near[0]])
+    far_kv = [swap(part, "ctx", core) for part in mid_kv for core in range(1, cores)]
+    mid_e, *mid = call(
+        functools.partial(mid_kernel, plan, mid_chunks),
+        "attend_mid",
+        (info, q_t, *mid_kv),
+        part_outs(mid_chunks),
+        [SMEM] + [VMEM] * (1 + len(mid_kv)),
+        [pltpu.VMEM((2 * HD, len(mid_kv) * keys), BF)],
+        len(mid_kv) * keys * 4 * HD,
+        8 * len(mid_kv) * keys * query_rows * HD,
+    )
+    far_keys = len(far_kv) * keys
     outs = call(
-        functools.partial(far_kernel, plan, far_chunks),
+        functools.partial(far_kernel, plan, far_chunks, 2),
         "attend_far",
-        (info, q_all, do_all, near_top, near_sum, near_mix, *far_kv),
-        [bf(rows, width)] * kv + [row, row, f32(HD, query_rows)] + [dkv] * (parts * len(far_kv)),
-        [SMEM] + [VMEM] * (5 + len(far_kv)),
+        (info, q_all, do_all, q_t, do_t, *near, *mid, *far_kv),
+        [bf(rows, width)] * kv + [row, row, row, column_out] + [dkv] * (parts * len(far_kv)),
+        [SMEM] + [VMEM] * (10 + len(far_kv)),
         [
             pltpu.VMEM((2 * HD, far_keys), BF),
             pltpu.VMEM((far_keys, plan.lanes), F32),
@@ -399,37 +433,44 @@
         16 * far_keys * query_rows * HD,
     )
     att_parts, outs = outs[:kv], outs[kv:]
-    (near_scale, delta, q_grad), far_dkv = outs[:3], outs[3:]
-
-    sums = [[] for _ in range(parts)]
-    for a in range(spans - 1):
-        earlier = []
-        for p in range(parts):
-            ours = [far_dkv[(a * cores + core) * parts + p] for core in range(cores)]
-            both = [ours[0]] + [swap(ours[core], "ctx", core) for core in range(1, cores)]
-            total = call(add_kernel, "sum_cores", after(both, earlier), [dkv])[0]
-            earlier = [total]
-            sums[p].append(swap(total, "head", (a + 1) * kv))
-    for core in reversed(range(cores)):
-        q_outs = [f32(HD, query_rows)] if core else [bf(rows, width)] * kv
+    (near_scale, mid_scale, delta, q_grad), far_dkv = outs[:4], outs[4:]
+
+    def back(rows_at, last, e, scale, q_grad, kv_refs, order):
+        count = len(rows_at)
+        q_outs = [bf(rows, width)] * kv if last else [column_out]
         outs = call(
-            functools.partial(near_back_kernel, plan, core),
-            "attend_near_back",
-            (q_all, do_all, near_e, near_scale, delta, q_grad, near_kv[core]),
-            q_outs + [dkv] * parts,
+            functools.partial(back_kernel, plan, rows_at, last, len(order)),
+            "attend_back",
+            (q_all, do_all, do_t, e, scale, delta, q_grad, *kv_refs, *order),
+            q_outs + [dkv] * (parts * count),
             None,
             [
-                pltpu.VMEM((2 * HD, keys), BF),
-                pltpu.VMEM((keys, query_rows), BF),
-                pltpu.VMEM((keys, query_rows), BF),
+                pltpu.VMEM((2 * HD, count * keys), BF),
+                pltpu.VMEM((count * keys, query_rows), BF),
+                pltpu.VMEM((count * keys, query_rows), BF),
             ],
-            keys * (4 * HD + 4 * query_rows),
-            12 * keys * query_rows * HD,
+            count * keys * (4 * HD + 4 * query_rows),
+            12 * count * keys * query_rows * HD,
         )
+        return outs[: len(q_outs)], outs[len(q_outs) :]
+
+    (q_grad,), mid_dkv = back(list(range(spans - 1)), False, mid_e, mid_scale, q_grad, mid_kv, [])
+    sums = [[] for _ in range(parts)]
+    totals = []
+    for a in range(spans - 1):
+        for p in reversed(range(parts)):
+            both = [mid_dkv[a * parts + p]]
+            for core in range(1, cores):
+                ours = far_dkv[(a * (cores - 1) + core - 1) * parts + p]
+                both.append(swap(ours, "ctx", core))
+            totals += call(add_kernel, "sum_cores", after(both, totals[-1:]), [dkv])
+            sums[p].append(swap(totals[-1], "head", (a + 1) * kv))
+    order = [swap(totals[-1][0, 0, :, :HD], "ctx", 1)] if cores > 1 else []
+    for core in reversed(range(cores)):
+        outs, parts_dkv = back([core], core == 0, near_e, near_scale, q_grad, [near_kv[core]], order)
         q_grad = outs[0]
         for p in range(parts):
-            part = outs[len(q_outs) + p]
-            sums[p].append(swap(part, "ctx", core) if core else part)
+            sums[p].append(swap(parts_dkv[p], "ctx", core) if core else parts_dkv[p])
     q_grad_parts = outs[:kv]
     z_parts = [None] * z_devices
     for p in range(parts):

time: 55.9 us -> 58.4 us (1.045)
  Pallas kernels: 14.9 us -> 17.6 us
  waiting for transfers between devices: 14.8 us -> 14.1 us
    pallas_call x13 -> x15, Pallas kernels: 14.9 us -> 17.6 us  [call(): pl.pallas_call(kernel, out_shape=list(outs), in_specs=specs or [VMEM] * l...]
    ppermute x21 -> x22, waiting for transfers between devices: 14.8 us -> 14.1 us  [swap(): return lax.ppermute(block, axis, [(i, i ^ mask) for i in range(size)])]
    ppermute x21 -> x22, starting transfers between devices: 21.1 us -> 21.4 us  [swap(): return lax.ppermute(block, axis, [(i, i ^ mask) for i in range(size)])]
  transfers between devices with their start and end apart: 21 -> 22, of which waited for: 9 -> 8; matrix products, arithmetic and copies ran while one was open for 4% -> 4% of each run, Pallas kernels for 15% -> 21%
where the time goes in v6:
time: 58.4 us; the launch traced here: 58.1 us
  starting transfers between devices  21.4 us (37%)
  Pallas kernels  17.6 us (30%)
  waiting for transfers between devices  14.1 us (24%)
  local copies, waits for them, and re-layouts  3.34 us (6%)
  between operations  0.79 us (1%)
  other arithmetic  0.77 us (1%)
    ppermute x22, starting transfers between devices, swap(): return lax.ppermute(block, axis, [(i, i ^ mask) for i in range(size)])  21.4 us
    pallas_call x15, Pallas kernels, call(): pl.pallas_call(kernel, out_shape=list(outs), in_specs=specs or [VMEM] * l...  17.6 us
    ppermute x22, waiting for transfers between devices, swap(): return lax.ppermute(block, axis, [(i, i ^ mask) for i in range(size)])  14.1 us
    unnamed x4, local copies, waits for them, and re-layouts  1.9 us
    dynamic_slice x2, local copies, waits for them, and re-layouts, shards(): lax.dynamic_slice_in_dim(block, mine, HD, 1)  1.44 us
  transfers between devices with their start and end apart: 22, of which 8 were waited for; matrix products, arithmetic and copies ran while one was open for 4% of the time, Pallas kernels for 21%

profile of v6, /device:TPU:0, one launch (start us, length us, event | category | flops | bytes accessed | tf_op | source)
XLA Modules:
  0.0 58.1 jit_solution(4146615399313047579)
XLA Ops:
  0.6 3.0 %collective-permute-start.1 = (bf16[64,256]{1,0:T(8,128)(2,1)}, bf16[64,256]{1,0:T(8,128)(2,1)S(1)}, u32[]{:S(2)}, u32[]{:S(2)}) collective-permute-start(bf16[64,256]{1,0:T(8,128)(2,1)} %bitcast.23), channel_id=1, source_target_pairs={{0,8},{8,0},{16,24},{24,16},{1,9},{9,1},{17,25},{25,17},{2,10},{10... | collective-permute-start | bytes 98312 | tf_op jit(solution)/shard_map/ppermute | solution.py:26
  3.6 0.1 collective-permute-start.2
  3.7 0.7 %constant_dynamic-slice_fusion.1 = bf16[64,128]{1,0:T(8,128)(2,1)S(1)} fusion(bf16[64,256]{1,0:T(8,128)(2,1)} %bitcast.24, s32[]{:T(128)S(6)} %select_n.14), kind=kLoop, calls=%fused_computation.5 | loop fusion | bytes 32772 | tf_op jit(solution)/shard_map/dynamic_slice | solution.py:362
  4.4 0.7 %constant_dynamic-slice_fusion = bf16[64,128]{1,0:T(8,128)(2,1)S(1)} fusion(bf16[64,256]{1,0:T(8,128)(2,1)} %bitcast.26, s32[]{:T(128)S(6)} %select_n.14), kind=kLoop, calls=%fused_computation.4 | loop fusion | bytes 32772 | tf_op jit(solution)/shard_map/dynamic_slice | solution.py:362
  5.2 0.9 %copy-done = bf16[2,32,2048]{2,1,0:T(8,128)(2,1)S(1)} copy-done((bf16[2,32,2048]{2,1,0:T(8,128)(2,1)S(1)}, bf16[2,32,2048]{2,1,0:T(8,128)(2,1)}, u32[]{:S(2)}) %copy-start) | copy-done | bytes 262168
  6.1 0.9 %copy-done.1 = bf16[2,32,2048]{2,1,0:T(8,128)(2,1)S(1)} copy-done((bf16[2,32,2048]{2,1,0:T(8,128)(2,1)S(1)}, bf16[2,32,2048]{2,1,0:T(8,128)(2,1)}, u32[]{:S(2)}) %copy-start.1) | copy-done | bytes 262168
  7.1 0.0 collective-permute-done.1.refs_1_
  7.1 0.6 %collective-permute-done.2.refs_2_ = bf16[64,256]{1,0:T(8,128)(2,1)S(1)} collective-permute-done((bf16[64,256]{1,0:T(8,128)(2,1)}, bf16[64,256]{1,0:T(8,128)(2,1)S(1)}, u32[]{:S(2)}, u32[]{:S(2)}) %collective-permute-start.2) | collective-permute-done | bytes 32800 | tf_op jit(solution)/shard_map/ppermute | solution.py:26
  7.8 3.7 %collective-permute-start.5 = (bf16[2,64,256]{2,1,0:T(8,128)(2,1)S(1)}, bf16[2,64,256]{2,1,0:T(8,128)(2,1)S(1)}, u32[]{:S(2)}, u32[]{:S(2)}) collective-permute-start(bf16[2,64,256]{2,1,0:T(8,128)(2,1)S(1)} %pack_kv.1), channel_id=1, source_target_pairs={{0,6},{1,7},{2,4},{3,5},{4,2},{5,3},{6,0},{7,1},{8,14},{9,15},{10,... | collective-permute-start | bytes 196616 | tf_op jit(solution)/shard_map/ppermute | solution.py:26
  11.4 0.0 collective-permute-start.4
  11.5 0.8 %collective-permute-start.3 = (bf16[2,64,256]{2,1,0:T(8,128)(2,1)S(1)}, bf16[2,64,256]{2,1,0:T(8,128)(2,1)S(1)}, u32[]{:S(2)}, u32[]{:S(2)}) collective-permute-start(bf16[2,64,256]{2,1,0:T(8,128)(2,1)S(1)} %pack_kv.1), channel_id=1, source_target_pairs={{0,2},{1,3},{2,0},{3,1},{4,6},{5,7},{6,4},{7,5},{8,10},{9,11},{10,... | collective-permute-start | bytes 196616 | tf_op jit(solution)/shard_map/ppermute | solution.py:26
  12.2 1.3 %collective-permute-start = (bf16[2,64,1024]{2,1,0:T(8,128)(2,1)S(1)}, bf16[2,64,1024]{2,1,0:T(8,128)(2,1)S(1)}, u32[]{:S(2)}, u32[]{:S(2)}) collective-permute-start(bf16[2,64,1024]{2,1,0:T(8,128)(2,1)S(1)} %get-tuple-element.51), channel_id=1, source_target_pairs={{0,8},{8,0},{16,24},{24,16},{1,9},{9,1},{17,25},{25,17},{2,10},{10... | collective-permute-start | bytes 786440 | tf_op jit(solution)/shard_map/ppermute | solution.py:26
  13.5 0.7 %collective-permute-done.5 = bf16[2,64,256]{2,1,0:T(8,128)(2,1)S(1)} collective-permute-done((bf16[2,64,256]{2,1,0:T(8,128)(2,1)S(1)}, bf16[2,64,256]{2,1,0:T(8,128)(2,1)S(1)}, u32[]{:S(2)}, u32[]{:S(2)}) %collective-permute-start.5) | collective-permute-done | bytes 65568 | tf_op jit(solution)/shard_map/ppermute | solution.py:26
  14.3 2.5 %collective-permute-done.4 = bf16[2,64,256]{2,1,0:T(8,128)(2,1)S(1)} collective-permute-done((bf16[2,64,256]{2,1,0:T(8,128)(2,1)S(1)}, bf16[2,64,256]{2,1,0:T(8,128)(2,1)S(1)}, u32[]{:S(2)}, u32[]{:S(2)}) %collective-permute-start.4) | collective-permute-done | bytes 65568 | tf_op jit(solution)/shard_map/ppermute | solution.py:26
  16.8 0.1 collective-permute-start.6
  16.9 1.6 %collective-permute-start.7 = (bf16[4,2,64,256]{3,2,1,0:T(8,128)(2,1)S(1)}, bf16[4,2,64,256]{3,2,1,0:T(8,128)(2,1)S(1)}, u32[]{:S(2)}, u32[]{:S(2)}) collective-permute-start(bf16[4,2,64,256]{3,2,1,0:T(8,128)(2,1)S(1)} %pad_maximum_fusion.refs_2_.refs_0_), channel_id=1, source_target_pairs={{0,16},{8,24},{16,0},{24,8},{1,17},{9,25},{17,1},{25,9},{2,18},{10... | collective-permute-start | bytes 786440 | tf_op jit(solution)/shard_map/ppermute | solution.py:26
  18.5 0.7 %pad_add_fusion.info_ref = s32[18]{0:T(128)S(1)} fusion(s32[16]{0:T(128)} %param.9, s32[1]{0:T(128)} %bitcast.2, s32[1]{0:T(128)} %bitcast.1), kind=kLoop, calls=%fused_computation.3 | loop fusion | flops 36 | bytes 144 | tf_op jit(solution)/shard_map/concatenate | solution.py:342
  19.2 0.0 collective-permute-done.refs_1_
  19.2 0.0 collective-permute-done.6.refs_3_.refs_0_
  19.2 3.3 %attend_near.1 = (bf16[1024,128]{1,0:T(8,128)(2,1)S(1)}, bf16[1024,128]{1,0:T(8,128)(2,1)S(1)}, bf16[128,1024]{1,0:T(8,128)(2,1)S(1)}, bf16[128,1024]{1,0:T(8,12...) custom-call(s32[18]{0:T(128)S(1)} %pad_add_fusion.info_ref, ...), custom_call_target="tpu_custom_call" | custom-call | flops 1073741824 | bytes 6824008 | tf_op jit(solution)/shard_map/attend_near/pallas_call | solution.py:41
  22.5 3.1 %collective-permute-done.7.refs_0_ = bf16[4,2,64,256]{3,2,1,0:T(8,128)(2,1)S(1)} collective-permute-done((bf16[4,2,64,256]{3,2,1,0:T(8,128)(2,1)S(1)}, bf16[4,2,64,256]{3,2,1,0:T(8,128)(2,1)S(1)}, u32[]{:S(2)}, u32[]{:S(2)}) %collective-permute-start.7) | collective-permute-done | bytes 262176 | tf_op jit(solution)/shard_map/ppermute | solution.py:26
  25.6 0.0 collective-permute-start.8
  25.6 2.5 %attend_mid.1 = (f32[512,1024]{1,0:T(8,128)S(1)}, f32[1,1024]{1,0:T(1,128)S(1)}, f32[1,1024]{1,0:T(1,128)S(1)}, f32[128,1024]{1,0:T(8,128)S(1)}) custom-call(s32[18]{0:T(128)S(1)} %pad_add_fusion.info_ref, bf16[128,1024]{1,0:T(8,128)(2,1)S(1)} %get-tuple-element.55.q_t, bf16[4,2,64,256]{3,2,1,0:T(8,128)(2,1)S(1)} %collective-permute-done.7.refs_0_), custom_call_target="tpu_custom_call" | custom-call | flops 536870912 | bytes 3153992 | tf_op jit(solution)/shard_map/attend_mid/pallas_call | solution.py:41
  28.1 4.5 %attend_far.1 = (bf16[64,1024]{1,0:T(8,128)(2,1)S(1)}, bf16[64,1024]{1,0:T(8,128)(2,1)S(1)}, f32[1,1024]{1,0:T(1,128)S(1)}, f32[1,1024]{1,0:T(1,128)S(1)}, f32[1...) custom-call(s32[18]{0:T(128)S(1)} %pad_add_fusion.info_ref, ...), custom_call_target="tpu_custom_call" | custom-call | flops 1073741824 | bytes 3436616 | tf_op jit(solution)/shard_map/attend_far/pallas_call | solution.py:41
  32.6 0.6 collective-permute-start.11
  33.2 0.1 collective-permute-start.10
  33.3 1.9 %attend_back.3 = (f32[128,1024]{1,0:T(8,128)S(1)}, bf16[2,2,64,256]{3,2,1,0:T(8,128)(2,1)S(1)}, bf16[2,2,64,256]{3,2,1,0:T(8,128)(2,1)S(1)}) custom-call(bf16[1024,128]{1,0:T(8,128)(2,1)S(1)} %get-tuple-element.53.q_all, bf16[1024,128]{1,0:T(8,128)(2,1)S(1)} %get-tuple-element.54.do_all, bf16[128,1024]{1,0:T(8,128)(2,1)S(1)} %get-tuple-element.56.do_t, ...), custom_call_target="tpu_custom_call" | custom-call | flops 805306368 | bytes 4464640 | tf_op jit(solution)/shard_map/attend_back/pallas_call | solution.py:41
  35.3 0.5 collective-permute-start.12
  35.8 1.5 %collective-permute-start.14 = (bf16[2,2,64,256]{3,2,1,0:T(8,128)(2,1)S(1)}, bf16[2,2,64,256]{3,2,1,0:T(8,128)(2,1)S(1)}, u32[]{:S(2)}, u32[]{:S(2)}) collective-permute-start(bf16[2,2,64,256]{3,2,1,0:T(8,128)(2,1)S(1)} %sum_cores.3), channel_id=1, source_target_pairs={{0,16},{8,24},{16,0},{24,8},{1,17},{9,25},{17,1},{25,9},{2,18},{10... | collective-permute-start | bytes 393224 | tf_op jit(solution)/shard_map/ppermute | solution.py:26
  37.3 0.0 collective-permute-done.12.refs_1_
  37.3 1.9 %attend_back.4 = (f32[128,1024]{1,0:T(8,128)S(1)}, bf16[2,2,64,256]{3,2,1,0:T(8,128)(2,1)S(1)}, bf16[2,2,64,256]{3,2,1,0:T(8,128)(2,1)S(1)}) custom-call(bf16[1024,128]{1,0:T(8,128)(2,1)S(1)} %get-tuple-element.53.q_all, bf16[1024,128]{1,0:T(8,128)(2,1)S(1)} %get-tuple-element.54.do_all, bf16[128,1024]{1,0:T(8,128)(2,1)S(1)} %get-tuple-element.56.do_t, ...), custom_call_target="tpu_custom_call" | custom-call | flops 805306368 | bytes 6578176 | tf_op jit(solution)/shard_map/attend_back/pallas_call | solution.py:41
  39.2 0.1 collective-permute-start.15
  39.2 1.2 %collective-permute-start.18 = (bf16[2,2,64,256]{3,2,1,0:T(8,128)(2,1)S(1)}, bf16[2,2,64,256]{3,2,1,0:T(8,128)(2,1)S(1)}, u32[]{:S(2)}, u32[]{:S(2)}) collective-permute-start(bf16[2,2,64,256]{3,2,1,0:T(8,128)(2,1)S(1)} %sum_cores.2), channel_id=1, source_target_pairs={{0,16},{8,24},{16,0},{24,8},{1,17},{9,25},{17,1},{25,9},{2,18},{10... | collective-permute-start | bytes 393224 | tf_op jit(solution)/shard_map/ppermute | solution.py:26
  40.4 1.2 %collective-permute-start.9 = (bf16[64,1024]{1,0:T(8,128)(2,1)S(1)}, bf16[64,1024]{1,0:T(8,128)(2,1)S(1)}, u32[]{:S(2)}, u32[]{:S(2)}) collective-permute-start(bf16[64,1024]{1,0:T(8,128)(2,1)S(1)} %get-tuple-element.65), channel_id=1, source_target_pairs={{0,8},{8,0},{16,24},{24,16},{1,9},{9,1},{17,25},{25,17},{2,10},{10... | collective-permute-start | bytes 393224 | tf_op jit(solution)/shard_map/ppermute | solution.py:26
  41.6 1.9 %attend_back.5 = (bf16[64,1024]{1,0:T(8,128)(2,1)S(1)}, bf16[64,1024]{1,0:T(8,128)(2,1)S(1)}, bf16[2,2,64,256]{3,2,1,0:T(8,128)(2,1)S(1)}, bf16[2,2,64,256]{3,2,1,0:T(8,128)(2,1)S(1)}) custom-call(bf16[1024,128]{1,0:T(8,128)(2,1)S(1)} %get-tuple-element.53.q_all, bf16[1024,128]{1,0:T(8,128)(2,1)S(1)} %get-tuple-element.54.do_all, ...), custom_call_target="tpu_custom_call" | custom-call | flops 805306368 | bytes 6316032 | tf_op jit(solution)/shard_map/attend_back/pallas_call | solution.py:41
  43.5 0.9 %collective-permute-start.13 = (bf16[64,1024]{1,0:T(8,128)(2,1)S(1)}, bf16[64,1024]{1,0:T(8,128)(2,1)S(1)}, u32[]{:S(2)}, u32[]{:S(2)}) collective-permute-start(bf16[64,1024]{1,0:T(8,128)(2,1)S(1)} %get-tuple-element.81), channel_id=1, source_target_pairs={{0,8},{8,0},{16,24},{24,16},{1,9},{9,1},{17,25},{25,17},{2,10},{10... | collective-permute-start | bytes 393224 | tf_op jit(solution)/shard_map/ppermute | solution.py:26
  44.4 0.1 sum_heads.2
  44.4 1.9 %collective-permute-start.16 = (bf16[2,64,256]{2,1,0:T(8,128)(2,1)S(1)}, bf16[2,64,256]{2,1,0:T(8,128)(2,1)S(1)}, u32[]{:S(2)}, u32[]{:S(2)}) collective-permute-start(bf16[2,64,256]{2,1,0:T(8,128)(2,1)S(1)} %get-tuple-element.86), channel_id=1, source_target_pairs={{0,4},{1,5},{2,6},{3,7},{4,0},{5,1},{6,2},{7,3},{8,12},{9,13},{10,... | collective-permute-start | bytes 196616 | tf_op jit(solution)/shard_map/ppermute | solution.py:26
  46.3 1.1 %collective-permute-start.17 = (bf16[2,64,256]{2,1,0:T(8,128)(2,1)S(1)}, bf16[2,64,256]{2,1,0:T(8,128)(2,1)S(1)}, u32[]{:S(2)}, u32[]{:S(2)}) collective-permute-start(bf16[2,64,256]{2,1,0:T(8,128)(2,1)S(1)} %get-tuple-element.87), channel_id=1, source_target_pairs={{0,6},{1,7},{2,4},{3,5},{4,2},{5,3},{6,0},{7,1},{8,14},{9,15},{10,... | collective-permute-start | bytes 196616 | tf_op jit(solution)/shard_map/ppermute | solution.py:26
  47.5 0.1 sum_heads.3
  47.5 0.6 collective-permute-start.20
  48.1 3.7 %collective-permute-done.16.refs_0_ = bf16[2,64,256]{2,1,0:T(8,128)(2,1)S(1)} collective-permute-done((bf16[2,64,256]{2,1,0:T(8,128)(2,1)S(1)}, bf16[2,64,256]{2,1,0:T(8,128)(2,1)S(1)}, u32[]{:S(2)}, u32[]{:S(2)}) %collective-permute-start.16) | collective-permute-done | bytes 65568 | tf_op jit(solution)/shard_map/ppermute | solution.py:26
  51.8 0.9 %collective-permute-done.17.refs_1_ = bf16[2,64,256]{2,1,0:T(8,128)(2,1)S(1)} collective-permute-done((bf16[2,64,256]{2,1,0:T(8,128)(2,1)S(1)}, bf16[2,64,256]{2,1,0:T(8,128)(2,1)S(1)}, u32[]{:S(2)}, u32[]{:S(2)}) %collective-permute-start.17) | collective-permute-done | bytes 65568 | tf_op jit(solution)/shard_map/ppermute | solution.py:26
  52.7 0.7 %collective-permute-done.20.refs_3_ = bf16[2,64,256]{2,1,0:T(8,128)(2,1)S(1)} collective-permute-done((bf16[2,64,256]{2,1,0:T(8,128)(2,1)S(1)}, bf16[2,64,256]{2,1,0:T(8,128)(2,1)S(1)}, u32[]{:S(2)}, u32[]{:S(2)}) %collective-permute-start.20) | collective-permute-done | bytes 65568 | tf_op jit(solution)/shard_map/ppermute | solution.py:26
  53.4 1.3 %collective-permute-start.21 = (bf16[64,256]{1,0:T(8,128)(2,1)S(1)}, bf16[64,256]{1,0:T(8,128)(2,1)S(1)}, u32[]{:S(2)}, u32[]{:S(2)}) collective-permute-start(bf16[64,256]{1,0:T(8,128)(2,1)S(1)} %get-tuple-element.93), channel_id=1, source_target_pairs={{0,8},{8,0},{16,24},{24,16},{1,9},{9,1},{17,25},{25,17},{2,10},{10... | collective-permute-start | bytes 98312 | tf_op jit(solution)/shard_map/ppermute | solution.py:26
  54.8 0.8 %finish_q.1 = (bf16[64,2048]{1,0:T(8,128)(2,1)}, bf16[64,2048]{1,0:T(8,128)(2,1)}) custom-call(s32[1]{0:T(128)} %bitcast.group_ref, bf16[64,1024]{1,0:T(8,128)(2,1)S(1)} %get-tuple-element.64.refs_0_, bf16[64,1024]{1,0:T(8,128)(2,1)S(1)} %collective-permute-done.9.refs_1_, bf16[64,1024]{1,0:T(8,128)(2,1)S(1)} %get-tuple-element.80.refs_2_, ...), custom_call_target="tpu_custom_call" | custom-call | bytes 1048580 | tf_op jit(solution)/shard_map/finish_q/pallas_call | solution.py:41
  55.6 1.8 %collective-permute-done.21.refs_1_ = bf16[64,256]{1,0:T(8,128)(2,1)S(1)} collective-permute-done((bf16[64,256]{1,0:T(8,128)(2,1)S(1)}, bf16[64,256]{1,0:T(8,128)(2,1)S(1)}, u32[]{:S(2)}, u32[]{:S(2)}) %collective-permute-start.21) | collective-permute-done | bytes 32800 | tf_op jit(solution)/shard_map/ppermute | solution.py:26
  57.4 0.6 %finish_kv.1 = (bf16[64,256]{1,0:T(8,128)(2,1)}, bf16[64,256]{1,0:T(8,128)(2,1)}) custom-call(s32[1]{0:T(128)} %bitcast.group_ref, bf16[64,256]{1,0:T(8,128)(2,1)S(1)} %get-tuple-element.92.refs_0_, bf16[64,256]{1,0:T(8,128)(2,1)S(1)} %collective-permute-done.21.refs_1_), custom_call_target="tpu_custom_call" | custom-call | bytes 131076 | tf_op jit(solution)/shard_map/finish_kv/pallas_call | solution.py:41
  (21 shorter events, 0.2 us)
Async XLA Ops:
  0.6 6.5 %collective-permute-start.1 = (bf16[64,256]{1,0:T(8,128)(2,1)}, bf16[64,256]{1,0:T(8,128)(2,1)S(1)}, u32[]{:S(2)}, u32[]{:S(2)}) collective-permute-start(bf16[64,256]{1,0:T(8,128)(2,1)} %bitcast.23), channel_id=1, source_target_pairs={{0,8},{8,0},{16,24},{24,16},{1,9},{9,1},{17,25},{25,17},{2,10},{10... | collective-permute-start | bytes 98312 | tf_op jit(solution)/shard_map/ppermute | solution.py:26
  3.6 4.1 %collective-permute-start.2 = (bf16[64,256]{1,0:T(8,128)(2,1)}, bf16[64,256]{1,0:T(8,128)(2,1)S(1)}, u32[]{:S(2)}, u32[]{:S(2)}) collective-permute-start(bf16[64,256]{1,0:T(8,128)(2,1)} %bitcast.25), channel_id=1, source_target_pairs={{0,8},{8,0},{16,24},{24,16},{1,9},{9,1},{17,25},{25,17},{2,10},{10... | collective-permute-start | bytes 98312 | tf_op jit(solution)/shard_map/ppermute | solution.py:26
  5.2 0.9 %copy-start = (bf16[2,32,2048]{2,1,0:T(8,128)(2,1)S(1)}, bf16[2,32,2048]{2,1,0:T(8,128)(2,1)}, u32[]{:S(2)}) copy-start(bf16[2,32,2048]{2,1,0:T(8,128)(2,1)} %param.5) | copy-start | bytes 786436
  6.1 0.9 %copy-start.1 = (bf16[2,32,2048]{2,1,0:T(8,128)(2,1)S(1)}, bf16[2,32,2048]{2,1,0:T(8,128)(2,1)}, u32[]{:S(2)}) copy-start(bf16[2,32,2048]{2,1,0:T(8,128)(2,1)} %param.8) | copy-start | bytes 786436
  7.8 6.5 %collective-permute-start.5 = (bf16[2,64,256]{2,1,0:T(8,128)(2,1)S(1)}, bf16[2,64,256]{2,1,0:T(8,128)(2,1)S(1)}, u32[]{:S(2)}, u32[]{:S(2)}) collective-permute-start(bf16[2,64,256]{2,1,0:T(8,128)(2,1)S(1)} %pack_kv.1), channel_id=1, source_target_pairs={{0,6},{1,7},{2,4},{3,5},{4,2},{5,3},{6,0},{7,1},{8,14},{9,15},{10,... | collective-permute-start | bytes 196616 | tf_op jit(solution)/shard_map/ppermute | solution.py:26
  11.4 5.3 %collective-permute-start.4 = (bf16[2,64,256]{2,1,0:T(8,128)(2,1)S(1)}, bf16[2,64,256]{2,1,0:T(8,128)(2,1)S(1)}, u32[]{:S(2)}, u32[]{:S(2)}) collective-permute-start(bf16[2,64,256]{2,1,0:T(8,128)(2,1)S(1)} %pack_kv.1), channel_id=1, source_target_pairs={{0,4},{1,5},{2,6},{3,7},{4,0},{5,1},{6,2},{7,3},{8,12},{9,13},{10,... | collective-permute-start | bytes 196616 | tf_op jit(solution)/shard_map/ppermute | solution.py:26
  11.5 5.3 %collective-permute-start.3 = (bf16[2,64,256]{2,1,0:T(8,128)(2,1)S(1)}, bf16[2,64,256]{2,1,0:T(8,128)(2,1)S(1)}, u32[]{:S(2)}, u32[]{:S(2)}) collective-permute-start(bf16[2,64,256]{2,1,0:T(8,128)(2,1)S(1)} %pack_kv.1), channel_id=1, source_target_pairs={{0,2},{1,3},{2,0},{3,1},{4,6},{5,7},{6,4},{7,5},{8,10},{9,11},{10,... | collective-permute-start | bytes 196616 | tf_op jit(solution)/shard_map/ppermute | solution.py:26
  12.2 7.0 %collective-permute-start = (bf16[2,64,1024]{2,1,0:T(8,128)(2,1)S(1)}, bf16[2,64,1024]{2,1,0:T(8,128)(2,1)S(1)}, u32[]{:S(2)}, u32[]{:S(2)}) collective-permute-start(bf16[2,64,1024]{2,1,0:T(8,128)(2,1)S(1)} %get-tuple-element.51), channel_id=1, source_target_pairs={{0,8},{8,0},{16,24},{24,16},{1,9},{9,1},{17,25},{25,17},{2,10},{10... | collective-permute-start | bytes 786440 | tf_op jit(solution)/shard_map/ppermute | solution.py:26
  16.8 2.4 %collective-permute-start.6 = (bf16[4,2,64,256]{3,2,1,0:T(8,128)(2,1)S(1)}, bf16[4,2,64,256]{3,2,1,0:T(8,128)(2,1)S(1)}, u32[]{:S(2)}, u32[]{:S(2)}) collective-permute-start(bf16[4,2,64,256]{3,2,1,0:T(8,128)(2,1)S(1)} %pad_maximum_fusion.refs_2_.refs_0_), channel_id=1, source_target_pairs={{0,1},{1,0},{2,3},{3,2},{4,5},{5,4},{6,7},{7,6},{8,9},{9,8},{10,11... | collective-permute-start | bytes 786440 | tf_op jit(solution)/shard_map/ppermute | solution.py:26
  16.9 8.7 %collective-permute-start.7 = (bf16[4,2,64,256]{3,2,1,0:T(8,128)(2,1)S(1)}, bf16[4,2,64,256]{3,2,1,0:T(8,128)(2,1)S(1)}, u32[]{:S(2)}, u32[]{:S(2)}) collective-permute-start(bf16[4,2,64,256]{3,2,1,0:T(8,128)(2,1)S(1)} %pad_maximum_fusion.refs_2_.refs_0_), channel_id=1, source_target_pairs={{0,16},{8,24},{16,0},{24,8},{1,17},{9,25},{17,1},{25,9},{2,18},{10... | collective-permute-start | bytes 786440 | tf_op jit(solution)/shard_map/ppermute | solution.py:26
  25.6 2.5 %collective-permute-start.8 = (bf16[4,2,64,256]{3,2,1,0:T(8,128)(2,1)S(1)}, bf16[4,2,64,256]{3,2,1,0:T(8,128)(2,1)S(1)}, u32[]{:S(2)}, u32[]{:S(2)}) collective-permute-start(bf16[4,2,64,256]{3,2,1,0:T(8,128)(2,1)S(1)} %collective-permute-done.7.refs_0_), channel_id=1, source_target_pairs={{0,1},{1,0},{2,3},{3,2},{4,5},{5,4},{6,7},{7,6},{8,9},{9,8},{10,11... | collective-permute-start | bytes 786440 | tf_op jit(solution)/shard_map/ppermute | solution.py:26
  32.6 2.5 %collective-permute-start.11 = (bf16[2,2,64,256]{3,2,1,0:T(8,128)(2,1)S(1)}, bf16[2,2,64,256]{3,2,1,0:T(8,128)(2,1)S(1)}, u32[]{:S(2)}, u32[]{:S(2)}) collective-permute-start(bf16[2,2,64,256]{3,2,1,0:T(8,128)(2,1)S(1)} %get-tuple-element.76), channel_id=1, source_target_pairs={{0,1},{1,0},{2,3},{3,2},{4,5},{5,4},{6,7},{7,6},{8,9},{9,8},{10,11... | collective-permute-start | bytes 393224 | tf_op jit(solution)/shard_map/ppermute | solution.py:26
  33.2 2.0 %collective-permute-start.10 = (bf16[2,2,64,256]{3,2,1,0:T(8,128)(2,1)S(1)}, bf16[2,2,64,256]{3,2,1,0:T(8,128)(2,1)S(1)}, u32[]{:S(2)}, u32[]{:S(2)}) collective-permute-start(bf16[2,2,64,256]{3,2,1,0:T(8,128)(2,1)S(1)} %get-tuple-element.74), channel_id=1, source_target_pairs={{0,1},{1,0},{2,3},{3,2},{4,5},{5,4},{6,7},{7,6},{8,9},{9,8},{10,11... | collective-permute-start | bytes 393224 | tf_op jit(solution)/shard_map/ppermute | solution.py:26
  35.3 2.0 %collective-permute-start.12 = (bf16[64,128]{1,0:T(8,128)(2,1)S(1)}, bf16[64,128]{1,0:T(8,128)(2,1)S(1)}, u32[]{:S(2)}, u32[]{:S(2)}) collective-permute-start(bf16[64,128]{1,0:T(8,128)(2,1)S(1)} %slice_bitcast_fusion), channel_id=1, source_target_pairs={{0,1},{1,0},{2,3},{3,2},{4,5},{5,4},{6,7},{7,6},{8,9},{9,8},{10,11... | collective-permute-start | bytes 49160 | tf_op jit(solution)/shard_map/ppermute | solution.py:26
  35.8 7.7 %collective-permute-start.14 = (bf16[2,2,64,256]{3,2,1,0:T(8,128)(2,1)S(1)}, bf16[2,2,64,256]{3,2,1,0:T(8,128)(2,1)S(1)}, u32[]{:S(2)}, u32[]{:S(2)}) collective-permute-start(bf16[2,2,64,256]{3,2,1,0:T(8,128)(2,1)S(1)} %sum_cores.3), channel_id=1, source_target_pairs={{0,16},{8,24},{16,0},{24,8},{1,17},{9,25},{17,1},{25,9},{2,18},{10... | collective-permute-start | bytes 393224 | tf_op jit(solution)/shard_map/ppermute | solution.py:26
  39.2 5.2 %collective-permute-start.15 = (bf16[2,2,64,256]{3,2,1,0:T(8,128)(2,1)S(1)}, bf16[2,2,64,256]{3,2,1,0:T(8,128)(2,1)S(1)}, u32[]{:S(2)}, u32[]{:S(2)}) collective-permute-start(bf16[2,2,64,256]{3,2,1,0:T(8,128)(2,1)S(1)} %get-tuple-element.84), channel_id=1, source_target_pairs={{0,1},{1,0},{2,3},{3,2},{4,5},{5,4},{6,7},{7,6},{8,9},{9,8},{10,11... | collective-permute-start | bytes 393224 | tf_op jit(solution)/shard_map/ppermute | solution.py:26
  39.2 7.1 %collective-permute-start.18 = (bf16[2,2,64,256]{3,2,1,0:T(8,128)(2,1)S(1)}, bf16[2,2,64,256]{3,2,1,0:T(8,128)(2,1)S(1)}, u32[]{:S(2)}, u32[]{:S(2)}) collective-permute-start(bf16[2,2,64,256]{3,2,1,0:T(8,128)(2,1)S(1)} %sum_cores.2), channel_id=1, source_target_pairs={{0,16},{8,24},{16,0},{24,8},{1,17},{9,25},{17,1},{25,9},{2,18},{10... | collective-permute-start | bytes 393224 | tf_op jit(solution)/shard_map/ppermute | solution.py:26
  40.4 7.1 %collective-permute-start.19 = (bf16[2,2,64,256]{3,2,1,0:T(8,128)(2,1)S(1)}, bf16[2,2,64,256]{3,2,1,0:T(8,128)(2,1)S(1)}, u32[]{:S(2)}, u32[]{:S(2)}) collective-permute-start(bf16[2,2,64,256]{3,2,1,0:T(8,128)(2,1)S(1)} %get-tuple-element.88), channel_id=1, source_target_pairs={{0,1},{1,0},{2,3},{3,2},{4,5},{5,4},{6,7},{7,6},{8,9},{9,8},{10,11... | collective-permute-start | bytes 393224 | tf_op jit(solution)/shard_map/ppermute | solution.py:26
  40.4 14.3 %collective-permute-start.9 = (bf16[64,1024]{1,0:T(8,128)(2,1)S(1)}, bf16[64,1024]{1,0:T(8,128)(2,1)S(1)}, u32[]{:S(2)}, u32[]{:S(2)}) collective-permute-start(bf16[64,1024]{1,0:T(8,128)(2,1)S(1)} %get-tuple-element.65), channel_id=1, source_target_pairs={{0,8},{8,0},{16,24},{24,16},{1,9},{9,1},{17,25},{25,17},{2,10},{10... | collective-permute-start | bytes 393224 | tf_op jit(solution)/shard_map/ppermute | solution.py:26
  43.5 11.3 %collective-permute-start.13 = (bf16[64,1024]{1,0:T(8,128)(2,1)S(1)}, bf16[64,1024]{1,0:T(8,128)(2,1)S(1)}, u32[]{:S(2)}, u32[]{:S(2)}) collective-permute-start(bf16[64,1024]{1,0:T(8,128)(2,1)S(1)} %get-tuple-element.81), channel_id=1, source_target_pairs={{0,8},{8,0},{16,24},{24,16},{1,9},{9,1},{17,25},{25,17},{2,10},{10... | collective-permute-start | bytes 393224 | tf_op jit(solution)/shard_map/ppermute | solution.py:26
  44.4 7.3 %collective-permute-start.16 = (bf16[2,64,256]{2,1,0:T(8,128)(2,1)S(1)}, bf16[2,64,256]{2,1,0:T(8,128)(2,1)S(1)}, u32[]{:S(2)}, u32[]{:S(2)}) collective-permute-start(bf16[2,64,256]{2,1,0:T(8,128)(2,1)S(1)} %get-tuple-element.86), channel_id=1, source_target_pairs={{0,4},{1,5},{2,6},{3,7},{4,0},{5,1},{6,2},{7,3},{8,12},{9,13},{10,... | collective-permute-start | bytes 196616 | tf_op jit(solution)/shard_map/ppermute | solution.py:26
  46.3 6.3 %collective-permute-start.17 = (bf16[2,64,256]{2,1,0:T(8,128)(2,1)S(1)}, bf16[2,64,256]{2,1,0:T(8,128)(2,1)S(1)}, u32[]{:S(2)}, u32[]{:S(2)}) collective-permute-start(bf16[2,64,256]{2,1,0:T(8,128)(2,1)S(1)} %get-tuple-element.87), channel_id=1, source_target_pairs={{0,6},{1,7},{2,4},{3,5},{4,2},{5,3},{6,0},{7,1},{8,14},{9,15},{10,... | collective-permute-start | bytes 196616 | tf_op jit(solution)/shard_map/ppermute | solution.py:26
  47.5 5.9 %collective-permute-start.20 = (bf16[2,64,256]{2,1,0:T(8,128)(2,1)S(1)}, bf16[2,64,256]{2,1,0:T(8,128)(2,1)S(1)}, u32[]{:S(2)}, u32[]{:S(2)}) collective-permute-start(bf16[2,64,256]{2,1,0:T(8,128)(2,1)S(1)} %get-tuple-element.91), channel_id=1, source_target_pairs={{0,2},{1,3},{2,0},{3,1},{4,6},{5,7},{6,4},{7,5},{8,10},{9,11},{10,... | collective-permute-start | bytes 196616 | tf_op jit(solution)/shard_map/ppermute | solution.py:26
  53.4 4.0 %collective-permute-start.21 = (bf16[64,256]{1,0:T(8,128)(2,1)S(1)}, bf16[64,256]{1,0:T(8,128)(2,1)S(1)}, u32[]{:S(2)}, u32[]{:S(2)}) collective-permute-start(bf16[64,256]{1,0:T(8,128)(2,1)S(1)} %get-tuple-element.93), channel_id=1, source_target_pairs={{0,8},{8,0},{16,24},{24,16},{1,9},{9,1},{17,25},{25,17},{2,10},{10... | collective-permute-start | bytes 98312 | tf_op jit(solution)/shard_map/ppermute | solution.py:26

commit v7 on v6

--- a/solution.py
+++ b/solution.py
@@ -177,12 +177,16 @@
 
 
 def forward_part(plan, chunks, info_ref, q_t, kv_refs, e_ref, top_ref, sum_ref, mix_ref, turned_ref):
+    spans = [plan.at(tile) for tile in range(len(plan.tiles))]
+    tops = [
+        plan.scores(tile, chunks, kv_refs, q_t[:, at], e_ref, at, info_ref)
+        for tile, at in enumerate(spans)
+    ]
     plan.turn(kv_refs, turned_ref)
-    for tile in range(len(plan.tiles)):
-        at = plan.at(tile)
-        top = plan.scores(tile, chunks, kv_refs, q_t[:, at], e_ref, at, info_ref)
+    for at, top in zip(spans, tops):
         top_ref[:, at] = top
         sum_ref[:, at] = plan.exponents(len(chunks), e_ref, at, top)
+    for at in spans:
         mixed = jnp.zeros((HD, plan.lanes), F32)
         for i in range(len(chunks)):
             weights = e_ref[plan.keys_at(i), at].astype(BF)
@@ -217,40 +221,50 @@
     kv_refs, refs = refs[:count], refs[count:]
     att_refs, refs = refs[:kv], refs[kv:]
     scale_refs, (delta_ref, q_grad_ref), refs = refs[:others], refs[others : others + 2], refs[others + 2 :]
-    dkv_refs, (turned_ref, e_ref, p_ref, ds_ref) = refs[:-4], refs[-4:]
-    here = pl.ds(0, plan.lanes)
+    dkv_refs, (turned_ref, e_ref, w_ref, p_ref, ds_ref) = refs[:-5], refs[-5:]
+    spans = [plan.at(tile) for tile in range(len(plan.tiles))]
+    tops = [
+        plan.scores(tile, chunks, kv_refs, q_t[:, at], e_ref, at, info_ref)
+        for tile, at in enumerate(spans)
+    ]
     plan.turn(kv_refs, turned_ref)
-    for tile, (s, _) in enumerate(plan.tiles):
-        at = plan.at(tile)
-        top = plan.scores(tile, chunks, kv_refs, q_t[:, at], e_ref, here, info_ref)
+    for at in spans:
+        for i, ref in enumerate(kv_refs):
+            w_ref[plan.keys_at(i), at] = dot(plan.values(ref), do_t[:, at])
+    inverses, mixes = [], []
+    for at, top in zip(spans, tops):
         for top_ref, _, _ in partial:
             top = jnp.maximum(top, top_ref[:, at])
-        total = plan.exponents(count, e_ref, here, top)
+        total = plan.exponents(count, e_ref, at, top)
         factors = [jnp.exp2((top_ref[:, at] - top) * EXPO) for top_ref, _, _ in partial]
         for factor, (_, sum_ref, _) in zip(factors, partial):
             total = total + factor * sum_ref[:, at]
         inverse = 1.0 / total
+        for factor, scale_ref in zip(factors, scale_refs):
+            scale_ref[:, at] = factor * inverse
+        inverses.append(inverse)
+    for at, inverse in zip(spans, inverses):
         mixed = jnp.zeros((HD, plan.lanes), F32)
-        for factor, scale_ref, (_, _, mix_ref) in zip(factors, scale_refs, partial):
-            scale_ref[:, at] = factor * inverse
-            mixed = mixed + mix_ref[:, at] * (factor * inverse)
+        for scale_ref, (_, _, mix_ref) in zip(scale_refs, partial):
+            mixed = mixed + mix_ref[:, at] * scale_ref[:, at]
         for i in range(count):
-            probs = (e_ref[plan.keys_at(i), here] * inverse).astype(BF)
+            probs = (e_ref[plan.keys_at(i), at] * inverse).astype(BF)
             p_ref[plan.keys_at(i), at] = probs
             mixed = mixed + dot(turned_ref[pl.ds(HD, HD), plan.keys_at(i)], probs)
-        mixed = mixed.astype(BF).astype(F32)
-        plan.store_heads(att_refs[s], tile, mixed)
-        do = do_t[:, at]
-        delta = jnp.sum(do.astype(F32) * mixed, axis=0, keepdims=True)
-        delta_ref[:, at] = delta
+        mixes.append(mixed.astype(BF).astype(F32))
+    for at, mixed in zip(spans, mixes):
+        delta_ref[:, at] = jnp.sum(do_t[:, at].astype(F32) * mixed, axis=0, keepdims=True)
+    for at, inverse in zip(spans, inverses):
         q_grad = jnp.zeros((HD, plan.lanes), F32)
-        for i, ref in enumerate(kv_refs):
-            probs = e_ref[plan.keys_at(i), here] * inverse
-            grad_s = (probs * (dot(plan.values(ref), do) - delta)).astype(BF)
+        for i in range(count):
+            probs = e_ref[plan.keys_at(i), at] * inverse
+            grad_s = (probs * (w_ref[plan.keys_at(i), at] - delta_ref[:, at])).astype(BF)
             ds_ref[plan.keys_at(i), at] = grad_s
             q_grad = q_grad + dot(turned_ref[pl.ds(0, HD), plan.keys_at(i)], grad_s)
         q_grad_ref[:, at] = q_grad
     plan.back(kv_refs, dkv_refs, p_ref, ds_ref, q_all, do_all)
+    for tile, mixed in enumerate(mixes):
+        plan.store_heads(att_refs[plan.tiles[tile][0]], tile, mixed)
 
 
 def back_kernel(plan, rows_at, last, order, q_all, do_all, do_t, e_ref, scale_ref, delta_ref, q_grad_in, *refs):
@@ -258,21 +272,23 @@
     kv_refs, refs = refs[:count], refs[count + order :]
     refs, (turned_ref, p_ref, ds_ref) = refs[:-3], refs[-3:]
     outs, dkv_refs = refs[: -plan.parts * count], refs[-plan.parts * count :]
-    plan.turn(kv_refs, turned_ref)
-    for tile, (s, _) in enumerate(plan.tiles):
-        at = plan.at(tile)
-        q_grad = q_grad_in[:, at]
+    spans = [plan.at(tile) for tile in range(len(plan.tiles))]
+    for at in spans:
         for i, ref in enumerate(kv_refs):
             probs = e_ref[plan.keys_at(rows_at[i]), at] * scale_ref[:, at]
             p_ref[plan.keys_at(i), at] = probs.astype(BF)
             grad_s = (probs * (dot(plan.values(ref), do_t[:, at]) - delta_ref[:, at])).astype(BF)
             ds_ref[plan.keys_at(i), at] = grad_s
-            q_grad = q_grad + dot(turned_ref[pl.ds(0, HD), plan.keys_at(i)], grad_s)
+    plan.turn(kv_refs, turned_ref)
+    plan.back(kv_refs, dkv_refs, p_ref, ds_ref, q_all, do_all)
+    for tile, at in enumerate(spans):
+        q_grad = q_grad_in[:, at]
+        for i in range(count):
+            q_grad = q_grad + dot(turned_ref[pl.ds(0, HD), plan.keys_at(i)], ds_ref[plan.keys_at(i), at])
         if last:
-            plan.store_heads(outs[s], tile, q_grad * SCALING)
+            plan.store_heads(outs[plan.tiles[tile][0]], tile, q_grad * SCALING)
         else:
             outs[0][:, at] = q_grad
-    plan.back(kv_refs, dkv_refs, p_ref, ds_ref, q_all, do_all)
 
 
 def add_kernel(*refs):
@@ -425,11 +441,12 @@
         [SMEM] + [VMEM] * (10 + len(far_kv)),
         [
             pltpu.VMEM((2 * HD, far_keys), BF),
-            pltpu.VMEM((far_keys, plan.lanes), F32),
+            pltpu.VMEM((far_keys, query_rows), F32),
+            pltpu.VMEM((far_keys, query_rows), F32),
             pltpu.VMEM((far_keys, query_rows), BF),
             pltpu.VMEM((far_keys, query_rows), BF),
         ],
-        far_keys * (4 * HD + 4 * plan.lanes + 4 * query_rows),
+        far_keys * (4 * HD + 12 * query_rows),
         16 * far_keys * query_rows * HD,
     )
     att_parts, outs = outs[:kv], outs[kv:]

time: 58.4 us -> 54.2 us (0.928)
  Pallas kernels: 17.6 us -> 12.7 us
  waiting for transfers between devices: 14.1 us -> 14.7 us
    pallas_call x15, Pallas kernels: 17.6 us -> 12.7 us  [call(): pl.pallas_call(kernel, out_shape=list(outs), in_specs=specs or [VMEM] * l...]
  transfers between devices with their start and end apart: 22 -> 22, of which waited for: 8 -> 9; matrix products, arithmetic and copies ran while one was open for 4% -> 4% of each run, Pallas kernels for 21% -> 17%
where the time goes in v7:
time: 54.2 us; the launch traced here: 53.9 us
  starting transfers between devices  21.6 us (40%)
  waiting for transfers between devices  14.7 us (27%)
  Pallas kernels  12.7 us (23%)
  local copies, waits for them, and re-layouts  3.34 us (6%)
  between operations  0.79 us (1%)
  other arithmetic  0.77 us (1%)
    ppermute x22, starting transfers between devices, swap(): return lax.ppermute(block, axis, [(i, i ^ mask) for i in range(size)])  21.6 us
    ppermute x22, waiting for transfers between devices, swap(): return lax.ppermute(block, axis, [(i, i ^ mask) for i in range(size)])  14.7 us
    pallas_call x15, Pallas kernels, call(): pl.pallas_call(kernel, out_shape=list(outs), in_specs=specs or [VMEM] * l...  12.7 us
    unnamed x4, local copies, waits for them, and re-layouts  1.9 us
    dynamic_slice x2, local copies, waits for them, and re-layouts, shards(): lax.dynamic_slice_in_dim(block, mine, HD, 1)  1.44 us
  transfers between devices with their start and end apart: 22, of which 9 were waited for; matrix products, arithmetic and copies ran while one was open for 4% of the time, Pallas kernels for 17%

profile of v7, /device:TPU:0, one launch (start us, length us, event | category | flops | bytes accessed | tf_op | source)
XLA Modules:
  0.0 53.9 jit_solution(10352244985735673288)
XLA Ops:
  0.6 3.0 %collective-permute-start.1 = (bf16[64,256]{1,0:T(8,128)(2,1)}, bf16[64,256]{1,0:T(8,128)(2,1)S(1)}, u32[]{:S(2)}, u32[]{:S(2)}) collective-permute-start(bf16[64,256]{1,0:T(8,128)(2,1)} %bitcast.23), channel_id=1, source_target_pairs={{0,8},{8,0},{16,24},{24,16},{1,9},{9,1},{17,25},{25,17},{2,10},{10... | collective-permute-start | bytes 98312 | tf_op jit(solution)/shard_map/ppermute | solution.py:26
  3.6 0.1 collective-permute-start.2
  3.7 0.7 %constant_dynamic-slice_fusion.1 = bf16[64,128]{1,0:T(8,128)(2,1)S(1)} fusion(bf16[64,256]{1,0:T(8,128)(2,1)} %bitcast.24, s32[]{:T(128)S(6)} %select_n.14), kind=kLoop, calls=%fused_computation.5 | loop fusion | bytes 32772 | tf_op jit(solution)/shard_map/dynamic_slice | solution.py:378
  4.4 0.7 %constant_dynamic-slice_fusion = bf16[64,128]{1,0:T(8,128)(2,1)S(1)} fusion(bf16[64,256]{1,0:T(8,128)(2,1)} %bitcast.26, s32[]{:T(128)S(6)} %select_n.14), kind=kLoop, calls=%fused_computation.4 | loop fusion | bytes 32772 | tf_op jit(solution)/shard_map/dynamic_slice | solution.py:378
  5.2 0.9 %copy-done = bf16[2,32,2048]{2,1,0:T(8,128)(2,1)S(1)} copy-done((bf16[2,32,2048]{2,1,0:T(8,128)(2,1)S(1)}, bf16[2,32,2048]{2,1,0:T(8,128)(2,1)}, u32[]{:S(2)}) %copy-start) | copy-done | bytes 262168
  6.1 0.9 %copy-done.1 = bf16[2,32,2048]{2,1,0:T(8,128)(2,1)S(1)} copy-done((bf16[2,32,2048]{2,1,0:T(8,128)(2,1)S(1)}, bf16[2,32,2048]{2,1,0:T(8,128)(2,1)}, u32[]{:S(2)}) %copy-start.1) | copy-done | bytes 262168
  7.1 0.0 collective-permute-done.1.refs_1_
  7.1 0.6 %collective-permute-done.2.refs_2_ = bf16[64,256]{1,0:T(8,128)(2,1)S(1)} collective-permute-done((bf16[64,256]{1,0:T(8,128)(2,1)}, bf16[64,256]{1,0:T(8,128)(2,1)S(1)}, u32[]{:S(2)}, u32[]{:S(2)}) %collective-permute-start.2) | collective-permute-done | bytes 32800 | tf_op jit(solution)/shard_map/ppermute | solution.py:26
  7.8 3.7 %collective-permute-start.5 = (bf16[2,64,256]{2,1,0:T(8,128)(2,1)S(1)}, bf16[2,64,256]{2,1,0:T(8,128)(2,1)S(1)}, u32[]{:S(2)}, u32[]{:S(2)}) collective-permute-start(bf16[2,64,256]{2,1,0:T(8,128)(2,1)S(1)} %pack_kv.1), channel_id=1, source_target_pairs={{0,6},{1,7},{2,4},{3,5},{4,2},{5,3},{6,0},{7,1},{8,14},{9,15},{10,... | collective-permute-start | bytes 196616 | tf_op jit(solution)/shard_map/ppermute | solution.py:26
  11.4 0.0 collective-permute-start.4
  11.5 0.8 %collective-permute-start.3 = (bf16[2,64,256]{2,1,0:T(8,128)(2,1)S(1)}, bf16[2,64,256]{2,1,0:T(8,128)(2,1)S(1)}, u32[]{:S(2)}, u32[]{:S(2)}) collective-permute-start(bf16[2,64,256]{2,1,0:T(8,128)(2,1)S(1)} %pack_kv.1), channel_id=1, source_target_pairs={{0,2},{1,3},{2,0},{3,1},{4,6},{5,7},{6,4},{7,5},{8,10},{9,11},{10,... | collective-permute-start | bytes 196616 | tf_op jit(solution)/shard_map/ppermute | solution.py:26
  12.2 1.3 %collective-permute-start = (bf16[2,64,1024]{2,1,0:T(8,128)(2,1)S(1)}, bf16[2,64,1024]{2,1,0:T(8,128)(2,1)S(1)}, u32[]{:S(2)}, u32[]{:S(2)}) collective-permute-start(bf16[2,64,1024]{2,1,0:T(8,128)(2,1)S(1)} %get-tuple-element.51), channel_id=1, source_target_pairs={{0,8},{8,0},{16,24},{24,16},{1,9},{9,1},{17,25},{25,17},{2,10},{10... | collective-permute-start | bytes 786440 | tf_op jit(solution)/shard_map/ppermute | solution.py:26
  13.5 0.7 %collective-permute-done.5 = bf16[2,64,256]{2,1,0:T(8,128)(2,1)S(1)} collective-permute-done((bf16[2,64,256]{2,1,0:T(8,128)(2,1)S(1)}, bf16[2,64,256]{2,1,0:T(8,128)(2,1)S(1)}, u32[]{:S(2)}, u32[]{:S(2)}) %collective-permute-start.5) | collective-permute-done | bytes 65568 | tf_op jit(solution)/shard_map/ppermute | solution.py:26
  14.3 2.5 %collective-permute-done.4 = bf16[2,64,256]{2,1,0:T(8,128)(2,1)S(1)} collective-permute-done((bf16[2,64,256]{2,1,0:T(8,128)(2,1)S(1)}, bf16[2,64,256]{2,1,0:T(8,128)(2,1)S(1)}, u32[]{:S(2)}, u32[]{:S(2)}) %collective-permute-start.4) | collective-permute-done | bytes 65568 | tf_op jit(solution)/shard_map/ppermute | solution.py:26
  16.8 0.0 collective-permute-done.3
  16.8 0.1 collective-permute-start.6
  16.9 1.6 %collective-permute-start.7 = (bf16[4,2,64,256]{3,2,1,0:T(8,128)(2,1)S(1)}, bf16[4,2,64,256]{3,2,1,0:T(8,128)(2,1)S(1)}, u32[]{:S(2)}, u32[]{:S(2)}) collective-permute-start(bf16[4,2,64,256]{3,2,1,0:T(8,128)(2,1)S(1)} %pad_maximum_fusion.refs_2_.refs_0_), channel_id=1, source_target_pairs={{0,16},{8,24},{16,0},{24,8},{1,17},{9,25},{17,1},{25,9},{2,18},{10... | collective-permute-start | bytes 786440 | tf_op jit(solution)/shard_map/ppermute | solution.py:26
  18.5 0.7 %pad_add_fusion.info_ref = s32[18]{0:T(128)S(1)} fusion(s32[16]{0:T(128)} %param.9, s32[1]{0:T(128)} %bitcast.2, s32[1]{0:T(128)} %bitcast.1), kind=kLoop, calls=%fused_computation.3 | loop fusion | flops 36 | bytes 144 | tf_op jit(solution)/shard_map/concatenate | solution.py:358
  19.2 0.0 collective-permute-done.refs_1_
  19.2 0.0 collective-permute-done.6.refs_3_.refs_0_
  19.2 2.7 %attend_near.1 = (bf16[1024,128]{1,0:T(8,128)(2,1)S(1)}, bf16[1024,128]{1,0:T(8,128)(2,1)S(1)}, bf16[128,1024]{1,0:T(8,128)(2,1)S(1)}, bf16[128,1024]{1,0:T(8,12...) custom-call(s32[18]{0:T(128)S(1)} %pad_add_fusion.info_ref, ...), custom_call_target="tpu_custom_call" | custom-call | flops 1073741824 | bytes 6824008 | tf_op jit(solution)/shard_map/attend_near/pallas_call | solution.py:41
  21.9 3.7 %collective-permute-done.7.refs_0_ = bf16[4,2,64,256]{3,2,1,0:T(8,128)(2,1)S(1)} collective-permute-done((bf16[4,2,64,256]{3,2,1,0:T(8,128)(2,1)S(1)}, bf16[4,2,64,256]{3,2,1,0:T(8,128)(2,1)S(1)}, u32[]{:S(2)}, u32[]{:S(2)}) %collective-permute-start.7) | collective-permute-done | bytes 262176 | tf_op jit(solution)/shard_map/ppermute | solution.py:26
  25.6 1.7 %attend_mid.1 = (f32[512,1024]{1,0:T(8,128)S(1)}, f32[1,1024]{1,0:T(1,128)S(1)}, f32[1,1024]{1,0:T(1,128)S(1)}, f32[128,1024]{1,0:T(8,128)S(1)}) custom-call(s32[18]{0:T(128)S(1)} %pad_add_fusion.info_ref, bf16[128,1024]{1,0:T(8,128)(2,1)S(1)} %get-tuple-element.55.q_t, bf16[4,2,64,256]{3,2,1,0:T(8,128)(2,1)S(1)} %collective-permute-done.7.refs_0_), custom_call_target="tpu_custom_call" | custom-call | flops 536870912 | bytes 3153992 | tf_op jit(solution)/shard_map/attend_mid/pallas_call | solution.py:41
  27.4 3.1 %attend_far.1 = (bf16[64,1024]{1,0:T(8,128)(2,1)S(1)}, bf16[64,1024]{1,0:T(8,128)(2,1)S(1)}, f32[1,1024]{1,0:T(1,128)S(1)}, f32[1,1024]{1,0:T(1,128)S(1)}, f32[1...) custom-call(s32[18]{0:T(128)S(1)} %pad_add_fusion.info_ref, ...), custom_call_target="tpu_custom_call" | custom-call | flops 1073741824 | bytes 3436616 | tf_op jit(solution)/shard_map/attend_far/pallas_call | solution.py:41
  30.4 0.6 %collective-permute-start.11 = (bf16[2,2,64,256]{3,2,1,0:T(8,128)(2,1)S(1)}, bf16[2,2,64,256]{3,2,1,0:T(8,128)(2,1)S(1)}, u32[]{:S(2)}, u32[]{:S(2)}) collective-permute-start(bf16[2,2,64,256]{3,2,1,0:T(8,128)(2,1)S(1)} %get-tuple-element.76), channel_id=1, source_target_pairs={{0,1},{1,0},{2,3},{3,2},{4,5},{5,4},{6,7},{7,6},{8,9},{9,8},{10,11... | collective-permute-start | bytes 393224 | tf_op jit(solution)/shard_map/ppermute | solution.py:26
  31.0 0.1 collective-permute-start.10
  31.1 1.1 %attend_back.3 = (f32[128,1024]{1,0:T(8,128)S(1)}, bf16[2,2,64,256]{3,2,1,0:T(8,128)(2,1)S(1)}, bf16[2,2,64,256]{3,2,1,0:T(8,128)(2,1)S(1)}) custom-call(bf16[1024,128]{1,0:T(8,128)(2,1)S(1)} %get-tuple-element.53.q_all, bf16[1024,128]{1,0:T(8,128)(2,1)S(1)} %get-tuple-element.54.do_all, bf16[128,1024]{1,0:T(8,128)(2,1)S(1)} %get-tuple-element.56.do_t, ...), custom_call_target="tpu_custom_call" | custom-call | flops 805306368 | bytes 4464640 | tf_op jit(solution)/shard_map/attend_back/pallas_call | solution.py:41
  32.3 0.1 collective-permute-done.10.refs_1_
  32.4 0.4 collective-permute-start.12
  32.8 1.5 %collective-permute-start.14 = (bf16[2,2,64,256]{3,2,1,0:T(8,128)(2,1)S(1)}, bf16[2,2,64,256]{3,2,1,0:T(8,128)(2,1)S(1)}, u32[]{:S(2)}, u32[]{:S(2)}) collective-permute-start(bf16[2,2,64,256]{3,2,1,0:T(8,128)(2,1)S(1)} %sum_cores.3), channel_id=1, source_target_pairs={{0,16},{8,24},{16,0},{24,8},{1,17},{9,25},{17,1},{25,9},{2,18},{10... | collective-permute-start | bytes 393224 | tf_op jit(solution)/shard_map/ppermute | solution.py:26
  34.4 1.1 %attend_back.4 = (f32[128,1024]{1,0:T(8,128)S(1)}, bf16[2,2,64,256]{3,2,1,0:T(8,128)(2,1)S(1)}, bf16[2,2,64,256]{3,2,1,0:T(8,128)(2,1)S(1)}) custom-call(bf16[1024,128]{1,0:T(8,128)(2,1)S(1)} %get-tuple-element.53.q_all, bf16[1024,128]{1,0:T(8,128)(2,1)S(1)} %get-tuple-element.54.do_all, bf16[128,1024]{1,0:T(8,128)(2,1)S(1)} %get-tuple-element.56.do_t, ...), custom_call_target="tpu_custom_call" | custom-call | flops 805306368 | bytes 6578176 | tf_op jit(solution)/shard_map/attend_back/pallas_call | solution.py:41
  35.5 0.1 collective-permute-start.15
  35.6 1.2 %collective-permute-start.18 = (bf16[2,2,64,256]{3,2,1,0:T(8,128)(2,1)S(1)}, bf16[2,2,64,256]{3,2,1,0:T(8,128)(2,1)S(1)}, u32[]{:S(2)}, u32[]{:S(2)}) collective-permute-start(bf16[2,2,64,256]{3,2,1,0:T(8,128)(2,1)S(1)} %sum_cores.2), channel_id=1, source_target_pairs={{0,16},{8,24},{16,0},{24,8},{1,17},{9,25},{17,1},{25,9},{2,18},{10... | collective-permute-start | bytes 393224 | tf_op jit(solution)/shard_map/ppermute | solution.py:26
  36.8 1.2 %collective-permute-start.9 = (bf16[64,1024]{1,0:T(8,128)(2,1)S(1)}, bf16[64,1024]{1,0:T(8,128)(2,1)S(1)}, u32[]{:S(2)}, u32[]{:S(2)}) collective-permute-start(bf16[64,1024]{1,0:T(8,128)(2,1)S(1)} %get-tuple-element.65), channel_id=1, source_target_pairs={{0,8},{8,0},{16,24},{24,16},{1,9},{9,1},{17,25},{25,17},{2,10},{10... | collective-permute-start | bytes 393224 | tf_op jit(solution)/shard_map/ppermute | solution.py:26
  38.0 1.2 %attend_back.5 = (bf16[64,1024]{1,0:T(8,128)(2,1)S(1)}, bf16[64,1024]{1,0:T(8,128)(2,1)S(1)}, bf16[2,2,64,256]{3,2,1,0:T(8,128)(2,1)S(1)}, bf16[2,2,64,256]{3,2,1,0:T(8,128)(2,1)S(1)}) custom-call(bf16[1024,128]{1,0:T(8,128)(2,1)S(1)} %get-tuple-element.53.q_all, bf16[1024,128]{1,0:T(8,128)(2,1)S(1)} %get-tuple-element.54.do_all, ...), custom_call_target="tpu_custom_call" | custom-call | flops 805306368 | bytes 6316032 | tf_op jit(solution)/shard_map/attend_back/pallas_call | solution.py:41
  39.2 0.8 %collective-permute-start.13 = (bf16[64,1024]{1,0:T(8,128)(2,1)S(1)}, bf16[64,1024]{1,0:T(8,128)(2,1)S(1)}, u32[]{:S(2)}, u32[]{:S(2)}) collective-permute-start(bf16[64,1024]{1,0:T(8,128)(2,1)S(1)} %get-tuple-element.81), channel_id=1, source_target_pairs={{0,8},{8,0},{16,24},{24,16},{1,9},{9,1},{17,25},{25,17},{2,10},{10... | collective-permute-start | bytes 393224 | tf_op jit(solution)/shard_map/ppermute | solution.py:26
  40.1 0.1 sum_heads.2
  40.1 1.9 %collective-permute-start.16 = (bf16[2,64,256]{2,1,0:T(8,128)(2,1)S(1)}, bf16[2,64,256]{2,1,0:T(8,128)(2,1)S(1)}, u32[]{:S(2)}, u32[]{:S(2)}) collective-permute-start(bf16[2,64,256]{2,1,0:T(8,128)(2,1)S(1)} %get-tuple-element.86), channel_id=1, source_target_pairs={{0,4},{1,5},{2,6},{3,7},{4,0},{5,1},{6,2},{7,3},{8,12},{9,13},{10,... | collective-permute-start | bytes 196616 | tf_op jit(solution)/shard_map/ppermute | solution.py:26
  42.1 1.8 %collective-permute-start.17 = (bf16[2,64,256]{2,1,0:T(8,128)(2,1)S(1)}, bf16[2,64,256]{2,1,0:T(8,128)(2,1)S(1)}, u32[]{:S(2)}, u32[]{:S(2)}) collective-permute-start(bf16[2,64,256]{2,1,0:T(8,128)(2,1)S(1)} %get-tuple-element.87), channel_id=1, source_target_pairs={{0,6},{1,7},{2,4},{3,5},{4,2},{5,3},{6,0},{7,1},{8,14},{9,15},{10,... | collective-permute-start | bytes 196616 | tf_op jit(solution)/shard_map/ppermute | solution.py:26
  43.8 0.1 sum_heads.3
  43.9 0.2 collective-permute-start.20
  44.0 3.4 %collective-permute-done.16.refs_0_ = bf16[2,64,256]{2,1,0:T(8,128)(2,1)S(1)} collective-permute-done((bf16[2,64,256]{2,1,0:T(8,128)(2,1)S(1)}, bf16[2,64,256]{2,1,0:T(8,128)(2,1)S(1)}, u32[]{:S(2)}, u32[]{:S(2)}) %collective-permute-start.16) | collective-permute-done | bytes 65568 | tf_op jit(solution)/shard_map/ppermute | solution.py:26
  47.5 0.9 %collective-permute-done.17.refs_1_ = bf16[2,64,256]{2,1,0:T(8,128)(2,1)S(1)} collective-permute-done((bf16[2,64,256]{2,1,0:T(8,128)(2,1)S(1)}, bf16[2,64,256]{2,1,0:T(8,128)(2,1)S(1)}, u32[]{:S(2)}, u32[]{:S(2)}) %collective-permute-start.17) | collective-permute-done | bytes 65568 | tf_op jit(solution)/shard_map/ppermute | solution.py:26
  48.4 0.9 %collective-permute-done.20.refs_3_ = bf16[2,64,256]{2,1,0:T(8,128)(2,1)S(1)} collective-permute-done((bf16[2,64,256]{2,1,0:T(8,128)(2,1)S(1)}, bf16[2,64,256]{2,1,0:T(8,128)(2,1)S(1)}, u32[]{:S(2)}, u32[]{:S(2)}) %collective-permute-start.20) | collective-permute-done | bytes 65568 | tf_op jit(solution)/shard_map/ppermute | solution.py:26
  49.3 1.3 %collective-permute-start.21 = (bf16[64,256]{1,0:T(8,128)(2,1)S(1)}, bf16[64,256]{1,0:T(8,128)(2,1)S(1)}, u32[]{:S(2)}, u32[]{:S(2)}) collective-permute-start(bf16[64,256]{1,0:T(8,128)(2,1)S(1)} %get-tuple-element.93), channel_id=1, source_target_pairs={{0,8},{8,0},{16,24},{24,16},{1,9},{9,1},{17,25},{25,17},{2,10},{10... | collective-permute-start | bytes 98312 | tf_op jit(solution)/shard_map/ppermute | solution.py:26
  50.6 0.8 %finish_q.1 = (bf16[64,2048]{1,0:T(8,128)(2,1)}, bf16[64,2048]{1,0:T(8,128)(2,1)}) custom-call(s32[1]{0:T(128)} %bitcast.group_ref, bf16[64,1024]{1,0:T(8,128)(2,1)S(1)} %get-tuple-element.64.refs_0_, bf16[64,1024]{1,0:T(8,128)(2,1)S(1)} %collective-permute-done.9.refs_1_, bf16[64,1024]{1,0:T(8,128)(2,1)S(1)} %get-tuple-element.80.refs_2_, ...), custom_call_target="tpu_custom_call" | custom-call | bytes 1048580 | tf_op jit(solution)/shard_map/finish_q/pallas_call | solution.py:41
  51.5 1.8 %collective-permute-done.21.refs_1_ = bf16[64,256]{1,0:T(8,128)(2,1)S(1)} collective-permute-done((bf16[64,256]{1,0:T(8,128)(2,1)S(1)}, bf16[64,256]{1,0:T(8,128)(2,1)S(1)}, u32[]{:S(2)}, u32[]{:S(2)}) %collective-permute-start.21) | collective-permute-done | bytes 32800 | tf_op jit(solution)/shard_map/ppermute | solution.py:26
  53.3 0.6 %finish_kv.1 = (bf16[64,256]{1,0:T(8,128)(2,1)}, bf16[64,256]{1,0:T(8,128)(2,1)}) custom-call(s32[1]{0:T(128)} %bitcast.group_ref, bf16[64,256]{1,0:T(8,128)(2,1)S(1)} %get-tuple-element.92.refs_0_, bf16[64,256]{1,0:T(8,128)(2,1)S(1)} %collective-permute-done.21.refs_1_), custom_call_target="tpu_custom_call" | custom-call | bytes 131076 | tf_op jit(solution)/shard_map/finish_kv/pallas_call | solution.py:41
  (21 shorter events, 0.2 us)
Async XLA Ops:
  0.6 6.5 %collective-permute-start.1 = (bf16[64,256]{1,0:T(8,128)(2,1)}, bf16[64,256]{1,0:T(8,128)(2,1)S(1)}, u32[]{:S(2)}, u32[]{:S(2)}) collective-permute-start(bf16[64,256]{1,0:T(8,128)(2,1)} %bitcast.23), channel_id=1, source_target_pairs={{0,8},{8,0},{16,24},{24,16},{1,9},{9,1},{17,25},{25,17},{2,10},{10... | collective-permute-start | bytes 98312 | tf_op jit(solution)/shard_map/ppermute | solution.py:26
  3.6 4.1 %collective-permute-start.2 = (bf16[64,256]{1,0:T(8,128)(2,1)}, bf16[64,256]{1,0:T(8,128)(2,1)S(1)}, u32[]{:S(2)}, u32[]{:S(2)}) collective-permute-start(bf16[64,256]{1,0:T(8,128)(2,1)} %bitcast.25), channel_id=1, source_target_pairs={{0,8},{8,0},{16,24},{24,16},{1,9},{9,1},{17,25},{25,17},{2,10},{10... | collective-permute-start | bytes 98312 | tf_op jit(solution)/shard_map/ppermute | solution.py:26
  5.2 0.9 %copy-start = (bf16[2,32,2048]{2,1,0:T(8,128)(2,1)S(1)}, bf16[2,32,2048]{2,1,0:T(8,128)(2,1)}, u32[]{:S(2)}) copy-start(bf16[2,32,2048]{2,1,0:T(8,128)(2,1)} %param.5) | copy-start | bytes 786436
  6.1 0.9 %copy-start.1 = (bf16[2,32,2048]{2,1,0:T(8,128)(2,1)S(1)}, bf16[2,32,2048]{2,1,0:T(8,128)(2,1)}, u32[]{:S(2)}) copy-start(bf16[2,32,2048]{2,1,0:T(8,128)(2,1)} %param.8) | copy-start | bytes 786436
  7.8 6.5 %collective-permute-start.5 = (bf16[2,64,256]{2,1,0:T(8,128)(2,1)S(1)}, bf16[2,64,256]{2,1,0:T(8,128)(2,1)S(1)}, u32[]{:S(2)}, u32[]{:S(2)}) collective-permute-start(bf16[2,64,256]{2,1,0:T(8,128)(2,1)S(1)} %pack_kv.1), channel_id=1, source_target_pairs={{0,6},{1,7},{2,4},{3,5},{4,2},{5,3},{6,0},{7,1},{8,14},{9,15},{10,... | collective-permute-start | bytes 196616 | tf_op jit(solution)/shard_map/ppermute | solution.py:26
  11.4 5.3 %collective-permute-start.4 = (bf16[2,64,256]{2,1,0:T(8,128)(2,1)S(1)}, bf16[2,64,256]{2,1,0:T(8,128)(2,1)S(1)}, u32[]{:S(2)}, u32[]{:S(2)}) collective-permute-start(bf16[2,64,256]{2,1,0:T(8,128)(2,1)S(1)} %pack_kv.1), channel_id=1, source_target_pairs={{0,4},{1,5},{2,6},{3,7},{4,0},{5,1},{6,2},{7,3},{8,12},{9,13},{10,... | collective-permute-start | bytes 196616 | tf_op jit(solution)/shard_map/ppermute | solution.py:26
  11.5 5.3 %collective-permute-start.3 = (bf16[2,64,256]{2,1,0:T(8,128)(2,1)S(1)}, bf16[2,64,256]{2,1,0:T(8,128)(2,1)S(1)}, u32[]{:S(2)}, u32[]{:S(2)}) collective-permute-start(bf16[2,64,256]{2,1,0:T(8,128)(2,1)S(1)} %pack_kv.1), channel_id=1, source_target_pairs={{0,2},{1,3},{2,0},{3,1},{4,6},{5,7},{6,4},{7,5},{8,10},{9,11},{10,... | collective-permute-start | bytes 196616 | tf_op jit(solution)/shard_map/ppermute | solution.py:26
  12.2 7.0 %collective-permute-start = (bf16[2,64,1024]{2,1,0:T(8,128)(2,1)S(1)}, bf16[2,64,1024]{2,1,0:T(8,128)(2,1)S(1)}, u32[]{:S(2)}, u32[]{:S(2)}) collective-permute-start(bf16[2,64,1024]{2,1,0:T(8,128)(2,1)S(1)} %get-tuple-element.51), channel_id=1, source_target_pairs={{0,8},{8,0},{16,24},{24,16},{1,9},{9,1},{17,25},{25,17},{2,10},{10... | collective-permute-start | bytes 786440 | tf_op jit(solution)/shard_map/ppermute | solution.py:26
  16.8 2.4 %collective-permute-start.6 = (bf16[4,2,64,256]{3,2,1,0:T(8,128)(2,1)S(1)}, bf16[4,2,64,256]{3,2,1,0:T(8,128)(2,1)S(1)}, u32[]{:S(2)}, u32[]{:S(2)}) collective-permute-start(bf16[4,2,64,256]{3,2,1,0:T(8,128)(2,1)S(1)} %pad_maximum_fusion.refs_2_.refs_0_), channel_id=1, source_target_pairs={{0,1},{1,0},{2,3},{3,2},{4,5},{5,4},{6,7},{7,6},{8,9},{9,8},{10,11... | collective-permute-start | bytes 786440 | tf_op jit(solution)/shard_map/ppermute | solution.py:26
  16.9 8.7 %collective-permute-start.7 = (bf16[4,2,64,256]{3,2,1,0:T(8,128)(2,1)S(1)}, bf16[4,2,64,256]{3,2,1,0:T(8,128)(2,1)S(1)}, u32[]{:S(2)}, u32[]{:S(2)}) collective-permute-start(bf16[4,2,64,256]{3,2,1,0:T(8,128)(2,1)S(1)} %pad_maximum_fusion.refs_2_.refs_0_), channel_id=1, source_target_pairs={{0,16},{8,24},{16,0},{24,8},{1,17},{9,25},{17,1},{25,9},{2,18},{10... | collective-permute-start | bytes 786440 | tf_op jit(solution)/shard_map/ppermute | solution.py:26
  25.6 1.7 %collective-permute-start.8 = (bf16[4,2,64,256]{3,2,1,0:T(8,128)(2,1)S(1)}, bf16[4,2,64,256]{3,2,1,0:T(8,128)(2,1)S(1)}, u32[]{:S(2)}, u32[]{:S(2)}) collective-permute-start(bf16[4,2,64,256]{3,2,1,0:T(8,128)(2,1)S(1)} %collective-permute-done.7.refs_0_), channel_id=1, source_target_pairs={{0,1},{1,0},{2,3},{3,2},{4,5},{5,4},{6,7},{7,6},{8,9},{9,8},{10,11... | collective-permute-start | bytes 786440 | tf_op jit(solution)/shard_map/ppermute | solution.py:26
  30.4 1.8 %collective-permute-start.11 = (bf16[2,2,64,256]{3,2,1,0:T(8,128)(2,1)S(1)}, bf16[2,2,64,256]{3,2,1,0:T(8,128)(2,1)S(1)}, u32[]{:S(2)}, u32[]{:S(2)}) collective-permute-start(bf16[2,2,64,256]{3,2,1,0:T(8,128)(2,1)S(1)} %get-tuple-element.76), channel_id=1, source_target_pairs={{0,1},{1,0},{2,3},{3,2},{4,5},{5,4},{6,7},{7,6},{8,9},{9,8},{10,11... | collective-permute-start | bytes 393224 | tf_op jit(solution)/shard_map/ppermute | solution.py:26
  31.0 1.3 %collective-permute-start.10 = (bf16[2,2,64,256]{3,2,1,0:T(8,128)(2,1)S(1)}, bf16[2,2,64,256]{3,2,1,0:T(8,128)(2,1)S(1)}, u32[]{:S(2)}, u32[]{:S(2)}) collective-permute-start(bf16[2,2,64,256]{3,2,1,0:T(8,128)(2,1)S(1)} %get-tuple-element.74), channel_id=1, source_target_pairs={{0,1},{1,0},{2,3},{3,2},{4,5},{5,4},{6,7},{7,6},{8,9},{9,8},{10,11... | collective-permute-start | bytes 393224 | tf_op jit(solution)/shard_map/ppermute | solution.py:26
  32.4 2.0 %collective-permute-start.12 = (bf16[64,128]{1,0:T(8,128)(2,1)S(1)}, bf16[64,128]{1,0:T(8,128)(2,1)S(1)}, u32[]{:S(2)}, u32[]{:S(2)}) collective-permute-start(bf16[64,128]{1,0:T(8,128)(2,1)S(1)} %slice_bitcast_fusion), channel_id=1, source_target_pairs={{0,1},{1,0},{2,3},{3,2},{4,5},{5,4},{6,7},{7,6},{8,9},{9,8},{10,11... | collective-permute-start | bytes 49160 | tf_op jit(solution)/shard_map/ppermute | solution.py:26
  32.8 6.4 %collective-permute-start.14 = (bf16[2,2,64,256]{3,2,1,0:T(8,128)(2,1)S(1)}, bf16[2,2,64,256]{3,2,1,0:T(8,128)(2,1)S(1)}, u32[]{:S(2)}, u32[]{:S(2)}) collective-permute-start(bf16[2,2,64,256]{3,2,1,0:T(8,128)(2,1)S(1)} %sum_cores.3), channel_id=1, source_target_pairs={{0,16},{8,24},{16,0},{24,8},{1,17},{9,25},{17,1},{25,9},{2,18},{10... | collective-permute-start | bytes 393224 | tf_op jit(solution)/shard_map/ppermute | solution.py:26
  35.5 4.6 %collective-permute-start.15 = (bf16[2,2,64,256]{3,2,1,0:T(8,128)(2,1)S(1)}, bf16[2,2,64,256]{3,2,1,0:T(8,128)(2,1)S(1)}, u32[]{:S(2)}, u32[]{:S(2)}) collective-permute-start(bf16[2,2,64,256]{3,2,1,0:T(8,128)(2,1)S(1)} %get-tuple-element.84), channel_id=1, source_target_pairs={{0,1},{1,0},{2,3},{3,2},{4,5},{5,4},{6,7},{7,6},{8,9},{9,8},{10,11... | collective-permute-start | bytes 393224 | tf_op jit(solution)/shard_map/ppermute | solution.py:26
  35.6 6.5 %collective-permute-start.18 = (bf16[2,2,64,256]{3,2,1,0:T(8,128)(2,1)S(1)}, bf16[2,2,64,256]{3,2,1,0:T(8,128)(2,1)S(1)}, u32[]{:S(2)}, u32[]{:S(2)}) collective-permute-start(bf16[2,2,64,256]{3,2,1,0:T(8,128)(2,1)S(1)} %sum_cores.2), channel_id=1, source_target_pairs={{0,16},{8,24},{16,0},{24,8},{1,17},{9,25},{17,1},{25,9},{2,18},{10... | collective-permute-start | bytes 393224 | tf_op jit(solution)/shard_map/ppermute | solution.py:26
  36.8 7.1 %collective-permute-start.19 = (bf16[2,2,64,256]{3,2,1,0:T(8,128)(2,1)S(1)}, bf16[2,2,64,256]{3,2,1,0:T(8,128)(2,1)S(1)}, u32[]{:S(2)}, u32[]{:S(2)}) collective-permute-start(bf16[2,2,64,256]{3,2,1,0:T(8,128)(2,1)S(1)} %get-tuple-element.88), channel_id=1, source_target_pairs={{0,1},{1,0},{2,3},{3,2},{4,5},{5,4},{6,7},{7,6},{8,9},{9,8},{10,11... | collective-permute-start | bytes 393224 | tf_op jit(solution)/shard_map/ppermute | solution.py:26
  36.8 13.9 %collective-permute-start.9 = (bf16[64,1024]{1,0:T(8,128)(2,1)S(1)}, bf16[64,1024]{1,0:T(8,128)(2,1)S(1)}, u32[]{:S(2)}, u32[]{:S(2)}) collective-permute-start(bf16[64,1024]{1,0:T(8,128)(2,1)S(1)} %get-tuple-element.65), channel_id=1, source_target_pairs={{0,8},{8,0},{16,24},{24,16},{1,9},{9,1},{17,25},{25,17},{2,10},{10... | collective-permute-start | bytes 393224 | tf_op jit(solution)/shard_map/ppermute | solution.py:26
  39.2 11.4 %collective-permute-start.13 = (bf16[64,1024]{1,0:T(8,128)(2,1)S(1)}, bf16[64,1024]{1,0:T(8,128)(2,1)S(1)}, u32[]{:S(2)}, u32[]{:S(2)}) collective-permute-start(bf16[64,1024]{1,0:T(8,128)(2,1)S(1)} %get-tuple-element.81), channel_id=1, source_target_pairs={{0,8},{8,0},{16,24},{24,16},{1,9},{9,1},{17,25},{25,17},{2,10},{10... | collective-permute-start | bytes 393224 | tf_op jit(solution)/shard_map/ppermute | solution.py:26
  40.1 7.3 %collective-permute-start.16 = (bf16[2,64,256]{2,1,0:T(8,128)(2,1)S(1)}, bf16[2,64,256]{2,1,0:T(8,128)(2,1)S(1)}, u32[]{:S(2)}, u32[]{:S(2)}) collective-permute-start(bf16[2,64,256]{2,1,0:T(8,128)(2,1)S(1)} %get-tuple-element.86), channel_id=1, source_target_pairs={{0,4},{1,5},{2,6},{3,7},{4,0},{5,1},{6,2},{7,3},{8,12},{9,13},{10,... | collective-permute-start | bytes 196616 | tf_op jit(solution)/shard_map/ppermute | solution.py:26
  42.1 6.3 %collective-permute-start.17 = (bf16[2,64,256]{2,1,0:T(8,128)(2,1)S(1)}, bf16[2,64,256]{2,1,0:T(8,128)(2,1)S(1)}, u32[]{:S(2)}, u32[]{:S(2)}) collective-permute-start(bf16[2,64,256]{2,1,0:T(8,128)(2,1)S(1)} %get-tuple-element.87), channel_id=1, source_target_pairs={{0,6},{1,7},{2,4},{3,5},{4,2},{5,3},{6,0},{7,1},{8,14},{9,15},{10,... | collective-permute-start | bytes 196616 | tf_op jit(solution)/shard_map/ppermute | solution.py:26
  43.9 5.4 %collective-permute-start.20 = (bf16[2,64,256]{2,1,0:T(8,128)(2,1)S(1)}, bf16[2,64,256]{2,1,0:T(8,128)(2,1)S(1)}, u32[]{:S(2)}, u32[]{:S(2)}) collective-permute-start(bf16[2,64,256]{2,1,0:T(8,128)(2,1)S(1)} %get-tuple-element.91), channel_id=1, source_target_pairs={{0,2},{1,3},{2,0},{3,1},{4,6},{5,7},{6,4},{7,5},{8,10},{9,11},{10,... | collective-permute-start | bytes 196616 | tf_op jit(solution)/shard_map/ppermute | solution.py:26
  49.3 4.0 %collective-permute-start.21 = (bf16[64,256]{1,0:T(8,128)(2,1)S(1)}, bf16[64,256]{1,0:T(8,128)(2,1)S(1)}, u32[]{:S(2)}, u32[]{:S(2)}) collective-permute-start(bf16[64,256]{1,0:T(8,128)(2,1)S(1)} %get-tuple-element.93), channel_id=1, source_target_pairs={{0,8},{8,0},{16,24},{24,16},{1,9},{9,1},{17,25},{25,17},{2,10},{10... | collective-permute-start | bytes 98312 | tf_op jit(solution)/shard_map/ppermute | solution.py:26

commit v8 on v7

--- a/solution.py
+++ b/solution.py
@@ -85,6 +85,16 @@
                 out_refs[s][1] = grad_ref[:, cols]
 
 
+def stack_kernel(count, *refs):
+    ins, refs = refs[:count], refs[count:]
+    passed = len(refs) // 2
+    refs, out_ref = refs[:-1], refs[-1]
+    for i, ref in enumerate(ins):
+        out_ref[i] = ref[...]
+    if passed:
+        refs[-1][...] = refs[0][...]
+
+
 class Plan:
     def __init__(self, kv, block_len, block_rows, rows, group, cores, z_devices, parts):
         self.kv, self.block_len, self.block_rows, self.rows = kv, block_len, block_rows, rows
@@ -93,8 +103,7 @@
         self.tile_rows = block_rows if block_rows % 16 == 0 else rows
         self.lanes = group * self.tile_rows
         self.query_rows = kv * group * rows
-        self.part_keys = self.z_part * kv * rows
-        self.chunk_keys = parts * self.part_keys
+        self.chunk_keys = self.z_part * kv * rows
         self.tiles = [(s, start) for s in range(kv) for start in range(0, rows, self.tile_rows)]
 
     def zone(self, part):
@@ -119,11 +128,11 @@
 
     def masked(self, scores, gap, chunk, info_ref):
         head, ctx = info_ref[0], info_ref[1]
-        a, core = chunk
+        a, core, part = chunk
         for j in range(self.chunk_keys // self.block_rows):
             m, rest = divmod(j, self.kv * self.blocks)
             s, b = divmod(rest, self.blocks)
-            stored = (ctx ^ (m * self.cores + core)) * self.blocks + b
+            stored = (ctx ^ (self.zone(part)[m] * self.cores + core)) * self.blocks + b
             first = info_ref[2 + stored] * self.block_len + (head ^ (a * self.kv + s)) * self.block_rows
             block = scores[j * self.block_rows : (j + 1) * self.block_rows]
             yield j * self.block_rows, jnp.where(gap >= first, block, LOWEST)
@@ -166,14 +175,12 @@
             piece = block[n * self.tile_rows : (n + 1) * self.tile_rows]
             out_ref[pl.ds(start, self.tile_rows), pl.ds(n * HD, HD)] = piece
 
-    def back(self, kv_refs, dkv_refs, p_ref, ds_ref, q_ref, do_ref):
+    def back(self, dkv_refs, p_ref, ds_ref, q_ref, do_ref):
         shape = (self.z_part, self.kv, self.rows, HD)
-        for i in range(len(kv_refs)):
-            for part in range(self.parts):
-                at = pl.ds(i * self.chunk_keys + self.zone(part)[0] * self.kv * self.rows, self.part_keys)
-                out_ref = dkv_refs[i * self.parts + part]
-                out_ref[:, :, :, :HD] = dot(ds_ref[at, :], q_ref[...]).astype(BF).reshape(shape)
-                out_ref[:, :, :, HD:] = dot(p_ref[at, :], do_ref[...]).astype(BF).reshape(shape)
+        for i, out_ref in enumerate(dkv_refs):
+            at = self.keys_at(i)
+            out_ref[:, :, :, :HD] = dot(ds_ref[at, :], q_ref[...]).astype(BF).reshape(shape)
+            out_ref[:, :, :, HD:] = dot(p_ref[at, :], do_ref[...]).astype(BF).reshape(shape)
 
 
 def forward_part(plan, chunks, info_ref, q_t, kv_refs, e_ref, top_ref, sum_ref, mix_ref, turned_ref):
@@ -194,11 +201,8 @@
         mix_ref[:, at] = mixed
 
 
-def near_kernel(plan, chunks, info_ref, *refs):
-    kv, count = plan.kv, len(chunks)
-    q_parts, refs = refs[:kv], refs[kv:]
-    kv_refs, refs = refs[:count], refs[count:]
-    (q_all, do_all, q_t, do_t), refs = refs[:4], refs[4:]
+def turn_kernel(plan, *refs):
+    q_parts, (q_all, do_all, q_t, do_t) = refs[:-4], refs[-4:]
     for tile, (s, start) in enumerate(plan.tiles):
         span = pl.ds(start, plan.tile_rows)
         for n in range(plan.group):
@@ -208,11 +212,10 @@
         at = plan.at(tile)
         q_t[:, at] = q_all[at, :].T
         do_t[:, at] = do_all[at, :].T
-    forward_part(plan, chunks, info_ref, q_t, kv_refs, *refs)
-
-
-def mid_kernel(plan, chunks, info_ref, q_t, *refs):
-    forward_part(plan, chunks, info_ref, q_t, refs[: len(chunks)], *refs[len(chunks) :])
+
+
+def part_kernel(plan, chunks, info_ref, q_t, *refs):
+    forward_part(plan, chunks, info_ref, q_t, refs[: len(chunks)], *refs[-5:])
 
 
 def far_kernel(plan, chunks, others, info_ref, q_all, do_all, q_t, do_t, *refs):
@@ -262,7 +265,7 @@
             ds_ref[plan.keys_at(i), at] = grad_s
             q_grad = q_grad + dot(turned_ref[pl.ds(0, HD), plan.keys_at(i)], grad_s)
         q_grad_ref[:, at] = q_grad
-    plan.back(kv_refs, dkv_refs, p_ref, ds_ref, q_all, do_all)
+    plan.back(dkv_refs, p_ref, ds_ref, q_all, do_all)
     for tile, mixed in enumerate(mixes):
         plan.store_heads(att_refs[plan.tiles[tile][0]], tile, mixed)
 
@@ -271,7 +274,7 @@
     count = len(rows_at)
     kv_refs, refs = refs[:count], refs[count + order :]
     refs, (turned_ref, p_ref, ds_ref) = refs[:-3], refs[-3:]
-    outs, dkv_refs = refs[: -plan.parts * count], refs[-plan.parts * count :]
+    outs, dkv_refs = refs[:-count], refs[-count:]
     spans = [plan.at(tile) for tile in range(len(plan.tiles))]
     for at in spans:
         for i, ref in enumerate(kv_refs):
@@ -280,7 +283,7 @@
             grad_s = (probs * (dot(plan.values(ref), do_t[:, at]) - delta_ref[:, at])).astype(BF)
             ds_ref[plan.keys_at(i), at] = grad_s
     plan.turn(kv_refs, turned_ref)
-    plan.back(kv_refs, dkv_refs, p_ref, ds_ref, q_all, do_all)
+    plan.back(dkv_refs, p_ref, ds_ref, q_all, do_all)
     for tile, at in enumerate(spans):
         q_grad = q_grad_in[:, at]
         for i in range(count):
@@ -371,6 +374,8 @@
     def with_swaps(blocks):
         return [blocks[0]] + [swap(blocks[s], "head", s) for s in range(1, kv)]
 
+    dkv = bf(z_part, kv, rows, 2 * HD)
+
     key_parts = with_swaps([key_vectors] * kv)[1:]
     value_parts = with_swaps([value_vectors] * kv)[1:]
     mine = (head % kv) * HD
@@ -395,50 +400,69 @@
     pieces = [swap(piece, "ctx", m * cores) for m in reversed(range(1, z_devices))]
     pieces = [piece] + pieces[::-1]
     q_parts = with_swaps(q_parts)
-    column = jnp.stack(pieces)
-    columns = [swap(column, "head", a * kv) for a in range(1, spans)]
-    near_kv = [column] + [swap(column, "ctx", core) for core in range(1, cores)]
-    near_chunks = [(0, core) for core in range(cores)]
-    mid_chunks = [(a, 0) for a in range(1, spans)]
-    far_chunks = [(a, core) for a in range(1, spans) for core in range(1, cores)]
+    column, handed, order = [None] * parts, [None] * parts, []
+    for p in reversed(range(parts)):
+        parcels = [pieces[m] for m in plan.zone(p)]
+        extra = [column[p + 1], *order] if order else []
+        *handed_on, column[p] = call(
+            functools.partial(stack_kernel, len(parcels)),
+            "stack",
+            (*parcels, *extra),
+            [dkv] * (1 + bool(extra)),
+        )
+        handed[p] = column[p]
+        if extra:
+            handed[p + 1] = handed_on[0]
+        order = [swap(column[p][0, 0, :, :HD], "ctx", 1)] if cores > 1 and p else []
+    columns = [[swap(half, "head", a * kv) for half in column] for a in range(1, spans)]
+    near_kv = [column] + [[swap(half, "ctx", core) for half in handed] for core in range(1, cores)]
+    near_flat = [half for pair in near_kv for half in pair]
+    each = range(parts)
+    near_chunks = [(0, core, p) for core in range(cores) for p in each]
+    mid_chunks = [(a, 0, p) for a in range(1, spans) for p in each]
+    far_chunks = [(a, core, p) for a in range(1, spans) for core in range(1, cores) for p in each]
 
     keys = plan.chunk_keys
     query_rows = plan.query_rows
     row, column_out = f32(1, query_rows), f32(HD, query_rows)
-    dkv = bf(z_part, kv, rows, 2 * HD)
-
-    def part_outs(chunks):
-        return [f32(len(chunks) * keys, query_rows), row, row, column_out]
-
-    q_all, do_all, q_t, do_t, near_e, *near = call(
-        functools.partial(near_kernel, plan, near_chunks),
-        "attend_near",
-        (info, *q_parts, *near_kv),
-        [bf(query_rows, HD)] * 2 + [bf(HD, query_rows)] * 2 + part_outs(near_chunks),
-        [SMEM] + [VMEM] * (kv + len(near_kv)),
-        [pltpu.VMEM((2 * HD, cores * keys), BF)],
-        cores * keys * 4 * HD,
-        8 * cores * keys * query_rows * HD,
-    )
-    mid_kv = after(columns, [near[0]])
-    far_kv = [swap(part, "ctx", core) for part in mid_kv for core in range(1, cores)]
-    mid_e, *mid = call(
-        functools.partial(mid_kernel, plan, mid_chunks),
-        "attend_mid",
-        (info, q_t, *mid_kv),
-        part_outs(mid_chunks),
-        [SMEM] + [VMEM] * (1 + len(mid_kv)),
-        [pltpu.VMEM((2 * HD, len(mid_kv) * keys), BF)],
-        len(mid_kv) * keys * 4 * HD,
-        8 * len(mid_kv) * keys * query_rows * HD,
-    )
+
+    q_all, do_all, q_t, do_t = call(
+        functools.partial(turn_kernel, plan),
+        "turn",
+        q_parts,
+        [bf(query_rows, HD)] * 2 + [bf(HD, query_rows)] * 2,
+    )
+
+    def forward(name, chunks, kv_refs, order):
+        size = len(chunks) * keys
+        return call(
+            functools.partial(part_kernel, plan, chunks),
+            name,
+            (info, q_t, *kv_refs, *order),
+            [f32(size, query_rows), row, row, column_out],
+            [SMEM] + [VMEM] * (1 + len(kv_refs) + len(order)),
+            [pltpu.VMEM((2 * HD, size), BF)],
+            size * 4 * HD,
+            8 * size * query_rows * HD,
+        )
+
+    mids, order = [None] * parts, []
+    for p in reversed(each):
+        if p + 1 < parts or parts == 1:
+            near_e, *near = forward("attend_near", near_chunks, near_flat, order)
+            order = [near[0]]
+            for pair in columns:
+                pair[p] = after([pair[p]], order)[0]
+        mids[p] = forward("attend_mid", [c for c in mid_chunks if c[2] == p], [pair[p] for pair in columns], order)
+        order = [mids[p][1]]
+    far_kv = [swap(pair[p], "ctx", core) for pair in columns for core in range(1, cores) for p in each]
     far_keys = len(far_kv) * keys
     outs = call(
-        functools.partial(far_kernel, plan, far_chunks, 2),
+        functools.partial(far_kernel, plan, far_chunks, 1 + parts),
         "attend_far",
-        (info, q_all, do_all, q_t, do_t, *near, *mid, *far_kv),
-        [bf(rows, width)] * kv + [row, row, row, column_out] + [dkv] * (parts * len(far_kv)),
-        [SMEM] + [VMEM] * (10 + len(far_kv)),
+        (info, q_all, do_all, q_t, do_t, *near, *[r for mid in mids for r in mid[1:]], *far_kv),
+        [bf(rows, width)] * kv + [row] * (2 + parts) + [column_out] + [dkv] * len(far_kv),
+        [SMEM] + [VMEM] * (7 + 3 * parts + len(far_kv)),
         [
             pltpu.VMEM((2 * HD, far_keys), BF),
             pltpu.VMEM((far_keys, query_rows), F32),
@@ -450,7 +474,8 @@
         16 * far_keys * query_rows * HD,
     )
     att_parts, outs = outs[:kv], outs[kv:]
-    (near_scale, mid_scale, delta, q_grad), far_dkv = outs[:4], outs[4:]
+    (near_scale, *mid_scales), outs = outs[: 1 + parts], outs[1 + parts :]
+    (delta, q_grad), far_dkv = outs[:2], outs[2:]
 
     def back(rows_at, last, e, scale, q_grad, kv_refs, order):
         count = len(rows_at)
@@ -459,7 +484,7 @@
             functools.partial(back_kernel, plan, rows_at, last, len(order)),
             "attend_back",
             (q_all, do_all, do_t, e, scale, delta, q_grad, *kv_refs, *order),
-            q_outs + [dkv] * (parts * count),
+            q_outs + [dkv] * count,
             None,
             [
                 pltpu.VMEM((2 * HD, count * keys), BF),
@@ -471,12 +496,15 @@
         )
         return outs[: len(q_outs)], outs[len(q_outs) :]
 
-    (q_grad,), mid_dkv = back(list(range(spans - 1)), False, mid_e, mid_scale, q_grad, mid_kv, [])
     sums = [[] for _ in range(parts)]
     totals = []
-    for a in range(spans - 1):
-        for p in reversed(range(parts)):
-            both = [mid_dkv[a * parts + p]]
+    for p in reversed(each):
+        mid_kv = [pair[p] for pair in columns]
+        (q_grad,), mid_dkv = back(
+            list(range(len(mid_kv))), False, mids[p][0], mid_scales[p], q_grad, mid_kv, []
+        )
+        for a in range(spans - 1):
+            both = [mid_dkv[a]]
             for core in range(1, cores):
                 ours = far_dkv[(a * (cores - 1) + core - 1) * parts + p]
                 both.append(swap(ours, "ctx", core))
@@ -484,7 +512,9 @@
             sums[p].append(swap(totals[-1], "head", (a + 1) * kv))
     order = [swap(totals[-1][0, 0, :, :HD], "ctx", 1)] if cores > 1 else []
     for core in reversed(range(cores)):
-        outs, parts_dkv = back([core], core == 0, near_e, near_scale, q_grad, [near_kv[core]], order)
+        outs, parts_dkv = back(
+            [core * parts + p for p in each], core == 0, near_e, near_scale, q_grad, near_kv[core], order
+        )
         q_grad = outs[0]
         for p in range(parts):
             sums[p].append(swap(parts_dkv[p], "ctx", core) if core else parts_dkv[p])

time: 54.2 us -> 54.1 us (level)
  Pallas kernels: 12.7 us -> 13.9 us
  starting transfers between devices: 21.6 us -> 20.5 us
    pallas_call x15 -> x20, Pallas kernels: 12.7 us -> 13.9 us  [call(): pl.pallas_call(kernel, out_shape=list(outs), in_specs=specs or [VMEM] * l...]
    ppermute x22 -> x26, starting transfers between devices: 21.6 us -> 20.5 us  [swap(): return lax.ppermute(block, axis, [(i, i ^ mask) for i in range(size)])]
    ppermute x22 -> x26, waiting for transfers between devices: 14.7 us -> 14.4 us  [swap(): return lax.ppermute(block, axis, [(i, i ^ mask) for i in range(size)])]
  transfers between devices with their start and end apart: 22 -> 26, of which waited for: 9 -> 10; matrix products, arithmetic and copies ran while one was open for 4% -> 4% of each run, Pallas kernels for 17% -> 19%
where the time goes in v8:
time: 54.1 us; the launch traced here: 53.8 us
  starting transfers between devices  20.5 us (38%)
  waiting for transfers between devices  14.4 us (27%)
  Pallas kernels  13.9 us (26%)
  local copies, waits for them, and re-layouts  3.34 us (6%)
  between operations  0.86 us (2%)
  other arithmetic  0.74 us (1%)
    ppermute x26, starting transfers between devices, swap(): return lax.ppermute(block, axis, [(i, i ^ mask) for i in range(size)])  20.5 us
    ppermute x26, waiting for transfers between devices, swap(): return lax.ppermute(block, axis, [(i, i ^ mask) for i in range(size)])  14.4 us
    pallas_call x20, Pallas kernels, call(): pl.pallas_call(kernel, out_shape=list(outs), in_specs=specs or [VMEM] * l...  13.9 us
    unnamed x4, local copies, waits for them, and re-layouts  1.9 us
    dynamic_slice x2, local copies, waits for them, and re-layouts, shards(): lax.dynamic_slice_in_dim(block, mine, HD, 1)  1.44 us
  transfers between devices with their start and end apart: 26, of which 10 were waited for; matrix products, arithmetic and copies ran while one was open for 4% of the time, Pallas kernels for 19%

profile of v8, /device:TPU:0, one launch (start us, length us, event | category | flops | bytes accessed | tf_op | source)
XLA Modules:
  0.0 53.8 jit_solution(15234700084604451743)
XLA Ops:
  0.6 3.0 %collective-permute-start.1 = (bf16[64,256]{1,0:T(8,128)(2,1)}, bf16[64,256]{1,0:T(8,128)(2,1)S(1)}, u32[]{:S(2)}, u32[]{:S(2)}) collective-permute-start(bf16[64,256]{1,0:T(8,128)(2,1)} %bitcast.17), channel_id=1, source_target_pairs={{0,8},{8,0},{16,24},{24,16},{1,9},{9,1},{17,25},{25,17},{2,10},{10... | collective-permute-start | bytes 98312 | tf_op jit(solution)/shard_map/ppermute | solution.py:26
  3.6 0.1 collective-permute-start.2
  3.7 0.7 %constant_dynamic-slice_fusion.1 = bf16[64,128]{1,0:T(8,128)(2,1)S(1)} fusion(bf16[64,256]{1,0:T(8,128)(2,1)} %bitcast.18, s32[]{:T(128)S(6)} %select_n.14), kind=kLoop, calls=%fused_computation.5 | loop fusion | bytes 32772 | tf_op jit(solution)/shard_map/dynamic_slice | solution.py:383
  4.4 0.7 %constant_dynamic-slice_fusion = bf16[64,128]{1,0:T(8,128)(2,1)S(1)} fusion(bf16[64,256]{1,0:T(8,128)(2,1)} %bitcast.20, s32[]{:T(128)S(6)} %select_n.14), kind=kLoop, calls=%fused_computation.4 | loop fusion | bytes 32772 | tf_op jit(solution)/shard_map/dynamic_slice | solution.py:383
  5.2 0.9 %copy-done = bf16[2,32,2048]{2,1,0:T(8,128)(2,1)S(1)} copy-done((bf16[2,32,2048]{2,1,0:T(8,128)(2,1)S(1)}, bf16[2,32,2048]{2,1,0:T(8,128)(2,1)}, u32[]{:S(2)}) %copy-start) | copy-done | bytes 262168
  6.1 0.9 %copy-done.1 = bf16[2,32,2048]{2,1,0:T(8,128)(2,1)S(1)} copy-done((bf16[2,32,2048]{2,1,0:T(8,128)(2,1)S(1)}, bf16[2,32,2048]{2,1,0:T(8,128)(2,1)}, u32[]{:S(2)}) %copy-start.1) | copy-done | bytes 262168
  7.1 0.6 %collective-permute-done.2.refs_2_ = bf16[64,256]{1,0:T(8,128)(2,1)S(1)} collective-permute-done((bf16[64,256]{1,0:T(8,128)(2,1)}, bf16[64,256]{1,0:T(8,128)(2,1)S(1)}, u32[]{:S(2)}, u32[]{:S(2)}) %collective-permute-start.2) | collective-permute-done | bytes 32800 | tf_op jit(solution)/shard_map/ppermute | solution.py:26
  7.8 1.6 %collective-permute-start.5 = (bf16[2,64,256]{2,1,0:T(8,128)(2,1)S(1)}, bf16[2,64,256]{2,1,0:T(8,128)(2,1)S(1)}, u32[]{:S(2)}, u32[]{:S(2)}) collective-permute-start(bf16[2,64,256]{2,1,0:T(8,128)(2,1)S(1)} %pack_kv.1.refs_0_), channel_id=1, source_target_pairs={{0,2},{1,3},{2,0},{3,1},{4,6},{5,7},{6,4},{7,5},{8,10},{9,11},{10,... | collective-permute-start | bytes 196616 | tf_op jit(solution)/shard_map/ppermute | solution.py:26
  9.4 1.3 %collective-permute-start = (bf16[2,64,1024]{2,1,0:T(8,128)(2,1)S(1)}, bf16[2,64,1024]{2,1,0:T(8,128)(2,1)S(1)}, u32[]{:S(2)}, u32[]{:S(2)}) collective-permute-start(bf16[2,64,1024]{2,1,0:T(8,128)(2,1)S(1)} %get-tuple-element.59), channel_id=1, source_target_pairs={{0,8},{8,0},{16,24},{24,16},{1,9},{9,1},{17,25},{25,17},{2,10},{10... | collective-permute-start | bytes 786440 | tf_op jit(solution)/shard_map/ppermute | solution.py:26
  10.7 2.5 %collective-permute-start.4 = (bf16[2,64,256]{2,1,0:T(8,128)(2,1)S(1)}, bf16[2,64,256]{2,1,0:T(8,128)(2,1)S(1)}, u32[]{:S(2)}, u32[]{:S(2)}) collective-permute-start(bf16[2,64,256]{2,1,0:T(8,128)(2,1)S(1)} %pack_kv.1.refs_0_), channel_id=1, source_target_pairs={{0,6},{1,7},{2,4},{3,5},{4,2},{5,3},{6,0},{7,1},{8,14},{9,15},{10,... | collective-permute-start | bytes 196616 | tf_op jit(solution)/shard_map/ppermute | solution.py:26
  13.2 0.1 collective-permute-start.3
  13.3 1.6 %collective-permute-start.9 = (bf16[2,2,64,256]{3,2,1,0:T(8,128)(2,1)S(1)}, bf16[2,2,64,256]{3,2,1,0:T(8,128)(2,1)S(1)}, u32[]{:S(2)}, u32[]{:S(2)}) collective-permute-start(bf16[2,2,64,256]{3,2,1,0:T(8,128)(2,1)S(1)} %stack.10.refs_2_.refs_1_), channel_id=1, source_target_pairs={{0,16},{8,24},{16,0},{24,8},{1,17},{9,25},{17,1},{25,9},{2,18},{10... | collective-permute-start | bytes 393224 | tf_op jit(solution)/shard_map/ppermute | solution.py:26
  14.9 1.9 %collective-permute-done.4.refs_1_ = bf16[2,64,256]{2,1,0:T(8,128)(2,1)S(1)} collective-permute-done((bf16[2,64,256]{2,1,0:T(8,128)(2,1)S(1)}, bf16[2,64,256]{2,1,0:T(8,128)(2,1)S(1)}, u32[]{:S(2)}, u32[]{:S(2)}) %collective-permute-start.4) | collective-permute-done | bytes 65568 | tf_op jit(solution)/shard_map/ppermute | solution.py:26
  16.8 2.3 %collective-permute-done.3.refs_0_ = bf16[2,64,256]{2,1,0:T(8,128)(2,1)S(1)} collective-permute-done((bf16[2,64,256]{2,1,0:T(8,128)(2,1)S(1)}, bf16[2,64,256]{2,1,0:T(8,128)(2,1)S(1)}, u32[]{:S(2)}, u32[]{:S(2)}) %collective-permute-start.3) | collective-permute-done | bytes 65568 | tf_op jit(solution)/shard_map/ppermute | solution.py:26
  19.1 1.6 %collective-permute-start.10 = (bf16[2,2,64,256]{3,2,1,0:T(8,128)(2,1)S(1)}, bf16[2,2,64,256]{3,2,1,0:T(8,128)(2,1)S(1)}, u32[]{:S(2)}, u32[]{:S(2)}) collective-permute-start(bf16[2,2,64,256]{3,2,1,0:T(8,128)(2,1)S(1)} %get-tuple-element.65.refs_0_), channel_id=1, source_target_pairs={{0,16},{8,24},{16,0},{24,8},{1,17},{9,25},{17,1},{25,9},{2,18},{10... | collective-permute-start | bytes 393224 | tf_op jit(solution)/shard_map/ppermute | solution.py:26
  20.7 0.5 collective-permute-start.8
  21.2 0.7 %pad_add_fusion.info_ref = s32[18]{0:T(128)S(1)} fusion(s32[16]{0:T(128)} %param.9, s32[1]{0:T(128)} %bitcast.2, s32[1]{0:T(128)} %bitcast.1), kind=kLoop, calls=%fused_computation.3 | loop fusion | flops 36 | bytes 144 | tf_op jit(solution)/shard_map/concatenate | solution.py:361
  22.0 0.2 turn.1
  22.2 1.3 %attend_mid.2 = (f32[256,1024]{1,0:T(8,128)S(1)}, f32[1,1024]{1,0:T(1,128)S(1)}, f32[1,1024]{1,0:T(1,128)S(1)}, f32[128,1024]{1,0:T(8,128)S(1)}) custom-call(s32[18]{0:T(128)S(1)} %pad_add_fusion.info_ref, bf16[128,1024]{1,0:T(8,128)(2,1)S(1)} %get-tuple-element.62.q_t, bf16[2,2,64,256]{3,2,1,0:T(8,128)(2,1)S(1)} %collective-permute-done.9.refs_0_), custom_call_target="tpu_custom_call" | custom-call | flops 268435456 | bytes 1974344 | tf_op jit(solution)/shard_map/attend_mid/pallas_call | solution.py:41
  23.5 2.6 %attend_near.1 = (f32[1024,1024]{1,0:T(8,128)S(1)}, f32[1,1024]{1,0:T(1,128)S(1)}, f32[1,1024]{1,0:T(1,128)S(1)}, f32[128,1024]{1,0:T(8,128)S(1)}) custom-call(s32[18]{0:T(128)S(1)} %pad_add_fusion.info_ref, bf16[128,1024]{1,0:T(8,128)(2,1)S(1)} %get-tuple-element.62.q_t, bf16[2,2,64,256]{3,2,1,0:T(8,128)(2,1)S(1)} %get-tuple-element.65.refs_0_, ...), custom_call_target="tpu_custom_call" | custom-call | flops 1073741824 | bytes 5517384 | tf_op jit(solution)/shard_map/attend_near/pallas_call | solution.py:41
  26.0 0.6 %collective-permute-start.11 = (bf16[2,2,64,256]{3,2,1,0:T(8,128)(2,1)S(1)}, bf16[2,2,64,256]{3,2,1,0:T(8,128)(2,1)S(1)}, u32[]{:S(2)}, u32[]{:S(2)}) collective-permute-start(bf16[2,2,64,256]{3,2,1,0:T(8,128)(2,1)S(1)} %collective-permute-done.10.refs_0_), channel_id=1, source_target_pairs={{0,1},{1,0},{2,3},{3,2},{4,5},{5,4},{6,7},{7,6},{8,9},{9,8},{10,11... | collective-permute-start | bytes 393224 | tf_op jit(solution)/shard_map/ppermute | solution.py:26
  26.6 1.2 %attend_mid.3 = (f32[256,1024]{1,0:T(8,128)S(1)}, f32[1,1024]{1,0:T(1,128)S(1)}, f32[1,1024]{1,0:T(1,128)S(1)}, f32[128,1024]{1,0:T(8,128)S(1)}) custom-call(s32[18]{0:T(128)S(1)} %pad_add_fusion.info_ref, bf16[128,1024]{1,0:T(8,128)(2,1)S(1)} %get-tuple-element.62.q_t, bf16[2,2,64,256]{3,2,1,0:T(8,128)(2,1)S(1)} %collective-permute-done.10.refs_0_, ...), custom_call_target="tpu_custom_call" | custom-call | flops 268435456 | bytes 1978440 | tf_op jit(solution)/shard_map/attend_mid/pallas_call | solution.py:41
  27.9 3.2 %attend_far.1 = (bf16[64,1024]{1,0:T(8,128)(2,1)S(1)}, bf16[64,1024]{1,0:T(8,128)(2,1)S(1)}, f32[1,1024]{1,0:T(1,128)S(1)}, f32[1,1024]{1,0:T(1,128)S(1)}, f32[1...) custom-call(s32[18]{0:T(128)S(1)} %pad_add_fusion.info_ref, ...), custom_call_target="tpu_custom_call" | custom-call | flops 1073741824 | bytes 3973192 | tf_op jit(solution)/shard_map/attend_far/pallas_call | solution.py:41
  31.1 0.1 collective-permute-start.15
  31.2 0.5 collective-permute-start.14
  31.7 0.6 %attend_back.4 = (f32[128,1024]{1,0:T(8,128)S(1)}, bf16[2,2,64,256]{3,2,1,0:T(8,128)(2,1)S(1)}) custom-call(bf16[1024,128]{1,0:T(8,128)(2,1)S(1)} %get-tuple-element.60.q_all, bf16[1024,128]{1,0:T(8,128)(2,1)S(1)} %get-tuple-element.61.do_all, bf16[128,1024]{1,0:T(8,128)(2,1)S(1)} %get-tuple-element.63.do_t, f32[256,1024]{1,0:T(8,128)S(1)} %get-tuple-element.84.e_ref, ...), custom_call_target="tpu_custom_call" | custom-call | flops 402653184 | bytes 3153920 | tf_op jit(solution)/shard_map/attend_back/pallas_call | solution.py:41
  32.3 0.6 %attend_back.5 = (f32[128,1024]{1,0:T(8,128)S(1)}, bf16[2,2,64,256]{3,2,1,0:T(8,128)(2,1)S(1)}) custom-call(bf16[1024,128]{1,0:T(8,128)(2,1)S(1)} %get-tuple-element.60.q_all, bf16[1024,128]{1,0:T(8,128)(2,1)S(1)} %get-tuple-element.61.do_all, bf16[128,1024]{1,0:T(8,128)(2,1)S(1)} %get-tuple-element.63.do_t, f32[256,1024]{1,0:T(8,128)S(1)} %get-tuple-element.82.e_ref, ...), custom_call_target="tpu_custom_call" | custom-call | flops 402653184 | bytes 3153920 | tf_op jit(solution)/shard_map/attend_back/pallas_call | solution.py:41
  33.1 0.1 collective-permute-start.16
  33.2 0.5 collective-permute-start.18
  33.7 0.6 %collective-permute-done.16.refs_2_ = bf16[64,128]{1,0:T(8,128)(2,1)S(1)} collective-permute-done((bf16[64,128]{1,0:T(8,128)(2,1)S(1)}, bf16[64,128]{1,0:T(8,128)(2,1)S(1)}, u32[]{:S(2)}, u32[]{:S(2)}) %collective-permute-start.16) | collective-permute-done | bytes 16416 | tf_op jit(solution)/shard_map/ppermute | solution.py:26
  34.3 1.1 %attend_back.6 = (f32[128,1024]{1,0:T(8,128)S(1)}, bf16[2,2,64,256]{3,2,1,0:T(8,128)(2,1)S(1)}, bf16[2,2,64,256]{3,2,1,0:T(8,128)(2,1)S(1)}) custom-call(bf16[1024,128]{1,0:T(8,128)(2,1)S(1)} %get-tuple-element.60.q_all, bf16[1024,128]{1,0:T(8,128)(2,1)S(1)} %get-tuple-element.61.do_all, bf16[128,1024]{1,0:T(8,128)(2,1)S(1)} %get-tuple-element.63.do_t, ...), custom_call_target="tpu_custom_call" | custom-call | flops 805306368 | bytes 6578176 | tf_op jit(solution)/shard_map/attend_back/pallas_call | solution.py:41
  35.5 0.2 collective-permute-start.19
  35.7 0.9 %collective-permute-start.22 = (bf16[2,2,64,256]{3,2,1,0:T(8,128)(2,1)S(1)}, bf16[2,2,64,256]{3,2,1,0:T(8,128)(2,1)S(1)}, u32[]{:S(2)}, u32[]{:S(2)}) collective-permute-start(bf16[2,2,64,256]{3,2,1,0:T(8,128)(2,1)S(1)} %sum_cores.2), channel_id=1, source_target_pairs={{0,16},{8,24},{16,0},{24,8},{1,17},{9,25},{17,1},{25,9},{2,18},{10... | collective-permute-start | bytes 393224 | tf_op jit(solution)/shard_map/ppermute | solution.py:26
  36.7 0.7 %collective-permute-start.13 = (bf16[64,1024]{1,0:T(8,128)(2,1)S(1)}, bf16[64,1024]{1,0:T(8,128)(2,1)S(1)}, u32[]{:S(2)}, u32[]{:S(2)}) collective-permute-start(bf16[64,1024]{1,0:T(8,128)(2,1)S(1)} %get-tuple-element.78), channel_id=1, source_target_pairs={{0,8},{8,0},{16,24},{24,16},{1,9},{9,1},{17,25},{25,17},{2,10},{10... | collective-permute-start | bytes 393224 | tf_op jit(solution)/shard_map/ppermute | solution.py:26
  37.4 1.2 %attend_back.7 = (bf16[64,1024]{1,0:T(8,128)(2,1)S(1)}, bf16[64,1024]{1,0:T(8,128)(2,1)S(1)}, bf16[2,2,64,256]{3,2,1,0:T(8,128)(2,1)S(1)}, bf16[2,2,64,256]{3,2,1,0:T(8,128)(2,1)S(1)}) custom-call(bf16[1024,128]{1,0:T(8,128)(2,1)S(1)} %get-tuple-element.60.q_all, bf16[1024,128]{1,0:T(8,128)(2,1)S(1)} %get-tuple-element.61.do_all, ...), custom_call_target="tpu_custom_call" | custom-call | flops 805306368 | bytes 6316032 | tf_op jit(solution)/shard_map/attend_back/pallas_call | solution.py:41
  38.6 0.8 %collective-permute-done.18.refs_0_ = bf16[2,2,64,256]{3,2,1,0:T(8,128)(2,1)S(1)} collective-permute-done((bf16[2,2,64,256]{3,2,1,0:T(8,128)(2,1)S(1)}, bf16[2,2,64,256]{3,2,1,0:T(8,128)(2,1)S(1)}, u32[]{:S(2)}, u32[]{:S(2)}) %collective-permute-start.18) | collective-permute-done | bytes 131104 | tf_op jit(solution)/shard_map/ppermute | solution.py:26
  39.4 0.7 %collective-permute-start.17 = (bf16[64,1024]{1,0:T(8,128)(2,1)S(1)}, bf16[64,1024]{1,0:T(8,128)(2,1)S(1)}, u32[]{:S(2)}, u32[]{:S(2)}) collective-permute-start(bf16[64,1024]{1,0:T(8,128)(2,1)S(1)} %get-tuple-element.97), channel_id=1, source_target_pairs={{0,8},{8,0},{16,24},{24,16},{1,9},{9,1},{17,25},{25,17},{2,10},{10... | collective-permute-start | bytes 393224 | tf_op jit(solution)/shard_map/ppermute | solution.py:26
  40.2 0.5 collective-permute-start.20
  40.7 1.2 %collective-permute-done.22.refs_0_ = bf16[2,2,64,256]{3,2,1,0:T(8,128)(2,1)S(1)} collective-permute-done((bf16[2,2,64,256]{3,2,1,0:T(8,128)(2,1)S(1)}, bf16[2,2,64,256]{3,2,1,0:T(8,128)(2,1)S(1)}, u32[]{:S(2)}, u32[]{:S(2)}) %collective-permute-start.22) | collective-permute-done | bytes 131104 | tf_op jit(solution)/shard_map/ppermute | solution.py:26
  41.9 2.2 %collective-permute-start.21 = (bf16[2,64,256]{2,1,0:T(8,128)(2,1)S(1)}, bf16[2,64,256]{2,1,0:T(8,128)(2,1)S(1)}, u32[]{:S(2)}, u32[]{:S(2)}) collective-permute-start(bf16[2,64,256]{2,1,0:T(8,128)(2,1)S(1)} %get-tuple-element.103), channel_id=1, source_target_pairs={{0,6},{1,7},{2,4},{3,5},{4,2},{5,3},{6,0},{7,1},{8,14},{9,15},{10,... | collective-permute-start | bytes 196616 | tf_op jit(solution)/shard_map/ppermute | solution.py:26
  44.1 0.1 collective-permute-start.24
  44.2 3.0 %collective-permute-done.20.refs_0_ = bf16[2,64,256]{2,1,0:T(8,128)(2,1)S(1)} collective-permute-done((bf16[2,64,256]{2,1,0:T(8,128)(2,1)S(1)}, bf16[2,64,256]{2,1,0:T(8,128)(2,1)S(1)}, u32[]{:S(2)}, u32[]{:S(2)}) %collective-permute-start.20) | collective-permute-done | bytes 65568 | tf_op jit(solution)/shard_map/ppermute | solution.py:26
  47.2 1.0 %collective-permute-done.21.refs_1_ = bf16[2,64,256]{2,1,0:T(8,128)(2,1)S(1)} collective-permute-done((bf16[2,64,256]{2,1,0:T(8,128)(2,1)S(1)}, bf16[2,64,256]{2,1,0:T(8,128)(2,1)S(1)}, u32[]{:S(2)}, u32[]{:S(2)}) %collective-permute-start.21) | collective-permute-done | bytes 65568 | tf_op jit(solution)/shard_map/ppermute | solution.py:26
  48.2 0.9 %collective-permute-done.24.refs_3_ = bf16[2,64,256]{2,1,0:T(8,128)(2,1)S(1)} collective-permute-done((bf16[2,64,256]{2,1,0:T(8,128)(2,1)S(1)}, bf16[2,64,256]{2,1,0:T(8,128)(2,1)S(1)}, u32[]{:S(2)}, u32[]{:S(2)}) %collective-permute-start.24) | collective-permute-done | bytes 65568 | tf_op jit(solution)/shard_map/ppermute | solution.py:26
  49.1 1.0 %collective-permute-start.25 = (bf16[64,256]{1,0:T(8,128)(2,1)S(1)}, bf16[64,256]{1,0:T(8,128)(2,1)S(1)}, u32[]{:S(2)}, u32[]{:S(2)}) collective-permute-start(bf16[64,256]{1,0:T(8,128)(2,1)S(1)} %get-tuple-element.109), channel_id=1, source_target_pairs={{0,8},{8,0},{16,24},{24,16},{1,9},{9,1},{17,25},{25,17},{2,10},{10... | collective-permute-start | bytes 98312 | tf_op jit(solution)/shard_map/ppermute | solution.py:26
  50.2 0.8 %finish_q.1 = (bf16[64,2048]{1,0:T(8,128)(2,1)}, bf16[64,2048]{1,0:T(8,128)(2,1)}) custom-call(s32[1]{0:T(128)} %bitcast.group_ref, bf16[64,1024]{1,0:T(8,128)(2,1)S(1)} %get-tuple-element.77.refs_0_, bf16[64,1024]{1,0:T(8,128)(2,1)S(1)} %collective-permute-done.13.refs_1_, bf16[64,1024]{1,0:T(8,128)(2,1)S(1)} %get-tuple-element.96.refs_2_, ...), custom_call_target="tpu_custom_call" | custom-call | bytes 1048580 | tf_op jit(solution)/shard_map/finish_q/pallas_call | solution.py:41
  51.0 2.1 %collective-permute-done.25.refs_1_ = bf16[64,256]{1,0:T(8,128)(2,1)S(1)} collective-permute-done((bf16[64,256]{1,0:T(8,128)(2,1)S(1)}, bf16[64,256]{1,0:T(8,128)(2,1)S(1)}, u32[]{:S(2)}, u32[]{:S(2)}) %collective-permute-start.25) | collective-permute-done | bytes 32800 | tf_op jit(solution)/shard_map/ppermute | solution.py:26
  53.1 0.6 %finish_kv.1 = (bf16[64,256]{1,0:T(8,128)(2,1)}, bf16[64,256]{1,0:T(8,128)(2,1)}) custom-call(s32[1]{0:T(128)} %bitcast.group_ref, bf16[64,256]{1,0:T(8,128)(2,1)S(1)} %get-tuple-element.108.refs_0_, bf16[64,256]{1,0:T(8,128)(2,1)S(1)} %collective-permute-done.25.refs_1_), custom_call_target="tpu_custom_call" | custom-call | bytes 131076 | tf_op jit(solution)/shard_map/finish_kv/pallas_call | solution.py:41
  (34 shorter events, 0.4 us)
Async XLA Ops:
  0.6 6.5 %collective-permute-start.1 = (bf16[64,256]{1,0:T(8,128)(2,1)}, bf16[64,256]{1,0:T(8,128)(2,1)S(1)}, u32[]{:S(2)}, u32[]{:S(2)}) collective-permute-start(bf16[64,256]{1,0:T(8,128)(2,1)} %bitcast.17), channel_id=1, source_target_pairs={{0,8},{8,0},{16,24},{24,16},{1,9},{9,1},{17,25},{25,17},{2,10},{10... | collective-permute-start | bytes 98312 | tf_op jit(solution)/shard_map/ppermute | solution.py:26
  3.6 4.1 %collective-permute-start.2 = (bf16[64,256]{1,0:T(8,128)(2,1)}, bf16[64,256]{1,0:T(8,128)(2,1)S(1)}, u32[]{:S(2)}, u32[]{:S(2)}) collective-permute-start(bf16[64,256]{1,0:T(8,128)(2,1)} %bitcast.19), channel_id=1, source_target_pairs={{0,8},{8,0},{16,24},{24,16},{1,9},{9,1},{17,25},{25,17},{2,10},{10... | collective-permute-start | bytes 98312 | tf_op jit(solution)/shard_map/ppermute | solution.py:26
  5.2 0.9 %copy-start = (bf16[2,32,2048]{2,1,0:T(8,128)(2,1)S(1)}, bf16[2,32,2048]{2,1,0:T(8,128)(2,1)}, u32[]{:S(2)}) copy-start(bf16[2,32,2048]{2,1,0:T(8,128)(2,1)} %param.5) | copy-start | bytes 786436
  6.1 0.9 %copy-start.1 = (bf16[2,32,2048]{2,1,0:T(8,128)(2,1)S(1)}, bf16[2,32,2048]{2,1,0:T(8,128)(2,1)}, u32[]{:S(2)}) copy-start(bf16[2,32,2048]{2,1,0:T(8,128)(2,1)} %param.8) | copy-start | bytes 786436
  7.8 5.6 %collective-permute-start.5 = (bf16[2,64,256]{2,1,0:T(8,128)(2,1)S(1)}, bf16[2,64,256]{2,1,0:T(8,128)(2,1)S(1)}, u32[]{:S(2)}, u32[]{:S(2)}) collective-permute-start(bf16[2,64,256]{2,1,0:T(8,128)(2,1)S(1)} %pack_kv.1.refs_0_), channel_id=1, source_target_pairs={{0,2},{1,3},{2,0},{3,1},{4,6},{5,7},{6,4},{7,5},{8,10},{9,11},{10,... | collective-permute-start | bytes 196616 | tf_op jit(solution)/shard_map/ppermute | solution.py:26
  9.4 12.5 %collective-permute-start = (bf16[2,64,1024]{2,1,0:T(8,128)(2,1)S(1)}, bf16[2,64,1024]{2,1,0:T(8,128)(2,1)S(1)}, u32[]{:S(2)}, u32[]{:S(2)}) collective-permute-start(bf16[2,64,1024]{2,1,0:T(8,128)(2,1)S(1)} %get-tuple-element.59), channel_id=1, source_target_pairs={{0,8},{8,0},{16,24},{24,16},{1,9},{9,1},{17,25},{25,17},{2,10},{10... | collective-permute-start | bytes 786440 | tf_op jit(solution)/shard_map/ppermute | solution.py:26
  10.7 6.1 %collective-permute-start.4 = (bf16[2,64,256]{2,1,0:T(8,128)(2,1)S(1)}, bf16[2,64,256]{2,1,0:T(8,128)(2,1)S(1)}, u32[]{:S(2)}, u32[]{:S(2)}) collective-permute-start(bf16[2,64,256]{2,1,0:T(8,128)(2,1)S(1)} %pack_kv.1.refs_0_), channel_id=1, source_target_pairs={{0,6},{1,7},{2,4},{3,5},{4,2},{5,3},{6,0},{7,1},{8,14},{9,15},{10,... | collective-permute-start | bytes 196616 | tf_op jit(solution)/shard_map/ppermute | solution.py:26
  13.2 5.9 %collective-permute-start.3 = (bf16[2,64,256]{2,1,0:T(8,128)(2,1)S(1)}, bf16[2,64,256]{2,1,0:T(8,128)(2,1)S(1)}, u32[]{:S(2)}, u32[]{:S(2)}) collective-permute-start(bf16[2,64,256]{2,1,0:T(8,128)(2,1)S(1)} %pack_kv.1.refs_0_), channel_id=1, source_target_pairs={{0,4},{1,5},{2,6},{3,7},{4,0},{5,1},{6,2},{7,3},{8,12},{9,13},{10,... | collective-permute-start | bytes 196616 | tf_op jit(solution)/shard_map/ppermute | solution.py:26
  13.3 8.6 %collective-permute-start.9 = (bf16[2,2,64,256]{3,2,1,0:T(8,128)(2,1)S(1)}, bf16[2,2,64,256]{3,2,1,0:T(8,128)(2,1)S(1)}, u32[]{:S(2)}, u32[]{:S(2)}) collective-permute-start(bf16[2,2,64,256]{3,2,1,0:T(8,128)(2,1)S(1)} %stack.10.refs_2_.refs_1_), channel_id=1, source_target_pairs={{0,16},{8,24},{16,0},{24,8},{1,17},{9,25},{17,1},{25,9},{2,18},{10... | collective-permute-start | bytes 393224 | tf_op jit(solution)/shard_map/ppermute | solution.py:26
  14.9 4.1 %collective-permute-start.6 = (bf16[64,128]{1,0:T(8,128)(2,1)S(1)}, bf16[64,128]{1,0:T(8,128)(2,1)S(1)}, u32[]{:S(2)}, u32[]{:S(2)}) collective-permute-start(bf16[64,128]{1,0:T(8,128)(2,1)S(1)} %slice_bitcast_fusion.1), channel_id=1, source_target_pairs={{0,1},{1,0},{2,3},{3,2},{4,5},{5,4},{6,7},{7,6},{8,9},{9,8},{10,11... | collective-permute-start | bytes 49160 | tf_op jit(solution)/shard_map/ppermute | solution.py:26
  19.1 6.9 %collective-permute-start.10 = (bf16[2,2,64,256]{3,2,1,0:T(8,128)(2,1)S(1)}, bf16[2,2,64,256]{3,2,1,0:T(8,128)(2,1)S(1)}, u32[]{:S(2)}, u32[]{:S(2)}) collective-permute-start(bf16[2,2,64,256]{3,2,1,0:T(8,128)(2,1)S(1)} %get-tuple-element.65.refs_0_), channel_id=1, source_target_pairs={{0,16},{8,24},{16,0},{24,8},{1,17},{9,25},{17,1},{25,9},{2,18},{10... | collective-permute-start | bytes 393224 | tf_op jit(solution)/shard_map/ppermute | solution.py:26
  20.7 2.8 %collective-permute-start.7 = (bf16[2,2,64,256]{3,2,1,0:T(8,128)(2,1)S(1)}, bf16[2,2,64,256]{3,2,1,0:T(8,128)(2,1)S(1)}, u32[]{:S(2)}, u32[]{:S(2)}) collective-permute-start(bf16[2,2,64,256]{3,2,1,0:T(8,128)(2,1)S(1)} %get-tuple-element.65.refs_0_), channel_id=1, source_target_pairs={{0,1},{1,0},{2,3},{3,2},{4,5},{5,4},{6,7},{7,6},{8,9},{9,8},{10,11... | collective-permute-start | bytes 393224 | tf_op jit(solution)/shard_map/ppermute | solution.py:26
  20.7 2.7 %collective-permute-start.8 = (bf16[2,2,64,256]{3,2,1,0:T(8,128)(2,1)S(1)}, bf16[2,2,64,256]{3,2,1,0:T(8,128)(2,1)S(1)}, u32[]{:S(2)}, u32[]{:S(2)}) collective-permute-start(bf16[2,2,64,256]{3,2,1,0:T(8,128)(2,1)S(1)} %get-tuple-element.66), channel_id=1, source_target_pairs={{0,1},{1,0},{2,3},{3,2},{4,5},{5,4},{6,7},{7,6},{8,9},{9,8},{10,11... | collective-permute-start | bytes 393224 | tf_op jit(solution)/shard_map/ppermute | solution.py:26
  21.9 5.9 %collective-permute-start.12 = (bf16[2,2,64,256]{3,2,1,0:T(8,128)(2,1)S(1)}, bf16[2,2,64,256]{3,2,1,0:T(8,128)(2,1)S(1)}, u32[]{:S(2)}, u32[]{:S(2)}) collective-permute-start(bf16[2,2,64,256]{3,2,1,0:T(8,128)(2,1)S(1)} %collective-permute-done.9.refs_0_), channel_id=1, source_target_pairs={{0,1},{1,0},{2,3},{3,2},{4,5},{5,4},{6,7},{7,6},{8,9},{9,8},{10,11... | collective-permute-start | bytes 393224 | tf_op jit(solution)/shard_map/ppermute | solution.py:26
  26.0 1.8 %collective-permute-start.11 = (bf16[2,2,64,256]{3,2,1,0:T(8,128)(2,1)S(1)}, bf16[2,2,64,256]{3,2,1,0:T(8,128)(2,1)S(1)}, u32[]{:S(2)}, u32[]{:S(2)}) collective-permute-start(bf16[2,2,64,256]{3,2,1,0:T(8,128)(2,1)S(1)} %collective-permute-done.10.refs_0_), channel_id=1, source_target_pairs={{0,1},{1,0},{2,3},{3,2},{4,5},{5,4},{6,7},{7,6},{8,9},{9,8},{10,11... | collective-permute-start | bytes 393224 | tf_op jit(solution)/shard_map/ppermute | solution.py:26
  31.1 1.9 %collective-permute-start.15 = (bf16[2,2,64,256]{3,2,1,0:T(8,128)(2,1)S(1)}, bf16[2,2,64,256]{3,2,1,0:T(8,128)(2,1)S(1)}, u32[]{:S(2)}, u32[]{:S(2)}) collective-permute-start(bf16[2,2,64,256]{3,2,1,0:T(8,128)(2,1)S(1)} %get-tuple-element.92), channel_id=1, source_target_pairs={{0,1},{1,0},{2,3},{3,2},{4,5},{5,4},{6,7},{7,6},{8,9},{9,8},{10,11... | collective-permute-start | bytes 393224 | tf_op jit(solution)/shard_map/ppermute | solution.py:26
  31.2 1.8 %collective-permute-start.14 = (bf16[2,2,64,256]{3,2,1,0:T(8,128)(2,1)S(1)}, bf16[2,2,64,256]{3,2,1,0:T(8,128)(2,1)S(1)}, u32[]{:S(2)}, u32[]{:S(2)}) collective-permute-start(bf16[2,2,64,256]{3,2,1,0:T(8,128)(2,1)S(1)} %get-tuple-element.90), channel_id=1, source_target_pairs={{0,1},{1,0},{2,3},{3,2},{4,5},{5,4},{6,7},{7,6},{8,9},{9,8},{10,11... | collective-permute-start | bytes 393224 | tf_op jit(solution)/shard_map/ppermute | solution.py:26
  33.1 1.2 %collective-permute-start.16 = (bf16[64,128]{1,0:T(8,128)(2,1)S(1)}, bf16[64,128]{1,0:T(8,128)(2,1)S(1)}, u32[]{:S(2)}, u32[]{:S(2)}) collective-permute-start(bf16[64,128]{1,0:T(8,128)(2,1)S(1)} %slice_bitcast_fusion), channel_id=1, source_target_pairs={{0,1},{1,0},{2,3},{3,2},{4,5},{5,4},{6,7},{7,6},{8,9},{9,8},{10,11... | collective-permute-start | bytes 49160 | tf_op jit(solution)/shard_map/ppermute | solution.py:26
  33.2 6.2 %collective-permute-start.18 = (bf16[2,2,64,256]{3,2,1,0:T(8,128)(2,1)S(1)}, bf16[2,2,64,256]{3,2,1,0:T(8,128)(2,1)S(1)}, u32[]{:S(2)}, u32[]{:S(2)}) collective-permute-start(bf16[2,2,64,256]{3,2,1,0:T(8,128)(2,1)S(1)} %sum_cores.3), channel_id=1, source_target_pairs={{0,16},{8,24},{16,0},{24,8},{1,17},{9,25},{17,1},{25,9},{2,18},{10... | collective-permute-start | bytes 393224 | tf_op jit(solution)/shard_map/ppermute | solution.py:26
  35.5 4.7 %collective-permute-start.19 = (bf16[2,2,64,256]{3,2,1,0:T(8,128)(2,1)S(1)}, bf16[2,2,64,256]{3,2,1,0:T(8,128)(2,1)S(1)}, u32[]{:S(2)}, u32[]{:S(2)}) collective-permute-start(bf16[2,2,64,256]{3,2,1,0:T(8,128)(2,1)S(1)} %get-tuple-element.100), channel_id=1, source_target_pairs={{0,1},{1,0},{2,3},{3,2},{4,5},{5,4},{6,7},{7,6},{8,9},{9,8},{10,11... | collective-permute-start | bytes 393224 | tf_op jit(solution)/shard_map/ppermute | solution.py:26
  35.7 6.2 %collective-permute-start.22 = (bf16[2,2,64,256]{3,2,1,0:T(8,128)(2,1)S(1)}, bf16[2,2,64,256]{3,2,1,0:T(8,128)(2,1)S(1)}, u32[]{:S(2)}, u32[]{:S(2)}) collective-permute-start(bf16[2,2,64,256]{3,2,1,0:T(8,128)(2,1)S(1)} %sum_cores.2), channel_id=1, source_target_pairs={{0,16},{8,24},{16,0},{24,8},{1,17},{9,25},{17,1},{25,9},{2,18},{10... | collective-permute-start | bytes 393224 | tf_op jit(solution)/shard_map/ppermute | solution.py:26
  36.6 7.4 %collective-permute-start.23 = (bf16[2,2,64,256]{3,2,1,0:T(8,128)(2,1)S(1)}, bf16[2,2,64,256]{3,2,1,0:T(8,128)(2,1)S(1)}, u32[]{:S(2)}, u32[]{:S(2)}) collective-permute-start(bf16[2,2,64,256]{3,2,1,0:T(8,128)(2,1)S(1)} %get-tuple-element.104), channel_id=1, source_target_pairs={{0,1},{1,0},{2,3},{3,2},{4,5},{5,4},{6,7},{7,6},{8,9},{9,8},{10,11... | collective-permute-start | bytes 393224 | tf_op jit(solution)/shard_map/ppermute | solution.py:26
  36.7 13.5 %collective-permute-start.13 = (bf16[64,1024]{1,0:T(8,128)(2,1)S(1)}, bf16[64,1024]{1,0:T(8,128)(2,1)S(1)}, u32[]{:S(2)}, u32[]{:S(2)}) collective-permute-start(bf16[64,1024]{1,0:T(8,128)(2,1)S(1)} %get-tuple-element.78), channel_id=1, source_target_pairs={{0,8},{8,0},{16,24},{24,16},{1,9},{9,1},{17,25},{25,17},{2,10},{10... | collective-permute-start | bytes 393224 | tf_op jit(solution)/shard_map/ppermute | solution.py:26
  39.4 10.8 %collective-permute-start.17 = (bf16[64,1024]{1,0:T(8,128)(2,1)S(1)}, bf16[64,1024]{1,0:T(8,128)(2,1)S(1)}, u32[]{:S(2)}, u32[]{:S(2)}) collective-permute-start(bf16[64,1024]{1,0:T(8,128)(2,1)S(1)} %get-tuple-element.97), channel_id=1, source_target_pairs={{0,8},{8,0},{16,24},{24,16},{1,9},{9,1},{17,25},{25,17},{2,10},{10... | collective-permute-start | bytes 393224 | tf_op jit(solution)/shard_map/ppermute | solution.py:26
  40.2 7.0 %collective-permute-start.20 = (bf16[2,64,256]{2,1,0:T(8,128)(2,1)S(1)}, bf16[2,64,256]{2,1,0:T(8,128)(2,1)S(1)}, u32[]{:S(2)}, u32[]{:S(2)}) collective-permute-start(bf16[2,64,256]{2,1,0:T(8,128)(2,1)S(1)} %get-tuple-element.102), channel_id=1, source_target_pairs={{0,4},{1,5},{2,6},{3,7},{4,0},{5,1},{6,2},{7,3},{8,12},{9,13},{10,... | collective-permute-start | bytes 196616 | tf_op jit(solution)/shard_map/ppermute | solution.py:26
  41.9 6.3 %collective-permute-start.21 = (bf16[2,64,256]{2,1,0:T(8,128)(2,1)S(1)}, bf16[2,64,256]{2,1,0:T(8,128)(2,1)S(1)}, u32[]{:S(2)}, u32[]{:S(2)}) collective-permute-start(bf16[2,64,256]{2,1,0:T(8,128)(2,1)S(1)} %get-tuple-element.103), channel_id=1, source_target_pairs={{0,6},{1,7},{2,4},{3,5},{4,2},{5,3},{6,0},{7,1},{8,14},{9,15},{10,... | collective-permute-start | bytes 196616 | tf_op jit(solution)/shard_map/ppermute | solution.py:26
  44.1 5.0 %collective-permute-start.24 = (bf16[2,64,256]{2,1,0:T(8,128)(2,1)S(1)}, bf16[2,64,256]{2,1,0:T(8,128)(2,1)S(1)}, u32[]{:S(2)}, u32[]{:S(2)}) collective-permute-start(bf16[2,64,256]{2,1,0:T(8,128)(2,1)S(1)} %get-tuple-element.107), channel_id=1, source_target_pairs={{0,2},{1,3},{2,0},{3,1},{4,6},{5,7},{6,4},{7,5},{8,10},{9,11},{10,... | collective-permute-start | bytes 196616 | tf_op jit(solution)/shard_map/ppermute | solution.py:26
  49.1 4.0 %collective-permute-start.25 = (bf16[64,256]{1,0:T(8,128)(2,1)S(1)}, bf16[64,256]{1,0:T(8,128)(2,1)S(1)}, u32[]{:S(2)}, u32[]{:S(2)}) collective-permute-start(bf16[64,256]{1,0:T(8,128)(2,1)S(1)} %get-tuple-element.109), channel_id=1, source_target_pairs={{0,8},{8,0},{16,24},{24,16},{1,9},{9,1},{17,25},{25,17},{2,10},{10... | collective-permute-start | bytes 98312 | tf_op jit(solution)/shard_map/ppermute | solution.py:26

commit v9 on v8

--- a/solution.py
+++ b/solution.py
@@ -86,13 +86,8 @@
 
 
 def stack_kernel(count, *refs):
-    ins, refs = refs[:count], refs[count:]
-    passed = len(refs) // 2
-    refs, out_ref = refs[:-1], refs[-1]
-    for i, ref in enumerate(ins):
-        out_ref[i] = ref[...]
-    if passed:
-        refs[-1][...] = refs[0][...]
+    for i, ref in enumerate(refs[:count]):
+        refs[-1][i] = ref[...]
 
 
 class Plan:
@@ -219,12 +214,11 @@
 
 
 def far_kernel(plan, chunks, others, info_ref, q_all, do_all, q_t, do_t, *refs):
-    kv, count = plan.kv, len(chunks)
+    count = len(chunks)
     partial, refs = [refs[3 * i : 3 * i + 3] for i in range(others)], refs[3 * others :]
     kv_refs, refs = refs[:count], refs[count:]
-    att_refs, refs = refs[:kv], refs[kv:]
-    scale_refs, (delta_ref, q_grad_ref), refs = refs[:others], refs[others : others + 2], refs[others + 2 :]
-    dkv_refs, (turned_ref, e_ref, w_ref, p_ref, ds_ref) = refs[:-5], refs[-5:]
+    scale_refs, (delta_ref, mixed_ref, ds_ref), refs = refs[:others], refs[others : others + 3], refs[others + 3 :]
+    dkv_refs, (turned_ref, e_ref, w_ref, p_ref) = refs[:-4], refs[-4:]
     spans = [plan.at(tile) for tile in range(len(plan.tiles))]
     tops = [
         plan.scores(tile, chunks, kv_refs, q_t[:, at], e_ref, at, info_ref)
@@ -234,7 +228,7 @@
     for at in spans:
         for i, ref in enumerate(kv_refs):
             w_ref[plan.keys_at(i), at] = dot(plan.values(ref), do_t[:, at])
-    inverses, mixes = [], []
+    inverses = []
     for at, top in zip(spans, tops):
         for top_ref, _, _ in partial:
             top = jnp.maximum(top, top_ref[:, at])
@@ -254,38 +248,44 @@
             probs = (e_ref[plan.keys_at(i), at] * inverse).astype(BF)
             p_ref[plan.keys_at(i), at] = probs
             mixed = mixed + dot(turned_ref[pl.ds(HD, HD), plan.keys_at(i)], probs)
-        mixes.append(mixed.astype(BF).astype(F32))
-    for at, mixed in zip(spans, mixes):
-        delta_ref[:, at] = jnp.sum(do_t[:, at].astype(F32) * mixed, axis=0, keepdims=True)
+        mixed = mixed.astype(BF)
+        mixed_ref[:, at] = mixed
+        delta_ref[:, at] = jnp.sum(do_t[:, at].astype(F32) * mixed.astype(F32), axis=0, keepdims=True)
     for at, inverse in zip(spans, inverses):
-        q_grad = jnp.zeros((HD, plan.lanes), F32)
         for i in range(count):
             probs = e_ref[plan.keys_at(i), at] * inverse
-            grad_s = (probs * (w_ref[plan.keys_at(i), at] - delta_ref[:, at])).astype(BF)
-            ds_ref[plan.keys_at(i), at] = grad_s
-            q_grad = q_grad + dot(turned_ref[pl.ds(0, HD), plan.keys_at(i)], grad_s)
-        q_grad_ref[:, at] = q_grad
+            ds_ref[plan.keys_at(i), at] = (probs * (w_ref[plan.keys_at(i), at] - delta_ref[:, at])).astype(BF)
     plan.back(dkv_refs, p_ref, ds_ref, q_all, do_all)
-    for tile, mixed in enumerate(mixes):
-        plan.store_heads(att_refs[plan.tiles[tile][0]], tile, mixed)
-
-
-def back_kernel(plan, rows_at, last, order, q_all, do_all, do_t, e_ref, scale_ref, delta_ref, q_grad_in, *refs):
-    count = len(rows_at)
+
+
+def tail_kernel(plan, order, mixed_ref, ds_ref, q_grad_in, *refs):
+    ins, (*att_refs, q_grad_ref, turned_ref) = refs[: -plan.kv - 2], refs[-plan.kv - 2 :]
+    plan.turn(ins[: len(ins) - order], turned_ref)
+    for tile, (s, _) in enumerate(plan.tiles):
+        at = plan.at(tile)
+        q_grad_ref[:, at] = q_grad_in[:, at] + dot(turned_ref[pl.ds(0, HD), :], ds_ref[:, at])
+        plan.store_heads(att_refs[s], tile, mixed_ref[:, at].astype(F32))
+
+
+def back_kernel(plan, units, last, order, follows, groups, q_all, do_all, do_t, delta_ref, *refs):
+    count = len(units)
+    e_refs, scale_refs, refs = refs[:groups], refs[groups : 2 * groups], refs[2 * groups :]
+    q_grad_in, refs = refs[:follows], refs[follows:]
     kv_refs, refs = refs[:count], refs[count + order :]
     refs, (turned_ref, p_ref, ds_ref) = refs[:-3], refs[-3:]
     outs, dkv_refs = refs[:-count], refs[-count:]
     spans = [plan.at(tile) for tile in range(len(plan.tiles))]
     for at in spans:
         for i, ref in enumerate(kv_refs):
-            probs = e_ref[plan.keys_at(rows_at[i]), at] * scale_ref[:, at]
+            group, row = units[i]
+            probs = e_refs[group][plan.keys_at(row), at] * scale_refs[group][:, at]
             p_ref[plan.keys_at(i), at] = probs.astype(BF)
             grad_s = (probs * (dot(plan.values(ref), do_t[:, at]) - delta_ref[:, at])).astype(BF)
             ds_ref[plan.keys_at(i), at] = grad_s
     plan.turn(kv_refs, turned_ref)
     plan.back(dkv_refs, p_ref, ds_ref, q_all, do_all)
     for tile, at in enumerate(spans):
-        q_grad = q_grad_in[:, at]
+        q_grad = q_grad_in[0][:, at] if follows else jnp.zeros((HD, plan.lanes), F32)
         for i in range(count):
             q_grad = q_grad + dot(turned_ref[pl.ds(0, HD), plan.keys_at(i)], ds_ref[plan.keys_at(i), at])
         if last:
@@ -316,6 +316,13 @@
         for ref in ins[1:]:
             total = total + ref[s].astype(F32)
         out_ref[...] = total.astype(BF)
+
+
+def sum_far_kernel(*refs):
+    total = refs[0][...].astype(F32)
+    for ref in refs[1:-1]:
+        total = total + ref[...].astype(F32)
+    refs[-1][...] = total
 
 
 def finish_kv_kernel(kv, group_ref, *refs):
@@ -400,25 +407,7 @@
     pieces = [swap(piece, "ctx", m * cores) for m in reversed(range(1, z_devices))]
     pieces = [piece] + pieces[::-1]
     q_parts = with_swaps(q_parts)
-    column, handed, order = [None] * parts, [None] * parts, []
-    for p in reversed(range(parts)):
-        parcels = [pieces[m] for m in plan.zone(p)]
-        extra = [column[p + 1], *order] if order else []
-        *handed_on, column[p] = call(
-            functools.partial(stack_kernel, len(parcels)),
-            "stack",
-            (*parcels, *extra),
-            [dkv] * (1 + bool(extra)),
-        )
-        handed[p] = column[p]
-        if extra:
-            handed[p + 1] = handed_on[0]
-        order = [swap(column[p][0, 0, :, :HD], "ctx", 1)] if cores > 1 and p else []
-    columns = [[swap(half, "head", a * kv) for half in column] for a in range(1, spans)]
-    near_kv = [column] + [[swap(half, "ctx", core) for half in handed] for core in range(1, cores)]
-    near_flat = [half for pair in near_kv for half in pair]
     each = range(parts)
-    near_chunks = [(0, core, p) for core in range(cores) for p in each]
     mid_chunks = [(a, 0, p) for a in range(1, spans) for p in each]
     far_chunks = [(a, core, p) for a in range(1, spans) for core in range(1, cores) for p in each]
 
@@ -433,7 +422,7 @@
         [bf(query_rows, HD)] * 2 + [bf(HD, query_rows)] * 2,
     )
 
-    def forward(name, chunks, kv_refs, order):
+    def forward(name, chunks, kv_refs, order, flops=8):
         size = len(chunks) * keys
         return call(
             functools.partial(part_kernel, plan, chunks),
@@ -443,47 +432,59 @@
             [SMEM] + [VMEM] * (1 + len(kv_refs) + len(order)),
             [pltpu.VMEM((2 * HD, size), BF)],
             size * 4 * HD,
-            8 * size * query_rows * HD,
+            flops * size * query_rows * HD,
         )
 
-    mids, order = [None] * parts, []
+    nears, mids, near_kv, order = [None] * parts, [None] * parts, [None] * parts, []
+    columns = [[None] * parts for _ in range(1, spans)]
+
+    def mid(p, order):
+        chunks = [chunk for chunk in mid_chunks if chunk[2] == p]
+        return forward("attend_mid", chunks, [pair[p] for pair in columns], order)
+
     for p in reversed(each):
-        if p + 1 < parts or parts == 1:
-            near_e, *near = forward("attend_near", near_chunks, near_flat, order)
-            order = [near[0]]
-            for pair in columns:
-                pair[p] = after([pair[p]], order)[0]
-        mids[p] = forward("attend_mid", [c for c in mid_chunks if c[2] == p], [pair[p] for pair in columns], order)
-        order = [mids[p][1]]
+        parcels = [pieces[m] for m in plan.zone(p)]
+        part = call(functools.partial(stack_kernel, len(parcels)), "stack", (*parcels, *order), [dkv])[0]
+        for a in range(1, spans):
+            columns[a - 1][p] = swap(part, "head", a * kv)
+        near_kv[p] = [part] + [swap(part, "ctx", core) for core in range(1, cores)]
+        if p + 1 < parts:
+            mids[p + 1] = mid(p + 1, order)
+            order = [mids[p + 1][1]]
+        chunks = [(0, core, p) for core in range(cores)]
+        nears[p] = forward("attend_near", chunks, near_kv[p], order, 0 if p else 8)
+        order = [nears[p][1]]
+    for pair in columns:
+        pair[0] = after([pair[0]], order)[0]
+    mids[0] = mid(0, order)
+    partials = nears + mids
     far_kv = [swap(pair[p], "ctx", core) for pair in columns for core in range(1, cores) for p in each]
     far_keys = len(far_kv) * keys
     outs = call(
-        functools.partial(far_kernel, plan, far_chunks, 1 + parts),
+        functools.partial(far_kernel, plan, far_chunks, len(partials)),
         "attend_far",
-        (info, q_all, do_all, q_t, do_t, *near, *[r for mid in mids for r in mid[1:]], *far_kv),
-        [bf(rows, width)] * kv + [row] * (2 + parts) + [column_out] + [dkv] * len(far_kv),
-        [SMEM] + [VMEM] * (7 + 3 * parts + len(far_kv)),
+        (info, q_all, do_all, q_t, do_t, *[ref for part in partials for ref in part[1:]], *far_kv),
+        [row] * (len(partials) + 1) + [bf(HD, query_rows), bf(far_keys, query_rows)] + [dkv] * len(far_kv),
+        [SMEM] + [VMEM] * (4 + 3 * len(partials) + len(far_kv)),
         [
             pltpu.VMEM((2 * HD, far_keys), BF),
             pltpu.VMEM((far_keys, query_rows), F32),
             pltpu.VMEM((far_keys, query_rows), F32),
             pltpu.VMEM((far_keys, query_rows), BF),
-            pltpu.VMEM((far_keys, query_rows), BF),
         ],
         far_keys * (4 * HD + 12 * query_rows),
         16 * far_keys * query_rows * HD,
     )
-    att_parts, outs = outs[:kv], outs[kv:]
-    (near_scale, *mid_scales), outs = outs[: 1 + parts], outs[1 + parts :]
-    (delta, q_grad), far_dkv = outs[:2], outs[2:]
-
-    def back(rows_at, last, e, scale, q_grad, kv_refs, order):
-        count = len(rows_at)
+    scales, (delta, mixed, far_ds, *far_dkv) = outs[: len(partials)], outs[len(partials) :]
+
+    def back(units, last, parts_of, follows, kv_refs, order):
+        count = len(units)
         q_outs = [bf(rows, width)] * kv if last else [column_out]
+        es, of_scales = [partials[i][0] for i in parts_of], [scales[i] for i in parts_of]
         outs = call(
-            functools.partial(back_kernel, plan, rows_at, last, len(order)),
+            functools.partial(back_kernel, plan, units, last, len(order), len(follows), len(parts_of)),
             "attend_back",
-            (q_all, do_all, do_t, e, scale, delta, q_grad, *kv_refs, *order),
+            (q_all, do_all, do_t, delta, *es, *of_scales, *follows, *kv_refs, *order),
             q_outs + [dkv] * count,
             None,
             [
@@ -497,12 +498,11 @@
         return outs[: len(q_outs)], outs[len(q_outs) :]
 
     sums = [[] for _ in range(parts)]
-    totals = []
+    totals, follows = [], []
     for p in reversed(each):
         mid_kv = [pair[p] for pair in columns]
-        (q_grad,), mid_dkv = back(
-            list(range(len(mid_kv))), False, mids[p][0], mid_scales[p], q_grad, mid_kv, []
-        )
+        units = [(0, i) for i in range(len(mid_kv))]
+        follows, mid_dkv = back(units, False, [parts + p], follows, mid_kv, [])
         for a in range(spans - 1):
             both = [mid_dkv[a]]
             for core in range(1, cores):
@@ -511,14 +511,24 @@
             totals += call(add_kernel, "sum_cores", after(both, totals[-1:]), [dkv])
             sums[p].append(swap(totals[-1], "head", (a + 1) * kv))
     order = [swap(totals[-1][0, 0, :, :HD], "ctx", 1)] if cores > 1 else []
+    *att_parts, q_grad = call(
+        functools.partial(tail_kernel, plan, len(order)),
+        "attend_tail",
+        (mixed, far_ds, *follows, *far_kv, *order),
+        [bf(rows, width)] * kv + [column_out],
+        None,
+        [pltpu.VMEM((2 * HD, far_keys), BF)],
+        far_keys * 4 * HD,
+        2 * far_keys * query_rows * HD,
+    )
+    follows = [q_grad]
     for core in reversed(range(cores)):
-        outs, parts_dkv = back(
-            [core * parts + p for p in each], core == 0, near_e, near_scale, q_grad, near_kv[core], order
-        )
-        q_grad = outs[0]
-        for p in range(parts):
+        units = [(p, core) for p in each]
+        kv_refs = [near_kv[p][core] for p in each]
+        follows, parts_dkv = back(units, core == 0, list(each), follows, kv_refs, order)
+        for p in each:
             sums[p].append(swap(parts_dkv[p], "ctx", core) if core else parts_dkv[p])
-    q_grad_parts = outs[:kv]
+    q_grad_parts = follows
     z_parts = [None] * z_devices
     for p in range(parts):
         totals = call(
@@ -530,7 +540,10 @@
 
         for m, total in zip(plan.zone(p), totals):
             z_parts[m] = swap(total, "ctx", m * cores) if m else total
-    ordered = [z_parts[m] for p in range(parts) for m in plan.zone(p)]
+    ordered = [z_parts[m] for p in each for m in plan.zone(p)]
+    if parts > 1:
+        far_z = call(sum_far_kernel, "sum_far_z", ordered[:z_part], [f32(kv, rows, 2 * HD)])
+        ordered = [*far_z, *ordered[z_part:]]
     pair_parts = call(
         functools.partial(sum_z_kernel, kv), "sum_z", ordered, [bf(rows, 2 * HD)] * kv
     )

time: 54.1 us -> 58 us (1.072)
  starting transfers between devices: 20.5 us -> 23.8 us
  Pallas kernels: 13.9 us -> 15.1 us
  waiting for transfers between devices: 14.4 us -> 13.8 us
    ppermute x26 -> x25, starting transfers between devices: 20.5 us -> 23.8 us  [swap(): return lax.ppermute(block, axis, [(i, i ^ mask) for i in range(size)])]
    pallas_call x20 -> x23, Pallas kernels: 13.9 us -> 15.1 us  [call(): pl.pallas_call(kernel, out_shape=list(outs), in_specs=specs or [VMEM] * l...]
    ppermute x26 -> x25, waiting for transfers between devices: 14.4 us -> 13.8 us  [swap(): return lax.ppermute(block, axis, [(i, i ^ mask) for i in range(size)])]
  transfers between devices with their start and end apart: 26 -> 25, of which waited for: 10 -> 8; matrix products, arithmetic and copies ran while one was open for 4% -> 4% of each run, Pallas kernels for 19% -> 19%
where the time goes in v9:
time: 58 us; the launch traced here: 57.7 us
  starting transfers between devices  23.8 us (41%)
  Pallas kernels  15.1 us (26%)
  waiting for transfers between devices  13.8 us (24%)
  local copies, waits for them, and re-layouts  3.34 us (6%)
  between operations  0.89 us (2%)
  other arithmetic  0.74 us (1%)
    ppermute x25, starting transfers between devices, swap(): return lax.ppermute(block, axis, [(i, i ^ mask) for i in range(size)])  23.8 us
    pallas_call x23, Pallas kernels, call(): pl.pallas_call(kernel, out_shape=list(outs), in_specs=specs or [VMEM] * l...  15.1 us
    ppermute x25, waiting for transfers between devices, swap(): return lax.ppermute(block, axis, [(i, i ^ mask) for i in range(size)])  13.8 us
    unnamed x4, local copies, waits for them, and re-layouts  1.9 us
    dynamic_slice x2, local copies, waits for them, and re-layouts, shards(): lax.dynamic_slice_in_dim(block, mine, HD, 1)  1.44 us
  transfers between devices with their start and end apart: 25, of which 8 were waited for; matrix products, arithmetic and copies ran while one was open for 4% of the time, Pallas kernels for 19%

profile of v9, /device:TPU:0, one launch (start us, length us, event | category | flops | bytes accessed | tf_op | source)
XLA Modules:
  0.0 57.7 jit_solution(16036122510883255506)
XLA Ops:
  0.6 3.0 %collective-permute-start.1 = (bf16[64,256]{1,0:T(8,128)(2,1)}, bf16[64,256]{1,0:T(8,128)(2,1)S(1)}, u32[]{:S(2)}, u32[]{:S(2)}) collective-permute-start(bf16[64,256]{1,0:T(8,128)(2,1)} %bitcast.15), channel_id=1, source_target_pairs={{0,8},{8,0},{16,24},{24,16},{1,9},{9,1},{17,25},{25,17},{2,10},{10... | collective-permute-start | bytes 98312 | tf_op jit(solution)/shard_map/ppermute | solution.py:26
  3.6 0.1 collective-permute-start.2
  3.7 0.9 %copy-done = bf16[2,32,2048]{2,1,0:T(8,128)(2,1)S(1)} copy-done((bf16[2,32,2048]{2,1,0:T(8,128)(2,1)S(1)}, bf16[2,32,2048]{2,1,0:T(8,128)(2,1)}, u32[]{:S(2)}) %copy-start) | copy-done | bytes 262168
  4.7 0.9 %copy-done.1 = bf16[2,32,2048]{2,1,0:T(8,128)(2,1)S(1)} copy-done((bf16[2,32,2048]{2,1,0:T(8,128)(2,1)S(1)}, bf16[2,32,2048]{2,1,0:T(8,128)(2,1)}, u32[]{:S(2)}) %copy-start.1) | copy-done | bytes 262168
  5.7 2.0 %collective-permute-start = (bf16[2,64,1024]{2,1,0:T(8,128)(2,1)S(1)}, bf16[2,64,1024]{2,1,0:T(8,128)(2,1)S(1)}, u32[]{:S(2)}, u32[]{:S(2)}) collective-permute-start(bf16[2,64,1024]{2,1,0:T(8,128)(2,1)S(1)} %get-tuple-element.64), channel_id=1, source_target_pairs={{0,8},{8,0},{16,24},{24,16},{1,9},{9,1},{17,25},{25,17},{2,10},{10... | collective-permute-start | bytes 786440 | tf_op jit(solution)/shard_map/ppermute | solution.py:26
  7.7 0.7 %constant_dynamic-slice_fusion.1 = bf16[64,128]{1,0:T(8,128)(2,1)S(1)} fusion(bf16[64,256]{1,0:T(8,128)(2,1)} %bitcast.16, s32[]{:T(128)S(6)} %select_n.14), kind=kLoop, calls=%fused_computation.4 | loop fusion | bytes 32772 | tf_op jit(solution)/shard_map/dynamic_slice | solution.py:390
  8.4 0.7 %constant_dynamic-slice_fusion = bf16[64,128]{1,0:T(8,128)(2,1)S(1)} fusion(bf16[64,256]{1,0:T(8,128)(2,1)} %bitcast.18, s32[]{:T(128)S(6)} %select_n.14), kind=kLoop, calls=%fused_computation.3 | loop fusion | bytes 32772 | tf_op jit(solution)/shard_map/dynamic_slice | solution.py:390
  9.2 1.6 %collective-permute-start.5 = (bf16[2,64,256]{2,1,0:T(8,128)(2,1)S(1)}, bf16[2,64,256]{2,1,0:T(8,128)(2,1)S(1)}, u32[]{:S(2)}, u32[]{:S(2)}) collective-permute-start(bf16[2,64,256]{2,1,0:T(8,128)(2,1)S(1)} %pack_kv.1.refs_0_), channel_id=1, source_target_pairs={{0,2},{1,3},{2,0},{3,1},{4,6},{5,7},{6,4},{7,5},{8,10},{9,11},{10,... | collective-permute-start | bytes 196616 | tf_op jit(solution)/shard_map/ppermute | solution.py:26
  10.8 2.7 %collective-permute-done.5.refs_1_ = bf16[2,64,256]{2,1,0:T(8,128)(2,1)S(1)} collective-permute-done((bf16[2,64,256]{2,1,0:T(8,128)(2,1)S(1)}, bf16[2,64,256]{2,1,0:T(8,128)(2,1)S(1)}, u32[]{:S(2)}, u32[]{:S(2)}) %collective-permute-start.5) | collective-permute-done | bytes 65568 | tf_op jit(solution)/shard_map/ppermute | solution.py:26
  13.5 0.1 collective-permute-start.6
  13.6 3.7 %collective-permute-start.4 = (bf16[2,64,256]{2,1,0:T(8,128)(2,1)S(1)}, bf16[2,64,256]{2,1,0:T(8,128)(2,1)S(1)}, u32[]{:S(2)}, u32[]{:S(2)}) collective-permute-start(bf16[2,64,256]{2,1,0:T(8,128)(2,1)S(1)} %pack_kv.1.refs_0_), channel_id=1, source_target_pairs={{0,6},{1,7},{2,4},{3,5},{4,2},{5,3},{6,0},{7,1},{8,14},{9,15},{10,... | collective-permute-start | bytes 196616 | tf_op jit(solution)/shard_map/ppermute | solution.py:26
  17.3 1.5 %collective-permute-start.8 = (bf16[2,2,64,256]{3,2,1,0:T(8,128)(2,1)S(1)}, bf16[2,2,64,256]{3,2,1,0:T(8,128)(2,1)S(1)}, u32[]{:S(2)}, u32[]{:S(2)}) collective-permute-start(bf16[2,2,64,256]{3,2,1,0:T(8,128)(2,1)S(1)} %stack.10.refs_0_.refs_6_), channel_id=1, source_target_pairs={{0,16},{8,24},{16,0},{24,8},{1,17},{9,25},{17,1},{25,9},{2,18},{10... | collective-permute-start | bytes 393224 | tf_op jit(solution)/shard_map/ppermute | solution.py:26
  18.8 0.7 %pad_add_fusion.info_ref = s32[18]{0:T(128)S(1)} fusion(s32[16]{0:T(128)} %param.9, s32[1]{0:T(128)} %bitcast.2, s32[1]{0:T(128)} %bitcast.1), kind=kLoop, calls=%fused_computation.2 | loop fusion | flops 36 | bytes 144 | tf_op jit(solution)/shard_map/concatenate | solution.py:368
  19.5 0.2 turn.1
  19.7 1.7 %attend_near.2 = (f32[512,1024]{1,0:T(8,128)S(1)}, f32[1,1024]{1,0:T(1,128)S(1)}, f32[1,1024]{1,0:T(1,128)S(1)}, f32[128,1024]{1,0:T(8,128)S(1)}) custom-call(s32[18]{0:T(128)S(1)} %pad_add_fusion.info_ref, bf16[128,1024]{1,0:T(8,128)(2,1)S(1)} %get-tuple-element.67.q_t, bf16[2,2,64,256]{3,2,1,0:T(8,128)(2,1)S(1)} %stack.10.refs_0_.refs_6_, ...), custom_call_target="tpu_custom_call" | custom-call | bytes 3153992 | tf_op jit(solution)/shard_map/attend_near/pallas_call | solution.py:41
  21.5 1.8 %collective-permute-done.3.refs_0_ = bf16[2,64,256]{2,1,0:T(8,128)(2,1)S(1)} collective-permute-done((bf16[2,64,256]{2,1,0:T(8,128)(2,1)S(1)}, bf16[2,64,256]{2,1,0:T(8,128)(2,1)S(1)}, u32[]{:S(2)}, u32[]{:S(2)}) %collective-permute-start.3) | collective-permute-done | bytes 65568 | tf_op jit(solution)/shard_map/ppermute | solution.py:26
  23.3 0.1 collective-permute-start.7
  23.4 1.6 %collective-permute-start.9 = (bf16[2,2,64,256]{3,2,1,0:T(8,128)(2,1)S(1)}, bf16[2,2,64,256]{3,2,1,0:T(8,128)(2,1)S(1)}, u32[]{:S(2)}, u32[]{:S(2)}) collective-permute-start(bf16[2,2,64,256]{3,2,1,0:T(8,128)(2,1)S(1)} %stack.11.refs_0_.refs_5_), channel_id=1, source_target_pairs={{0,16},{8,24},{16,0},{24,8},{1,17},{9,25},{17,1},{25,9},{2,18},{10... | collective-permute-start | bytes 393224 | tf_op jit(solution)/shard_map/ppermute | solution.py:26
  25.0 0.2 collective-permute-start.11
  25.2 1.3 %attend_mid.2 = (f32[256,1024]{1,0:T(8,128)S(1)}, f32[1,1024]{1,0:T(1,128)S(1)}, f32[1,1024]{1,0:T(1,128)S(1)}, f32[128,1024]{1,0:T(8,128)S(1)}) custom-call(s32[18]{0:T(128)S(1)} %pad_add_fusion.info_ref, bf16[128,1024]{1,0:T(8,128)(2,1)S(1)} %get-tuple-element.67.q_t, bf16[2,2,64,256]{3,2,1,0:T(8,128)(2,1)S(1)} %collective-permute-done.8.refs_0_.refs_2_, ...), custom_call_target="tpu_custom_call" | custom-call | flops 268435456 | bytes 1978440 | tf_op jit(solution)/shard_map/attend_mid/pallas_call | solution.py:41
  26.4 1.7 %attend_near.3 = (f32[512,1024]{1,0:T(8,128)S(1)}, f32[1,1024]{1,0:T(1,128)S(1)}, f32[1,1024]{1,0:T(1,128)S(1)}, f32[128,1024]{1,0:T(8,128)S(1)}) custom-call(s32[18]{0:T(128)S(1)} %pad_add_fusion.info_ref, bf16[128,1024]{1,0:T(8,128)(2,1)S(1)} %get-tuple-element.67.q_t, bf16[2,2,64,256]{3,2,1,0:T(8,128)(2,1)S(1)} %stack.11.refs_0_.refs_5_, ...), custom_call_target="tpu_custom_call" | custom-call | flops 536870912 | bytes 3158088 | tf_op jit(solution)/shard_map/attend_near/pallas_call | solution.py:41
  28.2 1.2 %collective-permute-done.9.refs_0_.refs_3_ = bf16[2,2,64,256]{3,2,1,0:T(8,128)(2,1)S(1)} collective-permute-done((bf16[2,2,64,256]{3,2,1,0:T(8,128)(2,1)S(1)}, bf16[2,2,64,256]{3,2,1,0:T(8,128)(2,1)S(1)}, u32[]{:S(2)}, u32[]{:S(2)}) %collective-permute-start.9) | collective-permute-done | bytes 131104 | tf_op jit(solution)/shard_map/ppermute | solution.py:26
  29.3 1.3 %attend_mid.3 = (f32[256,1024]{1,0:T(8,128)S(1)}, f32[1,1024]{1,0:T(1,128)S(1)}, f32[1,1024]{1,0:T(1,128)S(1)}, f32[128,1024]{1,0:T(8,128)S(1)}) custom-call(s32[18]{0:T(128)S(1)} %pad_add_fusion.info_ref, bf16[128,1024]{1,0:T(8,128)(2,1)S(1)} %get-tuple-element.67.q_t, bf16[2,2,64,256]{3,2,1,0:T(8,128)(2,1)S(1)} %collective-permute-done.9.refs_0_.refs_3_, ...), custom_call_target="tpu_custom_call" | custom-call | flops 268435456 | bytes 1978440 | tf_op jit(solution)/shard_map/attend_mid/pallas_call | solution.py:41
  30.6 0.1 collective-permute-done.10.refs_12_.refs_0_
  30.7 3.2 %attend_far.1 = (f32[1,1024]{1,0:T(1,128)S(1)}, f32[1,1024]{1,0:T(1,128)S(1)}, f32[1,1024]{1,0:T(1,128)S(1)}, f32[1,1024]{1,0:T(1,128)S(1)}, f32[1,1024]{1,0:T(1...) custom-call(s32[18]{0:T(128)S(1)} %pad_add_fusion.info_ref, ...), custom_call_target="tpu_custom_call" | custom-call | flops 1073741824 | bytes 5034056 | tf_op jit(solution)/shard_map/attend_far/pallas_call | solution.py:41
  33.9 0.5 collective-permute-start.13
  34.4 0.1 collective-permute-start.12
  34.5 0.6 %attend_back.4 = (f32[128,1024]{1,0:T(8,128)S(1)}, bf16[2,2,64,256]{3,2,1,0:T(8,128)(2,1)S(1)}) custom-call(bf16[1024,128]{1,0:T(8,128)(2,1)S(1)} %get-tuple-element.65.q_all, bf16[1024,128]{1,0:T(8,128)(2,1)S(1)} %get-tuple-element.66.do_all, bf16[128,1024]{1,0:T(8,128)(2,1)S(1)} %get-tuple-element.68.do_t, f32[1,1024]{1,0:T(1,128)S(1)} %get-tuple-element.85.delta_ref, ...), custom_call_target="tpu_custom_call" | custom-call | flops 402653184 | bytes 2629632 | tf_op jit(solution)/shard_map/attend_back/pallas_call | solution.py:41
  35.1 0.6 %attend_back.5 = (f32[128,1024]{1,0:T(8,128)S(1)}, bf16[2,2,64,256]{3,2,1,0:T(8,128)(2,1)S(1)}) custom-call(bf16[1024,128]{1,0:T(8,128)(2,1)S(1)} %get-tuple-element.65.q_all, bf16[1024,128]{1,0:T(8,128)(2,1)S(1)} %get-tuple-element.66.do_all, bf16[128,1024]{1,0:T(8,128)(2,1)S(1)} %get-tuple-element.68.do_t, f32[1,1024]{1,0:T(1,128)S(1)} %get-tuple-element.85.delta_ref, ...), custom_call_target="tpu_custom_call" | custom-call | flops 402653184 | bytes 3153920 | tf_op jit(solution)/shard_map/attend_back/pallas_call | solution.py:41
  35.9 0.5 collective-permute-start.14
  36.4 1.5 %collective-permute-start.17 = (bf16[2,2,64,256]{3,2,1,0:T(8,128)(2,1)S(1)}, bf16[2,2,64,256]{3,2,1,0:T(8,128)(2,1)S(1)}, u32[]{:S(2)}, u32[]{:S(2)}) collective-permute-start(bf16[2,2,64,256]{3,2,1,0:T(8,128)(2,1)S(1)} %sum_cores.3), channel_id=1, source_target_pairs={{0,16},{8,24},{16,0},{24,8},{1,17},{9,25},{17,1},{25,9},{2,18},{10... | collective-permute-start | bytes 393224 | tf_op jit(solution)/shard_map/ppermute | solution.py:26
  37.9 0.3 attend_tail.1
  38.3 1.1 %attend_back.6 = (f32[128,1024]{1,0:T(8,128)S(1)}, bf16[2,2,64,256]{3,2,1,0:T(8,128)(2,1)S(1)}, bf16[2,2,64,256]{3,2,1,0:T(8,128)(2,1)S(1)}) custom-call(bf16[1024,128]{1,0:T(8,128)(2,1)S(1)} %get-tuple-element.65.q_all, bf16[1024,128]{1,0:T(8,128)(2,1)S(1)} %get-tuple-element.66.do_all, bf16[128,1024]{1,0:T(8,128)(2,1)S(1)} %get-tuple-element.68.do_t, ...), custom_call_target="tpu_custom_call" | custom-call | flops 805306368 | bytes 6582272 | tf_op jit(solution)/shard_map/attend_back/pallas_call | solution.py:41
  39.4 0.1 collective-permute-start.18
  39.5 1.2 %collective-permute-start.21 = (bf16[2,2,64,256]{3,2,1,0:T(8,128)(2,1)S(1)}, bf16[2,2,64,256]{3,2,1,0:T(8,128)(2,1)S(1)}, u32[]{:S(2)}, u32[]{:S(2)}) collective-permute-start(bf16[2,2,64,256]{3,2,1,0:T(8,128)(2,1)S(1)} %sum_cores.2), channel_id=1, source_target_pairs={{0,16},{8,24},{16,0},{24,8},{1,17},{9,25},{17,1},{25,9},{2,18},{10... | collective-permute-start | bytes 393224 | tf_op jit(solution)/shard_map/ppermute | solution.py:26
  40.7 0.5 collective-permute-start.15
  41.2 1.2 %attend_back.7 = (bf16[64,1024]{1,0:T(8,128)(2,1)S(1)}, bf16[64,1024]{1,0:T(8,128)(2,1)S(1)}, bf16[2,2,64,256]{3,2,1,0:T(8,128)(2,1)S(1)}, bf16[2,2,64,256]{3,2,1,0:T(8,128)(2,1)S(1)}) custom-call(bf16[1024,128]{1,0:T(8,128)(2,1)S(1)} %get-tuple-element.65.q_all, bf16[1024,128]{1,0:T(8,128)(2,1)S(1)} %get-tuple-element.66.do_all, ...), custom_call_target="tpu_custom_call" | custom-call | flops 805306368 | bytes 6320128 | tf_op jit(solution)/shard_map/attend_back/pallas_call | solution.py:41
  42.4 1.5 %collective-permute-start.16 = (bf16[64,1024]{1,0:T(8,128)(2,1)S(1)}, bf16[64,1024]{1,0:T(8,128)(2,1)S(1)}, u32[]{:S(2)}, u32[]{:S(2)}) collective-permute-start(bf16[64,1024]{1,0:T(8,128)(2,1)S(1)} %get-tuple-element.107), channel_id=1, source_target_pairs={{0,8},{8,0},{16,24},{24,16},{1,9},{9,1},{17,25},{25,17},{2,10},{10... | collective-permute-start | bytes 393224 | tf_op jit(solution)/shard_map/ppermute | solution.py:26
  44.0 0.8 %collective-permute-start.19 = (bf16[2,64,256]{2,1,0:T(8,128)(2,1)S(1)}, bf16[2,64,256]{2,1,0:T(8,128)(2,1)S(1)}, u32[]{:S(2)}, u32[]{:S(2)}) collective-permute-start(bf16[2,64,256]{2,1,0:T(8,128)(2,1)S(1)} %get-tuple-element.112), channel_id=1, source_target_pairs={{0,4},{1,5},{2,6},{3,7},{4,0},{5,1},{6,2},{7,3},{8,12},{9,13},{10,... | collective-permute-start | bytes 196616 | tf_op jit(solution)/shard_map/ppermute | solution.py:26
  44.9 0.5 collective-permute-done.21.refs_0_
  45.4 2.5 %collective-permute-start.20 = (bf16[2,64,256]{2,1,0:T(8,128)(2,1)S(1)}, bf16[2,64,256]{2,1,0:T(8,128)(2,1)S(1)}, u32[]{:S(2)}, u32[]{:S(2)}) collective-permute-start(bf16[2,64,256]{2,1,0:T(8,128)(2,1)S(1)} %get-tuple-element.113), channel_id=1, source_target_pairs={{0,6},{1,7},{2,4},{3,5},{4,2},{5,3},{6,0},{7,1},{8,14},{9,15},{10,... | collective-permute-start | bytes 196616 | tf_op jit(solution)/shard_map/ppermute | solution.py:26
  47.9 0.1 collective-permute-start.23
  48.0 3.7 %collective-permute-done.19.refs_0_ = bf16[2,64,256]{2,1,0:T(8,128)(2,1)S(1)} collective-permute-done((bf16[2,64,256]{2,1,0:T(8,128)(2,1)S(1)}, bf16[2,64,256]{2,1,0:T(8,128)(2,1)S(1)}, u32[]{:S(2)}, u32[]{:S(2)}) %collective-permute-start.19) | collective-permute-done | bytes 65568 | tf_op jit(solution)/shard_map/ppermute | solution.py:26
  51.7 1.3 %collective-permute-done.23.refs_2_ = bf16[2,64,256]{2,1,0:T(8,128)(2,1)S(1)} collective-permute-done((bf16[2,64,256]{2,1,0:T(8,128)(2,1)S(1)}, bf16[2,64,256]{2,1,0:T(8,128)(2,1)S(1)}, u32[]{:S(2)}, u32[]{:S(2)}) %collective-permute-start.23) | collective-permute-done | bytes 65568 | tf_op jit(solution)/shard_map/ppermute | solution.py:26
  53.0 0.6 %collective-permute-start.24 = (bf16[64,256]{1,0:T(8,128)(2,1)S(1)}, bf16[64,256]{1,0:T(8,128)(2,1)S(1)}, u32[]{:S(2)}, u32[]{:S(2)}) collective-permute-start(bf16[64,256]{1,0:T(8,128)(2,1)S(1)} %get-tuple-element.119), channel_id=1, source_target_pairs={{0,8},{8,0},{16,24},{24,16},{1,9},{9,1},{17,25},{25,17},{2,10},{10... | collective-permute-start | bytes 98312 | tf_op jit(solution)/shard_map/ppermute | solution.py:26
  53.7 0.8 %finish_q.1 = (bf16[64,2048]{1,0:T(8,128)(2,1)}, bf16[64,2048]{1,0:T(8,128)(2,1)}) custom-call(s32[1]{0:T(128)} %bitcast.group_ref, bf16[64,1024]{1,0:T(8,128)(2,1)S(1)} %get-tuple-element.98.refs_0_, bf16[64,1024]{1,0:T(8,128)(2,1)S(1)} %collective-permute-done.15.refs_1_, bf16[64,1024]{1,0:T(8,128)(2,1)S(1)} %get-tuple-element.106.refs_2_, ...), custom_call_target="tpu_custom_call" | custom-call | bytes 1048580 | tf_op jit(solution)/shard_map/finish_q/pallas_call | solution.py:41
  54.5 2.5 %collective-permute-done.24.refs_1_ = bf16[64,256]{1,0:T(8,128)(2,1)S(1)} collective-permute-done((bf16[64,256]{1,0:T(8,128)(2,1)S(1)}, bf16[64,256]{1,0:T(8,128)(2,1)S(1)}, u32[]{:S(2)}, u32[]{:S(2)}) %collective-permute-start.24) | collective-permute-done | bytes 32800 | tf_op jit(solution)/shard_map/ppermute | solution.py:26
  57.0 0.6 %finish_kv.1 = (bf16[64,256]{1,0:T(8,128)(2,1)}, bf16[64,256]{1,0:T(8,128)(2,1)}) custom-call(s32[1]{0:T(128)} %bitcast.group_ref, bf16[64,256]{1,0:T(8,128)(2,1)S(1)} %get-tuple-element.118.refs_0_, bf16[64,256]{1,0:T(8,128)(2,1)S(1)} %collective-permute-done.24.refs_1_), custom_call_target="tpu_custom_call" | custom-call | bytes 131076 | tf_op jit(solution)/shard_map/finish_kv/pallas_call | solution.py:41
  (34 shorter events, 0.4 us)
Async XLA Ops:
  0.6 8.5 %collective-permute-start.1 = (bf16[64,256]{1,0:T(8,128)(2,1)}, bf16[64,256]{1,0:T(8,128)(2,1)S(1)}, u32[]{:S(2)}, u32[]{:S(2)}) collective-permute-start(bf16[64,256]{1,0:T(8,128)(2,1)} %bitcast.15), channel_id=1, source_target_pairs={{0,8},{8,0},{16,24},{24,16},{1,9},{9,1},{17,25},{25,17},{2,10},{10... | collective-permute-start | bytes 98312 | tf_op jit(solution)/shard_map/ppermute | solution.py:26
  3.6 5.5 %collective-permute-start.2 = (bf16[64,256]{1,0:T(8,128)(2,1)}, bf16[64,256]{1,0:T(8,128)(2,1)S(1)}, u32[]{:S(2)}, u32[]{:S(2)}) collective-permute-start(bf16[64,256]{1,0:T(8,128)(2,1)} %bitcast.17), channel_id=1, source_target_pairs={{0,8},{8,0},{16,24},{24,16},{1,9},{9,1},{17,25},{25,17},{2,10},{10... | collective-permute-start | bytes 98312 | tf_op jit(solution)/shard_map/ppermute | solution.py:26
  3.7 0.9 %copy-start = (bf16[2,32,2048]{2,1,0:T(8,128)(2,1)S(1)}, bf16[2,32,2048]{2,1,0:T(8,128)(2,1)}, u32[]{:S(2)}) copy-start(bf16[2,32,2048]{2,1,0:T(8,128)(2,1)} %param.5) | copy-start | bytes 786436
  4.7 0.9 %copy-start.1 = (bf16[2,32,2048]{2,1,0:T(8,128)(2,1)S(1)}, bf16[2,32,2048]{2,1,0:T(8,128)(2,1)}, u32[]{:S(2)}) copy-start(bf16[2,32,2048]{2,1,0:T(8,128)(2,1)} %param.8) | copy-start | bytes 786436
  5.7 13.8 %collective-permute-start = (bf16[2,64,1024]{2,1,0:T(8,128)(2,1)S(1)}, bf16[2,64,1024]{2,1,0:T(8,128)(2,1)S(1)}, u32[]{:S(2)}, u32[]{:S(2)}) collective-permute-start(bf16[2,64,1024]{2,1,0:T(8,128)(2,1)S(1)} %get-tuple-element.64), channel_id=1, source_target_pairs={{0,8},{8,0},{16,24},{24,16},{1,9},{9,1},{17,25},{25,17},{2,10},{10... | collective-permute-start | bytes 786440 | tf_op jit(solution)/shard_map/ppermute | solution.py:26
  9.2 4.3 %collective-permute-start.5 = (bf16[2,64,256]{2,1,0:T(8,128)(2,1)S(1)}, bf16[2,64,256]{2,1,0:T(8,128)(2,1)S(1)}, u32[]{:S(2)}, u32[]{:S(2)}) collective-permute-start(bf16[2,64,256]{2,1,0:T(8,128)(2,1)S(1)} %pack_kv.1.refs_0_), channel_id=1, source_target_pairs={{0,2},{1,3},{2,0},{3,1},{4,6},{5,7},{6,4},{7,5},{8,10},{9,11},{10,... | collective-permute-start | bytes 196616 | tf_op jit(solution)/shard_map/ppermute | solution.py:26
  13.5 6.2 %collective-permute-start.6 = (bf16[2,2,64,256]{3,2,1,0:T(8,128)(2,1)S(1)}, bf16[2,2,64,256]{3,2,1,0:T(8,128)(2,1)S(1)}, u32[]{:S(2)}, u32[]{:S(2)}) collective-permute-start(bf16[2,2,64,256]{3,2,1,0:T(8,128)(2,1)S(1)} %stack.10.refs_0_.refs_6_), channel_id=1, source_target_pairs={{0,1},{1,0},{2,3},{3,2},{4,5},{5,4},{6,7},{7,6},{8,9},{9,8},{10,11... | collective-permute-start | bytes 393224 | tf_op jit(solution)/shard_map/ppermute | solution.py:26
  13.6 7.9 %collective-permute-start.4 = (bf16[2,64,256]{2,1,0:T(8,128)(2,1)S(1)}, bf16[2,64,256]{2,1,0:T(8,128)(2,1)S(1)}, u32[]{:S(2)}, u32[]{:S(2)}) collective-permute-start(bf16[2,64,256]{2,1,0:T(8,128)(2,1)S(1)} %pack_kv.1.refs_0_), channel_id=1, source_target_pairs={{0,6},{1,7},{2,4},{3,5},{4,2},{5,3},{6,0},{7,1},{8,14},{9,15},{10,... | collective-permute-start | bytes 196616 | tf_op jit(solution)/shard_map/ppermute | solution.py:26
  17.2 6.1 %collective-permute-start.3 = (bf16[2,64,256]{2,1,0:T(8,128)(2,1)S(1)}, bf16[2,64,256]{2,1,0:T(8,128)(2,1)S(1)}, u32[]{:S(2)}, u32[]{:S(2)}) collective-permute-start(bf16[2,64,256]{2,1,0:T(8,128)(2,1)S(1)} %pack_kv.1.refs_0_), channel_id=1, source_target_pairs={{0,4},{1,5},{2,6},{3,7},{4,0},{5,1},{6,2},{7,3},{8,12},{9,13},{10,... | collective-permute-start | bytes 196616 | tf_op jit(solution)/shard_map/ppermute | solution.py:26
  17.3 7.7 %collective-permute-start.8 = (bf16[2,2,64,256]{3,2,1,0:T(8,128)(2,1)S(1)}, bf16[2,2,64,256]{3,2,1,0:T(8,128)(2,1)S(1)}, u32[]{:S(2)}, u32[]{:S(2)}) collective-permute-start(bf16[2,2,64,256]{3,2,1,0:T(8,128)(2,1)S(1)} %stack.10.refs_0_.refs_6_), channel_id=1, source_target_pairs={{0,16},{8,24},{16,0},{24,8},{1,17},{9,25},{17,1},{25,9},{2,18},{10... | collective-permute-start | bytes 393224 | tf_op jit(solution)/shard_map/ppermute | solution.py:26
  23.3 3.1 %collective-permute-start.7 = (bf16[2,2,64,256]{3,2,1,0:T(8,128)(2,1)S(1)}, bf16[2,2,64,256]{3,2,1,0:T(8,128)(2,1)S(1)}, u32[]{:S(2)}, u32[]{:S(2)}) collective-permute-start(bf16[2,2,64,256]{3,2,1,0:T(8,128)(2,1)S(1)} %stack.11.refs_0_.refs_5_), channel_id=1, source_target_pairs={{0,1},{1,0},{2,3},{3,2},{4,5},{5,4},{6,7},{7,6},{8,9},{9,8},{10,11... | collective-permute-start | bytes 393224 | tf_op jit(solution)/shard_map/ppermute | solution.py:26
  23.4 5.9 %collective-permute-start.9 = (bf16[2,2,64,256]{3,2,1,0:T(8,128)(2,1)S(1)}, bf16[2,2,64,256]{3,2,1,0:T(8,128)(2,1)S(1)}, u32[]{:S(2)}, u32[]{:S(2)}) collective-permute-start(bf16[2,2,64,256]{3,2,1,0:T(8,128)(2,1)S(1)} %stack.11.refs_0_.refs_5_), channel_id=1, source_target_pairs={{0,16},{8,24},{16,0},{24,8},{1,17},{9,25},{17,1},{25,9},{2,18},{10... | collective-permute-start | bytes 393224 | tf_op jit(solution)/shard_map/ppermute | solution.py:26
  25.0 5.6 %collective-permute-start.11 = (bf16[2,2,64,256]{3,2,1,0:T(8,128)(2,1)S(1)}, bf16[2,2,64,256]{3,2,1,0:T(8,128)(2,1)S(1)}, u32[]{:S(2)}, u32[]{:S(2)}) collective-permute-start(bf16[2,2,64,256]{3,2,1,0:T(8,128)(2,1)S(1)} %collective-permute-done.8.refs_0_.refs_2_), channel_id=1, source_target_pairs={{0,1},{1,0},{2,3},{3,2},{4,5},{5,4},{6,7},{7,6},{8,9},{9,8},{10,11... | collective-permute-start | bytes 393224 | tf_op jit(solution)/shard_map/ppermute | solution.py:26
  29.3 1.3 %collective-permute-start.10 = (bf16[2,2,64,256]{3,2,1,0:T(8,128)(2,1)S(1)}, bf16[2,2,64,256]{3,2,1,0:T(8,128)(2,1)S(1)}, u32[]{:S(2)}, u32[]{:S(2)}) collective-permute-start(bf16[2,2,64,256]{3,2,1,0:T(8,128)(2,1)S(1)} %collective-permute-done.9.refs_0_.refs_3_), channel_id=1, source_target_pairs={{0,1},{1,0},{2,3},{3,2},{4,5},{5,4},{6,7},{7,6},{8,9},{9,8},{10,11... | collective-permute-start | bytes 393224 | tf_op jit(solution)/shard_map/ppermute | solution.py:26
  33.9 1.9 %collective-permute-start.13 = (bf16[2,2,64,256]{3,2,1,0:T(8,128)(2,1)S(1)}, bf16[2,2,64,256]{3,2,1,0:T(8,128)(2,1)S(1)}, u32[]{:S(2)}, u32[]{:S(2)}) collective-permute-start(bf16[2,2,64,256]{3,2,1,0:T(8,128)(2,1)S(1)} %get-tuple-element.95), channel_id=1, source_target_pairs={{0,1},{1,0},{2,3},{3,2},{4,5},{5,4},{6,7},{7,6},{8,9},{9,8},{10,11... | collective-permute-start | bytes 393224 | tf_op jit(solution)/shard_map/ppermute | solution.py:26
  34.4 1.4 %collective-permute-start.12 = (bf16[2,2,64,256]{3,2,1,0:T(8,128)(2,1)S(1)}, bf16[2,2,64,256]{3,2,1,0:T(8,128)(2,1)S(1)}, u32[]{:S(2)}, u32[]{:S(2)}) collective-permute-start(bf16[2,2,64,256]{3,2,1,0:T(8,128)(2,1)S(1)} %get-tuple-element.93), channel_id=1, source_target_pairs={{0,1},{1,0},{2,3},{3,2},{4,5},{5,4},{6,7},{7,6},{8,9},{9,8},{10,11... | collective-permute-start | bytes 393224 | tf_op jit(solution)/shard_map/ppermute | solution.py:26
  35.9 2.0 %collective-permute-start.14 = (bf16[64,128]{1,0:T(8,128)(2,1)S(1)}, bf16[64,128]{1,0:T(8,128)(2,1)S(1)}, u32[]{:S(2)}, u32[]{:S(2)}) collective-permute-start(bf16[64,128]{1,0:T(8,128)(2,1)S(1)} %slice_bitcast_fusion), channel_id=1, source_target_pairs={{0,1},{1,0},{2,3},{3,2},{4,5},{5,4},{6,7},{7,6},{8,9},{9,8},{10,11... | collective-permute-start | bytes 49160 | tf_op jit(solution)/shard_map/ppermute | solution.py:26
  36.4 6.0 %collective-permute-start.17 = (bf16[2,2,64,256]{3,2,1,0:T(8,128)(2,1)S(1)}, bf16[2,2,64,256]{3,2,1,0:T(8,128)(2,1)S(1)}, u32[]{:S(2)}, u32[]{:S(2)}) collective-permute-start(bf16[2,2,64,256]{3,2,1,0:T(8,128)(2,1)S(1)} %sum_cores.3), channel_id=1, source_target_pairs={{0,16},{8,24},{16,0},{24,8},{1,17},{9,25},{17,1},{25,9},{2,18},{10... | collective-permute-start | bytes 393224 | tf_op jit(solution)/shard_map/ppermute | solution.py:26
  39.4 4.6 %collective-permute-start.18 = (bf16[2,2,64,256]{3,2,1,0:T(8,128)(2,1)S(1)}, bf16[2,2,64,256]{3,2,1,0:T(8,128)(2,1)S(1)}, u32[]{:S(2)}, u32[]{:S(2)}) collective-permute-start(bf16[2,2,64,256]{3,2,1,0:T(8,128)(2,1)S(1)} %get-tuple-element.110), channel_id=1, source_target_pairs={{0,1},{1,0},{2,3},{3,2},{4,5},{5,4},{6,7},{7,6},{8,9},{9,8},{10,11... | collective-permute-start | bytes 393224 | tf_op jit(solution)/shard_map/ppermute | solution.py:26
  39.5 5.9 %collective-permute-start.21 = (bf16[2,2,64,256]{3,2,1,0:T(8,128)(2,1)S(1)}, bf16[2,2,64,256]{3,2,1,0:T(8,128)(2,1)S(1)}, u32[]{:S(2)}, u32[]{:S(2)}) collective-permute-start(bf16[2,2,64,256]{3,2,1,0:T(8,128)(2,1)S(1)} %sum_cores.2), channel_id=1, source_target_pairs={{0,16},{8,24},{16,0},{24,8},{1,17},{9,25},{17,1},{25,9},{2,18},{10... | collective-permute-start | bytes 393224 | tf_op jit(solution)/shard_map/ppermute | solution.py:26
  40.7 7.2 %collective-permute-start.22 = (bf16[2,2,64,256]{3,2,1,0:T(8,128)(2,1)S(1)}, bf16[2,2,64,256]{3,2,1,0:T(8,128)(2,1)S(1)}, u32[]{:S(2)}, u32[]{:S(2)}) collective-permute-start(bf16[2,2,64,256]{3,2,1,0:T(8,128)(2,1)S(1)} %get-tuple-element.114), channel_id=1, source_target_pairs={{0,1},{1,0},{2,3},{3,2},{4,5},{5,4},{6,7},{7,6},{8,9},{9,8},{10,11... | collective-permute-start | bytes 393224 | tf_op jit(solution)/shard_map/ppermute | solution.py:26
  40.7 13.0 %collective-permute-start.15 = (bf16[64,1024]{1,0:T(8,128)(2,1)S(1)}, bf16[64,1024]{1,0:T(8,128)(2,1)S(1)}, u32[]{:S(2)}, u32[]{:S(2)}) collective-permute-start(bf16[64,1024]{1,0:T(8,128)(2,1)S(1)} %get-tuple-element.99), channel_id=1, source_target_pairs={{0,8},{8,0},{16,24},{24,16},{1,9},{9,1},{17,25},{25,17},{2,10},{10... | collective-permute-start | bytes 393224 | tf_op jit(solution)/shard_map/ppermute | solution.py:26
  42.4 11.2 %collective-permute-start.16 = (bf16[64,1024]{1,0:T(8,128)(2,1)S(1)}, bf16[64,1024]{1,0:T(8,128)(2,1)S(1)}, u32[]{:S(2)}, u32[]{:S(2)}) collective-permute-start(bf16[64,1024]{1,0:T(8,128)(2,1)S(1)} %get-tuple-element.107), channel_id=1, source_target_pairs={{0,8},{8,0},{16,24},{24,16},{1,9},{9,1},{17,25},{25,17},{2,10},{10... | collective-permute-start | bytes 393224 | tf_op jit(solution)/shard_map/ppermute | solution.py:26
  44.0 7.7 %collective-permute-start.19 = (bf16[2,64,256]{2,1,0:T(8,128)(2,1)S(1)}, bf16[2,64,256]{2,1,0:T(8,128)(2,1)S(1)}, u32[]{:S(2)}, u32[]{:S(2)}) collective-permute-start(bf16[2,64,256]{2,1,0:T(8,128)(2,1)S(1)} %get-tuple-element.112), channel_id=1, source_target_pairs={{0,4},{1,5},{2,6},{3,7},{4,0},{5,1},{6,2},{7,3},{8,12},{9,13},{10,... | collective-permute-start | bytes 196616 | tf_op jit(solution)/shard_map/ppermute | solution.py:26
  45.4 6.3 %collective-permute-start.20 = (bf16[2,64,256]{2,1,0:T(8,128)(2,1)S(1)}, bf16[2,64,256]{2,1,0:T(8,128)(2,1)S(1)}, u32[]{:S(2)}, u32[]{:S(2)}) collective-permute-start(bf16[2,64,256]{2,1,0:T(8,128)(2,1)S(1)} %get-tuple-element.113), channel_id=1, source_target_pairs={{0,6},{1,7},{2,4},{3,5},{4,2},{5,3},{6,0},{7,1},{8,14},{9,15},{10,... | collective-permute-start | bytes 196616 | tf_op jit(solution)/shard_map/ppermute | solution.py:26
  47.9 5.1 %collective-permute-start.23 = (bf16[2,64,256]{2,1,0:T(8,128)(2,1)S(1)}, bf16[2,64,256]{2,1,0:T(8,128)(2,1)S(1)}, u32[]{:S(2)}, u32[]{:S(2)}) collective-permute-start(bf16[2,64,256]{2,1,0:T(8,128)(2,1)S(1)} %get-tuple-element.117), channel_id=1, source_target_pairs={{0,2},{1,3},{2,0},{3,1},{4,6},{5,7},{6,4},{7,5},{8,10},{9,11},{10,... | collective-permute-start | bytes 196616 | tf_op jit(solution)/shard_map/ppermute | solution.py:26
  53.0 4.0 %collective-permute-start.24 = (bf16[64,256]{1,0:T(8,128)(2,1)S(1)}, bf16[64,256]{1,0:T(8,128)(2,1)S(1)}, u32[]{:S(2)}, u32[]{:S(2)}) collective-permute-start(bf16[64,256]{1,0:T(8,128)(2,1)S(1)} %get-tuple-element.119), channel_id=1, source_target_pairs={{0,8},{8,0},{16,24},{24,16},{1,9},{9,1},{17,25},{25,17},{2,10},{10... | collective-permute-start | bytes 98312 | tf_op jit(solution)/shard_map/ppermute | solution.py:26

commit v10 on v8

--- a/solution.py
+++ b/solution.py
@@ -58,19 +58,6 @@
 
 def dot_rows(left, right):
     return lax.dot_general(left, right, (((1,), (1,)), ((), ())), preferred_element_type=F32)
-
-
-def pack_kv_kernel(kv, group_ref, *refs):
-    out_ref = refs[-1]
-    out_ref[0] = refs[0][...]
-    for g in range(kv):
-
-        @pl.when(group_ref[0] == g)
-        def _():
-            cols = pl.ds(g * HD, HD)
-            for s in range(1, kv):
-                out_ref[s, :, :HD] = refs[2 * s - 1][:, cols]
-                out_ref[s, :, HD:] = refs[2 * s][:, cols]
 
 
 def pack_q_kernel(kv, group_ref, query_ref, grad_ref, *out_refs):
@@ -201,7 +188,7 @@
         mix_ref[:, at] = mixed
 
 
-def turn_kernel(plan, *refs):
+def turn_kernel(plan, info_ref, *refs):
     q_parts, (q_all, do_all, q_t, do_t) = refs[:-4], refs[-4:]
     for tile, (s, start) in enumerate(plan.tiles):
         span = pl.ds(start, plan.tile_rows)
@@ -318,6 +305,13 @@
         out_ref[...] = total.astype(BF)
 
 
+def sum_far_kernel(*refs):
+    total = refs[0][...].astype(F32)
+    for ref in refs[1:-1]:
+        total = total + ref[...].astype(F32)
+    refs[-1][...] = total
+
+
 def finish_kv_kernel(kv, group_ref, *refs):
     key_ref, value_ref = refs[kv:]
     for g in range(kv):
@@ -376,12 +370,16 @@
 
     dkv = bf(z_part, kv, rows, 2 * HD)
 
-    key_parts = with_swaps([key_vectors] * kv)[1:]
-    value_parts = with_swaps([value_vectors] * kv)[1:]
-    mine = (head % kv) * HD
-    own = jnp.concatenate(
-        [lax.dynamic_slice_in_dim(block, mine, HD, 1) for block in (key_vectors, value_vectors)], axis=1
-    )
+    def of_head(g):
+        picked = []
+        for block in (key_vectors, value_vectors):
+            out = block[:, :HD]
+            for i in range(1, kv):
+                out = jnp.where(g == i, block[:, i * HD : (i + 1) * HD], out)
+            picked.append(out)
+        return jnp.concatenate(picked, axis=1)
+
+    piece = jnp.stack(with_swaps([of_head((head % kv) ^ s) for s in range(kv)]))
     q_parts = call(
         functools.partial(pack_q_kernel, kv),
         "pack_q",
@@ -389,17 +387,17 @@
         [bf(2, rows, width)] * kv,
         [SMEM, VMEM, VMEM],
     )
-    own = after([own], q_parts[1:])[0]
-    piece = call(
-        functools.partial(pack_kv_kernel, kv),
-        "pack_kv",
-        (own_group, own, *[part for pair in zip(key_parts, value_parts) for part in pair]),
-        [bf(kv, rows, 2 * HD)],
-        [SMEM] + [VMEM] * (2 * kv - 1),
-    )[0]
     pieces = [swap(piece, "ctx", m * cores) for m in reversed(range(1, z_devices))]
     pieces = [piece] + pieces[::-1]
     q_parts = with_swaps(q_parts)
+    query_rows = plan.query_rows
+    q_all, do_all, q_t, do_t = call(
+        functools.partial(turn_kernel, plan),
+        "turn",
+        (info, *q_parts),
+        [bf(query_rows, HD)] * 2 + [bf(HD, query_rows)] * 2,
+        [SMEM] + [VMEM] * kv,
+    )
     column, handed, order = [None] * parts, [None] * parts, []
     for p in reversed(range(parts)):
         parcels = [pieces[m] for m in plan.zone(p)]
@@ -413,7 +411,7 @@
         handed[p] = column[p]
         if extra:
             handed[p + 1] = handed_on[0]
-        order = [swap(column[p][0, 0, :, :HD], "ctx", 1)] if cores > 1 and p else []
+        order = [q_t] if p else []
     columns = [[swap(half, "head", a * kv) for half in column] for a in range(1, spans)]
     near_kv = [column] + [[swap(half, "ctx", core) for half in handed] for core in range(1, cores)]
     near_flat = [half for pair in near_kv for half in pair]
@@ -425,13 +423,6 @@
     keys = plan.chunk_keys
     query_rows = plan.query_rows
     row, column_out = f32(1, query_rows), f32(HD, query_rows)
-
-    q_all, do_all, q_t, do_t = call(
-        functools.partial(turn_kernel, plan),
-        "turn",
-        q_parts,
-        [bf(query_rows, HD)] * 2 + [bf(HD, query_rows)] * 2,
-    )
 
     def forward(name, chunks, kv_refs, order):
         size = len(chunks) * keys
@@ -530,7 +521,10 @@
 
         for m, total in zip(plan.zone(p), totals):
             z_parts[m] = swap(total, "ctx", m * cores) if m else total
-    ordered = [z_parts[m] for p in range(parts) for m in plan.zone(p)]
+    ordered = [z_parts[m] for p in each for m in plan.zone(p)]
+    if parts > 1:
+        far_z = call(sum_far_kernel, "sum_far_z", ordered[:z_part], [f32(kv, rows, 2 * HD)], flops=1 << 32)
+        ordered = [*far_z, *ordered[z_part:]]
     pair_parts = call(
         functools.partial(sum_z_kernel, kv), "sum_z", ordered, [bf(rows, 2 * HD)] * kv
     )

time: 54.1 us -> 50 us (0.924)
  waiting for transfers between devices: 14.4 us -> 8.38 us
  starting transfers between devices: 20.5 us -> 22.7 us
  local copies, waits for them, and re-layouts: 3.34 us -> 1.9 us
  other arithmetic: 0.74 us -> 1.53 us
    ppermute x26 -> x24, waiting for transfers between devices: 14.4 us -> 8.38 us  [swap(): return lax.ppermute(block, axis, [(i, i ^ mask) for i in range(size)])]
    ppermute x26 -> x24, starting transfers between devices: 20.5 us -> 22.7 us  [swap(): return lax.ppermute(block, axis, [(i, i ^ mask) for i in range(size)])]
    dynamic_slice x2 -> x0, local copies, waits for them, and re-layouts: 1.44 us -> none  [shards(): lax.dynamic_slice_in_dim(block, mine, HD, 1)]
    select_n x0 -> x1, other arithmetic: none -> 0.78 us  [of_head(): out = jnp.where(g == i, block[:, i * HD:(i + 1) * HD], out)]
  transfers between devices with their start and end apart: 26 -> 24, of which waited for: 10 -> 7; matrix products, arithmetic and copies ran while one was open for 4% -> 1% of each run, Pallas kernels for 19% -> 21%
where the time goes in v10:
time: 50 us; the launch traced here: 49.8 us
  starting transfers between devices  22.7 us (45%)
  Pallas kernels  14.4 us (29%)
  waiting for transfers between devices  8.38 us (17%)
  local copies, waits for them, and re-layouts  1.9 us (4%)
  other arithmetic  1.53 us (3%)
  between operations  0.88 us (2%)
    ppermute x24, starting transfers between devices, swap(): return lax.ppermute(block, axis, [(i, i ^ mask) for i in range(size)])  22.7 us
    pallas_call x20, Pallas kernels, call(): pl.pallas_call(kernel, out_shape=list(outs), in_specs=specs or [VMEM] * l...  14.4 us
    ppermute x24, waiting for transfers between devices, swap(): return lax.ppermute(block, axis, [(i, i ^ mask) for i in range(size)])  8.38 us
    unnamed x4, local copies, waits for them, and re-layouts  1.9 us
  transfers between devices with their start and end apart: 24, of which 7 were waited for; matrix products, arithmetic and copies ran while one was open for 1% of the time, Pallas kernels for 21%

profile of v10, /device:TPU:0, one launch (start us, length us, event | category | flops | bytes accessed | tf_op | source)
XLA Modules:
  0.0 49.8 jit_solution(13013349754037166199)
XLA Ops:
  0.6 0.8 %broadcast_select_fusion.2 = (bf16[64,128]{1,0:T(8,128)(2,1)S(1)}, bf16[64,128]{1,0:T(8,128)(2,1)S(1)}, bf16[64,128]{1,0:T(8,128)(2,1)S(1)}, bf16[64,128]{1,0:T(8,128)(2,1)S(1)}) fusion(pred[]{:T(512)S(6)} %eq.12, bf16[64,256]{1,0:T(8,128)(2,1)} %bitcast.18, pred[]{:T(512)S(6)} %eq.13, bf16[64,256]{1,0:T(8,128)(2,1)} %bitcast.19), kind=kLoop, calls=%fused_computation.6 | loop fusion | flops 32768 | bytes 131074 | tf_op jit(solution)/shard_map/jit(_where)/select_n | solution.py:378
  1.4 3.0 %collective-permute-start.1 = (bf16[64,256]{1,0:T(8,128)(2,1)S(1)}, bf16[64,256]{1,0:T(8,128)(2,1)S(1)}, u32[]{:S(2)}, u32[]{:S(2)}) collective-permute-start(bf16[64,256]{1,0:T(8,128)(2,1)S(1)} %pad_maximum_fusion.1), channel_id=1, source_target_pairs={{0,8},{8,0},{16,24},{24,16},{1,9},{9,1},{17,25},{25,17},{2,10},{10... | collective-permute-start | bytes 98312 | tf_op jit(solution)/shard_map/ppermute | solution.py:26
  4.4 0.9 %copy-done = bf16[2,32,2048]{2,1,0:T(8,128)(2,1)S(1)} copy-done((bf16[2,32,2048]{2,1,0:T(8,128)(2,1)S(1)}, bf16[2,32,2048]{2,1,0:T(8,128)(2,1)}, u32[]{:S(2)}) %copy-start) | copy-done | bytes 262168
  5.4 0.9 %copy-done.1 = bf16[2,32,2048]{2,1,0:T(8,128)(2,1)S(1)} copy-done((bf16[2,32,2048]{2,1,0:T(8,128)(2,1)S(1)}, bf16[2,32,2048]{2,1,0:T(8,128)(2,1)}, u32[]{:S(2)}) %copy-start.1) | copy-done | bytes 262168
  6.4 0.1 collective-permute-start
  6.5 0.0 collective-permute-done.1
  6.5 2.1 %collective-permute-start.4 = (bf16[2,64,256]{2,1,0:T(8,128)(2,1)S(1)}, bf16[2,64,256]{2,1,0:T(8,128)(2,1)S(1)}, u32[]{:S(2)}, u32[]{:S(2)}) collective-permute-start(bf16[2,64,256]{2,1,0:T(8,128)(2,1)S(1)} %pad_maximum_fusion.refs_0_), channel_id=1, source_target_pairs={{0,2},{1,3},{2,0},{3,1},{4,6},{5,7},{6,4},{7,5},{8,10},{9,11},{10,... | collective-permute-start | bytes 196616 | tf_op jit(solution)/shard_map/ppermute | solution.py:26
  8.7 2.5 %collective-permute-start.3 = (bf16[2,64,256]{2,1,0:T(8,128)(2,1)S(1)}, bf16[2,64,256]{2,1,0:T(8,128)(2,1)S(1)}, u32[]{:S(2)}, u32[]{:S(2)}) collective-permute-start(bf16[2,64,256]{2,1,0:T(8,128)(2,1)S(1)} %pad_maximum_fusion.refs_0_), channel_id=1, source_target_pairs={{0,6},{1,7},{2,4},{3,5},{4,2},{5,3},{6,0},{7,1},{8,14},{9,15},{10,... | collective-permute-start | bytes 196616 | tf_op jit(solution)/shard_map/ppermute | solution.py:26
  11.1 0.1 collective-permute-start.2
  11.3 1.7 %collective-permute-start.7 = (bf16[2,2,64,256]{3,2,1,0:T(8,128)(2,1)S(1)}, bf16[2,2,64,256]{3,2,1,0:T(8,128)(2,1)S(1)}, u32[]{:S(2)}, u32[]{:S(2)}) collective-permute-start(bf16[2,2,64,256]{3,2,1,0:T(8,128)(2,1)S(1)} %stack.22.refs_2_.refs_1_), channel_id=1, source_target_pairs={{0,16},{8,24},{16,0},{24,8},{1,17},{9,25},{17,1},{25,9},{2,18},{10... | collective-permute-start | bytes 393224 | tf_op jit(solution)/shard_map/ppermute | solution.py:26
  12.9 0.7 %pad_add_fusion.info_ref = s32[18]{0:T(128)S(1)} fusion(s32[16]{0:T(128)} %param.9, s32[1]{0:T(128)} %bitcast.2, s32[1]{0:T(128)} %bitcast.1), kind=kLoop, calls=%fused_computation.8 | loop fusion | flops 36 | bytes 144 | tf_op jit(solution)/shard_map/concatenate | solution.py:355
  13.7 0.5 %collective-permute-done.refs_1_ = bf16[2,64,1024]{2,1,0:T(8,128)(2,1)S(1)} collective-permute-done((bf16[2,64,1024]{2,1,0:T(8,128)(2,1)S(1)}, bf16[2,64,1024]{2,1,0:T(8,128)(2,1)S(1)}, u32[]{:S(2)}, u32[]{:S(2)}) %collective-permute-start) | collective-permute-done | bytes 262176 | tf_op jit(solution)/shard_map/ppermute | solution.py:26
  14.2 0.7 %turn.1 = (bf16[1024,128]{1,0:T(8,128)(2,1)S(1)}, bf16[1024,128]{1,0:T(8,128)(2,1)S(1)}, bf16[128,1024]{1,0:T(8,128)(2,1)S(1)}, bf16[128,1024]{1,0:T(8,128)(2,1)S(1)}) custom-call(s32[18]{0:T(128)S(1)} %pad_add_fusion.info_ref, bf16[2,64,1024]{2,1,0:T(8,128)(2,1)S(1)} %get-tuple-element.57.refs_0_, bf16[2,64,1024]{2,1,0:T(8,128)(2,1)S(1)} %collective-permute-done.refs_1_), custom_call_target="tpu_custom_call" | custom-call | bytes 1572936 | tf_op jit(solution)/shard_map/turn/pallas_call | solution.py:41
  15.0 0.0 collective-permute-done.3.refs_1_
  15.0 2.1 %collective-permute-done.2.refs_0_ = bf16[2,64,256]{2,1,0:T(8,128)(2,1)S(1)} collective-permute-done((bf16[2,64,256]{2,1,0:T(8,128)(2,1)S(1)}, bf16[2,64,256]{2,1,0:T(8,128)(2,1)S(1)}, u32[]{:S(2)}, u32[]{:S(2)}) %collective-permute-start.2) | collective-permute-done | bytes 65568 | tf_op jit(solution)/shard_map/ppermute | solution.py:26
  17.1 0.1 collective-permute-start.6
  17.1 0.5 collective-permute-start.5
  17.6 1.5 %collective-permute-start.8 = (bf16[2,2,64,256]{3,2,1,0:T(8,128)(2,1)S(1)}, bf16[2,2,64,256]{3,2,1,0:T(8,128)(2,1)S(1)}, u32[]{:S(2)}, u32[]{:S(2)}) collective-permute-start(bf16[2,2,64,256]{3,2,1,0:T(8,128)(2,1)S(1)} %get-tuple-element.63.refs_0_), channel_id=1, source_target_pairs={{0,16},{8,24},{16,0},{24,8},{1,17},{9,25},{17,1},{25,9},{2,18},{10... | collective-permute-start | bytes 393224 | tf_op jit(solution)/shard_map/ppermute | solution.py:26
  19.2 1.3 %attend_mid.2 = (f32[256,1024]{1,0:T(8,128)S(1)}, f32[1,1024]{1,0:T(1,128)S(1)}, f32[1,1024]{1,0:T(1,128)S(1)}, f32[128,1024]{1,0:T(8,128)S(1)}) custom-call(s32[18]{0:T(128)S(1)} %pad_add_fusion.info_ref, bf16[128,1024]{1,0:T(8,128)(2,1)S(1)} %get-tuple-element.61.refs_3_.q_t, bf16[2,2,64,256]{3,2,1,0:T(8,128)(2,1)S(1)} %collective-permute-done.7.refs_0_), custom_call_target="tpu_custom_call" | custom-call | flops 268435456 | bytes 1974344 | tf_op jit(solution)/shard_map/attend_mid/pallas_call | solution.py:41
  20.4 2.6 %attend_near.1 = (f32[1024,1024]{1,0:T(8,128)S(1)}, f32[1,1024]{1,0:T(1,128)S(1)}, f32[1,1024]{1,0:T(1,128)S(1)}, f32[128,1024]{1,0:T(8,128)S(1)}) custom-call(s32[18]{0:T(128)S(1)} %pad_add_fusion.info_ref, bf16[128,1024]{1,0:T(8,128)(2,1)S(1)} %get-tuple-element.61.refs_3_.q_t, bf16[2,2,64,256]{3,2,1,0:T(8,128)(2,1)S(1)} %get-tuple-element.63.refs_0_, ...), custom_call_target="tpu_custom_call" | custom-call | flops 1073741824 | bytes 5517384 | tf_op jit(solution)/shard_map/attend_near/pallas_call | solution.py:41
  23.0 0.1 collective-permute-done.8.refs_0_
  23.1 0.5 collective-permute-start.9
  23.6 1.3 %attend_mid.3 = (f32[256,1024]{1,0:T(8,128)S(1)}, f32[1,1024]{1,0:T(1,128)S(1)}, f32[1,1024]{1,0:T(1,128)S(1)}, f32[128,1024]{1,0:T(8,128)S(1)}) custom-call(s32[18]{0:T(128)S(1)} %pad_add_fusion.info_ref, bf16[128,1024]{1,0:T(8,128)(2,1)S(1)} %get-tuple-element.61.refs_3_.q_t, bf16[2,2,64,256]{3,2,1,0:T(8,128)(2,1)S(1)} %collective-permute-done.8.refs_0_, ...), custom_call_target="tpu_custom_call" | custom-call | flops 268435456 | bytes 1978440 | tf_op jit(solution)/shard_map/attend_mid/pallas_call | solution.py:41
  24.9 3.2 %attend_far.1 = (bf16[64,1024]{1,0:T(8,128)(2,1)S(1)}, bf16[64,1024]{1,0:T(8,128)(2,1)S(1)}, f32[1,1024]{1,0:T(1,128)S(1)}, f32[1,1024]{1,0:T(1,128)S(1)}, f32[1...) custom-call(s32[18]{0:T(128)S(1)} %pad_add_fusion.info_ref, ...), custom_call_target="tpu_custom_call" | custom-call | flops 1073741824 | bytes 3973192 | tf_op jit(solution)/shard_map/attend_far/pallas_call | solution.py:41
  28.1 0.1 collective-permute-start.13
  28.2 0.5 collective-permute-start.12
  28.7 0.6 %attend_back.4 = (f32[128,1024]{1,0:T(8,128)S(1)}, bf16[2,2,64,256]{3,2,1,0:T(8,128)(2,1)S(1)}) custom-call(bf16[1024,128]{1,0:T(8,128)(2,1)S(1)} %get-tuple-element.59.q_all, bf16[1024,128]{1,0:T(8,128)(2,1)S(1)} %get-tuple-element.60.do_all, bf16[128,1024]{1,0:T(8,128)(2,1)S(1)} %get-tuple-element.62.do_t, f32[256,1024]{1,0:T(8,128)S(1)} %get-tuple-element.82.e_ref, ...), custom_call_target="tpu_custom_call" | custom-call | flops 402653184 | bytes 3153920 | tf_op jit(solution)/shard_map/attend_back/pallas_call | solution.py:41
  29.3 0.6 %attend_back.5 = (f32[128,1024]{1,0:T(8,128)S(1)}, bf16[2,2,64,256]{3,2,1,0:T(8,128)(2,1)S(1)}) custom-call(bf16[1024,128]{1,0:T(8,128)(2,1)S(1)} %get-tuple-element.59.q_all, bf16[1024,128]{1,0:T(8,128)(2,1)S(1)} %get-tuple-element.60.do_all, bf16[128,1024]{1,0:T(8,128)(2,1)S(1)} %get-tuple-element.62.do_t, f32[256,1024]{1,0:T(8,128)S(1)} %get-tuple-element.80.e_ref, ...), custom_call_target="tpu_custom_call" | custom-call | flops 402653184 | bytes 3153920 | tf_op jit(solution)/shard_map/attend_back/pallas_call | solution.py:41
  30.1 0.1 collective-permute-start.14
  30.2 1.5 %collective-permute-start.16 = (bf16[2,2,64,256]{3,2,1,0:T(8,128)(2,1)S(1)}, bf16[2,2,64,256]{3,2,1,0:T(8,128)(2,1)S(1)}, u32[]{:S(2)}, u32[]{:S(2)}) collective-permute-start(bf16[2,2,64,256]{3,2,1,0:T(8,128)(2,1)S(1)} %sum_cores.3), channel_id=1, source_target_pairs={{0,16},{8,24},{16,0},{24,8},{1,17},{9,25},{17,1},{25,9},{2,18},{10... | collective-permute-start | bytes 393224 | tf_op jit(solution)/shard_map/ppermute | solution.py:26
  31.7 1.1 %attend_back.6 = (f32[128,1024]{1,0:T(8,128)S(1)}, bf16[2,2,64,256]{3,2,1,0:T(8,128)(2,1)S(1)}, bf16[2,2,64,256]{3,2,1,0:T(8,128)(2,1)S(1)}) custom-call(bf16[1024,128]{1,0:T(8,128)(2,1)S(1)} %get-tuple-element.59.q_all, bf16[1024,128]{1,0:T(8,128)(2,1)S(1)} %get-tuple-element.60.do_all, bf16[128,1024]{1,0:T(8,128)(2,1)S(1)} %get-tuple-element.62.do_t, ...), custom_call_target="tpu_custom_call" | custom-call | flops 805306368 | bytes 6578176 | tf_op jit(solution)/shard_map/attend_back/pallas_call | solution.py:41
  32.8 0.1 collective-permute-start.17
  32.9 1.2 %collective-permute-start.20 = (bf16[2,2,64,256]{3,2,1,0:T(8,128)(2,1)S(1)}, bf16[2,2,64,256]{3,2,1,0:T(8,128)(2,1)S(1)}, u32[]{:S(2)}, u32[]{:S(2)}) collective-permute-start(bf16[2,2,64,256]{3,2,1,0:T(8,128)(2,1)S(1)} %sum_cores.2), channel_id=1, source_target_pairs={{0,16},{8,24},{16,0},{24,8},{1,17},{9,25},{17,1},{25,9},{2,18},{10... | collective-permute-start | bytes 393224 | tf_op jit(solution)/shard_map/ppermute | solution.py:26
  34.1 1.2 %attend_back.7 = (bf16[64,1024]{1,0:T(8,128)(2,1)S(1)}, bf16[64,1024]{1,0:T(8,128)(2,1)S(1)}, bf16[2,2,64,256]{3,2,1,0:T(8,128)(2,1)S(1)}, bf16[2,2,64,256]{3,2,1,0:T(8,128)(2,1)S(1)}) custom-call(bf16[1024,128]{1,0:T(8,128)(2,1)S(1)} %get-tuple-element.59.q_all, bf16[1024,128]{1,0:T(8,128)(2,1)S(1)} %get-tuple-element.60.do_all, ...), custom_call_target="tpu_custom_call" | custom-call | flops 805306368 | bytes 6316032 | tf_op jit(solution)/shard_map/attend_back/pallas_call | solution.py:41
  35.3 0.8 %collective-permute-done.16.refs_0_ = bf16[2,2,64,256]{3,2,1,0:T(8,128)(2,1)S(1)} collective-permute-done((bf16[2,2,64,256]{3,2,1,0:T(8,128)(2,1)S(1)}, bf16[2,2,64,256]{3,2,1,0:T(8,128)(2,1)S(1)}, u32[]{:S(2)}, u32[]{:S(2)}) %collective-permute-start.16) | collective-permute-done | bytes 131104 | tf_op jit(solution)/shard_map/ppermute | solution.py:26
  36.1 0.1 sum_heads.2
  36.1 0.9 %collective-permute-start.18 = (bf16[2,64,256]{2,1,0:T(8,128)(2,1)S(1)}, bf16[2,64,256]{2,1,0:T(8,128)(2,1)S(1)}, u32[]{:S(2)}, u32[]{:S(2)}) collective-permute-start(bf16[2,64,256]{2,1,0:T(8,128)(2,1)S(1)} %get-tuple-element.100), channel_id=1, source_target_pairs={{0,4},{1,5},{2,6},{3,7},{4,0},{5,1},{6,2},{7,3},{8,12},{9,13},{10,... | collective-permute-start | bytes 196616 | tf_op jit(solution)/shard_map/ppermute | solution.py:26
  37.0 1.7 %collective-permute-start.19 = (bf16[2,64,256]{2,1,0:T(8,128)(2,1)S(1)}, bf16[2,64,256]{2,1,0:T(8,128)(2,1)S(1)}, u32[]{:S(2)}, u32[]{:S(2)}) collective-permute-start(bf16[2,64,256]{2,1,0:T(8,128)(2,1)S(1)} %get-tuple-element.101), channel_id=1, source_target_pairs={{0,6},{1,7},{2,4},{3,5},{4,2},{5,3},{6,0},{7,1},{8,14},{9,15},{10,... | collective-permute-start | bytes 196616 | tf_op jit(solution)/shard_map/ppermute | solution.py:26
  38.7 1.5 %collective-permute-start.11 = (bf16[64,1024]{1,0:T(8,128)(2,1)S(1)}, bf16[64,1024]{1,0:T(8,128)(2,1)S(1)}, u32[]{:S(2)}, u32[]{:S(2)}) collective-permute-start(bf16[64,1024]{1,0:T(8,128)(2,1)S(1)} %get-tuple-element.76), channel_id=1, source_target_pairs={{0,8},{8,0},{16,24},{24,16},{1,9},{9,1},{17,25},{25,17},{2,10},{10... | collective-permute-start | bytes 393224 | tf_op jit(solution)/shard_map/ppermute | solution.py:26
  40.2 0.5 %collective-permute-start.15 = (bf16[64,1024]{1,0:T(8,128)(2,1)S(1)}, bf16[64,1024]{1,0:T(8,128)(2,1)S(1)}, u32[]{:S(2)}, u32[]{:S(2)}) collective-permute-start(bf16[64,1024]{1,0:T(8,128)(2,1)S(1)} %get-tuple-element.95), channel_id=1, source_target_pairs={{0,8},{8,0},{16,24},{24,16},{1,9},{9,1},{17,25},{25,17},{2,10},{10... | collective-permute-start | bytes 393224 | tf_op jit(solution)/shard_map/ppermute | solution.py:26
  40.7 0.1 sum_heads.3
  40.8 1.0 %collective-permute-start.22 = (bf16[2,64,256]{2,1,0:T(8,128)(2,1)S(1)}, bf16[2,64,256]{2,1,0:T(8,128)(2,1)S(1)}, u32[]{:S(2)}, u32[]{:S(2)}) collective-permute-start(bf16[2,64,256]{2,1,0:T(8,128)(2,1)S(1)} %get-tuple-element.105), channel_id=1, source_target_pairs={{0,2},{1,3},{2,0},{3,1},{4,6},{5,7},{6,4},{7,5},{8,10},{9,11},{10,... | collective-permute-start | bytes 196616 | tf_op jit(solution)/shard_map/ppermute | solution.py:26
  41.8 1.8 %collective-permute-done.18.refs_0_ = bf16[2,64,256]{2,1,0:T(8,128)(2,1)S(1)} collective-permute-done((bf16[2,64,256]{2,1,0:T(8,128)(2,1)S(1)}, bf16[2,64,256]{2,1,0:T(8,128)(2,1)S(1)}, u32[]{:S(2)}, u32[]{:S(2)}) %collective-permute-start.18) | collective-permute-done | bytes 65568 | tf_op jit(solution)/shard_map/ppermute | solution.py:26
  43.7 1.4 %collective-permute-done.22.refs_2_ = bf16[2,64,256]{2,1,0:T(8,128)(2,1)S(1)} collective-permute-done((bf16[2,64,256]{2,1,0:T(8,128)(2,1)S(1)}, bf16[2,64,256]{2,1,0:T(8,128)(2,1)S(1)}, u32[]{:S(2)}, u32[]{:S(2)}) %collective-permute-start.22) | collective-permute-done | bytes 65568 | tf_op jit(solution)/shard_map/ppermute | solution.py:26
  45.1 1.6 %collective-permute-start.23 = (bf16[64,256]{1,0:T(8,128)(2,1)S(1)}, bf16[64,256]{1,0:T(8,128)(2,1)S(1)}, u32[]{:S(2)}, u32[]{:S(2)}) collective-permute-start(bf16[64,256]{1,0:T(8,128)(2,1)S(1)} %get-tuple-element.107), channel_id=1, source_target_pairs={{0,8},{8,0},{16,24},{24,16},{1,9},{9,1},{17,25},{25,17},{2,10},{10... | collective-permute-start | bytes 98312 | tf_op jit(solution)/shard_map/ppermute | solution.py:26
  46.7 0.8 %finish_q.1 = (bf16[64,2048]{1,0:T(8,128)(2,1)}, bf16[64,2048]{1,0:T(8,128)(2,1)}) custom-call(s32[1]{0:T(128)} %bitcast.group_ref, bf16[64,1024]{1,0:T(8,128)(2,1)S(1)} %get-tuple-element.75.refs_0_, bf16[64,1024]{1,0:T(8,128)(2,1)S(1)} %collective-permute-done.11.refs_1_, bf16[64,1024]{1,0:T(8,128)(2,1)S(1)} %get-tuple-element.94.refs_2_, ...), custom_call_target="tpu_custom_call" | custom-call | bytes 1048580 | tf_op jit(solution)/shard_map/finish_q/pallas_call | solution.py:41
  47.6 1.6 %collective-permute-done.23.refs_1_ = bf16[64,256]{1,0:T(8,128)(2,1)S(1)} collective-permute-done((bf16[64,256]{1,0:T(8,128)(2,1)S(1)}, bf16[64,256]{1,0:T(8,128)(2,1)S(1)}, u32[]{:S(2)}, u32[]{:S(2)}) %collective-permute-start.23) | collective-permute-done | bytes 32800 | tf_op jit(solution)/shard_map/ppermute | solution.py:26
  49.1 0.6 %finish_kv.1 = (bf16[64,256]{1,0:T(8,128)(2,1)}, bf16[64,256]{1,0:T(8,128)(2,1)}) custom-call(s32[1]{0:T(128)} %bitcast.group_ref, bf16[64,256]{1,0:T(8,128)(2,1)S(1)} %get-tuple-element.106.refs_0_, bf16[64,256]{1,0:T(8,128)(2,1)S(1)} %collective-permute-done.23.refs_1_), custom_call_target="tpu_custom_call" | custom-call | bytes 131076 | tf_op jit(solution)/shard_map/finish_kv/pallas_call | solution.py:41
  (30 shorter events, 0.2 us)
Async XLA Ops:
  1.4 5.0 %collective-permute-start.1 = (bf16[64,256]{1,0:T(8,128)(2,1)S(1)}, bf16[64,256]{1,0:T(8,128)(2,1)S(1)}, u32[]{:S(2)}, u32[]{:S(2)}) collective-permute-start(bf16[64,256]{1,0:T(8,128)(2,1)S(1)} %pad_maximum_fusion.1), channel_id=1, source_target_pairs={{0,8},{8,0},{16,24},{24,16},{1,9},{9,1},{17,25},{25,17},{2,10},{10... | collective-permute-start | bytes 98312 | tf_op jit(solution)/shard_map/ppermute | solution.py:26
  4.4 0.9 %copy-start = (bf16[2,32,2048]{2,1,0:T(8,128)(2,1)S(1)}, bf16[2,32,2048]{2,1,0:T(8,128)(2,1)}, u32[]{:S(2)}) copy-start(bf16[2,32,2048]{2,1,0:T(8,128)(2,1)} %param.5) | copy-start | bytes 786436
  5.4 0.9 %copy-start.1 = (bf16[2,32,2048]{2,1,0:T(8,128)(2,1)S(1)}, bf16[2,32,2048]{2,1,0:T(8,128)(2,1)}, u32[]{:S(2)}) copy-start(bf16[2,32,2048]{2,1,0:T(8,128)(2,1)} %param.8) | copy-start | bytes 786436
  6.4 7.8 %collective-permute-start = (bf16[2,64,1024]{2,1,0:T(8,128)(2,1)S(1)}, bf16[2,64,1024]{2,1,0:T(8,128)(2,1)S(1)}, u32[]{:S(2)}, u32[]{:S(2)}) collective-permute-start(bf16[2,64,1024]{2,1,0:T(8,128)(2,1)S(1)} %get-tuple-element.58), channel_id=1, source_target_pairs={{0,8},{8,0},{16,24},{24,16},{1,9},{9,1},{17,25},{25,17},{2,10},{10... | collective-permute-start | bytes 786440 | tf_op jit(solution)/shard_map/ppermute | solution.py:26
  6.5 4.7 %collective-permute-start.4 = (bf16[2,64,256]{2,1,0:T(8,128)(2,1)S(1)}, bf16[2,64,256]{2,1,0:T(8,128)(2,1)S(1)}, u32[]{:S(2)}, u32[]{:S(2)}) collective-permute-start(bf16[2,64,256]{2,1,0:T(8,128)(2,1)S(1)} %pad_maximum_fusion.refs_0_), channel_id=1, source_target_pairs={{0,2},{1,3},{2,0},{3,1},{4,6},{5,7},{6,4},{7,5},{8,10},{9,11},{10,... | collective-permute-start | bytes 196616 | tf_op jit(solution)/shard_map/ppermute | solution.py:26
  8.7 6.3 %collective-permute-start.3 = (bf16[2,64,256]{2,1,0:T(8,128)(2,1)S(1)}, bf16[2,64,256]{2,1,0:T(8,128)(2,1)S(1)}, u32[]{:S(2)}, u32[]{:S(2)}) collective-permute-start(bf16[2,64,256]{2,1,0:T(8,128)(2,1)S(1)} %pad_maximum_fusion.refs_0_), channel_id=1, source_target_pairs={{0,6},{1,7},{2,4},{3,5},{4,2},{5,3},{6,0},{7,1},{8,14},{9,15},{10,... | collective-permute-start | bytes 196616 | tf_op jit(solution)/shard_map/ppermute | solution.py:26
  11.1 5.9 %collective-permute-start.2 = (bf16[2,64,256]{2,1,0:T(8,128)(2,1)S(1)}, bf16[2,64,256]{2,1,0:T(8,128)(2,1)S(1)}, u32[]{:S(2)}, u32[]{:S(2)}) collective-permute-start(bf16[2,64,256]{2,1,0:T(8,128)(2,1)S(1)} %pad_maximum_fusion.refs_0_), channel_id=1, source_target_pairs={{0,4},{1,5},{2,6},{3,7},{4,0},{5,1},{6,2},{7,3},{8,12},{9,13},{10,... | collective-permute-start | bytes 196616 | tf_op jit(solution)/shard_map/ppermute | solution.py:26
  11.3 7.9 %collective-permute-start.7 = (bf16[2,2,64,256]{3,2,1,0:T(8,128)(2,1)S(1)}, bf16[2,2,64,256]{3,2,1,0:T(8,128)(2,1)S(1)}, u32[]{:S(2)}, u32[]{:S(2)}) collective-permute-start(bf16[2,2,64,256]{3,2,1,0:T(8,128)(2,1)S(1)} %stack.22.refs_2_.refs_1_), channel_id=1, source_target_pairs={{0,16},{8,24},{16,0},{24,8},{1,17},{9,25},{17,1},{25,9},{2,18},{10... | collective-permute-start | bytes 393224 | tf_op jit(solution)/shard_map/ppermute | solution.py:26
  17.1 3.4 %collective-permute-start.6 = (bf16[2,2,64,256]{3,2,1,0:T(8,128)(2,1)S(1)}, bf16[2,2,64,256]{3,2,1,0:T(8,128)(2,1)S(1)}, u32[]{:S(2)}, u32[]{:S(2)}) collective-permute-start(bf16[2,2,64,256]{3,2,1,0:T(8,128)(2,1)S(1)} %get-tuple-element.64), channel_id=1, source_target_pairs={{0,1},{1,0},{2,3},{3,2},{4,5},{5,4},{6,7},{7,6},{8,9},{9,8},{10,11... | collective-permute-start | bytes 393224 | tf_op jit(solution)/shard_map/ppermute | solution.py:26
  17.1 3.3 %collective-permute-start.5 = (bf16[2,2,64,256]{3,2,1,0:T(8,128)(2,1)S(1)}, bf16[2,2,64,256]{3,2,1,0:T(8,128)(2,1)S(1)}, u32[]{:S(2)}, u32[]{:S(2)}) collective-permute-start(bf16[2,2,64,256]{3,2,1,0:T(8,128)(2,1)S(1)} %get-tuple-element.63.refs_0_), channel_id=1, source_target_pairs={{0,1},{1,0},{2,3},{3,2},{4,5},{5,4},{6,7},{7,6},{8,9},{9,8},{10,11... | collective-permute-start | bytes 393224 | tf_op jit(solution)/shard_map/ppermute | solution.py:26
  17.6 5.5 %collective-permute-start.8 = (bf16[2,2,64,256]{3,2,1,0:T(8,128)(2,1)S(1)}, bf16[2,2,64,256]{3,2,1,0:T(8,128)(2,1)S(1)}, u32[]{:S(2)}, u32[]{:S(2)}) collective-permute-start(bf16[2,2,64,256]{3,2,1,0:T(8,128)(2,1)S(1)} %get-tuple-element.63.refs_0_), channel_id=1, source_target_pairs={{0,16},{8,24},{16,0},{24,8},{1,17},{9,25},{17,1},{25,9},{2,18},{10... | collective-permute-start | bytes 393224 | tf_op jit(solution)/shard_map/ppermute | solution.py:26
  19.2 5.7 %collective-permute-start.10 = (bf16[2,2,64,256]{3,2,1,0:T(8,128)(2,1)S(1)}, bf16[2,2,64,256]{3,2,1,0:T(8,128)(2,1)S(1)}, u32[]{:S(2)}, u32[]{:S(2)}) collective-permute-start(bf16[2,2,64,256]{3,2,1,0:T(8,128)(2,1)S(1)} %collective-permute-done.7.refs_0_), channel_id=1, source_target_pairs={{0,1},{1,0},{2,3},{3,2},{4,5},{5,4},{6,7},{7,6},{8,9},{9,8},{10,11... | collective-permute-start | bytes 393224 | tf_op jit(solution)/shard_map/ppermute | solution.py:26
  23.1 1.8 %collective-permute-start.9 = (bf16[2,2,64,256]{3,2,1,0:T(8,128)(2,1)S(1)}, bf16[2,2,64,256]{3,2,1,0:T(8,128)(2,1)S(1)}, u32[]{:S(2)}, u32[]{:S(2)}) collective-permute-start(bf16[2,2,64,256]{3,2,1,0:T(8,128)(2,1)S(1)} %collective-permute-done.8.refs_0_), channel_id=1, source_target_pairs={{0,1},{1,0},{2,3},{3,2},{4,5},{5,4},{6,7},{7,6},{8,9},{9,8},{10,11... | collective-permute-start | bytes 393224 | tf_op jit(solution)/shard_map/ppermute | solution.py:26
  28.1 1.9 %collective-permute-start.13 = (bf16[2,2,64,256]{3,2,1,0:T(8,128)(2,1)S(1)}, bf16[2,2,64,256]{3,2,1,0:T(8,128)(2,1)S(1)}, u32[]{:S(2)}, u32[]{:S(2)}) collective-permute-start(bf16[2,2,64,256]{3,2,1,0:T(8,128)(2,1)S(1)} %get-tuple-element.90), channel_id=1, source_target_pairs={{0,1},{1,0},{2,3},{3,2},{4,5},{5,4},{6,7},{7,6},{8,9},{9,8},{10,11... | collective-permute-start | bytes 393224 | tf_op jit(solution)/shard_map/ppermute | solution.py:26
  28.2 1.8 %collective-permute-start.12 = (bf16[2,2,64,256]{3,2,1,0:T(8,128)(2,1)S(1)}, bf16[2,2,64,256]{3,2,1,0:T(8,128)(2,1)S(1)}, u32[]{:S(2)}, u32[]{:S(2)}) collective-permute-start(bf16[2,2,64,256]{3,2,1,0:T(8,128)(2,1)S(1)} %get-tuple-element.88), channel_id=1, source_target_pairs={{0,1},{1,0},{2,3},{3,2},{4,5},{5,4},{6,7},{7,6},{8,9},{9,8},{10,11... | collective-permute-start | bytes 393224 | tf_op jit(solution)/shard_map/ppermute | solution.py:26
  30.1 1.6 %collective-permute-start.14 = (bf16[64,128]{1,0:T(8,128)(2,1)S(1)}, bf16[64,128]{1,0:T(8,128)(2,1)S(1)}, u32[]{:S(2)}, u32[]{:S(2)}) collective-permute-start(bf16[64,128]{1,0:T(8,128)(2,1)S(1)} %slice_bitcast_fusion), channel_id=1, source_target_pairs={{0,1},{1,0},{2,3},{3,2},{4,5},{5,4},{6,7},{7,6},{8,9},{9,8},{10,11... | collective-permute-start | bytes 49160 | tf_op jit(solution)/shard_map/ppermute | solution.py:26
  30.2 5.8 %collective-permute-start.16 = (bf16[2,2,64,256]{3,2,1,0:T(8,128)(2,1)S(1)}, bf16[2,2,64,256]{3,2,1,0:T(8,128)(2,1)S(1)}, u32[]{:S(2)}, u32[]{:S(2)}) collective-permute-start(bf16[2,2,64,256]{3,2,1,0:T(8,128)(2,1)S(1)} %sum_cores.3), channel_id=1, source_target_pairs={{0,16},{8,24},{16,0},{24,8},{1,17},{9,25},{17,1},{25,9},{2,18},{10... | collective-permute-start | bytes 393224 | tf_op jit(solution)/shard_map/ppermute | solution.py:26
  32.8 3.2 %collective-permute-start.17 = (bf16[2,2,64,256]{3,2,1,0:T(8,128)(2,1)S(1)}, bf16[2,2,64,256]{3,2,1,0:T(8,128)(2,1)S(1)}, u32[]{:S(2)}, u32[]{:S(2)}) collective-permute-start(bf16[2,2,64,256]{3,2,1,0:T(8,128)(2,1)S(1)} %get-tuple-element.98), channel_id=1, source_target_pairs={{0,1},{1,0},{2,3},{3,2},{4,5},{5,4},{6,7},{7,6},{8,9},{9,8},{10,11... | collective-permute-start | bytes 393224 | tf_op jit(solution)/shard_map/ppermute | solution.py:26
  32.9 7.3 %collective-permute-start.20 = (bf16[2,2,64,256]{3,2,1,0:T(8,128)(2,1)S(1)}, bf16[2,2,64,256]{3,2,1,0:T(8,128)(2,1)S(1)}, u32[]{:S(2)}, u32[]{:S(2)}) collective-permute-start(bf16[2,2,64,256]{3,2,1,0:T(8,128)(2,1)S(1)} %sum_cores.2), channel_id=1, source_target_pairs={{0,16},{8,24},{16,0},{24,8},{1,17},{9,25},{17,1},{25,9},{2,18},{10... | collective-permute-start | bytes 393224 | tf_op jit(solution)/shard_map/ppermute | solution.py:26
  34.1 6.7 %collective-permute-start.21 = (bf16[2,2,64,256]{3,2,1,0:T(8,128)(2,1)S(1)}, bf16[2,2,64,256]{3,2,1,0:T(8,128)(2,1)S(1)}, u32[]{:S(2)}, u32[]{:S(2)}) collective-permute-start(bf16[2,2,64,256]{3,2,1,0:T(8,128)(2,1)S(1)} %get-tuple-element.102), channel_id=1, source_target_pairs={{0,1},{1,0},{2,3},{3,2},{4,5},{5,4},{6,7},{7,6},{8,9},{9,8},{10,11... | collective-permute-start | bytes 393224 | tf_op jit(solution)/shard_map/ppermute | solution.py:26
  36.1 7.6 %collective-permute-start.18 = (bf16[2,64,256]{2,1,0:T(8,128)(2,1)S(1)}, bf16[2,64,256]{2,1,0:T(8,128)(2,1)S(1)}, u32[]{:S(2)}, u32[]{:S(2)}) collective-permute-start(bf16[2,64,256]{2,1,0:T(8,128)(2,1)S(1)} %get-tuple-element.100), channel_id=1, source_target_pairs={{0,4},{1,5},{2,6},{3,7},{4,0},{5,1},{6,2},{7,3},{8,12},{9,13},{10,... | collective-permute-start | bytes 196616 | tf_op jit(solution)/shard_map/ppermute | solution.py:26
  37.0 6.7 %collective-permute-start.19 = (bf16[2,64,256]{2,1,0:T(8,128)(2,1)S(1)}, bf16[2,64,256]{2,1,0:T(8,128)(2,1)S(1)}, u32[]{:S(2)}, u32[]{:S(2)}) collective-permute-start(bf16[2,64,256]{2,1,0:T(8,128)(2,1)S(1)} %get-tuple-element.101), channel_id=1, source_target_pairs={{0,6},{1,7},{2,4},{3,5},{4,2},{5,3},{6,0},{7,1},{8,14},{9,15},{10,... | collective-permute-start | bytes 196616 | tf_op jit(solution)/shard_map/ppermute | solution.py:26
  38.7 8.0 %collective-permute-start.11 = (bf16[64,1024]{1,0:T(8,128)(2,1)S(1)}, bf16[64,1024]{1,0:T(8,128)(2,1)S(1)}, u32[]{:S(2)}, u32[]{:S(2)}) collective-permute-start(bf16[64,1024]{1,0:T(8,128)(2,1)S(1)} %get-tuple-element.76), channel_id=1, source_target_pairs={{0,8},{8,0},{16,24},{24,16},{1,9},{9,1},{17,25},{25,17},{2,10},{10... | collective-permute-start | bytes 393224 | tf_op jit(solution)/shard_map/ppermute | solution.py:26
  40.2 6.5 %collective-permute-start.15 = (bf16[64,1024]{1,0:T(8,128)(2,1)S(1)}, bf16[64,1024]{1,0:T(8,128)(2,1)S(1)}, u32[]{:S(2)}, u32[]{:S(2)}) collective-permute-start(bf16[64,1024]{1,0:T(8,128)(2,1)S(1)} %get-tuple-element.95), channel_id=1, source_target_pairs={{0,8},{8,0},{16,24},{24,16},{1,9},{9,1},{17,25},{25,17},{2,10},{10... | collective-permute-start | bytes 393224 | tf_op jit(solution)/shard_map/ppermute | solution.py:26
  40.8 4.3 %collective-permute-start.22 = (bf16[2,64,256]{2,1,0:T(8,128)(2,1)S(1)}, bf16[2,64,256]{2,1,0:T(8,128)(2,1)S(1)}, u32[]{:S(2)}, u32[]{:S(2)}) collective-permute-start(bf16[2,64,256]{2,1,0:T(8,128)(2,1)S(1)} %get-tuple-element.105), channel_id=1, source_target_pairs={{0,2},{1,3},{2,0},{3,1},{4,6},{5,7},{6,4},{7,5},{8,10},{9,11},{10,... | collective-permute-start | bytes 196616 | tf_op jit(solution)/shard_map/ppermute | solution.py:26
  45.1 4.0 %collective-permute-start.23 = (bf16[64,256]{1,0:T(8,128)(2,1)S(1)}, bf16[64,256]{1,0:T(8,128)(2,1)S(1)}, u32[]{:S(2)}, u32[]{:S(2)}) collective-permute-start(bf16[64,256]{1,0:T(8,128)(2,1)S(1)} %get-tuple-element.107), channel_id=1, source_target_pairs={{0,8},{8,0},{16,24},{24,16},{1,9},{9,1},{17,25},{25,17},{2,10},{10... | collective-permute-start | bytes 98312 | tf_op jit(solution)/shard_map/ppermute | solution.py:26

commit v11 on v10

--- a/solution.py
+++ b/solution.py
@@ -91,6 +91,7 @@
         self.lanes = group * self.tile_rows
         self.query_rows = kv * group * rows
         self.chunk_keys = self.z_part * kv * rows
+        self.slices = self.chunk_keys // block_rows
         self.tiles = [(s, start) for s in range(kv) for start in range(0, rows, self.tile_rows)]
 
     def zone(self, part):
@@ -113,16 +114,24 @@
             pos = jnp.where(row // self.block_rows == b, first + row % self.block_rows, pos)
         return pos - lax.broadcasted_iota(jnp.int32, (self.block_rows, self.lanes), 0)
 
-    def masked(self, scores, gap, chunk, info_ref):
+    def firsts(self, chunk, info_ref):
         head, ctx = info_ref[0], info_ref[1]
         a, core, part = chunk
-        for j in range(self.chunk_keys // self.block_rows):
+        for j in range(self.slices):
             m, rest = divmod(j, self.kv * self.blocks)
             s, b = divmod(rest, self.blocks)
             stored = (ctx ^ (self.zone(part)[m] * self.cores + core)) * self.blocks + b
-            first = info_ref[2 + stored] * self.block_len + (head ^ (a * self.kv + s)) * self.block_rows
-            block = scores[j * self.block_rows : (j + 1) * self.block_rows]
-            yield j * self.block_rows, jnp.where(gap >= first, block, LOWEST)
+            yield info_ref[2 + stored] * self.block_len + (head ^ (a * self.kv + s)) * self.block_rows
+
+    def first_at(self, chunk):
+        a, core, part = chunk
+        return ((a * self.cores + core) * self.parts + part) * self.slices
+
+    def masked(self, scores, gap, chunk, first_ref):
+        for j in range(self.slices):
+            row = j * self.block_rows
+            first = first_ref[pl.ds(self.first_at(chunk) + j, 1), :]
+            yield row, jnp.where(gap >= first, scores[row : row + self.block_rows], LOWEST)
 
     def turn(self, kv_refs, turned_ref):
         for i, ref in enumerate(kv_refs):
@@ -137,12 +146,12 @@
     def fold(self, block):
         return block.reshape(block.shape[0] // 8, 8, self.lanes)
 
-    def scores(self, tile, chunks, kv_refs, q_t, e_ref, cols, info_ref):
-        gap = self.gap(tile, info_ref)
+    def scores(self, tile, chunks, kv_refs, q_t, e_ref, cols, gap_ref, first_ref):
+        gap = gap_ref[pl.ds(tile * self.block_rows, self.block_rows), :]
         top = jnp.full((8, self.lanes), FLOOR, F32)
         for i, ref in enumerate(kv_refs):
             scores = dot(self.keys(ref), q_t)
-            for row, part in self.masked(scores, gap, chunks[i], info_ref):
+            for row, part in self.masked(scores, gap, chunks[i], first_ref):
                 e_ref[pl.ds(i * self.chunk_keys + row, part.shape[0]), cols] = part
                 top = jnp.maximum(top, jnp.max(self.fold(part), axis=0))
         return jnp.max(top, axis=0, keepdims=True)
@@ -155,12 +164,12 @@
             total = total + jnp.sum(self.fold(part), axis=0)
         return jnp.sum(total, axis=0, keepdims=True)
 
-    def store_heads(self, out_ref, tile, turned):
+    def store_heads(self, out_ref, kind, tile, turned):
         s, start = self.tiles[tile]
         block = turned.T.astype(BF)
         for n in range(self.group):
             piece = block[n * self.tile_rows : (n + 1) * self.tile_rows]
-            out_ref[pl.ds(start, self.tile_rows), pl.ds(n * HD, HD)] = piece
+            out_ref[kind, pl.ds(start, self.tile_rows), pl.ds(n * HD, HD)] = piece
 
     def back(self, dkv_refs, p_ref, ds_ref, q_ref, do_ref):
         shape = (self.z_part, self.kv, self.rows, HD)
@@ -170,10 +179,10 @@
             out_ref[:, :, :, HD:] = dot(p_ref[at, :], do_ref[...]).astype(BF).reshape(shape)
 
 
-def forward_part(plan, chunks, info_ref, q_t, kv_refs, e_ref, top_ref, sum_ref, mix_ref, turned_ref):
+def forward_part(plan, chunks, gap_ref, first_ref, q_t, kv_refs, e_ref, top_ref, sum_ref, mix_ref, turned_ref):
     spans = [plan.at(tile) for tile in range(len(plan.tiles))]
     tops = [
-        plan.scores(tile, chunks, kv_refs, q_t[:, at], e_ref, at, info_ref)
+        plan.scores(tile, chunks, kv_refs, q_t[:, at], e_ref, at, gap_ref, first_ref)
         for tile, at in enumerate(spans)
     ]
     plan.turn(kv_refs, turned_ref)
@@ -188,8 +197,8 @@
         mix_ref[:, at] = mixed
 
 
-def turn_kernel(plan, info_ref, *refs):
-    q_parts, (q_all, do_all, q_t, do_t) = refs[:-4], refs[-4:]
+def turn_kernel(plan, chunks, info_ref, *refs):
+    q_parts, (q_all, do_all, q_t, do_t, gap_ref, first_ref) = refs[:-6], refs[-6:]
     for tile, (s, start) in enumerate(plan.tiles):
         span = pl.ds(start, plan.tile_rows)
         for n in range(plan.group):
@@ -199,29 +208,33 @@
         at = plan.at(tile)
         q_t[:, at] = q_all[at, :].T
         do_t[:, at] = do_all[at, :].T
-
-
-def part_kernel(plan, chunks, info_ref, q_t, *refs):
-    forward_part(plan, chunks, info_ref, q_t, refs[: len(chunks)], *refs[-5:])
-
-
-def far_kernel(plan, chunks, others, info_ref, q_all, do_all, q_t, do_t, *refs):
-    kv, count = plan.kv, len(chunks)
+        gap_ref[pl.ds(tile * plan.block_rows, plan.block_rows), :] = plan.gap(tile, info_ref)
+    for chunk in chunks:
+        for j, first in enumerate(plan.firsts(chunk, info_ref)):
+            first_ref[pl.ds(plan.first_at(chunk) + j, 1), :] = jnp.full((1, plan.lanes), first, jnp.int32)
+
+
+def part_kernel(plan, chunks, gap_ref, first_ref, q_t, *refs):
+    forward_part(plan, chunks, gap_ref, first_ref, q_t, refs[: len(chunks)], *refs[-5:])
+
+
+def far_kernel(plan, chunks, others, gap_ref, first_ref, q_all, do_all, q_t, do_t, *refs):
+    count = len(chunks)
     partial, refs = [refs[3 * i : 3 * i + 3] for i in range(others)], refs[3 * others :]
     kv_refs, refs = refs[:count], refs[count:]
-    att_refs, refs = refs[:kv], refs[kv:]
-    scale_refs, (delta_ref, q_grad_ref), refs = refs[:others], refs[others : others + 2], refs[others + 2 :]
+    scale_refs, refs = refs[:others], refs[others:]
+    (delta_ref, mixed_ref, q_grad_ref), refs = refs[:3], refs[3:]
     dkv_refs, (turned_ref, e_ref, w_ref, p_ref, ds_ref) = refs[:-5], refs[-5:]
     spans = [plan.at(tile) for tile in range(len(plan.tiles))]
     tops = [
-        plan.scores(tile, chunks, kv_refs, q_t[:, at], e_ref, at, info_ref)
+        plan.scores(tile, chunks, kv_refs, q_t[:, at], e_ref, at, gap_ref, first_ref)
         for tile, at in enumerate(spans)
     ]
     plan.turn(kv_refs, turned_ref)
     for at in spans:
         for i, ref in enumerate(kv_refs):
             w_ref[plan.keys_at(i), at] = dot(plan.values(ref), do_t[:, at])
-    inverses, mixes = [], []
+    inverses = []
     for at, top in zip(spans, tops):
         for top_ref, _, _ in partial:
             top = jnp.maximum(top, top_ref[:, at])
@@ -241,9 +254,9 @@
             probs = (e_ref[plan.keys_at(i), at] * inverse).astype(BF)
             p_ref[plan.keys_at(i), at] = probs
             mixed = mixed + dot(turned_ref[pl.ds(HD, HD), plan.keys_at(i)], probs)
-        mixes.append(mixed.astype(BF).astype(F32))
-    for at, mixed in zip(spans, mixes):
-        delta_ref[:, at] = jnp.sum(do_t[:, at].astype(F32) * mixed, axis=0, keepdims=True)
+        mixed = mixed.astype(BF)
+        mixed_ref[:, at] = mixed
+        delta_ref[:, at] = jnp.sum(do_t[:, at].astype(F32) * mixed.astype(F32), axis=0, keepdims=True)
     for at, inverse in zip(spans, inverses):
         q_grad = jnp.zeros((HD, plan.lanes), F32)
         for i in range(count):
@@ -253,12 +266,11 @@
             q_grad = q_grad + dot(turned_ref[pl.ds(0, HD), plan.keys_at(i)], grad_s)
         q_grad_ref[:, at] = q_grad
     plan.back(dkv_refs, p_ref, ds_ref, q_all, do_all)
-    for tile, mixed in enumerate(mixes):
-        plan.store_heads(att_refs[plan.tiles[tile][0]], tile, mixed)
 
 
 def back_kernel(plan, rows_at, last, order, q_all, do_all, do_t, e_ref, scale_ref, delta_ref, q_grad_in, *refs):
     count = len(rows_at)
+    mixed_ref, refs = refs[:last], refs[last:]
     kv_refs, refs = refs[:count], refs[count + order :]
     refs, (turned_ref, p_ref, ds_ref) = refs[:-3], refs[-3:]
     outs, dkv_refs = refs[:-count], refs[-count:]
@@ -276,7 +288,9 @@
         for i in range(count):
             q_grad = q_grad + dot(turned_ref[pl.ds(0, HD), plan.keys_at(i)], ds_ref[plan.keys_at(i), at])
         if last:
-            plan.store_heads(outs[plan.tiles[tile][0]], tile, q_grad * SCALING)
+            out_ref = outs[plan.tiles[tile][0]]
+            plan.store_heads(out_ref, 0, tile, mixed_ref[0][:, at].astype(F32))
+            plan.store_heads(out_ref, 1, tile, q_grad * SCALING)
         else:
             outs[0][:, at] = q_grad
 
@@ -313,7 +327,7 @@
 
 
 def finish_kv_kernel(kv, group_ref, *refs):
-    key_ref, value_ref = refs[kv:]
+    key_ref, value_ref = refs[kv + 1 :]
     for g in range(kv):
 
         @pl.when(group_ref[0] == g)
@@ -325,16 +339,17 @@
 
 
 def finish_q_kernel(kv, group_ref, *refs):
-    att_ref, grad_ref = refs[2 * kv :]
-    width = refs[0].shape[1]
+    att_ref, grad_ref, done_ref = refs[kv:]
+    done_ref[...] = jnp.zeros_like(done_ref)
+    width = refs[0].shape[2]
     for g in range(kv):
 
         @pl.when(group_ref[0] == g)
         def _():
             for s in range(kv):
                 cols = pl.ds((g ^ s) * width, width)
-                att_ref[:, cols] = refs[s][...]
-                grad_ref[:, cols] = refs[kv + s][...]
+                att_ref[:, cols] = refs[s][0]
+                grad_ref[:, cols] = refs[s][1]
 
 
 def shards(queries, key_vectors, value_vectors, out_grad, block_order):
@@ -365,6 +380,9 @@
     def f32(*dims):
         return jax.ShapeDtypeStruct(dims, F32)
 
+    def i32(*dims):
+        return jax.ShapeDtypeStruct(dims, jnp.int32)
+
     def with_swaps(blocks):
         return [blocks[0]] + [swap(blocks[s], "head", s) for s in range(1, kv)]
 
@@ -391,11 +409,17 @@
     pieces = [piece] + pieces[::-1]
     q_parts = with_swaps(q_parts)
     query_rows = plan.query_rows
-    q_all, do_all, q_t, do_t = call(
-        functools.partial(turn_kernel, plan),
+    chunks = [(a, core, p) for a in range(spans) for core in range(cores) for p in range(parts)]
+    q_all, do_all, q_t, do_t, gap, firsts = call(
+        functools.partial(turn_kernel, plan, chunks),
         "turn",
         (info, *q_parts),
-        [bf(query_rows, HD)] * 2 + [bf(HD, query_rows)] * 2,
+        [
+            *[bf(query_rows, HD)] * 2,
+            *[bf(HD, query_rows)] * 2,
+            i32(len(plan.tiles) * block_rows, plan.lanes),
+            i32(len(chunks) * plan.slices, plan.lanes),
+        ],
         [SMEM] + [VMEM] * kv,
     )
     column, handed, order = [None] * parts, [None] * parts, []
@@ -429,9 +453,9 @@
         return call(
             functools.partial(part_kernel, plan, chunks),
             name,
-            (info, q_t, *kv_refs, *order),
+            (gap, firsts, q_t, *kv_refs, *order),
             [f32(size, query_rows), row, row, column_out],
-            [SMEM] + [VMEM] * (1 + len(kv_refs) + len(order)),
+            None,
             [pltpu.VMEM((2 * HD, size), BF)],
             size * 4 * HD,
             8 * size * query_rows * HD,
@@ -451,9 +475,9 @@
     outs = call(
         functools.partial(far_kernel, plan, far_chunks, 1 + parts),
         "attend_far",
-        (info, q_all, do_all, q_t, do_t, *near, *[r for mid in mids for r in mid[1:]], *far_kv),
-        [bf(rows, width)] * kv + [row] * (2 + parts) + [column_out] + [dkv] * len(far_kv),
-        [SMEM] + [VMEM] * (7 + 3 * parts + len(far_kv)),
+        (gap, firsts, q_all, do_all, q_t, do_t, *near, *[r for mid in mids for r in mid[1:]], *far_kv),
+        [row] * (2 + parts) + [bf(HD, query_rows), column_out] + [dkv] * len(far_kv),
+        None,
         [
             pltpu.VMEM((2 * HD, far_keys), BF),
             pltpu.VMEM((far_keys, query_rows), F32),
@@ -464,17 +488,16 @@
         far_keys * (4 * HD + 12 * query_rows),
         16 * far_keys * query_rows * HD,
     )
-    att_parts, outs = outs[:kv], outs[kv:]
     (near_scale, *mid_scales), outs = outs[: 1 + parts], outs[1 + parts :]
-    (delta, q_grad), far_dkv = outs[:2], outs[2:]
+    (delta, mixed, q_grad), far_dkv = outs[:3], outs[3:]
 
     def back(rows_at, last, e, scale, q_grad, kv_refs, order):
         count = len(rows_at)
-        q_outs = [bf(rows, width)] * kv if last else [column_out]
+        q_outs = [bf(2, rows, width)] * kv if last else [column_out]
         outs = call(
             functools.partial(back_kernel, plan, rows_at, last, len(order)),
             "attend_back",
-            (q_all, do_all, do_t, e, scale, delta, q_grad, *kv_refs, *order),
+            (q_all, do_all, do_t, e, scale, delta, q_grad, *[mixed] * last, *kv_refs, *order),
             q_outs + [dkv] * count,
             None,
             [
@@ -509,7 +532,7 @@
         q_grad = outs[0]
         for p in range(parts):
             sums[p].append(swap(parts_dkv[p], "ctx", core) if core else parts_dkv[p])
-    q_grad_parts = outs[:kv]
+    q_parts = outs[:kv]
     z_parts = [None] * z_devices
     for p in range(parts):
         totals = call(
@@ -519,6 +542,8 @@
             [bf(kv, rows, 2 * HD)] * z_part,
         )
 
+        if p == parts - 1:
+            q_parts = with_swaps(after(q_parts, totals[:1]))
         for m, total in zip(plan.zone(p), totals):
             z_parts[m] = swap(total, "ctx", m * cores) if m else total
     ordered = [z_parts[m] for p in each for m in plan.zone(p)]
@@ -529,19 +554,19 @@
         functools.partial(sum_z_kernel, kv), "sum_z", ordered, [bf(rows, 2 * HD)] * kv
     )
     pair_parts = with_swaps(pair_parts)
-    attended, query_grad = call(
+    attended, query_grad, done = call(
         functools.partial(finish_q_kernel, kv),
         "finish_q",
-        (own_group, *with_swaps(att_parts), *with_swaps(q_grad_parts)),
-        [bf(rows, query_width)] * 2,
-        [SMEM] + [VMEM] * (2 * kv),
+        (own_group, *q_parts),
+        [bf(rows, query_width)] * 2 + [f32(8, HD)],
+        [SMEM] + [VMEM] * kv,
     )
     key_grad, value_grad = call(
         functools.partial(finish_kv_kernel, kv),
         "finish_kv",
-        (own_group, *pair_parts),
+        (own_group, *pair_parts, done),
         [bf(rows, kv * HD)] * 2,
-        [SMEM] + [VMEM] * kv,
+        [SMEM] + [VMEM] * (kv + 1),
     )
     return (
         attended.reshape(halves, block_rows, query_width),

time: 50 us -> 49 us (0.980)
  waiting for transfers between devices: 8.38 us -> 10.5 us
  Pallas kernels: 14.4 us -> 12.3 us
  starting transfers between devices: 22.7 us -> 21.6 us
    ppermute x24 -> x23, waiting for transfers between devices: 8.38 us -> 10.5 us  [swap(): return lax.ppermute(block, axis, [(i, i ^ mask) for i in range(size)])]
    pallas_call x20, Pallas kernels: 14.4 us -> 12.3 us  [call(): pl.pallas_call(kernel, out_shape=list(outs), in_specs=specs or [VMEM] * l...]
    ppermute x24 -> x23, starting transfers between devices: 22.7 us -> 21.6 us  [swap(): return lax.ppermute(block, axis, [(i, i ^ mask) for i in range(size)])]
  transfers between devices with their start and end apart: 24 -> 23, of which waited for: 7 -> 10; matrix products, arithmetic and copies ran while one was open for 1% -> 2% of each run, Pallas kernels for 21% -> 18%
where the time goes in v11:
time: 49 us; the launch traced here: 48.8 us
  starting transfers between devices  21.6 us (44%)
  Pallas kernels  12.3 us (25%)
  waiting for transfers between devices  10.5 us (21%)
  local copies, waits for them, and re-layouts  1.9 us (4%)
  other arithmetic  1.53 us (3%)
  between operations  0.87 us (2%)
    ppermute x23, starting transfers between devices, swap(): return lax.ppermute(block, axis, [(i, i ^ mask) for i in range(size)])  21.6 us
    pallas_call x20, Pallas kernels, call(): pl.pallas_call(kernel, out_shape=list(outs), in_specs=specs or [VMEM] * l...  12.3 us
    ppermute x23, waiting for transfers between devices, swap(): return lax.ppermute(block, axis, [(i, i ^ mask) for i in range(size)])  10.5 us
    unnamed x4, local copies, waits for them, and re-layouts  1.9 us
  transfers between devices with their start and end apart: 23, of which 10 were waited for; matrix products, arithmetic and copies ran while one was open for 2% of the time, Pallas kernels for 18%

profile of v11, /device:TPU:0, one launch (start us, length us, event | category | flops | bytes accessed | tf_op | source)
XLA Modules:
  0.0 48.8 jit_solution(1962524056752031708)
XLA Ops:
  0.6 0.8 %broadcast_select_fusion.2 = (bf16[64,128]{1,0:T(8,128)(2,1)S(1)}, bf16[64,128]{1,0:T(8,128)(2,1)S(1)}, bf16[64,128]{1,0:T(8,128)(2,1)S(1)}, bf16[64,128]{1,0:T(8,128)(2,1)S(1)}) fusion(pred[]{:T(512)S(6)} %eq.12, bf16[64,256]{1,0:T(8,128)(2,1)} %bitcast.18, pred[]{:T(512)S(6)} %eq.13, bf16[64,256]{1,0:T(8,128)(2,1)} %bitcast.19), kind=kLoop, calls=%fused_computation.6 | loop fusion | flops 32768 | bytes 131074 | tf_op jit(solution)/shard_map/jit(_where)/select_n | solution.py:396
  1.4 3.0 %collective-permute-start.1 = (bf16[64,256]{1,0:T(8,128)(2,1)S(1)}, bf16[64,256]{1,0:T(8,128)(2,1)S(1)}, u32[]{:S(2)}, u32[]{:S(2)}) collective-permute-start(bf16[64,256]{1,0:T(8,128)(2,1)S(1)} %pad_maximum_fusion.1), channel_id=1, source_target_pairs={{0,8},{8,0},{16,24},{24,16},{1,9},{9,1},{17,25},{25,17},{2,10},{10... | collective-permute-start | bytes 98312 | tf_op jit(solution)/shard_map/ppermute | solution.py:26
  4.4 0.9 %copy-done = bf16[2,32,2048]{2,1,0:T(8,128)(2,1)S(1)} copy-done((bf16[2,32,2048]{2,1,0:T(8,128)(2,1)S(1)}, bf16[2,32,2048]{2,1,0:T(8,128)(2,1)}, u32[]{:S(2)}) %copy-start) | copy-done | bytes 262168
  5.4 0.9 %copy-done.1 = bf16[2,32,2048]{2,1,0:T(8,128)(2,1)S(1)} copy-done((bf16[2,32,2048]{2,1,0:T(8,128)(2,1)S(1)}, bf16[2,32,2048]{2,1,0:T(8,128)(2,1)}, u32[]{:S(2)}) %copy-start.1) | copy-done | bytes 262168
  6.4 0.1 collective-permute-start
  6.5 2.1 %collective-permute-start.4 = (bf16[2,64,256]{2,1,0:T(8,128)(2,1)S(1)}, bf16[2,64,256]{2,1,0:T(8,128)(2,1)S(1)}, u32[]{:S(2)}, u32[]{:S(2)}) collective-permute-start(bf16[2,64,256]{2,1,0:T(8,128)(2,1)S(1)} %pad_maximum_fusion.refs_0_), channel_id=1, source_target_pairs={{0,2},{1,3},{2,0},{3,1},{4,6},{5,7},{6,4},{7,5},{8,10},{9,11},{10,... | collective-permute-start | bytes 196616 | tf_op jit(solution)/shard_map/ppermute | solution.py:26
  8.7 2.5 %collective-permute-start.3 = (bf16[2,64,256]{2,1,0:T(8,128)(2,1)S(1)}, bf16[2,64,256]{2,1,0:T(8,128)(2,1)S(1)}, u32[]{:S(2)}, u32[]{:S(2)}) collective-permute-start(bf16[2,64,256]{2,1,0:T(8,128)(2,1)S(1)} %pad_maximum_fusion.refs_0_), channel_id=1, source_target_pairs={{0,6},{1,7},{2,4},{3,5},{4,2},{5,3},{6,0},{7,1},{8,14},{9,15},{10,... | collective-permute-start | bytes 196616 | tf_op jit(solution)/shard_map/ppermute | solution.py:26
  11.1 0.1 collective-permute-start.2
  11.3 1.7 %collective-permute-start.7 = (bf16[2,2,64,256]{3,2,1,0:T(8,128)(2,1)S(1)}, bf16[2,2,64,256]{3,2,1,0:T(8,128)(2,1)S(1)}, u32[]{:S(2)}, u32[]{:S(2)}) collective-permute-start(bf16[2,2,64,256]{3,2,1,0:T(8,128)(2,1)S(1)} %stack.22.refs_2_.refs_1_), channel_id=1, source_target_pairs={{0,16},{8,24},{16,0},{24,8},{1,17},{9,25},{17,1},{25,9},{2,18},{10... | collective-permute-start | bytes 393224 | tf_op jit(solution)/shard_map/ppermute | solution.py:26
  12.9 0.7 %pad_add_fusion.info_ref = s32[18]{0:T(128)S(1)} fusion(s32[16]{0:T(128)} %param.9, s32[1]{0:T(128)} %bitcast.2, s32[1]{0:T(128)} %bitcast.1), kind=kLoop, calls=%fused_computation.8 | loop fusion | flops 36 | bytes 144 | tf_op jit(solution)/shard_map/concatenate | solution.py:370
  13.7 0.5 %collective-permute-done.refs_1_ = bf16[2,64,1024]{2,1,0:T(8,128)(2,1)S(1)} collective-permute-done((bf16[2,64,1024]{2,1,0:T(8,128)(2,1)S(1)}, bf16[2,64,1024]{2,1,0:T(8,128)(2,1)S(1)}, u32[]{:S(2)}, u32[]{:S(2)}) %collective-permute-start) | collective-permute-done | bytes 262176 | tf_op jit(solution)/shard_map/ppermute | solution.py:26
  14.2 0.8 %turn.1 = (bf16[1024,128]{1,0:T(8,128)(2,1)S(1)}, bf16[1024,128]{1,0:T(8,128)(2,1)S(1)}, bf16[128,1024]{1,0:T(8,128)(2,1)S(1)}, bf16[128,1024]{1,0:T(8,128)(2,1)...) custom-call(s32[18]{0:T(128)S(1)} %pad_add_fusion.info_ref, bf16[2,64,1024]{2,1,0:T(8,128)(2,1)S(1)} %get-tuple-element.61.refs_0_, ...), custom_call_target="tpu_custom_call" | custom-call | bytes 1769544 | tf_op jit(solution)/shard_map/turn/pallas_call | solution.py:41
  15.0 2.1 %collective-permute-done.2.refs_0_ = bf16[2,64,256]{2,1,0:T(8,128)(2,1)S(1)} collective-permute-done((bf16[2,64,256]{2,1,0:T(8,128)(2,1)S(1)}, bf16[2,64,256]{2,1,0:T(8,128)(2,1)S(1)}, u32[]{:S(2)}, u32[]{:S(2)}) %collective-permute-start.2) | collective-permute-done | bytes 65568 | tf_op jit(solution)/shard_map/ppermute | solution.py:26
  17.1 0.1 collective-permute-start.6
  17.1 0.5 %collective-permute-start.5 = (bf16[2,2,64,256]{3,2,1,0:T(8,128)(2,1)S(1)}, bf16[2,2,64,256]{3,2,1,0:T(8,128)(2,1)S(1)}, u32[]{:S(2)}, u32[]{:S(2)}) collective-permute-start(bf16[2,2,64,256]{3,2,1,0:T(8,128)(2,1)S(1)} %get-tuple-element.69.refs_0_.refs_1_), channel_id=1, source_target_pairs={{0,1},{1,0},{2,3},{3,2},{4,5},{5,4},{6,7},{7,6},{8,9},{9,8},{10,11... | collective-permute-start | bytes 393224 | tf_op jit(solution)/shard_map/ppermute | solution.py:26
  17.6 1.5 %collective-permute-start.8 = (bf16[2,2,64,256]{3,2,1,0:T(8,128)(2,1)S(1)}, bf16[2,2,64,256]{3,2,1,0:T(8,128)(2,1)S(1)}, u32[]{:S(2)}, u32[]{:S(2)}) collective-permute-start(bf16[2,2,64,256]{3,2,1,0:T(8,128)(2,1)S(1)} %get-tuple-element.69.refs_0_.refs_1_), channel_id=1, source_target_pairs={{0,16},{8,24},{16,0},{24,8},{1,17},{9,25},{17,1},{25,9},{2,18},{10... | collective-permute-start | bytes 393224 | tf_op jit(solution)/shard_map/ppermute | solution.py:26
  19.2 0.7 %attend_mid.2 = (f32[256,1024]{1,0:T(8,128)S(1)}, f32[1,1024]{1,0:T(1,128)S(1)}, f32[1,1024]{1,0:T(1,128)S(1)}, f32[128,1024]{1,0:T(8,128)S(1)}) custom-call(s32[128,256]{1,0:T(8,128)S(1)} %get-tuple-element.66.gap_ref, s32[64,256]{1,0:T(8,128)S(1)} %get-tuple-element.67.first_ref, bf16[128,1024]{1,0:T(8,128)(2,1)S(1)} %get-tuple-element.68.refs_3_.q_t, ...), custom_call_target="tpu_custom_call" | custom-call | flops 268435456 | bytes 2170880 | tf_op jit(solution)/shard_map/attend_mid/pallas_call | solution.py:41
  19.9 2.0 %attend_near.1 = (f32[1024,1024]{1,0:T(8,128)S(1)}, f32[1,1024]{1,0:T(1,128)S(1)}, f32[1,1024]{1,0:T(1,128)S(1)}, f32[128,1024]{1,0:T(8,128)S(1)}) custom-call(s32[128,256]{1,0:T(8,128)S(1)} %get-tuple-element.66.gap_ref, s32[64,256]{1,0:T(8,128)S(1)} %get-tuple-element.67.first_ref, bf16[128,1024]{1,0:T(8,128)(2,1)S(1)} %get-tuple-element.68.refs_3_.q_t, ...), custom_call_target="tpu_custom_call" | custom-call | flops 1073741824 | bytes 5713920 | tf_op jit(solution)/shard_map/attend_near/pallas_call | solution.py:41
  21.9 1.2 %collective-permute-done.8.refs_0_ = bf16[2,2,64,256]{3,2,1,0:T(8,128)(2,1)S(1)} collective-permute-done((bf16[2,2,64,256]{3,2,1,0:T(8,128)(2,1)S(1)}, bf16[2,2,64,256]{3,2,1,0:T(8,128)(2,1)S(1)}, u32[]{:S(2)}, u32[]{:S(2)}) %collective-permute-start.8) | collective-permute-done | bytes 131104 | tf_op jit(solution)/shard_map/ppermute | solution.py:26
  23.1 0.7 %attend_mid.3 = (f32[256,1024]{1,0:T(8,128)S(1)}, f32[1,1024]{1,0:T(1,128)S(1)}, f32[1,1024]{1,0:T(1,128)S(1)}, f32[128,1024]{1,0:T(8,128)S(1)}) custom-call(s32[128,256]{1,0:T(8,128)S(1)} %get-tuple-element.66.gap_ref, s32[64,256]{1,0:T(8,128)S(1)} %get-tuple-element.67.first_ref, bf16[128,1024]{1,0:T(8,128)(2,1)S(1)} %get-tuple-element.68.refs_3_.q_t, ...), custom_call_target="tpu_custom_call" | custom-call | flops 268435456 | bytes 2174976 | tf_op jit(solution)/shard_map/attend_mid/pallas_call | solution.py:41
  23.9 0.6 %collective-permute-done.9.refs_9_ = bf16[2,2,64,256]{3,2,1,0:T(8,128)(2,1)S(1)} collective-permute-done((bf16[2,2,64,256]{3,2,1,0:T(8,128)(2,1)S(1)}, bf16[2,2,64,256]{3,2,1,0:T(8,128)(2,1)S(1)}, u32[]{:S(2)}, u32[]{:S(2)}) %collective-permute-start.9) | collective-permute-done | bytes 131104 | tf_op jit(solution)/shard_map/ppermute | solution.py:26
  24.5 2.6 %attend_far.1 = (f32[1,1024]{1,0:T(1,128)S(1)}, f32[1,1024]{1,0:T(1,128)S(1)}, f32[1,1024]{1,0:T(1,128)S(1)}, f32[1,1024]{1,0:T(1,128)S(1)}, bf16[128,1024]{1,0:...) custom-call(s32[128,256]{1,0:T(8,128)S(1)} %get-tuple-element.66.gap, ...), custom_call_target="tpu_custom_call" | custom-call | flops 1073741824 | bytes 4169728 | tf_op jit(solution)/shard_map/attend_far/pallas_call | solution.py:41
  27.1 0.2 collective-permute-start.12
  27.3 0.4 collective-permute-start.11
  27.7 0.6 %attend_back.4 = (f32[128,1024]{1,0:T(8,128)S(1)}, bf16[2,2,64,256]{3,2,1,0:T(8,128)(2,1)S(1)}) custom-call(bf16[1024,128]{1,0:T(8,128)(2,1)S(1)} %get-tuple-element.63.q_all, bf16[1024,128]{1,0:T(8,128)(2,1)S(1)} %get-tuple-element.64.do_all, bf16[128,1024]{1,0:T(8,128)(2,1)S(1)} %get-tuple-element.65.do_t, f32[256,1024]{1,0:T(8,128)S(1)} %get-tuple-element.86.e_ref, ...), custom_call_target="tpu_custom_call" | custom-call | flops 402653184 | bytes 3153920 | tf_op jit(solution)/shard_map/attend_back/pallas_call | solution.py:41
  28.3 0.7 %attend_back.5 = (f32[128,1024]{1,0:T(8,128)S(1)}, bf16[2,2,64,256]{3,2,1,0:T(8,128)(2,1)S(1)}) custom-call(bf16[1024,128]{1,0:T(8,128)(2,1)S(1)} %get-tuple-element.63.q_all, bf16[1024,128]{1,0:T(8,128)(2,1)S(1)} %get-tuple-element.64.do_all, bf16[128,1024]{1,0:T(8,128)(2,1)S(1)} %get-tuple-element.65.do_t, f32[256,1024]{1,0:T(8,128)S(1)} %get-tuple-element.84.e_ref, ...), custom_call_target="tpu_custom_call" | custom-call | flops 402653184 | bytes 3153920 | tf_op jit(solution)/shard_map/attend_back/pallas_call | solution.py:41
  29.1 0.2 collective-permute-start.13
  29.3 1.5 %collective-permute-start.17 = (bf16[2,2,64,256]{3,2,1,0:T(8,128)(2,1)S(1)}, bf16[2,2,64,256]{3,2,1,0:T(8,128)(2,1)S(1)}, u32[]{:S(2)}, u32[]{:S(2)}) collective-permute-start(bf16[2,2,64,256]{3,2,1,0:T(8,128)(2,1)S(1)} %sum_cores.3), channel_id=1, source_target_pairs={{0,16},{8,24},{16,0},{24,8},{1,17},{9,25},{17,1},{25,9},{2,18},{10... | collective-permute-start | bytes 393224 | tf_op jit(solution)/shard_map/ppermute | solution.py:26
  30.8 1.2 %attend_back.6 = (f32[128,1024]{1,0:T(8,128)S(1)}, bf16[2,2,64,256]{3,2,1,0:T(8,128)(2,1)S(1)}, bf16[2,2,64,256]{3,2,1,0:T(8,128)(2,1)S(1)}) custom-call(bf16[1024,128]{1,0:T(8,128)(2,1)S(1)} %get-tuple-element.63.q_all, bf16[1024,128]{1,0:T(8,128)(2,1)S(1)} %get-tuple-element.64.do_all, bf16[128,1024]{1,0:T(8,128)(2,1)S(1)} %get-tuple-element.65.do_t, ...), custom_call_target="tpu_custom_call" | custom-call | flops 805306368 | bytes 6578176 | tf_op jit(solution)/shard_map/attend_back/pallas_call | solution.py:41
  32.0 0.1 collective-permute-start.18
  32.2 1.1 %collective-permute-start.14 = (bf16[2,2,64,256]{3,2,1,0:T(8,128)(2,1)S(1)}, bf16[2,2,64,256]{3,2,1,0:T(8,128)(2,1)S(1)}, u32[]{:S(2)}, u32[]{:S(2)}) collective-permute-start(bf16[2,2,64,256]{3,2,1,0:T(8,128)(2,1)S(1)} %sum_cores.2), channel_id=1, source_target_pairs={{0,16},{8,24},{16,0},{24,8},{1,17},{9,25},{17,1},{25,9},{2,18},{10... | collective-permute-start | bytes 393224 | tf_op jit(solution)/shard_map/ppermute | solution.py:26
  33.3 0.1 collective-permute-start.15
  33.3 1.2 %attend_back.7 = (bf16[2,64,1024]{2,1,0:T(8,128)(2,1)S(1)}, bf16[2,64,1024]{2,1,0:T(8,128)(2,1)S(1)}, bf16[2,2,64,256]{3,2,1,0:T(8,128)(2,1)S(1)}, bf16[2,2,64,256]{3,2,1,0:T(8,128)(2,1)S(1)}) custom-call(bf16[1024,128]{1,0:T(8,128)(2,1)S(1)} %get-tuple-element.63.q_all, bf16[1024,128]{1,0:T(8,128)(2,1)S(1)} %get-tuple-element.64.do_all, ...), custom_call_target="tpu_custom_call" | custom-call | flops 805306368 | bytes 6840320 | tf_op jit(solution)/shard_map/attend_back/pallas_call | solution.py:41
  34.6 0.5 collective-permute-done.17.refs_0_
  35.1 0.1 sum_heads.3
  35.1 0.9 %collective-permute-start.19 = (bf16[2,64,256]{2,1,0:T(8,128)(2,1)S(1)}, bf16[2,64,256]{2,1,0:T(8,128)(2,1)S(1)}, u32[]{:S(2)}, u32[]{:S(2)}) collective-permute-start(bf16[2,64,256]{2,1,0:T(8,128)(2,1)S(1)} %get-tuple-element.110), channel_id=1, source_target_pairs={{0,4},{1,5},{2,6},{3,7},{4,0},{5,1},{6,2},{7,3},{8,12},{9,13},{10,... | collective-permute-start | bytes 196616 | tf_op jit(solution)/shard_map/ppermute | solution.py:26
  36.0 1.7 %collective-permute-start.20 = (bf16[2,64,256]{2,1,0:T(8,128)(2,1)S(1)}, bf16[2,64,256]{2,1,0:T(8,128)(2,1)S(1)}, u32[]{:S(2)}, u32[]{:S(2)}) collective-permute-start(bf16[2,64,256]{2,1,0:T(8,128)(2,1)S(1)} %get-tuple-element.111), channel_id=1, source_target_pairs={{0,6},{1,7},{2,4},{3,5},{4,2},{5,3},{6,0},{7,1},{8,14},{9,15},{10,... | collective-permute-start | bytes 196616 | tf_op jit(solution)/shard_map/ppermute | solution.py:26
  37.7 0.3 collective-permute-done.14.refs_0_
  38.0 0.1 sum_heads.2
  38.1 0.7 %collective-permute-start.21 = (bf16[2,64,256]{2,1,0:T(8,128)(2,1)S(1)}, bf16[2,64,256]{2,1,0:T(8,128)(2,1)S(1)}, u32[]{:S(2)}, u32[]{:S(2)}) collective-permute-start(bf16[2,64,256]{2,1,0:T(8,128)(2,1)S(1)} %get-tuple-element.112), channel_id=1, source_target_pairs={{0,2},{1,3},{2,0},{3,1},{4,6},{5,7},{6,4},{7,5},{8,10},{9,11},{10,... | collective-permute-start | bytes 196616 | tf_op jit(solution)/shard_map/ppermute | solution.py:26
  38.8 1.5 %collective-permute-start.16 = (bf16[2,64,1024]{2,1,0:T(8,128)(2,1)S(1)}, bf16[2,64,1024]{2,1,0:T(8,128)(2,1)S(1)}, u32[]{:S(2)}, u32[]{:S(2)}) collective-permute-start(bf16[2,64,1024]{2,1,0:T(8,128)(2,1)S(1)} %get-tuple-element.105), channel_id=1, source_target_pairs={{0,8},{8,0},{16,24},{24,16},{1,9},{9,1},{17,25},{25,17},{2,10},{10... | collective-permute-start | bytes 786440 | tf_op jit(solution)/shard_map/ppermute | solution.py:26
  40.3 2.5 %collective-permute-done.19.refs_0_ = bf16[2,64,256]{2,1,0:T(8,128)(2,1)S(1)} collective-permute-done((bf16[2,64,256]{2,1,0:T(8,128)(2,1)S(1)}, bf16[2,64,256]{2,1,0:T(8,128)(2,1)S(1)}, u32[]{:S(2)}, u32[]{:S(2)}) %collective-permute-start.19) | collective-permute-done | bytes 65568 | tf_op jit(solution)/shard_map/ppermute | solution.py:26
  42.8 1.2 %collective-permute-done.21.refs_2_ = bf16[2,64,256]{2,1,0:T(8,128)(2,1)S(1)} collective-permute-done((bf16[2,64,256]{2,1,0:T(8,128)(2,1)S(1)}, bf16[2,64,256]{2,1,0:T(8,128)(2,1)S(1)}, u32[]{:S(2)}, u32[]{:S(2)}) %collective-permute-start.21) | collective-permute-done | bytes 65568 | tf_op jit(solution)/shard_map/ppermute | solution.py:26
  44.1 1.6 %collective-permute-start.22 = (bf16[64,256]{1,0:T(8,128)(2,1)S(1)}, bf16[64,256]{1,0:T(8,128)(2,1)S(1)}, u32[]{:S(2)}, u32[]{:S(2)}) collective-permute-start(bf16[64,256]{1,0:T(8,128)(2,1)S(1)} %get-tuple-element.114), channel_id=1, source_target_pairs={{0,8},{8,0},{16,24},{24,16},{1,9},{9,1},{17,25},{25,17},{2,10},{10... | collective-permute-start | bytes 98312 | tf_op jit(solution)/shard_map/ppermute | solution.py:26
  45.7 0.5 %collective-permute-done.16.refs_1_ = bf16[2,64,1024]{2,1,0:T(8,128)(2,1)S(1)} collective-permute-done((bf16[2,64,1024]{2,1,0:T(8,128)(2,1)S(1)}, bf16[2,64,1024]{2,1,0:T(8,128)(2,1)S(1)}, u32[]{:S(2)}, u32[]{:S(2)}) %collective-permute-start.16) | collective-permute-done | bytes 262176 | tf_op jit(solution)/shard_map/ppermute | solution.py:26
  46.2 0.8 %finish_q.1 = (bf16[64,2048]{1,0:T(8,128)(2,1)}, bf16[64,2048]{1,0:T(8,128)(2,1)}, f32[8,128]{1,0:T(8,128)S(1)}) custom-call(s32[1]{0:T(128)} %bitcast.group_ref, bf16[2,64,1024]{2,1,0:T(8,128)(2,1)S(1)} %get-tuple-element.104.refs_0_, bf16[2,64,1024]{2,1,0:T(8,128)(2,1)S(1)} %collective-permute-done.16.refs_1_), custom_call_target="tpu_custom_call" | custom-call | bytes 1052676 | tf_op jit(solution)/shard_map/finish_q/pallas_call | solution.py:41
  47.0 1.1 %collective-permute-done.22.refs_1_ = bf16[64,256]{1,0:T(8,128)(2,1)S(1)} collective-permute-done((bf16[64,256]{1,0:T(8,128)(2,1)S(1)}, bf16[64,256]{1,0:T(8,128)(2,1)S(1)}, u32[]{:S(2)}, u32[]{:S(2)}) %collective-permute-start.22) | collective-permute-done | bytes 32800 | tf_op jit(solution)/shard_map/ppermute | solution.py:26
  48.1 0.6 %finish_kv.1 = (bf16[64,256]{1,0:T(8,128)(2,1)}, bf16[64,256]{1,0:T(8,128)(2,1)}) custom-call(s32[1]{0:T(128)} %bitcast.group_ref, bf16[64,256]{1,0:T(8,128)(2,1)S(1)} %get-tuple-element.113.refs_0_, bf16[64,256]{1,0:T(8,128)(2,1)S(1)} %collective-permute-done.22.refs_1_, f32[8,128]{1,0:T(8,128)S(1)} %get-tuple-element.115.refs_2_), custom_call_target="tpu_custom_call" | custom-call | bytes 135172 | tf_op jit(solution)/shard_map/finish_kv/pallas_call | solution.py:41
  (28 shorter events, 0.2 us)
Async XLA Ops:
  1.4 5.0 %collective-permute-start.1 = (bf16[64,256]{1,0:T(8,128)(2,1)S(1)}, bf16[64,256]{1,0:T(8,128)(2,1)S(1)}, u32[]{:S(2)}, u32[]{:S(2)}) collective-permute-start(bf16[64,256]{1,0:T(8,128)(2,1)S(1)} %pad_maximum_fusion.1), channel_id=1, source_target_pairs={{0,8},{8,0},{16,24},{24,16},{1,9},{9,1},{17,25},{25,17},{2,10},{10... | collective-permute-start | bytes 98312 | tf_op jit(solution)/shard_map/ppermute | solution.py:26
  4.4 0.9 %copy-start = (bf16[2,32,2048]{2,1,0:T(8,128)(2,1)S(1)}, bf16[2,32,2048]{2,1,0:T(8,128)(2,1)}, u32[]{:S(2)}) copy-start(bf16[2,32,2048]{2,1,0:T(8,128)(2,1)} %param.5) | copy-start | bytes 786436
  5.4 0.9 %copy-start.1 = (bf16[2,32,2048]{2,1,0:T(8,128)(2,1)S(1)}, bf16[2,32,2048]{2,1,0:T(8,128)(2,1)}, u32[]{:S(2)}) copy-start(bf16[2,32,2048]{2,1,0:T(8,128)(2,1)} %param.8) | copy-start | bytes 786436
  6.4 7.8 %collective-permute-start = (bf16[2,64,1024]{2,1,0:T(8,128)(2,1)S(1)}, bf16[2,64,1024]{2,1,0:T(8,128)(2,1)S(1)}, u32[]{:S(2)}, u32[]{:S(2)}) collective-permute-start(bf16[2,64,1024]{2,1,0:T(8,128)(2,1)S(1)} %get-tuple-element.62), channel_id=1, source_target_pairs={{0,8},{8,0},{16,24},{24,16},{1,9},{9,1},{17,25},{25,17},{2,10},{10... | collective-permute-start | bytes 786440 | tf_op jit(solution)/shard_map/ppermute | solution.py:26
  6.5 4.7 %collective-permute-start.4 = (bf16[2,64,256]{2,1,0:T(8,128)(2,1)S(1)}, bf16[2,64,256]{2,1,0:T(8,128)(2,1)S(1)}, u32[]{:S(2)}, u32[]{:S(2)}) collective-permute-start(bf16[2,64,256]{2,1,0:T(8,128)(2,1)S(1)} %pad_maximum_fusion.refs_0_), channel_id=1, source_target_pairs={{0,2},{1,3},{2,0},{3,1},{4,6},{5,7},{6,4},{7,5},{8,10},{9,11},{10,... | collective-permute-start | bytes 196616 | tf_op jit(solution)/shard_map/ppermute | solution.py:26
  8.7 6.3 %collective-permute-start.3 = (bf16[2,64,256]{2,1,0:T(8,128)(2,1)S(1)}, bf16[2,64,256]{2,1,0:T(8,128)(2,1)S(1)}, u32[]{:S(2)}, u32[]{:S(2)}) collective-permute-start(bf16[2,64,256]{2,1,0:T(8,128)(2,1)S(1)} %pad_maximum_fusion.refs_0_), channel_id=1, source_target_pairs={{0,6},{1,7},{2,4},{3,5},{4,2},{5,3},{6,0},{7,1},{8,14},{9,15},{10,... | collective-permute-start | bytes 196616 | tf_op jit(solution)/shard_map/ppermute | solution.py:26
  11.1 5.9 %collective-permute-start.2 = (bf16[2,64,256]{2,1,0:T(8,128)(2,1)S(1)}, bf16[2,64,256]{2,1,0:T(8,128)(2,1)S(1)}, u32[]{:S(2)}, u32[]{:S(2)}) collective-permute-start(bf16[2,64,256]{2,1,0:T(8,128)(2,1)S(1)} %pad_maximum_fusion.refs_0_), channel_id=1, source_target_pairs={{0,4},{1,5},{2,6},{3,7},{4,0},{5,1},{6,2},{7,3},{8,12},{9,13},{10,... | collective-permute-start | bytes 196616 | tf_op jit(solution)/shard_map/ppermute | solution.py:26
  11.3 7.9 %collective-permute-start.7 = (bf16[2,2,64,256]{3,2,1,0:T(8,128)(2,1)S(1)}, bf16[2,2,64,256]{3,2,1,0:T(8,128)(2,1)S(1)}, u32[]{:S(2)}, u32[]{:S(2)}) collective-permute-start(bf16[2,2,64,256]{3,2,1,0:T(8,128)(2,1)S(1)} %stack.22.refs_2_.refs_1_), channel_id=1, source_target_pairs={{0,16},{8,24},{16,0},{24,8},{1,17},{9,25},{17,1},{25,9},{2,18},{10... | collective-permute-start | bytes 393224 | tf_op jit(solution)/shard_map/ppermute | solution.py:26
  17.1 2.8 %collective-permute-start.6 = (bf16[2,2,64,256]{3,2,1,0:T(8,128)(2,1)S(1)}, bf16[2,2,64,256]{3,2,1,0:T(8,128)(2,1)S(1)}, u32[]{:S(2)}, u32[]{:S(2)}) collective-permute-start(bf16[2,2,64,256]{3,2,1,0:T(8,128)(2,1)S(1)} %get-tuple-element.70), channel_id=1, source_target_pairs={{0,1},{1,0},{2,3},{3,2},{4,5},{5,4},{6,7},{7,6},{8,9},{9,8},{10,11... | collective-permute-start | bytes 393224 | tf_op jit(solution)/shard_map/ppermute | solution.py:26
  17.1 2.8 %collective-permute-start.5 = (bf16[2,2,64,256]{3,2,1,0:T(8,128)(2,1)S(1)}, bf16[2,2,64,256]{3,2,1,0:T(8,128)(2,1)S(1)}, u32[]{:S(2)}, u32[]{:S(2)}) collective-permute-start(bf16[2,2,64,256]{3,2,1,0:T(8,128)(2,1)S(1)} %get-tuple-element.69.refs_0_.refs_1_), channel_id=1, source_target_pairs={{0,1},{1,0},{2,3},{3,2},{4,5},{5,4},{6,7},{7,6},{8,9},{9,8},{10,11... | collective-permute-start | bytes 393224 | tf_op jit(solution)/shard_map/ppermute | solution.py:26
  17.6 5.5 %collective-permute-start.8 = (bf16[2,2,64,256]{3,2,1,0:T(8,128)(2,1)S(1)}, bf16[2,2,64,256]{3,2,1,0:T(8,128)(2,1)S(1)}, u32[]{:S(2)}, u32[]{:S(2)}) collective-permute-start(bf16[2,2,64,256]{3,2,1,0:T(8,128)(2,1)S(1)} %get-tuple-element.69.refs_0_.refs_1_), channel_id=1, source_target_pairs={{0,16},{8,24},{16,0},{24,8},{1,17},{9,25},{17,1},{25,9},{2,18},{10... | collective-permute-start | bytes 393224 | tf_op jit(solution)/shard_map/ppermute | solution.py:26
  19.2 4.7 %collective-permute-start.10 = (bf16[2,2,64,256]{3,2,1,0:T(8,128)(2,1)S(1)}, bf16[2,2,64,256]{3,2,1,0:T(8,128)(2,1)S(1)}, u32[]{:S(2)}, u32[]{:S(2)}) collective-permute-start(bf16[2,2,64,256]{3,2,1,0:T(8,128)(2,1)S(1)} %collective-permute-done.7.refs_0_), channel_id=1, source_target_pairs={{0,1},{1,0},{2,3},{3,2},{4,5},{5,4},{6,7},{7,6},{8,9},{9,8},{10,11... | collective-permute-start | bytes 393224 | tf_op jit(solution)/shard_map/ppermute | solution.py:26
  23.1 1.3 %collective-permute-start.9 = (bf16[2,2,64,256]{3,2,1,0:T(8,128)(2,1)S(1)}, bf16[2,2,64,256]{3,2,1,0:T(8,128)(2,1)S(1)}, u32[]{:S(2)}, u32[]{:S(2)}) collective-permute-start(bf16[2,2,64,256]{3,2,1,0:T(8,128)(2,1)S(1)} %collective-permute-done.8.refs_0_), channel_id=1, source_target_pairs={{0,1},{1,0},{2,3},{3,2},{4,5},{5,4},{6,7},{7,6},{8,9},{9,8},{10,11... | collective-permute-start | bytes 393224 | tf_op jit(solution)/shard_map/ppermute | solution.py:26
  27.1 1.9 %collective-permute-start.12 = (bf16[2,2,64,256]{3,2,1,0:T(8,128)(2,1)S(1)}, bf16[2,2,64,256]{3,2,1,0:T(8,128)(2,1)S(1)}, u32[]{:S(2)}, u32[]{:S(2)}) collective-permute-start(bf16[2,2,64,256]{3,2,1,0:T(8,128)(2,1)S(1)} %get-tuple-element.94), channel_id=1, source_target_pairs={{0,1},{1,0},{2,3},{3,2},{4,5},{5,4},{6,7},{7,6},{8,9},{9,8},{10,11... | collective-permute-start | bytes 393224 | tf_op jit(solution)/shard_map/ppermute | solution.py:26
  27.3 1.7 %collective-permute-start.11 = (bf16[2,2,64,256]{3,2,1,0:T(8,128)(2,1)S(1)}, bf16[2,2,64,256]{3,2,1,0:T(8,128)(2,1)S(1)}, u32[]{:S(2)}, u32[]{:S(2)}) collective-permute-start(bf16[2,2,64,256]{3,2,1,0:T(8,128)(2,1)S(1)} %get-tuple-element.92), channel_id=1, source_target_pairs={{0,1},{1,0},{2,3},{3,2},{4,5},{5,4},{6,7},{7,6},{8,9},{9,8},{10,11... | collective-permute-start | bytes 393224 | tf_op jit(solution)/shard_map/ppermute | solution.py:26
  29.1 1.8 %collective-permute-start.13 = (bf16[64,128]{1,0:T(8,128)(2,1)S(1)}, bf16[64,128]{1,0:T(8,128)(2,1)S(1)}, u32[]{:S(2)}, u32[]{:S(2)}) collective-permute-start(bf16[64,128]{1,0:T(8,128)(2,1)S(1)} %slice_bitcast_fusion), channel_id=1, source_target_pairs={{0,1},{1,0},{2,3},{3,2},{4,5},{5,4},{6,7},{7,6},{8,9},{9,8},{10,11... | collective-permute-start | bytes 49160 | tf_op jit(solution)/shard_map/ppermute | solution.py:26
  29.3 5.8 %collective-permute-start.17 = (bf16[2,2,64,256]{3,2,1,0:T(8,128)(2,1)S(1)}, bf16[2,2,64,256]{3,2,1,0:T(8,128)(2,1)S(1)}, u32[]{:S(2)}, u32[]{:S(2)}) collective-permute-start(bf16[2,2,64,256]{3,2,1,0:T(8,128)(2,1)S(1)} %sum_cores.3), channel_id=1, source_target_pairs={{0,16},{8,24},{16,0},{24,8},{1,17},{9,25},{17,1},{25,9},{2,18},{10... | collective-permute-start | bytes 393224 | tf_op jit(solution)/shard_map/ppermute | solution.py:26
  32.0 3.0 %collective-permute-start.18 = (bf16[2,2,64,256]{3,2,1,0:T(8,128)(2,1)S(1)}, bf16[2,2,64,256]{3,2,1,0:T(8,128)(2,1)S(1)}, u32[]{:S(2)}, u32[]{:S(2)}) collective-permute-start(bf16[2,2,64,256]{3,2,1,0:T(8,128)(2,1)S(1)} %get-tuple-element.108), channel_id=1, source_target_pairs={{0,1},{1,0},{2,3},{3,2},{4,5},{5,4},{6,7},{7,6},{8,9},{9,8},{10,11... | collective-permute-start | bytes 393224 | tf_op jit(solution)/shard_map/ppermute | solution.py:26
  32.2 5.9 %collective-permute-start.14 = (bf16[2,2,64,256]{3,2,1,0:T(8,128)(2,1)S(1)}, bf16[2,2,64,256]{3,2,1,0:T(8,128)(2,1)S(1)}, u32[]{:S(2)}, u32[]{:S(2)}) collective-permute-start(bf16[2,2,64,256]{3,2,1,0:T(8,128)(2,1)S(1)} %sum_cores.2), channel_id=1, source_target_pairs={{0,16},{8,24},{16,0},{24,8},{1,17},{9,25},{17,1},{25,9},{2,18},{10... | collective-permute-start | bytes 393224 | tf_op jit(solution)/shard_map/ppermute | solution.py:26
  33.3 4.7 %collective-permute-start.15 = (bf16[2,2,64,256]{3,2,1,0:T(8,128)(2,1)S(1)}, bf16[2,2,64,256]{3,2,1,0:T(8,128)(2,1)S(1)}, u32[]{:S(2)}, u32[]{:S(2)}) collective-permute-start(bf16[2,2,64,256]{3,2,1,0:T(8,128)(2,1)S(1)} %get-tuple-element.101), channel_id=1, source_target_pairs={{0,1},{1,0},{2,3},{3,2},{4,5},{5,4},{6,7},{7,6},{8,9},{9,8},{10,11... | collective-permute-start | bytes 393224 | tf_op jit(solution)/shard_map/ppermute | solution.py:26
  35.1 7.7 %collective-permute-start.19 = (bf16[2,64,256]{2,1,0:T(8,128)(2,1)S(1)}, bf16[2,64,256]{2,1,0:T(8,128)(2,1)S(1)}, u32[]{:S(2)}, u32[]{:S(2)}) collective-permute-start(bf16[2,64,256]{2,1,0:T(8,128)(2,1)S(1)} %get-tuple-element.110), channel_id=1, source_target_pairs={{0,4},{1,5},{2,6},{3,7},{4,0},{5,1},{6,2},{7,3},{8,12},{9,13},{10,... | collective-permute-start | bytes 196616 | tf_op jit(solution)/shard_map/ppermute | solution.py:26
  36.0 6.8 %collective-permute-start.20 = (bf16[2,64,256]{2,1,0:T(8,128)(2,1)S(1)}, bf16[2,64,256]{2,1,0:T(8,128)(2,1)S(1)}, u32[]{:S(2)}, u32[]{:S(2)}) collective-permute-start(bf16[2,64,256]{2,1,0:T(8,128)(2,1)S(1)} %get-tuple-element.111), channel_id=1, source_target_pairs={{0,6},{1,7},{2,4},{3,5},{4,2},{5,3},{6,0},{7,1},{8,14},{9,15},{10,... | collective-permute-start | bytes 196616 | tf_op jit(solution)/shard_map/ppermute | solution.py:26
  38.1 6.0 %collective-permute-start.21 = (bf16[2,64,256]{2,1,0:T(8,128)(2,1)S(1)}, bf16[2,64,256]{2,1,0:T(8,128)(2,1)S(1)}, u32[]{:S(2)}, u32[]{:S(2)}) collective-permute-start(bf16[2,64,256]{2,1,0:T(8,128)(2,1)S(1)} %get-tuple-element.112), channel_id=1, source_target_pairs={{0,2},{1,3},{2,0},{3,1},{4,6},{5,7},{6,4},{7,5},{8,10},{9,11},{10,... | collective-permute-start | bytes 196616 | tf_op jit(solution)/shard_map/ppermute | solution.py:26
  38.8 7.4 %collective-permute-start.16 = (bf16[2,64,1024]{2,1,0:T(8,128)(2,1)S(1)}, bf16[2,64,1024]{2,1,0:T(8,128)(2,1)S(1)}, u32[]{:S(2)}, u32[]{:S(2)}) collective-permute-start(bf16[2,64,1024]{2,1,0:T(8,128)(2,1)S(1)} %get-tuple-element.105), channel_id=1, source_target_pairs={{0,8},{8,0},{16,24},{24,16},{1,9},{9,1},{17,25},{25,17},{2,10},{10... | collective-permute-start | bytes 786440 | tf_op jit(solution)/shard_map/ppermute | solution.py:26
  44.1 4.0 %collective-permute-start.22 = (bf16[64,256]{1,0:T(8,128)(2,1)S(1)}, bf16[64,256]{1,0:T(8,128)(2,1)S(1)}, u32[]{:S(2)}, u32[]{:S(2)}) collective-permute-start(bf16[64,256]{1,0:T(8,128)(2,1)S(1)} %get-tuple-element.114), channel_id=1, source_target_pairs={{0,8},{8,0},{16,24},{24,16},{1,9},{9,1},{17,25},{25,17},{2,10},{10... | collective-permute-start | bytes 98312 | tf_op jit(solution)/shard_map/ppermute | solution.py:26

commit v12 on v11

--- a/solution.py
+++ b/solution.py
@@ -435,7 +435,7 @@
         handed[p] = column[p]
         if extra:
             handed[p + 1] = handed_on[0]
-        order = [q_t] if p else []
+        order = q_parts[1:] if p else []
     columns = [[swap(half, "head", a * kv) for half in column] for a in range(1, spans)]
     near_kv = [column] + [[swap(half, "ctx", core) for half in handed] for core in range(1, cores)]
     near_flat = [half for pair in near_kv for half in pair]

time: 49 us -> 49 us (level)
  transfers between devices with their start and end apart: 23 -> 23, of which waited for: 10 -> 9; matrix products, arithmetic and copies ran while one was open for 2% -> 2% of each run, Pallas kernels for 18% -> 18%
where the time goes in v12:
time: 49 us; the launch traced here: 48.7 us
  starting transfers between devices  21.9 us (45%)
  Pallas kernels  12.3 us (25%)
  waiting for transfers between devices  10.3 us (21%)
  local copies, waits for them, and re-layouts  1.9 us (4%)
  other arithmetic  1.53 us (3%)
  between operations  0.87 us (2%)
    ppermute x23, starting transfers between devices, swap(): return lax.ppermute(block, axis, [(i, i ^ mask) for i in range(size)])  21.9 us
    pallas_call x20, Pallas kernels, call(): pl.pallas_call(kernel, out_shape=list(outs), in_specs=specs or [VMEM] * l...  12.3 us
    ppermute x23, waiting for transfers between devices, swap(): return lax.ppermute(block, axis, [(i, i ^ mask) for i in range(size)])  10.3 us
    unnamed x4, local copies, waits for them, and re-layouts  1.9 us
  transfers between devices with their start and end apart: 23, of which 9 were waited for; matrix products, arithmetic and copies ran while one was open for 2% of the time, Pallas kernels for 18%

profile of v12, /device:TPU:0, one launch (start us, length us, event | category | flops | bytes accessed | tf_op | source)
XLA Modules:
  0.0 48.7 jit_solution(2957965530662633665)
XLA Ops:
  0.6 0.8 %broadcast_select_fusion.2 = (bf16[64,128]{1,0:T(8,128)(2,1)S(1)}, bf16[64,128]{1,0:T(8,128)(2,1)S(1)}, bf16[64,128]{1,0:T(8,128)(2,1)S(1)}, bf16[64,128]{1,0:T(8,128)(2,1)S(1)}) fusion(pred[]{:T(512)S(6)} %eq.12, bf16[64,256]{1,0:T(8,128)(2,1)} %bitcast.18, pred[]{:T(512)S(6)} %eq.13, bf16[64,256]{1,0:T(8,128)(2,1)} %bitcast.19), kind=kLoop, calls=%fused_computation.6 | loop fusion | flops 32768 | bytes 131074 | tf_op jit(solution)/shard_map/jit(_where)/select_n | solution.py:396
  1.4 3.0 %collective-permute-start.1 = (bf16[64,256]{1,0:T(8,128)(2,1)S(1)}, bf16[64,256]{1,0:T(8,128)(2,1)S(1)}, u32[]{:S(2)}, u32[]{:S(2)}) collective-permute-start(bf16[64,256]{1,0:T(8,128)(2,1)S(1)} %pad_maximum_fusion.1), channel_id=1, source_target_pairs={{0,8},{8,0},{16,24},{24,16},{1,9},{9,1},{17,25},{25,17},{2,10},{10... | collective-permute-start | bytes 98312 | tf_op jit(solution)/shard_map/ppermute | solution.py:26
  4.4 0.9 %copy-done = bf16[2,32,2048]{2,1,0:T(8,128)(2,1)S(1)} copy-done((bf16[2,32,2048]{2,1,0:T(8,128)(2,1)S(1)}, bf16[2,32,2048]{2,1,0:T(8,128)(2,1)}, u32[]{:S(2)}) %copy-start) | copy-done | bytes 262168
  5.4 0.9 %copy-done.1 = bf16[2,32,2048]{2,1,0:T(8,128)(2,1)S(1)} copy-done((bf16[2,32,2048]{2,1,0:T(8,128)(2,1)S(1)}, bf16[2,32,2048]{2,1,0:T(8,128)(2,1)}, u32[]{:S(2)}) %copy-start.1) | copy-done | bytes 262168
  6.4 0.1 collective-permute-start
  6.5 2.1 %collective-permute-start.4 = (bf16[2,64,256]{2,1,0:T(8,128)(2,1)S(1)}, bf16[2,64,256]{2,1,0:T(8,128)(2,1)S(1)}, u32[]{:S(2)}, u32[]{:S(2)}) collective-permute-start(bf16[2,64,256]{2,1,0:T(8,128)(2,1)S(1)} %pad_maximum_fusion.refs_0_), channel_id=1, source_target_pairs={{0,2},{1,3},{2,0},{3,1},{4,6},{5,7},{6,4},{7,5},{8,10},{9,11},{10,... | collective-permute-start | bytes 196616 | tf_op jit(solution)/shard_map/ppermute | solution.py:26
  8.7 2.5 %collective-permute-start.3 = (bf16[2,64,256]{2,1,0:T(8,128)(2,1)S(1)}, bf16[2,64,256]{2,1,0:T(8,128)(2,1)S(1)}, u32[]{:S(2)}, u32[]{:S(2)}) collective-permute-start(bf16[2,64,256]{2,1,0:T(8,128)(2,1)S(1)} %pad_maximum_fusion.refs_0_), channel_id=1, source_target_pairs={{0,6},{1,7},{2,4},{3,5},{4,2},{5,3},{6,0},{7,1},{8,14},{9,15},{10,... | collective-permute-start | bytes 196616 | tf_op jit(solution)/shard_map/ppermute | solution.py:26
  11.1 0.1 collective-permute-start.2
  11.3 1.7 %collective-permute-start.7 = (bf16[2,2,64,256]{3,2,1,0:T(8,128)(2,1)S(1)}, bf16[2,2,64,256]{3,2,1,0:T(8,128)(2,1)S(1)}, u32[]{:S(2)}, u32[]{:S(2)}) collective-permute-start(bf16[2,2,64,256]{3,2,1,0:T(8,128)(2,1)S(1)} %stack.22.refs_2_.refs_1_), channel_id=1, source_target_pairs={{0,16},{8,24},{16,0},{24,8},{1,17},{9,25},{17,1},{25,9},{2,18},{10... | collective-permute-start | bytes 393224 | tf_op jit(solution)/shard_map/ppermute | solution.py:26
  12.9 2.0 %collective-permute-done.3.refs_1_ = bf16[2,64,256]{2,1,0:T(8,128)(2,1)S(1)} collective-permute-done((bf16[2,64,256]{2,1,0:T(8,128)(2,1)S(1)}, bf16[2,64,256]{2,1,0:T(8,128)(2,1)S(1)}, u32[]{:S(2)}, u32[]{:S(2)}) %collective-permute-start.3) | collective-permute-done | bytes 65568 | tf_op jit(solution)/shard_map/ppermute | solution.py:26
  15.0 2.1 %collective-permute-done.2.refs_0_ = bf16[2,64,256]{2,1,0:T(8,128)(2,1)S(1)} collective-permute-done((bf16[2,64,256]{2,1,0:T(8,128)(2,1)S(1)}, bf16[2,64,256]{2,1,0:T(8,128)(2,1)S(1)}, u32[]{:S(2)}, u32[]{:S(2)}) %collective-permute-start.2) | collective-permute-done | bytes 65568 | tf_op jit(solution)/shard_map/ppermute | solution.py:26
  17.1 1.6 %collective-permute-start.8 = (bf16[2,2,64,256]{3,2,1,0:T(8,128)(2,1)S(1)}, bf16[2,2,64,256]{3,2,1,0:T(8,128)(2,1)S(1)}, u32[]{:S(2)}, u32[]{:S(2)}) collective-permute-start(bf16[2,2,64,256]{3,2,1,0:T(8,128)(2,1)S(1)} %get-tuple-element.69.refs_0_.refs_1_), channel_id=1, source_target_pairs={{0,16},{8,24},{16,0},{24,8},{1,17},{9,25},{17,1},{25,9},{2,18},{10... | collective-permute-start | bytes 393224 | tf_op jit(solution)/shard_map/ppermute | solution.py:26
  18.7 0.5 %collective-permute-start.6 = (bf16[2,2,64,256]{3,2,1,0:T(8,128)(2,1)S(1)}, bf16[2,2,64,256]{3,2,1,0:T(8,128)(2,1)S(1)}, u32[]{:S(2)}, u32[]{:S(2)}) collective-permute-start(bf16[2,2,64,256]{3,2,1,0:T(8,128)(2,1)S(1)} %get-tuple-element.70), channel_id=1, source_target_pairs={{0,1},{1,0},{2,3},{3,2},{4,5},{5,4},{6,7},{7,6},{8,9},{9,8},{10,11... | collective-permute-start | bytes 393224 | tf_op jit(solution)/shard_map/ppermute | solution.py:26
  19.2 0.7 %pad_add_fusion.info_ref = s32[18]{0:T(128)S(1)} fusion(s32[16]{0:T(128)} %param.9, s32[1]{0:T(128)} %bitcast.2, s32[1]{0:T(128)} %bitcast.1), kind=kLoop, calls=%fused_computation.8 | loop fusion | flops 36 | bytes 144 | tf_op jit(solution)/shard_map/concatenate | solution.py:370
  19.9 0.0 collective-permute-start.10
  19.9 0.8 %turn.1 = (bf16[1024,128]{1,0:T(8,128)(2,1)S(1)}, bf16[1024,128]{1,0:T(8,128)(2,1)S(1)}, bf16[128,1024]{1,0:T(8,128)(2,1)S(1)}, bf16[128,1024]{1,0:T(8,128)(2,1)...) custom-call(s32[18]{0:T(128)S(1)} %pad_add_fusion.info_ref, bf16[2,64,1024]{2,1,0:T(8,128)(2,1)S(1)} %get-tuple-element.61.refs_0_, ...), custom_call_target="tpu_custom_call" | custom-call | bytes 1769544 | tf_op jit(solution)/shard_map/turn/pallas_call | solution.py:41
  20.7 0.7 %attend_mid.2 = (f32[256,1024]{1,0:T(8,128)S(1)}, f32[1,1024]{1,0:T(1,128)S(1)}, f32[1,1024]{1,0:T(1,128)S(1)}, f32[128,1024]{1,0:T(8,128)S(1)}) custom-call(s32[128,256]{1,0:T(8,128)S(1)} %get-tuple-element.66.gap_ref, s32[64,256]{1,0:T(8,128)S(1)} %get-tuple-element.67.first_ref, bf16[128,1024]{1,0:T(8,128)(2,1)S(1)} %get-tuple-element.68.q_t, ...), custom_call_target="tpu_custom_call" | custom-call | flops 268435456 | bytes 2170880 | tf_op jit(solution)/shard_map/attend_mid/pallas_call | solution.py:41
  21.4 2.0 %attend_near.1 = (f32[1024,1024]{1,0:T(8,128)S(1)}, f32[1,1024]{1,0:T(1,128)S(1)}, f32[1,1024]{1,0:T(1,128)S(1)}, f32[128,1024]{1,0:T(8,128)S(1)}) custom-call(s32[128,256]{1,0:T(8,128)S(1)} %get-tuple-element.66.gap_ref, s32[64,256]{1,0:T(8,128)S(1)} %get-tuple-element.67.first_ref, bf16[128,1024]{1,0:T(8,128)(2,1)S(1)} %get-tuple-element.68.q_t, ...), custom_call_target="tpu_custom_call" | custom-call | flops 1073741824 | bytes 5713920 | tf_op jit(solution)/shard_map/attend_near/pallas_call | solution.py:41
  23.4 0.6 %collective-permute-start.9 = (bf16[2,2,64,256]{3,2,1,0:T(8,128)(2,1)S(1)}, bf16[2,2,64,256]{3,2,1,0:T(8,128)(2,1)S(1)}, u32[]{:S(2)}, u32[]{:S(2)}) collective-permute-start(bf16[2,2,64,256]{3,2,1,0:T(8,128)(2,1)S(1)} %collective-permute-done.8.refs_0_), channel_id=1, source_target_pairs={{0,1},{1,0},{2,3},{3,2},{4,5},{5,4},{6,7},{7,6},{8,9},{9,8},{10,11... | collective-permute-start | bytes 393224 | tf_op jit(solution)/shard_map/ppermute | solution.py:26
  24.0 0.7 %attend_mid.3 = (f32[256,1024]{1,0:T(8,128)S(1)}, f32[1,1024]{1,0:T(1,128)S(1)}, f32[1,1024]{1,0:T(1,128)S(1)}, f32[128,1024]{1,0:T(8,128)S(1)}) custom-call(s32[128,256]{1,0:T(8,128)S(1)} %get-tuple-element.66.gap_ref, s32[64,256]{1,0:T(8,128)S(1)} %get-tuple-element.67.first_ref, bf16[128,1024]{1,0:T(8,128)(2,1)S(1)} %get-tuple-element.68.q_t, ...), custom_call_target="tpu_custom_call" | custom-call | flops 268435456 | bytes 2174976 | tf_op jit(solution)/shard_map/attend_mid/pallas_call | solution.py:41
  24.7 0.2 collective-permute-done.9.refs_9_
  25.0 2.6 %attend_far.1 = (f32[1,1024]{1,0:T(1,128)S(1)}, f32[1,1024]{1,0:T(1,128)S(1)}, f32[1,1024]{1,0:T(1,128)S(1)}, f32[1,1024]{1,0:T(1,128)S(1)}, bf16[128,1024]{1,0:...) custom-call(s32[128,256]{1,0:T(8,128)S(1)} %get-tuple-element.66.gap, ...), custom_call_target="tpu_custom_call" | custom-call | flops 1073741824 | bytes 4169728 | tf_op jit(solution)/shard_map/attend_far/pallas_call | solution.py:41
  27.6 0.4 collective-permute-start.12
  28.1 0.2 collective-permute-start.11
  28.2 0.6 %attend_back.4 = (f32[128,1024]{1,0:T(8,128)S(1)}, bf16[2,2,64,256]{3,2,1,0:T(8,128)(2,1)S(1)}) custom-call(bf16[1024,128]{1,0:T(8,128)(2,1)S(1)} %get-tuple-element.63.q_all, bf16[1024,128]{1,0:T(8,128)(2,1)S(1)} %get-tuple-element.64.do_all, bf16[128,1024]{1,0:T(8,128)(2,1)S(1)} %get-tuple-element.65.do_t, f32[256,1024]{1,0:T(8,128)S(1)} %get-tuple-element.86.e_ref, ...), custom_call_target="tpu_custom_call" | custom-call | flops 402653184 | bytes 3153920 | tf_op jit(solution)/shard_map/attend_back/pallas_call | solution.py:41
  28.9 0.6 %attend_back.5 = (f32[128,1024]{1,0:T(8,128)S(1)}, bf16[2,2,64,256]{3,2,1,0:T(8,128)(2,1)S(1)}) custom-call(bf16[1024,128]{1,0:T(8,128)(2,1)S(1)} %get-tuple-element.63.q_all, bf16[1024,128]{1,0:T(8,128)(2,1)S(1)} %get-tuple-element.64.do_all, bf16[128,1024]{1,0:T(8,128)(2,1)S(1)} %get-tuple-element.65.do_t, f32[256,1024]{1,0:T(8,128)S(1)} %get-tuple-element.84.e_ref, ...), custom_call_target="tpu_custom_call" | custom-call | flops 402653184 | bytes 3153920 | tf_op jit(solution)/shard_map/attend_back/pallas_call | solution.py:41
  29.6 0.4 collective-permute-start.13
  30.1 0.5 %collective-permute-start.17 = (bf16[2,2,64,256]{3,2,1,0:T(8,128)(2,1)S(1)}, bf16[2,2,64,256]{3,2,1,0:T(8,128)(2,1)S(1)}, u32[]{:S(2)}, u32[]{:S(2)}) collective-permute-start(bf16[2,2,64,256]{3,2,1,0:T(8,128)(2,1)S(1)} %sum_cores.3), channel_id=1, source_target_pairs={{0,16},{8,24},{16,0},{24,8},{1,17},{9,25},{17,1},{25,9},{2,18},{10... | collective-permute-start | bytes 393224 | tf_op jit(solution)/shard_map/ppermute | solution.py:26
  30.6 0.3 collective-permute-done.13.refs_2_.refs_3_
  30.9 1.2 %attend_back.6 = (f32[128,1024]{1,0:T(8,128)S(1)}, bf16[2,2,64,256]{3,2,1,0:T(8,128)(2,1)S(1)}, bf16[2,2,64,256]{3,2,1,0:T(8,128)(2,1)S(1)}) custom-call(bf16[1024,128]{1,0:T(8,128)(2,1)S(1)} %get-tuple-element.63.q_all, bf16[1024,128]{1,0:T(8,128)(2,1)S(1)} %get-tuple-element.64.do_all, bf16[128,1024]{1,0:T(8,128)(2,1)S(1)} %get-tuple-element.65.do_t, ...), custom_call_target="tpu_custom_call" | custom-call | flops 805306368 | bytes 6578176 | tf_op jit(solution)/shard_map/attend_back/pallas_call | solution.py:41
  32.1 0.4 collective-permute-start.18
  32.5 0.9 %collective-permute-start.14 = (bf16[2,2,64,256]{3,2,1,0:T(8,128)(2,1)S(1)}, bf16[2,2,64,256]{3,2,1,0:T(8,128)(2,1)S(1)}, u32[]{:S(2)}, u32[]{:S(2)}) collective-permute-start(bf16[2,2,64,256]{3,2,1,0:T(8,128)(2,1)S(1)} %sum_cores.2), channel_id=1, source_target_pairs={{0,16},{8,24},{16,0},{24,8},{1,17},{9,25},{17,1},{25,9},{2,18},{10... | collective-permute-start | bytes 393224 | tf_op jit(solution)/shard_map/ppermute | solution.py:26
  33.4 0.2 collective-permute-start.15
  33.6 1.2 %attend_back.7 = (bf16[2,64,1024]{2,1,0:T(8,128)(2,1)S(1)}, bf16[2,64,1024]{2,1,0:T(8,128)(2,1)S(1)}, bf16[2,2,64,256]{3,2,1,0:T(8,128)(2,1)S(1)}, bf16[2,2,64,256]{3,2,1,0:T(8,128)(2,1)S(1)}) custom-call(bf16[1024,128]{1,0:T(8,128)(2,1)S(1)} %get-tuple-element.63.q_all, bf16[1024,128]{1,0:T(8,128)(2,1)S(1)} %get-tuple-element.64.do_all, ...), custom_call_target="tpu_custom_call" | custom-call | flops 805306368 | bytes 6840320 | tf_op jit(solution)/shard_map/attend_back/pallas_call | solution.py:41
  34.8 1.1 %collective-permute-done.17.refs_0_ = bf16[2,2,64,256]{3,2,1,0:T(8,128)(2,1)S(1)} collective-permute-done((bf16[2,2,64,256]{3,2,1,0:T(8,128)(2,1)S(1)}, bf16[2,2,64,256]{3,2,1,0:T(8,128)(2,1)S(1)}, u32[]{:S(2)}, u32[]{:S(2)}) %collective-permute-start.17) | collective-permute-done | bytes 131104 | tf_op jit(solution)/shard_map/ppermute | solution.py:26
  35.9 0.1 sum_heads.3
  36.0 0.8 %collective-permute-start.19 = (bf16[2,64,256]{2,1,0:T(8,128)(2,1)S(1)}, bf16[2,64,256]{2,1,0:T(8,128)(2,1)S(1)}, u32[]{:S(2)}, u32[]{:S(2)}) collective-permute-start(bf16[2,64,256]{2,1,0:T(8,128)(2,1)S(1)} %get-tuple-element.110), channel_id=1, source_target_pairs={{0,4},{1,5},{2,6},{3,7},{4,0},{5,1},{6,2},{7,3},{8,12},{9,13},{10,... | collective-permute-start | bytes 196616 | tf_op jit(solution)/shard_map/ppermute | solution.py:26
  36.8 1.8 %collective-permute-start.20 = (bf16[2,64,256]{2,1,0:T(8,128)(2,1)S(1)}, bf16[2,64,256]{2,1,0:T(8,128)(2,1)S(1)}, u32[]{:S(2)}, u32[]{:S(2)}) collective-permute-start(bf16[2,64,256]{2,1,0:T(8,128)(2,1)S(1)} %get-tuple-element.111), channel_id=1, source_target_pairs={{0,6},{1,7},{2,4},{3,5},{4,2},{5,3},{6,0},{7,1},{8,14},{9,15},{10,... | collective-permute-start | bytes 196616 | tf_op jit(solution)/shard_map/ppermute | solution.py:26
  38.6 0.1 sum_heads.2
  38.6 1.0 %collective-permute-start.21 = (bf16[2,64,256]{2,1,0:T(8,128)(2,1)S(1)}, bf16[2,64,256]{2,1,0:T(8,128)(2,1)S(1)}, u32[]{:S(2)}, u32[]{:S(2)}) collective-permute-start(bf16[2,64,256]{2,1,0:T(8,128)(2,1)S(1)} %get-tuple-element.112), channel_id=1, source_target_pairs={{0,2},{1,3},{2,0},{3,1},{4,6},{5,7},{6,4},{7,5},{8,10},{9,11},{10,... | collective-permute-start | bytes 196616 | tf_op jit(solution)/shard_map/ppermute | solution.py:26
  39.7 1.5 %collective-permute-start.16 = (bf16[2,64,1024]{2,1,0:T(8,128)(2,1)S(1)}, bf16[2,64,1024]{2,1,0:T(8,128)(2,1)S(1)}, u32[]{:S(2)}, u32[]{:S(2)}) collective-permute-start(bf16[2,64,1024]{2,1,0:T(8,128)(2,1)S(1)} %get-tuple-element.105), channel_id=1, source_target_pairs={{0,8},{8,0},{16,24},{24,16},{1,9},{9,1},{17,25},{25,17},{2,10},{10... | collective-permute-start | bytes 786440 | tf_op jit(solution)/shard_map/ppermute | solution.py:26
  41.2 2.4 %collective-permute-done.19.refs_0_ = bf16[2,64,256]{2,1,0:T(8,128)(2,1)S(1)} collective-permute-done((bf16[2,64,256]{2,1,0:T(8,128)(2,1)S(1)}, bf16[2,64,256]{2,1,0:T(8,128)(2,1)S(1)}, u32[]{:S(2)}, u32[]{:S(2)}) %collective-permute-start.19) | collective-permute-done | bytes 65568 | tf_op jit(solution)/shard_map/ppermute | solution.py:26
  43.6 0.5 %collective-permute-done.21.refs_2_ = bf16[2,64,256]{2,1,0:T(8,128)(2,1)S(1)} collective-permute-done((bf16[2,64,256]{2,1,0:T(8,128)(2,1)S(1)}, bf16[2,64,256]{2,1,0:T(8,128)(2,1)S(1)}, u32[]{:S(2)}, u32[]{:S(2)}) %collective-permute-start.21) | collective-permute-done | bytes 65568 | tf_op jit(solution)/shard_map/ppermute | solution.py:26
  44.1 1.6 %collective-permute-start.22 = (bf16[64,256]{1,0:T(8,128)(2,1)S(1)}, bf16[64,256]{1,0:T(8,128)(2,1)S(1)}, u32[]{:S(2)}, u32[]{:S(2)}) collective-permute-start(bf16[64,256]{1,0:T(8,128)(2,1)S(1)} %get-tuple-element.114), channel_id=1, source_target_pairs={{0,8},{8,0},{16,24},{24,16},{1,9},{9,1},{17,25},{25,17},{2,10},{10... | collective-permute-start | bytes 98312 | tf_op jit(solution)/shard_map/ppermute | solution.py:26
  45.7 1.1 %collective-permute-done.16.refs_1_ = bf16[2,64,1024]{2,1,0:T(8,128)(2,1)S(1)} collective-permute-done((bf16[2,64,1024]{2,1,0:T(8,128)(2,1)S(1)}, bf16[2,64,1024]{2,1,0:T(8,128)(2,1)S(1)}, u32[]{:S(2)}, u32[]{:S(2)}) %collective-permute-start.16) | collective-permute-done | bytes 262176 | tf_op jit(solution)/shard_map/ppermute | solution.py:26
  46.9 0.8 %finish_q.1 = (bf16[64,2048]{1,0:T(8,128)(2,1)}, bf16[64,2048]{1,0:T(8,128)(2,1)}, f32[8,128]{1,0:T(8,128)S(1)}) custom-call(s32[1]{0:T(128)} %bitcast.group_ref, bf16[2,64,1024]{2,1,0:T(8,128)(2,1)S(1)} %get-tuple-element.104.refs_0_, bf16[2,64,1024]{2,1,0:T(8,128)(2,1)S(1)} %collective-permute-done.16.refs_1_), custom_call_target="tpu_custom_call" | custom-call | bytes 1052676 | tf_op jit(solution)/shard_map/finish_q/pallas_call | solution.py:41
  47.7 0.4 collective-permute-done.22.refs_1_
  48.1 0.6 %finish_kv.1 = (bf16[64,256]{1,0:T(8,128)(2,1)}, bf16[64,256]{1,0:T(8,128)(2,1)}) custom-call(s32[1]{0:T(128)} %bitcast.group_ref, bf16[64,256]{1,0:T(8,128)(2,1)S(1)} %get-tuple-element.113.refs_0_, bf16[64,256]{1,0:T(8,128)(2,1)S(1)} %collective-permute-done.22.refs_1_, f32[8,128]{1,0:T(8,128)S(1)} %get-tuple-element.115.refs_2_), custom_call_target="tpu_custom_call" | custom-call | bytes 135172 | tf_op jit(solution)/shard_map/finish_kv/pallas_call | solution.py:41
  (28 shorter events, 0.2 us)
Async XLA Ops:
  1.4 5.0 %collective-permute-start.1 = (bf16[64,256]{1,0:T(8,128)(2,1)S(1)}, bf16[64,256]{1,0:T(8,128)(2,1)S(1)}, u32[]{:S(2)}, u32[]{:S(2)}) collective-permute-start(bf16[64,256]{1,0:T(8,128)(2,1)S(1)} %pad_maximum_fusion.1), channel_id=1, source_target_pairs={{0,8},{8,0},{16,24},{24,16},{1,9},{9,1},{17,25},{25,17},{2,10},{10... | collective-permute-start | bytes 98312 | tf_op jit(solution)/shard_map/ppermute | solution.py:26
  4.4 0.9 %copy-start = (bf16[2,32,2048]{2,1,0:T(8,128)(2,1)S(1)}, bf16[2,32,2048]{2,1,0:T(8,128)(2,1)}, u32[]{:S(2)}) copy-start(bf16[2,32,2048]{2,1,0:T(8,128)(2,1)} %param.5) | copy-start | bytes 786436
  5.4 0.9 %copy-start.1 = (bf16[2,32,2048]{2,1,0:T(8,128)(2,1)S(1)}, bf16[2,32,2048]{2,1,0:T(8,128)(2,1)}, u32[]{:S(2)}) copy-start(bf16[2,32,2048]{2,1,0:T(8,128)(2,1)} %param.8) | copy-start | bytes 786436
  6.4 10.7 %collective-permute-start = (bf16[2,64,1024]{2,1,0:T(8,128)(2,1)S(1)}, bf16[2,64,1024]{2,1,0:T(8,128)(2,1)S(1)}, u32[]{:S(2)}, u32[]{:S(2)}) collective-permute-start(bf16[2,64,1024]{2,1,0:T(8,128)(2,1)S(1)} %get-tuple-element.62), channel_id=1, source_target_pairs={{0,8},{8,0},{16,24},{24,16},{1,9},{9,1},{17,25},{25,17},{2,10},{10... | collective-permute-start | bytes 786440 | tf_op jit(solution)/shard_map/ppermute | solution.py:26
  6.5 4.7 %collective-permute-start.4 = (bf16[2,64,256]{2,1,0:T(8,128)(2,1)S(1)}, bf16[2,64,256]{2,1,0:T(8,128)(2,1)S(1)}, u32[]{:S(2)}, u32[]{:S(2)}) collective-permute-start(bf16[2,64,256]{2,1,0:T(8,128)(2,1)S(1)} %pad_maximum_fusion.refs_0_), channel_id=1, source_target_pairs={{0,2},{1,3},{2,0},{3,1},{4,6},{5,7},{6,4},{7,5},{8,10},{9,11},{10,... | collective-permute-start | bytes 196616 | tf_op jit(solution)/shard_map/ppermute | solution.py:26
  8.7 6.3 %collective-permute-start.3 = (bf16[2,64,256]{2,1,0:T(8,128)(2,1)S(1)}, bf16[2,64,256]{2,1,0:T(8,128)(2,1)S(1)}, u32[]{:S(2)}, u32[]{:S(2)}) collective-permute-start(bf16[2,64,256]{2,1,0:T(8,128)(2,1)S(1)} %pad_maximum_fusion.refs_0_), channel_id=1, source_target_pairs={{0,6},{1,7},{2,4},{3,5},{4,2},{5,3},{6,0},{7,1},{8,14},{9,15},{10,... | collective-permute-start | bytes 196616 | tf_op jit(solution)/shard_map/ppermute | solution.py:26
  11.1 5.9 %collective-permute-start.2 = (bf16[2,64,256]{2,1,0:T(8,128)(2,1)S(1)}, bf16[2,64,256]{2,1,0:T(8,128)(2,1)S(1)}, u32[]{:S(2)}, u32[]{:S(2)}) collective-permute-start(bf16[2,64,256]{2,1,0:T(8,128)(2,1)S(1)} %pad_maximum_fusion.refs_0_), channel_id=1, source_target_pairs={{0,4},{1,5},{2,6},{3,7},{4,0},{5,1},{6,2},{7,3},{8,12},{9,13},{10,... | collective-permute-start | bytes 196616 | tf_op jit(solution)/shard_map/ppermute | solution.py:26
  11.3 8.6 %collective-permute-start.7 = (bf16[2,2,64,256]{3,2,1,0:T(8,128)(2,1)S(1)}, bf16[2,2,64,256]{3,2,1,0:T(8,128)(2,1)S(1)}, u32[]{:S(2)}, u32[]{:S(2)}) collective-permute-start(bf16[2,2,64,256]{3,2,1,0:T(8,128)(2,1)S(1)} %stack.22.refs_2_.refs_1_), channel_id=1, source_target_pairs={{0,16},{8,24},{16,0},{24,8},{1,17},{9,25},{17,1},{25,9},{2,18},{10... | collective-permute-start | bytes 393224 | tf_op jit(solution)/shard_map/ppermute | solution.py:26
  17.1 6.4 %collective-permute-start.8 = (bf16[2,2,64,256]{3,2,1,0:T(8,128)(2,1)S(1)}, bf16[2,2,64,256]{3,2,1,0:T(8,128)(2,1)S(1)}, u32[]{:S(2)}, u32[]{:S(2)}) collective-permute-start(bf16[2,2,64,256]{3,2,1,0:T(8,128)(2,1)S(1)} %get-tuple-element.69.refs_0_.refs_1_), channel_id=1, source_target_pairs={{0,16},{8,24},{16,0},{24,8},{1,17},{9,25},{17,1},{25,9},{2,18},{10... | collective-permute-start | bytes 393224 | tf_op jit(solution)/shard_map/ppermute | solution.py:26
  18.7 2.8 %collective-permute-start.5 = (bf16[2,2,64,256]{3,2,1,0:T(8,128)(2,1)S(1)}, bf16[2,2,64,256]{3,2,1,0:T(8,128)(2,1)S(1)}, u32[]{:S(2)}, u32[]{:S(2)}) collective-permute-start(bf16[2,2,64,256]{3,2,1,0:T(8,128)(2,1)S(1)} %get-tuple-element.69.refs_0_.refs_1_), channel_id=1, source_target_pairs={{0,1},{1,0},{2,3},{3,2},{4,5},{5,4},{6,7},{7,6},{8,9},{9,8},{10,11... | collective-permute-start | bytes 393224 | tf_op jit(solution)/shard_map/ppermute | solution.py:26
  18.7 2.7 %collective-permute-start.6 = (bf16[2,2,64,256]{3,2,1,0:T(8,128)(2,1)S(1)}, bf16[2,2,64,256]{3,2,1,0:T(8,128)(2,1)S(1)}, u32[]{:S(2)}, u32[]{:S(2)}) collective-permute-start(bf16[2,2,64,256]{3,2,1,0:T(8,128)(2,1)S(1)} %get-tuple-element.70), channel_id=1, source_target_pairs={{0,1},{1,0},{2,3},{3,2},{4,5},{5,4},{6,7},{7,6},{8,9},{9,8},{10,11... | collective-permute-start | bytes 393224 | tf_op jit(solution)/shard_map/ppermute | solution.py:26
  19.9 4.8 %collective-permute-start.10 = (bf16[2,2,64,256]{3,2,1,0:T(8,128)(2,1)S(1)}, bf16[2,2,64,256]{3,2,1,0:T(8,128)(2,1)S(1)}, u32[]{:S(2)}, u32[]{:S(2)}) collective-permute-start(bf16[2,2,64,256]{3,2,1,0:T(8,128)(2,1)S(1)} %collective-permute-done.7.refs_0_), channel_id=1, source_target_pairs={{0,1},{1,0},{2,3},{3,2},{4,5},{5,4},{6,7},{7,6},{8,9},{9,8},{10,11... | collective-permute-start | bytes 393224 | tf_op jit(solution)/shard_map/ppermute | solution.py:26
  23.4 1.5 %collective-permute-start.9 = (bf16[2,2,64,256]{3,2,1,0:T(8,128)(2,1)S(1)}, bf16[2,2,64,256]{3,2,1,0:T(8,128)(2,1)S(1)}, u32[]{:S(2)}, u32[]{:S(2)}) collective-permute-start(bf16[2,2,64,256]{3,2,1,0:T(8,128)(2,1)S(1)} %collective-permute-done.8.refs_0_), channel_id=1, source_target_pairs={{0,1},{1,0},{2,3},{3,2},{4,5},{5,4},{6,7},{7,6},{8,9},{9,8},{10,11... | collective-permute-start | bytes 393224 | tf_op jit(solution)/shard_map/ppermute | solution.py:26
  27.6 1.9 %collective-permute-start.12 = (bf16[2,2,64,256]{3,2,1,0:T(8,128)(2,1)S(1)}, bf16[2,2,64,256]{3,2,1,0:T(8,128)(2,1)S(1)}, u32[]{:S(2)}, u32[]{:S(2)}) collective-permute-start(bf16[2,2,64,256]{3,2,1,0:T(8,128)(2,1)S(1)} %get-tuple-element.94), channel_id=1, source_target_pairs={{0,1},{1,0},{2,3},{3,2},{4,5},{5,4},{6,7},{7,6},{8,9},{9,8},{10,11... | collective-permute-start | bytes 393224 | tf_op jit(solution)/shard_map/ppermute | solution.py:26
  28.1 1.5 %collective-permute-start.11 = (bf16[2,2,64,256]{3,2,1,0:T(8,128)(2,1)S(1)}, bf16[2,2,64,256]{3,2,1,0:T(8,128)(2,1)S(1)}, u32[]{:S(2)}, u32[]{:S(2)}) collective-permute-start(bf16[2,2,64,256]{3,2,1,0:T(8,128)(2,1)S(1)} %get-tuple-element.92), channel_id=1, source_target_pairs={{0,1},{1,0},{2,3},{3,2},{4,5},{5,4},{6,7},{7,6},{8,9},{9,8},{10,11... | collective-permute-start | bytes 393224 | tf_op jit(solution)/shard_map/ppermute | solution.py:26
  29.6 1.3 %collective-permute-start.13 = (bf16[64,128]{1,0:T(8,128)(2,1)S(1)}, bf16[64,128]{1,0:T(8,128)(2,1)S(1)}, u32[]{:S(2)}, u32[]{:S(2)}) collective-permute-start(bf16[64,128]{1,0:T(8,128)(2,1)S(1)} %slice_bitcast_fusion), channel_id=1, source_target_pairs={{0,1},{1,0},{2,3},{3,2},{4,5},{5,4},{6,7},{7,6},{8,9},{9,8},{10,11... | collective-permute-start | bytes 49160 | tf_op jit(solution)/shard_map/ppermute | solution.py:26
  30.1 5.9 %collective-permute-start.17 = (bf16[2,2,64,256]{3,2,1,0:T(8,128)(2,1)S(1)}, bf16[2,2,64,256]{3,2,1,0:T(8,128)(2,1)S(1)}, u32[]{:S(2)}, u32[]{:S(2)}) collective-permute-start(bf16[2,2,64,256]{3,2,1,0:T(8,128)(2,1)S(1)} %sum_cores.3), channel_id=1, source_target_pairs={{0,16},{8,24},{16,0},{24,8},{1,17},{9,25},{17,1},{25,9},{2,18},{10... | collective-permute-start | bytes 393224 | tf_op jit(solution)/shard_map/ppermute | solution.py:26
  32.1 3.9 %collective-permute-start.18 = (bf16[2,2,64,256]{3,2,1,0:T(8,128)(2,1)S(1)}, bf16[2,2,64,256]{3,2,1,0:T(8,128)(2,1)S(1)}, u32[]{:S(2)}, u32[]{:S(2)}) collective-permute-start(bf16[2,2,64,256]{3,2,1,0:T(8,128)(2,1)S(1)} %get-tuple-element.108), channel_id=1, source_target_pairs={{0,1},{1,0},{2,3},{3,2},{4,5},{5,4},{6,7},{7,6},{8,9},{9,8},{10,11... | collective-permute-start | bytes 393224 | tf_op jit(solution)/shard_map/ppermute | solution.py:26
  32.5 6.1 %collective-permute-start.14 = (bf16[2,2,64,256]{3,2,1,0:T(8,128)(2,1)S(1)}, bf16[2,2,64,256]{3,2,1,0:T(8,128)(2,1)S(1)}, u32[]{:S(2)}, u32[]{:S(2)}) collective-permute-start(bf16[2,2,64,256]{3,2,1,0:T(8,128)(2,1)S(1)} %sum_cores.2), channel_id=1, source_target_pairs={{0,16},{8,24},{16,0},{24,8},{1,17},{9,25},{17,1},{25,9},{2,18},{10... | collective-permute-start | bytes 393224 | tf_op jit(solution)/shard_map/ppermute | solution.py:26
  33.4 5.2 %collective-permute-start.15 = (bf16[2,2,64,256]{3,2,1,0:T(8,128)(2,1)S(1)}, bf16[2,2,64,256]{3,2,1,0:T(8,128)(2,1)S(1)}, u32[]{:S(2)}, u32[]{:S(2)}) collective-permute-start(bf16[2,2,64,256]{3,2,1,0:T(8,128)(2,1)S(1)} %get-tuple-element.101), channel_id=1, source_target_pairs={{0,1},{1,0},{2,3},{3,2},{4,5},{5,4},{6,7},{7,6},{8,9},{9,8},{10,11... | collective-permute-start | bytes 393224 | tf_op jit(solution)/shard_map/ppermute | solution.py:26
  36.0 7.6 %collective-permute-start.19 = (bf16[2,64,256]{2,1,0:T(8,128)(2,1)S(1)}, bf16[2,64,256]{2,1,0:T(8,128)(2,1)S(1)}, u32[]{:S(2)}, u32[]{:S(2)}) collective-permute-start(bf16[2,64,256]{2,1,0:T(8,128)(2,1)S(1)} %get-tuple-element.110), channel_id=1, source_target_pairs={{0,4},{1,5},{2,6},{3,7},{4,0},{5,1},{6,2},{7,3},{8,12},{9,13},{10,... | collective-permute-start | bytes 196616 | tf_op jit(solution)/shard_map/ppermute | solution.py:26
  36.8 6.8 %collective-permute-start.20 = (bf16[2,64,256]{2,1,0:T(8,128)(2,1)S(1)}, bf16[2,64,256]{2,1,0:T(8,128)(2,1)S(1)}, u32[]{:S(2)}, u32[]{:S(2)}) collective-permute-start(bf16[2,64,256]{2,1,0:T(8,128)(2,1)S(1)} %get-tuple-element.111), channel_id=1, source_target_pairs={{0,6},{1,7},{2,4},{3,5},{4,2},{5,3},{6,0},{7,1},{8,14},{9,15},{10,... | collective-permute-start | bytes 196616 | tf_op jit(solution)/shard_map/ppermute | solution.py:26
  38.6 5.5 %collective-permute-start.21 = (bf16[2,64,256]{2,1,0:T(8,128)(2,1)S(1)}, bf16[2,64,256]{2,1,0:T(8,128)(2,1)S(1)}, u32[]{:S(2)}, u32[]{:S(2)}) collective-permute-start(bf16[2,64,256]{2,1,0:T(8,128)(2,1)S(1)} %get-tuple-element.112), channel_id=1, source_target_pairs={{0,2},{1,3},{2,0},{3,1},{4,6},{5,7},{6,4},{7,5},{8,10},{9,11},{10,... | collective-permute-start | bytes 196616 | tf_op jit(solution)/shard_map/ppermute | solution.py:26
  39.7 7.2 %collective-permute-start.16 = (bf16[2,64,1024]{2,1,0:T(8,128)(2,1)S(1)}, bf16[2,64,1024]{2,1,0:T(8,128)(2,1)S(1)}, u32[]{:S(2)}, u32[]{:S(2)}) collective-permute-start(bf16[2,64,1024]{2,1,0:T(8,128)(2,1)S(1)} %get-tuple-element.105), channel_id=1, source_target_pairs={{0,8},{8,0},{16,24},{24,16},{1,9},{9,1},{17,25},{25,17},{2,10},{10... | collective-permute-start | bytes 786440 | tf_op jit(solution)/shard_map/ppermute | solution.py:26
  44.1 4.0 %collective-permute-start.22 = (bf16[64,256]{1,0:T(8,128)(2,1)S(1)}, bf16[64,256]{1,0:T(8,128)(2,1)S(1)}, u32[]{:S(2)}, u32[]{:S(2)}) collective-permute-start(bf16[64,256]{1,0:T(8,128)(2,1)S(1)} %get-tuple-element.114), channel_id=1, source_target_pairs={{0,8},{8,0},{16,24},{24,16},{1,9},{9,1},{17,25},{25,17},{2,10},{10... | collective-permute-start | bytes 98312 | tf_op jit(solution)/shard_map/ppermute | solution.py:26

commit v13 on v11

--- a/solution.py
+++ b/solution.py
@@ -164,12 +164,12 @@
             total = total + jnp.sum(self.fold(part), axis=0)
         return jnp.sum(total, axis=0, keepdims=True)
 
-    def store_heads(self, out_ref, kind, tile, turned):
+    def store_heads(self, out_ref, tile, turned):
         s, start = self.tiles[tile]
         block = turned.T.astype(BF)
         for n in range(self.group):
             piece = block[n * self.tile_rows : (n + 1) * self.tile_rows]
-            out_ref[kind, pl.ds(start, self.tile_rows), pl.ds(n * HD, HD)] = piece
+            out_ref[pl.ds(start, self.tile_rows), pl.ds(n * HD, HD)] = piece
 
     def back(self, dkv_refs, p_ref, ds_ref, q_ref, do_ref):
         shape = (self.z_part, self.kv, self.rows, HD)
@@ -268,12 +268,13 @@
     plan.back(dkv_refs, p_ref, ds_ref, q_all, do_all)
 
 
-def back_kernel(plan, rows_at, last, order, q_all, do_all, do_t, e_ref, scale_ref, delta_ref, q_grad_in, *refs):
+def back_kernel(plan, rows_at, last, order, stores, q_all, do_all, do_t, e_ref, scale_ref, delta_ref, q_grad_in, *refs):
     count = len(rows_at)
-    mixed_ref, refs = refs[:last], refs[last:]
+    mixed_ref, refs = refs[:stores], refs[stores:]
     kv_refs, refs = refs[:count], refs[count + order :]
     refs, (turned_ref, p_ref, ds_ref) = refs[:-3], refs[-3:]
     outs, dkv_refs = refs[:-count], refs[-count:]
+    att_refs, outs = outs[: plan.kv * stores], outs[plan.kv * stores :]
     spans = [plan.at(tile) for tile in range(len(plan.tiles))]
     for at in spans:
         for i, ref in enumerate(kv_refs):
@@ -288,11 +289,11 @@
         for i in range(count):
             q_grad = q_grad + dot(turned_ref[pl.ds(0, HD), plan.keys_at(i)], ds_ref[plan.keys_at(i), at])
         if last:
-            out_ref = outs[plan.tiles[tile][0]]
-            plan.store_heads(out_ref, 0, tile, mixed_ref[0][:, at].astype(F32))
-            plan.store_heads(out_ref, 1, tile, q_grad * SCALING)
+            plan.store_heads(outs[plan.tiles[tile][0]], tile, q_grad * SCALING)
         else:
             outs[0][:, at] = q_grad
+        if stores:
+            plan.store_heads(att_refs[plan.tiles[tile][0]], tile, mixed_ref[0][:, at].astype(F32))
 
 
 def add_kernel(*refs):
@@ -302,8 +303,8 @@
     refs[-1][...] = total.astype(BF)
 
 
-def sum_heads_kernel(parts, *refs):
-    for m_z, out_ref in enumerate(refs[parts:]):
+def sum_heads_kernel(parts, order, *refs):
+    for m_z, out_ref in enumerate(refs[parts + order :]):
         total = refs[0][m_z].astype(F32)
         for ref in refs[1:parts]:
             total = total + ref[m_z].astype(F32)
@@ -339,17 +340,17 @@
 
 
 def finish_q_kernel(kv, group_ref, *refs):
-    att_ref, grad_ref, done_ref = refs[kv:]
+    att_ref, grad_ref, done_ref = refs[2 * kv :]
     done_ref[...] = jnp.zeros_like(done_ref)
-    width = refs[0].shape[2]
+    width = refs[0].shape[1]
     for g in range(kv):
 
         @pl.when(group_ref[0] == g)
         def _():
             for s in range(kv):
                 cols = pl.ds((g ^ s) * width, width)
-                att_ref[:, cols] = refs[s][0]
-                grad_ref[:, cols] = refs[s][1]
+                att_ref[:, cols] = refs[s][...]
+                grad_ref[:, cols] = refs[kv + s][...]
 
 
 def shards(queries, key_vectors, value_vectors, out_grad, block_order):
@@ -448,7 +449,7 @@
     query_rows = plan.query_rows
     row, column_out = f32(1, query_rows), f32(HD, query_rows)
 
-    def forward(name, chunks, kv_refs, order):
+    def forward(name, chunks, kv_refs, order, flops=8):
         size = len(chunks) * keys
         return call(
             functools.partial(part_kernel, plan, chunks),
@@ -458,7 +459,7 @@
             None,
             [pltpu.VMEM((2 * HD, size), BF)],
             size * 4 * HD,
-            8 * size * query_rows * HD,
+            flops * size * query_rows * HD,
         )
 
     mids, order = [None] * parts, []
@@ -468,7 +469,8 @@
             order = [near[0]]
             for pair in columns:
                 pair[p] = after([pair[p]], order)[0]
-        mids[p] = forward("attend_mid", [c for c in mid_chunks if c[2] == p], [pair[p] for pair in columns], order)
+        mid_part = [c for c in mid_chunks if c[2] == p]
+        mids[p] = forward("attend_mid", mid_part, [pair[p] for pair in columns], order)
         order = [mids[p][1]]
     far_kv = [swap(pair[p], "ctx", core) for pair in columns for core in range(1, cores) for p in each]
     far_keys = len(far_kv) * keys
@@ -491,13 +493,13 @@
     (near_scale, *mid_scales), outs = outs[: 1 + parts], outs[1 + parts :]
     (delta, mixed, q_grad), far_dkv = outs[:3], outs[3:]
 
-    def back(rows_at, last, e, scale, q_grad, kv_refs, order):
+    def back(rows_at, last, e, scale, q_grad, kv_refs, order, stores=False):
         count = len(rows_at)
-        q_outs = [bf(2, rows, width)] * kv if last else [column_out]
+        q_outs = [bf(rows, width)] * (kv * stores) + ([bf(rows, width)] * kv if last else [column_out])
         outs = call(
-            functools.partial(back_kernel, plan, rows_at, last, len(order)),
+            functools.partial(back_kernel, plan, rows_at, last, len(order), stores),
             "attend_back",
-            (q_all, do_all, do_t, e, scale, delta, q_grad, *[mixed] * last, *kv_refs, *order),
+            (q_all, do_all, do_t, e, scale, delta, q_grad, *[mixed] * stores, *kv_refs, *order),
             q_outs + [dkv] * count,
             None,
             [
@@ -526,24 +528,34 @@
             sums[p].append(swap(totals[-1], "head", (a + 1) * kv))
     order = [swap(totals[-1][0, 0, :, :HD], "ctx", 1)] if cores > 1 else []
     for core in reversed(range(cores)):
+        stores = core == cores - 1
         outs, parts_dkv = back(
-            [core * parts + p for p in each], core == 0, near_e, near_scale, q_grad, near_kv[core], order
+            [core * parts + p for p in each],
+            core == 0,
+            near_e,
+            near_scale,
+            q_grad,
+            near_kv[core],
+            order,
+            stores,
         )
+        if stores:
+            att_parts, outs = with_swaps(outs[:kv]), outs[kv:]
         q_grad = outs[0]
         for p in range(parts):
             sums[p].append(swap(parts_dkv[p], "ctx", core) if core else parts_dkv[p])
-    q_parts = outs[:kv]
+    q_grad_parts = outs
     z_parts = [None] * z_devices
     for p in range(parts):
+        order = att_parts[1:] if p else []
         totals = call(
-            functools.partial(sum_heads_kernel, len(sums[p])),
+            functools.partial(sum_heads_kernel, len(sums[p]), len(order)),
             "sum_heads",
-            sums[p],
+            (*sums[p], *order),
             [bf(kv, rows, 2 * HD)] * z_part,
         )
-
         if p == parts - 1:
-            q_parts = with_swaps(after(q_parts, totals[:1]))
+            q_grad_parts = with_swaps(after(q_grad_parts, totals[:1]))
         for m, total in zip(plan.zone(p), totals):
             z_parts[m] = swap(total, "ctx", m * cores) if m else total
     ordered = [z_parts[m] for p in each for m in plan.zone(p)]
@@ -557,9 +569,9 @@
     attended, query_grad, done = call(
         functools.partial(finish_q_kernel, kv),
         "finish_q",
-        (own_group, *q_parts),
+        (own_group, *att_parts, *q_grad_parts),
         [bf(rows, query_width)] * 2 + [f32(8, HD)],
-        [SMEM] + [VMEM] * kv,
+        [SMEM] + [VMEM] * (2 * kv),
     )
     key_grad, value_grad = call(
         functools.partial(finish_kv_kernel, kv),

time: 49 us -> 50.5 us (1.031)
  waiting for transfers between devices: 10.5 us -> 12.2 us
    ppermute x23 -> x24, waiting for transfers between devices: 10.5 us -> 12.2 us  [swap(): return lax.ppermute(block, axis, [(i, i ^ mask) for i in range(size)])]
    ppermute x23 -> x24, starting transfers between devices: 21.6 us -> 21.5 us  [swap(): return lax.ppermute(block, axis, [(i, i ^ mask) for i in range(size)])]
  transfers between devices with their start and end apart: 23 -> 24, of which waited for: 10 -> 7; matrix products, arithmetic and copies ran while one was open for 2% -> 1% of each run, Pallas kernels for 18% -> 18%
where the time goes in v13:
time: 50.5 us; the launch traced here: 50.2 us
  starting transfers between devices  21.5 us (43%)
  Pallas kernels  12.3 us (24%)
  waiting for transfers between devices  12.2 us (24%)
  local copies, waits for them, and re-layouts  1.9 us (4%)
  other arithmetic  1.53 us (3%)
  between operations  0.89 us (2%)
    ppermute x24, starting transfers between devices, swap(): return lax.ppermute(block, axis, [(i, i ^ mask) for i in range(size)])  21.5 us
    pallas_call x20, Pallas kernels, call(): pl.pallas_call(kernel, out_shape=list(outs), in_specs=specs or [VMEM] * l...  12.3 us
    ppermute x24, waiting for transfers between devices, swap(): return lax.ppermute(block, axis, [(i, i ^ mask) for i in range(size)])  12.2 us
    unnamed x4, local copies, waits for them, and re-layouts  1.9 us
  transfers between devices with their start and end apart: 24, of which 7 were waited for; matrix products, arithmetic and copies ran while one was open for 1% of the time, Pallas kernels for 18%

profile of v13, /device:TPU:0, one launch (start us, length us, event | category | flops | bytes accessed | tf_op | source)
XLA Modules:
  0.0 50.2 jit_solution(2089881794976052482)
XLA Ops:
  0.6 0.8 %broadcast_select_fusion.2 = (bf16[64,128]{1,0:T(8,128)(2,1)S(1)}, bf16[64,128]{1,0:T(8,128)(2,1)S(1)}, bf16[64,128]{1,0:T(8,128)(2,1)S(1)}, bf16[64,128]{1,0:T(8,128)(2,1)S(1)}) fusion(pred[]{:T(512)S(6)} %eq.12, bf16[64,256]{1,0:T(8,128)(2,1)} %bitcast.18, pred[]{:T(512)S(6)} %eq.13, bf16[64,256]{1,0:T(8,128)(2,1)} %bitcast.19), kind=kLoop, calls=%fused_computation.6 | loop fusion | flops 32768 | bytes 131074 | tf_op jit(solution)/shard_map/jit(_where)/select_n | solution.py:397
  1.4 3.0 %collective-permute-start.1 = (bf16[64,256]{1,0:T(8,128)(2,1)S(1)}, bf16[64,256]{1,0:T(8,128)(2,1)S(1)}, u32[]{:S(2)}, u32[]{:S(2)}) collective-permute-start(bf16[64,256]{1,0:T(8,128)(2,1)S(1)} %pad_maximum_fusion.1), channel_id=1, source_target_pairs={{0,8},{8,0},{16,24},{24,16},{1,9},{9,1},{17,25},{25,17},{2,10},{10... | collective-permute-start | bytes 98312 | tf_op jit(solution)/shard_map/ppermute | solution.py:26
  4.4 0.9 %copy-done = bf16[2,32,2048]{2,1,0:T(8,128)(2,1)S(1)} copy-done((bf16[2,32,2048]{2,1,0:T(8,128)(2,1)S(1)}, bf16[2,32,2048]{2,1,0:T(8,128)(2,1)}, u32[]{:S(2)}) %copy-start) | copy-done | bytes 262168
  5.4 0.9 %copy-done.1 = bf16[2,32,2048]{2,1,0:T(8,128)(2,1)S(1)} copy-done((bf16[2,32,2048]{2,1,0:T(8,128)(2,1)S(1)}, bf16[2,32,2048]{2,1,0:T(8,128)(2,1)}, u32[]{:S(2)}) %copy-start.1) | copy-done | bytes 262168
  6.4 0.1 collective-permute-start
  6.5 0.0 collective-permute-done.1
  6.5 2.1 %collective-permute-start.4 = (bf16[2,64,256]{2,1,0:T(8,128)(2,1)S(1)}, bf16[2,64,256]{2,1,0:T(8,128)(2,1)S(1)}, u32[]{:S(2)}, u32[]{:S(2)}) collective-permute-start(bf16[2,64,256]{2,1,0:T(8,128)(2,1)S(1)} %pad_maximum_fusion.refs_0_), channel_id=1, source_target_pairs={{0,2},{1,3},{2,0},{3,1},{4,6},{5,7},{6,4},{7,5},{8,10},{9,11},{10,... | collective-permute-start | bytes 196616 | tf_op jit(solution)/shard_map/ppermute | solution.py:26
  8.7 2.5 %collective-permute-start.3 = (bf16[2,64,256]{2,1,0:T(8,128)(2,1)S(1)}, bf16[2,64,256]{2,1,0:T(8,128)(2,1)S(1)}, u32[]{:S(2)}, u32[]{:S(2)}) collective-permute-start(bf16[2,64,256]{2,1,0:T(8,128)(2,1)S(1)} %pad_maximum_fusion.refs_0_), channel_id=1, source_target_pairs={{0,6},{1,7},{2,4},{3,5},{4,2},{5,3},{6,0},{7,1},{8,14},{9,15},{10,... | collective-permute-start | bytes 196616 | tf_op jit(solution)/shard_map/ppermute | solution.py:26
  11.1 0.1 collective-permute-start.2
  11.2 0.0 collective-permute-done.4.refs_1_
  11.3 1.7 %collective-permute-start.7 = (bf16[2,2,64,256]{3,2,1,0:T(8,128)(2,1)S(1)}, bf16[2,2,64,256]{3,2,1,0:T(8,128)(2,1)S(1)}, u32[]{:S(2)}, u32[]{:S(2)}) collective-permute-start(bf16[2,2,64,256]{3,2,1,0:T(8,128)(2,1)S(1)} %stack.22.refs_2_.refs_1_), channel_id=1, source_target_pairs={{0,16},{8,24},{16,0},{24,8},{1,17},{9,25},{17,1},{25,9},{2,18},{10... | collective-permute-start | bytes 393224 | tf_op jit(solution)/shard_map/ppermute | solution.py:26
  12.9 0.7 %pad_add_fusion.info_ref = s32[18]{0:T(128)S(1)} fusion(s32[16]{0:T(128)} %param.9, s32[1]{0:T(128)} %bitcast.2, s32[1]{0:T(128)} %bitcast.1), kind=kLoop, calls=%fused_computation.8 | loop fusion | flops 36 | bytes 144 | tf_op jit(solution)/shard_map/concatenate | solution.py:371
  13.7 0.5 %collective-permute-done.refs_1_ = bf16[2,64,1024]{2,1,0:T(8,128)(2,1)S(1)} collective-permute-done((bf16[2,64,1024]{2,1,0:T(8,128)(2,1)S(1)}, bf16[2,64,1024]{2,1,0:T(8,128)(2,1)S(1)}, u32[]{:S(2)}, u32[]{:S(2)}) %collective-permute-start) | collective-permute-done | bytes 262176 | tf_op jit(solution)/shard_map/ppermute | solution.py:26
  14.2 0.8 %turn.1 = (bf16[1024,128]{1,0:T(8,128)(2,1)S(1)}, bf16[1024,128]{1,0:T(8,128)(2,1)S(1)}, bf16[128,1024]{1,0:T(8,128)(2,1)S(1)}, bf16[128,1024]{1,0:T(8,128)(2,1)...) custom-call(s32[18]{0:T(128)S(1)} %pad_add_fusion.info_ref, bf16[2,64,1024]{2,1,0:T(8,128)(2,1)S(1)} %get-tuple-element.63.refs_0_, ...), custom_call_target="tpu_custom_call" | custom-call | bytes 1769544 | tf_op jit(solution)/shard_map/turn/pallas_call | solution.py:41
  15.0 2.1 %collective-permute-done.2.refs_0_ = bf16[2,64,256]{2,1,0:T(8,128)(2,1)S(1)} collective-permute-done((bf16[2,64,256]{2,1,0:T(8,128)(2,1)S(1)}, bf16[2,64,256]{2,1,0:T(8,128)(2,1)S(1)}, u32[]{:S(2)}, u32[]{:S(2)}) %collective-permute-start.2) | collective-permute-done | bytes 65568 | tf_op jit(solution)/shard_map/ppermute | solution.py:26
  17.1 0.1 collective-permute-start.6
  17.1 0.5 collective-permute-start.5
  17.6 1.5 %collective-permute-start.8 = (bf16[2,2,64,256]{3,2,1,0:T(8,128)(2,1)S(1)}, bf16[2,2,64,256]{3,2,1,0:T(8,128)(2,1)S(1)}, u32[]{:S(2)}, u32[]{:S(2)}) collective-permute-start(bf16[2,2,64,256]{3,2,1,0:T(8,128)(2,1)S(1)} %get-tuple-element.71.refs_0_), channel_id=1, source_target_pairs={{0,16},{8,24},{16,0},{24,8},{1,17},{9,25},{17,1},{25,9},{2,18},{10... | collective-permute-start | bytes 393224 | tf_op jit(solution)/shard_map/ppermute | solution.py:26
  19.2 0.7 %attend_mid.2 = (f32[256,1024]{1,0:T(8,128)S(1)}, f32[1,1024]{1,0:T(1,128)S(1)}, f32[1,1024]{1,0:T(1,128)S(1)}, f32[128,1024]{1,0:T(8,128)S(1)}) custom-call(s32[128,256]{1,0:T(8,128)S(1)} %get-tuple-element.68.gap_ref, s32[64,256]{1,0:T(8,128)S(1)} %get-tuple-element.69.first_ref, bf16[128,1024]{1,0:T(8,128)(2,1)S(1)} %get-tuple-element.70.refs_3_.q_t, ...), custom_call_target="tpu_custom_call" | custom-call | flops 268435456 | bytes 2170880 | tf_op jit(solution)/shard_map/attend_mid/pallas_call | solution.py:41
  19.9 2.0 %attend_near.1 = (f32[1024,1024]{1,0:T(8,128)S(1)}, f32[1,1024]{1,0:T(1,128)S(1)}, f32[1,1024]{1,0:T(1,128)S(1)}, f32[128,1024]{1,0:T(8,128)S(1)}) custom-call(s32[128,256]{1,0:T(8,128)S(1)} %get-tuple-element.68.gap_ref, s32[64,256]{1,0:T(8,128)S(1)} %get-tuple-element.69.first_ref, bf16[128,1024]{1,0:T(8,128)(2,1)S(1)} %get-tuple-element.70.refs_3_.q_t, ...), custom_call_target="tpu_custom_call" | custom-call | flops 1073741824 | bytes 5713920 | tf_op jit(solution)/shard_map/attend_near/pallas_call | solution.py:41
  21.9 1.2 %collective-permute-done.8.refs_0_ = bf16[2,2,64,256]{3,2,1,0:T(8,128)(2,1)S(1)} collective-permute-done((bf16[2,2,64,256]{3,2,1,0:T(8,128)(2,1)S(1)}, bf16[2,2,64,256]{3,2,1,0:T(8,128)(2,1)S(1)}, u32[]{:S(2)}, u32[]{:S(2)}) %collective-permute-start.8) | collective-permute-done | bytes 131104 | tf_op jit(solution)/shard_map/ppermute | solution.py:26
  23.1 0.7 %attend_mid.3 = (f32[256,1024]{1,0:T(8,128)S(1)}, f32[1,1024]{1,0:T(1,128)S(1)}, f32[1,1024]{1,0:T(1,128)S(1)}, f32[128,1024]{1,0:T(8,128)S(1)}) custom-call(s32[128,256]{1,0:T(8,128)S(1)} %get-tuple-element.68.gap_ref, s32[64,256]{1,0:T(8,128)S(1)} %get-tuple-element.69.first_ref, bf16[128,1024]{1,0:T(8,128)(2,1)S(1)} %get-tuple-element.70.refs_3_.q_t, ...), custom_call_target="tpu_custom_call" | custom-call | flops 268435456 | bytes 2174976 | tf_op jit(solution)/shard_map/attend_mid/pallas_call | solution.py:41
  23.9 0.6 %collective-permute-done.9.refs_9_ = bf16[2,2,64,256]{3,2,1,0:T(8,128)(2,1)S(1)} collective-permute-done((bf16[2,2,64,256]{3,2,1,0:T(8,128)(2,1)S(1)}, bf16[2,2,64,256]{3,2,1,0:T(8,128)(2,1)S(1)}, u32[]{:S(2)}, u32[]{:S(2)}) %collective-permute-start.9) | collective-permute-done | bytes 131104 | tf_op jit(solution)/shard_map/ppermute | solution.py:26
  24.5 2.6 %attend_far.1 = (f32[1,1024]{1,0:T(1,128)S(1)}, f32[1,1024]{1,0:T(1,128)S(1)}, f32[1,1024]{1,0:T(1,128)S(1)}, f32[1,1024]{1,0:T(1,128)S(1)}, bf16[128,1024]{1,0:...) custom-call(s32[128,256]{1,0:T(8,128)S(1)} %get-tuple-element.68.gap, ...), custom_call_target="tpu_custom_call" | custom-call | flops 1073741824 | bytes 4169728 | tf_op jit(solution)/shard_map/attend_far/pallas_call | solution.py:41
  27.1 0.2 collective-permute-start.12
  27.3 0.4 collective-permute-start.11
  27.7 0.6 %attend_back.4 = (f32[128,1024]{1,0:T(8,128)S(1)}, bf16[2,2,64,256]{3,2,1,0:T(8,128)(2,1)S(1)}) custom-call(bf16[1024,128]{1,0:T(8,128)(2,1)S(1)} %get-tuple-element.65.q_all, bf16[1024,128]{1,0:T(8,128)(2,1)S(1)} %get-tuple-element.66.do_all, bf16[128,1024]{1,0:T(8,128)(2,1)S(1)} %get-tuple-element.67.do_t, f32[256,1024]{1,0:T(8,128)S(1)} %get-tuple-element.88.e_ref, ...), custom_call_target="tpu_custom_call" | custom-call | flops 402653184 | bytes 3153920 | tf_op jit(solution)/shard_map/attend_back/pallas_call | solution.py:41
  28.3 0.7 %attend_back.5 = (f32[128,1024]{1,0:T(8,128)S(1)}, bf16[2,2,64,256]{3,2,1,0:T(8,128)(2,1)S(1)}) custom-call(bf16[1024,128]{1,0:T(8,128)(2,1)S(1)} %get-tuple-element.65.q_all, bf16[1024,128]{1,0:T(8,128)(2,1)S(1)} %get-tuple-element.66.do_all, bf16[128,1024]{1,0:T(8,128)(2,1)S(1)} %get-tuple-element.67.do_t, f32[256,1024]{1,0:T(8,128)S(1)} %get-tuple-element.86.e_ref, ...), custom_call_target="tpu_custom_call" | custom-call | flops 402653184 | bytes 3153920 | tf_op jit(solution)/shard_map/attend_back/pallas_call | solution.py:41
  29.1 0.2 collective-permute-start.13
  29.3 1.5 %collective-permute-start.18 = (bf16[2,2,64,256]{3,2,1,0:T(8,128)(2,1)S(1)}, bf16[2,2,64,256]{3,2,1,0:T(8,128)(2,1)S(1)}, u32[]{:S(2)}, u32[]{:S(2)}) collective-permute-start(bf16[2,2,64,256]{3,2,1,0:T(8,128)(2,1)S(1)} %sum_cores.3), channel_id=1, source_target_pairs={{0,16},{8,24},{16,0},{24,8},{1,17},{9,25},{17,1},{25,9},{2,18},{10... | collective-permute-start | bytes 393224 | tf_op jit(solution)/shard_map/ppermute | solution.py:26
  30.8 1.2 %attend_back.6 = (bf16[64,1024]{1,0:T(8,128)(2,1)S(1)}, bf16[64,1024]{1,0:T(8,128)(2,1)S(1)}, f32[128,1024]{1,0:T(8,128)S(1)}, bf16[2,2,64,256]{3,2,1,0:T(8,128)(2,1)S(1)}, bf16[2,2,64,256]{3,2,1,0:T(8,128)(2,1)S(1)}) custom-call(bf16[1024,128]{1,0:T(8,128)(2,1)S(1)} %get-tuple-element.65.q_all, bf16[1024,128]{1,0:T(8,128)(2,1)S(1)} %get-tuple-element.66.do_all, ...), custom_call_target="tpu_custom_call" | custom-call | flops 805306368 | bytes 7102464 | tf_op jit(solution)/shard_map/attend_back/pallas_call | solution.py:41
  32.0 0.1 collective-permute-start.19
  32.1 1.1 %collective-permute-start.15 = (bf16[2,2,64,256]{3,2,1,0:T(8,128)(2,1)S(1)}, bf16[2,2,64,256]{3,2,1,0:T(8,128)(2,1)S(1)}, u32[]{:S(2)}, u32[]{:S(2)}) collective-permute-start(bf16[2,2,64,256]{3,2,1,0:T(8,128)(2,1)S(1)} %sum_cores.2), channel_id=1, source_target_pairs={{0,16},{8,24},{16,0},{24,8},{1,17},{9,25},{17,1},{25,9},{2,18},{10... | collective-permute-start | bytes 393224 | tf_op jit(solution)/shard_map/ppermute | solution.py:26
  33.3 1.5 %collective-permute-start.14 = (bf16[64,1024]{1,0:T(8,128)(2,1)S(1)}, bf16[64,1024]{1,0:T(8,128)(2,1)S(1)}, u32[]{:S(2)}, u32[]{:S(2)}) collective-permute-start(bf16[64,1024]{1,0:T(8,128)(2,1)S(1)} %get-tuple-element.101), channel_id=1, source_target_pairs={{0,8},{8,0},{16,24},{24,16},{1,9},{9,1},{17,25},{25,17},{2,10},{10... | collective-permute-start | bytes 393224 | tf_op jit(solution)/shard_map/ppermute | solution.py:26
  34.8 1.2 %attend_back.7 = (bf16[64,1024]{1,0:T(8,128)(2,1)S(1)}, bf16[64,1024]{1,0:T(8,128)(2,1)S(1)}, bf16[2,2,64,256]{3,2,1,0:T(8,128)(2,1)S(1)}, bf16[2,2,64,256]{3,2,1,0:T(8,128)(2,1)S(1)}) custom-call(bf16[1024,128]{1,0:T(8,128)(2,1)S(1)} %get-tuple-element.65.q_all, bf16[1024,128]{1,0:T(8,128)(2,1)S(1)} %get-tuple-element.66.do_all, ...), custom_call_target="tpu_custom_call" | custom-call | flops 805306368 | bytes 6316032 | tf_op jit(solution)/shard_map/attend_back/pallas_call | solution.py:41
  36.0 0.1 sum_heads.3
  36.1 0.9 %collective-permute-start.20 = (bf16[2,64,256]{2,1,0:T(8,128)(2,1)S(1)}, bf16[2,64,256]{2,1,0:T(8,128)(2,1)S(1)}, u32[]{:S(2)}, u32[]{:S(2)}) collective-permute-start(bf16[2,64,256]{2,1,0:T(8,128)(2,1)S(1)} %get-tuple-element.114), channel_id=1, source_target_pairs={{0,4},{1,5},{2,6},{3,7},{4,0},{5,1},{6,2},{7,3},{8,12},{9,13},{10,... | collective-permute-start | bytes 196616 | tf_op jit(solution)/shard_map/ppermute | solution.py:26
  37.0 1.7 %collective-permute-start.21 = (bf16[2,64,256]{2,1,0:T(8,128)(2,1)S(1)}, bf16[2,64,256]{2,1,0:T(8,128)(2,1)S(1)}, u32[]{:S(2)}, u32[]{:S(2)}) collective-permute-start(bf16[2,64,256]{2,1,0:T(8,128)(2,1)S(1)} %get-tuple-element.115), channel_id=1, source_target_pairs={{0,6},{1,7},{2,4},{3,5},{4,2},{5,3},{6,0},{7,1},{8,14},{9,15},{10,... | collective-permute-start | bytes 196616 | tf_op jit(solution)/shard_map/ppermute | solution.py:26
  38.7 0.0 collective-permute-done.14.refs_3_.refs_1_
  38.7 0.1 sum_heads.2
  38.8 1.0 %collective-permute-start.22 = (bf16[2,64,256]{2,1,0:T(8,128)(2,1)S(1)}, bf16[2,64,256]{2,1,0:T(8,128)(2,1)S(1)}, u32[]{:S(2)}, u32[]{:S(2)}) collective-permute-start(bf16[2,64,256]{2,1,0:T(8,128)(2,1)S(1)} %get-tuple-element.116), channel_id=1, source_target_pairs={{0,2},{1,3},{2,0},{3,1},{4,6},{5,7},{6,4},{7,5},{8,10},{9,11},{10,... | collective-permute-start | bytes 196616 | tf_op jit(solution)/shard_map/ppermute | solution.py:26
  39.8 0.6 %collective-permute-start.17 = (bf16[64,1024]{1,0:T(8,128)(2,1)S(1)}, bf16[64,1024]{1,0:T(8,128)(2,1)S(1)}, u32[]{:S(2)}, u32[]{:S(2)}) collective-permute-start(bf16[64,1024]{1,0:T(8,128)(2,1)S(1)} %get-tuple-element.109), channel_id=1, source_target_pairs={{0,8},{8,0},{16,24},{24,16},{1,9},{9,1},{17,25},{25,17},{2,10},{10... | collective-permute-start | bytes 393224 | tf_op jit(solution)/shard_map/ppermute | solution.py:26
  40.4 3.8 %collective-permute-done.20.refs_0_ = bf16[2,64,256]{2,1,0:T(8,128)(2,1)S(1)} collective-permute-done((bf16[2,64,256]{2,1,0:T(8,128)(2,1)S(1)}, bf16[2,64,256]{2,1,0:T(8,128)(2,1)S(1)}, u32[]{:S(2)}, u32[]{:S(2)}) %collective-permute-start.20) | collective-permute-done | bytes 65568 | tf_op jit(solution)/shard_map/ppermute | solution.py:26
  44.3 1.3 %collective-permute-done.22.refs_2_ = bf16[2,64,256]{2,1,0:T(8,128)(2,1)S(1)} collective-permute-done((bf16[2,64,256]{2,1,0:T(8,128)(2,1)S(1)}, bf16[2,64,256]{2,1,0:T(8,128)(2,1)S(1)}, u32[]{:S(2)}, u32[]{:S(2)}) %collective-permute-start.22) | collective-permute-done | bytes 65568 | tf_op jit(solution)/shard_map/ppermute | solution.py:26
  45.6 0.6 %collective-permute-start.23 = (bf16[64,256]{1,0:T(8,128)(2,1)S(1)}, bf16[64,256]{1,0:T(8,128)(2,1)S(1)}, u32[]{:S(2)}, u32[]{:S(2)}) collective-permute-start(bf16[64,256]{1,0:T(8,128)(2,1)S(1)} %get-tuple-element.118), channel_id=1, source_target_pairs={{0,8},{8,0},{16,24},{24,16},{1,9},{9,1},{17,25},{25,17},{2,10},{10... | collective-permute-start | bytes 98312 | tf_op jit(solution)/shard_map/ppermute | solution.py:26
  46.2 0.8 %finish_q.1 = (bf16[64,2048]{1,0:T(8,128)(2,1)}, bf16[64,2048]{1,0:T(8,128)(2,1)}, f32[8,128]{1,0:T(8,128)S(1)}) custom-call(s32[1]{0:T(128)} %bitcast.group_ref, bf16[64,1024]{1,0:T(8,128)(2,1)S(1)} %get-tuple-element.100.refs_0_, bf16[64,1024]{1,0:T(8,128)(2,1)S(1)} %collective-permute-done.14.refs_3_.refs_1_, ...), custom_call_target="tpu_custom_call" | custom-call | bytes 1052676 | tf_op jit(solution)/shard_map/finish_q/pallas_call | solution.py:41
  47.0 2.6 %collective-permute-done.23.refs_1_ = bf16[64,256]{1,0:T(8,128)(2,1)S(1)} collective-permute-done((bf16[64,256]{1,0:T(8,128)(2,1)S(1)}, bf16[64,256]{1,0:T(8,128)(2,1)S(1)}, u32[]{:S(2)}, u32[]{:S(2)}) %collective-permute-start.23) | collective-permute-done | bytes 32800 | tf_op jit(solution)/shard_map/ppermute | solution.py:26
  49.6 0.6 %finish_kv.1 = (bf16[64,256]{1,0:T(8,128)(2,1)}, bf16[64,256]{1,0:T(8,128)(2,1)}) custom-call(s32[1]{0:T(128)} %bitcast.group_ref, bf16[64,256]{1,0:T(8,128)(2,1)S(1)} %get-tuple-element.117.refs_0_, bf16[64,256]{1,0:T(8,128)(2,1)S(1)} %collective-permute-done.23.refs_1_, f32[8,128]{1,0:T(8,128)S(1)} %get-tuple-element.119.refs_2_), custom_call_target="tpu_custom_call" | custom-call | bytes 135172 | tf_op jit(solution)/shard_map/finish_kv/pallas_call | solution.py:41
  (30 shorter events, 0.3 us)
Async XLA Ops:
  1.4 5.0 %collective-permute-start.1 = (bf16[64,256]{1,0:T(8,128)(2,1)S(1)}, bf16[64,256]{1,0:T(8,128)(2,1)S(1)}, u32[]{:S(2)}, u32[]{:S(2)}) collective-permute-start(bf16[64,256]{1,0:T(8,128)(2,1)S(1)} %pad_maximum_fusion.1), channel_id=1, source_target_pairs={{0,8},{8,0},{16,24},{24,16},{1,9},{9,1},{17,25},{25,17},{2,10},{10... | collective-permute-start | bytes 98312 | tf_op jit(solution)/shard_map/ppermute | solution.py:26
  4.4 0.9 %copy-start = (bf16[2,32,2048]{2,1,0:T(8,128)(2,1)S(1)}, bf16[2,32,2048]{2,1,0:T(8,128)(2,1)}, u32[]{:S(2)}) copy-start(bf16[2,32,2048]{2,1,0:T(8,128)(2,1)} %param.5) | copy-start | bytes 786436
  5.4 0.9 %copy-start.1 = (bf16[2,32,2048]{2,1,0:T(8,128)(2,1)S(1)}, bf16[2,32,2048]{2,1,0:T(8,128)(2,1)}, u32[]{:S(2)}) copy-start(bf16[2,32,2048]{2,1,0:T(8,128)(2,1)} %param.8) | copy-start | bytes 786436
  6.4 7.8 %collective-permute-start = (bf16[2,64,1024]{2,1,0:T(8,128)(2,1)S(1)}, bf16[2,64,1024]{2,1,0:T(8,128)(2,1)S(1)}, u32[]{:S(2)}, u32[]{:S(2)}) collective-permute-start(bf16[2,64,1024]{2,1,0:T(8,128)(2,1)S(1)} %get-tuple-element.64), channel_id=1, source_target_pairs={{0,8},{8,0},{16,24},{24,16},{1,9},{9,1},{17,25},{25,17},{2,10},{10... | collective-permute-start | bytes 786440 | tf_op jit(solution)/shard_map/ppermute | solution.py:26
  6.5 4.7 %collective-permute-start.4 = (bf16[2,64,256]{2,1,0:T(8,128)(2,1)S(1)}, bf16[2,64,256]{2,1,0:T(8,128)(2,1)S(1)}, u32[]{:S(2)}, u32[]{:S(2)}) collective-permute-start(bf16[2,64,256]{2,1,0:T(8,128)(2,1)S(1)} %pad_maximum_fusion.refs_0_), channel_id=1, source_target_pairs={{0,2},{1,3},{2,0},{3,1},{4,6},{5,7},{6,4},{7,5},{8,10},{9,11},{10,... | collective-permute-start | bytes 196616 | tf_op jit(solution)/shard_map/ppermute | solution.py:26
  8.7 6.3 %collective-permute-start.3 = (bf16[2,64,256]{2,1,0:T(8,128)(2,1)S(1)}, bf16[2,64,256]{2,1,0:T(8,128)(2,1)S(1)}, u32[]{:S(2)}, u32[]{:S(2)}) collective-permute-start(bf16[2,64,256]{2,1,0:T(8,128)(2,1)S(1)} %pad_maximum_fusion.refs_0_), channel_id=1, source_target_pairs={{0,6},{1,7},{2,4},{3,5},{4,2},{5,3},{6,0},{7,1},{8,14},{9,15},{10,... | collective-permute-start | bytes 196616 | tf_op jit(solution)/shard_map/ppermute | solution.py:26
  11.1 5.9 %collective-permute-start.2 = (bf16[2,64,256]{2,1,0:T(8,128)(2,1)S(1)}, bf16[2,64,256]{2,1,0:T(8,128)(2,1)S(1)}, u32[]{:S(2)}, u32[]{:S(2)}) collective-permute-start(bf16[2,64,256]{2,1,0:T(8,128)(2,1)S(1)} %pad_maximum_fusion.refs_0_), channel_id=1, source_target_pairs={{0,4},{1,5},{2,6},{3,7},{4,0},{5,1},{6,2},{7,3},{8,12},{9,13},{10,... | collective-permute-start | bytes 196616 | tf_op jit(solution)/shard_map/ppermute | solution.py:26
  11.3 7.9 %collective-permute-start.7 = (bf16[2,2,64,256]{3,2,1,0:T(8,128)(2,1)S(1)}, bf16[2,2,64,256]{3,2,1,0:T(8,128)(2,1)S(1)}, u32[]{:S(2)}, u32[]{:S(2)}) collective-permute-start(bf16[2,2,64,256]{3,2,1,0:T(8,128)(2,1)S(1)} %stack.22.refs_2_.refs_1_), channel_id=1, source_target_pairs={{0,16},{8,24},{16,0},{24,8},{1,17},{9,25},{17,1},{25,9},{2,18},{10... | collective-permute-start | bytes 393224 | tf_op jit(solution)/shard_map/ppermute | solution.py:26
  17.1 2.8 %collective-permute-start.6 = (bf16[2,2,64,256]{3,2,1,0:T(8,128)(2,1)S(1)}, bf16[2,2,64,256]{3,2,1,0:T(8,128)(2,1)S(1)}, u32[]{:S(2)}, u32[]{:S(2)}) collective-permute-start(bf16[2,2,64,256]{3,2,1,0:T(8,128)(2,1)S(1)} %get-tuple-element.72), channel_id=1, source_target_pairs={{0,1},{1,0},{2,3},{3,2},{4,5},{5,4},{6,7},{7,6},{8,9},{9,8},{10,11... | collective-permute-start | bytes 393224 | tf_op jit(solution)/shard_map/ppermute | solution.py:26
  17.1 2.8 %collective-permute-start.5 = (bf16[2,2,64,256]{3,2,1,0:T(8,128)(2,1)S(1)}, bf16[2,2,64,256]{3,2,1,0:T(8,128)(2,1)S(1)}, u32[]{:S(2)}, u32[]{:S(2)}) collective-permute-start(bf16[2,2,64,256]{3,2,1,0:T(8,128)(2,1)S(1)} %get-tuple-element.71.refs_0_), channel_id=1, source_target_pairs={{0,1},{1,0},{2,3},{3,2},{4,5},{5,4},{6,7},{7,6},{8,9},{9,8},{10,11... | collective-permute-start | bytes 393224 | tf_op jit(solution)/shard_map/ppermute | solution.py:26
  17.6 5.5 %collective-permute-start.8 = (bf16[2,2,64,256]{3,2,1,0:T(8,128)(2,1)S(1)}, bf16[2,2,64,256]{3,2,1,0:T(8,128)(2,1)S(1)}, u32[]{:S(2)}, u32[]{:S(2)}) collective-permute-start(bf16[2,2,64,256]{3,2,1,0:T(8,128)(2,1)S(1)} %get-tuple-element.71.refs_0_), channel_id=1, source_target_pairs={{0,16},{8,24},{16,0},{24,8},{1,17},{9,25},{17,1},{25,9},{2,18},{10... | collective-permute-start | bytes 393224 | tf_op jit(solution)/shard_map/ppermute | solution.py:26
  19.2 4.7 %collective-permute-start.10 = (bf16[2,2,64,256]{3,2,1,0:T(8,128)(2,1)S(1)}, bf16[2,2,64,256]{3,2,1,0:T(8,128)(2,1)S(1)}, u32[]{:S(2)}, u32[]{:S(2)}) collective-permute-start(bf16[2,2,64,256]{3,2,1,0:T(8,128)(2,1)S(1)} %collective-permute-done.7.refs_0_), channel_id=1, source_target_pairs={{0,1},{1,0},{2,3},{3,2},{4,5},{5,4},{6,7},{7,6},{8,9},{9,8},{10,11... | collective-permute-start | bytes 393224 | tf_op jit(solution)/shard_map/ppermute | solution.py:26
  23.1 1.3 %collective-permute-start.9 = (bf16[2,2,64,256]{3,2,1,0:T(8,128)(2,1)S(1)}, bf16[2,2,64,256]{3,2,1,0:T(8,128)(2,1)S(1)}, u32[]{:S(2)}, u32[]{:S(2)}) collective-permute-start(bf16[2,2,64,256]{3,2,1,0:T(8,128)(2,1)S(1)} %collective-permute-done.8.refs_0_), channel_id=1, source_target_pairs={{0,1},{1,0},{2,3},{3,2},{4,5},{5,4},{6,7},{7,6},{8,9},{9,8},{10,11... | collective-permute-start | bytes 393224 | tf_op jit(solution)/shard_map/ppermute | solution.py:26
  27.1 1.9 %collective-permute-start.12 = (bf16[2,2,64,256]{3,2,1,0:T(8,128)(2,1)S(1)}, bf16[2,2,64,256]{3,2,1,0:T(8,128)(2,1)S(1)}, u32[]{:S(2)}, u32[]{:S(2)}) collective-permute-start(bf16[2,2,64,256]{3,2,1,0:T(8,128)(2,1)S(1)} %get-tuple-element.97), channel_id=1, source_target_pairs={{0,1},{1,0},{2,3},{3,2},{4,5},{5,4},{6,7},{7,6},{8,9},{9,8},{10,11... | collective-permute-start | bytes 393224 | tf_op jit(solution)/shard_map/ppermute | solution.py:26
  27.3 1.7 %collective-permute-start.11 = (bf16[2,2,64,256]{3,2,1,0:T(8,128)(2,1)S(1)}, bf16[2,2,64,256]{3,2,1,0:T(8,128)(2,1)S(1)}, u32[]{:S(2)}, u32[]{:S(2)}) collective-permute-start(bf16[2,2,64,256]{3,2,1,0:T(8,128)(2,1)S(1)} %get-tuple-element.95), channel_id=1, source_target_pairs={{0,1},{1,0},{2,3},{3,2},{4,5},{5,4},{6,7},{7,6},{8,9},{9,8},{10,11... | collective-permute-start | bytes 393224 | tf_op jit(solution)/shard_map/ppermute | solution.py:26
  29.1 1.7 %collective-permute-start.13 = (bf16[64,128]{1,0:T(8,128)(2,1)S(1)}, bf16[64,128]{1,0:T(8,128)(2,1)S(1)}, u32[]{:S(2)}, u32[]{:S(2)}) collective-permute-start(bf16[64,128]{1,0:T(8,128)(2,1)S(1)} %slice_bitcast_fusion), channel_id=1, source_target_pairs={{0,1},{1,0},{2,3},{3,2},{4,5},{5,4},{6,7},{7,6},{8,9},{9,8},{10,11... | collective-permute-start | bytes 49160 | tf_op jit(solution)/shard_map/ppermute | solution.py:26
  29.3 6.7 %collective-permute-start.18 = (bf16[2,2,64,256]{3,2,1,0:T(8,128)(2,1)S(1)}, bf16[2,2,64,256]{3,2,1,0:T(8,128)(2,1)S(1)}, u32[]{:S(2)}, u32[]{:S(2)}) collective-permute-start(bf16[2,2,64,256]{3,2,1,0:T(8,128)(2,1)S(1)} %sum_cores.3), channel_id=1, source_target_pairs={{0,16},{8,24},{16,0},{24,8},{1,17},{9,25},{17,1},{25,9},{2,18},{10... | collective-permute-start | bytes 393224 | tf_op jit(solution)/shard_map/ppermute | solution.py:26
  32.0 4.0 %collective-permute-start.19 = (bf16[2,2,64,256]{3,2,1,0:T(8,128)(2,1)S(1)}, bf16[2,2,64,256]{3,2,1,0:T(8,128)(2,1)S(1)}, u32[]{:S(2)}, u32[]{:S(2)}) collective-permute-start(bf16[2,2,64,256]{3,2,1,0:T(8,128)(2,1)S(1)} %get-tuple-element.112), channel_id=1, source_target_pairs={{0,1},{1,0},{2,3},{3,2},{4,5},{5,4},{6,7},{7,6},{8,9},{9,8},{10,11... | collective-permute-start | bytes 393224 | tf_op jit(solution)/shard_map/ppermute | solution.py:26
  32.1 6.5 %collective-permute-start.15 = (bf16[2,2,64,256]{3,2,1,0:T(8,128)(2,1)S(1)}, bf16[2,2,64,256]{3,2,1,0:T(8,128)(2,1)S(1)}, u32[]{:S(2)}, u32[]{:S(2)}) collective-permute-start(bf16[2,2,64,256]{3,2,1,0:T(8,128)(2,1)S(1)} %sum_cores.2), channel_id=1, source_target_pairs={{0,16},{8,24},{16,0},{24,8},{1,17},{9,25},{17,1},{25,9},{2,18},{10... | collective-permute-start | bytes 393224 | tf_op jit(solution)/shard_map/ppermute | solution.py:26
  33.3 5.5 %collective-permute-start.14 = (bf16[64,1024]{1,0:T(8,128)(2,1)S(1)}, bf16[64,1024]{1,0:T(8,128)(2,1)S(1)}, u32[]{:S(2)}, u32[]{:S(2)}) collective-permute-start(bf16[64,1024]{1,0:T(8,128)(2,1)S(1)} %get-tuple-element.101), channel_id=1, source_target_pairs={{0,8},{8,0},{16,24},{24,16},{1,9},{9,1},{17,25},{25,17},{2,10},{10... | collective-permute-start | bytes 393224 | tf_op jit(solution)/shard_map/ppermute | solution.py:26
  34.8 4.0 %collective-permute-start.16 = (bf16[2,2,64,256]{3,2,1,0:T(8,128)(2,1)S(1)}, bf16[2,2,64,256]{3,2,1,0:T(8,128)(2,1)S(1)}, u32[]{:S(2)}, u32[]{:S(2)}) collective-permute-start(bf16[2,2,64,256]{3,2,1,0:T(8,128)(2,1)S(1)} %get-tuple-element.105), channel_id=1, source_target_pairs={{0,1},{1,0},{2,3},{3,2},{4,5},{5,4},{6,7},{7,6},{8,9},{9,8},{10,11... | collective-permute-start | bytes 393224 | tf_op jit(solution)/shard_map/ppermute | solution.py:26
  36.1 8.2 %collective-permute-start.20 = (bf16[2,64,256]{2,1,0:T(8,128)(2,1)S(1)}, bf16[2,64,256]{2,1,0:T(8,128)(2,1)S(1)}, u32[]{:S(2)}, u32[]{:S(2)}) collective-permute-start(bf16[2,64,256]{2,1,0:T(8,128)(2,1)S(1)} %get-tuple-element.114), channel_id=1, source_target_pairs={{0,4},{1,5},{2,6},{3,7},{4,0},{5,1},{6,2},{7,3},{8,12},{9,13},{10,... | collective-permute-start | bytes 196616 | tf_op jit(solution)/shard_map/ppermute | solution.py:26
  37.0 7.3 %collective-permute-start.21 = (bf16[2,64,256]{2,1,0:T(8,128)(2,1)S(1)}, bf16[2,64,256]{2,1,0:T(8,128)(2,1)S(1)}, u32[]{:S(2)}, u32[]{:S(2)}) collective-permute-start(bf16[2,64,256]{2,1,0:T(8,128)(2,1)S(1)} %get-tuple-element.115), channel_id=1, source_target_pairs={{0,6},{1,7},{2,4},{3,5},{4,2},{5,3},{6,0},{7,1},{8,14},{9,15},{10,... | collective-permute-start | bytes 196616 | tf_op jit(solution)/shard_map/ppermute | solution.py:26
  38.8 6.8 %collective-permute-start.22 = (bf16[2,64,256]{2,1,0:T(8,128)(2,1)S(1)}, bf16[2,64,256]{2,1,0:T(8,128)(2,1)S(1)}, u32[]{:S(2)}, u32[]{:S(2)}) collective-permute-start(bf16[2,64,256]{2,1,0:T(8,128)(2,1)S(1)} %get-tuple-element.116), channel_id=1, source_target_pairs={{0,2},{1,3},{2,0},{3,1},{4,6},{5,7},{6,4},{7,5},{8,10},{9,11},{10,... | collective-permute-start | bytes 196616 | tf_op jit(solution)/shard_map/ppermute | solution.py:26
  39.8 6.4 %collective-permute-start.17 = (bf16[64,1024]{1,0:T(8,128)(2,1)S(1)}, bf16[64,1024]{1,0:T(8,128)(2,1)S(1)}, u32[]{:S(2)}, u32[]{:S(2)}) collective-permute-start(bf16[64,1024]{1,0:T(8,128)(2,1)S(1)} %get-tuple-element.109), channel_id=1, source_target_pairs={{0,8},{8,0},{16,24},{24,16},{1,9},{9,1},{17,25},{25,17},{2,10},{10... | collective-permute-start | bytes 393224 | tf_op jit(solution)/shard_map/ppermute | solution.py:26
  45.6 4.0 %collective-permute-start.23 = (bf16[64,256]{1,0:T(8,128)(2,1)S(1)}, bf16[64,256]{1,0:T(8,128)(2,1)S(1)}, u32[]{:S(2)}, u32[]{:S(2)}) collective-permute-start(bf16[64,256]{1,0:T(8,128)(2,1)S(1)} %get-tuple-element.118), channel_id=1, source_target_pairs={{0,8},{8,0},{16,24},{24,16},{1,9},{9,1},{17,25},{25,17},{2,10},{10... | collective-permute-start | bytes 98312 | tf_op jit(solution)/shard_map/ppermute | solution.py:26

commit v14 on v12

--- a/solution.py
+++ b/solution.py
@@ -58,18 +58,6 @@
 
 def dot_rows(left, right):
     return lax.dot_general(left, right, (((1,), (1,)), ((), ())), preferred_element_type=F32)
-
-
-def pack_q_kernel(kv, group_ref, query_ref, grad_ref, *out_refs):
-    width = out_refs[0].shape[2]
-    for g in range(kv):
-
-        @pl.when(group_ref[0] == g)
-        def _():
-            for s in range(kv):
-                cols = pl.ds((g ^ s) * width, width)
-                out_refs[s][0] = query_ref[:, cols]
-                out_refs[s][1] = grad_ref[:, cols]
 
 
 def stack_kernel(count, *refs):
@@ -388,26 +376,22 @@
 
     dkv = bf(z_part, kv, rows, 2 * HD)
 
+    def pick(block, g, size):
+        out = block[:, :size]
+        for i in range(1, kv):
+            out = jnp.where(g == i, block[:, i * size : (i + 1) * size], out)
+        return out
+
     def of_head(g):
-        picked = []
-        for block in (key_vectors, value_vectors):
-            out = block[:, :HD]
-            for i in range(1, kv):
-                out = jnp.where(g == i, block[:, i * HD : (i + 1) * HD], out)
-            picked.append(out)
-        return jnp.concatenate(picked, axis=1)
+        return jnp.concatenate([pick(key_vectors, g, HD), pick(value_vectors, g, HD)], axis=1)
+
+    def queries_of(g):
+        return jnp.stack([pick(queries, g, width), pick(out_grad, g, width)])
 
     piece = jnp.stack(with_swaps([of_head((head % kv) ^ s) for s in range(kv)]))
-    q_parts = call(
-        functools.partial(pack_q_kernel, kv),
-        "pack_q",
-        (own_group, queries, out_grad),
-        [bf(2, rows, width)] * kv,
-        [SMEM, VMEM, VMEM],
-    )
+    q_parts = with_swaps([queries_of((head % kv) ^ s) for s in range(kv)])
     pieces = [swap(piece, "ctx", m * cores) for m in reversed(range(1, z_devices))]
     pieces = [piece] + pieces[::-1]
-    q_parts = with_swaps(q_parts)
     query_rows = plan.query_rows
     chunks = [(a, core, p) for a in range(spans) for core in range(cores) for p in range(parts)]
     q_all, do_all, q_t, do_t, gap, firsts = call(

time: 49 us -> 49.1 us (level)
  local copies, waits for them, and re-layouts: 1.9 us -> 0.01 us
  other arithmetic: 1.53 us -> 2.71 us
  waiting for transfers between devices: 10.3 us -> 11.3 us
    unnamed x4 -> x0, local copies, waits for them, and re-layouts: 1.9 us -> none
    another operation x0 -> x3, other arithmetic: none -> 1.18 us  [queries_of(): return jnp.stack([pick(queries, g, width), pick(out_grad, g, width)])]
    ppermute x23, waiting for transfers between devices: 10.3 us -> 11.3 us  [swap(): return lax.ppermute(block, axis, [(i, i ^ mask) for i in range(size)])]
    pallas_call x20 -> x19, Pallas kernels: 12.3 us -> 12.3 us  [call(): pl.pallas_call(kernel, out_shape=list(outs), in_specs=specs or [VMEM] * l...]
  transfers between devices with their start and end apart: 23 -> 23, of which waited for: 9 -> 11; matrix products, arithmetic and copies ran while one was open for 2% -> 4% of each run, Pallas kernels for 18% -> 18%
where the time goes in v14:
time: 49.1 us; the launch traced here: 48.9 us
  starting transfers between devices  21.7 us (44%)
  Pallas kernels  12.3 us (25%)
  waiting for transfers between devices  11.3 us (23%)
  other arithmetic  2.71 us (6%)
  between operations  0.85 us (2%)
    ppermute x23, starting transfers between devices, swap(): return lax.ppermute(block, axis, [(i, i ^ mask) for i in range(size)])  21.7 us
    pallas_call x19, Pallas kernels, call(): pl.pallas_call(kernel, out_shape=list(outs), in_specs=specs or [VMEM] * l...  12.3 us
    ppermute x23, waiting for transfers between devices, swap(): return lax.ppermute(block, axis, [(i, i ^ mask) for i in range(size)])  11.3 us
    another operation x3, other arithmetic, queries_of(): return jnp.stack([pick(queries, g, width), pick(out_grad, g, width)])  1.18 us
  transfers between devices with their start and end apart: 23, of which 11 were waited for; matrix products, arithmetic and copies ran while one was open for 4% of the time, Pallas kernels for 18%

profile of v14, /device:TPU:0, one launch (start us, length us, event | category | flops | bytes accessed | tf_op | source)
XLA Modules:
  0.0 48.9 jit_solution(13947810853789969506)
XLA Ops:
  0.6 0.8 %broadcast_select_fusion.2 = (bf16[64,128]{1,0:T(8,128)(2,1)S(1)}, bf16[64,128]{1,0:T(8,128)(2,1)S(1)}, bf16[64,128]{1,0:T(8,128)(2,1)S(1)}, bf16[64,128]{1,0:T(8,128)(2,1)S(1)}) fusion(pred[]{:T(512)S(6)} %eq.18, bf16[64,256]{1,0:T(8,128)(2,1)} %bitcast.26, pred[]{:T(512)S(6)} %eq.19, bf16[64,256]{1,0:T(8,128)(2,1)} %bitcast.27), kind=kLoop, calls=%fused_computation.12 | loop fusion | flops 32768 | bytes 131074 | tf_op jit(solution)/shard_map/jit(_where)/select_n | solution.py:382
  1.4 3.0 %collective-permute-start.1 = (bf16[64,256]{1,0:T(8,128)(2,1)S(1)}, bf16[64,256]{1,0:T(8,128)(2,1)S(1)}, u32[]{:S(2)}, u32[]{:S(2)}) collective-permute-start(bf16[64,256]{1,0:T(8,128)(2,1)S(1)} %pad_maximum_fusion.3), channel_id=1, source_target_pairs={{0,8},{8,0},{16,24},{24,16},{1,9},{9,1},{17,25},{25,17},{2,10},{10... | collective-permute-start | bytes 98312 | tf_op jit(solution)/shard_map/ppermute | solution.py:26
  4.4 1.1 %select_bitcast_fusion = (bf16[1,64,1024]{2,1,0:T(8,128)(2,1)S(1)}, bf16[1,64,1024]{2,1,0:T(8,128)(2,1)S(1)}, bf16[1,64,1024]{2,1,0:T(8,128)(2,1)S(1)}, bf16[1,64,1024]{2,1,0:T(8,128)(2,1)S(1)}) fusion(pred[]{:T(512)S(6)} %eq.19, bf16[64,2048]{1,0:T(8,128)(2,1)} %bitcast.24, pred[]{:T(512)S(6)} %eq.18, bf16[64,2048]{1,0:T(8,128)(2,1)} %bitcast.25), kind=kLoop, calls=%fused_computation.2 | loop fusion | flops 262144 | bytes 1048578 | tf_op jit(solution)/shard_map/stack | solution.py:389
  5.6 0.1 collective-permute-start
  5.7 0.6 %collective-permute-done.1 = bf16[64,256]{1,0:T(8,128)(2,1)S(1)} collective-permute-done((bf16[64,256]{1,0:T(8,128)(2,1)S(1)}, bf16[64,256]{1,0:T(8,128)(2,1)S(1)}, u32[]{:S(2)}, u32[]{:S(2)}) %collective-permute-start.1) | collective-permute-done | bytes 32800 | tf_op jit(solution)/shard_map/ppermute | solution.py:26
  6.3 2.2 %collective-permute-start.4 = (bf16[2,64,256]{2,1,0:T(8,128)(2,1)S(1)}, bf16[2,64,256]{2,1,0:T(8,128)(2,1)S(1)}, u32[]{:S(2)}, u32[]{:S(2)}) collective-permute-start(bf16[2,64,256]{2,1,0:T(8,128)(2,1)S(1)} %pad_maximum_fusion.2.refs_0_), channel_id=1, source_target_pairs={{0,2},{1,3},{2,0},{3,1},{4,6},{5,7},{6,4},{7,5},{8,10},{9,11},{10,... | collective-permute-start | bytes 196616 | tf_op jit(solution)/shard_map/ppermute | solution.py:26
  8.5 2.5 %collective-permute-start.3 = (bf16[2,64,256]{2,1,0:T(8,128)(2,1)S(1)}, bf16[2,64,256]{2,1,0:T(8,128)(2,1)S(1)}, u32[]{:S(2)}, u32[]{:S(2)}) collective-permute-start(bf16[2,64,256]{2,1,0:T(8,128)(2,1)S(1)} %pad_maximum_fusion.2.refs_0_), channel_id=1, source_target_pairs={{0,6},{1,7},{2,4},{3,5},{4,2},{5,3},{6,0},{7,1},{8,14},{9,15},{10,... | collective-permute-start | bytes 196616 | tf_op jit(solution)/shard_map/ppermute | solution.py:26
  11.0 0.1 collective-permute-start.2
  11.1 1.7 %collective-permute-start.7 = (bf16[2,2,64,256]{3,2,1,0:T(8,128)(2,1)S(1)}, bf16[2,2,64,256]{3,2,1,0:T(8,128)(2,1)S(1)}, u32[]{:S(2)}, u32[]{:S(2)}) collective-permute-start(bf16[2,2,64,256]{3,2,1,0:T(8,128)(2,1)S(1)} %stack.46.refs_2_.refs_1_), channel_id=1, source_target_pairs={{0,16},{8,24},{16,0},{24,8},{1,17},{9,25},{17,1},{25,9},{2,18},{10... | collective-permute-start | bytes 393224 | tf_op jit(solution)/shard_map/ppermute | solution.py:26
  12.8 1.9 %collective-permute-done.3.refs_1_ = bf16[2,64,256]{2,1,0:T(8,128)(2,1)S(1)} collective-permute-done((bf16[2,64,256]{2,1,0:T(8,128)(2,1)S(1)}, bf16[2,64,256]{2,1,0:T(8,128)(2,1)S(1)}, u32[]{:S(2)}, u32[]{:S(2)}) %collective-permute-start.3) | collective-permute-done | bytes 65568 | tf_op jit(solution)/shard_map/ppermute | solution.py:26
  14.7 2.1 %collective-permute-done.2.refs_0_ = bf16[2,64,256]{2,1,0:T(8,128)(2,1)S(1)} collective-permute-done((bf16[2,64,256]{2,1,0:T(8,128)(2,1)S(1)}, bf16[2,64,256]{2,1,0:T(8,128)(2,1)S(1)}, u32[]{:S(2)}, u32[]{:S(2)}) %collective-permute-start.2) | collective-permute-done | bytes 65568 | tf_op jit(solution)/shard_map/ppermute | solution.py:26
  16.9 1.6 %collective-permute-start.8 = (bf16[2,2,64,256]{3,2,1,0:T(8,128)(2,1)S(1)}, bf16[2,2,64,256]{3,2,1,0:T(8,128)(2,1)S(1)}, u32[]{:S(2)}, u32[]{:S(2)}) collective-permute-start(bf16[2,2,64,256]{3,2,1,0:T(8,128)(2,1)S(1)} %get-tuple-element.65.refs_0_.refs_1_), channel_id=1, source_target_pairs={{0,16},{8,24},{16,0},{24,8},{1,17},{9,25},{17,1},{25,9},{2,18},{10... | collective-permute-start | bytes 393224 | tf_op jit(solution)/shard_map/ppermute | solution.py:26
  18.5 0.5 %collective-permute-start.6 = (bf16[2,2,64,256]{3,2,1,0:T(8,128)(2,1)S(1)}, bf16[2,2,64,256]{3,2,1,0:T(8,128)(2,1)S(1)}, u32[]{:S(2)}, u32[]{:S(2)}) collective-permute-start(bf16[2,2,64,256]{3,2,1,0:T(8,128)(2,1)S(1)} %get-tuple-element.66), channel_id=1, source_target_pairs={{0,1},{1,0},{2,3},{3,2},{4,5},{5,4},{6,7},{7,6},{8,9},{9,8},{10,11... | collective-permute-start | bytes 393224 | tf_op jit(solution)/shard_map/ppermute | solution.py:26
  19.0 0.7 %pad_add_fusion.info_ref = s32[18]{0:T(128)S(1)} fusion(s32[16]{0:T(128)} %param.9, s32[1]{0:T(128)} %bitcast.2, s32[1]{0:T(128)} %bitcast.1), kind=kLoop, calls=%fused_computation.14 | loop fusion | flops 36 | bytes 144 | tf_op jit(solution)/shard_map/concatenate | solution.py:358
  19.7 0.8 %turn.1 = (bf16[1024,128]{1,0:T(8,128)(2,1)S(1)}, bf16[1024,128]{1,0:T(8,128)(2,1)S(1)}, bf16[128,1024]{1,0:T(8,128)(2,1)S(1)}, bf16[128,1024]{1,0:T(8,128)(2,1)...) custom-call(s32[18]{0:T(128)S(1)} %pad_add_fusion.info_ref, bf16[2,64,1024]{2,1,0:T(8,128)(2,1)S(1)} %pad_maximum_fusion.refs_0_, ...), custom_call_target="tpu_custom_call" | custom-call | bytes 1769544 | tf_op jit(solution)/shard_map/turn/pallas_call | solution.py:41
  20.5 0.7 %attend_mid.2 = (f32[256,1024]{1,0:T(8,128)S(1)}, f32[1,1024]{1,0:T(1,128)S(1)}, f32[1,1024]{1,0:T(1,128)S(1)}, f32[128,1024]{1,0:T(8,128)S(1)}) custom-call(s32[128,256]{1,0:T(8,128)S(1)} %get-tuple-element.62.gap_ref, s32[64,256]{1,0:T(8,128)S(1)} %get-tuple-element.63.first_ref, bf16[128,1024]{1,0:T(8,128)(2,1)S(1)} %get-tuple-element.64.q_t, ...), custom_call_target="tpu_custom_call" | custom-call | flops 268435456 | bytes 2170880 | tf_op jit(solution)/shard_map/attend_mid/pallas_call | solution.py:41
  21.2 2.0 %attend_near.1 = (f32[1024,1024]{1,0:T(8,128)S(1)}, f32[1,1024]{1,0:T(1,128)S(1)}, f32[1,1024]{1,0:T(1,128)S(1)}, f32[128,1024]{1,0:T(8,128)S(1)}) custom-call(s32[128,256]{1,0:T(8,128)S(1)} %get-tuple-element.62.gap_ref, s32[64,256]{1,0:T(8,128)S(1)} %get-tuple-element.63.first_ref, bf16[128,1024]{1,0:T(8,128)(2,1)S(1)} %get-tuple-element.64.q_t, ...), custom_call_target="tpu_custom_call" | custom-call | flops 1073741824 | bytes 5713920 | tf_op jit(solution)/shard_map/attend_near/pallas_call | solution.py:41
  23.3 0.6 %collective-permute-start.9 = (bf16[2,2,64,256]{3,2,1,0:T(8,128)(2,1)S(1)}, bf16[2,2,64,256]{3,2,1,0:T(8,128)(2,1)S(1)}, u32[]{:S(2)}, u32[]{:S(2)}) collective-permute-start(bf16[2,2,64,256]{3,2,1,0:T(8,128)(2,1)S(1)} %collective-permute-done.8.refs_0_), channel_id=1, source_target_pairs={{0,1},{1,0},{2,3},{3,2},{4,5},{5,4},{6,7},{7,6},{8,9},{9,8},{10,11... | collective-permute-start | bytes 393224 | tf_op jit(solution)/shard_map/ppermute | solution.py:26
  23.8 0.7 %attend_mid.3 = (f32[256,1024]{1,0:T(8,128)S(1)}, f32[1,1024]{1,0:T(1,128)S(1)}, f32[1,1024]{1,0:T(1,128)S(1)}, f32[128,1024]{1,0:T(8,128)S(1)}) custom-call(s32[128,256]{1,0:T(8,128)S(1)} %get-tuple-element.62.gap_ref, s32[64,256]{1,0:T(8,128)S(1)} %get-tuple-element.63.first_ref, bf16[128,1024]{1,0:T(8,128)(2,1)S(1)} %get-tuple-element.64.q_t, ...), custom_call_target="tpu_custom_call" | custom-call | flops 268435456 | bytes 2174976 | tf_op jit(solution)/shard_map/attend_mid/pallas_call | solution.py:41
  24.6 0.2 collective-permute-done.9.refs_9_
  24.8 2.6 %attend_far.1 = (f32[1,1024]{1,0:T(1,128)S(1)}, f32[1,1024]{1,0:T(1,128)S(1)}, f32[1,1024]{1,0:T(1,128)S(1)}, f32[1,1024]{1,0:T(1,128)S(1)}, bf16[128,1024]{1,0:...) custom-call(s32[128,256]{1,0:T(8,128)S(1)} %get-tuple-element.62.gap, ...), custom_call_target="tpu_custom_call" | custom-call | flops 1073741824 | bytes 4169728 | tf_op jit(solution)/shard_map/attend_far/pallas_call | solution.py:41
  27.5 0.4 collective-permute-start.12
  27.9 0.2 collective-permute-start.11
  28.0 0.6 %attend_back.4 = (f32[128,1024]{1,0:T(8,128)S(1)}, bf16[2,2,64,256]{3,2,1,0:T(8,128)(2,1)S(1)}) custom-call(bf16[1024,128]{1,0:T(8,128)(2,1)S(1)} %get-tuple-element.59.q_all, bf16[1024,128]{1,0:T(8,128)(2,1)S(1)} %get-tuple-element.60.do_all, bf16[128,1024]{1,0:T(8,128)(2,1)S(1)} %get-tuple-element.61.do_t, f32[256,1024]{1,0:T(8,128)S(1)} %get-tuple-element.82.e_ref, ...), custom_call_target="tpu_custom_call" | custom-call | flops 402653184 | bytes 3153920 | tf_op jit(solution)/shard_map/attend_back/pallas_call | solution.py:41
  28.7 0.6 %attend_back.5 = (f32[128,1024]{1,0:T(8,128)S(1)}, bf16[2,2,64,256]{3,2,1,0:T(8,128)(2,1)S(1)}) custom-call(bf16[1024,128]{1,0:T(8,128)(2,1)S(1)} %get-tuple-element.59.q_all, bf16[1024,128]{1,0:T(8,128)(2,1)S(1)} %get-tuple-element.60.do_all, bf16[128,1024]{1,0:T(8,128)(2,1)S(1)} %get-tuple-element.61.do_t, f32[256,1024]{1,0:T(8,128)S(1)} %get-tuple-element.80.e_ref, ...), custom_call_target="tpu_custom_call" | custom-call | flops 402653184 | bytes 3153920 | tf_op jit(solution)/shard_map/attend_back/pallas_call | solution.py:41
  29.5 0.4 collective-permute-start.13
  29.9 0.5 %collective-permute-start.17 = (bf16[2,2,64,256]{3,2,1,0:T(8,128)(2,1)S(1)}, bf16[2,2,64,256]{3,2,1,0:T(8,128)(2,1)S(1)}, u32[]{:S(2)}, u32[]{:S(2)}) collective-permute-start(bf16[2,2,64,256]{3,2,1,0:T(8,128)(2,1)S(1)} %sum_cores.3), channel_id=1, source_target_pairs={{0,16},{8,24},{16,0},{24,8},{1,17},{9,25},{17,1},{25,9},{2,18},{10... | collective-permute-start | bytes 393224 | tf_op jit(solution)/shard_map/ppermute | solution.py:26
  30.4 0.3 collective-permute-done.13.refs_2_.refs_3_
  30.7 1.2 %attend_back.6 = (f32[128,1024]{1,0:T(8,128)S(1)}, bf16[2,2,64,256]{3,2,1,0:T(8,128)(2,1)S(1)}, bf16[2,2,64,256]{3,2,1,0:T(8,128)(2,1)S(1)}) custom-call(bf16[1024,128]{1,0:T(8,128)(2,1)S(1)} %get-tuple-element.59.q_all, bf16[1024,128]{1,0:T(8,128)(2,1)S(1)} %get-tuple-element.60.do_all, bf16[128,1024]{1,0:T(8,128)(2,1)S(1)} %get-tuple-element.61.do_t, ...), custom_call_target="tpu_custom_call" | custom-call | flops 805306368 | bytes 6578176 | tf_op jit(solution)/shard_map/attend_back/pallas_call | solution.py:41
  31.9 0.4 collective-permute-start.18
  32.3 0.9 %collective-permute-start.14 = (bf16[2,2,64,256]{3,2,1,0:T(8,128)(2,1)S(1)}, bf16[2,2,64,256]{3,2,1,0:T(8,128)(2,1)S(1)}, u32[]{:S(2)}, u32[]{:S(2)}) collective-permute-start(bf16[2,2,64,256]{3,2,1,0:T(8,128)(2,1)S(1)} %sum_cores.2), channel_id=1, source_target_pairs={{0,16},{8,24},{16,0},{24,8},{1,17},{9,25},{17,1},{25,9},{2,18},{10... | collective-permute-start | bytes 393224 | tf_op jit(solution)/shard_map/ppermute | solution.py:26
  33.2 0.2 collective-permute-start.15
  33.4 1.2 %attend_back.7 = (bf16[2,64,1024]{2,1,0:T(8,128)(2,1)S(1)}, bf16[2,64,1024]{2,1,0:T(8,128)(2,1)S(1)}, bf16[2,2,64,256]{3,2,1,0:T(8,128)(2,1)S(1)}, bf16[2,2,64,256]{3,2,1,0:T(8,128)(2,1)S(1)}) custom-call(bf16[1024,128]{1,0:T(8,128)(2,1)S(1)} %get-tuple-element.59.q_all, bf16[1024,128]{1,0:T(8,128)(2,1)S(1)} %get-tuple-element.60.do_all, ...), custom_call_target="tpu_custom_call" | custom-call | flops 805306368 | bytes 6840320 | tf_op jit(solution)/shard_map/attend_back/pallas_call | solution.py:41
  34.7 1.1 %collective-permute-done.17.refs_0_ = bf16[2,2,64,256]{3,2,1,0:T(8,128)(2,1)S(1)} collective-permute-done((bf16[2,2,64,256]{3,2,1,0:T(8,128)(2,1)S(1)}, bf16[2,2,64,256]{3,2,1,0:T(8,128)(2,1)S(1)}, u32[]{:S(2)}, u32[]{:S(2)}) %collective-permute-start.17) | collective-permute-done | bytes 131104 | tf_op jit(solution)/shard_map/ppermute | solution.py:26
  35.7 0.1 sum_heads.3
  35.8 0.4 collective-permute-start.19
  36.2 1.9 %collective-permute-start.20 = (bf16[2,64,256]{2,1,0:T(8,128)(2,1)S(1)}, bf16[2,64,256]{2,1,0:T(8,128)(2,1)S(1)}, u32[]{:S(2)}, u32[]{:S(2)}) collective-permute-start(bf16[2,64,256]{2,1,0:T(8,128)(2,1)S(1)} %get-tuple-element.107), channel_id=1, source_target_pairs={{0,6},{1,7},{2,4},{3,5},{4,2},{5,3},{6,0},{7,1},{8,14},{9,15},{10,... | collective-permute-start | bytes 196616 | tf_op jit(solution)/shard_map/ppermute | solution.py:26
  38.1 0.1 collective-permute-done.14.refs_0_
  38.2 0.1 sum_heads.2
  38.3 1.2 %collective-permute-start.21 = (bf16[2,64,256]{2,1,0:T(8,128)(2,1)S(1)}, bf16[2,64,256]{2,1,0:T(8,128)(2,1)S(1)}, u32[]{:S(2)}, u32[]{:S(2)}) collective-permute-start(bf16[2,64,256]{2,1,0:T(8,128)(2,1)S(1)} %get-tuple-element.108), channel_id=1, source_target_pairs={{0,2},{1,3},{2,0},{3,1},{4,6},{5,7},{6,4},{7,5},{8,10},{9,11},{10,... | collective-permute-start | bytes 196616 | tf_op jit(solution)/shard_map/ppermute | solution.py:26
  39.5 1.5 %collective-permute-start.16 = (bf16[2,64,1024]{2,1,0:T(8,128)(2,1)S(1)}, bf16[2,64,1024]{2,1,0:T(8,128)(2,1)S(1)}, u32[]{:S(2)}, u32[]{:S(2)}) collective-permute-start(bf16[2,64,1024]{2,1,0:T(8,128)(2,1)S(1)} %get-tuple-element.101), channel_id=1, source_target_pairs={{0,8},{8,0},{16,24},{24,16},{1,9},{9,1},{17,25},{25,17},{2,10},{10... | collective-permute-start | bytes 786440 | tf_op jit(solution)/shard_map/ppermute | solution.py:26
  41.0 2.2 %collective-permute-done.19.refs_0_ = bf16[2,64,256]{2,1,0:T(8,128)(2,1)S(1)} collective-permute-done((bf16[2,64,256]{2,1,0:T(8,128)(2,1)S(1)}, bf16[2,64,256]{2,1,0:T(8,128)(2,1)S(1)}, u32[]{:S(2)}, u32[]{:S(2)}) %collective-permute-start.19) | collective-permute-done | bytes 65568 | tf_op jit(solution)/shard_map/ppermute | solution.py:26
  43.2 1.1 %collective-permute-done.21.refs_2_ = bf16[2,64,256]{2,1,0:T(8,128)(2,1)S(1)} collective-permute-done((bf16[2,64,256]{2,1,0:T(8,128)(2,1)S(1)}, bf16[2,64,256]{2,1,0:T(8,128)(2,1)S(1)}, u32[]{:S(2)}, u32[]{:S(2)}) %collective-permute-start.21) | collective-permute-done | bytes 65568 | tf_op jit(solution)/shard_map/ppermute | solution.py:26
  44.3 1.6 %collective-permute-start.22 = (bf16[64,256]{1,0:T(8,128)(2,1)S(1)}, bf16[64,256]{1,0:T(8,128)(2,1)S(1)}, u32[]{:S(2)}, u32[]{:S(2)}) collective-permute-start(bf16[64,256]{1,0:T(8,128)(2,1)S(1)} %get-tuple-element.110), channel_id=1, source_target_pairs={{0,8},{8,0},{16,24},{24,16},{1,9},{9,1},{17,25},{25,17},{2,10},{10... | collective-permute-start | bytes 98312 | tf_op jit(solution)/shard_map/ppermute | solution.py:26
  45.8 0.7 %collective-permute-done.16.refs_1_ = bf16[2,64,1024]{2,1,0:T(8,128)(2,1)S(1)} collective-permute-done((bf16[2,64,1024]{2,1,0:T(8,128)(2,1)S(1)}, bf16[2,64,1024]{2,1,0:T(8,128)(2,1)S(1)}, u32[]{:S(2)}, u32[]{:S(2)}) %collective-permute-start.16) | collective-permute-done | bytes 262176 | tf_op jit(solution)/shard_map/ppermute | solution.py:26
  46.5 0.8 %finish_q.1 = (bf16[64,2048]{1,0:T(8,128)(2,1)}, bf16[64,2048]{1,0:T(8,128)(2,1)}, f32[8,128]{1,0:T(8,128)S(1)}) custom-call(s32[1]{0:T(128)} %bitcast.group_ref, bf16[2,64,1024]{2,1,0:T(8,128)(2,1)S(1)} %get-tuple-element.100.refs_0_, bf16[2,64,1024]{2,1,0:T(8,128)(2,1)S(1)} %collective-permute-done.16.refs_1_), custom_call_target="tpu_custom_call" | custom-call | bytes 1052676 | tf_op jit(solution)/shard_map/finish_q/pallas_call | solution.py:41
  47.3 0.9 %collective-permute-done.22.refs_1_ = bf16[64,256]{1,0:T(8,128)(2,1)S(1)} collective-permute-done((bf16[64,256]{1,0:T(8,128)(2,1)S(1)}, bf16[64,256]{1,0:T(8,128)(2,1)S(1)}, u32[]{:S(2)}, u32[]{:S(2)}) %collective-permute-start.22) | collective-permute-done | bytes 32800 | tf_op jit(solution)/shard_map/ppermute | solution.py:26
  48.3 0.6 %finish_kv.1 = (bf16[64,256]{1,0:T(8,128)(2,1)}, bf16[64,256]{1,0:T(8,128)(2,1)}) custom-call(s32[1]{0:T(128)} %bitcast.group_ref, bf16[64,256]{1,0:T(8,128)(2,1)S(1)} %get-tuple-element.109.refs_0_, bf16[64,256]{1,0:T(8,128)(2,1)S(1)} %collective-permute-done.22.refs_1_, f32[8,128]{1,0:T(8,128)S(1)} %get-tuple-element.111.refs_2_), custom_call_target="tpu_custom_call" | custom-call | bytes 135172 | tf_op jit(solution)/shard_map/finish_kv/pallas_call | solution.py:41
  (26 shorter events, 0.3 us)
Async XLA Ops:
  1.4 4.9 %collective-permute-start.1 = (bf16[64,256]{1,0:T(8,128)(2,1)S(1)}, bf16[64,256]{1,0:T(8,128)(2,1)S(1)}, u32[]{:S(2)}, u32[]{:S(2)}) collective-permute-start(bf16[64,256]{1,0:T(8,128)(2,1)S(1)} %pad_maximum_fusion.3), channel_id=1, source_target_pairs={{0,8},{8,0},{16,24},{24,16},{1,9},{9,1},{17,25},{25,17},{2,10},{10... | collective-permute-start | bytes 98312 | tf_op jit(solution)/shard_map/ppermute | solution.py:26
  5.6 11.3 %collective-permute-start = (bf16[2,64,1024]{2,1,0:T(8,128)(2,1)S(1)}, bf16[2,64,1024]{2,1,0:T(8,128)(2,1)S(1)}, u32[]{:S(2)}, u32[]{:S(2)}) collective-permute-start(bf16[2,64,1024]{2,1,0:T(8,128)(2,1)S(1)} %pad_maximum_fusion.1), channel_id=1, source_target_pairs={{0,8},{8,0},{16,24},{24,16},{1,9},{9,1},{17,25},{25,17},{2,10},{10... | collective-permute-start | bytes 786440 | tf_op jit(solution)/shard_map/ppermute | solution.py:26
  6.3 4.8 %collective-permute-start.4 = (bf16[2,64,256]{2,1,0:T(8,128)(2,1)S(1)}, bf16[2,64,256]{2,1,0:T(8,128)(2,1)S(1)}, u32[]{:S(2)}, u32[]{:S(2)}) collective-permute-start(bf16[2,64,256]{2,1,0:T(8,128)(2,1)S(1)} %pad_maximum_fusion.2.refs_0_), channel_id=1, source_target_pairs={{0,2},{1,3},{2,0},{3,1},{4,6},{5,7},{6,4},{7,5},{8,10},{9,11},{10,... | collective-permute-start | bytes 196616 | tf_op jit(solution)/shard_map/ppermute | solution.py:26
  8.5 6.2 %collective-permute-start.3 = (bf16[2,64,256]{2,1,0:T(8,128)(2,1)S(1)}, bf16[2,64,256]{2,1,0:T(8,128)(2,1)S(1)}, u32[]{:S(2)}, u32[]{:S(2)}) collective-permute-start(bf16[2,64,256]{2,1,0:T(8,128)(2,1)S(1)} %pad_maximum_fusion.2.refs_0_), channel_id=1, source_target_pairs={{0,6},{1,7},{2,4},{3,5},{4,2},{5,3},{6,0},{7,1},{8,14},{9,15},{10,... | collective-permute-start | bytes 196616 | tf_op jit(solution)/shard_map/ppermute | solution.py:26
  11.0 5.9 %collective-permute-start.2 = (bf16[2,64,256]{2,1,0:T(8,128)(2,1)S(1)}, bf16[2,64,256]{2,1,0:T(8,128)(2,1)S(1)}, u32[]{:S(2)}, u32[]{:S(2)}) collective-permute-start(bf16[2,64,256]{2,1,0:T(8,128)(2,1)S(1)} %pad_maximum_fusion.2.refs_0_), channel_id=1, source_target_pairs={{0,4},{1,5},{2,6},{3,7},{4,0},{5,1},{6,2},{7,3},{8,12},{9,13},{10,... | collective-permute-start | bytes 196616 | tf_op jit(solution)/shard_map/ppermute | solution.py:26
  11.1 8.6 %collective-permute-start.7 = (bf16[2,2,64,256]{3,2,1,0:T(8,128)(2,1)S(1)}, bf16[2,2,64,256]{3,2,1,0:T(8,128)(2,1)S(1)}, u32[]{:S(2)}, u32[]{:S(2)}) collective-permute-start(bf16[2,2,64,256]{3,2,1,0:T(8,128)(2,1)S(1)} %stack.46.refs_2_.refs_1_), channel_id=1, source_target_pairs={{0,16},{8,24},{16,0},{24,8},{1,17},{9,25},{17,1},{25,9},{2,18},{10... | collective-permute-start | bytes 393224 | tf_op jit(solution)/shard_map/ppermute | solution.py:26
  16.9 6.4 %collective-permute-start.8 = (bf16[2,2,64,256]{3,2,1,0:T(8,128)(2,1)S(1)}, bf16[2,2,64,256]{3,2,1,0:T(8,128)(2,1)S(1)}, u32[]{:S(2)}, u32[]{:S(2)}) collective-permute-start(bf16[2,2,64,256]{3,2,1,0:T(8,128)(2,1)S(1)} %get-tuple-element.65.refs_0_.refs_1_), channel_id=1, source_target_pairs={{0,16},{8,24},{16,0},{24,8},{1,17},{9,25},{17,1},{25,9},{2,18},{10... | collective-permute-start | bytes 393224 | tf_op jit(solution)/shard_map/ppermute | solution.py:26
  18.5 2.8 %collective-permute-start.5 = (bf16[2,2,64,256]{3,2,1,0:T(8,128)(2,1)S(1)}, bf16[2,2,64,256]{3,2,1,0:T(8,128)(2,1)S(1)}, u32[]{:S(2)}, u32[]{:S(2)}) collective-permute-start(bf16[2,2,64,256]{3,2,1,0:T(8,128)(2,1)S(1)} %get-tuple-element.65.refs_0_.refs_1_), channel_id=1, source_target_pairs={{0,1},{1,0},{2,3},{3,2},{4,5},{5,4},{6,7},{7,6},{8,9},{9,8},{10,11... | collective-permute-start | bytes 393224 | tf_op jit(solution)/shard_map/ppermute | solution.py:26
  18.5 2.7 %collective-permute-start.6 = (bf16[2,2,64,256]{3,2,1,0:T(8,128)(2,1)S(1)}, bf16[2,2,64,256]{3,2,1,0:T(8,128)(2,1)S(1)}, u32[]{:S(2)}, u32[]{:S(2)}) collective-permute-start(bf16[2,2,64,256]{3,2,1,0:T(8,128)(2,1)S(1)} %get-tuple-element.66), channel_id=1, source_target_pairs={{0,1},{1,0},{2,3},{3,2},{4,5},{5,4},{6,7},{7,6},{8,9},{9,8},{10,11... | collective-permute-start | bytes 393224 | tf_op jit(solution)/shard_map/ppermute | solution.py:26
  19.7 4.8 %collective-permute-start.10 = (bf16[2,2,64,256]{3,2,1,0:T(8,128)(2,1)S(1)}, bf16[2,2,64,256]{3,2,1,0:T(8,128)(2,1)S(1)}, u32[]{:S(2)}, u32[]{:S(2)}) collective-permute-start(bf16[2,2,64,256]{3,2,1,0:T(8,128)(2,1)S(1)} %collective-permute-done.7.refs_0_), channel_id=1, source_target_pairs={{0,1},{1,0},{2,3},{3,2},{4,5},{5,4},{6,7},{7,6},{8,9},{9,8},{10,11... | collective-permute-start | bytes 393224 | tf_op jit(solution)/shard_map/ppermute | solution.py:26
  23.3 1.5 %collective-permute-start.9 = (bf16[2,2,64,256]{3,2,1,0:T(8,128)(2,1)S(1)}, bf16[2,2,64,256]{3,2,1,0:T(8,128)(2,1)S(1)}, u32[]{:S(2)}, u32[]{:S(2)}) collective-permute-start(bf16[2,2,64,256]{3,2,1,0:T(8,128)(2,1)S(1)} %collective-permute-done.8.refs_0_), channel_id=1, source_target_pairs={{0,1},{1,0},{2,3},{3,2},{4,5},{5,4},{6,7},{7,6},{8,9},{9,8},{10,11... | collective-permute-start | bytes 393224 | tf_op jit(solution)/shard_map/ppermute | solution.py:26
  27.5 1.9 %collective-permute-start.12 = (bf16[2,2,64,256]{3,2,1,0:T(8,128)(2,1)S(1)}, bf16[2,2,64,256]{3,2,1,0:T(8,128)(2,1)S(1)}, u32[]{:S(2)}, u32[]{:S(2)}) collective-permute-start(bf16[2,2,64,256]{3,2,1,0:T(8,128)(2,1)S(1)} %get-tuple-element.90), channel_id=1, source_target_pairs={{0,1},{1,0},{2,3},{3,2},{4,5},{5,4},{6,7},{7,6},{8,9},{9,8},{10,11... | collective-permute-start | bytes 393224 | tf_op jit(solution)/shard_map/ppermute | solution.py:26
  27.9 1.5 %collective-permute-start.11 = (bf16[2,2,64,256]{3,2,1,0:T(8,128)(2,1)S(1)}, bf16[2,2,64,256]{3,2,1,0:T(8,128)(2,1)S(1)}, u32[]{:S(2)}, u32[]{:S(2)}) collective-permute-start(bf16[2,2,64,256]{3,2,1,0:T(8,128)(2,1)S(1)} %get-tuple-element.88), channel_id=1, source_target_pairs={{0,1},{1,0},{2,3},{3,2},{4,5},{5,4},{6,7},{7,6},{8,9},{9,8},{10,11... | collective-permute-start | bytes 393224 | tf_op jit(solution)/shard_map/ppermute | solution.py:26
  29.5 1.3 %collective-permute-start.13 = (bf16[64,128]{1,0:T(8,128)(2,1)S(1)}, bf16[64,128]{1,0:T(8,128)(2,1)S(1)}, u32[]{:S(2)}, u32[]{:S(2)}) collective-permute-start(bf16[64,128]{1,0:T(8,128)(2,1)S(1)} %slice_bitcast_fusion), channel_id=1, source_target_pairs={{0,1},{1,0},{2,3},{3,2},{4,5},{5,4},{6,7},{7,6},{8,9},{9,8},{10,11... | collective-permute-start | bytes 49160 | tf_op jit(solution)/shard_map/ppermute | solution.py:26
  29.9 5.9 %collective-permute-start.17 = (bf16[2,2,64,256]{3,2,1,0:T(8,128)(2,1)S(1)}, bf16[2,2,64,256]{3,2,1,0:T(8,128)(2,1)S(1)}, u32[]{:S(2)}, u32[]{:S(2)}) collective-permute-start(bf16[2,2,64,256]{3,2,1,0:T(8,128)(2,1)S(1)} %sum_cores.3), channel_id=1, source_target_pairs={{0,16},{8,24},{16,0},{24,8},{1,17},{9,25},{17,1},{25,9},{2,18},{10... | collective-permute-start | bytes 393224 | tf_op jit(solution)/shard_map/ppermute | solution.py:26
  31.9 3.9 %collective-permute-start.18 = (bf16[2,2,64,256]{3,2,1,0:T(8,128)(2,1)S(1)}, bf16[2,2,64,256]{3,2,1,0:T(8,128)(2,1)S(1)}, u32[]{:S(2)}, u32[]{:S(2)}) collective-permute-start(bf16[2,2,64,256]{3,2,1,0:T(8,128)(2,1)S(1)} %get-tuple-element.104), channel_id=1, source_target_pairs={{0,1},{1,0},{2,3},{3,2},{4,5},{5,4},{6,7},{7,6},{8,9},{9,8},{10,11... | collective-permute-start | bytes 393224 | tf_op jit(solution)/shard_map/ppermute | solution.py:26
  32.3 5.9 %collective-permute-start.14 = (bf16[2,2,64,256]{3,2,1,0:T(8,128)(2,1)S(1)}, bf16[2,2,64,256]{3,2,1,0:T(8,128)(2,1)S(1)}, u32[]{:S(2)}, u32[]{:S(2)}) collective-permute-start(bf16[2,2,64,256]{3,2,1,0:T(8,128)(2,1)S(1)} %sum_cores.2), channel_id=1, source_target_pairs={{0,16},{8,24},{16,0},{24,8},{1,17},{9,25},{17,1},{25,9},{2,18},{10... | collective-permute-start | bytes 393224 | tf_op jit(solution)/shard_map/ppermute | solution.py:26
  33.2 5.0 %collective-permute-start.15 = (bf16[2,2,64,256]{3,2,1,0:T(8,128)(2,1)S(1)}, bf16[2,2,64,256]{3,2,1,0:T(8,128)(2,1)S(1)}, u32[]{:S(2)}, u32[]{:S(2)}) collective-permute-start(bf16[2,2,64,256]{3,2,1,0:T(8,128)(2,1)S(1)} %get-tuple-element.97), channel_id=1, source_target_pairs={{0,1},{1,0},{2,3},{3,2},{4,5},{5,4},{6,7},{7,6},{8,9},{9,8},{10,11... | collective-permute-start | bytes 393224 | tf_op jit(solution)/shard_map/ppermute | solution.py:26
  35.8 7.4 %collective-permute-start.19 = (bf16[2,64,256]{2,1,0:T(8,128)(2,1)S(1)}, bf16[2,64,256]{2,1,0:T(8,128)(2,1)S(1)}, u32[]{:S(2)}, u32[]{:S(2)}) collective-permute-start(bf16[2,64,256]{2,1,0:T(8,128)(2,1)S(1)} %get-tuple-element.106), channel_id=1, source_target_pairs={{0,4},{1,5},{2,6},{3,7},{4,0},{5,1},{6,2},{7,3},{8,12},{9,13},{10,... | collective-permute-start | bytes 196616 | tf_op jit(solution)/shard_map/ppermute | solution.py:26
  36.2 6.9 %collective-permute-start.20 = (bf16[2,64,256]{2,1,0:T(8,128)(2,1)S(1)}, bf16[2,64,256]{2,1,0:T(8,128)(2,1)S(1)}, u32[]{:S(2)}, u32[]{:S(2)}) collective-permute-start(bf16[2,64,256]{2,1,0:T(8,128)(2,1)S(1)} %get-tuple-element.107), channel_id=1, source_target_pairs={{0,6},{1,7},{2,4},{3,5},{4,2},{5,3},{6,0},{7,1},{8,14},{9,15},{10,... | collective-permute-start | bytes 196616 | tf_op jit(solution)/shard_map/ppermute | solution.py:26
  38.3 5.9 %collective-permute-start.21 = (bf16[2,64,256]{2,1,0:T(8,128)(2,1)S(1)}, bf16[2,64,256]{2,1,0:T(8,128)(2,1)S(1)}, u32[]{:S(2)}, u32[]{:S(2)}) collective-permute-start(bf16[2,64,256]{2,1,0:T(8,128)(2,1)S(1)} %get-tuple-element.108), channel_id=1, source_target_pairs={{0,2},{1,3},{2,0},{3,1},{4,6},{5,7},{6,4},{7,5},{8,10},{9,11},{10,... | collective-permute-start | bytes 196616 | tf_op jit(solution)/shard_map/ppermute | solution.py:26
  39.5 7.0 %collective-permute-start.16 = (bf16[2,64,1024]{2,1,0:T(8,128)(2,1)S(1)}, bf16[2,64,1024]{2,1,0:T(8,128)(2,1)S(1)}, u32[]{:S(2)}, u32[]{:S(2)}) collective-permute-start(bf16[2,64,1024]{2,1,0:T(8,128)(2,1)S(1)} %get-tuple-element.101), channel_id=1, source_target_pairs={{0,8},{8,0},{16,24},{24,16},{1,9},{9,1},{17,25},{25,17},{2,10},{10... | collective-permute-start | bytes 786440 | tf_op jit(solution)/shard_map/ppermute | solution.py:26
  44.3 4.0 %collective-permute-start.22 = (bf16[64,256]{1,0:T(8,128)(2,1)S(1)}, bf16[64,256]{1,0:T(8,128)(2,1)S(1)}, u32[]{:S(2)}, u32[]{:S(2)}) collective-permute-start(bf16[64,256]{1,0:T(8,128)(2,1)S(1)} %get-tuple-element.110), channel_id=1, source_target_pairs={{0,8},{8,0},{16,24},{24,16},{1,9},{9,1},{17,25},{25,17},{2,10},{10... | collective-permute-start | bytes 98312 | tf_op jit(solution)/shard_map/ppermute | solution.py:26

commit v15 on v14

--- a/solution.py
+++ b/solution.py
@@ -419,7 +419,7 @@
         handed[p] = column[p]
         if extra:
             handed[p + 1] = handed_on[0]
-        order = q_parts[1:] if p else []
+        order = list(after(q_parts[1:], [info])) if p else []
     columns = [[swap(half, "head", a * kv) for half in column] for a in range(1, spans)]
     near_kv = [column] + [[swap(half, "ctx", core) for half in handed] for core in range(1, cores)]
     near_flat = [half for pair in near_kv for half in pair]

time: 49.1 us -> 48.8 us (level)
  waiting for transfers between devices: 11.3 us -> 10.8 us
    ppermute x23, waiting for transfers between devices: 11.3 us -> 10.8 us  [swap(): return lax.ppermute(block, axis, [(i, i ^ mask) for i in range(size)])]
  transfers between devices with their start and end apart: 23 -> 23, of which waited for: 11 -> 10; matrix products, arithmetic and copies ran while one was open for 4% -> 4% of each run, Pallas kernels for 18% -> 18%
where the time goes in v15:
time: 48.8 us; the launch traced here: 48.5 us
  starting transfers between devices  22 us (45%)
  Pallas kernels  12.2 us (25%)
  waiting for transfers between devices  10.8 us (22%)
  other arithmetic  2.71 us (6%)
  between operations  0.86 us (2%)
    ppermute x23, starting transfers between devices, swap(): return lax.ppermute(block, axis, [(i, i ^ mask) for i in range(size)])  22 us
    pallas_call x19, Pallas kernels, call(): pl.pallas_call(kernel, out_shape=list(outs), in_specs=specs or [VMEM] * l...  12.2 us
    ppermute x23, waiting for transfers between devices, swap(): return lax.ppermute(block, axis, [(i, i ^ mask) for i in range(size)])  10.8 us
    another operation x3, other arithmetic, queries_of(): return jnp.stack([pick(queries, g, width), pick(out_grad, g, width)])  1.18 us
  transfers between devices with their start and end apart: 23, of which 10 were waited for; matrix products, arithmetic and copies ran while one was open for 4% of the time, Pallas kernels for 18%

profile of v15, /device:TPU:0, one launch (start us, length us, event | category | flops | bytes accessed | tf_op | source)
XLA Modules:
  0.0 48.5 jit_solution(16360324683020165305)
XLA Ops:
  0.6 0.8 %broadcast_select_fusion.2 = (bf16[64,128]{1,0:T(8,128)(2,1)S(1)}, bf16[64,128]{1,0:T(8,128)(2,1)S(1)}, bf16[64,128]{1,0:T(8,128)(2,1)S(1)}, bf16[64,128]{1,0:T(8,128)(2,1)S(1)}) fusion(pred[]{:T(512)S(6)} %eq.18, bf16[64,256]{1,0:T(8,128)(2,1)} %bitcast.26, pred[]{:T(512)S(6)} %eq.19, bf16[64,256]{1,0:T(8,128)(2,1)} %bitcast.27), kind=kLoop, calls=%fused_computation.12 | loop fusion | flops 32768 | bytes 131074 | tf_op jit(solution)/shard_map/jit(_where)/select_n | solution.py:382
  1.4 3.0 %collective-permute-start.1 = (bf16[64,256]{1,0:T(8,128)(2,1)S(1)}, bf16[64,256]{1,0:T(8,128)(2,1)S(1)}, u32[]{:S(2)}, u32[]{:S(2)}) collective-permute-start(bf16[64,256]{1,0:T(8,128)(2,1)S(1)} %pad_maximum_fusion.3), channel_id=1, source_target_pairs={{0,8},{8,0},{16,24},{24,16},{1,9},{9,1},{17,25},{25,17},{2,10},{10... | collective-permute-start | bytes 98312 | tf_op jit(solution)/shard_map/ppermute | solution.py:26
  4.4 1.1 %select_bitcast_fusion = (bf16[1,64,1024]{2,1,0:T(8,128)(2,1)S(1)}, bf16[1,64,1024]{2,1,0:T(8,128)(2,1)S(1)}, bf16[1,64,1024]{2,1,0:T(8,128)(2,1)S(1)}, bf16[1,64,1024]{2,1,0:T(8,128)(2,1)S(1)}) fusion(pred[]{:T(512)S(6)} %eq.19, bf16[64,2048]{1,0:T(8,128)(2,1)} %bitcast.24, pred[]{:T(512)S(6)} %eq.18, bf16[64,2048]{1,0:T(8,128)(2,1)} %bitcast.25), kind=kLoop, calls=%fused_computation.2 | loop fusion | flops 262144 | bytes 1048578 | tf_op jit(solution)/shard_map/stack | solution.py:389
  5.6 0.1 collective-permute-start
  5.7 0.6 %collective-permute-done.1 = bf16[64,256]{1,0:T(8,128)(2,1)S(1)} collective-permute-done((bf16[64,256]{1,0:T(8,128)(2,1)S(1)}, bf16[64,256]{1,0:T(8,128)(2,1)S(1)}, u32[]{:S(2)}, u32[]{:S(2)}) %collective-permute-start.1) | collective-permute-done | bytes 32800 | tf_op jit(solution)/shard_map/ppermute | solution.py:26
  6.3 2.2 %collective-permute-start.4 = (bf16[2,64,256]{2,1,0:T(8,128)(2,1)S(1)}, bf16[2,64,256]{2,1,0:T(8,128)(2,1)S(1)}, u32[]{:S(2)}, u32[]{:S(2)}) collective-permute-start(bf16[2,64,256]{2,1,0:T(8,128)(2,1)S(1)} %pad_maximum_fusion.2.refs_0_), channel_id=1, source_target_pairs={{0,2},{1,3},{2,0},{3,1},{4,6},{5,7},{6,4},{7,5},{8,10},{9,11},{10,... | collective-permute-start | bytes 196616 | tf_op jit(solution)/shard_map/ppermute | solution.py:26
  8.5 2.5 %collective-permute-start.3 = (bf16[2,64,256]{2,1,0:T(8,128)(2,1)S(1)}, bf16[2,64,256]{2,1,0:T(8,128)(2,1)S(1)}, u32[]{:S(2)}, u32[]{:S(2)}) collective-permute-start(bf16[2,64,256]{2,1,0:T(8,128)(2,1)S(1)} %pad_maximum_fusion.2.refs_0_), channel_id=1, source_target_pairs={{0,6},{1,7},{2,4},{3,5},{4,2},{5,3},{6,0},{7,1},{8,14},{9,15},{10,... | collective-permute-start | bytes 196616 | tf_op jit(solution)/shard_map/ppermute | solution.py:26
  11.0 0.1 collective-permute-start.2
  11.1 1.7 %collective-permute-start.7 = (bf16[2,2,64,256]{3,2,1,0:T(8,128)(2,1)S(1)}, bf16[2,2,64,256]{3,2,1,0:T(8,128)(2,1)S(1)}, u32[]{:S(2)}, u32[]{:S(2)}) collective-permute-start(bf16[2,2,64,256]{3,2,1,0:T(8,128)(2,1)S(1)} %stack.46.refs_2_.refs_1_), channel_id=1, source_target_pairs={{0,16},{8,24},{16,0},{24,8},{1,17},{9,25},{17,1},{25,9},{2,18},{10... | collective-permute-start | bytes 393224 | tf_op jit(solution)/shard_map/ppermute | solution.py:26
  12.8 0.7 %pad_add_fusion.info_ref = s32[18]{0:T(128)S(1)} fusion(s32[16]{0:T(128)} %param.9, s32[1]{0:T(128)} %bitcast.2, s32[1]{0:T(128)} %bitcast.1), kind=kLoop, calls=%fused_computation.14 | loop fusion | flops 36 | bytes 144 | tf_op jit(solution)/shard_map/concatenate | solution.py:358
  13.5 1.2 %collective-permute-done.3.refs_1_ = bf16[2,64,256]{2,1,0:T(8,128)(2,1)S(1)} collective-permute-done((bf16[2,64,256]{2,1,0:T(8,128)(2,1)S(1)}, bf16[2,64,256]{2,1,0:T(8,128)(2,1)S(1)}, u32[]{:S(2)}, u32[]{:S(2)}) %collective-permute-start.3) | collective-permute-done | bytes 65568 | tf_op jit(solution)/shard_map/ppermute | solution.py:26
  14.7 2.1 %collective-permute-done.2.refs_0_ = bf16[2,64,256]{2,1,0:T(8,128)(2,1)S(1)} collective-permute-done((bf16[2,64,256]{2,1,0:T(8,128)(2,1)S(1)}, bf16[2,64,256]{2,1,0:T(8,128)(2,1)S(1)}, u32[]{:S(2)}, u32[]{:S(2)}) %collective-permute-start.2) | collective-permute-done | bytes 65568 | tf_op jit(solution)/shard_map/ppermute | solution.py:26
  16.9 1.6 %collective-permute-start.8 = (bf16[2,2,64,256]{3,2,1,0:T(8,128)(2,1)S(1)}, bf16[2,2,64,256]{3,2,1,0:T(8,128)(2,1)S(1)}, u32[]{:S(2)}, u32[]{:S(2)}) collective-permute-start(bf16[2,2,64,256]{3,2,1,0:T(8,128)(2,1)S(1)} %get-tuple-element.67.refs_0_.refs_1_), channel_id=1, source_target_pairs={{0,16},{8,24},{16,0},{24,8},{1,17},{9,25},{17,1},{25,9},{2,18},{10... | collective-permute-start | bytes 393224 | tf_op jit(solution)/shard_map/ppermute | solution.py:26
  18.5 0.5 %collective-permute-start.6 = (bf16[2,2,64,256]{3,2,1,0:T(8,128)(2,1)S(1)}, bf16[2,2,64,256]{3,2,1,0:T(8,128)(2,1)S(1)}, u32[]{:S(2)}, u32[]{:S(2)}) collective-permute-start(bf16[2,2,64,256]{3,2,1,0:T(8,128)(2,1)S(1)} %get-tuple-element.68), channel_id=1, source_target_pairs={{0,1},{1,0},{2,3},{3,2},{4,5},{5,4},{6,7},{7,6},{8,9},{9,8},{10,11... | collective-permute-start | bytes 393224 | tf_op jit(solution)/shard_map/ppermute | solution.py:26
  19.0 0.1 collective-permute-start.10
  19.1 0.7 %turn.1 = (bf16[1024,128]{1,0:T(8,128)(2,1)S(1)}, bf16[1024,128]{1,0:T(8,128)(2,1)S(1)}, bf16[128,1024]{1,0:T(8,128)(2,1)S(1)}, bf16[128,1024]{1,0:T(8,128)(2,1)...) custom-call(s32[18]{0:T(128)S(1)} %pad_add_fusion.info_ref, bf16[2,64,1024]{2,1,0:T(8,128)(2,1)S(1)} %pad_maximum_fusion.refs_0_, ...), custom_call_target="tpu_custom_call" | custom-call | bytes 1769544 | tf_op jit(solution)/shard_map/turn/pallas_call | solution.py:41
  19.9 0.7 %attend_mid.2 = (f32[256,1024]{1,0:T(8,128)S(1)}, f32[1,1024]{1,0:T(1,128)S(1)}, f32[1,1024]{1,0:T(1,128)S(1)}, f32[128,1024]{1,0:T(8,128)S(1)}) custom-call(s32[128,256]{1,0:T(8,128)S(1)} %get-tuple-element.63.gap_ref, s32[64,256]{1,0:T(8,128)S(1)} %get-tuple-element.64.first_ref, bf16[128,1024]{1,0:T(8,128)(2,1)S(1)} %get-tuple-element.65.q_t, ...), custom_call_target="tpu_custom_call" | custom-call | flops 268435456 | bytes 2170880 | tf_op jit(solution)/shard_map/attend_mid/pallas_call | solution.py:41
  20.6 2.0 %attend_near.1 = (f32[1024,1024]{1,0:T(8,128)S(1)}, f32[1,1024]{1,0:T(1,128)S(1)}, f32[1,1024]{1,0:T(1,128)S(1)}, f32[128,1024]{1,0:T(8,128)S(1)}) custom-call(s32[128,256]{1,0:T(8,128)S(1)} %get-tuple-element.63.gap_ref, s32[64,256]{1,0:T(8,128)S(1)} %get-tuple-element.64.first_ref, bf16[128,1024]{1,0:T(8,128)(2,1)S(1)} %get-tuple-element.65.q_t, ...), custom_call_target="tpu_custom_call" | custom-call | flops 1073741824 | bytes 5713920 | tf_op jit(solution)/shard_map/attend_near/pallas_call | solution.py:41
  22.6 0.6 %collective-permute-start.9 = (bf16[2,2,64,256]{3,2,1,0:T(8,128)(2,1)S(1)}, bf16[2,2,64,256]{3,2,1,0:T(8,128)(2,1)S(1)}, u32[]{:S(2)}, u32[]{:S(2)}) collective-permute-start(bf16[2,2,64,256]{3,2,1,0:T(8,128)(2,1)S(1)} %collective-permute-done.8.refs_0_), channel_id=1, source_target_pairs={{0,1},{1,0},{2,3},{3,2},{4,5},{5,4},{6,7},{7,6},{8,9},{9,8},{10,11... | collective-permute-start | bytes 393224 | tf_op jit(solution)/shard_map/ppermute | solution.py:26
  23.2 0.7 %attend_mid.3 = (f32[256,1024]{1,0:T(8,128)S(1)}, f32[1,1024]{1,0:T(1,128)S(1)}, f32[1,1024]{1,0:T(1,128)S(1)}, f32[128,1024]{1,0:T(8,128)S(1)}) custom-call(s32[128,256]{1,0:T(8,128)S(1)} %get-tuple-element.63.gap_ref, s32[64,256]{1,0:T(8,128)S(1)} %get-tuple-element.64.first_ref, bf16[128,1024]{1,0:T(8,128)(2,1)S(1)} %get-tuple-element.65.q_t, ...), custom_call_target="tpu_custom_call" | custom-call | flops 268435456 | bytes 2174976 | tf_op jit(solution)/shard_map/attend_mid/pallas_call | solution.py:41
  23.9 0.2 collective-permute-done.9.refs_9_
  24.2 2.6 %attend_far.1 = (f32[1,1024]{1,0:T(1,128)S(1)}, f32[1,1024]{1,0:T(1,128)S(1)}, f32[1,1024]{1,0:T(1,128)S(1)}, f32[1,1024]{1,0:T(1,128)S(1)}, bf16[128,1024]{1,0:...) custom-call(s32[128,256]{1,0:T(8,128)S(1)} %get-tuple-element.63.gap, ...), custom_call_target="tpu_custom_call" | custom-call | flops 1073741824 | bytes 4169728 | tf_op jit(solution)/shard_map/attend_far/pallas_call | solution.py:41
  26.8 0.4 collective-permute-start.12
  27.2 0.1 collective-permute-start.11
  27.4 0.6 %attend_back.4 = (f32[128,1024]{1,0:T(8,128)S(1)}, bf16[2,2,64,256]{3,2,1,0:T(8,128)(2,1)S(1)}) custom-call(bf16[1024,128]{1,0:T(8,128)(2,1)S(1)} %get-tuple-element.60.q_all, bf16[1024,128]{1,0:T(8,128)(2,1)S(1)} %get-tuple-element.61.do_all, bf16[128,1024]{1,0:T(8,128)(2,1)S(1)} %get-tuple-element.62.do_t, f32[256,1024]{1,0:T(8,128)S(1)} %get-tuple-element.84.e_ref, ...), custom_call_target="tpu_custom_call" | custom-call | flops 402653184 | bytes 3153920 | tf_op jit(solution)/shard_map/attend_back/pallas_call | solution.py:41
  28.0 0.7 %attend_back.5 = (f32[128,1024]{1,0:T(8,128)S(1)}, bf16[2,2,64,256]{3,2,1,0:T(8,128)(2,1)S(1)}) custom-call(bf16[1024,128]{1,0:T(8,128)(2,1)S(1)} %get-tuple-element.60.q_all, bf16[1024,128]{1,0:T(8,128)(2,1)S(1)} %get-tuple-element.61.do_all, bf16[128,1024]{1,0:T(8,128)(2,1)S(1)} %get-tuple-element.62.do_t, f32[256,1024]{1,0:T(8,128)S(1)} %get-tuple-element.82.e_ref, ...), custom_call_target="tpu_custom_call" | custom-call | flops 402653184 | bytes 3153920 | tf_op jit(solution)/shard_map/attend_back/pallas_call | solution.py:41
  28.8 0.4 collective-permute-start.13
  29.2 0.5 %collective-permute-start.17 = (bf16[2,2,64,256]{3,2,1,0:T(8,128)(2,1)S(1)}, bf16[2,2,64,256]{3,2,1,0:T(8,128)(2,1)S(1)}, u32[]{:S(2)}, u32[]{:S(2)}) collective-permute-start(bf16[2,2,64,256]{3,2,1,0:T(8,128)(2,1)S(1)} %sum_cores.3), channel_id=1, source_target_pairs={{0,16},{8,24},{16,0},{24,8},{1,17},{9,25},{17,1},{25,9},{2,18},{10... | collective-permute-start | bytes 393224 | tf_op jit(solution)/shard_map/ppermute | solution.py:26
  29.7 0.3 collective-permute-done.13.refs_2_.refs_3_
  30.1 1.2 %attend_back.6 = (f32[128,1024]{1,0:T(8,128)S(1)}, bf16[2,2,64,256]{3,2,1,0:T(8,128)(2,1)S(1)}, bf16[2,2,64,256]{3,2,1,0:T(8,128)(2,1)S(1)}) custom-call(bf16[1024,128]{1,0:T(8,128)(2,1)S(1)} %get-tuple-element.60.q_all, bf16[1024,128]{1,0:T(8,128)(2,1)S(1)} %get-tuple-element.61.do_all, bf16[128,1024]{1,0:T(8,128)(2,1)S(1)} %get-tuple-element.62.do_t, ...), custom_call_target="tpu_custom_call" | custom-call | flops 805306368 | bytes 6578176 | tf_op jit(solution)/shard_map/attend_back/pallas_call | solution.py:41
  31.2 0.4 collective-permute-start.18
  31.6 0.9 %collective-permute-start.14 = (bf16[2,2,64,256]{3,2,1,0:T(8,128)(2,1)S(1)}, bf16[2,2,64,256]{3,2,1,0:T(8,128)(2,1)S(1)}, u32[]{:S(2)}, u32[]{:S(2)}) collective-permute-start(bf16[2,2,64,256]{3,2,1,0:T(8,128)(2,1)S(1)} %sum_cores.2), channel_id=1, source_target_pairs={{0,16},{8,24},{16,0},{24,8},{1,17},{9,25},{17,1},{25,9},{2,18},{10... | collective-permute-start | bytes 393224 | tf_op jit(solution)/shard_map/ppermute | solution.py:26
  32.6 0.2 collective-permute-start.15
  32.7 1.3 %attend_back.7 = (bf16[2,64,1024]{2,1,0:T(8,128)(2,1)S(1)}, bf16[2,64,1024]{2,1,0:T(8,128)(2,1)S(1)}, bf16[2,2,64,256]{3,2,1,0:T(8,128)(2,1)S(1)}, bf16[2,2,64,256]{3,2,1,0:T(8,128)(2,1)S(1)}) custom-call(bf16[1024,128]{1,0:T(8,128)(2,1)S(1)} %get-tuple-element.60.q_all, bf16[1024,128]{1,0:T(8,128)(2,1)S(1)} %get-tuple-element.61.do_all, ...), custom_call_target="tpu_custom_call" | custom-call | flops 805306368 | bytes 6840320 | tf_op jit(solution)/shard_map/attend_back/pallas_call | solution.py:41
  34.0 1.1 %collective-permute-done.17.refs_0_ = bf16[2,2,64,256]{3,2,1,0:T(8,128)(2,1)S(1)} collective-permute-done((bf16[2,2,64,256]{3,2,1,0:T(8,128)(2,1)S(1)}, bf16[2,2,64,256]{3,2,1,0:T(8,128)(2,1)S(1)}, u32[]{:S(2)}, u32[]{:S(2)}) %collective-permute-start.17) | collective-permute-done | bytes 131104 | tf_op jit(solution)/shard_map/ppermute | solution.py:26
  35.1 0.1 sum_heads.3
  35.1 1.1 %collective-permute-start.19 = (bf16[2,64,256]{2,1,0:T(8,128)(2,1)S(1)}, bf16[2,64,256]{2,1,0:T(8,128)(2,1)S(1)}, u32[]{:S(2)}, u32[]{:S(2)}) collective-permute-start(bf16[2,64,256]{2,1,0:T(8,128)(2,1)S(1)} %get-tuple-element.108), channel_id=1, source_target_pairs={{0,4},{1,5},{2,6},{3,7},{4,0},{5,1},{6,2},{7,3},{8,12},{9,13},{10,... | collective-permute-start | bytes 196616 | tf_op jit(solution)/shard_map/ppermute | solution.py:26
  36.2 1.9 %collective-permute-start.20 = (bf16[2,64,256]{2,1,0:T(8,128)(2,1)S(1)}, bf16[2,64,256]{2,1,0:T(8,128)(2,1)S(1)}, u32[]{:S(2)}, u32[]{:S(2)}) collective-permute-start(bf16[2,64,256]{2,1,0:T(8,128)(2,1)S(1)} %get-tuple-element.109), channel_id=1, source_target_pairs={{0,6},{1,7},{2,4},{3,5},{4,2},{5,3},{6,0},{7,1},{8,14},{9,15},{10,... | collective-permute-start | bytes 196616 | tf_op jit(solution)/shard_map/ppermute | solution.py:26
  38.1 0.1 sum_heads.2
  38.2 0.7 %collective-permute-start.21 = (bf16[2,64,256]{2,1,0:T(8,128)(2,1)S(1)}, bf16[2,64,256]{2,1,0:T(8,128)(2,1)S(1)}, u32[]{:S(2)}, u32[]{:S(2)}) collective-permute-start(bf16[2,64,256]{2,1,0:T(8,128)(2,1)S(1)} %get-tuple-element.110), channel_id=1, source_target_pairs={{0,2},{1,3},{2,0},{3,1},{4,6},{5,7},{6,4},{7,5},{8,10},{9,11},{10,... | collective-permute-start | bytes 196616 | tf_op jit(solution)/shard_map/ppermute | solution.py:26
  38.9 1.5 %collective-permute-start.16 = (bf16[2,64,1024]{2,1,0:T(8,128)(2,1)S(1)}, bf16[2,64,1024]{2,1,0:T(8,128)(2,1)S(1)}, u32[]{:S(2)}, u32[]{:S(2)}) collective-permute-start(bf16[2,64,1024]{2,1,0:T(8,128)(2,1)S(1)} %get-tuple-element.103), channel_id=1, source_target_pairs={{0,8},{8,0},{16,24},{24,16},{1,9},{9,1},{17,25},{25,17},{2,10},{10... | collective-permute-start | bytes 786440 | tf_op jit(solution)/shard_map/ppermute | solution.py:26
  40.4 2.7 %collective-permute-done.19.refs_0_ = bf16[2,64,256]{2,1,0:T(8,128)(2,1)S(1)} collective-permute-done((bf16[2,64,256]{2,1,0:T(8,128)(2,1)S(1)}, bf16[2,64,256]{2,1,0:T(8,128)(2,1)S(1)}, u32[]{:S(2)}, u32[]{:S(2)}) %collective-permute-start.19) | collective-permute-done | bytes 65568 | tf_op jit(solution)/shard_map/ppermute | solution.py:26
  43.1 0.8 %collective-permute-done.21.refs_2_ = bf16[2,64,256]{2,1,0:T(8,128)(2,1)S(1)} collective-permute-done((bf16[2,64,256]{2,1,0:T(8,128)(2,1)S(1)}, bf16[2,64,256]{2,1,0:T(8,128)(2,1)S(1)}, u32[]{:S(2)}, u32[]{:S(2)}) %collective-permute-start.21) | collective-permute-done | bytes 65568 | tf_op jit(solution)/shard_map/ppermute | solution.py:26
  43.9 1.6 %collective-permute-start.22 = (bf16[64,256]{1,0:T(8,128)(2,1)S(1)}, bf16[64,256]{1,0:T(8,128)(2,1)S(1)}, u32[]{:S(2)}, u32[]{:S(2)}) collective-permute-start(bf16[64,256]{1,0:T(8,128)(2,1)S(1)} %get-tuple-element.112), channel_id=1, source_target_pairs={{0,8},{8,0},{16,24},{24,16},{1,9},{9,1},{17,25},{25,17},{2,10},{10... | collective-permute-start | bytes 98312 | tf_op jit(solution)/shard_map/ppermute | solution.py:26
  45.5 1.0 %collective-permute-done.16.refs_1_ = bf16[2,64,1024]{2,1,0:T(8,128)(2,1)S(1)} collective-permute-done((bf16[2,64,1024]{2,1,0:T(8,128)(2,1)S(1)}, bf16[2,64,1024]{2,1,0:T(8,128)(2,1)S(1)}, u32[]{:S(2)}, u32[]{:S(2)}) %collective-permute-start.16) | collective-permute-done | bytes 262176 | tf_op jit(solution)/shard_map/ppermute | solution.py:26
  46.5 0.8 %finish_q.1 = (bf16[64,2048]{1,0:T(8,128)(2,1)}, bf16[64,2048]{1,0:T(8,128)(2,1)}, f32[8,128]{1,0:T(8,128)S(1)}) custom-call(s32[1]{0:T(128)} %bitcast.group_ref, bf16[2,64,1024]{2,1,0:T(8,128)(2,1)S(1)} %get-tuple-element.102.refs_0_, bf16[2,64,1024]{2,1,0:T(8,128)(2,1)S(1)} %collective-permute-done.16.refs_1_), custom_call_target="tpu_custom_call" | custom-call | bytes 1052676 | tf_op jit(solution)/shard_map/finish_q/pallas_call | solution.py:41
  47.3 0.6 %collective-permute-done.22.refs_1_ = bf16[64,256]{1,0:T(8,128)(2,1)S(1)} collective-permute-done((bf16[64,256]{1,0:T(8,128)(2,1)S(1)}, bf16[64,256]{1,0:T(8,128)(2,1)S(1)}, u32[]{:S(2)}, u32[]{:S(2)}) %collective-permute-start.22) | collective-permute-done | bytes 32800 | tf_op jit(solution)/shard_map/ppermute | solution.py:26
  47.9 0.6 %finish_kv.1 = (bf16[64,256]{1,0:T(8,128)(2,1)}, bf16[64,256]{1,0:T(8,128)(2,1)}) custom-call(s32[1]{0:T(128)} %bitcast.group_ref, bf16[64,256]{1,0:T(8,128)(2,1)S(1)} %get-tuple-element.111.refs_0_, bf16[64,256]{1,0:T(8,128)(2,1)S(1)} %collective-permute-done.22.refs_1_, f32[8,128]{1,0:T(8,128)S(1)} %get-tuple-element.113.refs_2_), custom_call_target="tpu_custom_call" | custom-call | bytes 135172 | tf_op jit(solution)/shard_map/finish_kv/pallas_call | solution.py:41
  (26 shorter events, 0.2 us)
Async XLA Ops:
  1.4 4.9 %collective-permute-start.1 = (bf16[64,256]{1,0:T(8,128)(2,1)S(1)}, bf16[64,256]{1,0:T(8,128)(2,1)S(1)}, u32[]{:S(2)}, u32[]{:S(2)}) collective-permute-start(bf16[64,256]{1,0:T(8,128)(2,1)S(1)} %pad_maximum_fusion.3), channel_id=1, source_target_pairs={{0,8},{8,0},{16,24},{24,16},{1,9},{9,1},{17,25},{25,17},{2,10},{10... | collective-permute-start | bytes 98312 | tf_op jit(solution)/shard_map/ppermute | solution.py:26
  5.6 7.9 %collective-permute-start = (bf16[2,64,1024]{2,1,0:T(8,128)(2,1)S(1)}, bf16[2,64,1024]{2,1,0:T(8,128)(2,1)S(1)}, u32[]{:S(2)}, u32[]{:S(2)}) collective-permute-start(bf16[2,64,1024]{2,1,0:T(8,128)(2,1)S(1)} %pad_maximum_fusion.1), channel_id=1, source_target_pairs={{0,8},{8,0},{16,24},{24,16},{1,9},{9,1},{17,25},{25,17},{2,10},{10... | collective-permute-start | bytes 786440 | tf_op jit(solution)/shard_map/ppermute | solution.py:26
  6.3 4.8 %collective-permute-start.4 = (bf16[2,64,256]{2,1,0:T(8,128)(2,1)S(1)}, bf16[2,64,256]{2,1,0:T(8,128)(2,1)S(1)}, u32[]{:S(2)}, u32[]{:S(2)}) collective-permute-start(bf16[2,64,256]{2,1,0:T(8,128)(2,1)S(1)} %pad_maximum_fusion.2.refs_0_), channel_id=1, source_target_pairs={{0,2},{1,3},{2,0},{3,1},{4,6},{5,7},{6,4},{7,5},{8,10},{9,11},{10,... | collective-permute-start | bytes 196616 | tf_op jit(solution)/shard_map/ppermute | solution.py:26
  8.5 6.2 %collective-permute-start.3 = (bf16[2,64,256]{2,1,0:T(8,128)(2,1)S(1)}, bf16[2,64,256]{2,1,0:T(8,128)(2,1)S(1)}, u32[]{:S(2)}, u32[]{:S(2)}) collective-permute-start(bf16[2,64,256]{2,1,0:T(8,128)(2,1)S(1)} %pad_maximum_fusion.2.refs_0_), channel_id=1, source_target_pairs={{0,6},{1,7},{2,4},{3,5},{4,2},{5,3},{6,0},{7,1},{8,14},{9,15},{10,... | collective-permute-start | bytes 196616 | tf_op jit(solution)/shard_map/ppermute | solution.py:26
  11.0 5.9 %collective-permute-start.2 = (bf16[2,64,256]{2,1,0:T(8,128)(2,1)S(1)}, bf16[2,64,256]{2,1,0:T(8,128)(2,1)S(1)}, u32[]{:S(2)}, u32[]{:S(2)}) collective-permute-start(bf16[2,64,256]{2,1,0:T(8,128)(2,1)S(1)} %pad_maximum_fusion.2.refs_0_), channel_id=1, source_target_pairs={{0,4},{1,5},{2,6},{3,7},{4,0},{5,1},{6,2},{7,3},{8,12},{9,13},{10,... | collective-permute-start | bytes 196616 | tf_op jit(solution)/shard_map/ppermute | solution.py:26
  11.1 7.9 %collective-permute-start.7 = (bf16[2,2,64,256]{3,2,1,0:T(8,128)(2,1)S(1)}, bf16[2,2,64,256]{3,2,1,0:T(8,128)(2,1)S(1)}, u32[]{:S(2)}, u32[]{:S(2)}) collective-permute-start(bf16[2,2,64,256]{3,2,1,0:T(8,128)(2,1)S(1)} %stack.46.refs_2_.refs_1_), channel_id=1, source_target_pairs={{0,16},{8,24},{16,0},{24,8},{1,17},{9,25},{17,1},{25,9},{2,18},{10... | collective-permute-start | bytes 393224 | tf_op jit(solution)/shard_map/ppermute | solution.py:26
  16.9 5.7 %collective-permute-start.8 = (bf16[2,2,64,256]{3,2,1,0:T(8,128)(2,1)S(1)}, bf16[2,2,64,256]{3,2,1,0:T(8,128)(2,1)S(1)}, u32[]{:S(2)}, u32[]{:S(2)}) collective-permute-start(bf16[2,2,64,256]{3,2,1,0:T(8,128)(2,1)S(1)} %get-tuple-element.67.refs_0_.refs_1_), channel_id=1, source_target_pairs={{0,16},{8,24},{16,0},{24,8},{1,17},{9,25},{17,1},{25,9},{2,18},{10... | collective-permute-start | bytes 393224 | tf_op jit(solution)/shard_map/ppermute | solution.py:26
  18.5 2.1 %collective-permute-start.5 = (bf16[2,2,64,256]{3,2,1,0:T(8,128)(2,1)S(1)}, bf16[2,2,64,256]{3,2,1,0:T(8,128)(2,1)S(1)}, u32[]{:S(2)}, u32[]{:S(2)}) collective-permute-start(bf16[2,2,64,256]{3,2,1,0:T(8,128)(2,1)S(1)} %get-tuple-element.67.refs_0_.refs_1_), channel_id=1, source_target_pairs={{0,1},{1,0},{2,3},{3,2},{4,5},{5,4},{6,7},{7,6},{8,9},{9,8},{10,11... | collective-permute-start | bytes 393224 | tf_op jit(solution)/shard_map/ppermute | solution.py:26
  18.5 2.1 %collective-permute-start.6 = (bf16[2,2,64,256]{3,2,1,0:T(8,128)(2,1)S(1)}, bf16[2,2,64,256]{3,2,1,0:T(8,128)(2,1)S(1)}, u32[]{:S(2)}, u32[]{:S(2)}) collective-permute-start(bf16[2,2,64,256]{3,2,1,0:T(8,128)(2,1)S(1)} %get-tuple-element.68), channel_id=1, source_target_pairs={{0,1},{1,0},{2,3},{3,2},{4,5},{5,4},{6,7},{7,6},{8,9},{9,8},{10,11... | collective-permute-start | bytes 393224 | tf_op jit(solution)/shard_map/ppermute | solution.py:26
  19.0 4.9 %collective-permute-start.10 = (bf16[2,2,64,256]{3,2,1,0:T(8,128)(2,1)S(1)}, bf16[2,2,64,256]{3,2,1,0:T(8,128)(2,1)S(1)}, u32[]{:S(2)}, u32[]{:S(2)}) collective-permute-start(bf16[2,2,64,256]{3,2,1,0:T(8,128)(2,1)S(1)} %collective-permute-done.7.refs_0_), channel_id=1, source_target_pairs={{0,1},{1,0},{2,3},{3,2},{4,5},{5,4},{6,7},{7,6},{8,9},{9,8},{10,11... | collective-permute-start | bytes 393224 | tf_op jit(solution)/shard_map/ppermute | solution.py:26
  22.6 1.5 %collective-permute-start.9 = (bf16[2,2,64,256]{3,2,1,0:T(8,128)(2,1)S(1)}, bf16[2,2,64,256]{3,2,1,0:T(8,128)(2,1)S(1)}, u32[]{:S(2)}, u32[]{:S(2)}) collective-permute-start(bf16[2,2,64,256]{3,2,1,0:T(8,128)(2,1)S(1)} %collective-permute-done.8.refs_0_), channel_id=1, source_target_pairs={{0,1},{1,0},{2,3},{3,2},{4,5},{5,4},{6,7},{7,6},{8,9},{9,8},{10,11... | collective-permute-start | bytes 393224 | tf_op jit(solution)/shard_map/ppermute | solution.py:26
  26.8 1.9 %collective-permute-start.12 = (bf16[2,2,64,256]{3,2,1,0:T(8,128)(2,1)S(1)}, bf16[2,2,64,256]{3,2,1,0:T(8,128)(2,1)S(1)}, u32[]{:S(2)}, u32[]{:S(2)}) collective-permute-start(bf16[2,2,64,256]{3,2,1,0:T(8,128)(2,1)S(1)} %get-tuple-element.92), channel_id=1, source_target_pairs={{0,1},{1,0},{2,3},{3,2},{4,5},{5,4},{6,7},{7,6},{8,9},{9,8},{10,11... | collective-permute-start | bytes 393224 | tf_op jit(solution)/shard_map/ppermute | solution.py:26
  27.2 1.5 %collective-permute-start.11 = (bf16[2,2,64,256]{3,2,1,0:T(8,128)(2,1)S(1)}, bf16[2,2,64,256]{3,2,1,0:T(8,128)(2,1)S(1)}, u32[]{:S(2)}, u32[]{:S(2)}) collective-permute-start(bf16[2,2,64,256]{3,2,1,0:T(8,128)(2,1)S(1)} %get-tuple-element.90), channel_id=1, source_target_pairs={{0,1},{1,0},{2,3},{3,2},{4,5},{5,4},{6,7},{7,6},{8,9},{9,8},{10,11... | collective-permute-start | bytes 393224 | tf_op jit(solution)/shard_map/ppermute | solution.py:26
  28.8 1.3 %collective-permute-start.13 = (bf16[64,128]{1,0:T(8,128)(2,1)S(1)}, bf16[64,128]{1,0:T(8,128)(2,1)S(1)}, u32[]{:S(2)}, u32[]{:S(2)}) collective-permute-start(bf16[64,128]{1,0:T(8,128)(2,1)S(1)} %slice_bitcast_fusion), channel_id=1, source_target_pairs={{0,1},{1,0},{2,3},{3,2},{4,5},{5,4},{6,7},{7,6},{8,9},{9,8},{10,11... | collective-permute-start | bytes 49160 | tf_op jit(solution)/shard_map/ppermute | solution.py:26
  29.2 5.9 %collective-permute-start.17 = (bf16[2,2,64,256]{3,2,1,0:T(8,128)(2,1)S(1)}, bf16[2,2,64,256]{3,2,1,0:T(8,128)(2,1)S(1)}, u32[]{:S(2)}, u32[]{:S(2)}) collective-permute-start(bf16[2,2,64,256]{3,2,1,0:T(8,128)(2,1)S(1)} %sum_cores.3), channel_id=1, source_target_pairs={{0,16},{8,24},{16,0},{24,8},{1,17},{9,25},{17,1},{25,9},{2,18},{10... | collective-permute-start | bytes 393224 | tf_op jit(solution)/shard_map/ppermute | solution.py:26
  31.2 3.9 %collective-permute-start.18 = (bf16[2,2,64,256]{3,2,1,0:T(8,128)(2,1)S(1)}, bf16[2,2,64,256]{3,2,1,0:T(8,128)(2,1)S(1)}, u32[]{:S(2)}, u32[]{:S(2)}) collective-permute-start(bf16[2,2,64,256]{3,2,1,0:T(8,128)(2,1)S(1)} %get-tuple-element.106), channel_id=1, source_target_pairs={{0,1},{1,0},{2,3},{3,2},{4,5},{5,4},{6,7},{7,6},{8,9},{9,8},{10,11... | collective-permute-start | bytes 393224 | tf_op jit(solution)/shard_map/ppermute | solution.py:26
  31.6 6.5 %collective-permute-start.14 = (bf16[2,2,64,256]{3,2,1,0:T(8,128)(2,1)S(1)}, bf16[2,2,64,256]{3,2,1,0:T(8,128)(2,1)S(1)}, u32[]{:S(2)}, u32[]{:S(2)}) collective-permute-start(bf16[2,2,64,256]{3,2,1,0:T(8,128)(2,1)S(1)} %sum_cores.2), channel_id=1, source_target_pairs={{0,16},{8,24},{16,0},{24,8},{1,17},{9,25},{17,1},{25,9},{2,18},{10... | collective-permute-start | bytes 393224 | tf_op jit(solution)/shard_map/ppermute | solution.py:26
  32.6 5.5 %collective-permute-start.15 = (bf16[2,2,64,256]{3,2,1,0:T(8,128)(2,1)S(1)}, bf16[2,2,64,256]{3,2,1,0:T(8,128)(2,1)S(1)}, u32[]{:S(2)}, u32[]{:S(2)}) collective-permute-start(bf16[2,2,64,256]{3,2,1,0:T(8,128)(2,1)S(1)} %get-tuple-element.99), channel_id=1, source_target_pairs={{0,1},{1,0},{2,3},{3,2},{4,5},{5,4},{6,7},{7,6},{8,9},{9,8},{10,11... | collective-permute-start | bytes 393224 | tf_op jit(solution)/shard_map/ppermute | solution.py:26
  35.1 7.9 %collective-permute-start.19 = (bf16[2,64,256]{2,1,0:T(8,128)(2,1)S(1)}, bf16[2,64,256]{2,1,0:T(8,128)(2,1)S(1)}, u32[]{:S(2)}, u32[]{:S(2)}) collective-permute-start(bf16[2,64,256]{2,1,0:T(8,128)(2,1)S(1)} %get-tuple-element.108), channel_id=1, source_target_pairs={{0,4},{1,5},{2,6},{3,7},{4,0},{5,1},{6,2},{7,3},{8,12},{9,13},{10,... | collective-permute-start | bytes 196616 | tf_op jit(solution)/shard_map/ppermute | solution.py:26
  36.2 6.9 %collective-permute-start.20 = (bf16[2,64,256]{2,1,0:T(8,128)(2,1)S(1)}, bf16[2,64,256]{2,1,0:T(8,128)(2,1)S(1)}, u32[]{:S(2)}, u32[]{:S(2)}) collective-permute-start(bf16[2,64,256]{2,1,0:T(8,128)(2,1)S(1)} %get-tuple-element.109), channel_id=1, source_target_pairs={{0,6},{1,7},{2,4},{3,5},{4,2},{5,3},{6,0},{7,1},{8,14},{9,15},{10,... | collective-permute-start | bytes 196616 | tf_op jit(solution)/shard_map/ppermute | solution.py:26
  38.2 5.7 %collective-permute-start.21 = (bf16[2,64,256]{2,1,0:T(8,128)(2,1)S(1)}, bf16[2,64,256]{2,1,0:T(8,128)(2,1)S(1)}, u32[]{:S(2)}, u32[]{:S(2)}) collective-permute-start(bf16[2,64,256]{2,1,0:T(8,128)(2,1)S(1)} %get-tuple-element.110), channel_id=1, source_target_pairs={{0,2},{1,3},{2,0},{3,1},{4,6},{5,7},{6,4},{7,5},{8,10},{9,11},{10,... | collective-permute-start | bytes 196616 | tf_op jit(solution)/shard_map/ppermute | solution.py:26
  38.9 7.6 %collective-permute-start.16 = (bf16[2,64,1024]{2,1,0:T(8,128)(2,1)S(1)}, bf16[2,64,1024]{2,1,0:T(8,128)(2,1)S(1)}, u32[]{:S(2)}, u32[]{:S(2)}) collective-permute-start(bf16[2,64,1024]{2,1,0:T(8,128)(2,1)S(1)} %get-tuple-element.103), channel_id=1, source_target_pairs={{0,8},{8,0},{16,24},{24,16},{1,9},{9,1},{17,25},{25,17},{2,10},{10... | collective-permute-start | bytes 786440 | tf_op jit(solution)/shard_map/ppermute | solution.py:26
  43.9 4.0 %collective-permute-start.22 = (bf16[64,256]{1,0:T(8,128)(2,1)S(1)}, bf16[64,256]{1,0:T(8,128)(2,1)S(1)}, u32[]{:S(2)}, u32[]{:S(2)}) collective-permute-start(bf16[64,256]{1,0:T(8,128)(2,1)S(1)} %get-tuple-element.112), channel_id=1, source_target_pairs={{0,8},{8,0},{16,24},{24,16},{1,9},{9,1},{17,25},{25,17},{2,10},{10... | collective-permute-start | bytes 98312 | tf_op jit(solution)/shard_map/ppermute | solution.py:26

commit v16 on v15

--- a/solution.py
+++ b/solution.py
@@ -185,8 +185,16 @@
         mix_ref[:, at] = mixed
 
 
-def turn_kernel(plan, chunks, info_ref, *refs):
-    q_parts, (q_all, do_all, q_t, do_t, gap_ref, first_ref) = refs[:-6], refs[-6:]
+def place_kernel(plan, chunks, info_ref, gap_ref, first_ref):
+    for tile in range(len(plan.tiles)):
+        gap_ref[pl.ds(tile * plan.block_rows, plan.block_rows), :] = plan.gap(tile, info_ref)
+    for chunk in chunks:
+        for j, first in enumerate(plan.firsts(chunk, info_ref)):
+            first_ref[pl.ds(plan.first_at(chunk) + j, 1), :] = jnp.full((1, plan.lanes), first, jnp.int32)
+
+
+def turn_kernel(plan, *refs):
+    q_parts, (q_all, do_all, q_t, do_t) = refs[:-4], refs[-4:]
     for tile, (s, start) in enumerate(plan.tiles):
         span = pl.ds(start, plan.tile_rows)
         for n in range(plan.group):
@@ -196,10 +204,6 @@
         at = plan.at(tile)
         q_t[:, at] = q_all[at, :].T
         do_t[:, at] = do_all[at, :].T
-        gap_ref[pl.ds(tile * plan.block_rows, plan.block_rows), :] = plan.gap(tile, info_ref)
-    for chunk in chunks:
-        for j, first in enumerate(plan.firsts(chunk, info_ref)):
-            first_ref[pl.ds(plan.first_at(chunk) + j, 1), :] = jnp.full((1, plan.lanes), first, jnp.int32)
 
 
 def part_kernel(plan, chunks, gap_ref, first_ref, q_t, *refs):
@@ -394,17 +398,18 @@
     pieces = [piece] + pieces[::-1]
     query_rows = plan.query_rows
     chunks = [(a, core, p) for a in range(spans) for core in range(cores) for p in range(parts)]
-    q_all, do_all, q_t, do_t, gap, firsts = call(
-        functools.partial(turn_kernel, plan, chunks),
+    gap, firsts = call(
+        functools.partial(place_kernel, plan, chunks),
+        "place",
+        (info,),
+        [i32(len(plan.tiles) * block_rows, plan.lanes), i32(len(chunks) * plan.slices, plan.lanes)],
+        [SMEM],
+    )
+    q_all, do_all, q_t, do_t = call(
+        functools.partial(turn_kernel, plan),
         "turn",
-        (info, *q_parts),
-        [
-            *[bf(query_rows, HD)] * 2,
-            *[bf(HD, query_rows)] * 2,
-            i32(len(plan.tiles) * block_rows, plan.lanes),
-            i32(len(chunks) * plan.slices, plan.lanes),
-        ],
-        [SMEM] + [VMEM] * kv,
+        q_parts,
+        [bf(query_rows, HD)] * 2 + [bf(HD, query_rows)] * 2,
     )
     column, handed, order = [None] * parts, [None] * parts, []
     for p in reversed(range(parts)):
@@ -419,7 +424,7 @@
         handed[p] = column[p]
         if extra:
             handed[p + 1] = handed_on[0]
-        order = list(after(q_parts[1:], [info])) if p else []
+        order = [*q_parts[1:], firsts] if p else []
     columns = [[swap(half, "head", a * kv) for half in column] for a in range(1, spans)]
     near_kv = [column] + [[swap(half, "ctx", core) for half in handed] for core in range(1, cores)]
     near_flat = [half for pair in near_kv for half in pair]

time: 48.8 us -> 48.2 us (0.988)
  waiting for transfers between devices: 10.8 us -> 9.68 us
    ppermute x23, waiting for transfers between devices: 10.8 us -> 9.68 us  [swap(): return lax.ppermute(block, axis, [(i, i ^ mask) for i in range(size)])]
    pallas_call x19 -> x20, Pallas kernels: 12.2 us -> 12.3 us  [call(): pl.pallas_call(kernel, out_shape=list(outs), in_specs=specs or [VMEM] * l...]
  transfers between devices with their start and end apart: 23 -> 23, of which waited for: 10 -> 9; matrix products, arithmetic and copies ran while one was open for 4% -> 4% of each run, Pallas kernels for 18% -> 19%
where the time goes in v16:
time: 48.2 us; the launch traced here: 48 us
  starting transfers between devices  22.4 us (46%)
  Pallas kernels  12.3 us (26%)
  waiting for transfers between devices  9.68 us (20%)
  other arithmetic  2.71 us (6%)
  between operations  0.87 us (2%)
    ppermute x23, starting transfers between devices, swap(): return lax.ppermute(block, axis, [(i, i ^ mask) for i in range(size)])  22.4 us
    pallas_call x20, Pallas kernels, call(): pl.pallas_call(kernel, out_shape=list(outs), in_specs=specs or [VMEM] * l...  12.3 us
    ppermute x23, waiting for transfers between devices, swap(): return lax.ppermute(block, axis, [(i, i ^ mask) for i in range(size)])  9.68 us
    another operation x3, other arithmetic, queries_of(): return jnp.stack([pick(queries, g, width), pick(out_grad, g, width)])  1.18 us
  transfers between devices with their start and end apart: 23, of which 9 were waited for; matrix products, arithmetic and copies ran while one was open for 4% of the time, Pallas kernels for 19%

profile of v16, /device:TPU:0, one launch (start us, length us, event | category | flops | bytes accessed | tf_op | source)
XLA Modules:
  0.0 48.0 jit_solution(15053912763032759623)
XLA Ops:
  0.6 0.8 %broadcast_select_fusion.2 = (bf16[64,128]{1,0:T(8,128)(2,1)S(1)}, bf16[64,128]{1,0:T(8,128)(2,1)S(1)}, bf16[64,128]{1,0:T(8,128)(2,1)S(1)}, bf16[64,128]{1,0:T(8,128)(2,1)S(1)}) fusion(pred[]{:T(512)S(6)} %eq.18, bf16[64,256]{1,0:T(8,128)(2,1)} %bitcast.26, pred[]{:T(512)S(6)} %eq.19, bf16[64,256]{1,0:T(8,128)(2,1)} %bitcast.27), kind=kLoop, calls=%fused_computation.12 | loop fusion | flops 32768 | bytes 131074 | tf_op jit(solution)/shard_map/jit(_where)/select_n | solution.py:386
  1.4 3.0 %collective-permute-start.1 = (bf16[64,256]{1,0:T(8,128)(2,1)S(1)}, bf16[64,256]{1,0:T(8,128)(2,1)S(1)}, u32[]{:S(2)}, u32[]{:S(2)}) collective-permute-start(bf16[64,256]{1,0:T(8,128)(2,1)S(1)} %pad_maximum_fusion.3), channel_id=1, source_target_pairs={{0,8},{8,0},{16,24},{24,16},{1,9},{9,1},{17,25},{25,17},{2,10},{10... | collective-permute-start | bytes 98312 | tf_op jit(solution)/shard_map/ppermute | solution.py:26
  4.4 1.1 %select_bitcast_fusion = (bf16[1,64,1024]{2,1,0:T(8,128)(2,1)S(1)}, bf16[1,64,1024]{2,1,0:T(8,128)(2,1)S(1)}, bf16[1,64,1024]{2,1,0:T(8,128)(2,1)S(1)}, bf16[1,64,1024]{2,1,0:T(8,128)(2,1)S(1)}) fusion(pred[]{:T(512)S(6)} %eq.19, bf16[64,2048]{1,0:T(8,128)(2,1)} %bitcast.24, pred[]{:T(512)S(6)} %eq.18, bf16[64,2048]{1,0:T(8,128)(2,1)} %bitcast.25), kind=kLoop, calls=%fused_computation.2 | loop fusion | flops 262144 | bytes 1048578 | tf_op jit(solution)/shard_map/stack | solution.py:393
  5.6 0.1 collective-permute-start
  5.7 0.6 %collective-permute-done.1 = bf16[64,256]{1,0:T(8,128)(2,1)S(1)} collective-permute-done((bf16[64,256]{1,0:T(8,128)(2,1)S(1)}, bf16[64,256]{1,0:T(8,128)(2,1)S(1)}, u32[]{:S(2)}, u32[]{:S(2)}) %collective-permute-start.1) | collective-permute-done | bytes 32800 | tf_op jit(solution)/shard_map/ppermute | solution.py:26
  6.3 2.2 %collective-permute-start.4 = (bf16[2,64,256]{2,1,0:T(8,128)(2,1)S(1)}, bf16[2,64,256]{2,1,0:T(8,128)(2,1)S(1)}, u32[]{:S(2)}, u32[]{:S(2)}) collective-permute-start(bf16[2,64,256]{2,1,0:T(8,128)(2,1)S(1)} %pad_maximum_fusion.2.refs_0_), channel_id=1, source_target_pairs={{0,2},{1,3},{2,0},{3,1},{4,6},{5,7},{6,4},{7,5},{8,10},{9,11},{10,... | collective-permute-start | bytes 196616 | tf_op jit(solution)/shard_map/ppermute | solution.py:26
  8.5 2.5 %collective-permute-start.3 = (bf16[2,64,256]{2,1,0:T(8,128)(2,1)S(1)}, bf16[2,64,256]{2,1,0:T(8,128)(2,1)S(1)}, u32[]{:S(2)}, u32[]{:S(2)}) collective-permute-start(bf16[2,64,256]{2,1,0:T(8,128)(2,1)S(1)} %pad_maximum_fusion.2.refs_0_), channel_id=1, source_target_pairs={{0,6},{1,7},{2,4},{3,5},{4,2},{5,3},{6,0},{7,1},{8,14},{9,15},{10,... | collective-permute-start | bytes 196616 | tf_op jit(solution)/shard_map/ppermute | solution.py:26
  11.0 0.1 collective-permute-start.2
  11.1 1.7 %collective-permute-start.7 = (bf16[2,2,64,256]{3,2,1,0:T(8,128)(2,1)S(1)}, bf16[2,2,64,256]{3,2,1,0:T(8,128)(2,1)S(1)}, u32[]{:S(2)}, u32[]{:S(2)}) collective-permute-start(bf16[2,2,64,256]{3,2,1,0:T(8,128)(2,1)S(1)} %stack.46.refs_2_.refs_1_), channel_id=1, source_target_pairs={{0,16},{8,24},{16,0},{24,8},{1,17},{9,25},{17,1},{25,9},{2,18},{10... | collective-permute-start | bytes 393224 | tf_op jit(solution)/shard_map/ppermute | solution.py:26
  12.8 0.7 %pad_add_fusion.info_ref = s32[18]{0:T(128)S(1)} fusion(s32[16]{0:T(128)} %param.9, s32[1]{0:T(128)} %bitcast.8, s32[1]{0:T(128)} %bitcast.7), kind=kLoop, calls=%fused_computation.14 | loop fusion | flops 36 | bytes 144 | tf_op jit(solution)/shard_map/concatenate | solution.py:362
  13.5 0.6 %place.1 = (s32[128,256]{1,0:T(8,128)S(1)}, s32[64,256]{1,0:T(8,128)S(1)}) custom-call(s32[18]{0:T(128)S(1)} %pad_add_fusion.info_ref), custom_call_target="tpu_custom_call" | custom-call | bytes 196680 | tf_op jit(solution)/shard_map/place/pallas_call | solution.py:41
  14.2 0.6 %collective-permute-done.3.refs_1_ = bf16[2,64,256]{2,1,0:T(8,128)(2,1)S(1)} collective-permute-done((bf16[2,64,256]{2,1,0:T(8,128)(2,1)S(1)}, bf16[2,64,256]{2,1,0:T(8,128)(2,1)S(1)}, u32[]{:S(2)}, u32[]{:S(2)}) %collective-permute-start.3) | collective-permute-done | bytes 65568 | tf_op jit(solution)/shard_map/ppermute | solution.py:26
  14.7 2.1 %collective-permute-done.2.refs_0_ = bf16[2,64,256]{2,1,0:T(8,128)(2,1)S(1)} collective-permute-done((bf16[2,64,256]{2,1,0:T(8,128)(2,1)S(1)}, bf16[2,64,256]{2,1,0:T(8,128)(2,1)S(1)}, u32[]{:S(2)}, u32[]{:S(2)}) %collective-permute-start.2) | collective-permute-done | bytes 65568 | tf_op jit(solution)/shard_map/ppermute | solution.py:26
  16.9 1.6 %collective-permute-start.8 = (bf16[2,2,64,256]{3,2,1,0:T(8,128)(2,1)S(1)}, bf16[2,2,64,256]{3,2,1,0:T(8,128)(2,1)S(1)}, u32[]{:S(2)}, u32[]{:S(2)}) collective-permute-start(bf16[2,2,64,256]{3,2,1,0:T(8,128)(2,1)S(1)} %get-tuple-element.65.refs_0_.refs_1_), channel_id=1, source_target_pairs={{0,16},{8,24},{16,0},{24,8},{1,17},{9,25},{17,1},{25,9},{2,18},{10... | collective-permute-start | bytes 393224 | tf_op jit(solution)/shard_map/ppermute | solution.py:26
  18.5 0.5 %collective-permute-start.6 = (bf16[2,2,64,256]{3,2,1,0:T(8,128)(2,1)S(1)}, bf16[2,2,64,256]{3,2,1,0:T(8,128)(2,1)S(1)}, u32[]{:S(2)}, u32[]{:S(2)}) collective-permute-start(bf16[2,2,64,256]{3,2,1,0:T(8,128)(2,1)S(1)} %get-tuple-element.66), channel_id=1, source_target_pairs={{0,1},{1,0},{2,3},{3,2},{4,5},{5,4},{6,7},{7,6},{8,9},{9,8},{10,11... | collective-permute-start | bytes 393224 | tf_op jit(solution)/shard_map/ppermute | solution.py:26
  19.0 0.1 collective-permute-start.10
  19.1 0.2 turn.1
  19.3 0.7 %attend_mid.2 = (f32[256,1024]{1,0:T(8,128)S(1)}, f32[1,1024]{1,0:T(1,128)S(1)}, f32[1,1024]{1,0:T(1,128)S(1)}, f32[128,1024]{1,0:T(8,128)S(1)}) custom-call(s32[128,256]{1,0:T(8,128)S(1)} %get-tuple-element.62.gap_ref, s32[64,256]{1,0:T(8,128)S(1)} %get-tuple-element.63.refs_4_.first_ref, bf16[128,1024]{1,0:T(8,128)(2,1)S(1)} %get-tuple-element.64.q_t, ...), custom_call_target="tpu_custom_call" | custom-call | flops 268435456 | bytes 2170880 | tf_op jit(solution)/shard_map/attend_mid/pallas_call | solution.py:41
  20.1 2.0 %attend_near.1 = (f32[1024,1024]{1,0:T(8,128)S(1)}, f32[1,1024]{1,0:T(1,128)S(1)}, f32[1,1024]{1,0:T(1,128)S(1)}, f32[128,1024]{1,0:T(8,128)S(1)}) custom-call(s32[128,256]{1,0:T(8,128)S(1)} %get-tuple-element.62.gap_ref, s32[64,256]{1,0:T(8,128)S(1)} %get-tuple-element.63.refs_4_.first_ref, bf16[128,1024]{1,0:T(8,128)(2,1)S(1)} %get-tuple-element.64.q_t, ...), custom_call_target="tpu_custom_call" | custom-call | flops 1073741824 | bytes 5713920 | tf_op jit(solution)/shard_map/attend_near/pallas_call | solution.py:41
  22.1 0.6 %collective-permute-start.9 = (bf16[2,2,64,256]{3,2,1,0:T(8,128)(2,1)S(1)}, bf16[2,2,64,256]{3,2,1,0:T(8,128)(2,1)S(1)}, u32[]{:S(2)}, u32[]{:S(2)}) collective-permute-start(bf16[2,2,64,256]{3,2,1,0:T(8,128)(2,1)S(1)} %collective-permute-done.8.refs_0_), channel_id=1, source_target_pairs={{0,1},{1,0},{2,3},{3,2},{4,5},{5,4},{6,7},{7,6},{8,9},{9,8},{10,11... | collective-permute-start | bytes 393224 | tf_op jit(solution)/shard_map/ppermute | solution.py:26
  22.6 0.7 %attend_mid.3 = (f32[256,1024]{1,0:T(8,128)S(1)}, f32[1,1024]{1,0:T(1,128)S(1)}, f32[1,1024]{1,0:T(1,128)S(1)}, f32[128,1024]{1,0:T(8,128)S(1)}) custom-call(s32[128,256]{1,0:T(8,128)S(1)} %get-tuple-element.62.gap_ref, s32[64,256]{1,0:T(8,128)S(1)} %get-tuple-element.63.refs_4_.first_ref, bf16[128,1024]{1,0:T(8,128)(2,1)S(1)} %get-tuple-element.64.q_t, ...), custom_call_target="tpu_custom_call" | custom-call | flops 268435456 | bytes 2174976 | tf_op jit(solution)/shard_map/attend_mid/pallas_call | solution.py:41
  23.4 0.2 collective-permute-done.9.refs_9_
  23.6 2.6 %attend_far.1 = (f32[1,1024]{1,0:T(1,128)S(1)}, f32[1,1024]{1,0:T(1,128)S(1)}, f32[1,1024]{1,0:T(1,128)S(1)}, f32[1,1024]{1,0:T(1,128)S(1)}, bf16[128,1024]{1,0:...) custom-call(s32[128,256]{1,0:T(8,128)S(1)} %get-tuple-element.62.gap, ...), custom_call_target="tpu_custom_call" | custom-call | flops 1073741824 | bytes 4169728 | tf_op jit(solution)/shard_map/attend_far/pallas_call | solution.py:41
  26.3 0.4 collective-permute-start.12
  26.7 0.1 collective-permute-start.11
  26.8 0.6 %attend_back.4 = (f32[128,1024]{1,0:T(8,128)S(1)}, bf16[2,2,64,256]{3,2,1,0:T(8,128)(2,1)S(1)}) custom-call(bf16[1024,128]{1,0:T(8,128)(2,1)S(1)} %get-tuple-element.59.q_all, bf16[1024,128]{1,0:T(8,128)(2,1)S(1)} %get-tuple-element.60.do_all, bf16[128,1024]{1,0:T(8,128)(2,1)S(1)} %get-tuple-element.61.do_t, f32[256,1024]{1,0:T(8,128)S(1)} %get-tuple-element.82.e_ref, ...), custom_call_target="tpu_custom_call" | custom-call | flops 402653184 | bytes 3153920 | tf_op jit(solution)/shard_map/attend_back/pallas_call | solution.py:41
  27.5 0.7 %attend_back.5 = (f32[128,1024]{1,0:T(8,128)S(1)}, bf16[2,2,64,256]{3,2,1,0:T(8,128)(2,1)S(1)}) custom-call(bf16[1024,128]{1,0:T(8,128)(2,1)S(1)} %get-tuple-element.59.q_all, bf16[1024,128]{1,0:T(8,128)(2,1)S(1)} %get-tuple-element.60.do_all, bf16[128,1024]{1,0:T(8,128)(2,1)S(1)} %get-tuple-element.61.do_t, f32[256,1024]{1,0:T(8,128)S(1)} %get-tuple-element.80.e_ref, ...), custom_call_target="tpu_custom_call" | custom-call | flops 402653184 | bytes 3153920 | tf_op jit(solution)/shard_map/attend_back/pallas_call | solution.py:41
  28.3 0.4 collective-permute-start.13
  28.7 1.0 %collective-permute-start.17 = (bf16[2,2,64,256]{3,2,1,0:T(8,128)(2,1)S(1)}, bf16[2,2,64,256]{3,2,1,0:T(8,128)(2,1)S(1)}, u32[]{:S(2)}, u32[]{:S(2)}) collective-permute-start(bf16[2,2,64,256]{3,2,1,0:T(8,128)(2,1)S(1)} %sum_cores.3), channel_id=1, source_target_pairs={{0,16},{8,24},{16,0},{24,8},{1,17},{9,25},{17,1},{25,9},{2,18},{10... | collective-permute-start | bytes 393224 | tf_op jit(solution)/shard_map/ppermute | solution.py:26
  29.7 1.2 %attend_back.6 = (f32[128,1024]{1,0:T(8,128)S(1)}, bf16[2,2,64,256]{3,2,1,0:T(8,128)(2,1)S(1)}, bf16[2,2,64,256]{3,2,1,0:T(8,128)(2,1)S(1)}) custom-call(bf16[1024,128]{1,0:T(8,128)(2,1)S(1)} %get-tuple-element.59.q_all, bf16[1024,128]{1,0:T(8,128)(2,1)S(1)} %get-tuple-element.60.do_all, bf16[128,1024]{1,0:T(8,128)(2,1)S(1)} %get-tuple-element.61.do_t, ...), custom_call_target="tpu_custom_call" | custom-call | flops 805306368 | bytes 6578176 | tf_op jit(solution)/shard_map/attend_back/pallas_call | solution.py:41
  30.8 0.3 collective-permute-start.18
  31.1 1.0 %collective-permute-start.14 = (bf16[2,2,64,256]{3,2,1,0:T(8,128)(2,1)S(1)}, bf16[2,2,64,256]{3,2,1,0:T(8,128)(2,1)S(1)}, u32[]{:S(2)}, u32[]{:S(2)}) collective-permute-start(bf16[2,2,64,256]{3,2,1,0:T(8,128)(2,1)S(1)} %sum_cores.2), channel_id=1, source_target_pairs={{0,16},{8,24},{16,0},{24,8},{1,17},{9,25},{17,1},{25,9},{2,18},{10... | collective-permute-start | bytes 393224 | tf_op jit(solution)/shard_map/ppermute | solution.py:26
  32.1 0.1 collective-permute-start.15
  32.2 1.2 %attend_back.7 = (bf16[2,64,1024]{2,1,0:T(8,128)(2,1)S(1)}, bf16[2,64,1024]{2,1,0:T(8,128)(2,1)S(1)}, bf16[2,2,64,256]{3,2,1,0:T(8,128)(2,1)S(1)}, bf16[2,2,64,256]{3,2,1,0:T(8,128)(2,1)S(1)}) custom-call(bf16[1024,128]{1,0:T(8,128)(2,1)S(1)} %get-tuple-element.59.q_all, bf16[1024,128]{1,0:T(8,128)(2,1)S(1)} %get-tuple-element.60.do_all, ...), custom_call_target="tpu_custom_call" | custom-call | flops 805306368 | bytes 6840320 | tf_op jit(solution)/shard_map/attend_back/pallas_call | solution.py:41
  33.4 1.0 %collective-permute-done.17.refs_0_ = bf16[2,2,64,256]{3,2,1,0:T(8,128)(2,1)S(1)} collective-permute-done((bf16[2,2,64,256]{3,2,1,0:T(8,128)(2,1)S(1)}, bf16[2,2,64,256]{3,2,1,0:T(8,128)(2,1)S(1)}, u32[]{:S(2)}, u32[]{:S(2)}) %collective-permute-start.17) | collective-permute-done | bytes 131104 | tf_op jit(solution)/shard_map/ppermute | solution.py:26
  34.4 0.1 sum_heads.3
  34.5 1.2 %collective-permute-start.19 = (bf16[2,64,256]{2,1,0:T(8,128)(2,1)S(1)}, bf16[2,64,256]{2,1,0:T(8,128)(2,1)S(1)}, u32[]{:S(2)}, u32[]{:S(2)}) collective-permute-start(bf16[2,64,256]{2,1,0:T(8,128)(2,1)S(1)} %get-tuple-element.106), channel_id=1, source_target_pairs={{0,4},{1,5},{2,6},{3,7},{4,0},{5,1},{6,2},{7,3},{8,12},{9,13},{10,... | collective-permute-start | bytes 196616 | tf_op jit(solution)/shard_map/ppermute | solution.py:26
  35.7 1.9 %collective-permute-start.20 = (bf16[2,64,256]{2,1,0:T(8,128)(2,1)S(1)}, bf16[2,64,256]{2,1,0:T(8,128)(2,1)S(1)}, u32[]{:S(2)}, u32[]{:S(2)}) collective-permute-start(bf16[2,64,256]{2,1,0:T(8,128)(2,1)S(1)} %get-tuple-element.107), channel_id=1, source_target_pairs={{0,6},{1,7},{2,4},{3,5},{4,2},{5,3},{6,0},{7,1},{8,14},{9,15},{10,... | collective-permute-start | bytes 196616 | tf_op jit(solution)/shard_map/ppermute | solution.py:26
  37.6 0.1 sum_heads.2
  37.6 0.7 %collective-permute-start.21 = (bf16[2,64,256]{2,1,0:T(8,128)(2,1)S(1)}, bf16[2,64,256]{2,1,0:T(8,128)(2,1)S(1)}, u32[]{:S(2)}, u32[]{:S(2)}) collective-permute-start(bf16[2,64,256]{2,1,0:T(8,128)(2,1)S(1)} %get-tuple-element.108), channel_id=1, source_target_pairs={{0,2},{1,3},{2,0},{3,1},{4,6},{5,7},{6,4},{7,5},{8,10},{9,11},{10,... | collective-permute-start | bytes 196616 | tf_op jit(solution)/shard_map/ppermute | solution.py:26
  38.3 1.5 %collective-permute-start.16 = (bf16[2,64,1024]{2,1,0:T(8,128)(2,1)S(1)}, bf16[2,64,1024]{2,1,0:T(8,128)(2,1)S(1)}, u32[]{:S(2)}, u32[]{:S(2)}) collective-permute-start(bf16[2,64,1024]{2,1,0:T(8,128)(2,1)S(1)} %get-tuple-element.101), channel_id=1, source_target_pairs={{0,8},{8,0},{16,24},{24,16},{1,9},{9,1},{17,25},{25,17},{2,10},{10... | collective-permute-start | bytes 786440 | tf_op jit(solution)/shard_map/ppermute | solution.py:26
  39.8 2.7 %collective-permute-done.19.refs_0_ = bf16[2,64,256]{2,1,0:T(8,128)(2,1)S(1)} collective-permute-done((bf16[2,64,256]{2,1,0:T(8,128)(2,1)S(1)}, bf16[2,64,256]{2,1,0:T(8,128)(2,1)S(1)}, u32[]{:S(2)}, u32[]{:S(2)}) %collective-permute-start.19) | collective-permute-done | bytes 65568 | tf_op jit(solution)/shard_map/ppermute | solution.py:26
  42.5 0.8 %collective-permute-done.21.refs_2_ = bf16[2,64,256]{2,1,0:T(8,128)(2,1)S(1)} collective-permute-done((bf16[2,64,256]{2,1,0:T(8,128)(2,1)S(1)}, bf16[2,64,256]{2,1,0:T(8,128)(2,1)S(1)}, u32[]{:S(2)}, u32[]{:S(2)}) %collective-permute-start.21) | collective-permute-done | bytes 65568 | tf_op jit(solution)/shard_map/ppermute | solution.py:26
  43.3 1.6 %collective-permute-start.22 = (bf16[64,256]{1,0:T(8,128)(2,1)S(1)}, bf16[64,256]{1,0:T(8,128)(2,1)S(1)}, u32[]{:S(2)}, u32[]{:S(2)}) collective-permute-start(bf16[64,256]{1,0:T(8,128)(2,1)S(1)} %get-tuple-element.110), channel_id=1, source_target_pairs={{0,8},{8,0},{16,24},{24,16},{1,9},{9,1},{17,25},{25,17},{2,10},{10... | collective-permute-start | bytes 98312 | tf_op jit(solution)/shard_map/ppermute | solution.py:26
  44.9 1.0 %collective-permute-done.16.refs_1_ = bf16[2,64,1024]{2,1,0:T(8,128)(2,1)S(1)} collective-permute-done((bf16[2,64,1024]{2,1,0:T(8,128)(2,1)S(1)}, bf16[2,64,1024]{2,1,0:T(8,128)(2,1)S(1)}, u32[]{:S(2)}, u32[]{:S(2)}) %collective-permute-start.16) | collective-permute-done | bytes 262176 | tf_op jit(solution)/shard_map/ppermute | solution.py:26
  45.9 0.8 %finish_q.1 = (bf16[64,2048]{1,0:T(8,128)(2,1)}, bf16[64,2048]{1,0:T(8,128)(2,1)}, f32[8,128]{1,0:T(8,128)S(1)}) custom-call(s32[1]{0:T(128)} %bitcast.group_ref, bf16[2,64,1024]{2,1,0:T(8,128)(2,1)S(1)} %get-tuple-element.100.refs_0_, bf16[2,64,1024]{2,1,0:T(8,128)(2,1)S(1)} %collective-permute-done.16.refs_1_), custom_call_target="tpu_custom_call" | custom-call | bytes 1052676 | tf_op jit(solution)/shard_map/finish_q/pallas_call | solution.py:41
  46.7 0.6 %collective-permute-done.22.refs_1_ = bf16[64,256]{1,0:T(8,128)(2,1)S(1)} collective-permute-done((bf16[64,256]{1,0:T(8,128)(2,1)S(1)}, bf16[64,256]{1,0:T(8,128)(2,1)S(1)}, u32[]{:S(2)}, u32[]{:S(2)}) %collective-permute-start.22) | collective-permute-done | bytes 32800 | tf_op jit(solution)/shard_map/ppermute | solution.py:26
  47.3 0.6 %finish_kv.1 = (bf16[64,256]{1,0:T(8,128)(2,1)}, bf16[64,256]{1,0:T(8,128)(2,1)}) custom-call(s32[1]{0:T(128)} %bitcast.group_ref, bf16[64,256]{1,0:T(8,128)(2,1)S(1)} %get-tuple-element.109.refs_0_, bf16[64,256]{1,0:T(8,128)(2,1)S(1)} %collective-permute-done.22.refs_1_, f32[8,128]{1,0:T(8,128)S(1)} %get-tuple-element.111.refs_2_), custom_call_target="tpu_custom_call" | custom-call | bytes 135172 | tf_op jit(solution)/shard_map/finish_kv/pallas_call | solution.py:41
  (27 shorter events, 0.3 us)
Async XLA Ops:
  1.4 4.9 %collective-permute-start.1 = (bf16[64,256]{1,0:T(8,128)(2,1)S(1)}, bf16[64,256]{1,0:T(8,128)(2,1)S(1)}, u32[]{:S(2)}, u32[]{:S(2)}) collective-permute-start(bf16[64,256]{1,0:T(8,128)(2,1)S(1)} %pad_maximum_fusion.3), channel_id=1, source_target_pairs={{0,8},{8,0},{16,24},{24,16},{1,9},{9,1},{17,25},{25,17},{2,10},{10... | collective-permute-start | bytes 98312 | tf_op jit(solution)/shard_map/ppermute | solution.py:26
  5.6 11.3 %collective-permute-start = (bf16[2,64,1024]{2,1,0:T(8,128)(2,1)S(1)}, bf16[2,64,1024]{2,1,0:T(8,128)(2,1)S(1)}, u32[]{:S(2)}, u32[]{:S(2)}) collective-permute-start(bf16[2,64,1024]{2,1,0:T(8,128)(2,1)S(1)} %pad_maximum_fusion.1), channel_id=1, source_target_pairs={{0,8},{8,0},{16,24},{24,16},{1,9},{9,1},{17,25},{25,17},{2,10},{10... | collective-permute-start | bytes 786440 | tf_op jit(solution)/shard_map/ppermute | solution.py:26
  6.3 4.8 %collective-permute-start.4 = (bf16[2,64,256]{2,1,0:T(8,128)(2,1)S(1)}, bf16[2,64,256]{2,1,0:T(8,128)(2,1)S(1)}, u32[]{:S(2)}, u32[]{:S(2)}) collective-permute-start(bf16[2,64,256]{2,1,0:T(8,128)(2,1)S(1)} %pad_maximum_fusion.2.refs_0_), channel_id=1, source_target_pairs={{0,2},{1,3},{2,0},{3,1},{4,6},{5,7},{6,4},{7,5},{8,10},{9,11},{10,... | collective-permute-start | bytes 196616 | tf_op jit(solution)/shard_map/ppermute | solution.py:26
  8.5 6.2 %collective-permute-start.3 = (bf16[2,64,256]{2,1,0:T(8,128)(2,1)S(1)}, bf16[2,64,256]{2,1,0:T(8,128)(2,1)S(1)}, u32[]{:S(2)}, u32[]{:S(2)}) collective-permute-start(bf16[2,64,256]{2,1,0:T(8,128)(2,1)S(1)} %pad_maximum_fusion.2.refs_0_), channel_id=1, source_target_pairs={{0,6},{1,7},{2,4},{3,5},{4,2},{5,3},{6,0},{7,1},{8,14},{9,15},{10,... | collective-permute-start | bytes 196616 | tf_op jit(solution)/shard_map/ppermute | solution.py:26
  11.0 5.9 %collective-permute-start.2 = (bf16[2,64,256]{2,1,0:T(8,128)(2,1)S(1)}, bf16[2,64,256]{2,1,0:T(8,128)(2,1)S(1)}, u32[]{:S(2)}, u32[]{:S(2)}) collective-permute-start(bf16[2,64,256]{2,1,0:T(8,128)(2,1)S(1)} %pad_maximum_fusion.2.refs_0_), channel_id=1, source_target_pairs={{0,4},{1,5},{2,6},{3,7},{4,0},{5,1},{6,2},{7,3},{8,12},{9,13},{10,... | collective-permute-start | bytes 196616 | tf_op jit(solution)/shard_map/ppermute | solution.py:26
  11.1 7.9 %collective-permute-start.7 = (bf16[2,2,64,256]{3,2,1,0:T(8,128)(2,1)S(1)}, bf16[2,2,64,256]{3,2,1,0:T(8,128)(2,1)S(1)}, u32[]{:S(2)}, u32[]{:S(2)}) collective-permute-start(bf16[2,2,64,256]{3,2,1,0:T(8,128)(2,1)S(1)} %stack.46.refs_2_.refs_1_), channel_id=1, source_target_pairs={{0,16},{8,24},{16,0},{24,8},{1,17},{9,25},{17,1},{25,9},{2,18},{10... | collective-permute-start | bytes 393224 | tf_op jit(solution)/shard_map/ppermute | solution.py:26
  16.9 5.2 %collective-permute-start.8 = (bf16[2,2,64,256]{3,2,1,0:T(8,128)(2,1)S(1)}, bf16[2,2,64,256]{3,2,1,0:T(8,128)(2,1)S(1)}, u32[]{:S(2)}, u32[]{:S(2)}) collective-permute-start(bf16[2,2,64,256]{3,2,1,0:T(8,128)(2,1)S(1)} %get-tuple-element.65.refs_0_.refs_1_), channel_id=1, source_target_pairs={{0,16},{8,24},{16,0},{24,8},{1,17},{9,25},{17,1},{25,9},{2,18},{10... | collective-permute-start | bytes 393224 | tf_op jit(solution)/shard_map/ppermute | solution.py:26
  18.5 1.6 %collective-permute-start.5 = (bf16[2,2,64,256]{3,2,1,0:T(8,128)(2,1)S(1)}, bf16[2,2,64,256]{3,2,1,0:T(8,128)(2,1)S(1)}, u32[]{:S(2)}, u32[]{:S(2)}) collective-permute-start(bf16[2,2,64,256]{3,2,1,0:T(8,128)(2,1)S(1)} %get-tuple-element.65.refs_0_.refs_1_), channel_id=1, source_target_pairs={{0,1},{1,0},{2,3},{3,2},{4,5},{5,4},{6,7},{7,6},{8,9},{9,8},{10,11... | collective-permute-start | bytes 393224 | tf_op jit(solution)/shard_map/ppermute | solution.py:26
  18.5 1.6 %collective-permute-start.6 = (bf16[2,2,64,256]{3,2,1,0:T(8,128)(2,1)S(1)}, bf16[2,2,64,256]{3,2,1,0:T(8,128)(2,1)S(1)}, u32[]{:S(2)}, u32[]{:S(2)}) collective-permute-start(bf16[2,2,64,256]{3,2,1,0:T(8,128)(2,1)S(1)} %get-tuple-element.66), channel_id=1, source_target_pairs={{0,1},{1,0},{2,3},{3,2},{4,5},{5,4},{6,7},{7,6},{8,9},{9,8},{10,11... | collective-permute-start | bytes 393224 | tf_op jit(solution)/shard_map/ppermute | solution.py:26
  19.0 4.4 %collective-permute-start.10 = (bf16[2,2,64,256]{3,2,1,0:T(8,128)(2,1)S(1)}, bf16[2,2,64,256]{3,2,1,0:T(8,128)(2,1)S(1)}, u32[]{:S(2)}, u32[]{:S(2)}) collective-permute-start(bf16[2,2,64,256]{3,2,1,0:T(8,128)(2,1)S(1)} %collective-permute-done.7.refs_0_), channel_id=1, source_target_pairs={{0,1},{1,0},{2,3},{3,2},{4,5},{5,4},{6,7},{7,6},{8,9},{9,8},{10,11... | collective-permute-start | bytes 393224 | tf_op jit(solution)/shard_map/ppermute | solution.py:26
  22.1 1.6 %collective-permute-start.9 = (bf16[2,2,64,256]{3,2,1,0:T(8,128)(2,1)S(1)}, bf16[2,2,64,256]{3,2,1,0:T(8,128)(2,1)S(1)}, u32[]{:S(2)}, u32[]{:S(2)}) collective-permute-start(bf16[2,2,64,256]{3,2,1,0:T(8,128)(2,1)S(1)} %collective-permute-done.8.refs_0_), channel_id=1, source_target_pairs={{0,1},{1,0},{2,3},{3,2},{4,5},{5,4},{6,7},{7,6},{8,9},{9,8},{10,11... | collective-permute-start | bytes 393224 | tf_op jit(solution)/shard_map/ppermute | solution.py:26
  26.3 1.9 %collective-permute-start.12 = (bf16[2,2,64,256]{3,2,1,0:T(8,128)(2,1)S(1)}, bf16[2,2,64,256]{3,2,1,0:T(8,128)(2,1)S(1)}, u32[]{:S(2)}, u32[]{:S(2)}) collective-permute-start(bf16[2,2,64,256]{3,2,1,0:T(8,128)(2,1)S(1)} %get-tuple-element.90), channel_id=1, source_target_pairs={{0,1},{1,0},{2,3},{3,2},{4,5},{5,4},{6,7},{7,6},{8,9},{9,8},{10,11... | collective-permute-start | bytes 393224 | tf_op jit(solution)/shard_map/ppermute | solution.py:26
  26.7 1.5 %collective-permute-start.11 = (bf16[2,2,64,256]{3,2,1,0:T(8,128)(2,1)S(1)}, bf16[2,2,64,256]{3,2,1,0:T(8,128)(2,1)S(1)}, u32[]{:S(2)}, u32[]{:S(2)}) collective-permute-start(bf16[2,2,64,256]{3,2,1,0:T(8,128)(2,1)S(1)} %get-tuple-element.88), channel_id=1, source_target_pairs={{0,1},{1,0},{2,3},{3,2},{4,5},{5,4},{6,7},{7,6},{8,9},{9,8},{10,11... | collective-permute-start | bytes 393224 | tf_op jit(solution)/shard_map/ppermute | solution.py:26
  28.3 1.4 %collective-permute-start.13 = (bf16[64,128]{1,0:T(8,128)(2,1)S(1)}, bf16[64,128]{1,0:T(8,128)(2,1)S(1)}, u32[]{:S(2)}, u32[]{:S(2)}) collective-permute-start(bf16[64,128]{1,0:T(8,128)(2,1)S(1)} %slice_bitcast_fusion), channel_id=1, source_target_pairs={{0,1},{1,0},{2,3},{3,2},{4,5},{5,4},{6,7},{7,6},{8,9},{9,8},{10,11... | collective-permute-start | bytes 49160 | tf_op jit(solution)/shard_map/ppermute | solution.py:26
  28.7 5.7 %collective-permute-start.17 = (bf16[2,2,64,256]{3,2,1,0:T(8,128)(2,1)S(1)}, bf16[2,2,64,256]{3,2,1,0:T(8,128)(2,1)S(1)}, u32[]{:S(2)}, u32[]{:S(2)}) collective-permute-start(bf16[2,2,64,256]{3,2,1,0:T(8,128)(2,1)S(1)} %sum_cores.3), channel_id=1, source_target_pairs={{0,16},{8,24},{16,0},{24,8},{1,17},{9,25},{17,1},{25,9},{2,18},{10... | collective-permute-start | bytes 393224 | tf_op jit(solution)/shard_map/ppermute | solution.py:26
  30.8 3.6 %collective-permute-start.18 = (bf16[2,2,64,256]{3,2,1,0:T(8,128)(2,1)S(1)}, bf16[2,2,64,256]{3,2,1,0:T(8,128)(2,1)S(1)}, u32[]{:S(2)}, u32[]{:S(2)}) collective-permute-start(bf16[2,2,64,256]{3,2,1,0:T(8,128)(2,1)S(1)} %get-tuple-element.104), channel_id=1, source_target_pairs={{0,1},{1,0},{2,3},{3,2},{4,5},{5,4},{6,7},{7,6},{8,9},{9,8},{10,11... | collective-permute-start | bytes 393224 | tf_op jit(solution)/shard_map/ppermute | solution.py:26
  31.1 6.5 %collective-permute-start.14 = (bf16[2,2,64,256]{3,2,1,0:T(8,128)(2,1)S(1)}, bf16[2,2,64,256]{3,2,1,0:T(8,128)(2,1)S(1)}, u32[]{:S(2)}, u32[]{:S(2)}) collective-permute-start(bf16[2,2,64,256]{3,2,1,0:T(8,128)(2,1)S(1)} %sum_cores.2), channel_id=1, source_target_pairs={{0,16},{8,24},{16,0},{24,8},{1,17},{9,25},{17,1},{25,9},{2,18},{10... | collective-permute-start | bytes 393224 | tf_op jit(solution)/shard_map/ppermute | solution.py:26
  32.1 5.5 %collective-permute-start.15 = (bf16[2,2,64,256]{3,2,1,0:T(8,128)(2,1)S(1)}, bf16[2,2,64,256]{3,2,1,0:T(8,128)(2,1)S(1)}, u32[]{:S(2)}, u32[]{:S(2)}) collective-permute-start(bf16[2,2,64,256]{3,2,1,0:T(8,128)(2,1)S(1)} %get-tuple-element.97), channel_id=1, source_target_pairs={{0,1},{1,0},{2,3},{3,2},{4,5},{5,4},{6,7},{7,6},{8,9},{9,8},{10,11... | collective-permute-start | bytes 393224 | tf_op jit(solution)/shard_map/ppermute | solution.py:26
  34.5 8.0 %collective-permute-start.19 = (bf16[2,64,256]{2,1,0:T(8,128)(2,1)S(1)}, bf16[2,64,256]{2,1,0:T(8,128)(2,1)S(1)}, u32[]{:S(2)}, u32[]{:S(2)}) collective-permute-start(bf16[2,64,256]{2,1,0:T(8,128)(2,1)S(1)} %get-tuple-element.106), channel_id=1, source_target_pairs={{0,4},{1,5},{2,6},{3,7},{4,0},{5,1},{6,2},{7,3},{8,12},{9,13},{10,... | collective-permute-start | bytes 196616 | tf_op jit(solution)/shard_map/ppermute | solution.py:26
  35.7 6.8 %collective-permute-start.20 = (bf16[2,64,256]{2,1,0:T(8,128)(2,1)S(1)}, bf16[2,64,256]{2,1,0:T(8,128)(2,1)S(1)}, u32[]{:S(2)}, u32[]{:S(2)}) collective-permute-start(bf16[2,64,256]{2,1,0:T(8,128)(2,1)S(1)} %get-tuple-element.107), channel_id=1, source_target_pairs={{0,6},{1,7},{2,4},{3,5},{4,2},{5,3},{6,0},{7,1},{8,14},{9,15},{10,... | collective-permute-start | bytes 196616 | tf_op jit(solution)/shard_map/ppermute | solution.py:26
  37.6 5.7 %collective-permute-start.21 = (bf16[2,64,256]{2,1,0:T(8,128)(2,1)S(1)}, bf16[2,64,256]{2,1,0:T(8,128)(2,1)S(1)}, u32[]{:S(2)}, u32[]{:S(2)}) collective-permute-start(bf16[2,64,256]{2,1,0:T(8,128)(2,1)S(1)} %get-tuple-element.108), channel_id=1, source_target_pairs={{0,2},{1,3},{2,0},{3,1},{4,6},{5,7},{6,4},{7,5},{8,10},{9,11},{10,... | collective-permute-start | bytes 196616 | tf_op jit(solution)/shard_map/ppermute | solution.py:26
  38.3 7.6 %collective-permute-start.16 = (bf16[2,64,1024]{2,1,0:T(8,128)(2,1)S(1)}, bf16[2,64,1024]{2,1,0:T(8,128)(2,1)S(1)}, u32[]{:S(2)}, u32[]{:S(2)}) collective-permute-start(bf16[2,64,1024]{2,1,0:T(8,128)(2,1)S(1)} %get-tuple-element.101), channel_id=1, source_target_pairs={{0,8},{8,0},{16,24},{24,16},{1,9},{9,1},{17,25},{25,17},{2,10},{10... | collective-permute-start | bytes 786440 | tf_op jit(solution)/shard_map/ppermute | solution.py:26
  43.3 4.0 %collective-permute-start.22 = (bf16[64,256]{1,0:T(8,128)(2,1)S(1)}, bf16[64,256]{1,0:T(8,128)(2,1)S(1)}, u32[]{:S(2)}, u32[]{:S(2)}) collective-permute-start(bf16[64,256]{1,0:T(8,128)(2,1)S(1)} %get-tuple-element.110), channel_id=1, source_target_pairs={{0,8},{8,0},{16,24},{24,16},{1,9},{9,1},{17,25},{25,17},{2,10},{10... | collective-permute-start | bytes 98312 | tf_op jit(solution)/shard_map/ppermute | solution.py:26

commit v17 on v16

--- a/solution.py
+++ b/solution.py
@@ -94,22 +94,24 @@
 
     def gap(self, tile, info_ref):
         s, start = self.tiles[tile]
-        head, ctx = info_ref[0], info_ref[1]
+        (place_ref, order_ref) = info_ref
+        head, ctx = place_ref[0], place_ref[1]
         row = lax.broadcasted_iota(jnp.int32, (1, self.lanes), 1) % self.tile_rows + start
         pos = jnp.zeros((1, self.lanes), jnp.int32)
         for b in range(start // self.block_rows, -(-(start + self.tile_rows) // self.block_rows)):
-            first = info_ref[2 + ctx * self.blocks + b] * self.block_len + (head ^ s) * self.block_rows
+            first = order_ref[ctx * self.blocks + b] * self.block_len + (head ^ s) * self.block_rows
             pos = jnp.where(row // self.block_rows == b, first + row % self.block_rows, pos)
         return pos - lax.broadcasted_iota(jnp.int32, (self.block_rows, self.lanes), 0)
 
     def firsts(self, chunk, info_ref):
-        head, ctx = info_ref[0], info_ref[1]
+        (place_ref, order_ref) = info_ref
+        head, ctx = place_ref[0], place_ref[1]
         a, core, part = chunk
         for j in range(self.slices):
             m, rest = divmod(j, self.kv * self.blocks)
             s, b = divmod(rest, self.blocks)
             stored = (ctx ^ (self.zone(part)[m] * self.cores + core)) * self.blocks + b
-            yield info_ref[2 + stored] * self.block_len + (head ^ (a * self.kv + s)) * self.block_rows
+            yield order_ref[stored] * self.block_len + (head ^ (a * self.kv + s)) * self.block_rows
 
     def first_at(self, chunk):
         a, core, part = chunk
@@ -185,7 +187,8 @@
         mix_ref[:, at] = mixed
 
 
-def place_kernel(plan, chunks, info_ref, gap_ref, first_ref):
+def place_kernel(plan, chunks, place_ref, order_ref, gap_ref, first_ref):
+    info_ref = (place_ref, order_ref)
     for tile in range(len(plan.tiles)):
         gap_ref[pl.ds(tile * plan.block_rows, plan.block_rows), :] = plan.gap(tile, info_ref)
     for chunk in chunks:
@@ -359,7 +362,6 @@
     z_part = plan.z_part
     head = lax.axis_index("head").astype(jnp.int32)
     place = jnp.stack([head, lax.axis_index("ctx").astype(jnp.int32)])
-    info = jnp.concatenate([place, block_order])
     own_group = (head % kv).reshape(1)
     queries = queries.reshape(rows, query_width)
     out_grad = out_grad.reshape(rows, query_width)
@@ -401,9 +403,9 @@
     gap, firsts = call(
         functools.partial(place_kernel, plan, chunks),
         "place",
-        (info,),
+        (place, block_order),
         [i32(len(plan.tiles) * block_rows, plan.lanes), i32(len(chunks) * plan.slices, plan.lanes)],
-        [SMEM],
+        [SMEM, SMEM],
     )
     q_all, do_all, q_t, do_t = call(
         functools.partial(turn_kernel, plan),

time: 48.2 us -> 48.2 us (level)
  local copies, waits for them, and re-layouts: 0.01 us -> 0.66 us
  other arithmetic: 2.71 us -> 2.06 us
    concatenate x1 -> x0, other arithmetic: 0.73 us -> none  [shards(): info = jnp.concatenate([place, block_order])]
    unnamed x0 -> x2, local copies, waits for them, and re-layouts: none -> 0.65 us
  transfers between devices with their start and end apart: 23 -> 23, of which waited for: 9 -> 9; matrix products, arithmetic and copies ran while one was open for 4% -> 3% of each run, Pallas kernels for 19% -> 19%
where the time goes in v17:
time: 48.2 us; the launch traced here: 48 us
  starting transfers between devices  22.4 us (46%)
  Pallas kernels  12.3 us (26%)
  waiting for transfers between devices  9.69 us (20%)
  other arithmetic  2.06 us (4%)
  between operations  0.87 us (2%)
  local copies, waits for them, and re-layouts  0.66 us (1%)
    ppermute x23, starting transfers between devices, swap(): return lax.ppermute(block, axis, [(i, i ^ mask) for i in range(size)])  22.4 us
    pallas_call x20, Pallas kernels, call(): pl.pallas_call(kernel, out_shape=list(outs), in_specs=specs or [VMEM] * l...  12.3 us
    ppermute x23, waiting for transfers between devices, swap(): return lax.ppermute(block, axis, [(i, i ^ mask) for i in range(size)])  9.69 us
    another operation x3, other arithmetic, queries_of(): return jnp.stack([pick(queries, g, width), pick(out_grad, g, width)])  1.18 us
  transfers between devices with their start and end apart: 23, of which 9 were waited for; matrix products, arithmetic and copies ran while one was open for 3% of the time, Pallas kernels for 19%

profile of v17, /device:TPU:0, one launch (start us, length us, event | category | flops | bytes accessed | tf_op | source)
XLA Modules:
  0.0 48.0 jit_solution(7740020547546818926)
XLA Ops:
  0.6 0.8 %broadcast_select_fusion.2 = (bf16[64,128]{1,0:T(8,128)(2,1)S(1)}, bf16[64,128]{1,0:T(8,128)(2,1)S(1)}, bf16[64,128]{1,0:T(8,128)(2,1)S(1)}, bf16[64,128]{1,0:T(8,128)(2,1)S(1)}) fusion(pred[]{:T(512)S(6)} %eq.18, bf16[64,256]{1,0:T(8,128)(2,1)} %bitcast.26, pred[]{:T(512)S(6)} %eq.19, bf16[64,256]{1,0:T(8,128)(2,1)} %bitcast.27), kind=kLoop, calls=%fused_computation.12 | loop fusion | flops 32768 | bytes 131074 | tf_op jit(solution)/shard_map/jit(_where)/select_n | solution.py:388
  1.4 3.0 %collective-permute-start.1 = (bf16[64,256]{1,0:T(8,128)(2,1)S(1)}, bf16[64,256]{1,0:T(8,128)(2,1)S(1)}, u32[]{:S(2)}, u32[]{:S(2)}) collective-permute-start(bf16[64,256]{1,0:T(8,128)(2,1)S(1)} %pad_maximum_fusion.3), channel_id=1, source_target_pairs={{0,8},{8,0},{16,24},{24,16},{1,9},{9,1},{17,25},{25,17},{2,10},{10... | collective-permute-start | bytes 98312 | tf_op jit(solution)/shard_map/ppermute | solution.py:26
  4.4 1.1 %select_bitcast_fusion = (bf16[1,64,1024]{2,1,0:T(8,128)(2,1)S(1)}, bf16[1,64,1024]{2,1,0:T(8,128)(2,1)S(1)}, bf16[1,64,1024]{2,1,0:T(8,128)(2,1)S(1)}, bf16[1,64,1024]{2,1,0:T(8,128)(2,1)S(1)}) fusion(pred[]{:T(512)S(6)} %eq.19, bf16[64,2048]{1,0:T(8,128)(2,1)} %bitcast.24, pred[]{:T(512)S(6)} %eq.18, bf16[64,2048]{1,0:T(8,128)(2,1)} %bitcast.25), kind=kLoop, calls=%fused_computation.2 | loop fusion | flops 262144 | bytes 1048578 | tf_op jit(solution)/shard_map/stack | solution.py:395
  5.6 0.1 collective-permute-start
  5.7 0.6 %collective-permute-done.1 = bf16[64,256]{1,0:T(8,128)(2,1)S(1)} collective-permute-done((bf16[64,256]{1,0:T(8,128)(2,1)S(1)}, bf16[64,256]{1,0:T(8,128)(2,1)S(1)}, u32[]{:S(2)}, u32[]{:S(2)}) %collective-permute-start.1) | collective-permute-done | bytes 32800 | tf_op jit(solution)/shard_map/ppermute | solution.py:26
  6.3 2.2 %collective-permute-start.4 = (bf16[2,64,256]{2,1,0:T(8,128)(2,1)S(1)}, bf16[2,64,256]{2,1,0:T(8,128)(2,1)S(1)}, u32[]{:S(2)}, u32[]{:S(2)}) collective-permute-start(bf16[2,64,256]{2,1,0:T(8,128)(2,1)S(1)} %pad_maximum_fusion.2.refs_0_), channel_id=1, source_target_pairs={{0,2},{1,3},{2,0},{3,1},{4,6},{5,7},{6,4},{7,5},{8,10},{9,11},{10,... | collective-permute-start | bytes 196616 | tf_op jit(solution)/shard_map/ppermute | solution.py:26
  8.5 2.5 %collective-permute-start.3 = (bf16[2,64,256]{2,1,0:T(8,128)(2,1)S(1)}, bf16[2,64,256]{2,1,0:T(8,128)(2,1)S(1)}, u32[]{:S(2)}, u32[]{:S(2)}) collective-permute-start(bf16[2,64,256]{2,1,0:T(8,128)(2,1)S(1)} %pad_maximum_fusion.2.refs_0_), channel_id=1, source_target_pairs={{0,6},{1,7},{2,4},{3,5},{4,2},{5,3},{6,0},{7,1},{8,14},{9,15},{10,... | collective-permute-start | bytes 196616 | tf_op jit(solution)/shard_map/ppermute | solution.py:26
  11.0 0.1 collective-permute-start.2
  11.1 1.7 %collective-permute-start.7 = (bf16[2,2,64,256]{3,2,1,0:T(8,128)(2,1)S(1)}, bf16[2,2,64,256]{3,2,1,0:T(8,128)(2,1)S(1)}, u32[]{:S(2)}, u32[]{:S(2)}) collective-permute-start(bf16[2,2,64,256]{3,2,1,0:T(8,128)(2,1)S(1)} %stack.50.refs_2_.refs_1_), channel_id=1, source_target_pairs={{0,16},{8,24},{16,0},{24,8},{1,17},{9,25},{17,1},{25,9},{2,18},{10... | collective-permute-start | bytes 393224 | tf_op jit(solution)/shard_map/ppermute | solution.py:26
  12.8 0.1 pad_add_fusion.place_ref
  12.9 0.7 %copy-done = s32[16]{0:T(128)S(1)} copy-done((s32[16]{0:T(128)S(1)}, s32[16]{0:T(128)}, u32[]{:S(2)}) %copy-start) | copy-done | bytes 88
  13.5 0.6 %place.1 = (s32[128,256]{1,0:T(8,128)S(1)}, s32[64,256]{1,0:T(8,128)S(1)}) custom-call(s32[2]{0:T(128)S(1)} %pad_add_fusion.place_ref, s32[16]{0:T(128)S(1)} %copy-done), custom_call_target="tpu_custom_call" | custom-call | bytes 196680 | tf_op jit(solution)/shard_map/place/pallas_call | solution.py:41
  14.2 0.6 %collective-permute-done.3.refs_1_ = bf16[2,64,256]{2,1,0:T(8,128)(2,1)S(1)} collective-permute-done((bf16[2,64,256]{2,1,0:T(8,128)(2,1)S(1)}, bf16[2,64,256]{2,1,0:T(8,128)(2,1)S(1)}, u32[]{:S(2)}, u32[]{:S(2)}) %collective-permute-start.3) | collective-permute-done | bytes 65568 | tf_op jit(solution)/shard_map/ppermute | solution.py:26
  14.7 2.1 %collective-permute-done.2.refs_0_ = bf16[2,64,256]{2,1,0:T(8,128)(2,1)S(1)} collective-permute-done((bf16[2,64,256]{2,1,0:T(8,128)(2,1)S(1)}, bf16[2,64,256]{2,1,0:T(8,128)(2,1)S(1)}, u32[]{:S(2)}, u32[]{:S(2)}) %collective-permute-start.2) | collective-permute-done | bytes 65568 | tf_op jit(solution)/shard_map/ppermute | solution.py:26
  16.9 1.6 %collective-permute-start.8 = (bf16[2,2,64,256]{3,2,1,0:T(8,128)(2,1)S(1)}, bf16[2,2,64,256]{3,2,1,0:T(8,128)(2,1)S(1)}, u32[]{:S(2)}, u32[]{:S(2)}) collective-permute-start(bf16[2,2,64,256]{3,2,1,0:T(8,128)(2,1)S(1)} %get-tuple-element.65.refs_0_.refs_1_), channel_id=1, source_target_pairs={{0,16},{8,24},{16,0},{24,8},{1,17},{9,25},{17,1},{25,9},{2,18},{10... | collective-permute-start | bytes 393224 | tf_op jit(solution)/shard_map/ppermute | solution.py:26
  18.5 0.5 %collective-permute-start.6 = (bf16[2,2,64,256]{3,2,1,0:T(8,128)(2,1)S(1)}, bf16[2,2,64,256]{3,2,1,0:T(8,128)(2,1)S(1)}, u32[]{:S(2)}, u32[]{:S(2)}) collective-permute-start(bf16[2,2,64,256]{3,2,1,0:T(8,128)(2,1)S(1)} %get-tuple-element.66), channel_id=1, source_target_pairs={{0,1},{1,0},{2,3},{3,2},{4,5},{5,4},{6,7},{7,6},{8,9},{9,8},{10,11... | collective-permute-start | bytes 393224 | tf_op jit(solution)/shard_map/ppermute | solution.py:26
  19.0 0.1 collective-permute-start.10
  19.1 0.2 turn.1
  19.3 0.7 %attend_mid.2 = (f32[256,1024]{1,0:T(8,128)S(1)}, f32[1,1024]{1,0:T(1,128)S(1)}, f32[1,1024]{1,0:T(1,128)S(1)}, f32[128,1024]{1,0:T(8,128)S(1)}) custom-call(s32[128,256]{1,0:T(8,128)S(1)} %get-tuple-element.62.gap_ref, s32[64,256]{1,0:T(8,128)S(1)} %get-tuple-element.63.refs_4_.first_ref, bf16[128,1024]{1,0:T(8,128)(2,1)S(1)} %get-tuple-element.64.q_t, ...), custom_call_target="tpu_custom_call" | custom-call | flops 268435456 | bytes 2170880 | tf_op jit(solution)/shard_map/attend_mid/pallas_call | solution.py:41
  20.1 2.0 %attend_near.1 = (f32[1024,1024]{1,0:T(8,128)S(1)}, f32[1,1024]{1,0:T(1,128)S(1)}, f32[1,1024]{1,0:T(1,128)S(1)}, f32[128,1024]{1,0:T(8,128)S(1)}) custom-call(s32[128,256]{1,0:T(8,128)S(1)} %get-tuple-element.62.gap_ref, s32[64,256]{1,0:T(8,128)S(1)} %get-tuple-element.63.refs_4_.first_ref, bf16[128,1024]{1,0:T(8,128)(2,1)S(1)} %get-tuple-element.64.q_t, ...), custom_call_target="tpu_custom_call" | custom-call | flops 1073741824 | bytes 5713920 | tf_op jit(solution)/shard_map/attend_near/pallas_call | solution.py:41
  22.1 0.6 %collective-permute-start.9 = (bf16[2,2,64,256]{3,2,1,0:T(8,128)(2,1)S(1)}, bf16[2,2,64,256]{3,2,1,0:T(8,128)(2,1)S(1)}, u32[]{:S(2)}, u32[]{:S(2)}) collective-permute-start(bf16[2,2,64,256]{3,2,1,0:T(8,128)(2,1)S(1)} %collective-permute-done.8.refs_0_), channel_id=1, source_target_pairs={{0,1},{1,0},{2,3},{3,2},{4,5},{5,4},{6,7},{7,6},{8,9},{9,8},{10,11... | collective-permute-start | bytes 393224 | tf_op jit(solution)/shard_map/ppermute | solution.py:26
  22.6 0.7 %attend_mid.3 = (f32[256,1024]{1,0:T(8,128)S(1)}, f32[1,1024]{1,0:T(1,128)S(1)}, f32[1,1024]{1,0:T(1,128)S(1)}, f32[128,1024]{1,0:T(8,128)S(1)}) custom-call(s32[128,256]{1,0:T(8,128)S(1)} %get-tuple-element.62.gap_ref, s32[64,256]{1,0:T(8,128)S(1)} %get-tuple-element.63.refs_4_.first_ref, bf16[128,1024]{1,0:T(8,128)(2,1)S(1)} %get-tuple-element.64.q_t, ...), custom_call_target="tpu_custom_call" | custom-call | flops 268435456 | bytes 2174976 | tf_op jit(solution)/shard_map/attend_mid/pallas_call | solution.py:41
  23.4 0.2 collective-permute-done.9.refs_9_
  23.6 2.6 %attend_far.1 = (f32[1,1024]{1,0:T(1,128)S(1)}, f32[1,1024]{1,0:T(1,128)S(1)}, f32[1,1024]{1,0:T(1,128)S(1)}, f32[1,1024]{1,0:T(1,128)S(1)}, bf16[128,1024]{1,0:...) custom-call(s32[128,256]{1,0:T(8,128)S(1)} %get-tuple-element.62.gap, ...), custom_call_target="tpu_custom_call" | custom-call | flops 1073741824 | bytes 4169728 | tf_op jit(solution)/shard_map/attend_far/pallas_call | solution.py:41
  26.3 0.4 collective-permute-start.12
  26.7 0.1 collective-permute-start.11
  26.8 0.6 %attend_back.4 = (f32[128,1024]{1,0:T(8,128)S(1)}, bf16[2,2,64,256]{3,2,1,0:T(8,128)(2,1)S(1)}) custom-call(bf16[1024,128]{1,0:T(8,128)(2,1)S(1)} %get-tuple-element.59.q_all, bf16[1024,128]{1,0:T(8,128)(2,1)S(1)} %get-tuple-element.60.do_all, bf16[128,1024]{1,0:T(8,128)(2,1)S(1)} %get-tuple-element.61.do_t, f32[256,1024]{1,0:T(8,128)S(1)} %get-tuple-element.82.e_ref, ...), custom_call_target="tpu_custom_call" | custom-call | flops 402653184 | bytes 3153920 | tf_op jit(solution)/shard_map/attend_back/pallas_call | solution.py:41
  27.5 0.7 %attend_back.5 = (f32[128,1024]{1,0:T(8,128)S(1)}, bf16[2,2,64,256]{3,2,1,0:T(8,128)(2,1)S(1)}) custom-call(bf16[1024,128]{1,0:T(8,128)(2,1)S(1)} %get-tuple-element.59.q_all, bf16[1024,128]{1,0:T(8,128)(2,1)S(1)} %get-tuple-element.60.do_all, bf16[128,1024]{1,0:T(8,128)(2,1)S(1)} %get-tuple-element.61.do_t, f32[256,1024]{1,0:T(8,128)S(1)} %get-tuple-element.80.e_ref, ...), custom_call_target="tpu_custom_call" | custom-call | flops 402653184 | bytes 3153920 | tf_op jit(solution)/shard_map/attend_back/pallas_call | solution.py:41
  28.3 0.4 collective-permute-start.13
  28.7 1.0 %collective-permute-start.17 = (bf16[2,2,64,256]{3,2,1,0:T(8,128)(2,1)S(1)}, bf16[2,2,64,256]{3,2,1,0:T(8,128)(2,1)S(1)}, u32[]{:S(2)}, u32[]{:S(2)}) collective-permute-start(bf16[2,2,64,256]{3,2,1,0:T(8,128)(2,1)S(1)} %sum_cores.3), channel_id=1, source_target_pairs={{0,16},{8,24},{16,0},{24,8},{1,17},{9,25},{17,1},{25,9},{2,18},{10... | collective-permute-start | bytes 393224 | tf_op jit(solution)/shard_map/ppermute | solution.py:26
  29.7 1.2 %attend_back.6 = (f32[128,1024]{1,0:T(8,128)S(1)}, bf16[2,2,64,256]{3,2,1,0:T(8,128)(2,1)S(1)}, bf16[2,2,64,256]{3,2,1,0:T(8,128)(2,1)S(1)}) custom-call(bf16[1024,128]{1,0:T(8,128)(2,1)S(1)} %get-tuple-element.59.q_all, bf16[1024,128]{1,0:T(8,128)(2,1)S(1)} %get-tuple-element.60.do_all, bf16[128,1024]{1,0:T(8,128)(2,1)S(1)} %get-tuple-element.61.do_t, ...), custom_call_target="tpu_custom_call" | custom-call | flops 805306368 | bytes 6578176 | tf_op jit(solution)/shard_map/attend_back/pallas_call | solution.py:41
  30.8 0.3 collective-permute-start.18
  31.1 1.0 %collective-permute-start.14 = (bf16[2,2,64,256]{3,2,1,0:T(8,128)(2,1)S(1)}, bf16[2,2,64,256]{3,2,1,0:T(8,128)(2,1)S(1)}, u32[]{:S(2)}, u32[]{:S(2)}) collective-permute-start(bf16[2,2,64,256]{3,2,1,0:T(8,128)(2,1)S(1)} %sum_cores.2), channel_id=1, source_target_pairs={{0,16},{8,24},{16,0},{24,8},{1,17},{9,25},{17,1},{25,9},{2,18},{10... | collective-permute-start | bytes 393224 | tf_op jit(solution)/shard_map/ppermute | solution.py:26
  32.1 0.1 collective-permute-start.15
  32.2 1.2 %attend_back.7 = (bf16[2,64,1024]{2,1,0:T(8,128)(2,1)S(1)}, bf16[2,64,1024]{2,1,0:T(8,128)(2,1)S(1)}, bf16[2,2,64,256]{3,2,1,0:T(8,128)(2,1)S(1)}, bf16[2,2,64,256]{3,2,1,0:T(8,128)(2,1)S(1)}) custom-call(bf16[1024,128]{1,0:T(8,128)(2,1)S(1)} %get-tuple-element.59.q_all, bf16[1024,128]{1,0:T(8,128)(2,1)S(1)} %get-tuple-element.60.do_all, ...), custom_call_target="tpu_custom_call" | custom-call | flops 805306368 | bytes 6840320 | tf_op jit(solution)/shard_map/attend_back/pallas_call | solution.py:41
  33.4 1.0 %collective-permute-done.17.refs_0_ = bf16[2,2,64,256]{3,2,1,0:T(8,128)(2,1)S(1)} collective-permute-done((bf16[2,2,64,256]{3,2,1,0:T(8,128)(2,1)S(1)}, bf16[2,2,64,256]{3,2,1,0:T(8,128)(2,1)S(1)}, u32[]{:S(2)}, u32[]{:S(2)}) %collective-permute-start.17) | collective-permute-done | bytes 131104 | tf_op jit(solution)/shard_map/ppermute | solution.py:26
  34.5 1.2 %collective-permute-start.19 = (bf16[2,64,256]{2,1,0:T(8,128)(2,1)S(1)}, bf16[2,64,256]{2,1,0:T(8,128)(2,1)S(1)}, u32[]{:S(2)}, u32[]{:S(2)}) collective-permute-start(bf16[2,64,256]{2,1,0:T(8,128)(2,1)S(1)} %get-tuple-element.106), channel_id=1, source_target_pairs={{0,4},{1,5},{2,6},{3,7},{4,0},{5,1},{6,2},{7,3},{8,12},{9,13},{10,... | collective-permute-start | bytes 196616 | tf_op jit(solution)/shard_map/ppermute | solution.py:26
  35.7 1.9 %collective-permute-start.20 = (bf16[2,64,256]{2,1,0:T(8,128)(2,1)S(1)}, bf16[2,64,256]{2,1,0:T(8,128)(2,1)S(1)}, u32[]{:S(2)}, u32[]{:S(2)}) collective-permute-start(bf16[2,64,256]{2,1,0:T(8,128)(2,1)S(1)} %get-tuple-element.107), channel_id=1, source_target_pairs={{0,6},{1,7},{2,4},{3,5},{4,2},{5,3},{6,0},{7,1},{8,14},{9,15},{10,... | collective-permute-start | bytes 196616 | tf_op jit(solution)/shard_map/ppermute | solution.py:26
  37.6 0.1 sum_heads.2
  37.6 0.7 %collective-permute-start.21 = (bf16[2,64,256]{2,1,0:T(8,128)(2,1)S(1)}, bf16[2,64,256]{2,1,0:T(8,128)(2,1)S(1)}, u32[]{:S(2)}, u32[]{:S(2)}) collective-permute-start(bf16[2,64,256]{2,1,0:T(8,128)(2,1)S(1)} %get-tuple-element.108), channel_id=1, source_target_pairs={{0,2},{1,3},{2,0},{3,1},{4,6},{5,7},{6,4},{7,5},{8,10},{9,11},{10,... | collective-permute-start | bytes 196616 | tf_op jit(solution)/shard_map/ppermute | solution.py:26
  38.3 1.5 %collective-permute-start.16 = (bf16[2,64,1024]{2,1,0:T(8,128)(2,1)S(1)}, bf16[2,64,1024]{2,1,0:T(8,128)(2,1)S(1)}, u32[]{:S(2)}, u32[]{:S(2)}) collective-permute-start(bf16[2,64,1024]{2,1,0:T(8,128)(2,1)S(1)} %get-tuple-element.101), channel_id=1, source_target_pairs={{0,8},{8,0},{16,24},{24,16},{1,9},{9,1},{17,25},{25,17},{2,10},{10... | collective-permute-start | bytes 786440 | tf_op jit(solution)/shard_map/ppermute | solution.py:26
  39.8 2.7 %collective-permute-done.19.refs_0_ = bf16[2,64,256]{2,1,0:T(8,128)(2,1)S(1)} collective-permute-done((bf16[2,64,256]{2,1,0:T(8,128)(2,1)S(1)}, bf16[2,64,256]{2,1,0:T(8,128)(2,1)S(1)}, u32[]{:S(2)}, u32[]{:S(2)}) %collective-permute-start.19) | collective-permute-done | bytes 65568 | tf_op jit(solution)/shard_map/ppermute | solution.py:26
  42.5 0.8 %collective-permute-done.21.refs_2_ = bf16[2,64,256]{2,1,0:T(8,128)(2,1)S(1)} collective-permute-done((bf16[2,64,256]{2,1,0:T(8,128)(2,1)S(1)}, bf16[2,64,256]{2,1,0:T(8,128)(2,1)S(1)}, u32[]{:S(2)}, u32[]{:S(2)}) %collective-permute-start.21) | collective-permute-done | bytes 65568 | tf_op jit(solution)/shard_map/ppermute | solution.py:26
  43.3 1.6 %collective-permute-start.22 = (bf16[64,256]{1,0:T(8,128)(2,1)S(1)}, bf16[64,256]{1,0:T(8,128)(2,1)S(1)}, u32[]{:S(2)}, u32[]{:S(2)}) collective-permute-start(bf16[64,256]{1,0:T(8,128)(2,1)S(1)} %get-tuple-element.110), channel_id=1, source_target_pairs={{0,8},{8,0},{16,24},{24,16},{1,9},{9,1},{17,25},{25,17},{2,10},{10... | collective-permute-start | bytes 98312 | tf_op jit(solution)/shard_map/ppermute | solution.py:26
  44.9 1.0 %collective-permute-done.16.refs_1_ = bf16[2,64,1024]{2,1,0:T(8,128)(2,1)S(1)} collective-permute-done((bf16[2,64,1024]{2,1,0:T(8,128)(2,1)S(1)}, bf16[2,64,1024]{2,1,0:T(8,128)(2,1)S(1)}, u32[]{:S(2)}, u32[]{:S(2)}) %collective-permute-start.16) | collective-permute-done | bytes 262176 | tf_op jit(solution)/shard_map/ppermute | solution.py:26
  45.9 0.8 %finish_q.1 = (bf16[64,2048]{1,0:T(8,128)(2,1)}, bf16[64,2048]{1,0:T(8,128)(2,1)}, f32[8,128]{1,0:T(8,128)S(1)}) custom-call(s32[1]{0:T(128)} %bitcast.group_ref, bf16[2,64,1024]{2,1,0:T(8,128)(2,1)S(1)} %get-tuple-element.100.refs_0_, bf16[2,64,1024]{2,1,0:T(8,128)(2,1)S(1)} %collective-permute-done.16.refs_1_), custom_call_target="tpu_custom_call" | custom-call | bytes 1052676 | tf_op jit(solution)/shard_map/finish_q/pallas_call | solution.py:41
  46.7 0.6 %collective-permute-done.22.refs_1_ = bf16[64,256]{1,0:T(8,128)(2,1)S(1)} collective-permute-done((bf16[64,256]{1,0:T(8,128)(2,1)S(1)}, bf16[64,256]{1,0:T(8,128)(2,1)S(1)}, u32[]{:S(2)}, u32[]{:S(2)}) %collective-permute-start.22) | collective-permute-done | bytes 32800 | tf_op jit(solution)/shard_map/ppermute | solution.py:26
  47.3 0.6 %finish_kv.1 = (bf16[64,256]{1,0:T(8,128)(2,1)}, bf16[64,256]{1,0:T(8,128)(2,1)}) custom-call(s32[1]{0:T(128)} %bitcast.group_ref, bf16[64,256]{1,0:T(8,128)(2,1)S(1)} %get-tuple-element.109.refs_0_, bf16[64,256]{1,0:T(8,128)(2,1)S(1)} %collective-permute-done.22.refs_1_, f32[8,128]{1,0:T(8,128)S(1)} %get-tuple-element.111.refs_2_), custom_call_target="tpu_custom_call" | custom-call | bytes 135172 | tf_op jit(solution)/shard_map/finish_kv/pallas_call | solution.py:41
  (29 shorter events, 0.3 us)
Async XLA Ops:
  1.4 4.9 %collective-permute-start.1 = (bf16[64,256]{1,0:T(8,128)(2,1)S(1)}, bf16[64,256]{1,0:T(8,128)(2,1)S(1)}, u32[]{:S(2)}, u32[]{:S(2)}) collective-permute-start(bf16[64,256]{1,0:T(8,128)(2,1)S(1)} %pad_maximum_fusion.3), channel_id=1, source_target_pairs={{0,8},{8,0},{16,24},{24,16},{1,9},{9,1},{17,25},{25,17},{2,10},{10... | collective-permute-start | bytes 98312 | tf_op jit(solution)/shard_map/ppermute | solution.py:26
  5.6 11.3 %collective-permute-start = (bf16[2,64,1024]{2,1,0:T(8,128)(2,1)S(1)}, bf16[2,64,1024]{2,1,0:T(8,128)(2,1)S(1)}, u32[]{:S(2)}, u32[]{:S(2)}) collective-permute-start(bf16[2,64,1024]{2,1,0:T(8,128)(2,1)S(1)} %pad_maximum_fusion.1), channel_id=1, source_target_pairs={{0,8},{8,0},{16,24},{24,16},{1,9},{9,1},{17,25},{25,17},{2,10},{10... | collective-permute-start | bytes 786440 | tf_op jit(solution)/shard_map/ppermute | solution.py:26
  6.3 4.8 %collective-permute-start.4 = (bf16[2,64,256]{2,1,0:T(8,128)(2,1)S(1)}, bf16[2,64,256]{2,1,0:T(8,128)(2,1)S(1)}, u32[]{:S(2)}, u32[]{:S(2)}) collective-permute-start(bf16[2,64,256]{2,1,0:T(8,128)(2,1)S(1)} %pad_maximum_fusion.2.refs_0_), channel_id=1, source_target_pairs={{0,2},{1,3},{2,0},{3,1},{4,6},{5,7},{6,4},{7,5},{8,10},{9,11},{10,... | collective-permute-start | bytes 196616 | tf_op jit(solution)/shard_map/ppermute | solution.py:26
  8.5 6.2 %collective-permute-start.3 = (bf16[2,64,256]{2,1,0:T(8,128)(2,1)S(1)}, bf16[2,64,256]{2,1,0:T(8,128)(2,1)S(1)}, u32[]{:S(2)}, u32[]{:S(2)}) collective-permute-start(bf16[2,64,256]{2,1,0:T(8,128)(2,1)S(1)} %pad_maximum_fusion.2.refs_0_), channel_id=1, source_target_pairs={{0,6},{1,7},{2,4},{3,5},{4,2},{5,3},{6,0},{7,1},{8,14},{9,15},{10,... | collective-permute-start | bytes 196616 | tf_op jit(solution)/shard_map/ppermute | solution.py:26
  11.0 5.9 %collective-permute-start.2 = (bf16[2,64,256]{2,1,0:T(8,128)(2,1)S(1)}, bf16[2,64,256]{2,1,0:T(8,128)(2,1)S(1)}, u32[]{:S(2)}, u32[]{:S(2)}) collective-permute-start(bf16[2,64,256]{2,1,0:T(8,128)(2,1)S(1)} %pad_maximum_fusion.2.refs_0_), channel_id=1, source_target_pairs={{0,4},{1,5},{2,6},{3,7},{4,0},{5,1},{6,2},{7,3},{8,12},{9,13},{10,... | collective-permute-start | bytes 196616 | tf_op jit(solution)/shard_map/ppermute | solution.py:26
  11.1 7.9 %collective-permute-start.7 = (bf16[2,2,64,256]{3,2,1,0:T(8,128)(2,1)S(1)}, bf16[2,2,64,256]{3,2,1,0:T(8,128)(2,1)S(1)}, u32[]{:S(2)}, u32[]{:S(2)}) collective-permute-start(bf16[2,2,64,256]{3,2,1,0:T(8,128)(2,1)S(1)} %stack.50.refs_2_.refs_1_), channel_id=1, source_target_pairs={{0,16},{8,24},{16,0},{24,8},{1,17},{9,25},{17,1},{25,9},{2,18},{10... | collective-permute-start | bytes 393224 | tf_op jit(solution)/shard_map/ppermute | solution.py:26
  12.9 0.7 %copy-start = (s32[16]{0:T(128)S(1)}, s32[16]{0:T(128)}, u32[]{:S(2)}) copy-start(s32[16]{0:T(128)} %order_ref.1) | copy-start | bytes 196
  16.9 5.2 %collective-permute-start.8 = (bf16[2,2,64,256]{3,2,1,0:T(8,128)(2,1)S(1)}, bf16[2,2,64,256]{3,2,1,0:T(8,128)(2,1)S(1)}, u32[]{:S(2)}, u32[]{:S(2)}) collective-permute-start(bf16[2,2,64,256]{3,2,1,0:T(8,128)(2,1)S(1)} %get-tuple-element.65.refs_0_.refs_1_), channel_id=1, source_target_pairs={{0,16},{8,24},{16,0},{24,8},{1,17},{9,25},{17,1},{25,9},{2,18},{10... | collective-permute-start | bytes 393224 | tf_op jit(solution)/shard_map/ppermute | solution.py:26
  18.5 1.6 %collective-permute-start.5 = (bf16[2,2,64,256]{3,2,1,0:T(8,128)(2,1)S(1)}, bf16[2,2,64,256]{3,2,1,0:T(8,128)(2,1)S(1)}, u32[]{:S(2)}, u32[]{:S(2)}) collective-permute-start(bf16[2,2,64,256]{3,2,1,0:T(8,128)(2,1)S(1)} %get-tuple-element.65.refs_0_.refs_1_), channel_id=1, source_target_pairs={{0,1},{1,0},{2,3},{3,2},{4,5},{5,4},{6,7},{7,6},{8,9},{9,8},{10,11... | collective-permute-start | bytes 393224 | tf_op jit(solution)/shard_map/ppermute | solution.py:26
  18.5 1.6 %collective-permute-start.6 = (bf16[2,2,64,256]{3,2,1,0:T(8,128)(2,1)S(1)}, bf16[2,2,64,256]{3,2,1,0:T(8,128)(2,1)S(1)}, u32[]{:S(2)}, u32[]{:S(2)}) collective-permute-start(bf16[2,2,64,256]{3,2,1,0:T(8,128)(2,1)S(1)} %get-tuple-element.66), channel_id=1, source_target_pairs={{0,1},{1,0},{2,3},{3,2},{4,5},{5,4},{6,7},{7,6},{8,9},{9,8},{10,11... | collective-permute-start | bytes 393224 | tf_op jit(solution)/shard_map/ppermute | solution.py:26
  19.0 4.4 %collective-permute-start.10 = (bf16[2,2,64,256]{3,2,1,0:T(8,128)(2,1)S(1)}, bf16[2,2,64,256]{3,2,1,0:T(8,128)(2,1)S(1)}, u32[]{:S(2)}, u32[]{:S(2)}) collective-permute-start(bf16[2,2,64,256]{3,2,1,0:T(8,128)(2,1)S(1)} %collective-permute-done.7.refs_0_), channel_id=1, source_target_pairs={{0,1},{1,0},{2,3},{3,2},{4,5},{5,4},{6,7},{7,6},{8,9},{9,8},{10,11... | collective-permute-start | bytes 393224 | tf_op jit(solution)/shard_map/ppermute | solution.py:26
  22.1 1.6 %collective-permute-start.9 = (bf16[2,2,64,256]{3,2,1,0:T(8,128)(2,1)S(1)}, bf16[2,2,64,256]{3,2,1,0:T(8,128)(2,1)S(1)}, u32[]{:S(2)}, u32[]{:S(2)}) collective-permute-start(bf16[2,2,64,256]{3,2,1,0:T(8,128)(2,1)S(1)} %collective-permute-done.8.refs_0_), channel_id=1, source_target_pairs={{0,1},{1,0},{2,3},{3,2},{4,5},{5,4},{6,7},{7,6},{8,9},{9,8},{10,11... | collective-permute-start | bytes 393224 | tf_op jit(solution)/shard_map/ppermute | solution.py:26
  26.3 1.9 %collective-permute-start.12 = (bf16[2,2,64,256]{3,2,1,0:T(8,128)(2,1)S(1)}, bf16[2,2,64,256]{3,2,1,0:T(8,128)(2,1)S(1)}, u32[]{:S(2)}, u32[]{:S(2)}) collective-permute-start(bf16[2,2,64,256]{3,2,1,0:T(8,128)(2,1)S(1)} %get-tuple-element.90), channel_id=1, source_target_pairs={{0,1},{1,0},{2,3},{3,2},{4,5},{5,4},{6,7},{7,6},{8,9},{9,8},{10,11... | collective-permute-start | bytes 393224 | tf_op jit(solution)/shard_map/ppermute | solution.py:26
  26.7 1.5 %collective-permute-start.11 = (bf16[2,2,64,256]{3,2,1,0:T(8,128)(2,1)S(1)}, bf16[2,2,64,256]{3,2,1,0:T(8,128)(2,1)S(1)}, u32[]{:S(2)}, u32[]{:S(2)}) collective-permute-start(bf16[2,2,64,256]{3,2,1,0:T(8,128)(2,1)S(1)} %get-tuple-element.88), channel_id=1, source_target_pairs={{0,1},{1,0},{2,3},{3,2},{4,5},{5,4},{6,7},{7,6},{8,9},{9,8},{10,11... | collective-permute-start | bytes 393224 | tf_op jit(solution)/shard_map/ppermute | solution.py:26
  28.3 1.4 %collective-permute-start.13 = (bf16[64,128]{1,0:T(8,128)(2,1)S(1)}, bf16[64,128]{1,0:T(8,128)(2,1)S(1)}, u32[]{:S(2)}, u32[]{:S(2)}) collective-permute-start(bf16[64,128]{1,0:T(8,128)(2,1)S(1)} %slice_bitcast_fusion), channel_id=1, source_target_pairs={{0,1},{1,0},{2,3},{3,2},{4,5},{5,4},{6,7},{7,6},{8,9},{9,8},{10,11... | collective-permute-start | bytes 49160 | tf_op jit(solution)/shard_map/ppermute | solution.py:26
  28.7 5.7 %collective-permute-start.17 = (bf16[2,2,64,256]{3,2,1,0:T(8,128)(2,1)S(1)}, bf16[2,2,64,256]{3,2,1,0:T(8,128)(2,1)S(1)}, u32[]{:S(2)}, u32[]{:S(2)}) collective-permute-start(bf16[2,2,64,256]{3,2,1,0:T(8,128)(2,1)S(1)} %sum_cores.3), channel_id=1, source_target_pairs={{0,16},{8,24},{16,0},{24,8},{1,17},{9,25},{17,1},{25,9},{2,18},{10... | collective-permute-start | bytes 393224 | tf_op jit(solution)/shard_map/ppermute | solution.py:26
  30.8 3.6 %collective-permute-start.18 = (bf16[2,2,64,256]{3,2,1,0:T(8,128)(2,1)S(1)}, bf16[2,2,64,256]{3,2,1,0:T(8,128)(2,1)S(1)}, u32[]{:S(2)}, u32[]{:S(2)}) collective-permute-start(bf16[2,2,64,256]{3,2,1,0:T(8,128)(2,1)S(1)} %get-tuple-element.104), channel_id=1, source_target_pairs={{0,1},{1,0},{2,3},{3,2},{4,5},{5,4},{6,7},{7,6},{8,9},{9,8},{10,11... | collective-permute-start | bytes 393224 | tf_op jit(solution)/shard_map/ppermute | solution.py:26
  31.1 6.5 %collective-permute-start.14 = (bf16[2,2,64,256]{3,2,1,0:T(8,128)(2,1)S(1)}, bf16[2,2,64,256]{3,2,1,0:T(8,128)(2,1)S(1)}, u32[]{:S(2)}, u32[]{:S(2)}) collective-permute-start(bf16[2,2,64,256]{3,2,1,0:T(8,128)(2,1)S(1)} %sum_cores.2), channel_id=1, source_target_pairs={{0,16},{8,24},{16,0},{24,8},{1,17},{9,25},{17,1},{25,9},{2,18},{10... | collective-permute-start | bytes 393224 | tf_op jit(solution)/shard_map/ppermute | solution.py:26
  32.1 5.5 %collective-permute-start.15 = (bf16[2,2,64,256]{3,2,1,0:T(8,128)(2,1)S(1)}, bf16[2,2,64,256]{3,2,1,0:T(8,128)(2,1)S(1)}, u32[]{:S(2)}, u32[]{:S(2)}) collective-permute-start(bf16[2,2,64,256]{3,2,1,0:T(8,128)(2,1)S(1)} %get-tuple-element.97), channel_id=1, source_target_pairs={{0,1},{1,0},{2,3},{3,2},{4,5},{5,4},{6,7},{7,6},{8,9},{9,8},{10,11... | collective-permute-start | bytes 393224 | tf_op jit(solution)/shard_map/ppermute | solution.py:26
  34.5 8.0 %collective-permute-start.19 = (bf16[2,64,256]{2,1,0:T(8,128)(2,1)S(1)}, bf16[2,64,256]{2,1,0:T(8,128)(2,1)S(1)}, u32[]{:S(2)}, u32[]{:S(2)}) collective-permute-start(bf16[2,64,256]{2,1,0:T(8,128)(2,1)S(1)} %get-tuple-element.106), channel_id=1, source_target_pairs={{0,4},{1,5},{2,6},{3,7},{4,0},{5,1},{6,2},{7,3},{8,12},{9,13},{10,... | collective-permute-start | bytes 196616 | tf_op jit(solution)/shard_map/ppermute | solution.py:26
  35.7 6.8 %collective-permute-start.20 = (bf16[2,64,256]{2,1,0:T(8,128)(2,1)S(1)}, bf16[2,64,256]{2,1,0:T(8,128)(2,1)S(1)}, u32[]{:S(2)}, u32[]{:S(2)}) collective-permute-start(bf16[2,64,256]{2,1,0:T(8,128)(2,1)S(1)} %get-tuple-element.107), channel_id=1, source_target_pairs={{0,6},{1,7},{2,4},{3,5},{4,2},{5,3},{6,0},{7,1},{8,14},{9,15},{10,... | collective-permute-start | bytes 196616 | tf_op jit(solution)/shard_map/ppermute | solution.py:26
  37.6 5.7 %collective-permute-start.21 = (bf16[2,64,256]{2,1,0:T(8,128)(2,1)S(1)}, bf16[2,64,256]{2,1,0:T(8,128)(2,1)S(1)}, u32[]{:S(2)}, u32[]{:S(2)}) collective-permute-start(bf16[2,64,256]{2,1,0:T(8,128)(2,1)S(1)} %get-tuple-element.108), channel_id=1, source_target_pairs={{0,2},{1,3},{2,0},{3,1},{4,6},{5,7},{6,4},{7,5},{8,10},{9,11},{10,... | collective-permute-start | bytes 196616 | tf_op jit(solution)/shard_map/ppermute | solution.py:26
  38.3 7.6 %collective-permute-start.16 = (bf16[2,64,1024]{2,1,0:T(8,128)(2,1)S(1)}, bf16[2,64,1024]{2,1,0:T(8,128)(2,1)S(1)}, u32[]{:S(2)}, u32[]{:S(2)}) collective-permute-start(bf16[2,64,1024]{2,1,0:T(8,128)(2,1)S(1)} %get-tuple-element.101), channel_id=1, source_target_pairs={{0,8},{8,0},{16,24},{24,16},{1,9},{9,1},{17,25},{25,17},{2,10},{10... | collective-permute-start | bytes 786440 | tf_op jit(solution)/shard_map/ppermute | solution.py:26
  43.3 4.0 %collective-permute-start.22 = (bf16[64,256]{1,0:T(8,128)(2,1)S(1)}, bf16[64,256]{1,0:T(8,128)(2,1)S(1)}, u32[]{:S(2)}, u32[]{:S(2)}) collective-permute-start(bf16[64,256]{1,0:T(8,128)(2,1)S(1)} %get-tuple-element.110), channel_id=1, source_target_pairs={{0,8},{8,0},{16,24},{24,16},{1,9},{9,1},{17,25},{25,17},{2,10},{10... | collective-permute-start | bytes 98312 | tf_op jit(solution)/shard_map/ppermute | solution.py:26
